TPU v7x, 32 devices: a whole 2x2x4 slice. The times are simulated.
32 devices in a mesh: groups: 2 (over x), node: 16 (over z, y, core).
Axes of the slice: x: 2, y: 2, z: 4, core: 2. Of those that a mesh axis runs over, the one named last changes fastest.
Arguments:
- hidden: bfloat16 [16384, 8192], P(('groups', 'node')), parts along dimension 0, may hold values from -60 to 60
- queries: bfloat16 [16384, 4096], P(('groups', 'node')), parts along dimension 0, may hold values from -240 to 240
- norm_gain: float32 [8192], replicated, may hold values from 0.5 to 2
- key_weight: bfloat16 [8192, 512], replicated, may hold values from -0.0625 to 0.0625
- value_weight: bfloat16 [8192, 512], replicated, may hold values from -0.0625 to 0.0625
- anc_ids: int32 [256, 7], P(('groups', 'node')), parts along dimension 0, may hold values from -1 to 111, as said below
- anc_cut: int32 [256, 7], P(('groups', 'node')), parts along dimension 0, may hold values from 0 to 64, as said below
Outputs:
- context: bfloat16 [16384, 4096], P(('groups', 'node')), parts along dimension 0
There are 2 independent parts, one for each index of `groups`. A program takes and returns all parts, laid end to end along the dimension named above; an argument that names none is the same for every part. Nothing has to cross between parts.
Inputs may be any that keep to these rules, and one draw needn't show every extreme that they name: `anc_ids`: block g lies on node index g // 8 and has depth d = (g // 8) // 2. Column k of its row, for k < d, names its (k+1)-th nearest ancestor, which lies on node index g // 8 - (k+1) * 2; columns k >= d hold -1. The list of a block's parent is the block's list shifted by one column. `anc_cut`: 0 exactly where anc_ids is -1. Column k + 1 of a block equals column k of its parent.
All inputs are finite; a program needn't handle non-finite values.
Results may differ from a plain program's by a relative error of at most 0.012.
The roundings to bfloat16 on the way count: a program that leaves them out, or rounds other values in their place, can miss the bound.
Values may be sent and summed in bfloat16 or wider, within the bound.
No kernel may reach another device: no remote copies, remote signals or barrier semaphores. Data moves between devices by JAX's collectives and lax.ppermute only.
A program may use at most 256 MiB of HBM per device.

v0:
```python
import jax
import jax.numpy as jnp
from jax import lax
from jax.sharding import PartitionSpec as P

HEAD_DIM = 128


def visibility(cuts, block):
    offsets = jnp.arange(block)
    count, depth = cuts.shape
    seen = offsets[None, None, :] < cuts[:, :, None]
    seen = jnp.broadcast_to(seen.reshape(count, 1, depth * block), (count, block, depth * block))
    causal = offsets[None, :] <= offsets[:, None]
    causal = jnp.broadcast_to(causal[None], (count, block, block))
    return jnp.concatenate([seen, causal], axis=2).astype(jnp.int32)


def shards(hidden, queries, norm_gain, key_weight, value_weight, anc_ids, anc_cut):
    rows = hidden.shape[0]
    blocks_here = anc_ids.shape[0]
    block = rows // blocks_here
    depth = anc_ids.shape[1]
    levels = depth + 1
    x = hidden.astype(jnp.float32)
    mean_sq = jnp.mean(x * x, axis=-1, keepdims=True)
    inverse = lax.rsqrt(mean_sq + 1e-05)
    normed = (x * inverse * norm_gain).astype(jnp.bfloat16)
    keys = jnp.dot(normed, key_weight, preferred_element_type=jnp.float32).astype(jnp.bfloat16)
    values = jnp.dot(normed, value_weight, preferred_element_type=jnp.float32).astype(jnp.bfloat16)
    width = keys.shape[1]
    stacked = jnp.concatenate([keys, values], axis=1)
    chains = lax.axis_size("node") // levels
    here = lax.axis_index("node")
    owners = here - chains * jnp.arange(1, levels, dtype=jnp.int32)
    offsets = jnp.arange(rows, dtype=jnp.int32)
    empty = jnp.zeros((depth, rows, 2 * width), jnp.bfloat16)
    piece = lax.all_gather(stacked, "node", axis=0, tiled=True)
    count = piece.shape[0]
    local = owners[:, None] * rows + offsets[None, :]
    valid = (owners[:, None] >= 0) & (local >= 0) & (local < count)
    taken = piece[jnp.clip(local, 0, count - 1)]
    fetched = jnp.where(valid[:, :, None], taken, empty)
    grouped = fetched.reshape(depth, blocks_here, block, 2 * width)
    slots = jnp.where(anc_ids >= 0, anc_ids % blocks_here, 0)
    picked = grouped[jnp.arange(depth)[None, :], slots]
    own = stacked.reshape(blocks_here, 1, block, 2 * width)
    every = jnp.concatenate([picked, own], axis=1).reshape(blocks_here, levels * block, 2 * width)
    kv_count = width // HEAD_DIM
    per_group = queries.shape[1] // width
    key_part = every[:, :, :width].reshape(blocks_here, levels * block, kv_count, HEAD_DIM)
    value_part = every[:, :, width:].reshape(blocks_here, levels * block, kv_count, HEAD_DIM)
    query_part = queries.reshape(blocks_here, block, kv_count, per_group, HEAD_DIM)
    scores = jnp.einsum(
        "bqgrd,bkgd->bgrqk", query_part, key_part, preferred_element_type=jnp.float32
    ) * HEAD_DIM ** (-0.5)
    visible = visibility(anc_cut, block)
    scores = jnp.where(visible[:, None, None] > 0, scores, -1e30)
    peak = jnp.max(scores, axis=-1, keepdims=True)
    expd = jnp.exp(scores - peak)
    total = jnp.sum(expd, axis=-1, keepdims=True)
    weights = (expd / total).astype(jnp.bfloat16)
    result = jnp.einsum(
        "bgrqk,bkgd->bqgrd", weights, value_part, preferred_element_type=jnp.float32
    )
    return result.astype(jnp.bfloat16).reshape(rows, queries.shape[1])


def solution(mesh):
    placed = (
        P(("groups", "node"), None),
        P(("groups", "node"), None),
        P(),
        P(),
        P(),
        P(("groups", "node"), None),
        P(("groups", "node"), None),
    )
    return jax.shard_map(
        shards, mesh=mesh, in_specs=placed, out_specs=P(("groups", "node"), None), check_vma=False
    )
```

profile of v0, /device:TPU:24, one launch (start us, length us, event | category | flops | bytes accessed | tf_op | source)
XLA Modules:
  0.0 340.9 jit_solution(3939323834362393916)
XLA Ops:
  6.5 0.0 copy-start.2
  6.5 0.0 all-gather.2.cloned.1.call-start
  6.5 5.1 %fusion.2 = f32[512]{0:T(512)S(1)} fusion(bf16[512,8192]{1,0:T(8,128)(2,1)} %param.7), kind=kLoop, calls=%fused_computation.9 | loop fusion | flops 12582400 | bytes 8390656 | tf_op jit(solution)/shard_map/reduce_sum | solution.py:26
  11.7 0.0 copy-done.2
  11.7 10.4 %fusion.18 = bf16[512,512]{0,1:T(8,128)(2,1)S(1)} fusion(bf16[8192,512]{1,0:T(8,128)(2,1)} %param.11, bf16[512,8192]{1,0:T(8,128)(2,1)} %param.7, f32[8192]{0:T(1024)S(1)} %copy-done.2, f32[512]{0:T(512)S(1)} %add_rsqrt_fusion), kind=kOutput, calls=%fused_computation.24 | convolution fusion | flops 4312006656 | bytes 17336320 | tf_op jit(solution)/shard_map/dot_general | solution.py:30
  22.1 0.0 copy-start.1
  22.1 0.0 copy-start
  22.1 10.4 %fusion.15 = bf16[512,512]{0,1:T(8,128)(2,1)S(1)} fusion(bf16[8192,512]{1,0:T(8,128)(2,1)} %param.10, bf16[512,8192]{1,0:T(8,128)(2,1)} %param.7, f32[8192]{0:T(1024)S(1)} %copy-done.2, f32[512]{0:T(512)S(1)} %add_rsqrt_fusion), kind=kOutput, calls=%fused_computation.23 | convolution fusion | flops 4312006656 | bytes 17336320 | tf_op jit(solution)/shard_map/dot_general | solution.py:29
  32.5 1.0 pad_maximum_fusion.1
  33.6 0.0 all-gather.2.cloned.1.call-update
  33.6 1.7 copy.20
  35.3 0.0 copy-done.1
  35.3 0.1 reshape.179
  35.4 0.1 lt.55
  35.5 0.1 compare_select_fusion
  35.6 0.0 copy-done
  35.6 0.1 lt.57
  35.6 0.1 lt.58
  35.7 5.5 %copy.34 = bf16[64,8,32,128]{3,2,1,0:T(8,128)(2,1)} copy(bf16[64,8,32,128]{3,1,2,0:T(8,128)(2,1)} %bitcast.52) | data formatting | bytes 8388608
  41.3 0.1 broadcast_in_dim.32
  41.4 0.2 convert_compare_fusion
  41.6 0.1 fusion.22
  41.7 121.5 %all-gather.2.cloned.1.call-done = bf16[8192,1024]{0,1:T(8,128)(2,1)} async-done(((bf16[512,1024]{0,1:T(8,128)(2,1)}), bf16[8192,1024]{0,1:T(8,128)(2,1)}) %all-gather.2.cloned.1.call-update) | async-done | bytes 16777232 | tf_op jit(solution)/shard_map/all_gather | solution.py:38
  163.2 22.4 %copy.19 = bf16[8192,1024]{1,0:T(8,128)(2,1)} copy(bf16[8192,1024]{0,1:T(8,128)(2,1)} %all-gather.2.cloned.1.call-done) | data formatting | bytes 33554432 | tf_op jit(solution)/shard_map/all_gather | solution.py:38
  185.7 24.3 %gather_fusion = bf16[3584,1024]{1,0:T(8,128)(2,1)} fusion(bf16[8192,1024]{1,0:T(8,128)(2,1)} %copy.19, s32[4096]{0:T(1024)S(1)} %pad_clamp_fusion), kind=kCustom, calls=%fused_computation | custom fusion | bytes 14694400 | tf_op jit(solution)/shard_map/gather | solution.py:42
  210.0 6.6 %broadcast_select_fusion = bf16[7,8,64,1024]{3,2,1,0:T(8,128)(2,1)} fusion(bf16[7,8,64,1024]{3,2,1,0:T(8,128)(2,1)} %bitcast.47, pred[7,8,64]{2,1,0:T(8,128)(4,1)S(1)} %fusion.22), kind=kLoop, calls=%fused_computation.17 | loop fusion | flops 3670016 | bytes 14683648 | tf_op jit(solution)/shard_map/jit(_where)/select_n | solution.py:43
  216.6 9.1 %gather_fusion.1 = bf16[56,64,1024]{2,1,0:T(8,128)(2,1)} fusion(bf16[7,8,64,1024]{3,2,1,0:T(8,128)(2,1)} %broadcast_select_fusion, s32[56]{0:T(128)S(1)} %reshape.179), kind=kCustom, calls=%fused_computation.1 | custom fusion | bytes 14680512 | tf_op jit(solution)/shard_map/gather | solution.py:46
  225.7 7.0 %pad_maximum_fusion = bf16[8,8,64,1024]{3,2,1,0:T(8,128)(2,1)} fusion(bf16[8,1,64,1024]{3,2,1,0:T(8,128)(2,1)S(1)} %bitcast.51, bf16[8,7,64,1024]{3,2,1,0:T(8,128)(2,1)} %bitcast.48), kind=kLoop, calls=%fused_computation.16 | loop fusion | flops 4194304 | bytes 16777216 | tf_op jit(solution)/shard_map/concatenate | solution.py:48
  232.7 5.8 %fusion.31 = (bf16[8,512,512]{2,1,0:T(8,128)(2,1)}, bf16[8,512,512]{2,1,0:T(8,128)(2,1)}) fusion(bf16[8,512,1024]{2,1,0:T(8,128)(2,1)} %bitcast.46), kind=kLoop, calls=%fused_computation.52 | loop fusion | bytes 16777216 | tf_op jit(solution)/shard_map/slice | solution.py:51
  238.5 6.4 %copy.23 = bf16[8,512,512]{1,2,0:T(8,128)(2,1)} copy(bf16[8,512,512]{2,1,0:T(8,128)(2,1)} %get-tuple-element.5) | data formatting | bytes 8388608 | tf_op jit(solution)/shard_map/slice | solution.py:51
  245.0 6.4 %copy.22 = bf16[8,512,512]{1,2,0:T(8,128)(2,1)} copy(bf16[8,512,512]{2,1,0:T(8,128)(2,1)} %get-tuple-element.6) | data formatting | bytes 8388608 | tf_op jit(solution)/shard_map/slice | solution.py:52
  251.4 19.0 %fusion.9 = f32[8,4,512,64,8]{2,3,4,1,0:T(8,128)} fusion(bf16[8,512,4,128,1]{1,3,4,2,0:T(8,128)(2,1)} %bitcast.50, bf16[8,64,4,8,128]{4,3,2,1,0:T(8,128)(2,1)} %bitcast.49), kind=kOutput, calls=%fused_computation.18 | convolution fusion | flops 2147483648 | bytes 41943040 | tf_op jit(solution)/shard_map/bqgrd,bkgd->bgrqk/dot_general | solution.py:54
  270.4 37.8 %fusion.32 = (f32[8,4,8,64]{3,2,1,0:T(8,128)S(1)}, f32[8,4,8,64,512]{4,3,2,1,0:T(8,128)}) fusion(f32[8,4,512,64,8]{2,3,4,1,0:T(8,128)} %fusion.9, pred[8,64,512]{2,1,0:T(8,128)(4,1)S(1)} %convert_compare_fusion), kind=kOutput, calls=%fused_computation.53 | output fusion | flops 50332160 | bytes 67436544 | tf_op jit(solution)/shard_map/sub | solution.py:60
  308.2 13.8 %convert_bitcast_fusion = bf16[8,64,4,8,128]{4,1,3,2,0:T(8,128)(2,1)S(1)} fusion(bf16[8,512,4,128,1]{1,3,4,2,0:T(8,128)(2,1)} %bitcast.53, f32[8,4,8,64,512]{4,3,2,1,0:T(8,128)} %get-tuple-element.8, f32[8,4,8,64]{3,2,1,0:T(8,128)S(1)} %get-tuple-element.7), kind=kOutput, calls=%fused_computation.20 | convolution fusion | flops 2166358016 | bytes 42008576 | tf_op jit(solution)/shard_map/bgrqk,bkgd->bqgrd/dot_general | solution.py:63
  322.0 4.8 %copy.27 = bf16[8,64,4,8,128]{4,3,2,1,0:T(8,128)(2,1)} copy(bf16[8,64,4,8,128]{4,1,3,2,0:T(8,128)(2,1)S(1)} %convert_bitcast_fusion) | data formatting | bytes 8388608 | tf_op jit(solution)/shard_map/convert_element_type | solution.py:66
  326.8 7.3 %reshape.170 = bf16[512,4096]{1,0:T(8,128)(2,1)} reshape(bf16[8,64,4,8,128]{4,3,2,1,0:T(8,128)(2,1)} %copy.27) | data formatting | bytes 8388608 | tf_op jit(solution)/shard_map/reshape | solution.py:66
  (11 shorter events, 0.1 us)
Async XLA Ops:
  6.5 5.1 %copy-start.2 = (f32[8192]{0:T(1024)S(1)}, f32[8192]{0:T(1024)}, u32[]{:S(2)}) copy-start(f32[8192]{0:T(1024)} %param.9) | copy-start | bytes 98308
  6.5 156.7 %all-gather.2.cloned.1.call-start = ((), (), s32[]{:S(2)}) async-start(), calls=%async_computation | async-start | bytes 17825792 | tf_op jit(solution)/shard_map/all_gather | solution.py:38
  22.1 13.2 %copy-start.1 = (s32[8,7]{1,0:T(8,128)S(1)}, s32[8,7]{1,0:T(8,128)}, u32[]{:S(2)}) copy-start(s32[8,7]{1,0:T(8,128)} %param.12) | copy-start | bytes 676
  22.1 13.5 %copy-start = (s32[8,7]{1,0:T(8,128)S(1)}, s32[8,7]{1,0:T(8,128)}, u32[]{:S(2)}) copy-start(s32[8,7]{1,0:T(8,128)} %param.13) | copy-start | bytes 676
Sparse Core Ops, SparseCore 0:
  33.7 129.4 all-gather.1
where the time goes:
time: 346 us; the launch traced here: 341 us
  waiting for transfers between devices  122 us (35%)
  local copies, waits for them, and re-layouts  94.2 us (27%)
  other arithmetic  58.1 us (17%)
  matrix products  53.6 us (15%)
  between operations  13.5 us (4%)
    all_gather x1, waiting for transfers between devices, shards(): piece = lax.all_gather(stacked, 'node', axis=0, tiled=True)  122 us
    sub x1, other arithmetic, shards(): expd = jnp.exp(scores - peak)  37.8 us
    gather x1, local copies, waits for them, and re-layouts, shards(): taken = piece[jnp.clip(local, 0, count - 1)]  24.3 us
    all_gather x1, local copies, waits for them, and re-layouts, shards(): piece = lax.all_gather(stacked, 'node', axis=0, tiled=True)  22.4 us
    dot_general x1, matrix products, shards(): jnp.einsum('bqgrd,bkgd->bgrqk', query_part, key_part, preferred_element_t...  19 us
    dot_general x1, matrix products, shards(): jnp.einsum('bgrqk,bkgd->bqgrd', weights, value_part, preferred_element_ty...  13.8 us
    slice x2, local copies, waits for them, and re-layouts, shards(): every[:, :, :width].reshape(blocks_here, levels * block, kv_count, HEAD_DIM)  12.3 us
    dot_general x1, matrix products, shards(): jnp.dot(normed, key_weight, preferred_element_type=jnp.float32)  10.4 us
  transfers between devices with their start and end apart: 1, of which 1 were waited for; matrix products, arithmetic and copies ran while one was open for 2% of the time, Pallas kernels for 0%

commit v1 on v0

v1 whole, which is shorter than its diff:
```python
import functools
import jax
import jax.numpy as jnp
from jax import lax
from jax.experimental import pallas as pl
from jax.experimental.pallas import tpu as pltpu
from jax.sharding import PartitionSpec as P

HEAD_DIM = 128
EPS = 1e-05
LOG2E = 1.4426950408889634
MASKED = -1e30
VMEM_BYTES = 56 * 1024 * 1024


def norm_project_kernel(x_ref, gain_ref, key_ref, value_ref, normed_ref, kv_ref):
    rows, features = x_ref.shape
    chunk = 512

    def square(c, acc):
        cols = pl.ds(pl.multiple_of(c * chunk, chunk), chunk)
        x = x_ref[:, cols].astype(jnp.float32)
        return acc + x * x

    acc = lax.fori_loop(0, features // chunk, square, jnp.zeros((rows, chunk), jnp.float32))
    mean_sq = jnp.sum(acc, axis=-1, keepdims=True) / features
    inverse = lax.rsqrt(mean_sq + EPS)

    def scale(c, carry):
        cols = pl.ds(pl.multiple_of(c * chunk, chunk), chunk)
        x = x_ref[:, cols].astype(jnp.float32)
        normed_ref[:, cols] = (x * inverse * gain_ref[:, cols]).astype(jnp.bfloat16)
        return carry

    lax.fori_loop(0, features // chunk, scale, 0)
    normed = normed_ref[...]
    for col, weight in enumerate((key_ref, value_ref)):
        part = jnp.dot(normed, weight[...], preferred_element_type=jnp.float32)
        kv_ref[:, col * HEAD_DIM : (col + 1) * HEAD_DIM] = part.astype(jnp.bfloat16)


def norm_project(hidden, gain, key_weight, value_weight):
    rows, features = hidden.shape
    step = rows // 4
    weight = pl.BlockSpec((features, HEAD_DIM), lambda i: (0, 0), pipeline_mode=pl.Buffered(1))
    return pl.pallas_call(
        norm_project_kernel,
        grid=(rows // step,),
        in_specs=[
            pl.BlockSpec((step, features), lambda i: (i, 0)),
            pl.BlockSpec((1, features), lambda i: (0, 0), pipeline_mode=pl.Buffered(1)),
            weight,
            weight,
        ],
        out_specs=[
            pl.BlockSpec((step, features), lambda i: (i, 0)),
            pl.BlockSpec((step, 2 * HEAD_DIM), lambda i: (i, 0)),
        ],
        out_shape=[
            jax.ShapeDtypeStruct((rows, features), jnp.bfloat16),
            jax.ShapeDtypeStruct((rows, 2 * HEAD_DIM), jnp.bfloat16),
        ],
        compiler_params=pltpu.CompilerParams(vmem_limit_bytes=VMEM_BYTES),
        cost_estimate=pl.CostEstimate(
            flops=4 * rows * features * HEAD_DIM, bytes_accessed=20 << 20, transcendentals=0
        ),
        name="norm_project",
    )(hidden, gain.reshape(1, features), key_weight, value_weight)


def project_kernel(normed_ref, key_ref, value_ref, *kv_refs):
    head = pl.program_id(0)
    normed = normed_ref[...]
    for col, weight in enumerate((key_ref, value_ref)):
        part = jnp.dot(normed, weight[...], preferred_element_type=jnp.float32).astype(jnp.bfloat16)
        for index, kv_ref in enumerate(kv_refs):

            @pl.when(head == index)
            def _(kv_ref=kv_ref, part=part, col=col):
                kv_ref[:, col * HEAD_DIM : (col + 1) * HEAD_DIM] = part


def project(normed, key_weight, value_weight, heads):
    rows, features = normed.shape
    weight = pl.BlockSpec((features, HEAD_DIM), lambda h: (0, h + 1))
    return pl.pallas_call(
        project_kernel,
        grid=(heads,),
        in_specs=[
            pl.BlockSpec((rows, features), lambda h: (0, 0), pipeline_mode=pl.Buffered(1)),
            weight,
            weight,
        ],
        out_specs=[pl.BlockSpec((rows, 2 * HEAD_DIM), lambda h: (0, 0)) for _ in range(heads)],
        out_shape=[jax.ShapeDtypeStruct((rows, 2 * HEAD_DIM), jnp.bfloat16) for _ in range(heads)],
        compiler_params=pltpu.CompilerParams(vmem_limit_bytes=VMEM_BYTES),
        cost_estimate=pl.CostEstimate(
            flops=4 * heads * rows * features * HEAD_DIM, bytes_accessed=20 << 20, transcendentals=0
        ),
        name="project",
    )(normed, key_weight, value_weight)


def attention_kernel(block, per_group, near, slot_ref, cut_ref, odd_ref, q_ref, own_ref, *refs):
    out_ref = refs[-1]
    straight, crossed = refs[:near], refs[near : 2 * near + 1]
    depth = slot_ref.shape[1]
    here = pl.program_id(0)
    odd = odd_ref[0] == 1
    pieces = []
    for k in range(depth):
        rows = pl.ds(pl.multiple_of(slot_ref[here, k] * block, block), block)
        if k % 2 == 1:
            pieces.append(straight[k // 2][rows, :])
        else:
            low = crossed[k // 2][rows, :]
            high = crossed[min(k // 2 + 1, near)][rows, :]
            pieces.append(jnp.where(odd, low, high))
    pieces.append(own_ref[pl.ds(pl.multiple_of(here * block, block), block), :])
    every = jnp.concatenate(pieces, axis=0)
    width = (depth + 1) * block
    keys, values = every[:, :HEAD_DIM], every[:, HEAD_DIM:]
    lane = lax.broadcasted_iota(jnp.int32, (block, width), 1)
    token = lax.broadcasted_iota(jnp.int32, (block, width), 0)
    limit = jnp.where(lane >= depth * block, token + (depth * block + 1), 0)
    for k in range(depth):
        inside = (lane >= k * block) & (lane < (k + 1) * block)
        limit = jnp.where(inside, cut_ref[here, k] + k * block, limit)
    bias = jnp.where(lane < limit, 0.0, MASKED)
    queries = jnp.concatenate(
        [q_ref[:, r * HEAD_DIM : (r + 1) * HEAD_DIM] for r in range(per_group)], axis=0
    )
    scores = lax.dot_general(
        queries, keys, (((1,), (1,)), ((), ())), preferred_element_type=jnp.float32
    )
    scores = (scores.reshape(per_group, block, width) + bias[None]).reshape(per_group * block, width)
    peak = jnp.max(scores, axis=-1, keepdims=True)
    weights = jnp.exp2((scores - peak) * (HEAD_DIM**-0.5 * LOG2E)).astype(jnp.bfloat16)
    padded = jnp.concatenate([values, jnp.ones_like(values)], axis=1)
    both = jnp.dot(weights, padded, preferred_element_type=jnp.float32)
    context = (both[:, :HEAD_DIM] / both[:, HEAD_DIM:]).astype(jnp.bfloat16)
    for r in range(per_group):
        out_ref[:, r * HEAD_DIM : (r + 1) * HEAD_DIM] = context[r * block : (r + 1) * block]


def attention(slots, cuts, odd, queries, own, straight, crossed, head, heads, previous):
    rows, features = queries.shape
    blocks = slots.shape[0]
    block = rows // blocks
    wide = features // heads
    near = len(straight)
    whole = pl.BlockSpec(own.shape, lambda b, *_: (0, 0), pipeline_mode=pl.Buffered(1))
    part = pl.BlockSpec((block, wide), lambda b, *_: (b, head))
    operands = [slots, cuts, odd, queries, own, *straight, *crossed]
    in_specs = [part] + [whole] * (1 + near + len(crossed))
    aliases = {}
    if previous is not None:
        aliases = {len(operands): 0}
        operands.append(previous)
        in_specs.append(pl.BlockSpec(memory_space=pl.ANY))
    return pl.pallas_call(
        functools.partial(attention_kernel, block, wide // HEAD_DIM, near),
        grid_spec=pltpu.PrefetchScalarGridSpec(
            num_scalar_prefetch=3, grid=(blocks,), in_specs=in_specs, out_specs=part
        ),
        out_shape=jax.ShapeDtypeStruct((rows, features), jnp.bfloat16),
        input_output_aliases=aliases,
        compiler_params=pltpu.CompilerParams(vmem_limit_bytes=VMEM_BYTES),
        cost_estimate=pl.CostEstimate(
            flops=4 * rows * features // heads * 8 * block,
            bytes_accessed=4 << 20,
            transcendentals=rows * wide // HEAD_DIM * 8 * block,
        ),
        name="attention",
    )(*operands)


def shards(hidden, queries, norm_gain, key_weight, value_weight, anc_ids, anc_cut):
    blocks, depth = anc_ids.shape
    levels = depth + 1
    size = lax.axis_size("node")
    chains = size // levels
    heads = key_weight.shape[1] // HEAD_DIM
    near = depth // 2
    half = [index // chains // 2 for index in range(size)]
    even = [index // chains % 2 == 0 for index in range(size)]
    other = [index + chains if even[index] else index - chains for index in range(size)]
    odd = (lax.axis_index("node") // chains % 2).astype(jnp.int32).reshape(1)
    slots = jnp.where(anc_ids >= 0, anc_ids % blocks, 0)

    normed, first = norm_project(hidden, norm_gain, key_weight, value_weight)
    rest = project(normed, key_weight, value_weight, heads - 1)
    own = [first, *rest]
    result = None
    for head in range(heads):
        piece = own[head]
        straight = [
            lax.ppermute(
                piece,
                "node",
                [(i, i + 2 * s * chains) for i in range(size) if i + 2 * s * chains < size],
            )
            for s in range(1, near + 1)
        ]
        crossed = [lax.ppermute(piece, "node", [(i, other[i]) for i in range(size) if even[i]])]
        for s in range(1, near + 1):
            pairs = [(i, other[i]) for i in range(size) if half[i] >= s]
            crossed.append(lax.ppermute(straight[s - 1], "node", pairs))
        result = attention(
            slots, anc_cut, odd, queries, piece, straight, crossed, head, heads, result
        )
    return result


def solution(mesh):
    placed = (
        P(("groups", "node"), None),
        P(("groups", "node"), None),
        P(),
        P(),
        P(),
        P(("groups", "node"), None),
        P(("groups", "node"), None),
    )
    return jax.shard_map(
        shards, mesh=mesh, in_specs=placed, out_specs=P(("groups", "node"), None), check_vma=False
    )
```

time: 346 us -> 225 us (0.65); the launches traced: 341 us -> 224 us
  local copies, waits for them, and re-layouts: 94.2 us -> 2.32 us
  Pallas kernels: 0 us -> 87.4 us
  starting transfers between devices: 0.01 us -> 69.4 us
  waiting for transfers between devices: 122 us -> 63.6 us
  other arithmetic: 58.1 us -> 0.6 us
  matrix products: 53.6 us -> 0 us
  between operations: 13.5 us -> 0.58 us
    all_gather x1 -> x0, waiting for transfers between devices: 122 us -> none  [shards(): piece = lax.all_gather(stacked, 'node', axis=0, tiled=True)]
    pallas_call x0 -> x6, Pallas kernels: none -> 87.4 us  [the longest x4 39.9 us: attention(): pl.pallas_call(functools.partial(attention_kernel, block, wide // HEAD_DI...]
    ppermute x0 -> x28, starting transfers between devices: none -> 69.4 us  [the longest x12 39.8 us: shards(): crossed.append(lax.ppermute(straight[s - 1], 'node', pairs))]
    ppermute x0 -> x28, waiting for transfers between devices: none -> 63.6 us  [the longest x12 55.6 us: shards(): lax.ppermute(piece, 'node', [(i, i + 2 * s * chains) for i in range(size)...]
    dot_general x4 -> x0, matrix products: 53.6 us -> none  [the longest x1 19 us: shards(): jnp.einsum('bqgrd,bkgd->bgrqk', query_part, key_part, preferred_element_t...]
    sub x1 -> x0, other arithmetic: 37.8 us -> none  [shards(): expd = jnp.exp(scores - peak)]
    gather x2 -> x0, local copies, waits for them, and re-layouts: 33.4 us -> none  [the longest x1 24.3 us: shards(): taken = piece[jnp.clip(local, 0, count - 1)]]
    all_gather x1 -> x0, local copies, waits for them, and re-layouts: 22.4 us -> none  [shards(): piece = lax.all_gather(stacked, 'node', axis=0, tiled=True)]
  transfers between devices with their start and end apart: 1 -> 28, of which waited for: 1 -> 11; matrix products, arithmetic and copies ran while one was open for 2% -> 0% of each run, Pallas kernels for 0% -> 13%
where the time goes in v1:
time: 225 us; the launch traced here: 224 us
  Pallas kernels  87.4 us (39%)
  starting transfers between devices  69.4 us (31%)
  waiting for transfers between devices  63.6 us (28%)
  local copies, waits for them, and re-layouts  2.32 us (1%)
    ppermute x12, waiting for transfers between devices, shards(): lax.ppermute(piece, 'node', [(i, i + 2 * s * chains) for i in range(size)...  55.6 us
    pallas_call x4, Pallas kernels, attention(): pl.pallas_call(functools.partial(attention_kernel, block, wide // HEAD_DI...  39.9 us
    ppermute x12, starting transfers between devices, shards(): crossed.append(lax.ppermute(straight[s - 1], 'node', pairs))  39.8 us
    pallas_call x1, Pallas kernels, project(): pl.pallas_call(project_kernel, grid=(heads,), in_specs=[pl.BlockSpec((row...  32.6 us
    ppermute x12, starting transfers between devices, shards(): lax.ppermute(piece, 'node', [(i, i + 2 * s * chains) for i in range(size)...  15.4 us
    pallas_call x1, Pallas kernels, norm_project(): pl.pallas_call(norm_project_kernel, grid=(rows // step,), in_specs=[pl.Bl...  14.8 us
    ppermute x4, starting transfers between devices, shards(): lax.ppermute(piece, 'node', [(i, other[i]) for i in range(size) if even[i]])  14.1 us
    ppermute x12, waiting for transfers between devices, shards(): crossed.append(lax.ppermute(straight[s - 1], 'node', pairs))  7.98 us
  transfers between devices with their start and end apart: 28, of which 11 were waited for; matrix products, arithmetic and copies ran while one was open for 0% of the time, Pallas kernels for 13%

profile of v1, /device:TPU:24, one launch (start us, length us, event | category | flops | bytes accessed | tf_op | source)
XLA Modules:
  0.0 223.9 jit_solution(5218642511499982228)
XLA Ops:
  0.0 14.8 %norm_project.1 = (bf16[512,8192]{1,0:T(8,128)(2,1)}, bf16[512,256]{1,0:T(8,128)(2,1)}) custom-call(bf16[512,8192]{1,0:T(8,128)(2,1)} %x_ref.1, f32[1,8192]{1,0:T(1,128)} %bitcast.2, bf16[8192,512]{1,0:T(8,128)(2,1)} %key_ref.3, bf16[8192,512]{1,0:T(8,128)(2,1)} %value_ref.3), custom_call_target="tpu_custom_call" | custom-call | flops 2147483648 | bytes 20971520 | tf_op jit(solution)/shard_map/norm_project/pallas_call | solution.py:46
  14.8 32.6 %project.1 = (bf16[512,256]{1,0:T(8,128)(2,1)}, bf16[512,256]{1,0:T(8,128)(2,1)}, bf16[512,256]{1,0:T(8,128)(2,1)}) custom-call(bf16[512,8192]{1,0:T(8,128)(2,1)} %get-tuple-element.10.normed_ref, bf16[8192,512]{1,0:T(8,128)(2,1)} %key_ref.3, bf16[8192,512]{1,0:T(8,128)(2,1)} %value_ref.3), custom_call_target="tpu_custom_call" | custom-call | flops 6442450944 | bytes 20971520 | tf_op jit(solution)/shard_map/project/pallas_call | solution.py:86
  47.4 1.3 collective-permute-start.2
  48.7 1.3 collective-permute-start.1
  50.0 1.3 collective-permute-start
  51.3 3.4 %collective-permute-start.10 = (bf16[512,256]{1,0:T(8,128)(2,1)}, bf16[512,256]{1,0:T(8,128)(2,1)S(1)}, u32[]{:S(2)}, u32[]{:S(2)}) collective-permute-start(bf16[512,256]{1,0:T(8,128)(2,1)} %get-tuple-element.12.own_ref), channel_id=1, source_target_pairs={{0,2},{1,3},{4,6},{5,7},{8,10},{9,11},{12,14},{13,15},{16,18},{17,... | collective-permute-start | bytes 786440 | tf_op jit(solution)/shard_map/ppermute | solution.py:205
  54.8 1.3 collective-permute-start.9
  56.1 4.6 %collective-permute-done.2.refs_2_ = bf16[512,256]{1,0:T(8,128)(2,1)S(1)} collective-permute-done((bf16[512,256]{1,0:T(8,128)(2,1)}, bf16[512,256]{1,0:T(8,128)(2,1)S(1)}, u32[]{:S(2)}, u32[]{:S(2)}) %collective-permute-start.2) | collective-permute-done | bytes 262176 | tf_op jit(solution)/shard_map/ppermute | solution.py:198
  60.7 1.3 collective-permute-start.8
  61.9 9.9 %collective-permute-done.1.refs_1_ = bf16[512,256]{1,0:T(8,128)(2,1)S(1)} collective-permute-done((bf16[512,256]{1,0:T(8,128)(2,1)}, bf16[512,256]{1,0:T(8,128)(2,1)S(1)}, u32[]{:S(2)}, u32[]{:S(2)}) %collective-permute-start.1) | collective-permute-done | bytes 262176 | tf_op jit(solution)/shard_map/ppermute | solution.py:198
  71.9 1.3 collective-permute-start.7
  73.2 3.4 %collective-permute-start.17 = (bf16[512,256]{1,0:T(8,128)(2,1)}, bf16[512,256]{1,0:T(8,128)(2,1)S(1)}, u32[]{:S(2)}, u32[]{:S(2)}) collective-permute-start(bf16[512,256]{1,0:T(8,128)(2,1)} %get-tuple-element.13.own_ref), channel_id=1, source_target_pairs={{0,2},{1,3},{4,6},{5,7},{8,10},{9,11},{12,14},{13,15},{16,18},{17,... | collective-permute-start | bytes 786440 | tf_op jit(solution)/shard_map/ppermute | solution.py:205
  76.7 1.3 collective-permute-start.16
  78.0 1.3 collective-permute-start.15
  79.3 25.1 %collective-permute-done.8.refs_1_ = bf16[512,256]{1,0:T(8,128)(2,1)S(1)} collective-permute-done((bf16[512,256]{1,0:T(8,128)(2,1)}, bf16[512,256]{1,0:T(8,128)(2,1)S(1)}, u32[]{:S(2)}, u32[]{:S(2)}) %collective-permute-start.8) | collective-permute-done | bytes 262176 | tf_op jit(solution)/shard_map/ppermute | solution.py:198
  104.4 1.3 collective-permute-start.14
  105.8 3.4 %collective-permute-start.24 = (bf16[512,256]{1,0:T(8,128)(2,1)S(1)}, bf16[512,256]{1,0:T(8,128)(2,1)S(1)}, u32[]{:S(2)}, u32[]{:S(2)}) collective-permute-start(bf16[512,256]{1,0:T(8,128)(2,1)S(1)} %copy-done.19), channel_id=1, source_target_pairs={{0,2},{1,3},{4,6},{5,7},{8,10},{9,11},{12,14},{13,15},{16,18},{17,... | collective-permute-start | bytes 786440 | tf_op jit(solution)/shard_map/ppermute | solution.py:205
  109.2 1.3 collective-permute-start.23
  110.6 1.3 collective-permute-start.22
  111.9 14.8 %collective-permute-done.15.refs_1_ = bf16[512,256]{1,0:T(8,128)(2,1)S(1)} collective-permute-done((bf16[512,256]{1,0:T(8,128)(2,1)}, bf16[512,256]{1,0:T(8,128)(2,1)S(1)}, u32[]{:S(2)}, u32[]{:S(2)}) %collective-permute-start.15) | collective-permute-done | bytes 262176 | tf_op jit(solution)/shard_map/ppermute | solution.py:198
  126.6 1.3 collective-permute-start.21
  127.9 3.8 %collective-permute-start.13 = (bf16[512,256]{1,0:T(8,128)(2,1)S(1)}, bf16[512,256]{1,0:T(8,128)(2,1)S(1)}, u32[]{:S(2)}, u32[]{:S(2)}) collective-permute-start(bf16[512,256]{1,0:T(8,128)(2,1)S(1)} %collective-permute-done.9.refs_2_), channel_id=1, source_target_pairs={{12,14},{13,15},{14,12},{15,13},{28,30},{29,31},{30,28},{31,29}} | collective-permute-start | bytes 786440 | tf_op jit(solution)/shard_map/ppermute | solution.py:208
  131.7 2.1 collective-permute-start.12
  133.8 3.8 %collective-permute-start.20 = (bf16[512,256]{1,0:T(8,128)(2,1)S(1)}, bf16[512,256]{1,0:T(8,128)(2,1)S(1)}, u32[]{:S(2)}, u32[]{:S(2)}) collective-permute-start(bf16[512,256]{1,0:T(8,128)(2,1)S(1)} %collective-permute-done.16.refs_2_), channel_id=1, source_target_pairs={{12,14},{13,15},{14,12},{15,13},{28,30},{29,31},{30,28},{31,29}} | collective-permute-start | bytes 786440 | tf_op jit(solution)/shard_map/ppermute | solution.py:208
  137.6 0.8 collective-permute-done.22.refs_1_
  138.3 3.4 %collective-permute-start.19 = (bf16[512,256]{1,0:T(8,128)(2,1)S(1)}, bf16[512,256]{1,0:T(8,128)(2,1)S(1)}, u32[]{:S(2)}, u32[]{:S(2)}) collective-permute-start(bf16[512,256]{1,0:T(8,128)(2,1)S(1)} %collective-permute-done.15.refs_1_), channel_id=1, source_target_pairs={{8,10},{9,11},{10,8},{11,9},{12,14},{13,15},{14,12},{15,13},{24,26... | collective-permute-start | bytes 786440 | tf_op jit(solution)/shard_map/ppermute | solution.py:208
  142.2 3.9 %collective-permute-start.18 = (bf16[512,256]{1,0:T(8,128)(2,1)S(1)}, bf16[512,256]{1,0:T(8,128)(2,1)}, u32[]{:S(2)}, u32[]{:S(2)}) collective-permute-start(bf16[512,256]{1,0:T(8,128)(2,1)S(1)} %collective-permute-done.14.refs_0_), channel_id=1, source_target_pairs={{4,6},{5,7},{6,4},{7,5},{8,10},{9,11},{10,8},{11,9},{12,14},{13,15... | collective-permute-start | bytes 786440 | tf_op jit(solution)/shard_map/ppermute | solution.py:208
  146.1 1.9 collective-permute-start.27
  148.1 3.9 %collective-permute-start.26 = (bf16[512,256]{1,0:T(8,128)(2,1)}, bf16[512,256]{1,0:T(8,128)(2,1)}, u32[]{:S(2)}, u32[]{:S(2)}) collective-permute-start(bf16[512,256]{1,0:T(8,128)(2,1)} %collective-permute-done.22.refs_1_), channel_id=1, source_target_pairs={{8,10},{9,11},{10,8},{11,9},{12,14},{13,15},{14,12},{15,13},{24,26... | collective-permute-start | bytes 786440 | tf_op jit(solution)/shard_map/ppermute | solution.py:208
  152.0 2.0 collective-permute-start.25
  154.0 1.8 collective-permute-done.19.refs_5_
  155.9 0.7 copy-done.14
  156.6 3.8 %collective-permute-start.11 = (bf16[512,256]{1,0:T(8,128)(2,1)S(1)}, bf16[512,256]{1,0:T(8,128)(2,1)}, u32[]{:S(2)}, u32[]{:S(2)}) collective-permute-start(bf16[512,256]{1,0:T(8,128)(2,1)S(1)} %collective-permute-done.7.refs_0_), channel_id=1, source_target_pairs={{4,6},{5,7},{6,4},{7,5},{8,10},{9,11},{10,8},{11,9},{12,14},{13,15... | collective-permute-start | bytes 786440 | tf_op jit(solution)/shard_map/ppermute | solution.py:208
  160.4 0.6 fusion.1.slot_ref
  161.0 0.6 collective-permute-done.18.refs_4_
  161.6 3.8 %collective-permute-start.3 = (bf16[512,256]{1,0:T(8,128)(2,1)}, bf16[512,256]{1,0:T(8,128)(2,1)S(1)}, u32[]{:S(2)}, u32[]{:S(2)}) collective-permute-start(bf16[512,256]{1,0:T(8,128)(2,1)} %get-tuple-element.11.own_ref), channel_id=1, source_target_pairs={{0,2},{1,3},{4,6},{5,7},{8,10},{9,11},{12,14},{13,15},{16,18},{17,... | collective-permute-start | bytes 786440 | tf_op jit(solution)/shard_map/ppermute | solution.py:205
  165.4 1.8 collective-permute-done.27.refs_6_
  167.2 3.8 %collective-permute-start.6 = (bf16[512,256]{1,0:T(8,128)(2,1)S(1)}, bf16[512,256]{1,0:T(8,128)(2,1)S(1)}, u32[]{:S(2)}, u32[]{:S(2)}) collective-permute-start(bf16[512,256]{1,0:T(8,128)(2,1)S(1)} %collective-permute-done.2.refs_2_), channel_id=1, source_target_pairs={{12,14},{13,15},{14,12},{15,13},{28,30},{29,31},{30,28},{31,29}} | collective-permute-start | bytes 786440 | tf_op jit(solution)/shard_map/ppermute | solution.py:208
  171.0 1.8 collective-permute-done.26.refs_5_
  172.8 3.8 %collective-permute-start.5 = (bf16[512,256]{1,0:T(8,128)(2,1)S(1)}, bf16[512,256]{1,0:T(8,128)(2,1)S(1)}, u32[]{:S(2)}, u32[]{:S(2)}) collective-permute-start(bf16[512,256]{1,0:T(8,128)(2,1)S(1)} %collective-permute-done.1.refs_1_), channel_id=1, source_target_pairs={{8,10},{9,11},{10,8},{11,9},{12,14},{13,15},{14,12},{15,13},{24,26... | collective-permute-start | bytes 786440 | tf_op jit(solution)/shard_map/ppermute | solution.py:208
  176.6 1.8 collective-permute-done.25.refs_4_
  178.4 3.8 %collective-permute-start.4 = (bf16[512,256]{1,0:T(8,128)(2,1)S(1)}, bf16[512,256]{1,0:T(8,128)(2,1)S(1)}, u32[]{:S(2)}, u32[]{:S(2)}) collective-permute-start(bf16[512,256]{1,0:T(8,128)(2,1)S(1)} %collective-permute-done.refs_0_), channel_id=1, source_target_pairs={{4,6},{5,7},{6,4},{7,5},{8,10},{9,11},{10,8},{11,9},{12,14},{13,15... | collective-permute-start | bytes 786440 | tf_op jit(solution)/shard_map/ppermute | solution.py:208
  182.2 10.0 %attention.4.refs_7_ = bf16[512,4096]{1,0:T(8,128)(2,1)} custom-call(s32[8,7]{1,0:T(8,128)} %fusion.1.slot_ref, s32[8,7]{1,0:T(8,128)} %cut_ref.7, s32[1]{0:T(128)} %bitcast.odd_ref, bf16[512,4096]{1,0:T(8,128)(2,1)} %q_ref.7, bf16[512,256]{1,0:T(8,128)(2,1)} %get-tuple-element.14.own_ref, bf16[512,256]{1,0:T(8,128)(2,1)} %collective-permute-done.21.refs_0_, ...), custom_call_target="tpu_custom_call" | custom-call | flops 1073741824 | bytes 4194304 | tf_op jit(solution)/shard_map/attention/pallas_call | solution.py:161
  192.3 10.0 %attention.5.refs_7_ = bf16[512,4096]{1,0:T(8,128)(2,1)} custom-call(s32[8,7]{1,0:T(8,128)} %fusion.1.slot_ref, s32[8,7]{1,0:T(8,128)} %cut_ref.7, s32[1]{0:T(128)} %bitcast.odd_ref, bf16[512,4096]{1,0:T(8,128)(2,1)} %q_ref.7, bf16[512,256]{1,0:T(8,128)(2,1)} %get-tuple-element.13.own_ref, ...), custom_call_target="tpu_custom_call", output_to_operand_aliasing={{}: (12, {})} | custom-call | flops 1073741824 | bytes 4194304 | tf_op jit(solution)/shard_map/attention/pallas_call | solution.py:161
  202.3 10.0 %attention.6.refs_7_ = bf16[512,4096]{1,0:T(8,128)(2,1)} custom-call(s32[8,7]{1,0:T(8,128)} %fusion.1.slot_ref, s32[8,7]{1,0:T(8,128)} %cut_ref.7, s32[1]{0:T(128)} %bitcast.odd_ref, bf16[512,4096]{1,0:T(8,128)(2,1)} %q_ref.7, bf16[512,256]{1,0:T(8,128)(2,1)} %get-tuple-element.12.own_ref, ...), custom_call_target="tpu_custom_call", output_to_operand_aliasing={{}: (12, {})} | custom-call | flops 1073741824 | bytes 4194304 | tf_op jit(solution)/shard_map/attention/pallas_call | solution.py:161
  212.3 0.7 copy-done.15
  213.2 0.7 copy-done.18
  213.9 10.0 %attention.7 = bf16[512,4096]{1,0:T(8,128)(2,1)} custom-call(s32[8,7]{1,0:T(8,128)} %fusion.1.slot_ref, s32[8,7]{1,0:T(8,128)} %cut_ref.7, s32[1]{0:T(128)} %bitcast.odd_ref, bf16[512,4096]{1,0:T(8,128)(2,1)} %q_ref.7, bf16[512,256]{1,0:T(8,128)(2,1)} %get-tuple-element.11.own_ref, bf16[512,256]{1,0:T(8,128)(2,1)} %copy-done.2, ...), custom_call_target="tpu_custom_call", output_to_operand_aliasing={{}: (12, {})} | custom-call | flops 1073741824 | bytes 4194304 | tf_op jit(solution)/shard_map/attention/pallas_call | solution.py:161
  (59 shorter events, 0.7 us)
Async XLA Ops:
  14.8 90.9 %copy-start.19 = (bf16[512,256]{1,0:T(8,128)(2,1)S(1)}, bf16[512,256]{1,0:T(8,128)(2,1)}, u32[]{:S(2)}) copy-start(bf16[512,256]{1,0:T(8,128)(2,1)} %get-tuple-element.14.own_ref) | copy-start | bytes 786436
  14.8 145.5 %copy-start.21 = (s32[8,7]{1,0:T(8,128)S(1)}, s32[8,7]{1,0:T(8,128)}, u32[]{:S(2)}) copy-start(s32[8,7]{1,0:T(8,128)} %param.12) | copy-start | bytes 676
  47.4 13.2 %collective-permute-start.2 = (bf16[512,256]{1,0:T(8,128)(2,1)}, bf16[512,256]{1,0:T(8,128)(2,1)S(1)}, u32[]{:S(2)}, u32[]{:S(2)}) collective-permute-start(bf16[512,256]{1,0:T(8,128)(2,1)} %get-tuple-element.11.own_ref), channel_id=1, source_target_pairs={{0,12},{1,13},{2,14},{3,15},{16,28},{17,29},{18,30},{19,31}} | collective-permute-start | bytes 786440 | tf_op jit(solution)/shard_map/ppermute | solution.py:198
  48.7 23.2 %collective-permute-start.1 = (bf16[512,256]{1,0:T(8,128)(2,1)}, bf16[512,256]{1,0:T(8,128)(2,1)S(1)}, u32[]{:S(2)}, u32[]{:S(2)}) collective-permute-start(bf16[512,256]{1,0:T(8,128)(2,1)} %get-tuple-element.11.own_ref), channel_id=1, source_target_pairs={{0,8},{1,9},{2,10},{3,11},{4,12},{5,13},{6,14},{7,15},{16,24},{17,... | collective-permute-start | bytes 786440 | tf_op jit(solution)/shard_map/ppermute | solution.py:198
  50.0 23.2 %collective-permute-start = (bf16[512,256]{1,0:T(8,128)(2,1)}, bf16[512,256]{1,0:T(8,128)(2,1)S(1)}, u32[]{:S(2)}, u32[]{:S(2)}) collective-permute-start(bf16[512,256]{1,0:T(8,128)(2,1)} %get-tuple-element.11.own_ref), channel_id=1, source_target_pairs={{0,4},{1,5},{2,6},{3,7},{4,8},{5,9},{6,10},{7,11},{8,12},{9,13},{1... | collective-permute-start | bytes 786440 | tf_op jit(solution)/shard_map/ppermute | solution.py:198
  51.3 25.3 %collective-permute-start.10 = (bf16[512,256]{1,0:T(8,128)(2,1)}, bf16[512,256]{1,0:T(8,128)(2,1)S(1)}, u32[]{:S(2)}, u32[]{:S(2)}) collective-permute-start(bf16[512,256]{1,0:T(8,128)(2,1)} %get-tuple-element.12.own_ref), channel_id=1, source_target_pairs={{0,2},{1,3},{4,6},{5,7},{8,10},{9,11},{12,14},{13,15},{16,18},{17,... | collective-permute-start | bytes 786440 | tf_op jit(solution)/shard_map/ppermute | solution.py:205
  54.8 23.2 %collective-permute-start.9 = (bf16[512,256]{1,0:T(8,128)(2,1)}, bf16[512,256]{1,0:T(8,128)(2,1)S(1)}, u32[]{:S(2)}, u32[]{:S(2)}) collective-permute-start(bf16[512,256]{1,0:T(8,128)(2,1)} %get-tuple-element.12.own_ref), channel_id=1, source_target_pairs={{0,12},{1,13},{2,14},{3,15},{16,28},{17,29},{18,30},{19,31}} | collective-permute-start | bytes 786440 | tf_op jit(solution)/shard_map/ppermute | solution.py:198
  60.7 131.5 %copy-start = (bf16[512,256]{1,0:T(8,128)(2,1)}, bf16[512,256]{1,0:T(8,128)(2,1)S(1)}, u32[]{:S(2)}) copy-start(bf16[512,256]{1,0:T(8,128)(2,1)S(1)} %collective-permute-done.2.refs_2_) | copy-start | bytes 786436
  60.7 43.8 %collective-permute-start.8 = (bf16[512,256]{1,0:T(8,128)(2,1)}, bf16[512,256]{1,0:T(8,128)(2,1)S(1)}, u32[]{:S(2)}, u32[]{:S(2)}) collective-permute-start(bf16[512,256]{1,0:T(8,128)(2,1)} %get-tuple-element.12.own_ref), channel_id=1, source_target_pairs={{0,8},{1,9},{2,10},{3,11},{4,12},{5,13},{6,14},{7,15},{16,24},{17,... | collective-permute-start | bytes 786440 | tf_op jit(solution)/shard_map/ppermute | solution.py:198
  71.9 120.3 %copy-start.1 = (bf16[512,256]{1,0:T(8,128)(2,1)}, bf16[512,256]{1,0:T(8,128)(2,1)S(1)}, u32[]{:S(2)}) copy-start(bf16[512,256]{1,0:T(8,128)(2,1)S(1)} %collective-permute-done.1.refs_1_) | copy-start | bytes 786436
  71.9 33.8 %collective-permute-start.7 = (bf16[512,256]{1,0:T(8,128)(2,1)}, bf16[512,256]{1,0:T(8,128)(2,1)S(1)}, u32[]{:S(2)}, u32[]{:S(2)}) collective-permute-start(bf16[512,256]{1,0:T(8,128)(2,1)} %get-tuple-element.12.own_ref), channel_id=1, source_target_pairs={{0,4},{1,5},{2,6},{3,7},{4,8},{5,9},{6,10},{7,11},{8,12},{9,13},{1... | collective-permute-start | bytes 786440 | tf_op jit(solution)/shard_map/ppermute | solution.py:198
  73.2 119.0 %copy-start.2 = (bf16[512,256]{1,0:T(8,128)(2,1)}, bf16[512,256]{1,0:T(8,128)(2,1)S(1)}, u32[]{:S(2)}) copy-start(bf16[512,256]{1,0:T(8,128)(2,1)S(1)} %collective-permute-done.refs_0_) | copy-start | bytes 786436
  73.2 36.0 %collective-permute-start.17 = (bf16[512,256]{1,0:T(8,128)(2,1)}, bf16[512,256]{1,0:T(8,128)(2,1)S(1)}, u32[]{:S(2)}, u32[]{:S(2)}) collective-permute-start(bf16[512,256]{1,0:T(8,128)(2,1)} %get-tuple-element.13.own_ref), channel_id=1, source_target_pairs={{0,2},{1,3},{4,6},{5,7},{8,10},{9,11},{12,14},{13,15},{16,18},{17,... | collective-permute-start | bytes 786440 | tf_op jit(solution)/shard_map/ppermute | solution.py:205
  76.7 115.5 %copy-start.3 = (bf16[512,256]{1,0:T(8,128)(2,1)}, bf16[512,256]{1,0:T(8,128)(2,1)S(1)}, u32[]{:S(2)}) copy-start(bf16[512,256]{1,0:T(8,128)(2,1)S(1)} %collective-permute-done.10.refs_3_) | copy-start | bytes 786436
  76.7 33.9 %collective-permute-start.16 = (bf16[512,256]{1,0:T(8,128)(2,1)}, bf16[512,256]{1,0:T(8,128)(2,1)S(1)}, u32[]{:S(2)}, u32[]{:S(2)}) collective-permute-start(bf16[512,256]{1,0:T(8,128)(2,1)} %get-tuple-element.13.own_ref), channel_id=1, source_target_pairs={{0,12},{1,13},{2,14},{3,15},{16,28},{17,29},{18,30},{19,31}} | collective-permute-start | bytes 786440 | tf_op jit(solution)/shard_map/ppermute | solution.py:198
  78.0 114.2 %copy-start.4 = (bf16[512,256]{1,0:T(8,128)(2,1)}, bf16[512,256]{1,0:T(8,128)(2,1)S(1)}, u32[]{:S(2)}) copy-start(bf16[512,256]{1,0:T(8,128)(2,1)S(1)} %collective-permute-done.9.refs_2_) | copy-start | bytes 786436
  78.0 48.6 %collective-permute-start.15 = (bf16[512,256]{1,0:T(8,128)(2,1)}, bf16[512,256]{1,0:T(8,128)(2,1)S(1)}, u32[]{:S(2)}, u32[]{:S(2)}) collective-permute-start(bf16[512,256]{1,0:T(8,128)(2,1)} %get-tuple-element.13.own_ref), channel_id=1, source_target_pairs={{0,8},{1,9},{2,10},{3,11},{4,12},{5,13},{6,14},{7,15},{16,24},{17,... | collective-permute-start | bytes 786440 | tf_op jit(solution)/shard_map/ppermute | solution.py:198
  104.4 87.8 %copy-start.5 = (bf16[512,256]{1,0:T(8,128)(2,1)}, bf16[512,256]{1,0:T(8,128)(2,1)S(1)}, u32[]{:S(2)}) copy-start(bf16[512,256]{1,0:T(8,128)(2,1)S(1)} %collective-permute-done.8.refs_1_) | copy-start | bytes 786436
  104.4 23.5 %collective-permute-start.14 = (bf16[512,256]{1,0:T(8,128)(2,1)}, bf16[512,256]{1,0:T(8,128)(2,1)S(1)}, u32[]{:S(2)}, u32[]{:S(2)}) collective-permute-start(bf16[512,256]{1,0:T(8,128)(2,1)} %get-tuple-element.13.own_ref), channel_id=1, source_target_pairs={{0,4},{1,5},{2,6},{3,7},{4,8},{5,9},{6,10},{7,11},{8,12},{9,13},{1... | collective-permute-start | bytes 786440 | tf_op jit(solution)/shard_map/ppermute | solution.py:198
  105.7 86.5 %copy-start.6 = (bf16[512,256]{1,0:T(8,128)(2,1)}, bf16[512,256]{1,0:T(8,128)(2,1)S(1)}, u32[]{:S(2)}) copy-start(bf16[512,256]{1,0:T(8,128)(2,1)S(1)} %collective-permute-done.7.refs_0_) | copy-start | bytes 786436
  105.8 25.9 %collective-permute-start.24 = (bf16[512,256]{1,0:T(8,128)(2,1)S(1)}, bf16[512,256]{1,0:T(8,128)(2,1)S(1)}, u32[]{:S(2)}, u32[]{:S(2)}) collective-permute-start(bf16[512,256]{1,0:T(8,128)(2,1)S(1)} %copy-done.19), channel_id=1, source_target_pairs={{0,2},{1,3},{4,6},{5,7},{8,10},{9,11},{12,14},{13,15},{16,18},{17,... | collective-permute-start | bytes 786440 | tf_op jit(solution)/shard_map/ppermute | solution.py:205
  109.2 83.0 %copy-start.7 = (bf16[512,256]{1,0:T(8,128)(2,1)}, bf16[512,256]{1,0:T(8,128)(2,1)S(1)}, u32[]{:S(2)}) copy-start(bf16[512,256]{1,0:T(8,128)(2,1)S(1)} %collective-permute-done.17.refs_3_) | copy-start | bytes 786436
  109.2 24.6 %collective-permute-start.23 = (bf16[512,256]{1,0:T(8,128)(2,1)S(1)}, bf16[512,256]{1,0:T(8,128)(2,1)}, u32[]{:S(2)}, u32[]{:S(2)}) collective-permute-start(bf16[512,256]{1,0:T(8,128)(2,1)S(1)} %copy-done.19), channel_id=1, source_target_pairs={{0,12},{1,13},{2,14},{3,15},{16,28},{17,29},{18,30},{19,31}} | collective-permute-start | bytes 786440 | tf_op jit(solution)/shard_map/ppermute | solution.py:198
  110.5 81.7 %copy-start.8 = (bf16[512,256]{1,0:T(8,128)(2,1)}, bf16[512,256]{1,0:T(8,128)(2,1)S(1)}, u32[]{:S(2)}) copy-start(bf16[512,256]{1,0:T(8,128)(2,1)S(1)} %collective-permute-done.16.refs_2_) | copy-start | bytes 786436
  110.6 27.8 %collective-permute-start.22 = (bf16[512,256]{1,0:T(8,128)(2,1)S(1)}, bf16[512,256]{1,0:T(8,128)(2,1)}, u32[]{:S(2)}, u32[]{:S(2)}) collective-permute-start(bf16[512,256]{1,0:T(8,128)(2,1)S(1)} %copy-done.19), channel_id=1, source_target_pairs={{0,8},{1,9},{2,10},{3,11},{4,12},{5,13},{6,14},{7,15},{16,24},{17,... | collective-permute-start | bytes 786440 | tf_op jit(solution)/shard_map/ppermute | solution.py:198
  126.6 65.6 %copy-start.9 = (bf16[512,256]{1,0:T(8,128)(2,1)}, bf16[512,256]{1,0:T(8,128)(2,1)S(1)}, u32[]{:S(2)}) copy-start(bf16[512,256]{1,0:T(8,128)(2,1)S(1)} %collective-permute-done.15.refs_1_) | copy-start | bytes 786436
  126.6 15.5 %collective-permute-start.21 = (bf16[512,256]{1,0:T(8,128)(2,1)S(1)}, bf16[512,256]{1,0:T(8,128)(2,1)}, u32[]{:S(2)}, u32[]{:S(2)}) collective-permute-start(bf16[512,256]{1,0:T(8,128)(2,1)S(1)} %copy-done.19), channel_id=1, source_target_pairs={{0,4},{1,5},{2,6},{3,7},{4,8},{5,9},{6,10},{7,11},{8,12},{9,13},{1... | collective-permute-start | bytes 786440 | tf_op jit(solution)/shard_map/ppermute | solution.py:198
  127.9 64.4 %copy-start.10 = (bf16[512,256]{1,0:T(8,128)(2,1)}, bf16[512,256]{1,0:T(8,128)(2,1)S(1)}, u32[]{:S(2)}) copy-start(bf16[512,256]{1,0:T(8,128)(2,1)S(1)} %collective-permute-done.14.refs_0_) | copy-start | bytes 786436
  127.9 18.2 %collective-permute-start.13 = (bf16[512,256]{1,0:T(8,128)(2,1)S(1)}, bf16[512,256]{1,0:T(8,128)(2,1)S(1)}, u32[]{:S(2)}, u32[]{:S(2)}) collective-permute-start(bf16[512,256]{1,0:T(8,128)(2,1)S(1)} %collective-permute-done.9.refs_2_), channel_id=1, source_target_pairs={{12,14},{13,15},{14,12},{15,13},{28,30},{29,31},{30,28},{31,29}} | collective-permute-start | bytes 786440 | tf_op jit(solution)/shard_map/ppermute | solution.py:208
  131.7 28.6 %copy-start.20 = (bf16[512,256]{1,0:T(8,128)(2,1)}, bf16[512,256]{1,0:T(8,128)(2,1)S(1)}, u32[]{:S(2)}) copy-start(bf16[512,256]{1,0:T(8,128)(2,1)S(1)} %collective-permute-done.24.refs_3_) | copy-start | bytes 786436
  131.7 16.4 %collective-permute-start.12 = (bf16[512,256]{1,0:T(8,128)(2,1)S(1)}, bf16[512,256]{1,0:T(8,128)(2,1)S(1)}, u32[]{:S(2)}, u32[]{:S(2)}) collective-permute-start(bf16[512,256]{1,0:T(8,128)(2,1)S(1)} %collective-permute-done.8.refs_1_), channel_id=1, source_target_pairs={{8,10},{9,11},{10,8},{11,9},{12,14},{13,15},{14,12},{15,13},{24,26... | collective-permute-start | bytes 786440 | tf_op jit(solution)/shard_map/ppermute | solution.py:208
  133.8 18.2 %collective-permute-start.20 = (bf16[512,256]{1,0:T(8,128)(2,1)S(1)}, bf16[512,256]{1,0:T(8,128)(2,1)S(1)}, u32[]{:S(2)}, u32[]{:S(2)}) collective-permute-start(bf16[512,256]{1,0:T(8,128)(2,1)S(1)} %collective-permute-done.16.refs_2_), channel_id=1, source_target_pairs={{12,14},{13,15},{14,12},{15,13},{28,30},{29,31},{30,28},{31,29}} | collective-permute-start | bytes 786440 | tf_op jit(solution)/shard_map/ppermute | solution.py:208
  138.3 17.5 %collective-permute-start.19 = (bf16[512,256]{1,0:T(8,128)(2,1)S(1)}, bf16[512,256]{1,0:T(8,128)(2,1)S(1)}, u32[]{:S(2)}, u32[]{:S(2)}) collective-permute-start(bf16[512,256]{1,0:T(8,128)(2,1)S(1)} %collective-permute-done.15.refs_1_), channel_id=1, source_target_pairs={{8,10},{9,11},{10,8},{11,9},{12,14},{13,15},{14,12},{15,13},{24,26... | collective-permute-start | bytes 786440 | tf_op jit(solution)/shard_map/ppermute | solution.py:208
  142.2 19.4 %collective-permute-start.18 = (bf16[512,256]{1,0:T(8,128)(2,1)S(1)}, bf16[512,256]{1,0:T(8,128)(2,1)}, u32[]{:S(2)}, u32[]{:S(2)}) collective-permute-start(bf16[512,256]{1,0:T(8,128)(2,1)S(1)} %collective-permute-done.14.refs_0_), channel_id=1, source_target_pairs={{4,6},{5,7},{6,4},{7,5},{8,10},{9,11},{10,8},{11,9},{12,14},{13,15... | collective-permute-start | bytes 786440 | tf_op jit(solution)/shard_map/ppermute | solution.py:208
  146.1 46.1 %copy-start.11 = (bf16[512,256]{1,0:T(8,128)(2,1)}, bf16[512,256]{1,0:T(8,128)(2,1)S(1)}, u32[]{:S(2)}) copy-start(bf16[512,256]{1,0:T(8,128)(2,1)S(1)} %collective-permute-done.13.refs_6_) | copy-start | bytes 786436
  146.1 21.0 %collective-permute-start.27 = (bf16[512,256]{1,0:T(8,128)(2,1)}, bf16[512,256]{1,0:T(8,128)(2,1)}, u32[]{:S(2)}, u32[]{:S(2)}) collective-permute-start(bf16[512,256]{1,0:T(8,128)(2,1)} %collective-permute-done.23.refs_2_), channel_id=1, source_target_pairs={{12,14},{13,15},{14,12},{15,13},{28,30},{29,31},{30,28},{31,29}} | collective-permute-start | bytes 786440 | tf_op jit(solution)/shard_map/ppermute | solution.py:208
  148.1 44.2 %copy-start.12 = (bf16[512,256]{1,0:T(8,128)(2,1)}, bf16[512,256]{1,0:T(8,128)(2,1)S(1)}, u32[]{:S(2)}) copy-start(bf16[512,256]{1,0:T(8,128)(2,1)S(1)} %collective-permute-done.12.refs_5_) | copy-start | bytes 786436
  148.1 24.7 %collective-permute-start.26 = (bf16[512,256]{1,0:T(8,128)(2,1)}, bf16[512,256]{1,0:T(8,128)(2,1)}, u32[]{:S(2)}, u32[]{:S(2)}) collective-permute-start(bf16[512,256]{1,0:T(8,128)(2,1)} %collective-permute-done.22.refs_1_), channel_id=1, source_target_pairs={{8,10},{9,11},{10,8},{11,9},{12,14},{13,15},{14,12},{15,13},{24,26... | collective-permute-start | bytes 786440 | tf_op jit(solution)/shard_map/ppermute | solution.py:208
  152.0 3.8 %copy-start.13 = (bf16[512,256]{1,0:T(8,128)(2,1)}, bf16[512,256]{1,0:T(8,128)(2,1)S(1)}, u32[]{:S(2)}) copy-start(bf16[512,256]{1,0:T(8,128)(2,1)S(1)} %collective-permute-done.20.refs_6_) | copy-start | bytes 786436
  152.0 26.4 %collective-permute-start.25 = (bf16[512,256]{1,0:T(8,128)(2,1)}, bf16[512,256]{1,0:T(8,128)(2,1)}, u32[]{:S(2)}, u32[]{:S(2)}) collective-permute-start(bf16[512,256]{1,0:T(8,128)(2,1)} %collective-permute-done.21.refs_0_), channel_id=1, source_target_pairs={{4,6},{5,7},{6,4},{7,5},{8,10},{9,11},{10,8},{11,9},{12,14},{13,15... | collective-permute-start | bytes 786440 | tf_op jit(solution)/shard_map/ppermute | solution.py:208
  155.9 0.7 copy-start.14
  156.6 45.7 %collective-permute-start.11 = (bf16[512,256]{1,0:T(8,128)(2,1)S(1)}, bf16[512,256]{1,0:T(8,128)(2,1)}, u32[]{:S(2)}, u32[]{:S(2)}) collective-permute-start(bf16[512,256]{1,0:T(8,128)(2,1)S(1)} %collective-permute-done.7.refs_0_), channel_id=1, source_target_pairs={{4,6},{5,7},{6,4},{7,5},{8,10},{9,11},{10,8},{11,9},{12,14},{13,15... | collective-permute-start | bytes 786440 | tf_op jit(solution)/shard_map/ppermute | solution.py:208
  161.6 50.7 %collective-permute-start.3 = (bf16[512,256]{1,0:T(8,128)(2,1)}, bf16[512,256]{1,0:T(8,128)(2,1)S(1)}, u32[]{:S(2)}, u32[]{:S(2)}) collective-permute-start(bf16[512,256]{1,0:T(8,128)(2,1)} %get-tuple-element.11.own_ref), channel_id=1, source_target_pairs={{0,2},{1,3},{4,6},{5,7},{8,10},{9,11},{12,14},{13,15},{16,18},{17,... | collective-permute-start | bytes 786440 | tf_op jit(solution)/shard_map/ppermute | solution.py:205
  167.2 45.1 %collective-permute-start.6 = (bf16[512,256]{1,0:T(8,128)(2,1)S(1)}, bf16[512,256]{1,0:T(8,128)(2,1)S(1)}, u32[]{:S(2)}, u32[]{:S(2)}) collective-permute-start(bf16[512,256]{1,0:T(8,128)(2,1)S(1)} %collective-permute-done.2.refs_2_), channel_id=1, source_target_pairs={{12,14},{13,15},{14,12},{15,13},{28,30},{29,31},{30,28},{31,29}} | collective-permute-start | bytes 786440 | tf_op jit(solution)/shard_map/ppermute | solution.py:208
  172.8 39.5 %collective-permute-start.5 = (bf16[512,256]{1,0:T(8,128)(2,1)S(1)}, bf16[512,256]{1,0:T(8,128)(2,1)S(1)}, u32[]{:S(2)}, u32[]{:S(2)}) collective-permute-start(bf16[512,256]{1,0:T(8,128)(2,1)S(1)} %collective-permute-done.1.refs_1_), channel_id=1, source_target_pairs={{8,10},{9,11},{10,8},{11,9},{12,14},{13,15},{14,12},{15,13},{24,26... | collective-permute-start | bytes 786440 | tf_op jit(solution)/shard_map/ppermute | solution.py:208
  178.4 33.9 %collective-permute-start.4 = (bf16[512,256]{1,0:T(8,128)(2,1)S(1)}, bf16[512,256]{1,0:T(8,128)(2,1)S(1)}, u32[]{:S(2)}, u32[]{:S(2)}) collective-permute-start(bf16[512,256]{1,0:T(8,128)(2,1)S(1)} %collective-permute-done.refs_0_), channel_id=1, source_target_pairs={{4,6},{5,7},{6,4},{7,5},{8,10},{9,11},{10,8},{11,9},{12,14},{13,15... | collective-permute-start | bytes 786440 | tf_op jit(solution)/shard_map/ppermute | solution.py:208
  212.3 0.8 copy-start.16
  212.3 0.9 copy-start.17
  (2 other events, 1.4 us)

commit v2 on v1

v2 whole, which is shorter than its diff:
```python
import functools
import jax
import jax.numpy as jnp
from jax import lax
from jax.experimental import pallas as pl
from jax.experimental.pallas import tpu as pltpu
from jax.sharding import PartitionSpec as P

HEAD_DIM = 128
EPS = 1e-05
LOG2E = 1.4426950408889634
MASKED = -1e30
MIB = 1024 * 1024
CHUNKS = 4
UNITS = 2


def norm_project_kernel(x_ref, gain_ref, key_ref, value_ref, normed_ref, kv_ref, x_scr, sq_scr, acc_scr):
    step = pl.program_id(0)
    rows, chunk = x_ref.shape
    features = chunk * CHUNKS
    width = key_ref.shape[1]
    lanes = 128

    @pl.when(step < CHUNKS)
    def _():
        acc = jnp.zeros((rows, lanes), jnp.float32)
        for c in range(chunk // lanes):
            x = x_ref[:, c * lanes : (c + 1) * lanes].astype(jnp.float32)
            acc += x * x
        x_scr[step] = x_ref[...]
        sq_scr[...] = jnp.where(step == 0, acc, sq_scr[...] + acc)

    @pl.when(step == CHUNKS)
    def _():
        mean_sq = jnp.sum(sq_scr[...], axis=-1, keepdims=True) / features
        sq_scr[...] = jnp.broadcast_to(lax.rsqrt(mean_sq + EPS), sq_scr.shape)

    @pl.when(step >= CHUNKS)
    def _():
        index = step - CHUNKS
        for c in range(chunk // lanes):
            cols = slice(c * lanes, (c + 1) * lanes)
            x = x_scr[index, :, cols].astype(jnp.float32)
            normed_ref[:, cols] = (x * sq_scr[...] * gain_ref[:, cols]).astype(jnp.bfloat16)
        normed = normed_ref[...]
        for part, weight in enumerate((key_ref, value_ref)):
            cols = slice(part * width, (part + 1) * width)
            term = jnp.dot(normed, weight[...], preferred_element_type=jnp.float32)
            total = jnp.where(index == 0, term, acc_scr[:, cols] + term)
            acc_scr[:, cols] = total

    @pl.when(step == 2 * CHUNKS - 1)
    def _():
        kv_ref[...] = acc_scr[...].astype(jnp.bfloat16)


def norm_project(hidden, gain, key_weight, value_weight):
    rows, features = hidden.shape
    chunk = features // CHUNKS
    width = key_weight.shape[1] // UNITS
    second = lambda i: jnp.maximum(i - CHUNKS, 0)
    weight = pl.BlockSpec((chunk, width), lambda i: (second(i), 0))
    return pl.pallas_call(
        norm_project_kernel,
        grid=(2 * CHUNKS,),
        in_specs=[
            pl.BlockSpec((rows, chunk), lambda i: (0, jnp.minimum(i, CHUNKS - 1))),
            pl.BlockSpec((1, chunk), lambda i: (0, second(i))),
            weight,
            weight,
        ],
        out_specs=[
            pl.BlockSpec((rows, chunk), lambda i: (0, second(i))),
            pl.BlockSpec((rows, 2 * width), lambda i: (0, 0)),
        ],
        out_shape=[
            jax.ShapeDtypeStruct((rows, features), jnp.bfloat16),
            jax.ShapeDtypeStruct((rows, 2 * width), jnp.bfloat16),
        ],
        scratch_shapes=[
            pltpu.VMEM((CHUNKS, rows, chunk), jnp.bfloat16),
            pltpu.VMEM((rows, 128), jnp.float32),
            pltpu.VMEM((rows, 2 * width), jnp.float32),
        ],
        compiler_params=pltpu.CompilerParams(vmem_limit_bytes=36 * MIB),
        cost_estimate=pl.CostEstimate(
            flops=4 * rows * features * width, bytes_accessed=24 * MIB, transcendentals=0
        ),
        name="norm_project",
    )(hidden, gain.reshape(1, features), key_weight, value_weight)


def project_kernel(normed_ref, key_ref, value_ref, kv_ref, acc_scr):
    step = pl.program_id(0)
    width = key_ref.shape[1]
    normed = normed_ref[...]
    for part, weight in enumerate((key_ref, value_ref)):
        cols = slice(part * width, (part + 1) * width)
        term = jnp.dot(normed, weight[...], preferred_element_type=jnp.float32)
        acc_scr[:, cols] = jnp.where(step == 0, term, acc_scr[:, cols] + term)

    @pl.when(step == CHUNKS - 1)
    def _():
        kv_ref[...] = acc_scr[...].astype(jnp.bfloat16)


def project(normed, key_weight, value_weight, unit):
    rows, features = normed.shape
    chunk = features // CHUNKS
    width = key_weight.shape[1] // UNITS
    weight = pl.BlockSpec((chunk, width), lambda i: (i, unit))
    return pl.pallas_call(
        project_kernel,
        grid=(CHUNKS,),
        in_specs=[pl.BlockSpec((rows, chunk), lambda i: (0, i)), weight, weight],
        out_specs=pl.BlockSpec((rows, 2 * width), lambda i: (0, 0)),
        out_shape=jax.ShapeDtypeStruct((rows, 2 * width), jnp.bfloat16),
        scratch_shapes=[pltpu.VMEM((rows, 2 * width), jnp.float32)],
        compiler_params=pltpu.CompilerParams(vmem_limit_bytes=24 * MIB),
        cost_estimate=pl.CostEstimate(
            flops=4 * rows * features * width, bytes_accessed=16 * MIB, transcendentals=0
        ),
        name="project",
    )(normed, key_weight, value_weight)


def attention_kernel(block, kv_heads, near, slot_ref, cut_ref, odd_ref, q_ref, own_ref, *refs):
    out_ref = refs[-1]
    straight, crossed = refs[:near], refs[near : 2 * near + 1]
    depth = slot_ref.shape[1]
    here = pl.program_id(0)
    odd = odd_ref[0] == 1
    per_group = q_ref.shape[1] // HEAD_DIM // kv_heads
    tile = 256
    together = tile // block
    scale = HEAD_DIM**-0.5 * LOG2E
    pieces = []
    for k in range(depth):
        rows = pl.ds(pl.multiple_of(slot_ref[here, k] * block, block), block)
        if k % 2 == 1:
            pieces.append(straight[k // 2][rows, :])
        else:
            low = crossed[k // 2][rows, :]
            high = crossed[min(k // 2 + 1, near)][rows, :]
            pieces.append(jnp.where(odd, low, high))
    pieces.append(own_ref[pl.ds(pl.multiple_of(here * block, block), block), :])
    every = jnp.concatenate(pieces, axis=0)
    token = lax.broadcasted_iota(jnp.int32, (block, 128), 0)
    lane = lax.broadcasted_iota(jnp.int32, (block, 128), 1)
    bias = []
    for k in range(depth):
        bias.append(jnp.where(token < cut_ref[here, k], 0.0, MASKED))
    bias.append(jnp.where(token <= lane % block, 0.0, MASKED))
    bias = [jnp.concatenate([b] * (tile // 128), axis=1) for b in bias]
    for head in range(kv_heads):
        keys = every[:, head * HEAD_DIM : (head + 1) * HEAD_DIM]
        values = every[:, (kv_heads + head) * HEAD_DIM : (kv_heads + head + 1) * HEAD_DIM]
        flipped = jnp.concatenate(
            [values.T, jnp.ones((16, values.shape[0]), jnp.bfloat16)], axis=0
        )
        for first in range(head * per_group, (head + 1) * per_group, together):
            queries = jnp.concatenate(
                [
                    q_ref[:, r * HEAD_DIM : (r + 1) * HEAD_DIM]
                    for r in range(first, first + together)
                ],
                axis=0,
            )
            scores = lax.dot_general(
                keys, queries, (((1,), (1,)), ((), ())), preferred_element_type=jnp.float32
            )
            parts = [scores[k * block : (k + 1) * block] + bias[k] for k in range(depth + 1)]
            peak = functools.reduce(jnp.maximum, parts)
            peak = jnp.max(peak, axis=0, keepdims=True)
            weights = jnp.concatenate(
                [jnp.exp2((part - peak) * scale).astype(jnp.bfloat16) for part in parts], axis=0
            )
            both = jnp.dot(flipped, weights, preferred_element_type=jnp.float32)
            context = both[:HEAD_DIM] * (1.0 / both[HEAD_DIM : HEAD_DIM + 1])
            context = context.T.astype(jnp.bfloat16)
            for r in range(together):
                cols = slice((first + r) * HEAD_DIM, (first + r + 1) * HEAD_DIM)
                out_ref[:, cols] = context[r * block : (r + 1) * block]


def attention(slots, cuts, odd, queries, own, straight, crossed, unit, previous):
    rows, features = queries.shape
    blocks, depth = slots.shape
    block = rows // blocks
    wide = features // UNITS
    near = len(straight)
    kv_heads = own.shape[1] // (2 * HEAD_DIM)
    whole = pl.BlockSpec(own.shape, lambda b, *_: (0, 0), pipeline_mode=pl.Buffered(1))
    part = pl.BlockSpec((block, wide), lambda b, *_: (b, unit))
    operands = [slots, cuts, odd, queries, own, *straight, *crossed]
    in_specs = [part] + [whole] * (1 + near + len(crossed))
    aliases = {}
    if previous is not None:
        aliases = {len(operands): 0}
        operands.append(previous)
        in_specs.append(pl.BlockSpec(memory_space=pl.ANY))
    return pl.pallas_call(
        functools.partial(attention_kernel, block, kv_heads, near),
        grid_spec=pltpu.PrefetchScalarGridSpec(
            num_scalar_prefetch=3, grid=(blocks,), in_specs=in_specs, out_specs=part
        ),
        out_shape=jax.ShapeDtypeStruct((rows, features), jnp.bfloat16),
        input_output_aliases=aliases,
        compiler_params=pltpu.CompilerParams(vmem_limit_bytes=24 * MIB),
        cost_estimate=pl.CostEstimate(
            flops=4 * rows * wide * (depth + 1) * block,
            bytes_accessed=8 * MIB,
            transcendentals=rows * wide // HEAD_DIM * (depth + 1) * block,
        ),
        name="attention",
    )(*operands)


def shards(hidden, queries, norm_gain, key_weight, value_weight, anc_ids, anc_cut):
    blocks, depth = anc_ids.shape
    levels = depth + 1
    size = lax.axis_size("node")
    chains = size // levels
    near = depth // 2
    half = [index // chains // 2 for index in range(size)]
    even = [index // chains % 2 == 0 for index in range(size)]
    other = [index + chains if even[index] else index - chains for index in range(size)]
    odd = (lax.axis_index("node") // chains % 2).astype(jnp.int32).reshape(1)
    slots = jnp.where(anc_ids >= 0, anc_ids % blocks, 0)

    def shifted(array, distance, least=0):
        shift = 2 * distance * chains
        pairs = [(i, i + shift) for i in range(size) if i + shift < size and half[i] >= least]
        return lax.ppermute(array, "node", pairs)

    normed, first = norm_project(hidden, norm_gain, key_weight, value_weight)
    own = [first] + [project(normed, key_weight, value_weight, unit) for unit in range(1, UNITS)]
    result = None
    for unit in range(UNITS):
        piece = own[unit]
        straight = []
        for s in range(1, near + 1):
            straight.append(shifted(piece, s) if s <= 2 else shifted(straight[-1], 1, s - 1))
        crossed = [lax.ppermute(piece, "node", [(i, other[i]) for i in range(size) if even[i]])]
        for s in range(1, near + 1):
            pairs = [(i, other[i]) for i in range(size) if half[i] >= s]
            crossed.append(lax.ppermute(straight[s - 1], "node", pairs))
        result = attention(slots, anc_cut, odd, queries, piece, straight, crossed, unit, result)
    return result


def solution(mesh):
    placed = (
        P(("groups", "node"), None),
        P(("groups", "node"), None),
        P(),
        P(),
        P(),
        P(("groups", "node"), None),
        P(("groups", "node"), None),
    )
    return jax.shard_map(
        shards, mesh=mesh, in_specs=placed, out_specs=P(("groups", "node"), None), check_vma=False
    )
```

time: 225 us -> 171 us (0.76)
  Pallas kernels: 87.4 us -> 51.6 us
  starting transfers between devices: 69.4 us -> 33.9 us
  local copies, waits for them, and re-layouts: 2.32 us -> 23.7 us
  waiting for transfers between devices: 63.6 us -> 59.7 us
    pallas_call x6 -> x4, Pallas kernels: 87.4 us -> 51.6 us  [the longest x2 34.8 us: attention(): pl.pallas_call(functools.partial(attention_kernel, block, kv_heads, near)...]
    unnamed x44 -> x34, local copies, waits for them, and re-layouts: 2.32 us -> 23.7 us
    ppermute x12 -> x6, starting transfers between devices: 39.8 us -> 19.5 us  [shards(): crossed.append(lax.ppermute(straight[s - 1], 'node', pairs))]
    ppermute x12 -> x6, waiting for transfers between devices: 55.6 us -> 44.8 us  [shifted(): return lax.ppermute(array, 'node', pairs)]
    ppermute x12 -> x6, starting transfers between devices: 15.4 us -> 7.72 us  [shifted(): return lax.ppermute(array, 'node', pairs)]
    ppermute x4 -> x2, starting transfers between devices: 14.1 us -> 6.69 us  [shards(): lax.ppermute(piece, 'node', [(i, other[i]) for i in range(size) if even[i]])]
    ppermute x12 -> x6, waiting for transfers between devices: 7.98 us -> 14.9 us  [shards(): crossed.append(lax.ppermute(straight[s - 1], 'node', pairs))]
  transfers between devices with their start and end apart: 28 -> 14, of which waited for: 11 -> 8; matrix products, arithmetic and copies ran while one was open for 0% -> 0% of each run, Pallas kernels for 13% -> 14%
where the time goes in v2:
time: 171 us; the launch traced here: 169 us
  waiting for transfers between devices  59.7 us (35%)
  Pallas kernels  51.6 us (30%)
  starting transfers between devices  33.9 us (20%)
  local copies, waits for them, and re-layouts  23.7 us (14%)
    ppermute x6, waiting for transfers between devices, shifted(): return lax.ppermute(array, 'node', pairs)  44.8 us
    pallas_call x2, Pallas kernels, attention(): pl.pallas_call(functools.partial(attention_kernel, block, kv_heads, near)...  34.8 us
    unnamed x34, local copies, waits for them, and re-layouts  23.7 us
    ppermute x6, starting transfers between devices, shards(): crossed.append(lax.ppermute(straight[s - 1], 'node', pairs))  19.5 us
    ppermute x6, waiting for transfers between devices, shards(): crossed.append(lax.ppermute(straight[s - 1], 'node', pairs))  14.9 us
    pallas_call x1, Pallas kernels, norm_project(): pl.pallas_call(norm_project_kernel, grid=(2 * CHUNKS,), in_specs=[pl.Bloc...  10.6 us
    ppermute x6, starting transfers between devices, shifted(): return lax.ppermute(array, 'node', pairs)  7.72 us
    ppermute x2, starting transfers between devices, shards(): lax.ppermute(piece, 'node', [(i, other[i]) for i in range(size) if even[i]])  6.69 us
  transfers between devices with their start and end apart: 14, of which 8 were waited for; matrix products, arithmetic and copies ran while one was open for 0% of the time, Pallas kernels for 14%

profile of v2, /device:TPU:24, one launch (start us, length us, event | category | flops | bytes accessed | tf_op | source)
XLA Modules:
  0.0 169.1 jit_solution(15565797489417301664)
XLA Ops:
  0.0 3.4 %copy-done.5 = bf16[512,8192]{1,0:T(8,128)(2,1)S(1)} copy-done((bf16[512,8192]{1,0:T(8,128)(2,1)S(1)}, bf16[512,8192]{1,0:T(8,128)(2,1)}, u32[]{:S(2)}) %copy-start.5) | copy-done | bytes 8388632
  3.4 0.8 copy-done.14
  4.1 10.6 %norm_project.1 = (bf16[512,8192]{1,0:T(8,128)(2,1)S(1)}, bf16[512,512]{1,0:T(8,128)(2,1)S(1)}) custom-call(bf16[512,8192]{1,0:T(8,128)(2,1)S(1)} %copy-done.5, f32[1,8192]{1,0:T(1,128)S(1)} %bitcast.2, bf16[8192,512]{1,0:T(8,128)(2,1)} %key_ref.3, bf16[8192,512]{1,0:T(8,128)(2,1)} %value_ref.3), custom_call_target="tpu_custom_call" | custom-call | flops 4294967296 | bytes 25165824 | tf_op jit(solution)/shard_map/norm_project/pallas_call | solution.py:64
  14.7 3.3 %copy-done.3 = bf16[512,8192]{1,0:T(8,128)(2,1)} copy-done((bf16[512,8192]{1,0:T(8,128)(2,1)}, bf16[512,8192]{1,0:T(8,128)(2,1)S(1)}, u32[]{:S(2)}) %copy-start.3) | copy-done | bytes 8388632
  18.0 1.3 collective-permute-start.8
  19.3 0.0 copy-start.1
  19.3 3.4 %copy-done.1 = bf16[8192,512]{1,0:T(8,128)(2,1)S(1)} copy-done((bf16[8192,512]{1,0:T(8,128)(2,1)S(1)}, bf16[8192,512]{1,0:T(8,128)(2,1)}, u32[]{:S(2)}) %copy-start.1) | copy-done | bytes 8388632
  22.7 3.4 %copy-done.4 = bf16[512,8192]{1,0:T(8,128)(2,1)S(1)} copy-done((bf16[512,8192]{1,0:T(8,128)(2,1)S(1)}, bf16[512,8192]{1,0:T(8,128)(2,1)}, u32[]{:S(2)}) %copy-start.4) | copy-done | bytes 8388632
  26.1 6.2 %project.1.own_ref = bf16[512,512]{1,0:T(8,128)(2,1)S(1)} custom-call(bf16[512,8192]{1,0:T(8,128)(2,1)S(1)} %copy-done.4, bf16[8192,512]{1,0:T(8,128)(2,1)S(1)} %copy-done, bf16[8192,512]{1,0:T(8,128)(2,1)S(1)} %copy-done.1), custom_call_target="tpu_custom_call" | custom-call | flops 4294967296 | bytes 16777216 | tf_op jit(solution)/shard_map/project/pallas_call | solution.py:113
  32.3 1.3 collective-permute-start.1
  33.6 1.3 collective-permute-start
  34.9 1.3 collective-permute-start.7
  36.2 20.8 %collective-permute-done.8.refs_1_ = bf16[512,512]{1,0:T(8,128)(2,1)S(1)} collective-permute-done((bf16[512,512]{1,0:T(8,128)(2,1)S(1)}, bf16[512,512]{1,0:T(8,128)(2,1)S(1)}, u32[]{:S(2)}, u32[]{:S(2)}) %collective-permute-start.8) | collective-permute-done | bytes 524320 | tf_op jit(solution)/shard_map/ppermute | solution.py:235
  57.0 1.3 collective-permute-start.9
  58.3 3.5 %collective-permute-start.10 = (bf16[512,512]{1,0:T(8,128)(2,1)S(1)}, bf16[512,512]{1,0:T(8,128)(2,1)S(1)}, u32[]{:S(2)}, u32[]{:S(2)}) collective-permute-start(bf16[512,512]{1,0:T(8,128)(2,1)S(1)} %get-tuple-element.8.own_ref), channel_id=1, source_target_pairs={{0,2},{1,3},{4,6},{5,7},{8,10},{9,11},{12,14},{13,15},{16,18},{17,... | collective-permute-start | bytes 1572872 | tf_op jit(solution)/shard_map/ppermute | solution.py:245
  61.8 6.4 %collective-permute-done.1.refs_1_ = bf16[512,512]{1,0:T(8,128)(2,1)S(1)} collective-permute-done((bf16[512,512]{1,0:T(8,128)(2,1)S(1)}, bf16[512,512]{1,0:T(8,128)(2,1)S(1)}, u32[]{:S(2)}, u32[]{:S(2)}) %collective-permute-start.1) | collective-permute-done | bytes 524320 | tf_op jit(solution)/shard_map/ppermute | solution.py:235
  68.2 1.3 collective-permute-start.2
  69.5 0.1 collective-permute-done.refs_0_
  69.6 3.4 %collective-permute-start.12 = (bf16[512,512]{1,0:T(8,128)(2,1)S(1)}, bf16[512,512]{1,0:T(8,128)(2,1)S(1)}, u32[]{:S(2)}, u32[]{:S(2)}) collective-permute-start(bf16[512,512]{1,0:T(8,128)(2,1)S(1)} %collective-permute-done.8.refs_1_), channel_id=1, source_target_pairs={{8,10},{9,11},{10,8},{11,9},{12,14},{13,15},{14,12},{15,13},{24,26... | collective-permute-start | bytes 1572872 | tf_op jit(solution)/shard_map/ppermute | solution.py:248
  73.0 7.8 %collective-permute-done.7.refs_0_ = bf16[512,512]{1,0:T(8,128)(2,1)S(1)} collective-permute-done((bf16[512,512]{1,0:T(8,128)(2,1)S(1)}, bf16[512,512]{1,0:T(8,128)(2,1)S(1)}, u32[]{:S(2)}, u32[]{:S(2)}) %collective-permute-start.7) | collective-permute-done | bytes 524320 | tf_op jit(solution)/shard_map/ppermute | solution.py:235
  80.8 3.4 %collective-permute-start.11 = (bf16[512,512]{1,0:T(8,128)(2,1)S(1)}, bf16[512,512]{1,0:T(8,128)(2,1)S(1)}, u32[]{:S(2)}, u32[]{:S(2)}) collective-permute-start(bf16[512,512]{1,0:T(8,128)(2,1)S(1)} %collective-permute-done.7.refs_0_), channel_id=1, source_target_pairs={{4,6},{5,7},{6,4},{7,5},{8,10},{9,11},{10,8},{11,9},{12,14},{13,15... | collective-permute-start | bytes 1572872 | tf_op jit(solution)/shard_map/ppermute | solution.py:248
  84.2 0.0 copy-start.6
  84.2 0.8 copy-done.6
  85.0 7.1 %collective-permute-done.9.refs_2_ = bf16[512,512]{1,0:T(8,128)(2,1)} collective-permute-done((bf16[512,512]{1,0:T(8,128)(2,1)S(1)}, bf16[512,512]{1,0:T(8,128)(2,1)}, u32[]{:S(2)}, u32[]{:S(2)}) %collective-permute-start.9) | collective-permute-done | bytes 524320 | tf_op jit(solution)/shard_map/ppermute | solution.py:235
  92.2 3.4 %collective-permute-start.13 = (bf16[512,512]{1,0:T(8,128)(2,1)}, bf16[512,512]{1,0:T(8,128)(2,1)}, u32[]{:S(2)}, u32[]{:S(2)}) collective-permute-start(bf16[512,512]{1,0:T(8,128)(2,1)} %collective-permute-done.9.refs_2_), channel_id=1, source_target_pairs={{12,14},{13,15},{14,12},{15,13},{28,30},{29,31},{30,28},{31,29}} | collective-permute-start | bytes 1572872 | tf_op jit(solution)/shard_map/ppermute | solution.py:248
  95.6 0.0 collective-permute-done.10.refs_3_
  95.6 0.8 copy-done.8
  96.4 3.2 %collective-permute-start.3 = (bf16[512,512]{1,0:T(8,128)(2,1)S(1)}, bf16[512,512]{1,0:T(8,128)(2,1)}, u32[]{:S(2)}, u32[]{:S(2)}) collective-permute-start(bf16[512,512]{1,0:T(8,128)(2,1)S(1)} %project.1.own_ref), channel_id=1, source_target_pairs={{0,2},{1,3},{4,6},{5,7},{8,10},{9,11},{12,14},{13,15},{16,18},{17,... | collective-permute-start | bytes 1572872 | tf_op jit(solution)/shard_map/ppermute | solution.py:245
  99.6 2.5 %collective-permute-done.2.refs_2_ = bf16[512,512]{1,0:T(8,128)(2,1)S(1)} collective-permute-done((bf16[512,512]{1,0:T(8,128)(2,1)S(1)}, bf16[512,512]{1,0:T(8,128)(2,1)S(1)}, u32[]{:S(2)}, u32[]{:S(2)}) %collective-permute-start.2) | collective-permute-done | bytes 524320 | tf_op jit(solution)/shard_map/ppermute | solution.py:235
  102.1 3.4 %collective-permute-start.5 = (bf16[512,512]{1,0:T(8,128)(2,1)S(1)}, bf16[512,512]{1,0:T(8,128)(2,1)}, u32[]{:S(2)}, u32[]{:S(2)}) collective-permute-start(bf16[512,512]{1,0:T(8,128)(2,1)S(1)} %collective-permute-done.1.refs_1_), channel_id=1, source_target_pairs={{8,10},{9,11},{10,8},{11,9},{12,14},{13,15},{14,12},{15,13},{24,26... | collective-permute-start | bytes 1572872 | tf_op jit(solution)/shard_map/ppermute | solution.py:248
  105.5 0.0 collective-permute-done.12.refs_5_
  105.6 0.8 copy-done.10
  106.4 2.4 %collective-permute-start.4 = (bf16[512,512]{1,0:T(8,128)(2,1)S(1)}, bf16[512,512]{1,0:T(8,128)(2,1)}, u32[]{:S(2)}, u32[]{:S(2)}) collective-permute-start(bf16[512,512]{1,0:T(8,128)(2,1)S(1)} %collective-permute-done.refs_0_), channel_id=1, source_target_pairs={{4,6},{5,7},{6,4},{7,5},{8,10},{9,11},{10,8},{11,9},{12,14},{13,15... | collective-permute-start | bytes 1572872 | tf_op jit(solution)/shard_map/ppermute | solution.py:248
  108.8 0.0 collective-permute-done.11.refs_4_
  108.8 0.8 copy-done.12
  109.6 3.4 %collective-permute-start.6 = (bf16[512,512]{1,0:T(8,128)(2,1)S(1)}, bf16[512,512]{1,0:T(8,128)(2,1)}, u32[]{:S(2)}, u32[]{:S(2)}) collective-permute-start(bf16[512,512]{1,0:T(8,128)(2,1)S(1)} %collective-permute-done.2.refs_2_), channel_id=1, source_target_pairs={{12,14},{13,15},{14,12},{15,13},{28,30},{29,31},{30,28},{31,29}} | collective-permute-start | bytes 1572872 | tf_op jit(solution)/shard_map/ppermute | solution.py:248
  113.1 0.0 collective-permute-done.13.refs_6_
  113.1 0.0 copy-start.2
  113.1 2.2 %copy-done.2 = bf16[512,4096]{1,0:T(8,128)(2,1)S(1)} copy-done((bf16[512,4096]{1,0:T(8,128)(2,1)S(1)}, bf16[512,4096]{1,0:T(8,128)(2,1)}, u32[]{:S(2)}) %copy-start.2) | copy-done | bytes 4194328
  115.3 1.0 copy-done.7
  116.3 1.0 copy-done.9
  117.4 1.0 copy-done.11
  118.4 1.0 copy-done.13
  119.5 17.2 %attention.2.refs_7_ = bf16[512,4096]{1,0:T(8,128)(2,1)} custom-call(s32[8,7]{1,0:T(8,128)S(1)} %fusion.1.slot_ref, s32[8,7]{1,0:T(8,128)S(1)} %copy-done.15, s32[1]{0:T(128)} %bitcast.odd_ref, bf16[512,4096]{1,0:T(8,128)(2,1)S(1)} %copy-done.2, bf16[512,512]{1,0:T(8,128)(2,1)S(1)} %get-tuple-element.8.own_ref, bf16[512,512]{1,0:T(8,128)(2,1)S(1)} %copy-done.7, ...), custom_call_target="tpu_custom_call" | custom-call | flops 2147483648 | bytes 8388608 | tf_op jit(solution)/shard_map/attention/pallas_call | solution.py:203
  136.7 0.0 collective-permute-done.3.refs_3_
  136.7 5.1 %collective-permute-done.4.refs_4_ = bf16[512,512]{1,0:T(8,128)(2,1)} collective-permute-done((bf16[512,512]{1,0:T(8,128)(2,1)S(1)}, bf16[512,512]{1,0:T(8,128)(2,1)}, u32[]{:S(2)}, u32[]{:S(2)}) %collective-permute-start.4) | collective-permute-done | bytes 524320 | tf_op jit(solution)/shard_map/ppermute | solution.py:248
  141.9 9.7 %collective-permute-done.6.refs_6_ = bf16[512,512]{1,0:T(8,128)(2,1)} collective-permute-done((bf16[512,512]{1,0:T(8,128)(2,1)S(1)}, bf16[512,512]{1,0:T(8,128)(2,1)}, u32[]{:S(2)}, u32[]{:S(2)}) %collective-permute-start.6) | collective-permute-done | bytes 524320 | tf_op jit(solution)/shard_map/ppermute | solution.py:248
  151.6 17.6 %attention.3 = bf16[512,4096]{1,0:T(8,128)(2,1)} custom-call(s32[8,7]{1,0:T(8,128)S(1)} %fusion.1.slot_ref, s32[8,7]{1,0:T(8,128)S(1)} %copy-done.15, s32[1]{0:T(128)} %bitcast.odd_ref, bf16[512,4096]{1,0:T(8,128)(2,1)S(1)} %copy-done.2, bf16[512,512]{1,0:T(8,128)(2,1)S(1)} %project.1.own_ref, ...), custom_call_target="tpu_custom_call", output_to_operand_aliasing={{}: (12, {})} | custom-call | flops 2147483648 | bytes 8388608 | tf_op jit(solution)/shard_map/attention/pallas_call | solution.py:203
  (19 shorter events, 0.0 us)
Async XLA Ops:
  0.0 3.4 %copy-start.5 = (bf16[512,8192]{1,0:T(8,128)(2,1)S(1)}, bf16[512,8192]{1,0:T(8,128)(2,1)}, u32[]{:S(2)}) copy-start(bf16[512,8192]{1,0:T(8,128)(2,1)} %x_ref.1) | copy-start | bytes 25165828
  3.4 0.8 copy-start.14
  4.1 15.2 %copy-start = (bf16[8192,512]{1,0:T(8,128)(2,1)S(1)}, bf16[8192,512]{1,0:T(8,128)(2,1)}, u32[]{:S(2)}) copy-start(bf16[8192,512]{1,0:T(8,128)(2,1)} %key_ref.3) | copy-start | bytes 25165828
  14.7 3.3 %copy-start.3 = (bf16[512,8192]{1,0:T(8,128)(2,1)}, bf16[512,8192]{1,0:T(8,128)(2,1)S(1)}, u32[]{:S(2)}) copy-start(bf16[512,8192]{1,0:T(8,128)(2,1)S(1)} %get-tuple-element.7.normed_ref) | copy-start | bytes 25165828
  18.0 39.0 %collective-permute-start.8 = (bf16[512,512]{1,0:T(8,128)(2,1)S(1)}, bf16[512,512]{1,0:T(8,128)(2,1)S(1)}, u32[]{:S(2)}, u32[]{:S(2)}) collective-permute-start(bf16[512,512]{1,0:T(8,128)(2,1)S(1)} %get-tuple-element.8.own_ref), channel_id=1, source_target_pairs={{0,8},{1,9},{2,10},{3,11},{4,12},{5,13},{6,14},{7,15},{16,24},{17,... | collective-permute-start | bytes 1572872 | tf_op jit(solution)/shard_map/ppermute | solution.py:235
  19.3 3.4 %copy-start.1 = (bf16[8192,512]{1,0:T(8,128)(2,1)S(1)}, bf16[8192,512]{1,0:T(8,128)(2,1)}, u32[]{:S(2)}) copy-start(bf16[8192,512]{1,0:T(8,128)(2,1)} %value_ref.3) | copy-start | bytes 25165828
  22.7 3.4 %copy-start.4 = (bf16[512,8192]{1,0:T(8,128)(2,1)S(1)}, bf16[512,8192]{1,0:T(8,128)(2,1)}, u32[]{:S(2)}) copy-start(bf16[512,8192]{1,0:T(8,128)(2,1)} %copy-done.3) | copy-start | bytes 25165828
  26.1 87.0 %copy-start.16 = (s32[8,7]{1,0:T(8,128)S(1)}, s32[8,7]{1,0:T(8,128)}, u32[]{:S(2)}) copy-start(s32[8,7]{1,0:T(8,128)} %param.12) | copy-start | bytes 676
  26.1 87.0 %copy-start.15 = (s32[8,7]{1,0:T(8,128)S(1)}, s32[8,7]{1,0:T(8,128)}, u32[]{:S(2)}) copy-start(s32[8,7]{1,0:T(8,128)} %cut_ref.3) | copy-start | bytes 676
  32.3 35.9 %collective-permute-start.1 = (bf16[512,512]{1,0:T(8,128)(2,1)S(1)}, bf16[512,512]{1,0:T(8,128)(2,1)S(1)}, u32[]{:S(2)}, u32[]{:S(2)}) collective-permute-start(bf16[512,512]{1,0:T(8,128)(2,1)S(1)} %project.1.own_ref), channel_id=1, source_target_pairs={{0,8},{1,9},{2,10},{3,11},{4,12},{5,13},{6,14},{7,15},{16,24},{17,... | collective-permute-start | bytes 1572872 | tf_op jit(solution)/shard_map/ppermute | solution.py:235
  33.6 36.0 %collective-permute-start = (bf16[512,512]{1,0:T(8,128)(2,1)S(1)}, bf16[512,512]{1,0:T(8,128)(2,1)S(1)}, u32[]{:S(2)}, u32[]{:S(2)}) collective-permute-start(bf16[512,512]{1,0:T(8,128)(2,1)S(1)} %project.1.own_ref), channel_id=1, source_target_pairs={{0,4},{1,5},{2,6},{3,7},{4,8},{5,9},{6,10},{7,11},{8,12},{9,13},{1... | collective-permute-start | bytes 1572872 | tf_op jit(solution)/shard_map/ppermute | solution.py:235
  34.9 45.9 %collective-permute-start.7 = (bf16[512,512]{1,0:T(8,128)(2,1)S(1)}, bf16[512,512]{1,0:T(8,128)(2,1)S(1)}, u32[]{:S(2)}, u32[]{:S(2)}) collective-permute-start(bf16[512,512]{1,0:T(8,128)(2,1)S(1)} %get-tuple-element.8.own_ref), channel_id=1, source_target_pairs={{0,4},{1,5},{2,6},{3,7},{4,8},{5,9},{6,10},{7,11},{8,12},{9,13},{1... | collective-permute-start | bytes 1572872 | tf_op jit(solution)/shard_map/ppermute | solution.py:235
  57.0 35.2 %collective-permute-start.9 = (bf16[512,512]{1,0:T(8,128)(2,1)S(1)}, bf16[512,512]{1,0:T(8,128)(2,1)}, u32[]{:S(2)}, u32[]{:S(2)}) collective-permute-start(bf16[512,512]{1,0:T(8,128)(2,1)S(1)} %collective-permute-done.8.refs_1_), channel_id=1, source_target_pairs={{8,12},{9,13},{10,14},{11,15},{24,28},{25,29},{26,30},{27,31}} | collective-permute-start | bytes 1572872 | tf_op jit(solution)/shard_map/ppermute | solution.py:235
  58.3 37.3 %collective-permute-start.10 = (bf16[512,512]{1,0:T(8,128)(2,1)S(1)}, bf16[512,512]{1,0:T(8,128)(2,1)S(1)}, u32[]{:S(2)}, u32[]{:S(2)}) collective-permute-start(bf16[512,512]{1,0:T(8,128)(2,1)S(1)} %get-tuple-element.8.own_ref), channel_id=1, source_target_pairs={{0,2},{1,3},{4,6},{5,7},{8,10},{9,11},{12,14},{13,15},{16,18},{17,... | collective-permute-start | bytes 1572872 | tf_op jit(solution)/shard_map/ppermute | solution.py:245
  68.2 34.0 %collective-permute-start.2 = (bf16[512,512]{1,0:T(8,128)(2,1)S(1)}, bf16[512,512]{1,0:T(8,128)(2,1)S(1)}, u32[]{:S(2)}, u32[]{:S(2)}) collective-permute-start(bf16[512,512]{1,0:T(8,128)(2,1)S(1)} %collective-permute-done.1.refs_1_), channel_id=1, source_target_pairs={{8,12},{9,13},{10,14},{11,15},{24,28},{25,29},{26,30},{27,31}} | collective-permute-start | bytes 1572872 | tf_op jit(solution)/shard_map/ppermute | solution.py:235
  69.6 36.0 %collective-permute-start.12 = (bf16[512,512]{1,0:T(8,128)(2,1)S(1)}, bf16[512,512]{1,0:T(8,128)(2,1)S(1)}, u32[]{:S(2)}, u32[]{:S(2)}) collective-permute-start(bf16[512,512]{1,0:T(8,128)(2,1)S(1)} %collective-permute-done.8.refs_1_), channel_id=1, source_target_pairs={{8,10},{9,11},{10,8},{11,9},{12,14},{13,15},{14,12},{15,13},{24,26... | collective-permute-start | bytes 1572872 | tf_op jit(solution)/shard_map/ppermute | solution.py:248
  80.8 28.0 %collective-permute-start.11 = (bf16[512,512]{1,0:T(8,128)(2,1)S(1)}, bf16[512,512]{1,0:T(8,128)(2,1)S(1)}, u32[]{:S(2)}, u32[]{:S(2)}) collective-permute-start(bf16[512,512]{1,0:T(8,128)(2,1)S(1)} %collective-permute-done.7.refs_0_), channel_id=1, source_target_pairs={{4,6},{5,7},{6,4},{7,5},{8,10},{9,11},{10,8},{11,9},{12,14},{13,15... | collective-permute-start | bytes 1572872 | tf_op jit(solution)/shard_map/ppermute | solution.py:248
  84.2 0.8 copy-start.6
  92.2 20.9 %collective-permute-start.13 = (bf16[512,512]{1,0:T(8,128)(2,1)}, bf16[512,512]{1,0:T(8,128)(2,1)}, u32[]{:S(2)}, u32[]{:S(2)}) collective-permute-start(bf16[512,512]{1,0:T(8,128)(2,1)} %collective-permute-done.9.refs_2_), channel_id=1, source_target_pairs={{12,14},{13,15},{14,12},{15,13},{28,30},{29,31},{30,28},{31,29}} | collective-permute-start | bytes 1572872 | tf_op jit(solution)/shard_map/ppermute | solution.py:248
  95.6 0.8 copy-start.8
  96.4 40.3 %collective-permute-start.3 = (bf16[512,512]{1,0:T(8,128)(2,1)S(1)}, bf16[512,512]{1,0:T(8,128)(2,1)}, u32[]{:S(2)}, u32[]{:S(2)}) collective-permute-start(bf16[512,512]{1,0:T(8,128)(2,1)S(1)} %project.1.own_ref), channel_id=1, source_target_pairs={{0,2},{1,3},{4,6},{5,7},{8,10},{9,11},{12,14},{13,15},{16,18},{17,... | collective-permute-start | bytes 1572872 | tf_op jit(solution)/shard_map/ppermute | solution.py:245
  102.1 34.6 %collective-permute-start.5 = (bf16[512,512]{1,0:T(8,128)(2,1)S(1)}, bf16[512,512]{1,0:T(8,128)(2,1)}, u32[]{:S(2)}, u32[]{:S(2)}) collective-permute-start(bf16[512,512]{1,0:T(8,128)(2,1)S(1)} %collective-permute-done.1.refs_1_), channel_id=1, source_target_pairs={{8,10},{9,11},{10,8},{11,9},{12,14},{13,15},{14,12},{15,13},{24,26... | collective-permute-start | bytes 1572872 | tf_op jit(solution)/shard_map/ppermute | solution.py:248
  105.6 0.8 copy-start.10
  106.4 35.5 %collective-permute-start.4 = (bf16[512,512]{1,0:T(8,128)(2,1)S(1)}, bf16[512,512]{1,0:T(8,128)(2,1)}, u32[]{:S(2)}, u32[]{:S(2)}) collective-permute-start(bf16[512,512]{1,0:T(8,128)(2,1)S(1)} %collective-permute-done.refs_0_), channel_id=1, source_target_pairs={{4,6},{5,7},{6,4},{7,5},{8,10},{9,11},{10,8},{11,9},{12,14},{13,15... | collective-permute-start | bytes 1572872 | tf_op jit(solution)/shard_map/ppermute | solution.py:248
  108.8 0.8 copy-start.12
  109.6 42.0 %collective-permute-start.6 = (bf16[512,512]{1,0:T(8,128)(2,1)S(1)}, bf16[512,512]{1,0:T(8,128)(2,1)}, u32[]{:S(2)}, u32[]{:S(2)}) collective-permute-start(bf16[512,512]{1,0:T(8,128)(2,1)S(1)} %collective-permute-done.2.refs_2_), channel_id=1, source_target_pairs={{12,14},{13,15},{14,12},{15,13},{28,30},{29,31},{30,28},{31,29}} | collective-permute-start | bytes 1572872 | tf_op jit(solution)/shard_map/ppermute | solution.py:248
  113.1 2.2 %copy-start.2 = (bf16[512,4096]{1,0:T(8,128)(2,1)S(1)}, bf16[512,4096]{1,0:T(8,128)(2,1)}, u32[]{:S(2)}) copy-start(bf16[512,4096]{1,0:T(8,128)(2,1)} %q_ref.3) | copy-start | bytes 12582916
  115.3 1.0 copy-start.7
  116.3 1.0 copy-start.9
  117.4 1.0 copy-start.11
  118.4 1.0 copy-start.13

commit v3 on v2

v3 whole, which is shorter than its diff:
```python
import functools
import jax
import jax.numpy as jnp
from jax import lax
from jax.experimental import pallas as pl
from jax.experimental.pallas import tpu as pltpu
from jax.sharding import PartitionSpec as P

HEAD_DIM = 128
EPS = 1e-05
LOG2E = 1.4426950408889634
MASKED = -1e30
MIB = 1024 * 1024
CHUNKS = 4
NORM_CHUNKS = 8
UNITS = 2
BLOCKS_PER_STEP = 2


def norm_project_kernel(
    x_hbm, gain_ref, key_hbm, value_hbm, normed_hbm, kv_ref,
    x_scr, key_scr, value_scr, normed_scr, acc_scr, x_sem, key_sem, value_sem, normed_sem,
):
    rows, features = x_scr.shape
    width = key_scr.shape[1]
    chunk = features // NORM_CHUNKS
    lanes = 128

    def columns(c):
        return slice(c * chunk, (c + 1) * chunk)

    def load_x(c):
        return pltpu.make_async_copy(
            x_hbm.at[:, columns(c)], x_scr.at[:, columns(c)], x_sem.at[c]
        )

    def load_weights(c):
        return [
            pltpu.make_async_copy(
                hbm.at[columns(c), pl.ds(0, width)], scr.at[columns(c), :], sem.at[c]
            )
            for hbm, scr, sem in ((key_hbm, key_scr, key_sem), (value_hbm, value_scr, value_sem))
        ]

    def store_normed(c):
        return pltpu.make_async_copy(
            normed_scr.at[:, columns(c)], normed_hbm.at[:, columns(c)], normed_sem.at[c]
        )

    for c in range(NORM_CHUNKS):
        load_x(c).start()
    for c in range(NORM_CHUNKS):
        for copy in load_weights(c):
            copy.start()

    squares = jnp.zeros((rows, lanes), jnp.float32)
    for c in range(NORM_CHUNKS):
        load_x(c).wait()
        for first in range(c * chunk, (c + 1) * chunk, lanes):
            x = x_scr[:, first : first + lanes].astype(jnp.float32)
            squares += x * x
    mean_sq = jnp.sum(squares, axis=-1, keepdims=True) / features
    inverse = jnp.broadcast_to(lax.rsqrt(mean_sq + EPS), (rows, lanes))

    def normalise(c):
        for first in range(c * chunk, (c + 1) * chunk, lanes):
            cols = slice(first, first + lanes)
            x = x_scr[:, cols].astype(jnp.float32)
            normed_scr[:, cols] = (x * inverse * gain_ref[:, cols]).astype(jnp.bfloat16)

    normalise(0)
    for c in range(NORM_CHUNKS):
        for copy in load_weights(c):
            copy.wait()
        store_normed(c).start()
        for part, weight in enumerate((key_scr, value_scr)):
            cols = slice(part * width, (part + 1) * width)
            term = jnp.dot(
                normed_scr[:, columns(c)], weight[columns(c), :], preferred_element_type=jnp.float32
            )
            if c == 0:
                acc_scr[:, cols] = term
            elif c < NORM_CHUNKS - 1:
                acc_scr[:, cols] += term
            else:
                kv_ref[:, cols] = (acc_scr[:, cols] + term).astype(jnp.bfloat16)
        if c < NORM_CHUNKS - 1:
            normalise(c + 1)
    for c in range(NORM_CHUNKS):
        store_normed(c).wait()


def norm_project(hidden, gain, key_weight, value_weight):
    rows, features = hidden.shape
    width = key_weight.shape[1] // UNITS
    whole = pl.BlockSpec(memory_space=pltpu.VMEM)
    remote = pl.BlockSpec(memory_space=pl.ANY)
    return pl.pallas_call(
        norm_project_kernel,
        in_specs=[remote, whole, remote, remote],
        out_specs=[remote, whole],
        out_shape=[
            jax.ShapeDtypeStruct((rows, features), jnp.bfloat16),
            jax.ShapeDtypeStruct((rows, 2 * width), jnp.bfloat16),
        ],
        scratch_shapes=[
            pltpu.VMEM((rows, features), jnp.bfloat16),
            pltpu.VMEM((features, width), jnp.bfloat16),
            pltpu.VMEM((features, width), jnp.bfloat16),
            pltpu.VMEM((rows, features), jnp.bfloat16),
            pltpu.VMEM((rows, 2 * width), jnp.float32),
            pltpu.SemaphoreType.DMA((NORM_CHUNKS,)),
            pltpu.SemaphoreType.DMA((NORM_CHUNKS,)),
            pltpu.SemaphoreType.DMA((NORM_CHUNKS,)),
            pltpu.SemaphoreType.DMA((NORM_CHUNKS,)),
        ],
        compiler_params=pltpu.CompilerParams(vmem_limit_bytes=57 * MIB),
        cost_estimate=pl.CostEstimate(
            flops=4 * rows * features * width, bytes_accessed=24 * MIB, transcendentals=0
        ),
        name="norm_project",
    )(hidden, gain.reshape(1, features), key_weight, value_weight)


def project_kernel(normed_ref, key_ref, value_ref, kv_ref, acc_scr):
    step = pl.program_id(0)
    width = key_ref.shape[1]
    normed = normed_ref[...]
    for part, weight in enumerate((key_ref, value_ref)):
        cols = slice(part * width, (part + 1) * width)
        term = jnp.dot(normed, weight[...], preferred_element_type=jnp.float32)
        acc_scr[:, cols] = jnp.where(step == 0, term, acc_scr[:, cols] + term)

    @pl.when(step == CHUNKS - 1)
    def _():
        kv_ref[...] = acc_scr[...].astype(jnp.bfloat16)


def project(normed, key_weight, value_weight, unit):
    rows, features = normed.shape
    chunk = features // CHUNKS
    width = key_weight.shape[1] // UNITS
    weight = pl.BlockSpec((chunk, width), lambda i: (i, unit))
    return pl.pallas_call(
        project_kernel,
        grid=(CHUNKS,),
        in_specs=[pl.BlockSpec((rows, chunk), lambda i: (0, i)), weight, weight],
        out_specs=pl.BlockSpec((rows, 2 * width), lambda i: (0, 0)),
        out_shape=jax.ShapeDtypeStruct((rows, 2 * width), jnp.bfloat16),
        scratch_shapes=[pltpu.VMEM((rows, 2 * width), jnp.float32)],
        compiler_params=pltpu.CompilerParams(vmem_limit_bytes=57 * MIB),
        cost_estimate=pl.CostEstimate(
            flops=4 * rows * features * width, bytes_accessed=16 * MIB, transcendentals=0
        ),
        name="project",
    )(normed, key_weight, value_weight)


def attention_kernel(block, kv_heads, near, slot_ref, cut_ref, odd_ref, q_ref, own_ref, *refs):
    out_ref = refs[-1]
    straight, crossed = refs[:near], refs[near : 2 * near + 1]
    depth = slot_ref.shape[1]
    odd = odd_ref[0] == 1
    per_group = q_ref.shape[1] // HEAD_DIM // kv_heads
    tile = 256
    together = tile // block
    scale = HEAD_DIM**-0.5 * LOG2E
    token = lax.broadcasted_iota(jnp.int32, (block, HEAD_DIM), 0)
    lane = lax.broadcasted_iota(jnp.int32, (block, HEAD_DIM), 1)
    hidden_later = jnp.where((lane >= block) & (lane - block > token), MASKED, 0.0)
    query_mask = jnp.where(lane == 0, 1.0, hidden_later).astype(jnp.bfloat16)
    query_mask = jnp.concatenate([query_mask] * together, axis=0)
    own_mask = jnp.where(lane - block == token, 1.0, 0.0).astype(jnp.bfloat16)

    def gather(local):
        here = pl.program_id(0) * BLOCKS_PER_STEP + local
        pieces, masks = [], []
        for k in range(depth):
            rows = pl.ds(pl.multiple_of(slot_ref[here, k] * block, block), block)
            if k % 2 == 1:
                pieces.append(straight[k // 2][rows, :])
            else:
                low = crossed[k // 2][rows, :]
                high = crossed[min(k // 2 + 1, near)][rows, :]
                pieces.append(jnp.where(odd, low, high))
            unseen = (lane == 0) & (token >= cut_ref[here, k])
            masks.append(jnp.where(unseen, MASKED, 0.0).astype(jnp.bfloat16))
        pieces.append(own_ref[pl.ds(pl.multiple_of(here * block, block), block), :])
        masks.append(own_mask)
        return jnp.concatenate(pieces, axis=0), jnp.concatenate(masks, axis=0)

    def score(local, head, first, every, mask):
        keys = jnp.concatenate([every[:, head * HEAD_DIM : (head + 1) * HEAD_DIM], mask], axis=1)
        rows = slice(local * block, (local + 1) * block)
        queries = jnp.concatenate(
            [
                q_ref[rows, r * HEAD_DIM : (r + 1) * HEAD_DIM]
                for r in range(first, first + together)
            ],
            axis=0,
        )
        queries = jnp.concatenate([queries, query_mask], axis=1)
        return lax.dot_general(
            keys, queries, (((1,), (1,)), ((), ())), preferred_element_type=jnp.float32
        )

    def finish(local, first, scores, flipped):
        peak = jnp.max(scores, axis=0, keepdims=True)
        weights = jnp.exp2((scores - peak) * scale).astype(jnp.bfloat16)
        both = jnp.dot(flipped, weights, preferred_element_type=jnp.float32)
        context = both[:HEAD_DIM] * (1.0 / both[HEAD_DIM : HEAD_DIM + 1])
        context = context.T.astype(jnp.bfloat16)
        for r in range(together):
            cols = slice((first + r) * HEAD_DIM, (first + r + 1) * HEAD_DIM)
            out_ref[local * block : (local + 1) * block, cols] = context[r * block : (r + 1) * block]

    waiting = None
    for local in range(BLOCKS_PER_STEP):
        every, mask = gather(local)
        for head in range(kv_heads):
            start = (kv_heads + head) * HEAD_DIM
            values = every[:, start : start + HEAD_DIM]
            flipped = jnp.concatenate(
                [values.T, jnp.ones((16, values.shape[0]), jnp.bfloat16)], axis=0
            )
            for first in range(head * per_group, (head + 1) * per_group, together):
                scores = score(local, head, first, every, mask)
                if waiting is not None:
                    finish(*waiting)
                waiting = (local, first, scores, flipped)
    finish(*waiting)


def attention(slots, cuts, odd, queries, own, straight, crossed, unit, previous):
    rows, features = queries.shape
    blocks, depth = slots.shape
    block = rows // blocks
    wide = features // UNITS
    near = len(straight)
    kv_heads = own.shape[1] // (2 * HEAD_DIM)
    whole = pl.BlockSpec(own.shape, lambda b, *_: (0, 0), pipeline_mode=pl.Buffered(1))
    part = pl.BlockSpec((BLOCKS_PER_STEP * block, wide), lambda b, *_: (b, unit))
    operands = [slots, cuts, odd, queries, own, *straight, *crossed]
    in_specs = [part] + [whole] * (1 + near + len(crossed))
    aliases = {}
    if previous is not None:
        aliases = {len(operands): 0}
        operands.append(previous)
        in_specs.append(pl.BlockSpec(memory_space=pl.ANY))
    return pl.pallas_call(
        functools.partial(attention_kernel, block, kv_heads, near),
        grid_spec=pltpu.PrefetchScalarGridSpec(
            num_scalar_prefetch=3, grid=(blocks // BLOCKS_PER_STEP,), in_specs=in_specs, out_specs=part
        ),
        out_shape=jax.ShapeDtypeStruct((rows, features), jnp.bfloat16),
        input_output_aliases=aliases,
        compiler_params=pltpu.CompilerParams(vmem_limit_bytes=24 * MIB),
        cost_estimate=pl.CostEstimate(
            flops=4 * rows * wide * (depth + 1) * block,
            bytes_accessed=8 * MIB,
            transcendentals=rows * wide // HEAD_DIM * (depth + 1) * block,
        ),
        name="attention",
    )(*operands)


def shards(hidden, queries, norm_gain, key_weight, value_weight, anc_ids, anc_cut):
    blocks, depth = anc_ids.shape
    levels = depth + 1
    size = lax.axis_size("node")
    chains = size // levels
    near = depth // 2
    half = [index // chains // 2 for index in range(size)]
    even = [index // chains % 2 == 0 for index in range(size)]
    other = [index + chains if even[index] else index - chains for index in range(size)]
    odd = (lax.axis_index("node") // chains % 2).astype(jnp.int32).reshape(1)
    slots = jnp.where(anc_ids >= 0, anc_ids % blocks, 0)

    def shifted(array, distance, least=0):
        shift = 2 * distance * chains
        pairs = [(i, i + shift) for i in range(size) if i + shift < size and half[i] >= least]
        return lax.ppermute(array, "node", pairs)

    normed, first = norm_project(hidden, norm_gain, key_weight, value_weight)
    own = [first] + [project(normed, key_weight, value_weight, unit) for unit in range(1, UNITS)]
    def after(array, *earlier):
        return lax.optimization_barrier((array, *earlier))[0]

    straight = [[] for _ in range(UNITS)]
    crossed = [[] for _ in range(UNITS)]
    waves = []
    for s in range(near + 1):
        for unit in range(UNITS):
            settled = waves[-2] if len(waves) >= 2 else ()
            source = own[unit] if s == 0 else straight[unit][s - 1]
            pairs = [(i, other[i]) for i in range(size) if (half[i] >= s if s else even[i])]
            crossed[unit].append(lax.ppermute(after(source, *settled), "node", pairs))
            wave = [crossed[unit][-1]]
            if s < near:
                ahead = after(own[unit] if s < 2 else straight[unit][-1], *settled)
                straight[unit].append(
                    shifted(ahead, s + 1) if s < 2 else shifted(ahead, 1, s)
                )
                wave.append(straight[unit][-1])
            waves.append(wave)
    result = None
    for unit in range(UNITS):
        result = attention(
            slots, anc_cut, odd, queries, own[unit], straight[unit], crossed[unit], unit, result
        )
    return result


def solution(mesh):
    placed = (
        P(("groups", "node"), None),
        P(("groups", "node"), None),
        P(),
        P(),
        P(),
        P(("groups", "node"), None),
        P(("groups", "node"), None),
    )
    return jax.shard_map(
        shards, mesh=mesh, in_specs=placed, out_specs=P(("groups", "node"), None), check_vma=False
    )
```

time: 171 us -> 149 us (0.87)
  local copies, waits for them, and re-layouts: 23.7 us -> 8.29 us
  starting transfers between devices: 33.9 us -> 24.6 us
  waiting for transfers between devices: 59.7 us -> 66.9 us
  Pallas kernels: 51.6 us -> 48.5 us
    unnamed x34 -> x30, local copies, waits for them, and re-layouts: 23.7 us -> 8.29 us
    pallas_call x2, Pallas kernels: 34.8 us -> 22.3 us  [attention(): pl.pallas_call(functools.partial(attention_kernel, block, kv_heads, near)...]
    ppermute x6, waiting for transfers between devices: 44.8 us -> 57.3 us  [shifted(): return lax.ppermute(array, 'node', pairs)]
    ppermute x8, starting transfers between devices: 26.1 us -> 16.9 us  [shards(): crossed[unit].append(lax.ppermute(after(source, *settled), 'node', pairs))]
    pallas_call x1, Pallas kernels: 10.6 us -> 16.8 us  [norm_project(): pl.pallas_call(norm_project_kernel, in_specs=[remote, whole, remote, remo...]
    ppermute x8, waiting for transfers between devices: 14.9 us -> 9.62 us  [shards(): crossed[unit].append(lax.ppermute(after(source, *settled), 'node', pairs))]
    pallas_call x1, Pallas kernels: 6.2 us -> 9.32 us  [project(): pl.pallas_call(project_kernel, grid=(CHUNKS,), in_specs=[pl.BlockSpec((ro...]
  transfers between devices with their start and end apart: 14 -> 14, of which waited for: 8 -> 9; matrix products, arithmetic and copies ran while one was open for 0% -> 0% of each run, Pallas kernels for 14% -> 14%
where the time goes in v3:
time: 149 us
  waiting for transfers between devices  66.9 us (45%)
  Pallas kernels  48.5 us (33%)
  starting transfers between devices  24.6 us (17%)
  local copies, waits for them, and re-layouts  8.29 us (6%)
    ppermute x6, waiting for transfers between devices, shifted(): return lax.ppermute(array, 'node', pairs)  57.3 us
    pallas_call x2, Pallas kernels, attention(): pl.pallas_call(functools.partial(attention_kernel, block, kv_heads, near)...  22.3 us
    ppermute x8, starting transfers between devices, shards(): crossed[unit].append(lax.ppermute(after(source, *settled), 'node', pairs))  16.9 us
    pallas_call x1, Pallas kernels, norm_project(): pl.pallas_call(norm_project_kernel, in_specs=[remote, whole, remote, remo...  16.8 us
    ppermute x8, waiting for transfers between devices, shards(): crossed[unit].append(lax.ppermute(after(source, *settled), 'node', pairs))  9.62 us
    pallas_call x1, Pallas kernels, project(): pl.pallas_call(project_kernel, grid=(CHUNKS,), in_specs=[pl.BlockSpec((ro...  9.32 us
    unnamed x30, local copies, waits for them, and re-layouts  8.29 us
    ppermute x6, starting transfers between devices, shifted(): return lax.ppermute(array, 'node', pairs)  7.73 us
  transfers between devices with their start and end apart: 14, of which 9 were waited for; matrix products, arithmetic and copies ran while one was open for 0% of the time, Pallas kernels for 14%

profile of v3, /device:TPU:24, one launch (start us, length us, event | category | flops | bytes accessed | tf_op | source)
XLA Modules:
  0.0 148.5 jit_solution(16657648084397766467)
XLA Ops:
  0.0 16.8 %norm_project.1 = (bf16[512,8192]{1,0:T(8,128)(2,1)}, bf16[512,512]{1,0:T(8,128)(2,1)}) custom-call(bf16[512,8192]{1,0:T(8,128)(2,1)} %x_hbm.1, f32[1,8192]{1,0:T(1,128)} %bitcast.2, bf16[8192,512]{1,0:T(8,128)(2,1)} %key_ref.1, bf16[8192,512]{1,0:T(8,128)(2,1)} %value_ref.1), custom_call_target="tpu_custom_call" | custom-call | flops 4294967296 | bytes 25165824 | tf_op jit(solution)/shard_map/norm_project/pallas_call | solution.py:98
  16.8 3.5 %collective-permute-start.8 = (bf16[512,512]{1,0:T(8,128)(2,1)}, bf16[512,512]{1,0:T(8,128)(2,1)S(1)}, u32[]{:S(2)}, u32[]{:S(2)}) collective-permute-start(bf16[512,512]{1,0:T(8,128)(2,1)} %get-tuple-element.21.own_ref), channel_id=1, source_target_pairs={{0,2},{1,3},{4,6},{5,7},{8,10},{9,11},{12,14},{13,15},{16,18},{17,... | collective-permute-start | bytes 1572872 | tf_op jit(solution)/shard_map/ppermute | solution.py:297
  20.3 1.3 collective-permute-start.7
  21.6 0.0 copy-start.2
  21.6 0.0 copy-start.14
  21.6 0.0 copy-start.13
  21.6 9.3 %project.1.own_ref = bf16[512,512]{1,0:T(8,128)(2,1)} custom-call(bf16[512,8192]{1,0:T(8,128)(2,1)} %get-tuple-element.15.normed_ref, bf16[8192,512]{1,0:T(8,128)(2,1)} %key_ref.1, bf16[8192,512]{1,0:T(8,128)(2,1)} %value_ref.1), custom_call_target="tpu_custom_call" | custom-call | flops 4294967296 | bytes 16777216 | tf_op jit(solution)/shard_map/project/pallas_call | solution.py:144
  30.9 1.3 collective-permute-start.1
  32.3 1.3 collective-permute-start
  33.6 0.0 collective-permute-done.8.refs_3_
  33.6 2.2 %collective-permute-done.7.refs_0_ = bf16[512,512]{1,0:T(8,128)(2,1)S(1)} collective-permute-done((bf16[512,512]{1,0:T(8,128)(2,1)}, bf16[512,512]{1,0:T(8,128)(2,1)S(1)}, u32[]{:S(2)}, u32[]{:S(2)}) %collective-permute-start.7) | collective-permute-done | bytes 524320 | tf_op jit(solution)/shard_map/ppermute | solution.py:282
  35.8 0.0 copy-done.2
  35.8 1.3 collective-permute-start.9
  37.1 1.9 %collective-permute-start.10 = (bf16[512,512]{1,0:T(8,128)(2,1)S(1)}, bf16[512,512]{1,0:T(8,128)(2,1)S(1)}, u32[]{:S(2)}, u32[]{:S(2)}) collective-permute-start(bf16[512,512]{1,0:T(8,128)(2,1)S(1)} %collective-permute-done.7.refs_0_), channel_id=1, source_target_pairs={{4,6},{5,7},{6,4},{7,5},{8,10},{9,11},{10,8},{11,9},{12,14},{13,15... | collective-permute-start | bytes 1572872 | tf_op jit(solution)/shard_map/ppermute | solution.py:297
  39.0 5.9 %collective-permute-done.1.refs_3_ = bf16[512,512]{1,0:T(8,128)(2,1)S(1)} collective-permute-done((bf16[512,512]{1,0:T(8,128)(2,1)}, bf16[512,512]{1,0:T(8,128)(2,1)S(1)}, u32[]{:S(2)}, u32[]{:S(2)}) %collective-permute-start.1) | collective-permute-done | bytes 524320 | tf_op jit(solution)/shard_map/ppermute | solution.py:297
  44.9 3.7 %collective-permute-done.refs_0_ = bf16[512,512]{1,0:T(8,128)(2,1)S(1)} collective-permute-done((bf16[512,512]{1,0:T(8,128)(2,1)}, bf16[512,512]{1,0:T(8,128)(2,1)S(1)}, u32[]{:S(2)}, u32[]{:S(2)}) %collective-permute-start) | collective-permute-done | bytes 524320 | tf_op jit(solution)/shard_map/ppermute | solution.py:282
  48.5 1.3 collective-permute-start.2
  49.8 1.9 %collective-permute-start.3 = (bf16[512,512]{1,0:T(8,128)(2,1)S(1)}, bf16[512,512]{1,0:T(8,128)(2,1)S(1)}, u32[]{:S(2)}, u32[]{:S(2)}) collective-permute-start(bf16[512,512]{1,0:T(8,128)(2,1)S(1)} %collective-permute-done.refs_0_), channel_id=1, source_target_pairs={{4,6},{5,7},{6,4},{7,5},{8,10},{9,11},{10,8},{11,9},{12,14},{13,15... | collective-permute-start | bytes 1572872 | tf_op jit(solution)/shard_map/ppermute | solution.py:297
  51.7 33.3 %collective-permute-done.9.refs_1_ = bf16[512,512]{1,0:T(8,128)(2,1)S(1)} collective-permute-done((bf16[512,512]{1,0:T(8,128)(2,1)S(1)}, bf16[512,512]{1,0:T(8,128)(2,1)S(1)}, u32[]{:S(2)}, u32[]{:S(2)}) %collective-permute-start.9) | collective-permute-done | bytes 524320 | tf_op jit(solution)/shard_map/ppermute | solution.py:282
  85.0 0.0 collective-permute-done.10.refs_4_
  85.0 0.8 copy-done.5
  85.8 1.9 %collective-permute-start.12 = (bf16[512,512]{1,0:T(8,128)(2,1)S(1)}, bf16[512,512]{1,0:T(8,128)(2,1)S(1)}, u32[]{:S(2)}, u32[]{:S(2)}) collective-permute-start(bf16[512,512]{1,0:T(8,128)(2,1)S(1)} %collective-permute-done.9.refs_1_), channel_id=1, source_target_pairs={{8,10},{9,11},{10,8},{11,9},{12,14},{13,15},{14,12},{15,13},{24,26... | collective-permute-start | bytes 1572872 | tf_op jit(solution)/shard_map/ppermute | solution.py:297
  87.7 1.3 collective-permute-start.11
  89.0 5.6 %collective-permute-done.2.refs_1_ = bf16[512,512]{1,0:T(8,128)(2,1)S(1)} collective-permute-done((bf16[512,512]{1,0:T(8,128)(2,1)}, bf16[512,512]{1,0:T(8,128)(2,1)S(1)}, u32[]{:S(2)}, u32[]{:S(2)}) %collective-permute-start.2) | collective-permute-done | bytes 524320 | tf_op jit(solution)/shard_map/ppermute | solution.py:282
  94.6 0.0 collective-permute-done.3.refs_4_
  94.6 0.8 copy-done.7
  95.4 1.9 %collective-permute-start.5 = (bf16[512,512]{1,0:T(8,128)(2,1)S(1)}, bf16[512,512]{1,0:T(8,128)(2,1)S(1)}, u32[]{:S(2)}, u32[]{:S(2)}) collective-permute-start(bf16[512,512]{1,0:T(8,128)(2,1)S(1)} %collective-permute-done.2.refs_1_), channel_id=1, source_target_pairs={{8,10},{9,11},{10,8},{11,9},{12,14},{13,15},{14,12},{15,13},{24,26... | collective-permute-start | bytes 1572872 | tf_op jit(solution)/shard_map/ppermute | solution.py:297
  97.3 1.3 collective-permute-start.4
  98.6 0.0 copy-start.3
  98.6 0.8 copy-done.3
  99.4 0.0 collective-permute-done.12.refs_5_
  99.4 0.8 copy-done.9
  100.2 5.7 %collective-permute-done.11.refs_2_ = bf16[512,512]{1,0:T(8,128)(2,1)} collective-permute-done((bf16[512,512]{1,0:T(8,128)(2,1)S(1)}, bf16[512,512]{1,0:T(8,128)(2,1)}, u32[]{:S(2)}, u32[]{:S(2)}) %collective-permute-start.11) | collective-permute-done | bytes 524320 | tf_op jit(solution)/shard_map/ppermute | solution.py:282
  105.9 2.6 %collective-permute-start.13 = (bf16[512,512]{1,0:T(8,128)(2,1)}, bf16[512,512]{1,0:T(8,128)(2,1)}, u32[]{:S(2)}, u32[]{:S(2)}) collective-permute-start(bf16[512,512]{1,0:T(8,128)(2,1)} %collective-permute-done.11.refs_2_), channel_id=1, source_target_pairs={{12,14},{13,15},{14,12},{15,13},{28,30},{29,31},{30,28},{31,29}} | collective-permute-start | bytes 1572872 | tf_op jit(solution)/shard_map/ppermute | solution.py:297
  108.5 0.9 collective-permute-done.5.refs_5_
  109.4 0.8 copy-done.11
  110.2 6.9 %collective-permute-done.4.refs_2_ = bf16[512,512]{1,0:T(8,128)(2,1)} collective-permute-done((bf16[512,512]{1,0:T(8,128)(2,1)S(1)}, bf16[512,512]{1,0:T(8,128)(2,1)}, u32[]{:S(2)}, u32[]{:S(2)}) %collective-permute-start.4) | collective-permute-done | bytes 524320 | tf_op jit(solution)/shard_map/ppermute | solution.py:282
  117.1 1.9 %collective-permute-start.6 = (bf16[512,512]{1,0:T(8,128)(2,1)}, bf16[512,512]{1,0:T(8,128)(2,1)}, u32[]{:S(2)}, u32[]{:S(2)}) collective-permute-start(bf16[512,512]{1,0:T(8,128)(2,1)} %collective-permute-done.4.refs_2_), channel_id=1, source_target_pairs={{12,14},{13,15},{14,12},{15,13},{28,30},{29,31},{30,28},{31,29}} | collective-permute-start | bytes 1572872 | tf_op jit(solution)/shard_map/ppermute | solution.py:297
  119.0 0.0 copy-done.14
  119.0 2.8 %collective-permute-done.13.refs_6_ = bf16[512,512]{1,0:T(8,128)(2,1)} collective-permute-done((bf16[512,512]{1,0:T(8,128)(2,1)}, bf16[512,512]{1,0:T(8,128)(2,1)}, u32[]{:S(2)}, u32[]{:S(2)}) %collective-permute-start.13) | collective-permute-done | bytes 524320 | tf_op jit(solution)/shard_map/ppermute | solution.py:297
  121.9 0.0 copy-done.13
  121.9 2.2 %copy-done = bf16[512,4096]{1,0:T(8,128)(2,1)S(1)} copy-done((bf16[512,4096]{1,0:T(8,128)(2,1)S(1)}, bf16[512,4096]{1,0:T(8,128)(2,1)}, u32[]{:S(2)}) %copy-start) | copy-done | bytes 4194328
  124.1 1.0 copy-done.6
  125.1 1.0 copy-done.10
  126.2 11.2 %attention.2.refs_7_ = bf16[512,4096]{1,0:T(8,128)(2,1)} custom-call(s32[8,7]{1,0:T(8,128)S(1)} %fusion.1.slot_ref, s32[8,7]{1,0:T(8,128)S(1)} %copy-done.13, s32[1]{0:T(128)} %bitcast.odd_ref, bf16[512,4096]{1,0:T(8,128)(2,1)S(1)} %copy-done, bf16[512,512]{1,0:T(8,128)(2,1)S(1)} %copy-done.2, bf16[512,512]{1,0:T(8,128)(2,1)S(1)} %collective-permute-done.7.refs_0_, ...), custom_call_target="tpu_custom_call" | custom-call | flops 2147483648 | bytes 8388608 | tf_op jit(solution)/shard_map/attention/pallas_call | solution.py:250
  137.3 0.0 collective-permute-done.6.refs_6_
  137.3 0.0 copy-done.4
  137.3 11.2 %attention.3 = bf16[512,4096]{1,0:T(8,128)(2,1)} custom-call(s32[8,7]{1,0:T(8,128)S(1)} %fusion.1.slot_ref, s32[8,7]{1,0:T(8,128)S(1)} %copy-done.13, s32[1]{0:T(128)} %bitcast.odd_ref, bf16[512,4096]{1,0:T(8,128)(2,1)S(1)} %copy-done, bf16[512,512]{1,0:T(8,128)(2,1)S(1)} %copy-done.1, ...), custom_call_target="tpu_custom_call", output_to_operand_aliasing={{}: (12, {})} | custom-call | flops 2147483648 | bytes 8388608 | tf_op jit(solution)/shard_map/attention/pallas_call | solution.py:250
  (15 shorter events, 0.0 us)
Async XLA Ops:
  16.8 16.7 %collective-permute-start.8 = (bf16[512,512]{1,0:T(8,128)(2,1)}, bf16[512,512]{1,0:T(8,128)(2,1)S(1)}, u32[]{:S(2)}, u32[]{:S(2)}) collective-permute-start(bf16[512,512]{1,0:T(8,128)(2,1)} %get-tuple-element.21.own_ref), channel_id=1, source_target_pairs={{0,2},{1,3},{4,6},{5,7},{8,10},{9,11},{12,14},{13,15},{16,18},{17,... | collective-permute-start | bytes 1572872 | tf_op jit(solution)/shard_map/ppermute | solution.py:297
  20.3 15.5 %collective-permute-start.7 = (bf16[512,512]{1,0:T(8,128)(2,1)}, bf16[512,512]{1,0:T(8,128)(2,1)S(1)}, u32[]{:S(2)}, u32[]{:S(2)}) collective-permute-start(bf16[512,512]{1,0:T(8,128)(2,1)} %get-tuple-element.21.own_ref), channel_id=1, source_target_pairs={{0,4},{1,5},{2,6},{3,7},{4,8},{5,9},{6,10},{7,11},{8,12},{9,13},{1... | collective-permute-start | bytes 1572872 | tf_op jit(solution)/shard_map/ppermute | solution.py:282
  21.6 14.2 %copy-start.2 = (bf16[512,512]{1,0:T(8,128)(2,1)S(1)}, bf16[512,512]{1,0:T(8,128)(2,1)}, u32[]{:S(2)}) copy-start(bf16[512,512]{1,0:T(8,128)(2,1)} %get-tuple-element.21.own_ref) | copy-start | bytes 1572868
  21.6 97.4 %copy-start.14 = (s32[8,7]{1,0:T(8,128)S(1)}, s32[8,7]{1,0:T(8,128)}, u32[]{:S(2)}) copy-start(s32[8,7]{1,0:T(8,128)} %param.12) | copy-start | bytes 676
  21.6 100.3 %copy-start.13 = (s32[8,7]{1,0:T(8,128)S(1)}, s32[8,7]{1,0:T(8,128)}, u32[]{:S(2)}) copy-start(s32[8,7]{1,0:T(8,128)} %cut_ref.3) | copy-start | bytes 676
  30.9 13.9 %collective-permute-start.1 = (bf16[512,512]{1,0:T(8,128)(2,1)}, bf16[512,512]{1,0:T(8,128)(2,1)S(1)}, u32[]{:S(2)}, u32[]{:S(2)}) collective-permute-start(bf16[512,512]{1,0:T(8,128)(2,1)} %project.1.own_ref), channel_id=1, source_target_pairs={{0,2},{1,3},{4,6},{5,7},{8,10},{9,11},{12,14},{13,15},{16,18},{17,... | collective-permute-start | bytes 1572872 | tf_op jit(solution)/shard_map/ppermute | solution.py:297
  32.3 16.3 %collective-permute-start = (bf16[512,512]{1,0:T(8,128)(2,1)}, bf16[512,512]{1,0:T(8,128)(2,1)S(1)}, u32[]{:S(2)}, u32[]{:S(2)}) collective-permute-start(bf16[512,512]{1,0:T(8,128)(2,1)} %project.1.own_ref), channel_id=1, source_target_pairs={{0,4},{1,5},{2,6},{3,7},{4,8},{5,9},{6,10},{7,11},{8,12},{9,13},{1... | collective-permute-start | bytes 1572872 | tf_op jit(solution)/shard_map/ppermute | solution.py:282
  35.8 49.2 %collective-permute-start.9 = (bf16[512,512]{1,0:T(8,128)(2,1)S(1)}, bf16[512,512]{1,0:T(8,128)(2,1)S(1)}, u32[]{:S(2)}, u32[]{:S(2)}) collective-permute-start(bf16[512,512]{1,0:T(8,128)(2,1)S(1)} %copy-done.2), channel_id=1, source_target_pairs={{0,8},{1,9},{2,10},{3,11},{4,12},{5,13},{6,14},{7,15},{16,24},{17,... | collective-permute-start | bytes 1572872 | tf_op jit(solution)/shard_map/ppermute | solution.py:282
  37.1 48.0 %collective-permute-start.10 = (bf16[512,512]{1,0:T(8,128)(2,1)S(1)}, bf16[512,512]{1,0:T(8,128)(2,1)S(1)}, u32[]{:S(2)}, u32[]{:S(2)}) collective-permute-start(bf16[512,512]{1,0:T(8,128)(2,1)S(1)} %collective-permute-done.7.refs_0_), channel_id=1, source_target_pairs={{4,6},{5,7},{6,4},{7,5},{8,10},{9,11},{10,8},{11,9},{12,14},{13,15... | collective-permute-start | bytes 1572872 | tf_op jit(solution)/shard_map/ppermute | solution.py:297
  48.5 46.1 %collective-permute-start.2 = (bf16[512,512]{1,0:T(8,128)(2,1)}, bf16[512,512]{1,0:T(8,128)(2,1)S(1)}, u32[]{:S(2)}, u32[]{:S(2)}) collective-permute-start(bf16[512,512]{1,0:T(8,128)(2,1)} %project.1.own_ref), channel_id=1, source_target_pairs={{0,8},{1,9},{2,10},{3,11},{4,12},{5,13},{6,14},{7,15},{16,24},{17,... | collective-permute-start | bytes 1572872 | tf_op jit(solution)/shard_map/ppermute | solution.py:282
  49.8 44.8 %collective-permute-start.3 = (bf16[512,512]{1,0:T(8,128)(2,1)S(1)}, bf16[512,512]{1,0:T(8,128)(2,1)S(1)}, u32[]{:S(2)}, u32[]{:S(2)}) collective-permute-start(bf16[512,512]{1,0:T(8,128)(2,1)S(1)} %collective-permute-done.refs_0_), channel_id=1, source_target_pairs={{4,6},{5,7},{6,4},{7,5},{8,10},{9,11},{10,8},{11,9},{12,14},{13,15... | collective-permute-start | bytes 1572872 | tf_op jit(solution)/shard_map/ppermute | solution.py:297
  85.0 0.8 copy-start.5
  85.8 13.6 %collective-permute-start.12 = (bf16[512,512]{1,0:T(8,128)(2,1)S(1)}, bf16[512,512]{1,0:T(8,128)(2,1)S(1)}, u32[]{:S(2)}, u32[]{:S(2)}) collective-permute-start(bf16[512,512]{1,0:T(8,128)(2,1)S(1)} %collective-permute-done.9.refs_1_), channel_id=1, source_target_pairs={{8,10},{9,11},{10,8},{11,9},{12,14},{13,15},{14,12},{15,13},{24,26... | collective-permute-start | bytes 1572872 | tf_op jit(solution)/shard_map/ppermute | solution.py:297
  87.7 18.2 %collective-permute-start.11 = (bf16[512,512]{1,0:T(8,128)(2,1)S(1)}, bf16[512,512]{1,0:T(8,128)(2,1)}, u32[]{:S(2)}, u32[]{:S(2)}) collective-permute-start(bf16[512,512]{1,0:T(8,128)(2,1)S(1)} %collective-permute-done.9.refs_1_), channel_id=1, source_target_pairs={{8,12},{9,13},{10,14},{11,15},{24,28},{25,29},{26,30},{27,31}} | collective-permute-start | bytes 1572872 | tf_op jit(solution)/shard_map/ppermute | solution.py:282
  94.6 0.8 copy-start.7
  95.4 14.0 %collective-permute-start.5 = (bf16[512,512]{1,0:T(8,128)(2,1)S(1)}, bf16[512,512]{1,0:T(8,128)(2,1)S(1)}, u32[]{:S(2)}, u32[]{:S(2)}) collective-permute-start(bf16[512,512]{1,0:T(8,128)(2,1)S(1)} %collective-permute-done.2.refs_1_), channel_id=1, source_target_pairs={{8,10},{9,11},{10,8},{11,9},{12,14},{13,15},{14,12},{15,13},{24,26... | collective-permute-start | bytes 1572872 | tf_op jit(solution)/shard_map/ppermute | solution.py:297
  97.3 19.7 %collective-permute-start.4 = (bf16[512,512]{1,0:T(8,128)(2,1)S(1)}, bf16[512,512]{1,0:T(8,128)(2,1)}, u32[]{:S(2)}, u32[]{:S(2)}) collective-permute-start(bf16[512,512]{1,0:T(8,128)(2,1)S(1)} %collective-permute-done.2.refs_1_), channel_id=1, source_target_pairs={{8,12},{9,13},{10,14},{11,15},{24,28},{25,29},{26,30},{27,31}} | collective-permute-start | bytes 1572872 | tf_op jit(solution)/shard_map/ppermute | solution.py:282
  98.6 0.8 copy-start.3
  99.4 0.8 copy-start.9
  105.9 16.0 %collective-permute-start.13 = (bf16[512,512]{1,0:T(8,128)(2,1)}, bf16[512,512]{1,0:T(8,128)(2,1)}, u32[]{:S(2)}, u32[]{:S(2)}) collective-permute-start(bf16[512,512]{1,0:T(8,128)(2,1)} %collective-permute-done.11.refs_2_), channel_id=1, source_target_pairs={{12,14},{13,15},{14,12},{15,13},{28,30},{29,31},{30,28},{31,29}} | collective-permute-start | bytes 1572872 | tf_op jit(solution)/shard_map/ppermute | solution.py:297
  109.4 0.8 copy-start.11
  117.1 20.3 %collective-permute-start.6 = (bf16[512,512]{1,0:T(8,128)(2,1)}, bf16[512,512]{1,0:T(8,128)(2,1)}, u32[]{:S(2)}, u32[]{:S(2)}) collective-permute-start(bf16[512,512]{1,0:T(8,128)(2,1)} %collective-permute-done.4.refs_2_), channel_id=1, source_target_pairs={{12,14},{13,15},{14,12},{15,13},{28,30},{29,31},{30,28},{31,29}} | collective-permute-start | bytes 1572872 | tf_op jit(solution)/shard_map/ppermute | solution.py:297
  121.9 2.2 %copy-start = (bf16[512,4096]{1,0:T(8,128)(2,1)S(1)}, bf16[512,4096]{1,0:T(8,128)(2,1)}, u32[]{:S(2)}) copy-start(bf16[512,4096]{1,0:T(8,128)(2,1)} %q_ref.3) | copy-start | bytes 12582916
  124.1 1.0 copy-start.6
  125.1 1.0 copy-start.10
  126.1 11.2 %copy-start.1 = (bf16[512,512]{1,0:T(8,128)(2,1)S(1)}, bf16[512,512]{1,0:T(8,128)(2,1)}, u32[]{:S(2)}) copy-start(bf16[512,512]{1,0:T(8,128)(2,1)} %project.1.own_ref) | copy-start | bytes 1572868
  126.1 11.2 %copy-start.4 = (bf16[512,512]{1,0:T(8,128)(2,1)S(1)}, bf16[512,512]{1,0:T(8,128)(2,1)}, u32[]{:S(2)}) copy-start(bf16[512,512]{1,0:T(8,128)(2,1)} %copy-done.3) | copy-start | bytes 1572868
  126.1 11.2 %copy-start.8 = (bf16[512,512]{1,0:T(8,128)(2,1)S(1)}, bf16[512,512]{1,0:T(8,128)(2,1)}, u32[]{:S(2)}) copy-start(bf16[512,512]{1,0:T(8,128)(2,1)} %copy-done.7) | copy-start | bytes 1572868
  126.2 11.2 %copy-start.12 = (bf16[512,512]{1,0:T(8,128)(2,1)S(1)}, bf16[512,512]{1,0:T(8,128)(2,1)}, u32[]{:S(2)}) copy-start(bf16[512,512]{1,0:T(8,128)(2,1)} %copy-done.11) | copy-start | bytes 1572868

commit v4 on v3

--- a/solution.py
+++ b/solution.py
@@ -47,26 +47,37 @@
             normed_scr.at[:, columns(c)], normed_hbm.at[:, columns(c)], normed_sem.at[c]
         )
 
+    def start_weights(c):
+        for copy in load_weights(c):
+            copy.start()
+
     for c in range(NORM_CHUNKS):
         load_x(c).start()
-    for c in range(NORM_CHUNKS):
-        for copy in load_weights(c):
-            copy.start()
-
-    squares = jnp.zeros((rows, lanes), jnp.float32)
+    band = 128
+    bands = [slice(first, first + band) for first in range(0, rows, band)]
+    ahead = NORM_CHUNKS // 2
+    squares = [jnp.zeros((band, lanes), jnp.float32) for _ in bands]
     for c in range(NORM_CHUNKS):
         load_x(c).wait()
-        for first in range(c * chunk, (c + 1) * chunk, lanes):
-            x = x_scr[:, first : first + lanes].astype(jnp.float32)
-            squares += x * x
-    mean_sq = jnp.sum(squares, axis=-1, keepdims=True) / features
-    inverse = jnp.broadcast_to(lax.rsqrt(mean_sq + EPS), (rows, lanes))
+        if c >= ahead:
+            start_weights(c - ahead)
+        for index, row in enumerate(bands):
+            for first in range(c * chunk, (c + 1) * chunk, lanes):
+                x = x_scr[row, first : first + lanes].astype(jnp.float32)
+                squares[index] += x * x
+    for c in range(NORM_CHUNKS - ahead, NORM_CHUNKS):
+        start_weights(c)
+    inverse = []
+    for total in squares:
+        mean_sq = jnp.sum(total, axis=-1, keepdims=True) / features
+        inverse.append(jnp.broadcast_to(lax.rsqrt(mean_sq + EPS), (band, lanes)))
 
     def normalise(c):
-        for first in range(c * chunk, (c + 1) * chunk, lanes):
-            cols = slice(first, first + lanes)
-            x = x_scr[:, cols].astype(jnp.float32)
-            normed_scr[:, cols] = (x * inverse * gain_ref[:, cols]).astype(jnp.bfloat16)
+        for index, row in enumerate(bands):
+            for first in range(c * chunk, (c + 1) * chunk, lanes):
+                cols = slice(first, first + lanes)
+                x = x_scr[row, cols].astype(jnp.float32)
+                normed_scr[row, cols] = (x * inverse[index] * gain_ref[:, cols]).astype(jnp.bfloat16)
 
     normalise(0)
     for c in range(NORM_CHUNKS):
@@ -156,11 +167,25 @@
     )(normed, key_weight, value_weight)
 
 
-def attention_kernel(block, kv_heads, near, slot_ref, cut_ref, odd_ref, q_ref, own_ref, *refs):
-    out_ref = refs[-1]
-    straight, crossed = refs[:near], refs[near : 2 * near + 1]
+def attention_kernel(block, near, slot_ref, cut_ref, odd_ref, q_ref, *refs):
+    own_hbm, straight, crossed = refs[0], refs[1 : near + 1], refs[near + 1 : 2 * near + 2]
+    out_ref, kv_scr, sems = refs[-3:]
     depth = slot_ref.shape[1]
-    odd = odd_ref[0] == 1
+    kv_heads = kv_scr.shape[2] // (2 * HEAD_DIM)
+
+    @pl.when(pl.program_id(0) == 0)
+    def _():
+        copies = [pltpu.make_async_copy(own_hbm, kv_scr.at[depth], sems.at[0])]
+        for s, ref in enumerate(straight):
+            copies.append(pltpu.make_async_copy(ref, kv_scr.at[2 * s + 1], sems.at[s + 1]))
+        for s, ref in enumerate(crossed):
+            level = 2 * lax.rem(s + odd_ref[0] + near, near + 1)
+            copies.append(pltpu.make_async_copy(ref, kv_scr.at[level], sems.at[near + s + 1]))
+        for copy in copies:
+            copy.start()
+        for copy in copies:
+            copy.wait()
+
     per_group = q_ref.shape[1] // HEAD_DIM // kv_heads
     tile = 256
     together = tile // block
@@ -177,15 +202,10 @@
         pieces, masks = [], []
         for k in range(depth):
             rows = pl.ds(pl.multiple_of(slot_ref[here, k] * block, block), block)
-            if k % 2 == 1:
-                pieces.append(straight[k // 2][rows, :])
-            else:
-                low = crossed[k // 2][rows, :]
-                high = crossed[min(k // 2 + 1, near)][rows, :]
-                pieces.append(jnp.where(odd, low, high))
+            pieces.append(kv_scr[k, rows, :])
             unseen = (lane == 0) & (token >= cut_ref[here, k])
             masks.append(jnp.where(unseen, MASKED, 0.0).astype(jnp.bfloat16))
-        pieces.append(own_ref[pl.ds(pl.multiple_of(here * block, block), block), :])
+        pieces.append(kv_scr[depth, pl.ds(pl.multiple_of(here * block, block), block), :])
         masks.append(own_mask)
         return jnp.concatenate(pieces, axis=0), jnp.concatenate(masks, axis=0)
 
@@ -237,24 +257,30 @@
     block = rows // blocks
     wide = features // UNITS
     near = len(straight)
-    kv_heads = own.shape[1] // (2 * HEAD_DIM)
-    whole = pl.BlockSpec(own.shape, lambda b, *_: (0, 0), pipeline_mode=pl.Buffered(1))
+    held = pl.BlockSpec(memory_space=pltpu.HBM)
     part = pl.BlockSpec((BLOCKS_PER_STEP * block, wide), lambda b, *_: (b, unit))
     operands = [slots, cuts, odd, queries, own, *straight, *crossed]
-    in_specs = [part] + [whole] * (1 + near + len(crossed))
+    in_specs = [part] + [held] * (1 + near + len(crossed))
     aliases = {}
     if previous is not None:
         aliases = {len(operands): 0}
         operands.append(previous)
-        in_specs.append(pl.BlockSpec(memory_space=pl.ANY))
+        in_specs.append(held)
     return pl.pallas_call(
-        functools.partial(attention_kernel, block, kv_heads, near),
+        functools.partial(attention_kernel, block, near),
         grid_spec=pltpu.PrefetchScalarGridSpec(
-            num_scalar_prefetch=3, grid=(blocks // BLOCKS_PER_STEP,), in_specs=in_specs, out_specs=part
+            num_scalar_prefetch=3,
+            grid=(blocks // BLOCKS_PER_STEP,),
+            in_specs=in_specs,
+            out_specs=part,
+            scratch_shapes=[
+                pltpu.VMEM((depth + 1, *own.shape), own.dtype),
+                pltpu.SemaphoreType.DMA((depth + 1,)),
+            ],
         ),
         out_shape=jax.ShapeDtypeStruct((rows, features), jnp.bfloat16),
         input_output_aliases=aliases,
-        compiler_params=pltpu.CompilerParams(vmem_limit_bytes=24 * MIB),
+        compiler_params=pltpu.CompilerParams(vmem_limit_bytes=57 * MIB),
         cost_estimate=pl.CostEstimate(
             flops=4 * rows * wide * (depth + 1) * block,
             bytes_accessed=8 * MIB,
@@ -276,37 +302,63 @@
     odd = (lax.axis_index("node") // chains % 2).astype(jnp.int32).reshape(1)
     slots = jnp.where(anc_ids >= 0, anc_ids % blocks, 0)
 
-    def shifted(array, distance, least=0):
-        shift = 2 * distance * chains
-        pairs = [(i, i + shift) for i in range(size) if i + shift < size and half[i] >= least]
-        return lax.ppermute(array, "node", pairs)
-
     normed, first = norm_project(hidden, norm_gain, key_weight, value_weight)
     own = [first] + [project(normed, key_weight, value_weight, unit) for unit in range(1, UNITS)]
     def after(array, *earlier):
         return lax.optimization_barrier((array, *earlier))[0]
 
-    straight = [[] for _ in range(UNITS)]
-    crossed = [[] for _ in range(UNITS)]
+    straight = [{} for _ in range(UNITS)]
+    crossed = [{} for _ in range(UNITS)]
+
+    def step_across(s, unit, settled):
+        source = own[unit] if s == 0 else straight[unit][s]
+        both_ways = unit == UNITS - 1 and s == 0
+        pairs = [
+            (i, other[i])
+            for i in range(size)
+            if half[i] >= s and (s > 0 or even[i] or (both_ways and half[i] == 0))
+        ]
+        crossed[unit][s] = lax.ppermute(after(source, *settled), "node", pairs)
+        return crossed[unit][s]
+
+    def step_along(s, unit, settled):
+        source = own[unit] if s == 1 else straight[unit][s - 1]
+        shift = 2 * chains
+        pairs = [(i, i + shift) for i in range(size - shift) if half[i] >= s - 1]
+        straight[unit][s] = lax.ppermute(after(source, *settled), "node", pairs)
+        return straight[unit][s]
+
+    def step_down(unit, settled):
+        shift = 2 * near * chains
+        pairs = [(i, i + shift) for i in range(size - shift)]
+        crossed[unit][near] = lax.ppermute(after(crossed[unit][0], *settled), "node", pairs)
+        return crossed[unit][near]
+
+    early, late = range(UNITS)
+    across = [(s, unit) for s in range(near - 1) for unit in (early, late)]
+    across += [(near - 1, early), (near, early), (near - 1, late)]
+    along = [(s, unit) for s in range(1, near + 1) for unit in (early, late)]
     waves = []
-    for s in range(near + 1):
-        for unit in range(UNITS):
-            settled = waves[-2] if len(waves) >= 2 else ()
-            source = own[unit] if s == 0 else straight[unit][s - 1]
-            pairs = [(i, other[i]) for i in range(size) if (half[i] >= s if s else even[i])]
-            crossed[unit].append(lax.ppermute(after(source, *settled), "node", pairs))
-            wave = [crossed[unit][-1]]
-            if s < near:
-                ahead = after(own[unit] if s < 2 else straight[unit][-1], *settled)
-                straight[unit].append(
-                    shifted(ahead, s + 1) if s < 2 else shifted(ahead, 1, s)
-                )
-                wave.append(straight[unit][-1])
-            waves.append(wave)
+    for index, (s, unit) in enumerate(across):
+        settled = waves[-2] if len(waves) >= 2 else ()
+        wave = [step_across(s, unit, settled)]
+        if index < len(along):
+            wave.append(step_along(*along[index], settled))
+        else:
+            wave.append(step_down(late, settled))
+        waves.append(wave)
     result = None
     for unit in range(UNITS):
         result = attention(
-            slots, anc_cut, odd, queries, own[unit], straight[unit], crossed[unit], unit, result
+            slots,
+            anc_cut,
+            odd,
+            queries,
+            own[unit],
+            [straight[unit][s] for s in range(1, near + 1)],
+            [crossed[unit][s] for s in range(near + 1)],
+            unit,
+            result,
         )
     return result
 

time: 149 us -> 123 us (0.83)
  waiting for transfers between devices: 66.9 us -> 46.7 us
  local copies, waits for them, and re-layouts: 8.29 us -> 0.04 us
    ppermute x14, waiting for transfers between devices: 66.9 us -> 46.7 us  [the longest x6 27.3 us: step_along(): straight[unit][s] = lax.ppermute(after(source, *settled), 'node', pairs)]
    unnamed x30 -> x20, local copies, waits for them, and re-layouts: 8.29 us -> 0.04 us
    pallas_call x2, Pallas kernels: 22.3 us -> 26.5 us  [attention(): pl.pallas_call(functools.partial(attention_kernel, block, near), grid_spe...]
    pallas_call x1, Pallas kernels: 16.8 us -> 13.3 us  [norm_project(): pl.pallas_call(norm_project_kernel, in_specs=[remote, whole, remote, remo...]
  transfers between devices with their start and end apart: 14 -> 14, of which waited for: 9 -> 9; matrix products, arithmetic and copies ran while one was open for 0% -> 0% of each run, Pallas kernels for 14% -> 18%
where the time goes in v4:
time: 123 us; the launch traced here: 122 us
  Pallas kernels  49 us (40%)
  waiting for transfers between devices  46.7 us (38%)
  starting transfers between devices  25.6 us (21%)
    ppermute x6, waiting for transfers between devices, step_along(): straight[unit][s] = lax.ppermute(after(source, *settled), 'node', pairs)  27.3 us
    pallas_call x2, Pallas kernels, attention(): pl.pallas_call(functools.partial(attention_kernel, block, near), grid_spe...  26.5 us
    ppermute x7, waiting for transfers between devices, step_across(): crossed[unit][s] = lax.ppermute(after(source, *settled), 'node', pairs)  19.4 us
    ppermute x7, starting transfers between devices, step_across(): crossed[unit][s] = lax.ppermute(after(source, *settled), 'node', pairs)  16.5 us
    pallas_call x1, Pallas kernels, norm_project(): pl.pallas_call(norm_project_kernel, in_specs=[remote, whole, remote, remo...  13.3 us
    pallas_call x1, Pallas kernels, project(): pl.pallas_call(project_kernel, grid=(CHUNKS,), in_specs=[pl.BlockSpec((ro...  9.27 us
    ppermute x6, starting transfers between devices, step_along(): straight[unit][s] = lax.ppermute(after(source, *settled), 'node', pairs)  7.74 us
  transfers between devices with their start and end apart: 14, of which 9 were waited for; matrix products, arithmetic and copies ran while one was open for 0% of the time, Pallas kernels for 18%

profile of v4, /device:TPU:24, one launch (start us, length us, event | category | flops | bytes accessed | tf_op | source)
XLA Modules:
  0.0 122.4 jit_solution(9266310180025471665)
XLA Ops:
  0.0 13.3 %norm_project.1 = (bf16[512,8192]{1,0:T(8,128)(2,1)}, bf16[512,512]{1,0:T(8,128)(2,1)}) custom-call(bf16[512,8192]{1,0:T(8,128)(2,1)} %x_hbm.1, f32[1,8192]{1,0:T(1,128)} %bitcast.2, bf16[8192,512]{1,0:T(8,128)(2,1)} %key_ref.1, bf16[8192,512]{1,0:T(8,128)(2,1)} %value_ref.1), custom_call_target="tpu_custom_call" | custom-call | flops 4294967296 | bytes 25165824 | tf_op jit(solution)/shard_map/norm_project/pallas_call | solution.py:109
  13.3 3.5 %collective-permute-start.6 = (bf16[512,512]{1,0:T(8,128)(2,1)}, bf16[512,512]{1,0:T(8,128)(2,1)S(1)}, u32[]{:S(2)}, u32[]{:S(2)}) collective-permute-start(bf16[512,512]{1,0:T(8,128)(2,1)} %get-tuple-element.17.refs_0_), channel_id=1, source_target_pairs={{0,2},{1,3},{4,6},{5,7},{8,10},{9,11},{12,14},{13,15},{16,18},{17,... | collective-permute-start | bytes 1572872 | tf_op jit(solution)/shard_map/ppermute | solution.py:321
  16.7 1.3 %collective-permute-start.5 = (bf16[512,512]{1,0:T(8,128)(2,1)}, bf16[512,512]{1,0:T(8,128)(2,1)S(1)}, u32[]{:S(2)}, u32[]{:S(2)}) collective-permute-start(bf16[512,512]{1,0:T(8,128)(2,1)} %get-tuple-element.17.refs_0_), channel_id=1, source_target_pairs={{0,4},{1,5},{2,6},{3,7},{4,8},{5,9},{6,10},{7,11},{8,12},{9,13},{1... | collective-permute-start | bytes 1572872 | tf_op jit(solution)/shard_map/ppermute | solution.py:328
  18.0 0.0 copy-start.9
  18.0 9.3 %project.1.refs_0_ = bf16[512,512]{1,0:T(8,128)(2,1)} custom-call(bf16[512,8192]{1,0:T(8,128)(2,1)} %get-tuple-element.14.normed_ref, bf16[8192,512]{1,0:T(8,128)(2,1)} %key_ref.1, bf16[8192,512]{1,0:T(8,128)(2,1)} %value_ref.1), custom_call_target="tpu_custom_call" | custom-call | flops 4294967296 | bytes 16777216 | tf_op jit(solution)/shard_map/project/pallas_call | solution.py:155
  27.3 1.3 %collective-permute-start.1 = (bf16[512,512]{1,0:T(8,128)(2,1)}, bf16[512,512]{1,0:T(8,128)(2,1)S(1)}, u32[]{:S(2)}, u32[]{:S(2)}) collective-permute-start(bf16[512,512]{1,0:T(8,128)(2,1)} %project.1.refs_0_), channel_id=1, source_target_pairs={{0,2},{1,3},{2,0},{3,1},{4,6},{5,7},{8,10},{9,11},{12,14},{13,15},... | collective-permute-start | bytes 1572872 | tf_op jit(solution)/shard_map/ppermute | solution.py:321
  28.6 1.3 %collective-permute-start = (bf16[512,512]{1,0:T(8,128)(2,1)}, bf16[512,512]{1,0:T(8,128)(2,1)S(1)}, u32[]{:S(2)}, u32[]{:S(2)}) collective-permute-start(bf16[512,512]{1,0:T(8,128)(2,1)} %project.1.refs_0_), channel_id=1, source_target_pairs={{0,4},{1,5},{2,6},{3,7},{4,8},{5,9},{6,10},{7,11},{8,12},{9,13},{1... | collective-permute-start | bytes 1572872 | tf_op jit(solution)/shard_map/ppermute | solution.py:328
  29.9 0.0 collective-permute-done.6.refs_4_
  29.9 0.0 copy-start.2
  29.9 2.3 %collective-permute-done.5.refs_1_ = bf16[512,512]{1,0:T(8,128)(2,1)S(1)} collective-permute-done((bf16[512,512]{1,0:T(8,128)(2,1)}, bf16[512,512]{1,0:T(8,128)(2,1)S(1)}, u32[]{:S(2)}, u32[]{:S(2)}) %collective-permute-start.5) | collective-permute-done | bytes 524320 | tf_op jit(solution)/shard_map/ppermute | solution.py:328
  32.2 0.0 copy-start.3
  32.2 1.9 %collective-permute-start.8 = (bf16[512,512]{1,0:T(8,128)(2,1)S(1)}, bf16[512,512]{1,0:T(8,128)(2,1)S(1)}, u32[]{:S(2)}, u32[]{:S(2)}) collective-permute-start(bf16[512,512]{1,0:T(8,128)(2,1)S(1)} %collective-permute-done.5.refs_1_), channel_id=1, source_target_pairs={{4,6},{5,7},{6,4},{7,5},{8,10},{9,11},{10,8},{11,9},{12,14},{13,15... | collective-permute-start | bytes 1572872 | tf_op jit(solution)/shard_map/ppermute | solution.py:321
  34.1 1.3 %collective-permute-start.7 = (bf16[512,512]{1,0:T(8,128)(2,1)S(1)}, bf16[512,512]{1,0:T(8,128)(2,1)S(1)}, u32[]{:S(2)}, u32[]{:S(2)}) collective-permute-start(bf16[512,512]{1,0:T(8,128)(2,1)S(1)} %collective-permute-done.5.refs_1_), channel_id=1, source_target_pairs={{4,8},{5,9},{6,10},{7,11},{8,12},{9,13},{10,14},{11,15},{20,24},{2... | collective-permute-start | bytes 1572872 | tf_op jit(solution)/shard_map/ppermute | solution.py:328
  35.4 5.8 %collective-permute-done.1.refs_4_ = bf16[512,512]{1,0:T(8,128)(2,1)S(1)} collective-permute-done((bf16[512,512]{1,0:T(8,128)(2,1)}, bf16[512,512]{1,0:T(8,128)(2,1)S(1)}, u32[]{:S(2)}, u32[]{:S(2)}) %collective-permute-start.1) | collective-permute-done | bytes 524320 | tf_op jit(solution)/shard_map/ppermute | solution.py:321
  41.2 0.0 copy-start
  41.2 5.0 %collective-permute-done.refs_1_ = bf16[512,512]{1,0:T(8,128)(2,1)S(1)} collective-permute-done((bf16[512,512]{1,0:T(8,128)(2,1)}, bf16[512,512]{1,0:T(8,128)(2,1)S(1)}, u32[]{:S(2)}, u32[]{:S(2)}) %collective-permute-start) | collective-permute-done | bytes 524320 | tf_op jit(solution)/shard_map/ppermute | solution.py:328
  46.2 1.9 %collective-permute-start.3 = (bf16[512,512]{1,0:T(8,128)(2,1)S(1)}, bf16[512,512]{1,0:T(8,128)(2,1)S(1)}, u32[]{:S(2)}, u32[]{:S(2)}) collective-permute-start(bf16[512,512]{1,0:T(8,128)(2,1)S(1)} %collective-permute-done.refs_1_), channel_id=1, source_target_pairs={{4,6},{5,7},{6,4},{7,5},{8,10},{9,11},{10,8},{11,9},{12,14},{13,15... | collective-permute-start | bytes 1572872 | tf_op jit(solution)/shard_map/ppermute | solution.py:321
  48.1 1.3 %collective-permute-start.2 = (bf16[512,512]{1,0:T(8,128)(2,1)S(1)}, bf16[512,512]{1,0:T(8,128)(2,1)S(1)}, u32[]{:S(2)}, u32[]{:S(2)}) collective-permute-start(bf16[512,512]{1,0:T(8,128)(2,1)S(1)} %collective-permute-done.refs_1_), channel_id=1, source_target_pairs={{4,8},{5,9},{6,10},{7,11},{8,12},{9,13},{10,14},{11,15},{20,24},{2... | collective-permute-start | bytes 1572872 | tf_op jit(solution)/shard_map/ppermute | solution.py:328
  49.4 2.9 %collective-permute-done.8.refs_5_ = bf16[512,512]{1,0:T(8,128)(2,1)S(1)} collective-permute-done((bf16[512,512]{1,0:T(8,128)(2,1)S(1)}, bf16[512,512]{1,0:T(8,128)(2,1)S(1)}, u32[]{:S(2)}, u32[]{:S(2)}) %collective-permute-start.8) | collective-permute-done | bytes 524320 | tf_op jit(solution)/shard_map/ppermute | solution.py:321
  52.4 5.1 %collective-permute-done.7.refs_2_ = bf16[512,512]{1,0:T(8,128)(2,1)S(1)} collective-permute-done((bf16[512,512]{1,0:T(8,128)(2,1)S(1)}, bf16[512,512]{1,0:T(8,128)(2,1)S(1)}, u32[]{:S(2)}, u32[]{:S(2)}) %collective-permute-start.7) | collective-permute-done | bytes 524320 | tf_op jit(solution)/shard_map/ppermute | solution.py:328
  57.4 1.3 %collective-permute-start.10 = (bf16[512,512]{1,0:T(8,128)(2,1)S(1)}, bf16[512,512]{1,0:T(8,128)(2,1)}, u32[]{:S(2)}, u32[]{:S(2)}) collective-permute-start(bf16[512,512]{1,0:T(8,128)(2,1)S(1)} %collective-permute-done.7.refs_2_), channel_id=1, source_target_pairs={{8,12},{9,13},{10,14},{11,15},{24,28},{25,29},{26,30},{27,31}} | collective-permute-start | bytes 1572872 | tf_op jit(solution)/shard_map/ppermute | solution.py:328
  58.7 1.9 %collective-permute-start.9 = (bf16[512,512]{1,0:T(8,128)(2,1)S(1)}, bf16[512,512]{1,0:T(8,128)(2,1)S(1)}, u32[]{:S(2)}, u32[]{:S(2)}) collective-permute-start(bf16[512,512]{1,0:T(8,128)(2,1)S(1)} %collective-permute-done.7.refs_2_), channel_id=1, source_target_pairs={{8,10},{9,11},{10,8},{11,9},{12,14},{13,15},{14,12},{15,13},{24,26... | collective-permute-start | bytes 1572872 | tf_op jit(solution)/shard_map/ppermute | solution.py:321
  60.7 2.9 %collective-permute-done.3.refs_5_ = bf16[512,512]{1,0:T(8,128)(2,1)S(1)} collective-permute-done((bf16[512,512]{1,0:T(8,128)(2,1)S(1)}, bf16[512,512]{1,0:T(8,128)(2,1)S(1)}, u32[]{:S(2)}, u32[]{:S(2)}) %collective-permute-start.3) | collective-permute-done | bytes 524320 | tf_op jit(solution)/shard_map/ppermute | solution.py:321
  63.6 5.1 %collective-permute-done.2.refs_2_ = bf16[512,512]{1,0:T(8,128)(2,1)S(1)} collective-permute-done((bf16[512,512]{1,0:T(8,128)(2,1)S(1)}, bf16[512,512]{1,0:T(8,128)(2,1)S(1)}, u32[]{:S(2)}, u32[]{:S(2)}) %collective-permute-start.2) | collective-permute-done | bytes 524320 | tf_op jit(solution)/shard_map/ppermute | solution.py:328
  68.7 9.9 %collective-permute-done.10.refs_3_ = bf16[512,512]{1,0:T(8,128)(2,1)} collective-permute-done((bf16[512,512]{1,0:T(8,128)(2,1)S(1)}, bf16[512,512]{1,0:T(8,128)(2,1)}, u32[]{:S(2)}, u32[]{:S(2)}) %collective-permute-start.10) | collective-permute-done | bytes 524320 | tf_op jit(solution)/shard_map/ppermute | solution.py:328
  78.6 1.9 %collective-permute-start.13 = (bf16[512,512]{1,0:T(8,128)(2,1)}, bf16[512,512]{1,0:T(8,128)(2,1)}, u32[]{:S(2)}, u32[]{:S(2)}) collective-permute-start(bf16[512,512]{1,0:T(8,128)(2,1)} %collective-permute-done.10.refs_3_), channel_id=1, source_target_pairs={{12,14},{13,15},{14,12},{15,13},{28,30},{29,31},{30,28},{31,29}} | collective-permute-start | bytes 1572872 | tf_op jit(solution)/shard_map/ppermute | solution.py:321
  80.5 1.3 %collective-permute-start.4 = (bf16[512,512]{1,0:T(8,128)(2,1)S(1)}, bf16[512,512]{1,0:T(8,128)(2,1)}, u32[]{:S(2)}, u32[]{:S(2)}) collective-permute-start(bf16[512,512]{1,0:T(8,128)(2,1)S(1)} %collective-permute-done.2.refs_2_), channel_id=1, source_target_pairs={{8,12},{9,13},{10,14},{11,15},{24,28},{25,29},{26,30},{27,31}} | collective-permute-start | bytes 1572872 | tf_op jit(solution)/shard_map/ppermute | solution.py:328
  81.8 0.0 collective-permute-done.9.refs_6_
  81.8 0.0 copy-done.6
  81.8 0.0 copy-start.8
  81.8 1.3 %collective-permute-start.12 = (bf16[512,512]{1,0:T(8,128)(2,1)S(1)}, bf16[512,512]{1,0:T(8,128)(2,1)}, u32[]{:S(2)}, u32[]{:S(2)}) collective-permute-start(bf16[512,512]{1,0:T(8,128)(2,1)S(1)} %collective-permute-done.1.refs_4_), channel_id=1, source_target_pairs={{0,12},{1,13},{2,14},{3,15},{16,28},{17,29},{18,30},{19,31}} | collective-permute-start | bytes 1572872 | tf_op jit(solution)/shard_map/ppermute | solution.py:334
  83.1 0.0 copy-done.7
  83.1 4.1 %collective-permute-start.11 = (bf16[512,512]{1,0:T(8,128)(2,1)S(1)}, bf16[512,512]{1,0:T(8,128)(2,1)}, u32[]{:S(2)}, u32[]{:S(2)}) collective-permute-start(bf16[512,512]{1,0:T(8,128)(2,1)S(1)} %collective-permute-done.2.refs_2_), channel_id=1, source_target_pairs={{8,10},{9,11},{10,8},{11,9},{12,14},{13,15},{14,12},{15,13},{24,26... | collective-permute-start | bytes 1572872 | tf_op jit(solution)/shard_map/ppermute | solution.py:321
  87.2 0.0 copy-done.8
  87.3 0.0 copy-done.9
  87.3 0.6 fusion.1.slot_ref
  87.9 7.7 %collective-permute-done.13.refs_7_ = bf16[512,512]{1,0:T(8,128)(2,1)} collective-permute-done((bf16[512,512]{1,0:T(8,128)(2,1)}, bf16[512,512]{1,0:T(8,128)(2,1)}, u32[]{:S(2)}, u32[]{:S(2)}) %collective-permute-start.13) | collective-permute-done | bytes 524320 | tf_op jit(solution)/shard_map/ppermute | solution.py:321
  95.6 0.0 copy-done.2
  95.6 0.0 copy-done.3
  95.6 13.2 %attention.2.refs_8_ = bf16[512,4096]{1,0:T(8,128)(2,1)} custom-call(s32[8,7]{1,0:T(8,128)} %fusion.1.slot_ref, s32[8,7]{1,0:T(8,128)} %cut_ref.3, s32[1]{0:T(128)} %bitcast.odd_ref, bf16[512,4096]{1,0:T(8,128)(2,1)} %q_ref.3, bf16[512,512]{1,0:T(8,128)(2,1)} %get-tuple-element.17.refs_0_, bf16[512,512]{1,0:T(8,128)(2,1)} %copy-done.3, ...), custom_call_target="tpu_custom_call" | custom-call | flops 2147483648 | bytes 8388608 | tf_op jit(solution)/shard_map/attention/pallas_call | solution.py:269
  108.9 0.0 collective-permute-done.4.refs_3_
  108.9 0.0 collective-permute-done.12.refs_7_
  108.9 0.0 collective-permute-done.11.refs_6_
  108.9 0.0 copy-done
  108.9 0.0 copy-done.1
  108.9 0.0 copy-done.4
  108.9 0.0 copy-done.5
  108.9 13.3 %attention.3 = bf16[512,4096]{1,0:T(8,128)(2,1)} custom-call(s32[8,7]{1,0:T(8,128)} %fusion.1.slot_ref, s32[8,7]{1,0:T(8,128)} %cut_ref.3, s32[1]{0:T(128)} %bitcast.odd_ref, bf16[512,4096]{1,0:T(8,128)(2,1)} %q_ref.3, bf16[512,512]{1,0:T(8,128)(2,1)} %project.1.refs_0_, bf16[512,512]{1,0:T(8,128)(2,1)} %copy-done.1, ...), custom_call_target="tpu_custom_call", output_to_operand_aliasing={{}: (12, {})} | custom-call | flops 2147483648 | bytes 8388608 | tf_op jit(solution)/shard_map/attention/pallas_call | solution.py:269
  (5 shorter events, 0.0 us)
Async XLA Ops:
  13.3 16.7 %collective-permute-start.6 = (bf16[512,512]{1,0:T(8,128)(2,1)}, bf16[512,512]{1,0:T(8,128)(2,1)S(1)}, u32[]{:S(2)}, u32[]{:S(2)}) collective-permute-start(bf16[512,512]{1,0:T(8,128)(2,1)} %get-tuple-element.17.refs_0_), channel_id=1, source_target_pairs={{0,2},{1,3},{4,6},{5,7},{8,10},{9,11},{12,14},{13,15},{16,18},{17,... | collective-permute-start | bytes 1572872 | tf_op jit(solution)/shard_map/ppermute | solution.py:321
  16.7 15.5 %collective-permute-start.5 = (bf16[512,512]{1,0:T(8,128)(2,1)}, bf16[512,512]{1,0:T(8,128)(2,1)S(1)}, u32[]{:S(2)}, u32[]{:S(2)}) collective-permute-start(bf16[512,512]{1,0:T(8,128)(2,1)} %get-tuple-element.17.refs_0_), channel_id=1, source_target_pairs={{0,4},{1,5},{2,6},{3,7},{4,8},{5,9},{6,10},{7,11},{8,12},{9,13},{1... | collective-permute-start | bytes 1572872 | tf_op jit(solution)/shard_map/ppermute | solution.py:328
  18.0 69.2 %copy-start.9 = (s32[8,7]{1,0:T(8,128)S(1)}, s32[8,7]{1,0:T(8,128)}, u32[]{:S(2)}) copy-start(s32[8,7]{1,0:T(8,128)} %param.12) | copy-start | bytes 676
  27.3 13.9 %collective-permute-start.1 = (bf16[512,512]{1,0:T(8,128)(2,1)}, bf16[512,512]{1,0:T(8,128)(2,1)S(1)}, u32[]{:S(2)}, u32[]{:S(2)}) collective-permute-start(bf16[512,512]{1,0:T(8,128)(2,1)} %project.1.refs_0_), channel_id=1, source_target_pairs={{0,2},{1,3},{2,0},{3,1},{4,6},{5,7},{8,10},{9,11},{12,14},{13,15},... | collective-permute-start | bytes 1572872 | tf_op jit(solution)/shard_map/ppermute | solution.py:321
  28.6 17.6 %collective-permute-start = (bf16[512,512]{1,0:T(8,128)(2,1)}, bf16[512,512]{1,0:T(8,128)(2,1)S(1)}, u32[]{:S(2)}, u32[]{:S(2)}) collective-permute-start(bf16[512,512]{1,0:T(8,128)(2,1)} %project.1.refs_0_), channel_id=1, source_target_pairs={{0,4},{1,5},{2,6},{3,7},{4,8},{5,9},{6,10},{7,11},{8,12},{9,13},{1... | collective-permute-start | bytes 1572872 | tf_op jit(solution)/shard_map/ppermute | solution.py:328
  29.9 65.7 %copy-start.2 = (bf16[512,512]{1,0:T(8,128)(2,1)}, bf16[512,512]{1,0:T(8,128)(2,1)S(1)}, u32[]{:S(2)}) copy-start(bf16[512,512]{1,0:T(8,128)(2,1)S(1)} %collective-permute-done.6.refs_4_) | copy-start | bytes 1572868
  32.2 63.4 %copy-start.3 = (bf16[512,512]{1,0:T(8,128)(2,1)}, bf16[512,512]{1,0:T(8,128)(2,1)S(1)}, u32[]{:S(2)}) copy-start(bf16[512,512]{1,0:T(8,128)(2,1)S(1)} %collective-permute-done.5.refs_1_) | copy-start | bytes 1572868
  32.2 20.1 %collective-permute-start.8 = (bf16[512,512]{1,0:T(8,128)(2,1)S(1)}, bf16[512,512]{1,0:T(8,128)(2,1)S(1)}, u32[]{:S(2)}, u32[]{:S(2)}) collective-permute-start(bf16[512,512]{1,0:T(8,128)(2,1)S(1)} %collective-permute-done.5.refs_1_), channel_id=1, source_target_pairs={{4,6},{5,7},{6,4},{7,5},{8,10},{9,11},{10,8},{11,9},{12,14},{13,15... | collective-permute-start | bytes 1572872 | tf_op jit(solution)/shard_map/ppermute | solution.py:321
  34.1 23.3 %collective-permute-start.7 = (bf16[512,512]{1,0:T(8,128)(2,1)S(1)}, bf16[512,512]{1,0:T(8,128)(2,1)S(1)}, u32[]{:S(2)}, u32[]{:S(2)}) collective-permute-start(bf16[512,512]{1,0:T(8,128)(2,1)S(1)} %collective-permute-done.5.refs_1_), channel_id=1, source_target_pairs={{4,8},{5,9},{6,10},{7,11},{8,12},{9,13},{10,14},{11,15},{20,24},{2... | collective-permute-start | bytes 1572872 | tf_op jit(solution)/shard_map/ppermute | solution.py:328
  41.2 67.7 %copy-start = (bf16[512,512]{1,0:T(8,128)(2,1)}, bf16[512,512]{1,0:T(8,128)(2,1)S(1)}, u32[]{:S(2)}) copy-start(bf16[512,512]{1,0:T(8,128)(2,1)S(1)} %collective-permute-done.1.refs_4_) | copy-start | bytes 1572868
  46.2 62.7 %copy-start.1 = (bf16[512,512]{1,0:T(8,128)(2,1)}, bf16[512,512]{1,0:T(8,128)(2,1)S(1)}, u32[]{:S(2)}) copy-start(bf16[512,512]{1,0:T(8,128)(2,1)S(1)} %collective-permute-done.refs_1_) | copy-start | bytes 1572868
  46.2 17.4 %collective-permute-start.3 = (bf16[512,512]{1,0:T(8,128)(2,1)S(1)}, bf16[512,512]{1,0:T(8,128)(2,1)S(1)}, u32[]{:S(2)}, u32[]{:S(2)}) collective-permute-start(bf16[512,512]{1,0:T(8,128)(2,1)S(1)} %collective-permute-done.refs_1_), channel_id=1, source_target_pairs={{4,6},{5,7},{6,4},{7,5},{8,10},{9,11},{10,8},{11,9},{12,14},{13,15... | collective-permute-start | bytes 1572872 | tf_op jit(solution)/shard_map/ppermute | solution.py:321
  48.1 20.6 %collective-permute-start.2 = (bf16[512,512]{1,0:T(8,128)(2,1)S(1)}, bf16[512,512]{1,0:T(8,128)(2,1)S(1)}, u32[]{:S(2)}, u32[]{:S(2)}) collective-permute-start(bf16[512,512]{1,0:T(8,128)(2,1)S(1)} %collective-permute-done.refs_1_), channel_id=1, source_target_pairs={{4,8},{5,9},{6,10},{7,11},{8,12},{9,13},{10,14},{11,15},{20,24},{2... | collective-permute-start | bytes 1572872 | tf_op jit(solution)/shard_map/ppermute | solution.py:328
  52.4 29.4 %copy-start.6 = (bf16[512,512]{1,0:T(8,128)(2,1)}, bf16[512,512]{1,0:T(8,128)(2,1)S(1)}, u32[]{:S(2)}) copy-start(bf16[512,512]{1,0:T(8,128)(2,1)S(1)} %collective-permute-done.8.refs_5_) | copy-start | bytes 1572868
  57.4 25.7 %copy-start.7 = (bf16[512,512]{1,0:T(8,128)(2,1)}, bf16[512,512]{1,0:T(8,128)(2,1)S(1)}, u32[]{:S(2)}) copy-start(bf16[512,512]{1,0:T(8,128)(2,1)S(1)} %collective-permute-done.7.refs_2_) | copy-start | bytes 1572868
  57.4 21.1 %collective-permute-start.10 = (bf16[512,512]{1,0:T(8,128)(2,1)S(1)}, bf16[512,512]{1,0:T(8,128)(2,1)}, u32[]{:S(2)}, u32[]{:S(2)}) collective-permute-start(bf16[512,512]{1,0:T(8,128)(2,1)S(1)} %collective-permute-done.7.refs_2_), channel_id=1, source_target_pairs={{8,12},{9,13},{10,14},{11,15},{24,28},{25,29},{26,30},{27,31}} | collective-permute-start | bytes 1572872 | tf_op jit(solution)/shard_map/ppermute | solution.py:328
  58.7 23.0 %collective-permute-start.9 = (bf16[512,512]{1,0:T(8,128)(2,1)S(1)}, bf16[512,512]{1,0:T(8,128)(2,1)S(1)}, u32[]{:S(2)}, u32[]{:S(2)}) collective-permute-start(bf16[512,512]{1,0:T(8,128)(2,1)S(1)} %collective-permute-done.7.refs_2_), channel_id=1, source_target_pairs={{8,10},{9,11},{10,8},{11,9},{12,14},{13,15},{14,12},{15,13},{24,26... | collective-permute-start | bytes 1572872 | tf_op jit(solution)/shard_map/ppermute | solution.py:321
  63.6 45.3 %copy-start.4 = (bf16[512,512]{1,0:T(8,128)(2,1)}, bf16[512,512]{1,0:T(8,128)(2,1)S(1)}, u32[]{:S(2)}) copy-start(bf16[512,512]{1,0:T(8,128)(2,1)S(1)} %collective-permute-done.3.refs_5_) | copy-start | bytes 1572868
  68.7 40.3 %copy-start.5 = (bf16[512,512]{1,0:T(8,128)(2,1)}, bf16[512,512]{1,0:T(8,128)(2,1)S(1)}, u32[]{:S(2)}) copy-start(bf16[512,512]{1,0:T(8,128)(2,1)S(1)} %collective-permute-done.2.refs_2_) | copy-start | bytes 1572868
  78.6 17.1 %collective-permute-start.13 = (bf16[512,512]{1,0:T(8,128)(2,1)}, bf16[512,512]{1,0:T(8,128)(2,1)}, u32[]{:S(2)}, u32[]{:S(2)}) collective-permute-start(bf16[512,512]{1,0:T(8,128)(2,1)} %collective-permute-done.10.refs_3_), channel_id=1, source_target_pairs={{12,14},{13,15},{14,12},{15,13},{28,30},{29,31},{30,28},{31,29}} | collective-permute-start | bytes 1572872 | tf_op jit(solution)/shard_map/ppermute | solution.py:321
  80.5 28.4 %collective-permute-start.4 = (bf16[512,512]{1,0:T(8,128)(2,1)S(1)}, bf16[512,512]{1,0:T(8,128)(2,1)}, u32[]{:S(2)}, u32[]{:S(2)}) collective-permute-start(bf16[512,512]{1,0:T(8,128)(2,1)S(1)} %collective-permute-done.2.refs_2_), channel_id=1, source_target_pairs={{8,12},{9,13},{10,14},{11,15},{24,28},{25,29},{26,30},{27,31}} | collective-permute-start | bytes 1572872 | tf_op jit(solution)/shard_map/ppermute | solution.py:328
  81.8 5.4 %copy-start.8 = (bf16[512,512]{1,0:T(8,128)(2,1)}, bf16[512,512]{1,0:T(8,128)(2,1)S(1)}, u32[]{:S(2)}) copy-start(bf16[512,512]{1,0:T(8,128)(2,1)S(1)} %collective-permute-done.9.refs_6_) | copy-start | bytes 1572868
  81.8 27.1 %collective-permute-start.12 = (bf16[512,512]{1,0:T(8,128)(2,1)S(1)}, bf16[512,512]{1,0:T(8,128)(2,1)}, u32[]{:S(2)}, u32[]{:S(2)}) collective-permute-start(bf16[512,512]{1,0:T(8,128)(2,1)S(1)} %collective-permute-done.1.refs_4_), channel_id=1, source_target_pairs={{0,12},{1,13},{2,14},{3,15},{16,28},{17,29},{18,30},{19,31}} | collective-permute-start | bytes 1572872 | tf_op jit(solution)/shard_map/ppermute | solution.py:334
  83.1 25.8 %collective-permute-start.11 = (bf16[512,512]{1,0:T(8,128)(2,1)S(1)}, bf16[512,512]{1,0:T(8,128)(2,1)}, u32[]{:S(2)}, u32[]{:S(2)}) collective-permute-start(bf16[512,512]{1,0:T(8,128)(2,1)S(1)} %collective-permute-done.2.refs_2_), channel_id=1, source_target_pairs={{8,10},{9,11},{10,8},{11,9},{12,14},{13,15},{14,12},{15,13},{24,26... | collective-permute-start | bytes 1572872 | tf_op jit(solution)/shard_map/ppermute | solution.py:321

commit v5 on v4

--- a/solution.py
+++ b/solution.py
@@ -12,61 +12,55 @@
 MASKED = -1e30
 MIB = 1024 * 1024
 CHUNKS = 4
-NORM_CHUNKS = 8
-UNITS = 2
-BLOCKS_PER_STEP = 2
+LOADS = 8
+BLOCKS_PER_STEP = 4
 
 
 def norm_project_kernel(
     x_hbm, gain_ref, key_hbm, value_hbm, normed_hbm, kv_ref,
-    x_scr, key_scr, value_scr, normed_scr, acc_scr, x_sem, key_sem, value_sem, normed_sem,
+    x_scr, weight_scr, normed_scr, x_sem, key_sem, value_sem, normed_sem,
 ):
     rows, features = x_scr.shape
-    width = key_scr.shape[1]
-    chunk = features // NORM_CHUNKS
+    piece = features // LOADS
+    chunk = features // CHUNKS
     lanes = 128
 
-    def columns(c):
-        return slice(c * chunk, (c + 1) * chunk)
-
     def load_x(c):
-        return pltpu.make_async_copy(
-            x_hbm.at[:, columns(c)], x_scr.at[:, columns(c)], x_sem.at[c]
-        )
+        cols = slice(c * piece, (c + 1) * piece)
+        return pltpu.make_async_copy(x_hbm.at[:, cols], x_scr.at[:, cols], x_sem.at[c])
 
     def load_weights(c):
+        span = slice(c * chunk, (c + 1) * chunk)
+        head = pl.ds(0, HEAD_DIM)
         return [
             pltpu.make_async_copy(
-                hbm.at[columns(c), pl.ds(0, width)], scr.at[columns(c), :], sem.at[c]
-            )
-            for hbm, scr, sem in ((key_hbm, key_scr, key_sem), (value_hbm, value_scr, value_sem))
+                key_hbm.at[span, head], weight_scr.at[span, :HEAD_DIM], key_sem.at[c]
+            ),
+            pltpu.make_async_copy(
+                value_hbm.at[span, head], weight_scr.at[span, HEAD_DIM:], value_sem.at[c]
+            ),
         ]
 
     def store_normed(c):
+        cols = slice(c * chunk, (c + 1) * chunk)
         return pltpu.make_async_copy(
-            normed_scr.at[:, columns(c)], normed_hbm.at[:, columns(c)], normed_sem.at[c]
-        )
-
-    def start_weights(c):
-        for copy in load_weights(c):
-            copy.start()
-
-    for c in range(NORM_CHUNKS):
+            normed_scr.at[:, cols], normed_hbm.at[:, cols], normed_sem.at[c]
+        )
+
+    for c in range(LOADS):
         load_x(c).start()
     band = 128
     bands = [slice(first, first + band) for first in range(0, rows, band)]
-    ahead = NORM_CHUNKS // 2
     squares = [jnp.zeros((band, lanes), jnp.float32) for _ in bands]
-    for c in range(NORM_CHUNKS):
+    for c in range(LOADS):
         load_x(c).wait()
-        if c >= ahead:
-            start_weights(c - ahead)
+        if c >= LOADS - CHUNKS:
+            for copy in load_weights(c - LOADS + CHUNKS):
+                copy.start()
         for index, row in enumerate(bands):
-            for first in range(c * chunk, (c + 1) * chunk, lanes):
+            for first in range(c * piece, (c + 1) * piece, lanes):
                 x = x_scr[row, first : first + lanes].astype(jnp.float32)
                 squares[index] += x * x
-    for c in range(NORM_CHUNKS - ahead, NORM_CHUNKS):
-        start_weights(c)
     inverse = []
     for total in squares:
         mean_sq = jnp.sum(total, axis=-1, keepdims=True) / features
@@ -80,88 +74,86 @@
                 normed_scr[row, cols] = (x * inverse[index] * gain_ref[:, cols]).astype(jnp.bfloat16)
 
     normalise(0)
-    for c in range(NORM_CHUNKS):
+    total = None
+    for c in range(CHUNKS):
         for copy in load_weights(c):
             copy.wait()
         store_normed(c).start()
-        for part, weight in enumerate((key_scr, value_scr)):
-            cols = slice(part * width, (part + 1) * width)
-            term = jnp.dot(
-                normed_scr[:, columns(c)], weight[columns(c), :], preferred_element_type=jnp.float32
-            )
-            if c == 0:
-                acc_scr[:, cols] = term
-            elif c < NORM_CHUNKS - 1:
-                acc_scr[:, cols] += term
-            else:
-                kv_ref[:, cols] = (acc_scr[:, cols] + term).astype(jnp.bfloat16)
-        if c < NORM_CHUNKS - 1:
+        span = slice(c * chunk, (c + 1) * chunk)
+        term = jnp.dot(
+            normed_scr[:, span], weight_scr[span, :], preferred_element_type=jnp.float32
+        )
+        total = term if total is None else total + term
+        if c < CHUNKS - 1:
             normalise(c + 1)
-    for c in range(NORM_CHUNKS):
+    kv_ref[...] = total.astype(jnp.bfloat16)
+    for c in range(CHUNKS):
         store_normed(c).wait()
 
 
 def norm_project(hidden, gain, key_weight, value_weight):
     rows, features = hidden.shape
-    width = key_weight.shape[1] // UNITS
     whole = pl.BlockSpec(memory_space=pltpu.VMEM)
-    remote = pl.BlockSpec(memory_space=pl.ANY)
+    held = pl.BlockSpec(memory_space=pltpu.HBM)
     return pl.pallas_call(
         norm_project_kernel,
-        in_specs=[remote, whole, remote, remote],
-        out_specs=[remote, whole],
+        in_specs=[held, whole, held, held],
+        out_specs=[held, whole],
         out_shape=[
             jax.ShapeDtypeStruct((rows, features), jnp.bfloat16),
-            jax.ShapeDtypeStruct((rows, 2 * width), jnp.bfloat16),
+            jax.ShapeDtypeStruct((rows, 2 * HEAD_DIM), jnp.bfloat16),
         ],
         scratch_shapes=[
             pltpu.VMEM((rows, features), jnp.bfloat16),
-            pltpu.VMEM((features, width), jnp.bfloat16),
-            pltpu.VMEM((features, width), jnp.bfloat16),
+            pltpu.VMEM((features, 2 * HEAD_DIM), jnp.bfloat16),
             pltpu.VMEM((rows, features), jnp.bfloat16),
-            pltpu.VMEM((rows, 2 * width), jnp.float32),
-            pltpu.SemaphoreType.DMA((NORM_CHUNKS,)),
-            pltpu.SemaphoreType.DMA((NORM_CHUNKS,)),
-            pltpu.SemaphoreType.DMA((NORM_CHUNKS,)),
-            pltpu.SemaphoreType.DMA((NORM_CHUNKS,)),
+            pltpu.SemaphoreType.DMA((LOADS,)),
+            pltpu.SemaphoreType.DMA((CHUNKS,)),
+            pltpu.SemaphoreType.DMA((CHUNKS,)),
+            pltpu.SemaphoreType.DMA((CHUNKS,)),
         ],
         compiler_params=pltpu.CompilerParams(vmem_limit_bytes=57 * MIB),
         cost_estimate=pl.CostEstimate(
-            flops=4 * rows * features * width, bytes_accessed=24 * MIB, transcendentals=0
+            flops=4 * rows * features * HEAD_DIM, bytes_accessed=24 * MIB, transcendentals=0
         ),
         name="norm_project",
     )(hidden, gain.reshape(1, features), key_weight, value_weight)
 
 
-def project_kernel(normed_ref, key_ref, value_ref, kv_ref, acc_scr):
+def project_kernel(normed_ref, key_ref, value_ref, *refs):
+    acc_scr = refs[-1]
     step = pl.program_id(0)
-    width = key_ref.shape[1]
     normed = normed_ref[...]
-    for part, weight in enumerate((key_ref, value_ref)):
-        cols = slice(part * width, (part + 1) * width)
-        term = jnp.dot(normed, weight[...], preferred_element_type=jnp.float32)
-        acc_scr[:, cols] = jnp.where(step == 0, term, acc_scr[:, cols] + term)
+    for index in range(len(refs) - 1):
+        head = slice(index * HEAD_DIM, (index + 1) * HEAD_DIM)
+        weight = jnp.concatenate([key_ref[:, head], value_ref[:, head]], axis=1)
+        term = jnp.dot(normed, weight, preferred_element_type=jnp.float32)
+        acc_scr[index] = jnp.where(step == 0, term, acc_scr[index] + term)
 
     @pl.when(step == CHUNKS - 1)
     def _():
-        kv_ref[...] = acc_scr[...].astype(jnp.bfloat16)
-
-
-def project(normed, key_weight, value_weight, unit):
+        for index in range(len(refs) - 1):
+            refs[index][...] = acc_scr[index].astype(jnp.bfloat16)
+
+
+def project(normed, key_weight, value_weight, first, heads):
     rows, features = normed.shape
     chunk = features // CHUNKS
-    width = key_weight.shape[1] // UNITS
-    weight = pl.BlockSpec((chunk, width), lambda i: (i, unit))
+    weight = pl.BlockSpec((chunk, heads * HEAD_DIM), lambda i: (i, first // heads))
     return pl.pallas_call(
         project_kernel,
         grid=(CHUNKS,),
         in_specs=[pl.BlockSpec((rows, chunk), lambda i: (0, i)), weight, weight],
-        out_specs=pl.BlockSpec((rows, 2 * width), lambda i: (0, 0)),
-        out_shape=jax.ShapeDtypeStruct((rows, 2 * width), jnp.bfloat16),
-        scratch_shapes=[pltpu.VMEM((rows, 2 * width), jnp.float32)],
+        out_specs=[pl.BlockSpec((rows, 2 * HEAD_DIM), lambda i: (0, 0)) for _ in range(heads)],
+        out_shape=[
+            jax.ShapeDtypeStruct((rows, 2 * HEAD_DIM), jnp.bfloat16) for _ in range(heads)
+        ],
+        scratch_shapes=[pltpu.VMEM((heads, rows, 2 * HEAD_DIM), jnp.float32)],
         compiler_params=pltpu.CompilerParams(vmem_limit_bytes=57 * MIB),
         cost_estimate=pl.CostEstimate(
-            flops=4 * rows * features * width, bytes_accessed=16 * MIB, transcendentals=0
+            flops=4 * heads * rows * features * HEAD_DIM,
+            bytes_accessed=(8 + 4 * heads) * MIB,
+            transcendentals=0,
         ),
         name="project",
     )(normed, key_weight, value_weight)
@@ -251,11 +243,11 @@
     finish(*waiting)
 
 
-def attention(slots, cuts, odd, queries, own, straight, crossed, unit, previous):
+def attention(slots, cuts, odd, queries, own, straight, crossed, unit, units, previous):
     rows, features = queries.shape
     blocks, depth = slots.shape
     block = rows // blocks
-    wide = features // UNITS
+    wide = features // units
     near = len(straight)
     held = pl.BlockSpec(memory_space=pltpu.HBM)
     part = pl.BlockSpec((BLOCKS_PER_STEP * block, wide), lambda b, *_: (b, unit))
@@ -296,6 +288,7 @@
     size = lax.axis_size("node")
     chains = size // levels
     near = depth // 2
+    heads = key_weight.shape[1] // HEAD_DIM
     half = [index // chains // 2 for index in range(size)]
     even = [index // chains % 2 == 0 for index in range(size)]
     other = [index + chains if even[index] else index - chains for index in range(size)]
@@ -303,63 +296,72 @@
     slots = jnp.where(anc_ids >= 0, anc_ids % blocks, 0)
 
     normed, first = norm_project(hidden, norm_gain, key_weight, value_weight)
-    own = [first] + [project(normed, key_weight, value_weight, unit) for unit in range(1, UNITS)]
-    def after(array, *earlier):
-        return lax.optimization_barrier((array, *earlier))[0]
-
-    straight = [{} for _ in range(UNITS)]
-    crossed = [{} for _ in range(UNITS)]
-
-    def step_across(s, unit, settled):
-        source = own[unit] if s == 0 else straight[unit][s]
-        both_ways = unit == UNITS - 1 and s == 0
+    own = [first]
+    own += project(normed, key_weight, value_weight, 1, 1)
+    own += project(normed, key_weight, value_weight, 2, heads - 2)
+    straight = [{} for _ in range(heads)]
+    crossed = [{} for _ in range(heads)]
+    early, late = range(heads // 2), range(heads // 2, heads)
+
+    def after(array, settled):
+        return lax.optimization_barrier((array, *settled))[0]
+
+    def step_across(s, head, settled):
+        source = own[head] if s == 0 else straight[head][s]
         pairs = [
             (i, other[i])
             for i in range(size)
-            if half[i] >= s and (s > 0 or even[i] or (both_ways and half[i] == 0))
+            if half[i] >= s and (s > 0 or even[i] or (head in late and half[i] == 0))
         ]
-        crossed[unit][s] = lax.ppermute(after(source, *settled), "node", pairs)
-        return crossed[unit][s]
-
-    def step_along(s, unit, settled):
-        source = own[unit] if s == 1 else straight[unit][s - 1]
+        crossed[head][s] = lax.ppermute(after(source, settled), "node", pairs)
+        return crossed[head][s]
+
+    def step_along(s, head, settled):
+        source = own[head] if s == 1 else straight[head][s - 1]
         shift = 2 * chains
         pairs = [(i, i + shift) for i in range(size - shift) if half[i] >= s - 1]
-        straight[unit][s] = lax.ppermute(after(source, *settled), "node", pairs)
-        return straight[unit][s]
-
-    def step_down(unit, settled):
+        straight[head][s] = lax.ppermute(after(source, settled), "node", pairs)
+        return straight[head][s]
+
+    def step_down(head, settled):
         shift = 2 * near * chains
         pairs = [(i, i + shift) for i in range(size - shift)]
-        crossed[unit][near] = lax.ppermute(after(crossed[unit][0], *settled), "node", pairs)
-        return crossed[unit][near]
-
-    early, late = range(UNITS)
-    across = [(s, unit) for s in range(near - 1) for unit in (early, late)]
-    across += [(near - 1, early), (near, early), (near - 1, late)]
-    along = [(s, unit) for s in range(1, near + 1) for unit in (early, late)]
+        crossed[head][near] = lax.ppermute(after(crossed[head][0], settled), "node", pairs)
+        return crossed[head][near]
+
+    across = [functools.partial(step_across, s, h) for s in range(near + 1) for h in early]
+    across += [functools.partial(step_across, s, h) for s in range(near) for h in late]
+    along = [functools.partial(step_along, s, h) for s in range(1, near + 1) for h in early]
+    along += [functools.partial(step_along, s, h) for s in range(1, near + 1) for h in late]
+    along += [functools.partial(step_down, h) for h in late]
     waves = []
-    for index, (s, unit) in enumerate(across):
-        settled = waves[-2] if len(waves) >= 2 else ()
-        wave = [step_across(s, unit, settled)]
-        if index < len(along):
-            wave.append(step_along(*along[index], settled))
-        else:
-            wave.append(step_down(late, settled))
-        waves.append(wave)
     result = None
-    for unit in range(UNITS):
-        result = attention(
+
+    def attend(head):
+        return attention(
             slots,
             anc_cut,
             odd,
             queries,
-            own[unit],
-            [straight[unit][s] for s in range(1, near + 1)],
-            [crossed[unit][s] for s in range(near + 1)],
-            unit,
+            own[head],
+            [straight[head][s] for s in range(1, near + 1)],
+            [crossed[head][s] for s in range(near + 1)],
+            head,
+            heads,
             result,
         )
+
+    free = len(early) * (near + 1)
+    for index, (one, two) in enumerate(zip(across, along, strict=True)):
+        lag = 2 if index < free // 2 else 3
+        settled = list(waves[-lag]) if len(waves) >= lag else []
+        head = (index - free - 2) // 2
+        if index >= free + 2 and index % 2 == free % 2 and head in early:
+            result = attend(head)
+            settled.append(result)
+        waves.append([one(settled), two(settled)])
+    for head in late:
+        result = attend(head)
     return result
 
 

time: 123 us -> 145 us (1.18)
  the two profiles are of different devices: /device:TPU:24 before, /device:TPU:0 now
where the time goes in v5:
time: 145 us; the launch traced here: 144 us
  starting transfers between devices  71.1 us (49%)
  Pallas kernels  63.1 us (44%)
  waiting for transfers between devices  5.38 us (4%)
  local copies, waits for them, and re-layouts  2.34 us (2%)
    pallas_call x4, Pallas kernels, attention(): pl.pallas_call(functools.partial(attention_kernel, block, near), grid_spe...  33.6 us
    ppermute x12, starting transfers between devices, step_along(): straight[head][s] = lax.ppermute(after(source, settled), 'node', pairs)  32.4 us
    ppermute x2, starting transfers between devices, step_down(): lax.ppermute(after(crossed[head][0], settled), 'node', pairs)  20.6 us
    ppermute x14, starting transfers between devices, step_across(): crossed[head][s] = lax.ppermute(after(source, settled), 'node', pairs)  18.1 us
    pallas_call x2, Pallas kernels, project(): pl.pallas_call(project_kernel, grid=(CHUNKS,), in_specs=[pl.BlockSpec((ro...  16.3 us
    pallas_call x1, Pallas kernels, norm_project(): pl.pallas_call(norm_project_kernel, in_specs=[held, whole, held, held], o...  13.2 us
    ppermute x12, waiting for transfers between devices, step_along(): straight[head][s] = lax.ppermute(after(source, settled), 'node', pairs)  4.03 us
  transfers between devices with their start and end apart: 28, of which 3 were waited for; matrix products, arithmetic and copies ran while one was open for 0% of the time, Pallas kernels for 29%

profile of v5, /device:TPU:0, one launch (start us, length us, event | category | flops | bytes accessed | tf_op | source)
XLA Modules:
  0.0 143.5 jit_solution(8166433011758301540)
XLA Ops:
  0.0 13.2 %norm_project.1 = (bf16[512,8192]{1,0:T(8,128)(2,1)}, bf16[512,256]{1,0:T(8,128)(2,1)}) custom-call(bf16[512,8192]{1,0:T(8,128)(2,1)} %x_hbm.1, f32[1,8192]{1,0:T(1,128)} %bitcast.2, bf16[8192,512]{1,0:T(8,128)(2,1)} %key_ref.3, bf16[8192,512]{1,0:T(8,128)(2,1)} %value_ref.3), custom_call_target="tpu_custom_call" | custom-call | flops 2147483648 | bytes 25165824 | tf_op jit(solution)/shard_map/norm_project/pallas_call | solution.py:98
  13.2 4.9 %collective-permute-start.1 = (bf16[512,256]{1,0:T(8,128)(2,1)}, bf16[512,256]{1,0:T(8,128)(2,1)S(1)}, u32[]{:S(2)}, u32[]{:S(2)}) collective-permute-start(bf16[512,256]{1,0:T(8,128)(2,1)} %get-tuple-element.31.refs_0_), channel_id=1, source_target_pairs={{0,2},{1,3},{4,6},{5,7},{8,10},{9,11},{12,14},{13,15},{16,18},{17,... | collective-permute-start | bytes 786440 | tf_op jit(solution)/shard_map/ppermute | solution.py:316
  18.1 3.5 %collective-permute-start = (bf16[512,256]{1,0:T(8,128)(2,1)}, bf16[512,256]{1,0:T(8,128)(2,1)S(1)}, u32[]{:S(2)}, u32[]{:S(2)}) collective-permute-start(bf16[512,256]{1,0:T(8,128)(2,1)} %get-tuple-element.31.refs_0_), channel_id=1, source_target_pairs={{0,4},{1,5},{2,6},{3,7},{4,8},{5,9},{6,10},{7,11},{8,12},{9,13},{1... | collective-permute-start | bytes 786440 | tf_op jit(solution)/shard_map/ppermute | solution.py:323
  21.6 7.0 %project.3.refs_0_ = bf16[512,256]{1,0:T(8,128)(2,1)} custom-call(bf16[512,8192]{1,0:T(8,128)(2,1)} %get-tuple-element.29.normed_ref, bf16[8192,512]{1,0:T(8,128)(2,1)} %key_ref.3, bf16[8192,512]{1,0:T(8,128)(2,1)} %value_ref.3), custom_call_target="tpu_custom_call" | custom-call | flops 2147483648 | bytes 12582912 | tf_op jit(solution)/shard_map/project/pallas_call | solution.py:143
  28.7 3.6 %collective-permute-start.4 = (bf16[512,256]{1,0:T(8,128)(2,1)}, bf16[512,256]{1,0:T(8,128)(2,1)S(1)}, u32[]{:S(2)}, u32[]{:S(2)}) collective-permute-start(bf16[512,256]{1,0:T(8,128)(2,1)} %project.3.refs_0_), channel_id=1, source_target_pairs={{0,4},{1,5},{2,6},{3,7},{4,8},{5,9},{6,10},{7,11},{8,12},{9,13},{1... | collective-permute-start | bytes 786440 | tf_op jit(solution)/shard_map/ppermute | solution.py:323
  32.3 1.3 collective-permute-start.3
  33.6 0.0 collective-permute-done.1.refs_4_
  33.6 0.7 collective-permute-start.2
  34.3 3.2 %collective-permute-done.4.refs_1_ = bf16[512,256]{1,0:T(8,128)(2,1)S(1)} collective-permute-done((bf16[512,256]{1,0:T(8,128)(2,1)}, bf16[512,256]{1,0:T(8,128)(2,1)S(1)}, u32[]{:S(2)}, u32[]{:S(2)}) %collective-permute-start.4) | collective-permute-done | bytes 262176 | tf_op jit(solution)/shard_map/ppermute | solution.py:323
  37.6 1.3 collective-permute-done.3.refs_4_
  38.9 0.7 collective-permute-start.9
  39.6 0.7 collective-permute-start.8
  40.2 0.7 collective-permute-start.13
  40.9 0.0 collective-permute-done.2.refs_2_
  41.0 0.7 collective-permute-start.6
  41.6 0.7 collective-permute-start.5
  42.3 9.2 %project.2 = (bf16[512,256]{1,0:T(8,128)(2,1)}, bf16[512,256]{1,0:T(8,128)(2,1)}) custom-call(bf16[512,8192]{1,0:T(8,128)(2,1)} %get-tuple-element.29.normed_ref, bf16[8192,512]{1,0:T(8,128)(2,1)} %key_ref.3, bf16[8192,512]{1,0:T(8,128)(2,1)} %value_ref.3), custom_call_target="tpu_custom_call" | custom-call | flops 4294967296 | bytes 16777216 | tf_op jit(solution)/shard_map/project/pallas_call | solution.py:143
  51.6 0.0 collective-permute-done.13.refs_5_
  51.6 0.7 collective-permute-start.15
  52.3 0.7 collective-permute-start.14
  53.0 12.1 %collective-permute-start.11 = (bf16[512,256]{1,0:T(8,128)(2,1)}, bf16[512,256]{1,0:T(8,128)(2,1)S(1)}, u32[]{:S(2)}, u32[]{:S(2)}) collective-permute-start(bf16[512,256]{1,0:T(8,128)(2,1)} %get-tuple-element.41.refs_0_), channel_id=1, source_target_pairs={{0,4},{1,5},{2,6},{3,7},{4,8},{5,9},{6,10},{7,11},{8,12},{9,13},{1... | collective-permute-start | bytes 786440 | tf_op jit(solution)/shard_map/ppermute | solution.py:323
  65.1 0.0 collective-permute-done.6.refs_3_
  65.1 0.7 collective-permute-start.10
  65.8 7.7 %collective-permute-start.7 = (bf16[512,256]{1,0:T(8,128)(2,1)}, bf16[512,256]{1,0:T(8,128)(2,1)S(1)}, u32[]{:S(2)}, u32[]{:S(2)}) collective-permute-start(bf16[512,256]{1,0:T(8,128)(2,1)} %get-tuple-element.44.refs_0_), channel_id=1, source_target_pairs={{0,4},{1,5},{2,6},{3,7},{4,8},{5,9},{6,10},{7,11},{8,12},{9,13},{1... | collective-permute-start | bytes 786440 | tf_op jit(solution)/shard_map/ppermute | solution.py:323
  73.5 0.7 collective-permute-start.21
  74.2 0.7 collective-permute-start.17
  75.0 1.9 %collective-permute-start.19 = (bf16[512,256]{1,0:T(8,128)(2,1)}, bf16[512,256]{1,0:T(8,128)(2,1)S(1)}, u32[]{:S(2)}, u32[]{:S(2)}) collective-permute-start(bf16[512,256]{1,0:T(8,128)(2,1)} %get-tuple-element.44.refs_0_), channel_id=1, source_target_pairs={{0,2},{1,3},{2,0},{3,1},{4,6},{5,7},{8,10},{9,11},{12,14},{13,15},... | collective-permute-start | bytes 786440 | tf_op jit(solution)/shard_map/ppermute | solution.py:316
  76.9 0.8 collective-permute-done.7.refs_1_
  77.7 0.7 collective-permute-start.12
  78.3 0.6 fusion.1.slot_ref
  78.9 3.2 %collective-permute-start.16 = (bf16[512,256]{1,0:T(8,128)(2,1)}, bf16[512,256]{1,0:T(8,128)(2,1)S(1)}, u32[]{:S(2)}, u32[]{:S(2)}) collective-permute-start(bf16[512,256]{1,0:T(8,128)(2,1)} %get-tuple-element.41.refs_0_), channel_id=1, source_target_pairs={{0,2},{1,3},{2,0},{3,1},{4,6},{5,7},{8,10},{9,11},{12,14},{13,15},... | collective-permute-start | bytes 786440 | tf_op jit(solution)/shard_map/ppermute | solution.py:316
  82.1 8.4 %attention.4.refs_8_ = bf16[512,4096]{1,0:T(8,128)(2,1)} custom-call(s32[8,7]{1,0:T(8,128)} %fusion.1.slot_ref, s32[8,7]{1,0:T(8,128)} %cut_ref.7, s32[1]{0:T(128)} %bitcast.odd_ref, bf16[512,4096]{1,0:T(8,128)(2,1)} %q_ref.7, bf16[512,256]{1,0:T(8,128)(2,1)} %get-tuple-element.31.refs_0_, bf16[512,256]{1,0:T(8,128)(2,1)} %copy-done.22, ...), custom_call_target="tpu_custom_call" | custom-call | flops 1073741824 | bytes 8388608 | tf_op jit(solution)/shard_map/attention/pallas_call | solution.py:261
  90.6 0.7 collective-permute-start.22
  91.3 0.9 collective-permute-start.23
  92.2 8.4 %attention.5.refs_8_ = bf16[512,4096]{1,0:T(8,128)(2,1)} custom-call(s32[8,7]{1,0:T(8,128)} %fusion.1.slot_ref, s32[8,7]{1,0:T(8,128)} %cut_ref.7, s32[1]{0:T(128)} %bitcast.odd_ref, bf16[512,4096]{1,0:T(8,128)(2,1)} %q_ref.7, bf16[512,256]{1,0:T(8,128)(2,1)} %project.3.refs_0_, bf16[512,256]{1,0:T(8,128)(2,1)} %copy-done, ...), custom_call_target="tpu_custom_call", output_to_operand_aliasing={{}: (12, {})} | custom-call | flops 1073741824 | bytes 8388608 | tf_op jit(solution)/shard_map/attention/pallas_call | solution.py:261
  100.7 0.7 collective-permute-start.26
  101.4 14.2 %collective-permute-start.27 = (bf16[512,256]{1,0:T(8,128)(2,1)S(1)}, bf16[512,256]{1,0:T(8,128)(2,1)S(1)}, u32[]{:S(2)}, u32[]{:S(2)}) collective-permute-start(bf16[512,256]{1,0:T(8,128)(2,1)S(1)} %collective-permute-done.16.refs_4_), channel_id=1, source_target_pairs={{0,12},{1,13},{2,14},{3,15},{16,28},{17,29},{18,30},{19,31}} | collective-permute-start | bytes 786440 | tf_op jit(solution)/shard_map/ppermute | solution.py:329
  115.6 0.7 collective-permute-start.20
  116.3 0.7 collective-permute-start.18
  117.0 0.7 collective-permute-start.24
  117.8 6.4 %collective-permute-start.25 = (bf16[512,256]{1,0:T(8,128)(2,1)S(1)}, bf16[512,256]{1,0:T(8,128)(2,1)S(1)}, u32[]{:S(2)}, u32[]{:S(2)}) collective-permute-start(bf16[512,256]{1,0:T(8,128)(2,1)S(1)} %collective-permute-done.19.refs_4_), channel_id=1, source_target_pairs={{0,12},{1,13},{2,14},{3,15},{16,28},{17,29},{18,30},{19,31}} | collective-permute-start | bytes 786440 | tf_op jit(solution)/shard_map/ppermute | solution.py:329
  124.2 0.7 copy-done.19
  124.9 8.4 %attention.6.refs_8_ = bf16[512,4096]{1,0:T(8,128)(2,1)} custom-call(s32[8,7]{1,0:T(8,128)} %fusion.1.slot_ref, s32[8,7]{1,0:T(8,128)} %cut_ref.7, s32[1]{0:T(128)} %bitcast.odd_ref, bf16[512,4096]{1,0:T(8,128)(2,1)} %q_ref.7, bf16[512,256]{1,0:T(8,128)(2,1)} %get-tuple-element.41.refs_0_, ...), custom_call_target="tpu_custom_call", output_to_operand_aliasing={{}: (12, {})} | custom-call | flops 1073741824 | bytes 8388608 | tf_op jit(solution)/shard_map/attention/pallas_call | solution.py:261
  133.4 0.7 copy-done.15
  134.1 0.1 copy-done.16
  134.2 0.1 copy-done.18
  134.3 0.7 copy-done.20
  135.0 8.4 %attention.7 = bf16[512,4096]{1,0:T(8,128)(2,1)} custom-call(s32[8,7]{1,0:T(8,128)} %fusion.1.slot_ref, s32[8,7]{1,0:T(8,128)} %cut_ref.7, s32[1]{0:T(128)} %bitcast.odd_ref, bf16[512,4096]{1,0:T(8,128)(2,1)} %q_ref.7, bf16[512,256]{1,0:T(8,128)(2,1)} %get-tuple-element.44.refs_0_, bf16[512,256]{1,0:T(8,128)(2,1)} %copy-done.2, ...), custom_call_target="tpu_custom_call", output_to_operand_aliasing={{}: (12, {})} | custom-call | flops 1073741824 | bytes 8388608 | tf_op jit(solution)/shard_map/attention/pallas_call | solution.py:261
  (74 shorter events, 0.2 us)
Async XLA Ops:
  13.2 20.4 %collective-permute-start.1 = (bf16[512,256]{1,0:T(8,128)(2,1)}, bf16[512,256]{1,0:T(8,128)(2,1)S(1)}, u32[]{:S(2)}, u32[]{:S(2)}) collective-permute-start(bf16[512,256]{1,0:T(8,128)(2,1)} %get-tuple-element.31.refs_0_), channel_id=1, source_target_pairs={{0,2},{1,3},{4,6},{5,7},{8,10},{9,11},{12,14},{13,15},{16,18},{17,... | collective-permute-start | bytes 786440 | tf_op jit(solution)/shard_map/ppermute | solution.py:316
  18.1 15.5 %collective-permute-start = (bf16[512,256]{1,0:T(8,128)(2,1)}, bf16[512,256]{1,0:T(8,128)(2,1)S(1)}, u32[]{:S(2)}, u32[]{:S(2)}) collective-permute-start(bf16[512,256]{1,0:T(8,128)(2,1)} %get-tuple-element.31.refs_0_), channel_id=1, source_target_pairs={{0,4},{1,5},{2,6},{3,7},{4,8},{5,9},{6,10},{7,11},{8,12},{9,13},{1... | collective-permute-start | bytes 786440 | tf_op jit(solution)/shard_map/ppermute | solution.py:323
  28.7 49.7 %copy-start.28 = (s32[8,7]{1,0:T(8,128)S(1)}, s32[8,7]{1,0:T(8,128)}, u32[]{:S(2)}) copy-start(s32[8,7]{1,0:T(8,128)} %param.12) | copy-start | bytes 676
  28.7 8.9 %collective-permute-start.4 = (bf16[512,256]{1,0:T(8,128)(2,1)}, bf16[512,256]{1,0:T(8,128)(2,1)S(1)}, u32[]{:S(2)}, u32[]{:S(2)}) collective-permute-start(bf16[512,256]{1,0:T(8,128)(2,1)} %project.3.refs_0_), channel_id=1, source_target_pairs={{0,4},{1,5},{2,6},{3,7},{4,8},{5,9},{6,10},{7,11},{8,12},{9,13},{1... | collective-permute-start | bytes 786440 | tf_op jit(solution)/shard_map/ppermute | solution.py:323
  32.3 6.6 %collective-permute-start.3 = (bf16[512,256]{1,0:T(8,128)(2,1)}, bf16[512,256]{1,0:T(8,128)(2,1)S(1)}, u32[]{:S(2)}, u32[]{:S(2)}) collective-permute-start(bf16[512,256]{1,0:T(8,128)(2,1)} %project.3.refs_0_), channel_id=1, source_target_pairs={{0,2},{1,3},{4,6},{5,7},{8,10},{9,11},{12,14},{13,15},{16,18},{17,... | collective-permute-start | bytes 786440 | tf_op jit(solution)/shard_map/ppermute | solution.py:316
  33.6 17.9 %copy-start.21 = (bf16[512,256]{1,0:T(8,128)(2,1)}, bf16[512,256]{1,0:T(8,128)(2,1)S(1)}, u32[]{:S(2)}) copy-start(bf16[512,256]{1,0:T(8,128)(2,1)S(1)} %collective-permute-done.1.refs_4_) | copy-start | bytes 786436
  33.6 17.9 %copy-start.22 = (bf16[512,256]{1,0:T(8,128)(2,1)}, bf16[512,256]{1,0:T(8,128)(2,1)S(1)}, u32[]{:S(2)}) copy-start(bf16[512,256]{1,0:T(8,128)(2,1)S(1)} %collective-permute-done.refs_1_) | copy-start | bytes 786436
  33.6 7.3 %collective-permute-start.2 = (bf16[512,256]{1,0:T(8,128)(2,1)S(1)}, bf16[512,256]{1,0:T(8,128)(2,1)S(1)}, u32[]{:S(2)}, u32[]{:S(2)}) collective-permute-start(bf16[512,256]{1,0:T(8,128)(2,1)S(1)} %collective-permute-done.refs_1_), channel_id=1, source_target_pairs={{4,8},{5,9},{6,10},{7,11},{8,12},{9,13},{10,14},{11,15},{20,24},{2... | collective-permute-start | bytes 786440 | tf_op jit(solution)/shard_map/ppermute | solution.py:323
  37.6 14.0 %copy-start = (bf16[512,256]{1,0:T(8,128)(2,1)}, bf16[512,256]{1,0:T(8,128)(2,1)S(1)}, u32[]{:S(2)}) copy-start(bf16[512,256]{1,0:T(8,128)(2,1)S(1)} %collective-permute-done.4.refs_1_) | copy-start | bytes 786436
  38.9 12.7 %copy-start.1 = (bf16[512,256]{1,0:T(8,128)(2,1)}, bf16[512,256]{1,0:T(8,128)(2,1)S(1)}, u32[]{:S(2)}) copy-start(bf16[512,256]{1,0:T(8,128)(2,1)S(1)} %collective-permute-done.3.refs_4_) | copy-start | bytes 786436
  38.9 12.7 %collective-permute-start.9 = (bf16[512,256]{1,0:T(8,128)(2,1)S(1)}, bf16[512,256]{1,0:T(8,128)(2,1)S(1)}, u32[]{:S(2)}, u32[]{:S(2)}) collective-permute-start(bf16[512,256]{1,0:T(8,128)(2,1)S(1)} %collective-permute-done.4.refs_1_), channel_id=1, source_target_pairs={{4,8},{5,9},{6,10},{7,11},{8,12},{9,13},{10,14},{11,15},{20,24},{2... | collective-permute-start | bytes 786440 | tf_op jit(solution)/shard_map/ppermute | solution.py:323
  39.6 13.4 %collective-permute-start.8 = (bf16[512,256]{1,0:T(8,128)(2,1)S(1)}, bf16[512,256]{1,0:T(8,128)(2,1)S(1)}, u32[]{:S(2)}, u32[]{:S(2)}) collective-permute-start(bf16[512,256]{1,0:T(8,128)(2,1)S(1)} %collective-permute-done.4.refs_1_), channel_id=1, source_target_pairs={{4,6},{5,7},{6,4},{7,5},{8,10},{9,11},{10,8},{11,9},{12,14},{13,15... | collective-permute-start | bytes 786440 | tf_op jit(solution)/shard_map/ppermute | solution.py:316
  40.2 11.4 %collective-permute-start.13 = (bf16[512,256]{1,0:T(8,128)(2,1)S(1)}, bf16[512,256]{1,0:T(8,128)(2,1)S(1)}, u32[]{:S(2)}, u32[]{:S(2)}) collective-permute-start(bf16[512,256]{1,0:T(8,128)(2,1)S(1)} %collective-permute-done.refs_1_), channel_id=1, source_target_pairs={{4,6},{5,7},{6,4},{7,5},{8,10},{9,11},{10,8},{11,9},{12,14},{13,15... | collective-permute-start | bytes 786440 | tf_op jit(solution)/shard_map/ppermute | solution.py:316
  40.9 10.6 %copy-start.23 = (bf16[512,256]{1,0:T(8,128)(2,1)}, bf16[512,256]{1,0:T(8,128)(2,1)S(1)}, u32[]{:S(2)}) copy-start(bf16[512,256]{1,0:T(8,128)(2,1)S(1)} %collective-permute-done.2.refs_2_) | copy-start | bytes 786436
  41.0 24.1 %collective-permute-start.6 = (bf16[512,256]{1,0:T(8,128)(2,1)S(1)}, bf16[512,256]{1,0:T(8,128)(2,1)S(1)}, u32[]{:S(2)}, u32[]{:S(2)}) collective-permute-start(bf16[512,256]{1,0:T(8,128)(2,1)S(1)} %collective-permute-done.2.refs_2_), channel_id=1, source_target_pairs={{8,12},{9,13},{10,14},{11,15},{24,28},{25,29},{26,30},{27,31}} | collective-permute-start | bytes 786440 | tf_op jit(solution)/shard_map/ppermute | solution.py:323
  41.6 24.2 %collective-permute-start.5 = (bf16[512,256]{1,0:T(8,128)(2,1)S(1)}, bf16[512,256]{1,0:T(8,128)(2,1)S(1)}, u32[]{:S(2)}, u32[]{:S(2)}) collective-permute-start(bf16[512,256]{1,0:T(8,128)(2,1)S(1)} %collective-permute-done.2.refs_2_), channel_id=1, source_target_pairs={{8,10},{9,11},{10,8},{11,9},{12,14},{13,15},{14,12},{15,13},{24,26... | collective-permute-start | bytes 786440 | tf_op jit(solution)/shard_map/ppermute | solution.py:316
  51.6 39.0 %copy-start.4 = (bf16[512,256]{1,0:T(8,128)(2,1)}, bf16[512,256]{1,0:T(8,128)(2,1)S(1)}, u32[]{:S(2)}) copy-start(bf16[512,256]{1,0:T(8,128)(2,1)S(1)} %collective-permute-done.9.refs_2_) | copy-start | bytes 786436
  51.6 23.3 %copy-start.24 = (bf16[512,256]{1,0:T(8,128)(2,1)}, bf16[512,256]{1,0:T(8,128)(2,1)S(1)}, u32[]{:S(2)}) copy-start(bf16[512,256]{1,0:T(8,128)(2,1)S(1)} %collective-permute-done.13.refs_5_) | copy-start | bytes 786436
  51.6 21.9 %collective-permute-start.15 = (bf16[512,256]{1,0:T(8,128)(2,1)S(1)}, bf16[512,256]{1,0:T(8,128)(2,1)S(1)}, u32[]{:S(2)}, u32[]{:S(2)}) collective-permute-start(bf16[512,256]{1,0:T(8,128)(2,1)S(1)} %collective-permute-done.9.refs_2_), channel_id=1, source_target_pairs={{8,12},{9,13},{10,14},{11,15},{24,28},{25,29},{26,30},{27,31}} | collective-permute-start | bytes 786440 | tf_op jit(solution)/shard_map/ppermute | solution.py:323
  52.3 21.9 %collective-permute-start.14 = (bf16[512,256]{1,0:T(8,128)(2,1)S(1)}, bf16[512,256]{1,0:T(8,128)(2,1)S(1)}, u32[]{:S(2)}, u32[]{:S(2)}) collective-permute-start(bf16[512,256]{1,0:T(8,128)(2,1)S(1)} %collective-permute-done.9.refs_2_), channel_id=1, source_target_pairs={{8,10},{9,11},{10,8},{11,9},{12,14},{13,15},{14,12},{15,13},{24,26... | collective-permute-start | bytes 786440 | tf_op jit(solution)/shard_map/ppermute | solution.py:316
  53.0 37.6 %copy-start.5 = (bf16[512,256]{1,0:T(8,128)(2,1)}, bf16[512,256]{1,0:T(8,128)(2,1)S(1)}, u32[]{:S(2)}) copy-start(bf16[512,256]{1,0:T(8,128)(2,1)S(1)} %collective-permute-done.8.refs_5_) | copy-start | bytes 786436
  53.0 21.2 %collective-permute-start.11 = (bf16[512,256]{1,0:T(8,128)(2,1)}, bf16[512,256]{1,0:T(8,128)(2,1)S(1)}, u32[]{:S(2)}, u32[]{:S(2)}) collective-permute-start(bf16[512,256]{1,0:T(8,128)(2,1)} %get-tuple-element.41.refs_0_), channel_id=1, source_target_pairs={{0,4},{1,5},{2,6},{3,7},{4,8},{5,9},{6,10},{7,11},{8,12},{9,13},{1... | collective-permute-start | bytes 786440 | tf_op jit(solution)/shard_map/ppermute | solution.py:323
  65.1 11.8 %copy-start.25 = (bf16[512,256]{1,0:T(8,128)(2,1)}, bf16[512,256]{1,0:T(8,128)(2,1)S(1)}, u32[]{:S(2)}) copy-start(bf16[512,256]{1,0:T(8,128)(2,1)S(1)} %collective-permute-done.6.refs_3_) | copy-start | bytes 786436
  65.1 9.8 %collective-permute-start.10 = (bf16[512,256]{1,0:T(8,128)(2,1)S(1)}, bf16[512,256]{1,0:T(8,128)(2,1)S(1)}, u32[]{:S(2)}, u32[]{:S(2)}) collective-permute-start(bf16[512,256]{1,0:T(8,128)(2,1)S(1)} %collective-permute-done.6.refs_3_), channel_id=1, source_target_pairs={{12,14},{13,15},{14,12},{15,13},{28,30},{29,31},{30,28},{31,29}} | collective-permute-start | bytes 786440 | tf_op jit(solution)/shard_map/ppermute | solution.py:316
  65.8 8.4 %copy-start.26 = (bf16[512,256]{1,0:T(8,128)(2,1)}, bf16[512,256]{1,0:T(8,128)(2,1)S(1)}, u32[]{:S(2)}) copy-start(bf16[512,256]{1,0:T(8,128)(2,1)S(1)} %collective-permute-done.5.refs_6_) | copy-start | bytes 786436
  65.8 11.8 %collective-permute-start.7 = (bf16[512,256]{1,0:T(8,128)(2,1)}, bf16[512,256]{1,0:T(8,128)(2,1)S(1)}, u32[]{:S(2)}, u32[]{:S(2)}) collective-permute-start(bf16[512,256]{1,0:T(8,128)(2,1)} %get-tuple-element.44.refs_0_), channel_id=1, source_target_pairs={{0,4},{1,5},{2,6},{3,7},{4,8},{5,9},{6,10},{7,11},{8,12},{9,13},{1... | collective-permute-start | bytes 786440 | tf_op jit(solution)/shard_map/ppermute | solution.py:323
  73.5 17.1 %copy-start.9 = (bf16[512,256]{1,0:T(8,128)(2,1)}, bf16[512,256]{1,0:T(8,128)(2,1)S(1)}, u32[]{:S(2)}) copy-start(bf16[512,256]{1,0:T(8,128)(2,1)S(1)} %collective-permute-done.15.refs_3_) | copy-start | bytes 786436
  73.5 17.1 %collective-permute-start.21 = (bf16[512,256]{1,0:T(8,128)(2,1)S(1)}, bf16[512,256]{1,0:T(8,128)(2,1)S(1)}, u32[]{:S(2)}, u32[]{:S(2)}) collective-permute-start(bf16[512,256]{1,0:T(8,128)(2,1)S(1)} %collective-permute-done.15.refs_3_), channel_id=1, source_target_pairs={{12,14},{13,15},{14,12},{15,13},{28,30},{29,31},{30,28},{31,29}} | collective-permute-start | bytes 786440 | tf_op jit(solution)/shard_map/ppermute | solution.py:316
  74.2 16.4 %copy-start.3 = (bf16[512,256]{1,0:T(8,128)(2,1)}, bf16[512,256]{1,0:T(8,128)(2,1)S(1)}, u32[]{:S(2)}) copy-start(bf16[512,256]{1,0:T(8,128)(2,1)S(1)} %collective-permute-done.11.refs_1_) | copy-start | bytes 786436
  74.2 16.4 %copy-start.10 = (bf16[512,256]{1,0:T(8,128)(2,1)}, bf16[512,256]{1,0:T(8,128)(2,1)S(1)}, u32[]{:S(2)}) copy-start(bf16[512,256]{1,0:T(8,128)(2,1)S(1)} %collective-permute-done.14.refs_6_) | copy-start | bytes 786436
  74.2 16.4 %collective-permute-start.17 = (bf16[512,256]{1,0:T(8,128)(2,1)S(1)}, bf16[512,256]{1,0:T(8,128)(2,1)S(1)}, u32[]{:S(2)}, u32[]{:S(2)}) collective-permute-start(bf16[512,256]{1,0:T(8,128)(2,1)S(1)} %collective-permute-done.11.refs_1_), channel_id=1, source_target_pairs={{4,8},{5,9},{6,10},{7,11},{8,12},{9,13},{10,14},{11,15},{20,24},{2... | collective-permute-start | bytes 786440 | tf_op jit(solution)/shard_map/ppermute | solution.py:323
  75.0 25.7 %collective-permute-start.19 = (bf16[512,256]{1,0:T(8,128)(2,1)}, bf16[512,256]{1,0:T(8,128)(2,1)S(1)}, u32[]{:S(2)}, u32[]{:S(2)}) collective-permute-start(bf16[512,256]{1,0:T(8,128)(2,1)} %get-tuple-element.44.refs_0_), channel_id=1, source_target_pairs={{0,2},{1,3},{2,0},{3,1},{4,6},{5,7},{8,10},{9,11},{12,14},{13,15},... | collective-permute-start | bytes 786440 | tf_op jit(solution)/shard_map/ppermute | solution.py:316
  77.7 38.0 %copy-start.2 = (bf16[512,256]{1,0:T(8,128)(2,1)}, bf16[512,256]{1,0:T(8,128)(2,1)S(1)}, u32[]{:S(2)}) copy-start(bf16[512,256]{1,0:T(8,128)(2,1)S(1)} %collective-permute-done.7.refs_1_) | copy-start | bytes 786436
  77.7 23.0 %collective-permute-start.12 = (bf16[512,256]{1,0:T(8,128)(2,1)S(1)}, bf16[512,256]{1,0:T(8,128)(2,1)S(1)}, u32[]{:S(2)}, u32[]{:S(2)}) collective-permute-start(bf16[512,256]{1,0:T(8,128)(2,1)S(1)} %collective-permute-done.7.refs_1_), channel_id=1, source_target_pairs={{4,8},{5,9},{6,10},{7,11},{8,12},{9,13},{10,14},{11,15},{20,24},{2... | collective-permute-start | bytes 786440 | tf_op jit(solution)/shard_map/ppermute | solution.py:323
  78.9 22.4 %collective-permute-start.16 = (bf16[512,256]{1,0:T(8,128)(2,1)}, bf16[512,256]{1,0:T(8,128)(2,1)S(1)}, u32[]{:S(2)}, u32[]{:S(2)}) collective-permute-start(bf16[512,256]{1,0:T(8,128)(2,1)} %get-tuple-element.41.refs_0_), channel_id=1, source_target_pairs={{0,2},{1,3},{2,0},{3,1},{4,6},{5,7},{8,10},{9,11},{12,14},{13,15},... | collective-permute-start | bytes 786440 | tf_op jit(solution)/shard_map/ppermute | solution.py:316
  90.6 10.0 %copy-start.8 = (bf16[512,256]{1,0:T(8,128)(2,1)}, bf16[512,256]{1,0:T(8,128)(2,1)S(1)}, u32[]{:S(2)}) copy-start(bf16[512,256]{1,0:T(8,128)(2,1)S(1)} %collective-permute-done.17.refs_2_) | copy-start | bytes 786436
  90.6 25.7 %collective-permute-start.22 = (bf16[512,256]{1,0:T(8,128)(2,1)S(1)}, bf16[512,256]{1,0:T(8,128)(2,1)S(1)}, u32[]{:S(2)}, u32[]{:S(2)}) collective-permute-start(bf16[512,256]{1,0:T(8,128)(2,1)S(1)} %collective-permute-done.11.refs_1_), channel_id=1, source_target_pairs={{4,6},{5,7},{6,4},{7,5},{8,10},{9,11},{10,8},{11,9},{12,14},{13,15... | collective-permute-start | bytes 786440 | tf_op jit(solution)/shard_map/ppermute | solution.py:316
  91.3 25.7 %collective-permute-start.23 = (bf16[512,256]{1,0:T(8,128)(2,1)S(1)}, bf16[512,256]{1,0:T(8,128)(2,1)S(1)}, u32[]{:S(2)}, u32[]{:S(2)}) collective-permute-start(bf16[512,256]{1,0:T(8,128)(2,1)S(1)} %collective-permute-done.17.refs_2_), channel_id=1, source_target_pairs={{8,12},{9,13},{10,14},{11,15},{24,28},{25,29},{26,30},{27,31}} | collective-permute-start | bytes 786440 | tf_op jit(solution)/shard_map/ppermute | solution.py:323
  100.6 32.7 %copy-start.6 = (bf16[512,256]{1,0:T(8,128)(2,1)}, bf16[512,256]{1,0:T(8,128)(2,1)S(1)}, u32[]{:S(2)}) copy-start(bf16[512,256]{1,0:T(8,128)(2,1)S(1)} %collective-permute-done.19.refs_4_) | copy-start | bytes 786436
  100.7 32.7 %copy-start.7 = (bf16[512,256]{1,0:T(8,128)(2,1)}, bf16[512,256]{1,0:T(8,128)(2,1)S(1)}, u32[]{:S(2)}) copy-start(bf16[512,256]{1,0:T(8,128)(2,1)S(1)} %collective-permute-done.12.refs_2_) | copy-start | bytes 786436
  100.7 17.1 %collective-permute-start.26 = (bf16[512,256]{1,0:T(8,128)(2,1)S(1)}, bf16[512,256]{1,0:T(8,128)(2,1)S(1)}, u32[]{:S(2)}, u32[]{:S(2)}) collective-permute-start(bf16[512,256]{1,0:T(8,128)(2,1)S(1)} %collective-permute-done.17.refs_2_), channel_id=1, source_target_pairs={{8,10},{9,11},{10,8},{11,9},{12,14},{13,15},{14,12},{15,13},{24,26... | collective-permute-start | bytes 786440 | tf_op jit(solution)/shard_map/ppermute | solution.py:316
  101.4 22.8 %copy-start.12 = (bf16[512,256]{1,0:T(8,128)(2,1)}, bf16[512,256]{1,0:T(8,128)(2,1)S(1)}, u32[]{:S(2)}) copy-start(bf16[512,256]{1,0:T(8,128)(2,1)S(1)} %collective-permute-done.16.refs_4_) | copy-start | bytes 786436
  101.4 22.8 %collective-permute-start.27 = (bf16[512,256]{1,0:T(8,128)(2,1)S(1)}, bf16[512,256]{1,0:T(8,128)(2,1)S(1)}, u32[]{:S(2)}, u32[]{:S(2)}) collective-permute-start(bf16[512,256]{1,0:T(8,128)(2,1)S(1)} %collective-permute-done.16.refs_4_), channel_id=1, source_target_pairs={{0,12},{1,13},{2,14},{3,15},{16,28},{17,29},{18,30},{19,31}} | collective-permute-start | bytes 786440 | tf_op jit(solution)/shard_map/ppermute | solution.py:329
  115.6 17.7 %collective-permute-start.20 = (bf16[512,256]{1,0:T(8,128)(2,1)S(1)}, bf16[512,256]{1,0:T(8,128)(2,1)S(1)}, u32[]{:S(2)}, u32[]{:S(2)}) collective-permute-start(bf16[512,256]{1,0:T(8,128)(2,1)S(1)} %collective-permute-done.7.refs_1_), channel_id=1, source_target_pairs={{4,6},{5,7},{6,4},{7,5},{8,10},{9,11},{10,8},{11,9},{12,14},{13,15... | collective-permute-start | bytes 786440 | tf_op jit(solution)/shard_map/ppermute | solution.py:316
  116.3 7.8 %copy-start.13 = (bf16[512,256]{1,0:T(8,128)(2,1)}, bf16[512,256]{1,0:T(8,128)(2,1)S(1)}, u32[]{:S(2)}) copy-start(bf16[512,256]{1,0:T(8,128)(2,1)S(1)} %collective-permute-done.22.refs_5_) | copy-start | bytes 786436
  116.3 17.0 %collective-permute-start.18 = (bf16[512,256]{1,0:T(8,128)(2,1)S(1)}, bf16[512,256]{1,0:T(8,128)(2,1)S(1)}, u32[]{:S(2)}, u32[]{:S(2)}) collective-permute-start(bf16[512,256]{1,0:T(8,128)(2,1)S(1)} %collective-permute-done.12.refs_2_), channel_id=1, source_target_pairs={{8,12},{9,13},{10,14},{11,15},{24,28},{25,29},{26,30},{27,31}} | collective-permute-start | bytes 786440 | tf_op jit(solution)/shard_map/ppermute | solution.py:323
  117.0 16.3 %collective-permute-start.24 = (bf16[512,256]{1,0:T(8,128)(2,1)S(1)}, bf16[512,256]{1,0:T(8,128)(2,1)S(1)}, u32[]{:S(2)}, u32[]{:S(2)}) collective-permute-start(bf16[512,256]{1,0:T(8,128)(2,1)S(1)} %collective-permute-done.12.refs_2_), channel_id=1, source_target_pairs={{8,10},{9,11},{10,8},{11,9},{12,14},{13,15},{14,12},{15,13},{24,26... | collective-permute-start | bytes 786440 | tf_op jit(solution)/shard_map/ppermute | solution.py:316
  117.8 15.7 %collective-permute-start.25 = (bf16[512,256]{1,0:T(8,128)(2,1)S(1)}, bf16[512,256]{1,0:T(8,128)(2,1)S(1)}, u32[]{:S(2)}, u32[]{:S(2)}) collective-permute-start(bf16[512,256]{1,0:T(8,128)(2,1)S(1)} %collective-permute-done.19.refs_4_), channel_id=1, source_target_pairs={{0,12},{1,13},{2,14},{3,15},{16,28},{17,29},{18,30},{19,31}} | collective-permute-start | bytes 786440 | tf_op jit(solution)/shard_map/ppermute | solution.py:329
  (9 other events, 26.2 us)

commit v6 on v4

--- a/solution.py
+++ b/solution.py
@@ -12,125 +12,128 @@
 MASKED = -1e30
 MIB = 1024 * 1024
 CHUNKS = 4
-NORM_CHUNKS = 8
+LOADS = 8
 UNITS = 2
 BLOCKS_PER_STEP = 2
 
 
 def norm_project_kernel(
     x_hbm, gain_ref, key_hbm, value_hbm, normed_hbm, kv_ref,
-    x_scr, key_scr, value_scr, normed_scr, acc_scr, x_sem, key_sem, value_sem, normed_sem,
+    x_scr, weight_scr, normed_scr, acc_scr, scale_scr, x_sem, key_sem, value_sem, normed_sem,
 ):
-    rows, features = x_scr.shape
-    width = key_scr.shape[1]
-    chunk = features // NORM_CHUNKS
+    loads, rows, chunk = x_scr.shape
+    width = weight_scr.shape[2] // 2
     lanes = 128
-
-    def columns(c):
-        return slice(c * chunk, (c + 1) * chunk)
+    band = 128
+
+    def span(c):
+        return pl.ds(pl.multiple_of(c * chunk, chunk), chunk)
 
     def load_x(c):
-        return pltpu.make_async_copy(
-            x_hbm.at[:, columns(c)], x_scr.at[:, columns(c)], x_sem.at[c]
-        )
+        return pltpu.make_async_copy(x_hbm.at[:, span(c)], x_scr.at[c], x_sem.at[c])
 
     def load_weights(c):
+        head = pl.ds(0, width)
         return [
             pltpu.make_async_copy(
-                hbm.at[columns(c), pl.ds(0, width)], scr.at[columns(c), :], sem.at[c]
-            )
-            for hbm, scr, sem in ((key_hbm, key_scr, key_sem), (value_hbm, value_scr, value_sem))
+                key_hbm.at[span(c), head], weight_scr.at[c, :, pl.ds(0, width)], key_sem.at[c]
+            ),
+            pltpu.make_async_copy(
+                value_hbm.at[span(c), head], weight_scr.at[c, :, pl.ds(width, width)], value_sem.at[c]
+            ),
         ]
 
     def store_normed(c):
-        return pltpu.make_async_copy(
-            normed_scr.at[:, columns(c)], normed_hbm.at[:, columns(c)], normed_sem.at[c]
-        )
-
-    def start_weights(c):
-        for copy in load_weights(c):
-            copy.start()
-
-    for c in range(NORM_CHUNKS):
+        return pltpu.make_async_copy(normed_scr.at[c], normed_hbm.at[:, span(c)], normed_sem.at[c])
+
+    for c in range(loads):
         load_x(c).start()
-    band = 128
-    bands = [slice(first, first + band) for first in range(0, rows, band)]
-    ahead = NORM_CHUNKS // 2
-    squares = [jnp.zeros((band, lanes), jnp.float32) for _ in bands]
-    for c in range(NORM_CHUNKS):
+    scale_scr[...] = jnp.zeros_like(scale_scr)
+
+    def square(c, carry):
         load_x(c).wait()
-        if c >= ahead:
-            start_weights(c - ahead)
-        for index, row in enumerate(bands):
-            for first in range(c * chunk, (c + 1) * chunk, lanes):
-                x = x_scr[row, first : first + lanes].astype(jnp.float32)
-                squares[index] += x * x
-    for c in range(NORM_CHUNKS - ahead, NORM_CHUNKS):
-        start_weights(c)
-    inverse = []
-    for total in squares:
-        mean_sq = jnp.sum(total, axis=-1, keepdims=True) / features
-        inverse.append(jnp.broadcast_to(lax.rsqrt(mean_sq + EPS), (band, lanes)))
+
+        @pl.when(c >= loads // 2)
+        def _():
+            for part in range(2):
+                for copy in load_weights(2 * (c - loads // 2) + part):
+                    copy.start()
+
+        for first in range(0, rows, band):
+            row = slice(first, first + band)
+            total = scale_scr[row, :]
+            for lane in range(0, chunk, lanes):
+                x = x_scr[c, row, lane : lane + lanes].astype(jnp.float32)
+                total += x * x
+            scale_scr[row, :] = total
+        return carry
+
+    lax.fori_loop(0, loads, square, 0)
+    mean_sq = jnp.sum(scale_scr[...], axis=-1, keepdims=True) / (loads * chunk)
+    scale_scr[...] = jnp.broadcast_to(lax.rsqrt(mean_sq + EPS), scale_scr.shape)
 
     def normalise(c):
-        for index, row in enumerate(bands):
-            for first in range(c * chunk, (c + 1) * chunk, lanes):
-                cols = slice(first, first + lanes)
-                x = x_scr[row, cols].astype(jnp.float32)
-                normed_scr[row, cols] = (x * inverse[index] * gain_ref[:, cols]).astype(jnp.bfloat16)
+        for first in range(0, rows, band):
+            row = slice(first, first + band)
+            inverse = scale_scr[row, :]
+            for lane in range(0, chunk, lanes):
+                cols = slice(lane, lane + lanes)
+                x = x_scr[c, row, cols].astype(jnp.float32)
+                gain = gain_ref[c, :, cols]
+                normed_scr[c, row, cols] = (x * inverse * gain).astype(jnp.bfloat16)
 
     normalise(0)
-    for c in range(NORM_CHUNKS):
+    acc_scr[...] = jnp.zeros_like(acc_scr)
+
+    def multiply(c, carry):
         for copy in load_weights(c):
             copy.wait()
         store_normed(c).start()
-        for part, weight in enumerate((key_scr, value_scr)):
-            cols = slice(part * width, (part + 1) * width)
-            term = jnp.dot(
-                normed_scr[:, columns(c)], weight[columns(c), :], preferred_element_type=jnp.float32
-            )
-            if c == 0:
-                acc_scr[:, cols] = term
-            elif c < NORM_CHUNKS - 1:
-                acc_scr[:, cols] += term
-            else:
-                kv_ref[:, cols] = (acc_scr[:, cols] + term).astype(jnp.bfloat16)
-        if c < NORM_CHUNKS - 1:
+        acc_scr[...] += jnp.dot(normed_scr[c], weight_scr[c], preferred_element_type=jnp.float32)
+
+        @pl.when(c < loads - 1)
+        def _():
             normalise(c + 1)
-    for c in range(NORM_CHUNKS):
+
+        return carry
+
+    lax.fori_loop(0, loads, multiply, 0)
+    kv_ref[...] = acc_scr[...].astype(jnp.bfloat16)
+    for c in range(loads):
         store_normed(c).wait()
 
 
 def norm_project(hidden, gain, key_weight, value_weight):
     rows, features = hidden.shape
     width = key_weight.shape[1] // UNITS
+    chunk = features // LOADS
     whole = pl.BlockSpec(memory_space=pltpu.VMEM)
-    remote = pl.BlockSpec(memory_space=pl.ANY)
+    held = pl.BlockSpec(memory_space=pltpu.HBM)
     return pl.pallas_call(
         norm_project_kernel,
-        in_specs=[remote, whole, remote, remote],
-        out_specs=[remote, whole],
+        in_specs=[held, whole, held, held],
+        out_specs=[held, whole],
         out_shape=[
             jax.ShapeDtypeStruct((rows, features), jnp.bfloat16),
             jax.ShapeDtypeStruct((rows, 2 * width), jnp.bfloat16),
         ],
         scratch_shapes=[
-            pltpu.VMEM((rows, features), jnp.bfloat16),
-            pltpu.VMEM((features, width), jnp.bfloat16),
-            pltpu.VMEM((features, width), jnp.bfloat16),
-            pltpu.VMEM((rows, features), jnp.bfloat16),
+            pltpu.VMEM((LOADS, rows, chunk), jnp.bfloat16),
+            pltpu.VMEM((LOADS, chunk, 2 * width), jnp.bfloat16),
+            pltpu.VMEM((LOADS, rows, chunk), jnp.bfloat16),
             pltpu.VMEM((rows, 2 * width), jnp.float32),
-            pltpu.SemaphoreType.DMA((NORM_CHUNKS,)),
-            pltpu.SemaphoreType.DMA((NORM_CHUNKS,)),
-            pltpu.SemaphoreType.DMA((NORM_CHUNKS,)),
-            pltpu.SemaphoreType.DMA((NORM_CHUNKS,)),
+            pltpu.VMEM((rows, 128), jnp.float32),
+            pltpu.SemaphoreType.DMA((LOADS,)),
+            pltpu.SemaphoreType.DMA((LOADS,)),
+            pltpu.SemaphoreType.DMA((LOADS,)),
+            pltpu.SemaphoreType.DMA((LOADS,)),
         ],
         compiler_params=pltpu.CompilerParams(vmem_limit_bytes=57 * MIB),
         cost_estimate=pl.CostEstimate(
             flops=4 * rows * features * width, bytes_accessed=24 * MIB, transcendentals=0
         ),
         name="norm_project",
-    )(hidden, gain.reshape(1, features), key_weight, value_weight)
+    )(hidden, gain.reshape(LOADS, 1, chunk), key_weight, value_weight)
 
 
 def project_kernel(normed_ref, key_ref, value_ref, kv_ref, acc_scr):
@@ -187,14 +190,12 @@
             copy.wait()
 
     per_group = q_ref.shape[1] // HEAD_DIM // kv_heads
-    tile = 256
-    together = tile // block
     scale = HEAD_DIM**-0.5 * LOG2E
     token = lax.broadcasted_iota(jnp.int32, (block, HEAD_DIM), 0)
     lane = lax.broadcasted_iota(jnp.int32, (block, HEAD_DIM), 1)
     hidden_later = jnp.where((lane >= block) & (lane - block > token), MASKED, 0.0)
     query_mask = jnp.where(lane == 0, 1.0, hidden_later).astype(jnp.bfloat16)
-    query_mask = jnp.concatenate([query_mask] * together, axis=0)
+    query_mask = jnp.concatenate([query_mask] * per_group, axis=0)
     own_mask = jnp.where(lane - block == token, 1.0, 0.0).astype(jnp.bfloat16)
 
     def gather(local):
@@ -209,45 +210,43 @@
         masks.append(own_mask)
         return jnp.concatenate(pieces, axis=0), jnp.concatenate(masks, axis=0)
 
-    def score(local, head, first, every, mask):
+    def score(local, head, every, mask):
         keys = jnp.concatenate([every[:, head * HEAD_DIM : (head + 1) * HEAD_DIM], mask], axis=1)
         rows = slice(local * block, (local + 1) * block)
+        first = head * per_group
         queries = jnp.concatenate(
             [
                 q_ref[rows, r * HEAD_DIM : (r + 1) * HEAD_DIM]
-                for r in range(first, first + together)
+                for r in range(first, first + per_group)
             ],
             axis=0,
         )
         queries = jnp.concatenate([queries, query_mask], axis=1)
         return lax.dot_general(
-            keys, queries, (((1,), (1,)), ((), ())), preferred_element_type=jnp.float32
+            queries, keys, (((1,), (1,)), ((), ())), preferred_element_type=jnp.float32
         )
 
-    def finish(local, first, scores, flipped):
-        peak = jnp.max(scores, axis=0, keepdims=True)
+    def finish(local, head, scores, values):
+        peak = jnp.max(scores, axis=-1, keepdims=True)
         weights = jnp.exp2((scores - peak) * scale).astype(jnp.bfloat16)
-        both = jnp.dot(flipped, weights, preferred_element_type=jnp.float32)
-        context = both[:HEAD_DIM] * (1.0 / both[HEAD_DIM : HEAD_DIM + 1])
-        context = context.T.astype(jnp.bfloat16)
-        for r in range(together):
-            cols = slice((first + r) * HEAD_DIM, (first + r + 1) * HEAD_DIM)
-            out_ref[local * block : (local + 1) * block, cols] = context[r * block : (r + 1) * block]
+        padded = jnp.concatenate([values, jnp.ones_like(values)], axis=1)
+        both = jnp.dot(weights, padded, preferred_element_type=jnp.float32)
+        context = (both[:, :HEAD_DIM] * (1.0 / both[:, HEAD_DIM:])).astype(jnp.bfloat16)
+        for r in range(per_group):
+            first = (head * per_group + r) * HEAD_DIM
+            out_ref[local * block : (local + 1) * block, first : first + HEAD_DIM] = context[
+                r * block : (r + 1) * block
+            ]
 
     waiting = None
     for local in range(BLOCKS_PER_STEP):
         every, mask = gather(local)
         for head in range(kv_heads):
             start = (kv_heads + head) * HEAD_DIM
-            values = every[:, start : start + HEAD_DIM]
-            flipped = jnp.concatenate(
-                [values.T, jnp.ones((16, values.shape[0]), jnp.bfloat16)], axis=0
-            )
-            for first in range(head * per_group, (head + 1) * per_group, together):
-                scores = score(local, head, first, every, mask)
-                if waiting is not None:
-                    finish(*waiting)
-                waiting = (local, first, scores, flipped)
+            scores = score(local, head, every, mask)
+            if waiting is not None:
+                finish(*waiting)
+            waiting = (local, head, scores, every[:, start : start + HEAD_DIM])
     finish(*waiting)
 
 
@@ -337,16 +336,15 @@
     early, late = range(UNITS)
     across = [(s, unit) for s in range(near - 1) for unit in (early, late)]
     across += [(near - 1, early), (near, early), (near - 1, late)]
-    along = [(s, unit) for s in range(1, near + 1) for unit in (early, late)]
-    waves = []
-    for index, (s, unit) in enumerate(across):
-        settled = waves[-2] if len(waves) >= 2 else ()
-        wave = [step_across(s, unit, settled)]
-        if index < len(along):
-            wave.append(step_along(*along[index], settled))
+    along = [(1, early), (1, late)]
+    along += [(s, early) for s in range(2, near + 1)] + [(s, late) for s in range(2, near + 1)]
+    y_chain, z_chain = [], []
+    for (s, unit), step in zip(across, [*along, None], strict=True):
+        y_chain.append(step_across(s, unit, y_chain[-2:-1]))
+        if step is not None:
+            z_chain.append(step_along(*step, z_chain[-2:-1]))
         else:
-            wave.append(step_down(late, settled))
-        waves.append(wave)
+            z_chain.append(step_down(late, z_chain[-2:-1]))
     result = None
     for unit in range(UNITS):
         result = attention(

time: 123 us -> 123 us (level)
  waiting for transfers between devices: 46.7 us -> 50.7 us
  Pallas kernels: 49 us -> 45.8 us
    ppermute x6, waiting for transfers between devices: 27.3 us -> 39.7 us  [step_along(): straight[unit][s] = lax.ppermute(after(source, *settled), 'node', pairs)]
    ppermute x7, waiting for transfers between devices: 19.4 us -> 10.7 us  [step_across(): crossed[unit][s] = lax.ppermute(after(source, *settled), 'node', pairs)]
    pallas_call x2, Pallas kernels: 26.5 us -> 22.6 us  [attention(): pl.pallas_call(functools.partial(attention_kernel, block, near), grid_spe...]
  transfers between devices with their start and end apart: 14 -> 14, of which waited for: 9 -> 9; matrix products, arithmetic and copies ran while one was open for 0% -> 0% of each run, Pallas kernels for 18% -> 17%
where the time goes in v6:
time: 123 us; the launch traced here: 122 us
  waiting for transfers between devices  50.7 us (41%)
  Pallas kernels  45.8 us (37%)
  starting transfers between devices  24.5 us (20%)
    ppermute x6, waiting for transfers between devices, step_along(): straight[unit][s] = lax.ppermute(after(source, *settled), 'node', pairs)  39.7 us
    pallas_call x2, Pallas kernels, attention(): pl.pallas_call(functools.partial(attention_kernel, block, near), grid_spe...  22.6 us
    ppermute x7, starting transfers between devices, step_across(): crossed[unit][s] = lax.ppermute(after(source, *settled), 'node', pairs)  15.5 us
    pallas_call x1, Pallas kernels, norm_project(): pl.pallas_call(norm_project_kernel, in_specs=[held, whole, held, held], o...  14 us
    ppermute x7, waiting for transfers between devices, step_across(): crossed[unit][s] = lax.ppermute(after(source, *settled), 'node', pairs)  10.7 us
    pallas_call x1, Pallas kernels, project(): pl.pallas_call(project_kernel, grid=(CHUNKS,), in_specs=[pl.BlockSpec((ro...  9.26 us
    ppermute x6, starting transfers between devices, step_along(): straight[unit][s] = lax.ppermute(after(source, *settled), 'node', pairs)  7.74 us
  transfers between devices with their start and end apart: 14, of which 9 were waited for; matrix products, arithmetic and copies ran while one was open for 0% of the time, Pallas kernels for 17%

profile of v6, /device:TPU:24, one launch (start us, length us, event | category | flops | bytes accessed | tf_op | source)
XLA Modules:
  0.0 122.0 jit_solution(11254974911192157990)
XLA Ops:
  0.0 14.0 %norm_project.1 = (bf16[512,8192]{1,0:T(8,128)(2,1)}, bf16[512,512]{1,0:T(8,128)(2,1)}) custom-call(bf16[512,8192]{1,0:T(8,128)(2,1)} %x_hbm.1, f32[8,1,1024]{2,1,0:T(1,128)} %bitcast.2, bf16[8192,512]{1,0:T(8,128)(2,1)} %key_ref.1, bf16[8192,512]{1,0:T(8,128)(2,1)} %value_ref.1), custom_call_target="tpu_custom_call" | custom-call | flops 4294967296 | bytes 25165824 | tf_op jit(solution)/shard_map/norm_project/pallas_call | solution.py:112
  14.0 1.3 %collective-permute-start.1 = (bf16[512,512]{1,0:T(8,128)(2,1)}, bf16[512,512]{1,0:T(8,128)(2,1)S(1)}, u32[]{:S(2)}, u32[]{:S(2)}) collective-permute-start(bf16[512,512]{1,0:T(8,128)(2,1)} %get-tuple-element.18.refs_0_), channel_id=1, source_target_pairs={{0,4},{1,5},{2,6},{3,7},{4,8},{5,9},{6,10},{7,11},{8,12},{9,13},{1... | collective-permute-start | bytes 1572872 | tf_op jit(solution)/shard_map/ppermute | solution.py:327
  15.3 3.5 %collective-permute-start.8 = (bf16[512,512]{1,0:T(8,128)(2,1)}, bf16[512,512]{1,0:T(8,128)(2,1)S(1)}, u32[]{:S(2)}, u32[]{:S(2)}) collective-permute-start(bf16[512,512]{1,0:T(8,128)(2,1)} %get-tuple-element.18.refs_0_), channel_id=1, source_target_pairs={{0,2},{1,3},{4,6},{5,7},{8,10},{9,11},{12,14},{13,15},{16,18},{17,... | collective-permute-start | bytes 1572872 | tf_op jit(solution)/shard_map/ppermute | solution.py:320
  18.8 0.0 copy-start.8
  18.8 9.3 %project.1.refs_0_ = bf16[512,512]{1,0:T(8,128)(2,1)} custom-call(bf16[512,8192]{1,0:T(8,128)(2,1)} %get-tuple-element.17.normed_ref, bf16[8192,512]{1,0:T(8,128)(2,1)} %key_ref.1, bf16[8192,512]{1,0:T(8,128)(2,1)} %value_ref.1), custom_call_target="tpu_custom_call" | custom-call | flops 4294967296 | bytes 16777216 | tf_op jit(solution)/shard_map/project/pallas_call | solution.py:158
  28.0 1.3 %collective-permute-start.6 = (bf16[512,512]{1,0:T(8,128)(2,1)}, bf16[512,512]{1,0:T(8,128)(2,1)S(1)}, u32[]{:S(2)}, u32[]{:S(2)}) collective-permute-start(bf16[512,512]{1,0:T(8,128)(2,1)} %project.1.refs_0_), channel_id=1, source_target_pairs={{0,2},{1,3},{2,0},{3,1},{4,6},{5,7},{8,10},{9,11},{12,14},{13,15},... | collective-permute-start | bytes 1572872 | tf_op jit(solution)/shard_map/ppermute | solution.py:320
  29.4 1.3 %collective-permute-start = (bf16[512,512]{1,0:T(8,128)(2,1)}, bf16[512,512]{1,0:T(8,128)(2,1)S(1)}, u32[]{:S(2)}, u32[]{:S(2)}) collective-permute-start(bf16[512,512]{1,0:T(8,128)(2,1)} %project.1.refs_0_), channel_id=1, source_target_pairs={{0,4},{1,5},{2,6},{3,7},{4,8},{5,9},{6,10},{7,11},{8,12},{9,13},{1... | collective-permute-start | bytes 1572872 | tf_op jit(solution)/shard_map/ppermute | solution.py:327
  30.7 0.0 collective-permute-done.1.refs_1_
  30.7 0.0 copy-start.2
  30.7 1.3 %collective-permute-start.2 = (bf16[512,512]{1,0:T(8,128)(2,1)S(1)}, bf16[512,512]{1,0:T(8,128)(2,1)S(1)}, u32[]{:S(2)}, u32[]{:S(2)}) collective-permute-start(bf16[512,512]{1,0:T(8,128)(2,1)S(1)} %collective-permute-done.1.refs_1_), channel_id=1, source_target_pairs={{4,8},{5,9},{6,10},{7,11},{8,12},{9,13},{10,14},{11,15},{20,24},{2... | collective-permute-start | bytes 1572872 | tf_op jit(solution)/shard_map/ppermute | solution.py:327
  32.0 0.0 collective-permute-done.8.refs_4_
  32.0 0.0 copy-start.3
  32.0 3.1 %collective-permute-start.9 = (bf16[512,512]{1,0:T(8,128)(2,1)S(1)}, bf16[512,512]{1,0:T(8,128)(2,1)S(1)}, u32[]{:S(2)}, u32[]{:S(2)}) collective-permute-start(bf16[512,512]{1,0:T(8,128)(2,1)S(1)} %collective-permute-done.1.refs_1_), channel_id=1, source_target_pairs={{4,6},{5,7},{6,4},{7,5},{8,10},{9,11},{10,8},{11,9},{12,14},{13,15... | collective-permute-start | bytes 1572872 | tf_op jit(solution)/shard_map/ppermute | solution.py:320
  35.1 7.0 %collective-permute-done.6.refs_4_ = bf16[512,512]{1,0:T(8,128)(2,1)S(1)} collective-permute-done((bf16[512,512]{1,0:T(8,128)(2,1)}, bf16[512,512]{1,0:T(8,128)(2,1)S(1)}, u32[]{:S(2)}, u32[]{:S(2)}) %collective-permute-start.6) | collective-permute-done | bytes 524320 | tf_op jit(solution)/shard_map/ppermute | solution.py:320
  42.0 0.0 copy-start
  42.0 4.9 %collective-permute-done.refs_1_ = bf16[512,512]{1,0:T(8,128)(2,1)S(1)} collective-permute-done((bf16[512,512]{1,0:T(8,128)(2,1)}, bf16[512,512]{1,0:T(8,128)(2,1)S(1)}, u32[]{:S(2)}, u32[]{:S(2)}) %collective-permute-start) | collective-permute-done | bytes 524320 | tf_op jit(solution)/shard_map/ppermute | solution.py:327
  46.9 0.0 copy-start.1
  47.0 1.9 %collective-permute-start.7 = (bf16[512,512]{1,0:T(8,128)(2,1)S(1)}, bf16[512,512]{1,0:T(8,128)(2,1)S(1)}, u32[]{:S(2)}, u32[]{:S(2)}) collective-permute-start(bf16[512,512]{1,0:T(8,128)(2,1)S(1)} %collective-permute-done.refs_1_), channel_id=1, source_target_pairs={{4,6},{5,7},{6,4},{7,5},{8,10},{9,11},{10,8},{11,9},{12,14},{13,15... | collective-permute-start | bytes 1572872 | tf_op jit(solution)/shard_map/ppermute | solution.py:320
  48.9 7.9 %collective-permute-done.2.refs_2_ = bf16[512,512]{1,0:T(8,128)(2,1)S(1)} collective-permute-done((bf16[512,512]{1,0:T(8,128)(2,1)S(1)}, bf16[512,512]{1,0:T(8,128)(2,1)S(1)}, u32[]{:S(2)}, u32[]{:S(2)}) %collective-permute-start.2) | collective-permute-done | bytes 524320 | tf_op jit(solution)/shard_map/ppermute | solution.py:327
  56.7 1.3 %collective-permute-start.4 = (bf16[512,512]{1,0:T(8,128)(2,1)S(1)}, bf16[512,512]{1,0:T(8,128)(2,1)}, u32[]{:S(2)}, u32[]{:S(2)}) collective-permute-start(bf16[512,512]{1,0:T(8,128)(2,1)S(1)} %collective-permute-done.2.refs_2_), channel_id=1, source_target_pairs={{8,12},{9,13},{10,14},{11,15},{24,28},{25,29},{26,30},{27,31}} | collective-permute-start | bytes 1572872 | tf_op jit(solution)/shard_map/ppermute | solution.py:327
  58.0 1.3 %collective-permute-start.3 = (bf16[512,512]{1,0:T(8,128)(2,1)S(1)}, bf16[512,512]{1,0:T(8,128)(2,1)}, u32[]{:S(2)}, u32[]{:S(2)}) collective-permute-start(bf16[512,512]{1,0:T(8,128)(2,1)S(1)} %collective-permute-done.refs_1_), channel_id=1, source_target_pairs={{4,8},{5,9},{6,10},{7,11},{8,12},{9,13},{10,14},{11,15},{20,24},{2... | collective-permute-start | bytes 1572872 | tf_op jit(solution)/shard_map/ppermute | solution.py:327
  59.3 0.0 collective-permute-done.9.refs_5_
  59.3 0.0 copy-start.6
  59.3 1.9 %collective-permute-start.10 = (bf16[512,512]{1,0:T(8,128)(2,1)S(1)}, bf16[512,512]{1,0:T(8,128)(2,1)S(1)}, u32[]{:S(2)}, u32[]{:S(2)}) collective-permute-start(bf16[512,512]{1,0:T(8,128)(2,1)S(1)} %collective-permute-done.2.refs_2_), channel_id=1, source_target_pairs={{8,10},{9,11},{10,8},{11,9},{12,14},{13,15},{14,12},{15,13},{24,26... | collective-permute-start | bytes 1572872 | tf_op jit(solution)/shard_map/ppermute | solution.py:320
  61.3 3.1 %collective-permute-done.7.refs_5_ = bf16[512,512]{1,0:T(8,128)(2,1)S(1)} collective-permute-done((bf16[512,512]{1,0:T(8,128)(2,1)S(1)}, bf16[512,512]{1,0:T(8,128)(2,1)S(1)}, u32[]{:S(2)}, u32[]{:S(2)}) %collective-permute-start.7) | collective-permute-done | bytes 524320 | tf_op jit(solution)/shard_map/ppermute | solution.py:320
  64.4 9.2 %collective-permute-done.4.refs_3_ = bf16[512,512]{1,0:T(8,128)(2,1)} collective-permute-done((bf16[512,512]{1,0:T(8,128)(2,1)S(1)}, bf16[512,512]{1,0:T(8,128)(2,1)}, u32[]{:S(2)}, u32[]{:S(2)}) %collective-permute-start.4) | collective-permute-done | bytes 524320 | tf_op jit(solution)/shard_map/ppermute | solution.py:327
  73.6 1.9 %collective-permute-start.13 = (bf16[512,512]{1,0:T(8,128)(2,1)}, bf16[512,512]{1,0:T(8,128)(2,1)}, u32[]{:S(2)}, u32[]{:S(2)}) collective-permute-start(bf16[512,512]{1,0:T(8,128)(2,1)} %collective-permute-done.4.refs_3_), channel_id=1, source_target_pairs={{12,14},{13,15},{14,12},{15,13},{28,30},{29,31},{30,28},{31,29}} | collective-permute-start | bytes 1572872 | tf_op jit(solution)/shard_map/ppermute | solution.py:320
  75.5 6.9 %collective-permute-done.3.refs_2_ = bf16[512,512]{1,0:T(8,128)(2,1)} collective-permute-done((bf16[512,512]{1,0:T(8,128)(2,1)S(1)}, bf16[512,512]{1,0:T(8,128)(2,1)}, u32[]{:S(2)}, u32[]{:S(2)}) %collective-permute-start.3) | collective-permute-done | bytes 524320 | tf_op jit(solution)/shard_map/ppermute | solution.py:327
  82.4 0.0 collective-permute-done.10.refs_6_
  82.4 0.0 copy-done.6
  82.4 1.9 %collective-permute-start.11 = (bf16[512,512]{1,0:T(8,128)(2,1)}, bf16[512,512]{1,0:T(8,128)(2,1)}, u32[]{:S(2)}, u32[]{:S(2)}) collective-permute-start(bf16[512,512]{1,0:T(8,128)(2,1)} %collective-permute-done.3.refs_2_), channel_id=1, source_target_pairs={{8,10},{9,11},{10,8},{11,9},{12,14},{13,15},{14,12},{15,13},{24,26... | collective-permute-start | bytes 1572872 | tf_op jit(solution)/shard_map/ppermute | solution.py:320
  84.4 0.0 copy-done.7
  84.4 1.3 %collective-permute-start.12 = (bf16[512,512]{1,0:T(8,128)(2,1)S(1)}, bf16[512,512]{1,0:T(8,128)(2,1)}, u32[]{:S(2)}, u32[]{:S(2)}) collective-permute-start(bf16[512,512]{1,0:T(8,128)(2,1)S(1)} %collective-permute-done.6.refs_4_), channel_id=1, source_target_pairs={{0,12},{1,13},{2,14},{3,15},{16,28},{17,29},{18,30},{19,31}} | collective-permute-start | bytes 1572872 | tf_op jit(solution)/shard_map/ppermute | solution.py:333
  85.7 1.3 %collective-permute-start.5 = (bf16[512,512]{1,0:T(8,128)(2,1)}, bf16[512,512]{1,0:T(8,128)(2,1)}, u32[]{:S(2)}, u32[]{:S(2)}) collective-permute-start(bf16[512,512]{1,0:T(8,128)(2,1)} %collective-permute-done.3.refs_2_), channel_id=1, source_target_pairs={{8,12},{9,13},{10,14},{11,15},{24,28},{25,29},{26,30},{27,31}} | collective-permute-start | bytes 1572872 | tf_op jit(solution)/shard_map/ppermute | solution.py:327
  87.0 0.0 copy-done.8
  87.0 0.6 fusion.1.slot_ref
  87.6 0.6 collective-permute-done.13.refs_7_
  88.2 0.0 copy-done.2
  88.2 0.0 copy-done.3
  88.2 0.0 copy-done.5
  88.2 11.3 %attention.2.refs_8_ = bf16[512,4096]{1,0:T(8,128)(2,1)} custom-call(s32[8,7]{1,0:T(8,128)} %fusion.1.slot_ref, s32[8,7]{1,0:T(8,128)} %cut_ref.3, s32[1]{0:T(128)} %bitcast.odd_ref, bf16[512,4096]{1,0:T(8,128)(2,1)} %q_ref.3, bf16[512,512]{1,0:T(8,128)(2,1)} %get-tuple-element.18.refs_0_, bf16[512,512]{1,0:T(8,128)(2,1)} %copy-done.2, ...), custom_call_target="tpu_custom_call" | custom-call | flops 2147483648 | bytes 8388608 | tf_op jit(solution)/shard_map/attention/pallas_call | solution.py:268
  99.5 0.0 collective-permute-done.11.refs_6_
  99.5 0.4 collective-permute-done.12.refs_7_
  99.8 10.8 %collective-permute-done.5.refs_3_ = bf16[512,512]{1,0:T(8,128)(2,1)} collective-permute-done((bf16[512,512]{1,0:T(8,128)(2,1)}, bf16[512,512]{1,0:T(8,128)(2,1)}, u32[]{:S(2)}, u32[]{:S(2)}) %collective-permute-start.5) | collective-permute-done | bytes 524320 | tf_op jit(solution)/shard_map/ppermute | solution.py:327
  110.7 0.0 copy-done
  110.7 0.0 copy-done.1
  110.7 0.0 copy-done.4
  110.7 11.3 %attention.3 = bf16[512,4096]{1,0:T(8,128)(2,1)} custom-call(s32[8,7]{1,0:T(8,128)} %fusion.1.slot_ref, s32[8,7]{1,0:T(8,128)} %cut_ref.3, s32[1]{0:T(128)} %bitcast.odd_ref, bf16[512,4096]{1,0:T(8,128)(2,1)} %q_ref.3, bf16[512,512]{1,0:T(8,128)(2,1)} %project.1.refs_0_, bf16[512,512]{1,0:T(8,128)(2,1)} %copy-done.1, ...), custom_call_target="tpu_custom_call", output_to_operand_aliasing={{}: (12, {})} | custom-call | flops 2147483648 | bytes 8388608 | tf_op jit(solution)/shard_map/attention/pallas_call | solution.py:268
  (3 shorter events, 0.0 us)
Async XLA Ops:
  14.0 16.7 %collective-permute-start.1 = (bf16[512,512]{1,0:T(8,128)(2,1)}, bf16[512,512]{1,0:T(8,128)(2,1)S(1)}, u32[]{:S(2)}, u32[]{:S(2)}) collective-permute-start(bf16[512,512]{1,0:T(8,128)(2,1)} %get-tuple-element.18.refs_0_), channel_id=1, source_target_pairs={{0,4},{1,5},{2,6},{3,7},{4,8},{5,9},{6,10},{7,11},{8,12},{9,13},{1... | collective-permute-start | bytes 1572872 | tf_op jit(solution)/shard_map/ppermute | solution.py:327
  15.3 16.7 %collective-permute-start.8 = (bf16[512,512]{1,0:T(8,128)(2,1)}, bf16[512,512]{1,0:T(8,128)(2,1)S(1)}, u32[]{:S(2)}, u32[]{:S(2)}) collective-permute-start(bf16[512,512]{1,0:T(8,128)(2,1)} %get-tuple-element.18.refs_0_), channel_id=1, source_target_pairs={{0,2},{1,3},{4,6},{5,7},{8,10},{9,11},{12,14},{13,15},{16,18},{17,... | collective-permute-start | bytes 1572872 | tf_op jit(solution)/shard_map/ppermute | solution.py:320
  18.8 68.2 %copy-start.8 = (s32[8,7]{1,0:T(8,128)S(1)}, s32[8,7]{1,0:T(8,128)}, u32[]{:S(2)}) copy-start(s32[8,7]{1,0:T(8,128)} %param.12) | copy-start | bytes 676
  28.0 14.0 %collective-permute-start.6 = (bf16[512,512]{1,0:T(8,128)(2,1)}, bf16[512,512]{1,0:T(8,128)(2,1)S(1)}, u32[]{:S(2)}, u32[]{:S(2)}) collective-permute-start(bf16[512,512]{1,0:T(8,128)(2,1)} %project.1.refs_0_), channel_id=1, source_target_pairs={{0,2},{1,3},{2,0},{3,1},{4,6},{5,7},{8,10},{9,11},{12,14},{13,15},... | collective-permute-start | bytes 1572872 | tf_op jit(solution)/shard_map/ppermute | solution.py:320
  29.4 17.6 %collective-permute-start = (bf16[512,512]{1,0:T(8,128)(2,1)}, bf16[512,512]{1,0:T(8,128)(2,1)S(1)}, u32[]{:S(2)}, u32[]{:S(2)}) collective-permute-start(bf16[512,512]{1,0:T(8,128)(2,1)} %project.1.refs_0_), channel_id=1, source_target_pairs={{0,4},{1,5},{2,6},{3,7},{4,8},{5,9},{6,10},{7,11},{8,12},{9,13},{1... | collective-permute-start | bytes 1572872 | tf_op jit(solution)/shard_map/ppermute | solution.py:327
  30.7 57.5 %copy-start.2 = (bf16[512,512]{1,0:T(8,128)(2,1)}, bf16[512,512]{1,0:T(8,128)(2,1)S(1)}, u32[]{:S(2)}) copy-start(bf16[512,512]{1,0:T(8,128)(2,1)S(1)} %collective-permute-done.1.refs_1_) | copy-start | bytes 1572868
  30.7 26.0 %collective-permute-start.2 = (bf16[512,512]{1,0:T(8,128)(2,1)S(1)}, bf16[512,512]{1,0:T(8,128)(2,1)S(1)}, u32[]{:S(2)}, u32[]{:S(2)}) collective-permute-start(bf16[512,512]{1,0:T(8,128)(2,1)S(1)} %collective-permute-done.1.refs_1_), channel_id=1, source_target_pairs={{4,8},{5,9},{6,10},{7,11},{8,12},{9,13},{10,14},{11,15},{20,24},{2... | collective-permute-start | bytes 1572872 | tf_op jit(solution)/shard_map/ppermute | solution.py:327
  32.0 56.2 %copy-start.3 = (bf16[512,512]{1,0:T(8,128)(2,1)}, bf16[512,512]{1,0:T(8,128)(2,1)S(1)}, u32[]{:S(2)}) copy-start(bf16[512,512]{1,0:T(8,128)(2,1)S(1)} %collective-permute-done.8.refs_4_) | copy-start | bytes 1572868
  32.0 27.3 %collective-permute-start.9 = (bf16[512,512]{1,0:T(8,128)(2,1)S(1)}, bf16[512,512]{1,0:T(8,128)(2,1)S(1)}, u32[]{:S(2)}, u32[]{:S(2)}) collective-permute-start(bf16[512,512]{1,0:T(8,128)(2,1)S(1)} %collective-permute-done.1.refs_1_), channel_id=1, source_target_pairs={{4,6},{5,7},{6,4},{7,5},{8,10},{9,11},{10,8},{11,9},{12,14},{13,15... | collective-permute-start | bytes 1572872 | tf_op jit(solution)/shard_map/ppermute | solution.py:320
  42.0 68.6 %copy-start = (bf16[512,512]{1,0:T(8,128)(2,1)}, bf16[512,512]{1,0:T(8,128)(2,1)S(1)}, u32[]{:S(2)}) copy-start(bf16[512,512]{1,0:T(8,128)(2,1)S(1)} %collective-permute-done.6.refs_4_) | copy-start | bytes 1572868
  46.9 63.7 %copy-start.1 = (bf16[512,512]{1,0:T(8,128)(2,1)}, bf16[512,512]{1,0:T(8,128)(2,1)S(1)}, u32[]{:S(2)}) copy-start(bf16[512,512]{1,0:T(8,128)(2,1)S(1)} %collective-permute-done.refs_1_) | copy-start | bytes 1572868
  47.0 17.5 %collective-permute-start.7 = (bf16[512,512]{1,0:T(8,128)(2,1)S(1)}, bf16[512,512]{1,0:T(8,128)(2,1)S(1)}, u32[]{:S(2)}, u32[]{:S(2)}) collective-permute-start(bf16[512,512]{1,0:T(8,128)(2,1)S(1)} %collective-permute-done.refs_1_), channel_id=1, source_target_pairs={{4,6},{5,7},{6,4},{7,5},{8,10},{9,11},{10,8},{11,9},{12,14},{13,15... | collective-permute-start | bytes 1572872 | tf_op jit(solution)/shard_map/ppermute | solution.py:320
  56.7 31.5 %copy-start.5 = (bf16[512,512]{1,0:T(8,128)(2,1)}, bf16[512,512]{1,0:T(8,128)(2,1)S(1)}, u32[]{:S(2)}) copy-start(bf16[512,512]{1,0:T(8,128)(2,1)S(1)} %collective-permute-done.2.refs_2_) | copy-start | bytes 1572868
  56.7 16.8 %collective-permute-start.4 = (bf16[512,512]{1,0:T(8,128)(2,1)S(1)}, bf16[512,512]{1,0:T(8,128)(2,1)}, u32[]{:S(2)}, u32[]{:S(2)}) collective-permute-start(bf16[512,512]{1,0:T(8,128)(2,1)S(1)} %collective-permute-done.2.refs_2_), channel_id=1, source_target_pairs={{8,12},{9,13},{10,14},{11,15},{24,28},{25,29},{26,30},{27,31}} | collective-permute-start | bytes 1572872 | tf_op jit(solution)/shard_map/ppermute | solution.py:327
  58.0 24.4 %collective-permute-start.3 = (bf16[512,512]{1,0:T(8,128)(2,1)S(1)}, bf16[512,512]{1,0:T(8,128)(2,1)}, u32[]{:S(2)}, u32[]{:S(2)}) collective-permute-start(bf16[512,512]{1,0:T(8,128)(2,1)S(1)} %collective-permute-done.refs_1_), channel_id=1, source_target_pairs={{4,8},{5,9},{6,10},{7,11},{8,12},{9,13},{10,14},{11,15},{20,24},{2... | collective-permute-start | bytes 1572872 | tf_op jit(solution)/shard_map/ppermute | solution.py:327
  59.3 23.1 %copy-start.6 = (bf16[512,512]{1,0:T(8,128)(2,1)}, bf16[512,512]{1,0:T(8,128)(2,1)S(1)}, u32[]{:S(2)}) copy-start(bf16[512,512]{1,0:T(8,128)(2,1)S(1)} %collective-permute-done.9.refs_5_) | copy-start | bytes 1572868
  59.3 23.1 %collective-permute-start.10 = (bf16[512,512]{1,0:T(8,128)(2,1)S(1)}, bf16[512,512]{1,0:T(8,128)(2,1)S(1)}, u32[]{:S(2)}, u32[]{:S(2)}) collective-permute-start(bf16[512,512]{1,0:T(8,128)(2,1)S(1)} %collective-permute-done.2.refs_2_), channel_id=1, source_target_pairs={{8,10},{9,11},{10,8},{11,9},{12,14},{13,15},{14,12},{15,13},{24,26... | collective-permute-start | bytes 1572872 | tf_op jit(solution)/shard_map/ppermute | solution.py:320
  64.4 46.3 %copy-start.4 = (bf16[512,512]{1,0:T(8,128)(2,1)}, bf16[512,512]{1,0:T(8,128)(2,1)S(1)}, u32[]{:S(2)}) copy-start(bf16[512,512]{1,0:T(8,128)(2,1)S(1)} %collective-permute-done.7.refs_5_) | copy-start | bytes 1572868
  73.6 14.6 %collective-permute-start.13 = (bf16[512,512]{1,0:T(8,128)(2,1)}, bf16[512,512]{1,0:T(8,128)(2,1)}, u32[]{:S(2)}, u32[]{:S(2)}) collective-permute-start(bf16[512,512]{1,0:T(8,128)(2,1)} %collective-permute-done.4.refs_3_), channel_id=1, source_target_pairs={{12,14},{13,15},{14,12},{15,13},{28,30},{29,31},{30,28},{31,29}} | collective-permute-start | bytes 1572872 | tf_op jit(solution)/shard_map/ppermute | solution.py:320
  82.4 1.9 %copy-start.7 = (bf16[512,512]{1,0:T(8,128)(2,1)}, bf16[512,512]{1,0:T(8,128)(2,1)S(1)}, u32[]{:S(2)}) copy-start(bf16[512,512]{1,0:T(8,128)(2,1)S(1)} %collective-permute-done.10.refs_6_) | copy-start | bytes 1572868
  82.4 17.0 %collective-permute-start.11 = (bf16[512,512]{1,0:T(8,128)(2,1)}, bf16[512,512]{1,0:T(8,128)(2,1)}, u32[]{:S(2)}, u32[]{:S(2)}) collective-permute-start(bf16[512,512]{1,0:T(8,128)(2,1)} %collective-permute-done.3.refs_2_), channel_id=1, source_target_pairs={{8,10},{9,11},{10,8},{11,9},{12,14},{13,15},{14,12},{15,13},{24,26... | collective-permute-start | bytes 1572872 | tf_op jit(solution)/shard_map/ppermute | solution.py:320
  84.4 15.5 %collective-permute-start.12 = (bf16[512,512]{1,0:T(8,128)(2,1)S(1)}, bf16[512,512]{1,0:T(8,128)(2,1)}, u32[]{:S(2)}, u32[]{:S(2)}) collective-permute-start(bf16[512,512]{1,0:T(8,128)(2,1)S(1)} %collective-permute-done.6.refs_4_), channel_id=1, source_target_pairs={{0,12},{1,13},{2,14},{3,15},{16,28},{17,29},{18,30},{19,31}} | collective-permute-start | bytes 1572872 | tf_op jit(solution)/shard_map/ppermute | solution.py:333
  85.7 25.0 %collective-permute-start.5 = (bf16[512,512]{1,0:T(8,128)(2,1)}, bf16[512,512]{1,0:T(8,128)(2,1)}, u32[]{:S(2)}, u32[]{:S(2)}) collective-permute-start(bf16[512,512]{1,0:T(8,128)(2,1)} %collective-permute-done.3.refs_2_), channel_id=1, source_target_pairs={{8,12},{9,13},{10,14},{11,15},{24,28},{25,29},{26,30},{27,31}} | collective-permute-start | bytes 1572872 | tf_op jit(solution)/shard_map/ppermute | solution.py:327

commit v7 on v6

--- a/solution.py
+++ b/solution.py
@@ -14,12 +14,12 @@
 CHUNKS = 4
 LOADS = 8
 UNITS = 2
-BLOCKS_PER_STEP = 2
+BLOCKS_PER_STEP = 4
 
 
 def norm_project_kernel(
     x_hbm, gain_ref, key_hbm, value_hbm, normed_hbm, kv_ref,
-    x_scr, weight_scr, normed_scr, acc_scr, scale_scr, x_sem, key_sem, value_sem, normed_sem,
+    x_scr, weight_scr, even_scr, odd_scr, acc_scr, scale_scr, x_sem, key_sem, value_sem, normed_sem,
 ):
     loads, rows, chunk = x_scr.shape
     width = weight_scr.shape[2] // 2
@@ -43,8 +43,10 @@
             ),
         ]
 
-    def store_normed(c):
-        return pltpu.make_async_copy(normed_scr.at[c], normed_hbm.at[:, span(c)], normed_sem.at[c])
+    def store_normed(normed_scr, c):
+        return pltpu.make_async_copy(
+            normed_scr.at[c // 2], normed_hbm.at[:, span(c)], normed_sem.at[c]
+        )
 
     for c in range(loads):
         load_x(c).start()
@@ -72,7 +74,7 @@
     mean_sq = jnp.sum(scale_scr[...], axis=-1, keepdims=True) / (loads * chunk)
     scale_scr[...] = jnp.broadcast_to(lax.rsqrt(mean_sq + EPS), scale_scr.shape)
 
-    def normalise(c):
+    def normalise(normed_scr, c):
         for first in range(0, rows, band):
             row = slice(first, first + band)
             inverse = scale_scr[row, :]
@@ -80,27 +82,37 @@
                 cols = slice(lane, lane + lanes)
                 x = x_scr[c, row, cols].astype(jnp.float32)
                 gain = gain_ref[c, :, cols]
-                normed_scr[c, row, cols] = (x * inverse * gain).astype(jnp.bfloat16)
-
-    normalise(0)
-    acc_scr[...] = jnp.zeros_like(acc_scr)
-
-    def multiply(c, carry):
+                normed_scr[c // 2, row, cols] = (x * inverse * gain).astype(jnp.bfloat16)
+
+    def multiply(normed_scr, c):
         for copy in load_weights(c):
             copy.wait()
-        store_normed(c).start()
-        acc_scr[...] += jnp.dot(normed_scr[c], weight_scr[c], preferred_element_type=jnp.float32)
-
-        @pl.when(c < loads - 1)
-        def _():
-            normalise(c + 1)
-
+        store_normed(normed_scr, c).start()
+        acc_scr[...] += jnp.dot(
+            normed_scr[c // 2], weight_scr[c], preferred_element_type=jnp.float32
+        )
+
+    normalise(even_scr, 0)
+    acc_scr[...] = jnp.zeros_like(acc_scr)
+
+    def pair(p, carry):
+        multiply(even_scr, 2 * p)
+        normalise(odd_scr, 2 * p + 1)
+        multiply(odd_scr, 2 * p + 1)
+        normalise(even_scr, 2 * p + 2)
         return carry
 
-    lax.fori_loop(0, loads, multiply, 0)
-    kv_ref[...] = acc_scr[...].astype(jnp.bfloat16)
+    lax.fori_loop(0, loads // 2 - 1, pair, 0)
+    multiply(even_scr, loads - 2)
+    normalise(odd_scr, loads - 1)
+    multiply(odd_scr, loads - 1)
+    for head in range(width // HEAD_DIM):
+        for part in range(2):
+            source = slice(part * width + head * HEAD_DIM, part * width + (head + 1) * HEAD_DIM)
+            target = slice((2 * head + part) * HEAD_DIM, (2 * head + part + 1) * HEAD_DIM)
+            kv_ref[:, target] = acc_scr[:, source].astype(jnp.bfloat16)
     for c in range(loads):
-        store_normed(c).wait()
+        store_normed(odd_scr if c % 2 else even_scr, c).wait()
 
 
 def norm_project(hidden, gain, key_weight, value_weight):
@@ -120,7 +132,8 @@
         scratch_shapes=[
             pltpu.VMEM((LOADS, rows, chunk), jnp.bfloat16),
             pltpu.VMEM((LOADS, chunk, 2 * width), jnp.bfloat16),
-            pltpu.VMEM((LOADS, rows, chunk), jnp.bfloat16),
+            pltpu.VMEM((LOADS // 2, rows, chunk), jnp.bfloat16),
+            pltpu.VMEM((LOADS // 2, rows, chunk), jnp.bfloat16),
             pltpu.VMEM((rows, 2 * width), jnp.float32),
             pltpu.VMEM((rows, 128), jnp.float32),
             pltpu.SemaphoreType.DMA((LOADS,)),
@@ -147,7 +160,11 @@
 
     @pl.when(step == CHUNKS - 1)
     def _():
-        kv_ref[...] = acc_scr[...].astype(jnp.bfloat16)
+        for head in range(width // HEAD_DIM):
+            for part in range(2):
+                source = slice(part * width + head * HEAD_DIM, part * width + (head + 1) * HEAD_DIM)
+                target = slice((2 * head + part) * HEAD_DIM, (2 * head + part + 1) * HEAD_DIM)
+                kv_ref[:, target] = acc_scr[:, source].astype(jnp.bfloat16)
 
 
 def project(normed, key_weight, value_weight, unit):
@@ -173,24 +190,40 @@
 def attention_kernel(block, near, slot_ref, cut_ref, odd_ref, q_ref, *refs):
     own_hbm, straight, crossed = refs[0], refs[1 : near + 1], refs[near + 1 : 2 * near + 2]
     out_ref, kv_scr, sems = refs[-3:]
-    depth = slot_ref.shape[1]
-    kv_heads = kv_scr.shape[2] // (2 * HEAD_DIM)
-
-    @pl.when(pl.program_id(0) == 0)
-    def _():
-        copies = [pltpu.make_async_copy(own_hbm, kv_scr.at[depth], sems.at[0])]
+    kv_heads, levels = kv_scr.shape[:2]
+    depth = levels - 1
+    width = kv_scr.shape[3]
+    per_group = q_ref.shape[1] // HEAD_DIM
+    head, step = pl.program_id(0), pl.program_id(1)
+    scale = HEAD_DIM**-0.5 * LOG2E
+
+    def fetch(index):
+        def copy(ref, level, number):
+            return pltpu.make_async_copy(
+                ref.at[:, pl.ds(pl.multiple_of(index * width, width), width)],
+                kv_scr.at[index, level],
+                sems.at[index, number],
+            )
+
+        copies = [copy(own_hbm, depth, 0)]
         for s, ref in enumerate(straight):
-            copies.append(pltpu.make_async_copy(ref, kv_scr.at[2 * s + 1], sems.at[s + 1]))
+            copies.append(copy(ref, 2 * s + 1, s + 1))
         for s, ref in enumerate(crossed):
             level = 2 * lax.rem(s + odd_ref[0] + near, near + 1)
-            copies.append(pltpu.make_async_copy(ref, kv_scr.at[level], sems.at[near + s + 1]))
-        for copy in copies:
-            copy.start()
-        for copy in copies:
+            copies.append(copy(ref, level, near + s + 1))
+        return copies
+
+    @pl.when((head == 0) & (step == 0))
+    def _():
+        for index in range(kv_heads):
+            for copy in fetch(index):
+                copy.start()
+
+    @pl.when(step == 0)
+    def _():
+        for copy in fetch(head):
             copy.wait()
 
-    per_group = q_ref.shape[1] // HEAD_DIM // kv_heads
-    scale = HEAD_DIM**-0.5 * LOG2E
     token = lax.broadcasted_iota(jnp.int32, (block, HEAD_DIM), 0)
     lane = lax.broadcasted_iota(jnp.int32, (block, HEAD_DIM), 1)
     hidden_later = jnp.where((lane >= block) & (lane - block > token), MASKED, 0.0)
@@ -198,55 +231,46 @@
     query_mask = jnp.concatenate([query_mask] * per_group, axis=0)
     own_mask = jnp.where(lane - block == token, 1.0, 0.0).astype(jnp.bfloat16)
 
-    def gather(local):
-        here = pl.program_id(0) * BLOCKS_PER_STEP + local
+    def score(local):
+        here = step * BLOCKS_PER_STEP + local
         pieces, masks = [], []
         for k in range(depth):
             rows = pl.ds(pl.multiple_of(slot_ref[here, k] * block, block), block)
-            pieces.append(kv_scr[k, rows, :])
+            pieces.append(kv_scr[head, k, rows, :])
             unseen = (lane == 0) & (token >= cut_ref[here, k])
             masks.append(jnp.where(unseen, MASKED, 0.0).astype(jnp.bfloat16))
-        pieces.append(kv_scr[depth, pl.ds(pl.multiple_of(here * block, block), block), :])
+        rows = pl.ds(pl.multiple_of(here * block, block), block)
+        pieces.append(kv_scr[head, depth, rows, :])
         masks.append(own_mask)
-        return jnp.concatenate(pieces, axis=0), jnp.concatenate(masks, axis=0)
-
-    def score(local, head, every, mask):
-        keys = jnp.concatenate([every[:, head * HEAD_DIM : (head + 1) * HEAD_DIM], mask], axis=1)
+        every = jnp.concatenate(pieces, axis=0)
+        keys = jnp.concatenate([every[:, :HEAD_DIM], jnp.concatenate(masks, axis=0)], axis=1)
         rows = slice(local * block, (local + 1) * block)
-        first = head * per_group
         queries = jnp.concatenate(
-            [
-                q_ref[rows, r * HEAD_DIM : (r + 1) * HEAD_DIM]
-                for r in range(first, first + per_group)
-            ],
-            axis=0,
+            [q_ref[rows, r * HEAD_DIM : (r + 1) * HEAD_DIM] for r in range(per_group)], axis=0
         )
         queries = jnp.concatenate([queries, query_mask], axis=1)
-        return lax.dot_general(
+        scores = lax.dot_general(
             queries, keys, (((1,), (1,)), ((), ())), preferred_element_type=jnp.float32
         )
-
-    def finish(local, head, scores, values):
+        return scores, every[:, HEAD_DIM:]
+
+    def finish(local, scores, values):
         peak = jnp.max(scores, axis=-1, keepdims=True)
         weights = jnp.exp2((scores - peak) * scale).astype(jnp.bfloat16)
         padded = jnp.concatenate([values, jnp.ones_like(values)], axis=1)
         both = jnp.dot(weights, padded, preferred_element_type=jnp.float32)
         context = (both[:, :HEAD_DIM] * (1.0 / both[:, HEAD_DIM:])).astype(jnp.bfloat16)
         for r in range(per_group):
-            first = (head * per_group + r) * HEAD_DIM
-            out_ref[local * block : (local + 1) * block, first : first + HEAD_DIM] = context[
+            out_ref[local * block : (local + 1) * block, r * HEAD_DIM : (r + 1) * HEAD_DIM] = context[
                 r * block : (r + 1) * block
             ]
 
     waiting = None
     for local in range(BLOCKS_PER_STEP):
-        every, mask = gather(local)
-        for head in range(kv_heads):
-            start = (kv_heads + head) * HEAD_DIM
-            scores = score(local, head, every, mask)
-            if waiting is not None:
-                finish(*waiting)
-            waiting = (local, head, scores, every[:, start : start + HEAD_DIM])
+        scores, values = score(local)
+        if waiting is not None:
+            finish(*waiting)
+        waiting = (local, scores, values)
     finish(*waiting)
 
 
@@ -257,7 +281,11 @@
     wide = features // UNITS
     near = len(straight)
     held = pl.BlockSpec(memory_space=pltpu.HBM)
-    part = pl.BlockSpec((BLOCKS_PER_STEP * block, wide), lambda b, *_: (b, unit))
+    kv_heads = own.shape[1] // (2 * HEAD_DIM)
+    per_head = wide // kv_heads
+    part = pl.BlockSpec(
+        (BLOCKS_PER_STEP * block, per_head), lambda h, b, *_: (b, unit * kv_heads + h)
+    )
     operands = [slots, cuts, odd, queries, own, *straight, *crossed]
     in_specs = [part] + [held] * (1 + near + len(crossed))
     aliases = {}
@@ -269,12 +297,12 @@
         functools.partial(attention_kernel, block, near),
         grid_spec=pltpu.PrefetchScalarGridSpec(
             num_scalar_prefetch=3,
-            grid=(blocks // BLOCKS_PER_STEP,),
+            grid=(kv_heads, blocks // BLOCKS_PER_STEP),
             in_specs=in_specs,
             out_specs=part,
             scratch_shapes=[
-                pltpu.VMEM((depth + 1, *own.shape), own.dtype),
-                pltpu.SemaphoreType.DMA((depth + 1,)),
+                pltpu.VMEM((kv_heads, depth + 1, rows, 2 * HEAD_DIM), own.dtype),
+                pltpu.SemaphoreType.DMA((kv_heads, depth + 1)),
             ],
         ),
         out_shape=jax.ShapeDtypeStruct((rows, features), jnp.bfloat16),
@@ -321,9 +349,9 @@
         return crossed[unit][s]
 
     def step_along(s, unit, settled):
-        source = own[unit] if s == 1 else straight[unit][s - 1]
-        shift = 2 * chains
-        pairs = [(i, i + shift) for i in range(size - shift) if half[i] >= s - 1]
+        source = straight[unit][1] if s == 2 else own[unit]
+        shift = 2 * (1 if s == 2 else s) * chains
+        pairs = [(i, i + shift) for i in range(size - shift) if half[i] >= (s == 2)]
         straight[unit][s] = lax.ppermute(after(source, *settled), "node", pairs)
         return straight[unit][s]
 
@@ -337,9 +365,10 @@
     across = [(s, unit) for s in range(near - 1) for unit in (early, late)]
     across += [(near - 1, early), (near, early), (near - 1, late)]
     along = [(1, early), (1, late)]
-    along += [(s, early) for s in range(2, near + 1)] + [(s, late) for s in range(2, near + 1)]
+    along += [(s, early) for s in range(2, near + 1)] + [(2, late), None]
+    along += [(s, late) for s in range(3, near + 1)]
     y_chain, z_chain = [], []
-    for (s, unit), step in zip(across, [*along, None], strict=True):
+    for (s, unit), step in zip(across, along, strict=True):
         y_chain.append(step_across(s, unit, y_chain[-2:-1]))
         if step is not None:
             z_chain.append(step_along(*step, z_chain[-2:-1]))

time: 123 us -> 127 us (1.033)
  the two profiles are of different devices: /device:TPU:24 before, /device:TPU:0 now
where the time goes in v7:
time: 127 us; the launch traced here: 126 us
  starting transfers between devices  62.5 us (49%)
  Pallas kernels  44.5 us (35%)
  waiting for transfers between devices  17.5 us (14%)
    ppermute x6, starting transfers between devices, step_along(): straight[unit][s] = lax.ppermute(after(source, *settled), 'node', pairs)  34.8 us
    pallas_call x2, Pallas kernels, attention(): pl.pallas_call(functools.partial(attention_kernel, block, near), grid_spe...  21.4 us
    ppermute x1, starting transfers between devices, step_down(): lax.ppermute(after(crossed[unit][0], *settled), 'node', pairs)  15.9 us
    pallas_call x1, Pallas kernels, norm_project(): pl.pallas_call(norm_project_kernel, in_specs=[held, whole, held, held], o...  13.7 us
    ppermute x6, waiting for transfers between devices, step_along(): straight[unit][s] = lax.ppermute(after(source, *settled), 'node', pairs)  13.4 us
    ppermute x7, starting transfers between devices, step_across(): crossed[unit][s] = lax.ppermute(after(source, *settled), 'node', pairs)  11.8 us
    pallas_call x1, Pallas kernels, project(): pl.pallas_call(project_kernel, grid=(CHUNKS,), in_specs=[pl.BlockSpec((ro...  9.35 us
    ppermute x7, waiting for transfers between devices, step_across(): crossed[unit][s] = lax.ppermute(after(source, *settled), 'node', pairs)  4.05 us
  transfers between devices with their start and end apart: 14, of which 3 were waited for; matrix products, arithmetic and copies ran while one was open for 0% of the time, Pallas kernels for 16%

profile of v7, /device:TPU:0, one launch (start us, length us, event | category | flops | bytes accessed | tf_op | source)
XLA Modules:
  0.0 126.1 jit_solution(12489001396084432697)
XLA Ops:
  0.0 13.7 %norm_project.1 = (bf16[512,8192]{1,0:T(8,128)(2,1)}, bf16[512,512]{1,0:T(8,128)(2,1)}) custom-call(bf16[512,8192]{1,0:T(8,128)(2,1)} %x_hbm.1, f32[8,1,1024]{2,1,0:T(1,128)} %bitcast.2, bf16[8192,512]{1,0:T(8,128)(2,1)} %key_ref.1, bf16[8192,512]{1,0:T(8,128)(2,1)} %value_ref.1), custom_call_target="tpu_custom_call" | custom-call | flops 4294967296 | bytes 25165824 | tf_op jit(solution)/shard_map/norm_project/pallas_call | solution.py:124
  13.7 4.9 %collective-permute-start.7 = (bf16[512,512]{1,0:T(8,128)(2,1)}, bf16[512,512]{1,0:T(8,128)(2,1)S(1)}, u32[]{:S(2)}, u32[]{:S(2)}) collective-permute-start(bf16[512,512]{1,0:T(8,128)(2,1)} %get-tuple-element.26.refs_0_), channel_id=1, source_target_pairs={{0,2},{1,3},{4,6},{5,7},{8,10},{9,11},{12,14},{13,15},{16,18},{17,... | collective-permute-start | bytes 1572872 | tf_op jit(solution)/shard_map/ppermute | solution.py:348
  18.6 3.5 %collective-permute-start.1 = (bf16[512,512]{1,0:T(8,128)(2,1)}, bf16[512,512]{1,0:T(8,128)(2,1)S(1)}, u32[]{:S(2)}, u32[]{:S(2)}) collective-permute-start(bf16[512,512]{1,0:T(8,128)(2,1)} %get-tuple-element.26.refs_0_), channel_id=1, source_target_pairs={{0,4},{1,5},{2,6},{3,7},{4,8},{5,9},{6,10},{7,11},{8,12},{9,13},{1... | collective-permute-start | bytes 1572872 | tf_op jit(solution)/shard_map/ppermute | solution.py:355
  22.2 0.0 copy-start.2
  22.2 0.0 copy-start.10
  22.2 9.4 %project.1.refs_0_ = bf16[512,512]{1,0:T(8,128)(2,1)} custom-call(bf16[512,8192]{1,0:T(8,128)(2,1)} %get-tuple-element.17.normed_ref, bf16[8192,512]{1,0:T(8,128)(2,1)} %key_ref.1, bf16[8192,512]{1,0:T(8,128)(2,1)} %value_ref.1), custom_call_target="tpu_custom_call" | custom-call | flops 4294967296 | bytes 16777216 | tf_op jit(solution)/shard_map/project/pallas_call | solution.py:175
  31.5 3.5 %collective-permute-start = (bf16[512,512]{1,0:T(8,128)(2,1)}, bf16[512,512]{1,0:T(8,128)(2,1)S(1)}, u32[]{:S(2)}, u32[]{:S(2)}) collective-permute-start(bf16[512,512]{1,0:T(8,128)(2,1)} %project.1.refs_0_), channel_id=1, source_target_pairs={{0,4},{1,5},{2,6},{3,7},{4,8},{5,9},{6,10},{7,11},{8,12},{9,13},{1... | collective-permute-start | bytes 1572872 | tf_op jit(solution)/shard_map/ppermute | solution.py:355
  35.0 1.9 %collective-permute-start.5 = (bf16[512,512]{1,0:T(8,128)(2,1)}, bf16[512,512]{1,0:T(8,128)(2,1)S(1)}, u32[]{:S(2)}, u32[]{:S(2)}) collective-permute-start(bf16[512,512]{1,0:T(8,128)(2,1)} %project.1.refs_0_), channel_id=1, source_target_pairs={{0,2},{1,3},{2,0},{3,1},{4,6},{5,7},{8,10},{9,11},{12,14},{13,15},... | collective-permute-start | bytes 1572872 | tf_op jit(solution)/shard_map/ppermute | solution.py:348
  36.9 0.0 collective-permute-done.7.refs_4_
  37.0 0.0 copy-start.3
  37.0 0.0 collective-permute-done.1.refs_1_
  37.0 0.0 copy-start.4
  37.0 0.7 collective-permute-start.2
  37.7 0.7 collective-permute-start.8
  38.4 7.5 %collective-permute-done.refs_1_ = bf16[512,512]{1,0:T(8,128)(2,1)S(1)} collective-permute-done((bf16[512,512]{1,0:T(8,128)(2,1)}, bf16[512,512]{1,0:T(8,128)(2,1)S(1)}, u32[]{:S(2)}, u32[]{:S(2)}) %collective-permute-start) | collective-permute-done | bytes 524320 | tf_op jit(solution)/shard_map/ppermute | solution.py:355
  45.9 4.0 %collective-permute-done.5.refs_4_ = bf16[512,512]{1,0:T(8,128)(2,1)S(1)} collective-permute-done((bf16[512,512]{1,0:T(8,128)(2,1)}, bf16[512,512]{1,0:T(8,128)(2,1)S(1)}, u32[]{:S(2)}, u32[]{:S(2)}) %collective-permute-start.5) | collective-permute-done | bytes 524320 | tf_op jit(solution)/shard_map/ppermute | solution.py:348
  50.0 0.7 collective-permute-start.6
  50.6 0.0 copy-done.2
  50.7 4.5 %collective-permute-start.11 = (bf16[512,512]{1,0:T(8,128)(2,1)S(1)}, bf16[512,512]{1,0:T(8,128)(2,1)}, u32[]{:S(2)}, u32[]{:S(2)}) collective-permute-start(bf16[512,512]{1,0:T(8,128)(2,1)S(1)} %copy-done.2), channel_id=1, source_target_pairs={{0,12},{1,13},{2,14},{3,15},{16,28},{17,29},{18,30},{19,31}} | collective-permute-start | bytes 1572872 | tf_op jit(solution)/shard_map/ppermute | solution.py:355
  55.1 0.0 collective-permute-done.2.refs_2_
  55.2 0.0 collective-permute-done.8.refs_5_
  55.2 0.7 collective-permute-start.9
  55.9 1.5 %collective-permute-start.3 = (bf16[512,512]{1,0:T(8,128)(2,1)S(1)}, bf16[512,512]{1,0:T(8,128)(2,1)}, u32[]{:S(2)}, u32[]{:S(2)}) collective-permute-start(bf16[512,512]{1,0:T(8,128)(2,1)S(1)} %collective-permute-done.refs_1_), channel_id=1, source_target_pairs={{4,8},{5,9},{6,10},{7,11},{8,12},{9,13},{10,14},{11,15},{20,24},{2... | collective-permute-start | bytes 1572872 | tf_op jit(solution)/shard_map/ppermute | solution.py:355
  57.3 0.0 collective-permute-done.6.refs_5_
  57.3 5.9 %collective-permute-done.11.refs_3_ = bf16[512,512]{1,0:T(8,128)(2,1)} collective-permute-done((bf16[512,512]{1,0:T(8,128)(2,1)S(1)}, bf16[512,512]{1,0:T(8,128)(2,1)}, u32[]{:S(2)}, u32[]{:S(2)}) %collective-permute-start.11) | collective-permute-done | bytes 524320 | tf_op jit(solution)/shard_map/ppermute | solution.py:355
  63.2 1.5 %collective-permute-start.13 = (bf16[512,512]{1,0:T(8,128)(2,1)}, bf16[512,512]{1,0:T(8,128)(2,1)}, u32[]{:S(2)}, u32[]{:S(2)}) collective-permute-start(bf16[512,512]{1,0:T(8,128)(2,1)} %collective-permute-done.11.refs_3_), channel_id=1, source_target_pairs={{12,14},{13,15},{14,12},{15,13},{28,30},{29,31},{30,28},{31,29}} | collective-permute-start | bytes 1572872 | tf_op jit(solution)/shard_map/ppermute | solution.py:348
  64.7 15.9 %collective-permute-start.12 = (bf16[512,512]{1,0:T(8,128)(2,1)S(1)}, bf16[512,512]{1,0:T(8,128)(2,1)S(1)}, u32[]{:S(2)}, u32[]{:S(2)}) collective-permute-start(bf16[512,512]{1,0:T(8,128)(2,1)S(1)} %collective-permute-done.5.refs_4_), channel_id=1, source_target_pairs={{0,12},{1,13},{2,14},{3,15},{16,28},{17,29},{18,30},{19,31}} | collective-permute-start | bytes 1572872 | tf_op jit(solution)/shard_map/ppermute | solution.py:361
  80.6 0.0 collective-permute-done.9.refs_6_
  80.6 0.0 copy-start.8
  80.7 0.0 collective-permute-done.3.refs_2_
  80.7 0.0 copy-done.6
  80.7 21.2 %collective-permute-start.4 = (bf16[512,512]{1,0:T(8,128)(2,1)}, bf16[512,512]{1,0:T(8,128)(2,1)}, u32[]{:S(2)}, u32[]{:S(2)}) collective-permute-start(bf16[512,512]{1,0:T(8,128)(2,1)} %project.1.refs_0_), channel_id=1, source_target_pairs={{0,12},{1,13},{2,14},{3,15},{16,28},{17,29},{18,30},{19,31}} | collective-permute-start | bytes 1572872 | tf_op jit(solution)/shard_map/ppermute | solution.py:355
  101.8 0.0 copy-done.7
  101.8 1.5 %collective-permute-start.10 = (bf16[512,512]{1,0:T(8,128)(2,1)}, bf16[512,512]{1,0:T(8,128)(2,1)}, u32[]{:S(2)}, u32[]{:S(2)}) collective-permute-start(bf16[512,512]{1,0:T(8,128)(2,1)} %collective-permute-done.3.refs_2_), channel_id=1, source_target_pairs={{8,10},{9,11},{10,8},{11,9},{12,14},{13,15},{14,12},{15,13},{24,26... | collective-permute-start | bytes 1572872 | tf_op jit(solution)/shard_map/ppermute | solution.py:348
  103.3 0.0 copy-done.8
  103.3 0.0 copy-done.10
  103.3 0.6 fusion.1.slot_ref
  103.9 0.0 collective-permute-done.13.refs_7_
  103.9 0.0 copy-done.4
  103.9 10.7 %attention.2.refs_8_ = bf16[512,4096]{1,0:T(8,128)(2,1)} custom-call(s32[8,7]{1,0:T(8,128)} %fusion.1.slot_ref, s32[8,7]{1,0:T(8,128)} %cut_ref.3, s32[1]{0:T(128)} %bitcast.odd_ref, bf16[512,4096]{1,0:T(8,128)(2,1)} %q_ref.3, bf16[512,512]{1,0:T(8,128)(2,1)} %get-tuple-element.26.refs_0_, bf16[512,512]{1,0:T(8,128)(2,1)} %copy-done.4, ...), custom_call_target="tpu_custom_call" | custom-call | flops 2147483648 | bytes 8388608 | tf_op jit(solution)/shard_map/attention/pallas_call | solution.py:296
  114.6 0.0 collective-permute-done.12.refs_7_
  114.6 0.0 collective-permute-done.4.refs_3_
  114.6 0.0 collective-permute-done.10.refs_6_
  114.6 0.0 copy-done
  114.7 0.0 copy-done.1
  114.7 0.0 copy-done.5
  114.7 0.7 copy-done.9
  115.4 10.7 %attention.3 = bf16[512,4096]{1,0:T(8,128)(2,1)} custom-call(s32[8,7]{1,0:T(8,128)} %fusion.1.slot_ref, s32[8,7]{1,0:T(8,128)} %cut_ref.3, s32[1]{0:T(128)} %bitcast.odd_ref, bf16[512,4096]{1,0:T(8,128)(2,1)} %q_ref.3, bf16[512,512]{1,0:T(8,128)(2,1)} %project.1.refs_0_, bf16[512,512]{1,0:T(8,128)(2,1)} %copy-done, ...), custom_call_target="tpu_custom_call", output_to_operand_aliasing={{}: (12, {})} | custom-call | flops 2147483648 | bytes 8388608 | tf_op jit(solution)/shard_map/attention/pallas_call | solution.py:296
  (7 shorter events, 0.0 us)
Async XLA Ops:
  13.7 23.2 %collective-permute-start.7 = (bf16[512,512]{1,0:T(8,128)(2,1)}, bf16[512,512]{1,0:T(8,128)(2,1)S(1)}, u32[]{:S(2)}, u32[]{:S(2)}) collective-permute-start(bf16[512,512]{1,0:T(8,128)(2,1)} %get-tuple-element.26.refs_0_), channel_id=1, source_target_pairs={{0,2},{1,3},{4,6},{5,7},{8,10},{9,11},{12,14},{13,15},{16,18},{17,... | collective-permute-start | bytes 1572872 | tf_op jit(solution)/shard_map/ppermute | solution.py:348
  18.6 18.3 %collective-permute-start.1 = (bf16[512,512]{1,0:T(8,128)(2,1)}, bf16[512,512]{1,0:T(8,128)(2,1)S(1)}, u32[]{:S(2)}, u32[]{:S(2)}) collective-permute-start(bf16[512,512]{1,0:T(8,128)(2,1)} %get-tuple-element.26.refs_0_), channel_id=1, source_target_pairs={{0,4},{1,5},{2,6},{3,7},{4,8},{5,9},{6,10},{7,11},{8,12},{9,13},{1... | collective-permute-start | bytes 1572872 | tf_op jit(solution)/shard_map/ppermute | solution.py:355
  22.2 28.5 %copy-start.2 = (bf16[512,512]{1,0:T(8,128)(2,1)S(1)}, bf16[512,512]{1,0:T(8,128)(2,1)}, u32[]{:S(2)}) copy-start(bf16[512,512]{1,0:T(8,128)(2,1)} %get-tuple-element.26.refs_0_) | copy-start | bytes 1572868
  22.2 81.1 %copy-start.10 = (s32[8,7]{1,0:T(8,128)S(1)}, s32[8,7]{1,0:T(8,128)}, u32[]{:S(2)}) copy-start(s32[8,7]{1,0:T(8,128)} %param.12) | copy-start | bytes 676
  31.5 14.4 %collective-permute-start = (bf16[512,512]{1,0:T(8,128)(2,1)}, bf16[512,512]{1,0:T(8,128)(2,1)S(1)}, u32[]{:S(2)}, u32[]{:S(2)}) collective-permute-start(bf16[512,512]{1,0:T(8,128)(2,1)} %project.1.refs_0_), channel_id=1, source_target_pairs={{0,4},{1,5},{2,6},{3,7},{4,8},{5,9},{6,10},{7,11},{8,12},{9,13},{1... | collective-permute-start | bytes 1572872 | tf_op jit(solution)/shard_map/ppermute | solution.py:355
  35.0 14.9 %collective-permute-start.5 = (bf16[512,512]{1,0:T(8,128)(2,1)}, bf16[512,512]{1,0:T(8,128)(2,1)S(1)}, u32[]{:S(2)}, u32[]{:S(2)}) collective-permute-start(bf16[512,512]{1,0:T(8,128)(2,1)} %project.1.refs_0_), channel_id=1, source_target_pairs={{0,2},{1,3},{2,0},{3,1},{4,6},{5,7},{8,10},{9,11},{12,14},{13,15},... | collective-permute-start | bytes 1572872 | tf_op jit(solution)/shard_map/ppermute | solution.py:348
  37.0 66.9 %copy-start.3 = (bf16[512,512]{1,0:T(8,128)(2,1)}, bf16[512,512]{1,0:T(8,128)(2,1)S(1)}, u32[]{:S(2)}) copy-start(bf16[512,512]{1,0:T(8,128)(2,1)S(1)} %collective-permute-done.7.refs_4_) | copy-start | bytes 1572868
  37.0 66.9 %copy-start.4 = (bf16[512,512]{1,0:T(8,128)(2,1)}, bf16[512,512]{1,0:T(8,128)(2,1)S(1)}, u32[]{:S(2)}) copy-start(bf16[512,512]{1,0:T(8,128)(2,1)S(1)} %collective-permute-done.1.refs_1_) | copy-start | bytes 1572868
  37.0 18.2 %collective-permute-start.2 = (bf16[512,512]{1,0:T(8,128)(2,1)S(1)}, bf16[512,512]{1,0:T(8,128)(2,1)S(1)}, u32[]{:S(2)}, u32[]{:S(2)}) collective-permute-start(bf16[512,512]{1,0:T(8,128)(2,1)S(1)} %collective-permute-done.1.refs_1_), channel_id=1, source_target_pairs={{4,8},{5,9},{6,10},{7,11},{8,12},{9,13},{10,14},{11,15},{20,24},{2... | collective-permute-start | bytes 1572872 | tf_op jit(solution)/shard_map/ppermute | solution.py:355
  37.7 17.5 %collective-permute-start.8 = (bf16[512,512]{1,0:T(8,128)(2,1)S(1)}, bf16[512,512]{1,0:T(8,128)(2,1)S(1)}, u32[]{:S(2)}, u32[]{:S(2)}) collective-permute-start(bf16[512,512]{1,0:T(8,128)(2,1)S(1)} %collective-permute-done.1.refs_1_), channel_id=1, source_target_pairs={{4,6},{5,7},{6,4},{7,5},{8,10},{9,11},{10,8},{11,9},{12,14},{13,15... | collective-permute-start | bytes 1572872 | tf_op jit(solution)/shard_map/ppermute | solution.py:348
  45.9 68.7 %copy-start = (bf16[512,512]{1,0:T(8,128)(2,1)}, bf16[512,512]{1,0:T(8,128)(2,1)S(1)}, u32[]{:S(2)}) copy-start(bf16[512,512]{1,0:T(8,128)(2,1)S(1)} %collective-permute-done.refs_1_) | copy-start | bytes 1572868
  50.0 64.7 %copy-start.1 = (bf16[512,512]{1,0:T(8,128)(2,1)}, bf16[512,512]{1,0:T(8,128)(2,1)S(1)}, u32[]{:S(2)}) copy-start(bf16[512,512]{1,0:T(8,128)(2,1)S(1)} %collective-permute-done.5.refs_4_) | copy-start | bytes 1572868
  50.0 7.4 %collective-permute-start.6 = (bf16[512,512]{1,0:T(8,128)(2,1)S(1)}, bf16[512,512]{1,0:T(8,128)(2,1)S(1)}, u32[]{:S(2)}, u32[]{:S(2)}) collective-permute-start(bf16[512,512]{1,0:T(8,128)(2,1)S(1)} %collective-permute-done.refs_1_), channel_id=1, source_target_pairs={{4,6},{5,7},{6,4},{7,5},{8,10},{9,11},{10,8},{11,9},{12,14},{13,15... | collective-permute-start | bytes 1572872 | tf_op jit(solution)/shard_map/ppermute | solution.py:348
  50.7 12.6 %collective-permute-start.11 = (bf16[512,512]{1,0:T(8,128)(2,1)S(1)}, bf16[512,512]{1,0:T(8,128)(2,1)}, u32[]{:S(2)}, u32[]{:S(2)}) collective-permute-start(bf16[512,512]{1,0:T(8,128)(2,1)S(1)} %copy-done.2), channel_id=1, source_target_pairs={{0,12},{1,13},{2,14},{3,15},{16,28},{17,29},{18,30},{19,31}} | collective-permute-start | bytes 1572872 | tf_op jit(solution)/shard_map/ppermute | solution.py:355
  55.2 25.5 %copy-start.6 = (bf16[512,512]{1,0:T(8,128)(2,1)}, bf16[512,512]{1,0:T(8,128)(2,1)S(1)}, u32[]{:S(2)}) copy-start(bf16[512,512]{1,0:T(8,128)(2,1)S(1)} %collective-permute-done.2.refs_2_) | copy-start | bytes 1572868
  55.2 46.7 %copy-start.7 = (bf16[512,512]{1,0:T(8,128)(2,1)}, bf16[512,512]{1,0:T(8,128)(2,1)S(1)}, u32[]{:S(2)}) copy-start(bf16[512,512]{1,0:T(8,128)(2,1)S(1)} %collective-permute-done.8.refs_5_) | copy-start | bytes 1572868
  55.2 25.5 %collective-permute-start.9 = (bf16[512,512]{1,0:T(8,128)(2,1)S(1)}, bf16[512,512]{1,0:T(8,128)(2,1)S(1)}, u32[]{:S(2)}, u32[]{:S(2)}) collective-permute-start(bf16[512,512]{1,0:T(8,128)(2,1)S(1)} %collective-permute-done.2.refs_2_), channel_id=1, source_target_pairs={{8,10},{9,11},{10,8},{11,9},{12,14},{13,15},{14,12},{15,13},{24,26... | collective-permute-start | bytes 1572872 | tf_op jit(solution)/shard_map/ppermute | solution.py:348
  55.9 24.8 %collective-permute-start.3 = (bf16[512,512]{1,0:T(8,128)(2,1)S(1)}, bf16[512,512]{1,0:T(8,128)(2,1)}, u32[]{:S(2)}, u32[]{:S(2)}) collective-permute-start(bf16[512,512]{1,0:T(8,128)(2,1)S(1)} %collective-permute-done.refs_1_), channel_id=1, source_target_pairs={{4,8},{5,9},{6,10},{7,11},{8,12},{9,13},{10,14},{11,15},{20,24},{2... | collective-permute-start | bytes 1572872 | tf_op jit(solution)/shard_map/ppermute | solution.py:355
  57.3 57.3 %copy-start.5 = (bf16[512,512]{1,0:T(8,128)(2,1)}, bf16[512,512]{1,0:T(8,128)(2,1)S(1)}, u32[]{:S(2)}) copy-start(bf16[512,512]{1,0:T(8,128)(2,1)S(1)} %collective-permute-done.6.refs_5_) | copy-start | bytes 1572868
  63.2 40.6 %collective-permute-start.13 = (bf16[512,512]{1,0:T(8,128)(2,1)}, bf16[512,512]{1,0:T(8,128)(2,1)}, u32[]{:S(2)}, u32[]{:S(2)}) collective-permute-start(bf16[512,512]{1,0:T(8,128)(2,1)} %collective-permute-done.11.refs_3_), channel_id=1, source_target_pairs={{12,14},{13,15},{14,12},{15,13},{28,30},{29,31},{30,28},{31,29}} | collective-permute-start | bytes 1572872 | tf_op jit(solution)/shard_map/ppermute | solution.py:348
  64.7 49.9 %collective-permute-start.12 = (bf16[512,512]{1,0:T(8,128)(2,1)S(1)}, bf16[512,512]{1,0:T(8,128)(2,1)S(1)}, u32[]{:S(2)}, u32[]{:S(2)}) collective-permute-start(bf16[512,512]{1,0:T(8,128)(2,1)S(1)} %collective-permute-done.5.refs_4_), channel_id=1, source_target_pairs={{0,12},{1,13},{2,14},{3,15},{16,28},{17,29},{18,30},{19,31}} | collective-permute-start | bytes 1572872 | tf_op jit(solution)/shard_map/ppermute | solution.py:361
  80.6 22.6 %copy-start.8 = (bf16[512,512]{1,0:T(8,128)(2,1)}, bf16[512,512]{1,0:T(8,128)(2,1)S(1)}, u32[]{:S(2)}) copy-start(bf16[512,512]{1,0:T(8,128)(2,1)S(1)} %collective-permute-done.9.refs_6_) | copy-start | bytes 1572868
  80.7 34.0 %collective-permute-start.4 = (bf16[512,512]{1,0:T(8,128)(2,1)}, bf16[512,512]{1,0:T(8,128)(2,1)}, u32[]{:S(2)}, u32[]{:S(2)}) collective-permute-start(bf16[512,512]{1,0:T(8,128)(2,1)} %project.1.refs_0_), channel_id=1, source_target_pairs={{0,12},{1,13},{2,14},{3,15},{16,28},{17,29},{18,30},{19,31}} | collective-permute-start | bytes 1572872 | tf_op jit(solution)/shard_map/ppermute | solution.py:355
  101.8 12.8 %collective-permute-start.10 = (bf16[512,512]{1,0:T(8,128)(2,1)}, bf16[512,512]{1,0:T(8,128)(2,1)}, u32[]{:S(2)}, u32[]{:S(2)}) collective-permute-start(bf16[512,512]{1,0:T(8,128)(2,1)} %collective-permute-done.3.refs_2_), channel_id=1, source_target_pairs={{8,10},{9,11},{10,8},{11,9},{12,14},{13,15},{14,12},{15,13},{24,26... | collective-permute-start | bytes 1572872 | tf_op jit(solution)/shard_map/ppermute | solution.py:348
  114.6 0.8 copy-start.9

commit v8 on v7

--- a/solution.py
+++ b/solution.py
@@ -19,10 +19,10 @@
 
 def norm_project_kernel(
     x_hbm, gain_ref, key_hbm, value_hbm, normed_hbm, kv_ref,
-    x_scr, weight_scr, even_scr, odd_scr, acc_scr, scale_scr, x_sem, key_sem, value_sem, normed_sem,
+    x_scr, key_scr, value_scr, even_scr, odd_scr, acc_scr, scale_scr, x_sem, key_sem, value_sem, normed_sem,
 ):
     loads, rows, chunk = x_scr.shape
-    width = weight_scr.shape[2] // 2
+    width = key_scr.shape[2] // UNITS
     lanes = 128
     band = 128
 
@@ -33,14 +33,9 @@
         return pltpu.make_async_copy(x_hbm.at[:, span(c)], x_scr.at[c], x_sem.at[c])
 
     def load_weights(c):
-        head = pl.ds(0, width)
         return [
-            pltpu.make_async_copy(
-                key_hbm.at[span(c), head], weight_scr.at[c, :, pl.ds(0, width)], key_sem.at[c]
-            ),
-            pltpu.make_async_copy(
-                value_hbm.at[span(c), head], weight_scr.at[c, :, pl.ds(width, width)], value_sem.at[c]
-            ),
+            pltpu.make_async_copy(hbm.at[span(c)], scr.at[c], sem.at[c])
+            for hbm, scr, sem in ((key_hbm, key_scr, key_sem), (value_hbm, value_scr, value_sem))
         ]
 
     def store_normed(normed_scr, c):
@@ -88,9 +83,11 @@
         for copy in load_weights(c):
             copy.wait()
         store_normed(normed_scr, c).start()
-        acc_scr[...] += jnp.dot(
-            normed_scr[c // 2], weight_scr[c], preferred_element_type=jnp.float32
-        )
+        normed = normed_scr[c // 2]
+        for part, weight in enumerate((key_scr, value_scr)):
+            acc_scr[:, part * width : (part + 1) * width] += jnp.dot(
+                normed, weight[c, :, :width], preferred_element_type=jnp.float32
+            )
 
     normalise(even_scr, 0)
     acc_scr[...] = jnp.zeros_like(acc_scr)
@@ -131,7 +128,8 @@
         ],
         scratch_shapes=[
             pltpu.VMEM((LOADS, rows, chunk), jnp.bfloat16),
-            pltpu.VMEM((LOADS, chunk, 2 * width), jnp.bfloat16),
+            pltpu.VMEM((LOADS, chunk, key_weight.shape[1]), jnp.bfloat16),
+            pltpu.VMEM((LOADS, chunk, key_weight.shape[1]), jnp.bfloat16),
             pltpu.VMEM((LOADS // 2, rows, chunk), jnp.bfloat16),
             pltpu.VMEM((LOADS // 2, rows, chunk), jnp.bfloat16),
             pltpu.VMEM((rows, 2 * width), jnp.float32),
@@ -149,13 +147,14 @@
     )(hidden, gain.reshape(LOADS, 1, chunk), key_weight, value_weight)
 
 
-def project_kernel(normed_ref, key_ref, value_ref, kv_ref, acc_scr):
+def project_kernel(unit, normed_ref, key_ref, value_ref, kv_ref, acc_scr):
     step = pl.program_id(0)
-    width = key_ref.shape[1]
+    width = key_ref.shape[1] // UNITS
+    mine = slice(unit * width, (unit + 1) * width)
     normed = normed_ref[...]
     for part, weight in enumerate((key_ref, value_ref)):
         cols = slice(part * width, (part + 1) * width)
-        term = jnp.dot(normed, weight[...], preferred_element_type=jnp.float32)
+        term = jnp.dot(normed, weight[:, mine], preferred_element_type=jnp.float32)
         acc_scr[:, cols] = jnp.where(step == 0, term, acc_scr[:, cols] + term)
 
     @pl.when(step == CHUNKS - 1)
@@ -171,9 +170,9 @@
     rows, features = normed.shape
     chunk = features // CHUNKS
     width = key_weight.shape[1] // UNITS
-    weight = pl.BlockSpec((chunk, width), lambda i: (i, unit))
+    weight = pl.BlockSpec((chunk, key_weight.shape[1]), lambda i: (i, 0))
     return pl.pallas_call(
-        project_kernel,
+        functools.partial(project_kernel, unit),
         grid=(CHUNKS,),
         in_specs=[pl.BlockSpec((rows, chunk), lambda i: (0, i)), weight, weight],
         out_specs=pl.BlockSpec((rows, 2 * width), lambda i: (0, 0)),
@@ -349,9 +348,9 @@
         return crossed[unit][s]
 
     def step_along(s, unit, settled):
-        source = straight[unit][1] if s == 2 else own[unit]
-        shift = 2 * (1 if s == 2 else s) * chains
-        pairs = [(i, i + shift) for i in range(size - shift) if half[i] >= (s == 2)]
+        source = own[unit] if s == 1 else straight[unit][s - 1]
+        shift = 2 * chains
+        pairs = [(i, i + shift) for i in range(size - shift) if half[i] >= s - 1]
         straight[unit][s] = lax.ppermute(after(source, *settled), "node", pairs)
         return straight[unit][s]
 
@@ -365,15 +364,15 @@
     across = [(s, unit) for s in range(near - 1) for unit in (early, late)]
     across += [(near - 1, early), (near, early), (near - 1, late)]
     along = [(1, early), (1, late)]
-    along += [(s, early) for s in range(2, near + 1)] + [(2, late), None]
-    along += [(s, late) for s in range(3, near + 1)]
+    along += [(s, early) for s in range(2, near + 1)] + [(s, late) for s in range(2, near)]
     y_chain, z_chain = [], []
-    for (s, unit), step in zip(across, along, strict=True):
-        y_chain.append(step_across(s, unit, y_chain[-2:-1]))
-        if step is not None:
-            z_chain.append(step_along(*step, z_chain[-2:-1]))
-        else:
-            z_chain.append(step_down(late, z_chain[-2:-1]))
+    for index, (s, unit) in enumerate(across):
+        second = [own[late]] if index == 2 else []
+        y_chain.append(step_across(s, unit, y_chain[-2:-1] + second))
+        if index < len(along):
+            z_chain.append(step_along(*along[index], z_chain[-2:-1] + second))
+    down = step_down(late, [z_chain[-2], y_chain[-3]])
+    step_along(near, late, [down])
     result = None
     for unit in range(UNITS):
         result = attention(

time: 127 us -> 124 us (0.976)
  the two profiles are of different devices: /device:TPU:0 before, /device:TPU:22 now
where the time goes in v8:
time: 124 us; the launch traced here: 123 us
  Pallas kernels  46.6 us (38%)
  waiting for transfers between devices  38.6 us (31%)
  starting transfers between devices  37.3 us (30%)
    pallas_call x2, Pallas kernels, attention(): pl.pallas_call(functools.partial(attention_kernel, block, near), grid_spe...  21.4 us
    ppermute x7, waiting for transfers between devices, step_across(): crossed[unit][s] = lax.ppermute(after(source, *settled), 'node', pairs)  20.6 us
    ppermute x6, starting transfers between devices, step_along(): straight[unit][s] = lax.ppermute(after(source, *settled), 'node', pairs)  20.4 us
    ppermute x6, waiting for transfers between devices, step_along(): straight[unit][s] = lax.ppermute(after(source, *settled), 'node', pairs)  18 us
    ppermute x7, starting transfers between devices, step_across(): crossed[unit][s] = lax.ppermute(after(source, *settled), 'node', pairs)  16.2 us
    pallas_call x1, Pallas kernels, norm_project(): pl.pallas_call(norm_project_kernel, in_specs=[held, whole, held, held], o...  14 us
    pallas_call x1, Pallas kernels, project(): pl.pallas_call(functools.partial(project_kernel, unit), grid=(CHUNKS,), i...  11.2 us
  transfers between devices with their start and end apart: 14, of which 8 were waited for; matrix products, arithmetic and copies ran while one was open for 0% of the time, Pallas kernels for 18%

profile of v8, /device:TPU:22, one launch (start us, length us, event | category | flops | bytes accessed | tf_op | source)
XLA Modules:
  0.0 123.4 jit_solution(17289669392404710259)
XLA Ops:
  0.0 14.0 %norm_project.1 = (bf16[512,8192]{1,0:T(8,128)(2,1)}, bf16[512,512]{1,0:T(8,128)(2,1)}) custom-call(bf16[512,8192]{1,0:T(8,128)(2,1)} %x_hbm.1, f32[8,1,1024]{2,1,0:T(1,128)} %bitcast.2, bf16[8192,512]{1,0:T(8,128)(2,1)} %key_ref.1, bf16[8192,512]{1,0:T(8,128)(2,1)} %value_ref.1), custom_call_target="tpu_custom_call" | custom-call | flops 4294967296 | bytes 25165824 | tf_op jit(solution)/shard_map/norm_project/pallas_call | solution.py:121
  14.0 1.3 %collective-permute-start.6 = (bf16[512,512]{1,0:T(8,128)(2,1)}, bf16[512,512]{1,0:T(8,128)(2,1)S(1)}, u32[]{:S(2)}, u32[]{:S(2)}) collective-permute-start(bf16[512,512]{1,0:T(8,128)(2,1)} %get-tuple-element.18.refs_0_), channel_id=1, source_target_pairs={{0,2},{1,3},{4,6},{5,7},{8,10},{9,11},{12,14},{13,15},{16,18},{17,... | collective-permute-start | bytes 1572872 | tf_op jit(solution)/shard_map/ppermute | solution.py:347
  15.3 3.5 %collective-permute-start.1 = (bf16[512,512]{1,0:T(8,128)(2,1)}, bf16[512,512]{1,0:T(8,128)(2,1)S(1)}, u32[]{:S(2)}, u32[]{:S(2)}) collective-permute-start(bf16[512,512]{1,0:T(8,128)(2,1)} %get-tuple-element.18.refs_0_), channel_id=1, source_target_pairs={{0,4},{1,5},{2,6},{3,7},{4,8},{5,9},{6,10},{7,11},{8,12},{9,13},{1... | collective-permute-start | bytes 1572872 | tf_op jit(solution)/shard_map/ppermute | solution.py:354
  18.8 0.0 copy-start.9
  18.8 11.2 %project.1.refs_0_ = bf16[512,512]{1,0:T(8,128)(2,1)} custom-call(bf16[512,8192]{1,0:T(8,128)(2,1)} %get-tuple-element.17.normed_ref, bf16[8192,512]{1,0:T(8,128)(2,1)} %key_ref.1, bf16[8192,512]{1,0:T(8,128)(2,1)} %value_ref.1), custom_call_target="tpu_custom_call" | custom-call | flops 4294967296 | bytes 16777216 | tf_op jit(solution)/shard_map/project/pallas_call | solution.py:174
  30.0 0.0 collective-permute-done.6.refs_4_
  30.0 0.0 copy-start
  30.0 1.1 collective-permute-done.1.refs_1_
  31.1 3.5 %collective-permute-start.2 = (bf16[512,512]{1,0:T(8,128)(2,1)S(1)}, bf16[512,512]{1,0:T(8,128)(2,1)S(1)}, u32[]{:S(2)}, u32[]{:S(2)}) collective-permute-start(bf16[512,512]{1,0:T(8,128)(2,1)S(1)} %collective-permute-done.1.refs_1_), channel_id=1, source_target_pairs={{4,8},{5,9},{6,10},{7,11},{8,12},{9,13},{10,14},{11,15},{20,24},{2... | collective-permute-start | bytes 1572872 | tf_op jit(solution)/shard_map/ppermute | solution.py:354
  34.5 4.3 %collective-permute-start.7 = (bf16[512,512]{1,0:T(8,128)(2,1)S(1)}, bf16[512,512]{1,0:T(8,128)(2,1)S(1)}, u32[]{:S(2)}, u32[]{:S(2)}) collective-permute-start(bf16[512,512]{1,0:T(8,128)(2,1)S(1)} %collective-permute-done.1.refs_1_), channel_id=1, source_target_pairs={{4,6},{5,7},{6,4},{7,5},{8,10},{9,11},{10,8},{11,9},{12,14},{13,15... | collective-permute-start | bytes 1572872 | tf_op jit(solution)/shard_map/ppermute | solution.py:347
  38.9 1.9 %collective-permute-start = (bf16[512,512]{1,0:T(8,128)(2,1)}, bf16[512,512]{1,0:T(8,128)(2,1)S(1)}, u32[]{:S(2)}, u32[]{:S(2)}) collective-permute-start(bf16[512,512]{1,0:T(8,128)(2,1)} %project.1.refs_0_), channel_id=1, source_target_pairs={{0,4},{1,5},{2,6},{3,7},{4,8},{5,9},{6,10},{7,11},{8,12},{9,13},{1... | collective-permute-start | bytes 1572872 | tf_op jit(solution)/shard_map/ppermute | solution.py:354
  40.8 1.3 %collective-permute-start.4 = (bf16[512,512]{1,0:T(8,128)(2,1)}, bf16[512,512]{1,0:T(8,128)(2,1)S(1)}, u32[]{:S(2)}, u32[]{:S(2)}) collective-permute-start(bf16[512,512]{1,0:T(8,128)(2,1)} %project.1.refs_0_), channel_id=1, source_target_pairs={{0,2},{1,3},{2,0},{3,1},{4,6},{5,7},{8,10},{9,11},{12,14},{13,15},... | collective-permute-start | bytes 1572872 | tf_op jit(solution)/shard_map/ppermute | solution.py:347
  42.1 5.7 %collective-permute-done.2.refs_2_ = bf16[512,512]{1,0:T(8,128)(2,1)S(1)} collective-permute-done((bf16[512,512]{1,0:T(8,128)(2,1)S(1)}, bf16[512,512]{1,0:T(8,128)(2,1)S(1)}, u32[]{:S(2)}, u32[]{:S(2)}) %collective-permute-start.2) | collective-permute-done | bytes 524320 | tf_op jit(solution)/shard_map/ppermute | solution.py:354
  47.8 0.0 copy-start.4
  47.8 3.9 %collective-permute-done.7.refs_5_ = bf16[512,512]{1,0:T(8,128)(2,1)S(1)} collective-permute-done((bf16[512,512]{1,0:T(8,128)(2,1)S(1)}, bf16[512,512]{1,0:T(8,128)(2,1)S(1)}, u32[]{:S(2)}, u32[]{:S(2)}) %collective-permute-start.7) | collective-permute-done | bytes 524320 | tf_op jit(solution)/shard_map/ppermute | solution.py:347
  51.7 0.0 copy-start.5
  51.7 1.9 %collective-permute-start.8 = (bf16[512,512]{1,0:T(8,128)(2,1)S(1)}, bf16[512,512]{1,0:T(8,128)(2,1)S(1)}, u32[]{:S(2)}, u32[]{:S(2)}) collective-permute-start(bf16[512,512]{1,0:T(8,128)(2,1)S(1)} %collective-permute-done.2.refs_2_), channel_id=1, source_target_pairs={{8,10},{9,11},{10,8},{11,9},{12,14},{13,15},{14,12},{15,13},{24,26... | collective-permute-start | bytes 1572872 | tf_op jit(solution)/shard_map/ppermute | solution.py:347
  53.6 3.4 %collective-permute-done.refs_1_ = bf16[512,512]{1,0:T(8,128)(2,1)S(1)} collective-permute-done((bf16[512,512]{1,0:T(8,128)(2,1)}, bf16[512,512]{1,0:T(8,128)(2,1)S(1)}, u32[]{:S(2)}, u32[]{:S(2)}) %collective-permute-start) | collective-permute-done | bytes 524320 | tf_op jit(solution)/shard_map/ppermute | solution.py:354
  57.0 4.3 %collective-permute-start.5 = (bf16[512,512]{1,0:T(8,128)(2,1)S(1)}, bf16[512,512]{1,0:T(8,128)(2,1)}, u32[]{:S(2)}, u32[]{:S(2)}) collective-permute-start(bf16[512,512]{1,0:T(8,128)(2,1)S(1)} %collective-permute-done.2.refs_2_), channel_id=1, source_target_pairs={{8,12},{9,13},{10,14},{11,15},{24,28},{25,29},{26,30},{27,31}} | collective-permute-start | bytes 1572872 | tf_op jit(solution)/shard_map/ppermute | solution.py:354
  61.3 1.6 %collective-permute-done.4.refs_4_ = bf16[512,512]{1,0:T(8,128)(2,1)S(1)} collective-permute-done((bf16[512,512]{1,0:T(8,128)(2,1)}, bf16[512,512]{1,0:T(8,128)(2,1)S(1)}, u32[]{:S(2)}, u32[]{:S(2)}) %collective-permute-start.4) | collective-permute-done | bytes 524320 | tf_op jit(solution)/shard_map/ppermute | solution.py:347
  62.9 2.3 %collective-permute-start.11 = (bf16[512,512]{1,0:T(8,128)(2,1)S(1)}, bf16[512,512]{1,0:T(8,128)(2,1)S(1)}, u32[]{:S(2)}, u32[]{:S(2)}) collective-permute-start(bf16[512,512]{1,0:T(8,128)(2,1)S(1)} %collective-permute-done.refs_1_), channel_id=1, source_target_pairs={{4,6},{5,7},{6,4},{7,5},{8,10},{9,11},{10,8},{11,9},{12,14},{13,15... | collective-permute-start | bytes 1572872 | tf_op jit(solution)/shard_map/ppermute | solution.py:347
  65.3 1.9 %collective-permute-start.3 = (bf16[512,512]{1,0:T(8,128)(2,1)S(1)}, bf16[512,512]{1,0:T(8,128)(2,1)}, u32[]{:S(2)}, u32[]{:S(2)}) collective-permute-start(bf16[512,512]{1,0:T(8,128)(2,1)S(1)} %collective-permute-done.refs_1_), channel_id=1, source_target_pairs={{4,8},{5,9},{6,10},{7,11},{8,12},{9,13},{10,14},{11,15},{20,24},{2... | collective-permute-start | bytes 1572872 | tf_op jit(solution)/shard_map/ppermute | solution.py:354
  67.2 7.0 %collective-permute-done.8.refs_6_ = bf16[512,512]{1,0:T(8,128)(2,1)S(1)} collective-permute-done((bf16[512,512]{1,0:T(8,128)(2,1)S(1)}, bf16[512,512]{1,0:T(8,128)(2,1)S(1)}, u32[]{:S(2)}, u32[]{:S(2)}) %collective-permute-start.8) | collective-permute-done | bytes 524320 | tf_op jit(solution)/shard_map/ppermute | solution.py:347
  74.1 0.0 collective-permute-done.5.refs_3_
  74.2 0.7 collective-permute-start.9
  74.8 8.2 %collective-permute-done.11.refs_5_ = bf16[512,512]{1,0:T(8,128)(2,1)S(1)} collective-permute-done((bf16[512,512]{1,0:T(8,128)(2,1)S(1)}, bf16[512,512]{1,0:T(8,128)(2,1)S(1)}, u32[]{:S(2)}, u32[]{:S(2)}) %collective-permute-start.11) | collective-permute-done | bytes 524320 | tf_op jit(solution)/shard_map/ppermute | solution.py:347
  83.0 1.4 %collective-permute-start.13 = (bf16[512,512]{1,0:T(8,128)(2,1)}, bf16[512,512]{1,0:T(8,128)(2,1)}, u32[]{:S(2)}, u32[]{:S(2)}) collective-permute-start(bf16[512,512]{1,0:T(8,128)(2,1)} %collective-permute-done.5.refs_3_), channel_id=1, source_target_pairs={{12,14},{13,15},{14,12},{15,13},{28,30},{29,31},{30,28},{31,29}} | collective-permute-start | bytes 1572872 | tf_op jit(solution)/shard_map/ppermute | solution.py:347
  84.4 7.9 %collective-permute-done.3.refs_2_ = bf16[512,512]{1,0:T(8,128)(2,1)} collective-permute-done((bf16[512,512]{1,0:T(8,128)(2,1)S(1)}, bf16[512,512]{1,0:T(8,128)(2,1)}, u32[]{:S(2)}, u32[]{:S(2)}) %collective-permute-start.3) | collective-permute-done | bytes 524320 | tf_op jit(solution)/shard_map/ppermute | solution.py:354
  92.3 3.7 %collective-permute-start.12 = (bf16[512,512]{1,0:T(8,128)(2,1)}, bf16[512,512]{1,0:T(8,128)(2,1)}, u32[]{:S(2)}, u32[]{:S(2)}) collective-permute-start(bf16[512,512]{1,0:T(8,128)(2,1)} %collective-permute-done.3.refs_2_), channel_id=1, source_target_pairs={{8,10},{9,11},{10,8},{11,9},{12,14},{13,15},{14,12},{15,13},{24,26... | collective-permute-start | bytes 1572872 | tf_op jit(solution)/shard_map/ppermute | solution.py:347
  96.0 0.0 collective-permute-done.9.refs_7_
  96.0 0.0 copy-done.6
  96.0 0.0 copy-start.8
  96.0 5.3 %collective-permute-start.10 = (bf16[512,512]{1,0:T(8,128)(2,1)}, bf16[512,512]{1,0:T(8,128)(2,1)}, u32[]{:S(2)}, u32[]{:S(2)}) collective-permute-start(bf16[512,512]{1,0:T(8,128)(2,1)} %collective-permute-done.3.refs_2_), channel_id=1, source_target_pairs={{8,12},{9,13},{10,14},{11,15},{24,28},{25,29},{26,30},{27,31}} | collective-permute-start | bytes 1572872 | tf_op jit(solution)/shard_map/ppermute | solution.py:354
  101.3 0.0 copy-done.7
  101.3 0.0 copy-done.8
  101.3 0.0 copy-done.9
  101.3 0.6 fusion.1.slot_ref
  101.9 0.0 collective-permute-done.13.refs_7_
  101.9 0.0 copy-done
  101.9 0.0 copy-done.1
  101.9 0.0 copy-done.4
  101.9 0.0 copy-done.5
  101.9 10.7 %attention.2.refs_8_ = bf16[512,4096]{1,0:T(8,128)(2,1)} custom-call(s32[8,7]{1,0:T(8,128)} %fusion.1.slot_ref, s32[8,7]{1,0:T(8,128)} %cut_ref.3, s32[1]{0:T(128)} %bitcast.odd_ref, bf16[512,4096]{1,0:T(8,128)(2,1)} %q_ref.3, bf16[512,512]{1,0:T(8,128)(2,1)} %get-tuple-element.18.refs_0_, bf16[512,512]{1,0:T(8,128)(2,1)} %copy-done.1, ...), custom_call_target="tpu_custom_call" | custom-call | flops 2147483648 | bytes 8388608 | tf_op jit(solution)/shard_map/attention/pallas_call | solution.py:295
  112.6 0.0 collective-permute-done.12.refs_6_
  112.6 0.0 collective-permute-done.10.refs_3_
  112.7 0.0 copy-done.2
  112.7 0.0 copy-done.3
  112.7 10.7 %attention.3 = bf16[512,4096]{1,0:T(8,128)(2,1)} custom-call(s32[8,7]{1,0:T(8,128)} %fusion.1.slot_ref, s32[8,7]{1,0:T(8,128)} %cut_ref.3, s32[1]{0:T(128)} %bitcast.odd_ref, bf16[512,4096]{1,0:T(8,128)(2,1)} %q_ref.3, bf16[512,512]{1,0:T(8,128)(2,1)} %project.1.refs_0_, bf16[512,512]{1,0:T(8,128)(2,1)} %copy-done.2, ...), custom_call_target="tpu_custom_call", output_to_operand_aliasing={{}: (12, {})} | custom-call | flops 2147483648 | bytes 8388608 | tf_op jit(solution)/shard_map/attention/pallas_call | solution.py:295
  (5 shorter events, 0.0 us)
Async XLA Ops:
  14.0 16.0 %collective-permute-start.6 = (bf16[512,512]{1,0:T(8,128)(2,1)}, bf16[512,512]{1,0:T(8,128)(2,1)S(1)}, u32[]{:S(2)}, u32[]{:S(2)}) collective-permute-start(bf16[512,512]{1,0:T(8,128)(2,1)} %get-tuple-element.18.refs_0_), channel_id=1, source_target_pairs={{0,2},{1,3},{4,6},{5,7},{8,10},{9,11},{12,14},{13,15},{16,18},{17,... | collective-permute-start | bytes 1572872 | tf_op jit(solution)/shard_map/ppermute | solution.py:347
  15.3 15.8 %collective-permute-start.1 = (bf16[512,512]{1,0:T(8,128)(2,1)}, bf16[512,512]{1,0:T(8,128)(2,1)S(1)}, u32[]{:S(2)}, u32[]{:S(2)}) collective-permute-start(bf16[512,512]{1,0:T(8,128)(2,1)} %get-tuple-element.18.refs_0_), channel_id=1, source_target_pairs={{0,4},{1,5},{2,6},{3,7},{4,8},{5,9},{6,10},{7,11},{8,12},{9,13},{1... | collective-permute-start | bytes 1572872 | tf_op jit(solution)/shard_map/ppermute | solution.py:354
  18.8 82.5 %copy-start.9 = (s32[8,7]{1,0:T(8,128)S(1)}, s32[8,7]{1,0:T(8,128)}, u32[]{:S(2)}) copy-start(s32[8,7]{1,0:T(8,128)} %param.12) | copy-start | bytes 676
  30.0 71.9 %copy-start = (bf16[512,512]{1,0:T(8,128)(2,1)}, bf16[512,512]{1,0:T(8,128)(2,1)S(1)}, u32[]{:S(2)}) copy-start(bf16[512,512]{1,0:T(8,128)(2,1)S(1)} %collective-permute-done.6.refs_4_) | copy-start | bytes 1572868
  31.1 70.8 %copy-start.1 = (bf16[512,512]{1,0:T(8,128)(2,1)}, bf16[512,512]{1,0:T(8,128)(2,1)S(1)}, u32[]{:S(2)}) copy-start(bf16[512,512]{1,0:T(8,128)(2,1)S(1)} %collective-permute-done.1.refs_1_) | copy-start | bytes 1572868
  31.1 16.7 %collective-permute-start.2 = (bf16[512,512]{1,0:T(8,128)(2,1)S(1)}, bf16[512,512]{1,0:T(8,128)(2,1)S(1)}, u32[]{:S(2)}, u32[]{:S(2)}) collective-permute-start(bf16[512,512]{1,0:T(8,128)(2,1)S(1)} %collective-permute-done.1.refs_1_), channel_id=1, source_target_pairs={{4,8},{5,9},{6,10},{7,11},{8,12},{9,13},{10,14},{11,15},{20,24},{2... | collective-permute-start | bytes 1572872 | tf_op jit(solution)/shard_map/ppermute | solution.py:354
  34.5 17.1 %collective-permute-start.7 = (bf16[512,512]{1,0:T(8,128)(2,1)S(1)}, bf16[512,512]{1,0:T(8,128)(2,1)S(1)}, u32[]{:S(2)}, u32[]{:S(2)}) collective-permute-start(bf16[512,512]{1,0:T(8,128)(2,1)S(1)} %collective-permute-done.1.refs_1_), channel_id=1, source_target_pairs={{4,6},{5,7},{6,4},{7,5},{8,10},{9,11},{10,8},{11,9},{12,14},{13,15... | collective-permute-start | bytes 1572872 | tf_op jit(solution)/shard_map/ppermute | solution.py:347
  38.9 18.1 %collective-permute-start = (bf16[512,512]{1,0:T(8,128)(2,1)}, bf16[512,512]{1,0:T(8,128)(2,1)S(1)}, u32[]{:S(2)}, u32[]{:S(2)}) collective-permute-start(bf16[512,512]{1,0:T(8,128)(2,1)} %project.1.refs_0_), channel_id=1, source_target_pairs={{0,4},{1,5},{2,6},{3,7},{4,8},{5,9},{6,10},{7,11},{8,12},{9,13},{1... | collective-permute-start | bytes 1572872 | tf_op jit(solution)/shard_map/ppermute | solution.py:354
  40.8 22.1 %collective-permute-start.4 = (bf16[512,512]{1,0:T(8,128)(2,1)}, bf16[512,512]{1,0:T(8,128)(2,1)S(1)}, u32[]{:S(2)}, u32[]{:S(2)}) collective-permute-start(bf16[512,512]{1,0:T(8,128)(2,1)} %project.1.refs_0_), channel_id=1, source_target_pairs={{0,2},{1,3},{2,0},{3,1},{4,6},{5,7},{8,10},{9,11},{12,14},{13,15},... | collective-permute-start | bytes 1572872 | tf_op jit(solution)/shard_map/ppermute | solution.py:347
  47.8 54.1 %copy-start.4 = (bf16[512,512]{1,0:T(8,128)(2,1)}, bf16[512,512]{1,0:T(8,128)(2,1)S(1)}, u32[]{:S(2)}) copy-start(bf16[512,512]{1,0:T(8,128)(2,1)S(1)} %collective-permute-done.2.refs_2_) | copy-start | bytes 1572868
  51.7 50.2 %copy-start.5 = (bf16[512,512]{1,0:T(8,128)(2,1)}, bf16[512,512]{1,0:T(8,128)(2,1)S(1)}, u32[]{:S(2)}) copy-start(bf16[512,512]{1,0:T(8,128)(2,1)S(1)} %collective-permute-done.7.refs_5_) | copy-start | bytes 1572868
  51.7 22.5 %collective-permute-start.8 = (bf16[512,512]{1,0:T(8,128)(2,1)S(1)}, bf16[512,512]{1,0:T(8,128)(2,1)S(1)}, u32[]{:S(2)}, u32[]{:S(2)}) collective-permute-start(bf16[512,512]{1,0:T(8,128)(2,1)S(1)} %collective-permute-done.2.refs_2_), channel_id=1, source_target_pairs={{8,10},{9,11},{10,8},{11,9},{12,14},{13,15},{14,12},{15,13},{24,26... | collective-permute-start | bytes 1572872 | tf_op jit(solution)/shard_map/ppermute | solution.py:347
  57.0 55.7 %copy-start.2 = (bf16[512,512]{1,0:T(8,128)(2,1)}, bf16[512,512]{1,0:T(8,128)(2,1)S(1)}, u32[]{:S(2)}) copy-start(bf16[512,512]{1,0:T(8,128)(2,1)S(1)} %collective-permute-done.refs_1_) | copy-start | bytes 1572868
  57.0 17.2 %collective-permute-start.5 = (bf16[512,512]{1,0:T(8,128)(2,1)S(1)}, bf16[512,512]{1,0:T(8,128)(2,1)}, u32[]{:S(2)}, u32[]{:S(2)}) collective-permute-start(bf16[512,512]{1,0:T(8,128)(2,1)S(1)} %collective-permute-done.2.refs_2_), channel_id=1, source_target_pairs={{8,12},{9,13},{10,14},{11,15},{24,28},{25,29},{26,30},{27,31}} | collective-permute-start | bytes 1572872 | tf_op jit(solution)/shard_map/ppermute | solution.py:354
  62.9 49.8 %copy-start.3 = (bf16[512,512]{1,0:T(8,128)(2,1)}, bf16[512,512]{1,0:T(8,128)(2,1)S(1)}, u32[]{:S(2)}) copy-start(bf16[512,512]{1,0:T(8,128)(2,1)S(1)} %collective-permute-done.4.refs_4_) | copy-start | bytes 1572868
  62.9 20.1 %collective-permute-start.11 = (bf16[512,512]{1,0:T(8,128)(2,1)S(1)}, bf16[512,512]{1,0:T(8,128)(2,1)S(1)}, u32[]{:S(2)}, u32[]{:S(2)}) collective-permute-start(bf16[512,512]{1,0:T(8,128)(2,1)S(1)} %collective-permute-done.refs_1_), channel_id=1, source_target_pairs={{4,6},{5,7},{6,4},{7,5},{8,10},{9,11},{10,8},{11,9},{12,14},{13,15... | collective-permute-start | bytes 1572872 | tf_op jit(solution)/shard_map/ppermute | solution.py:347
  65.3 27.0 %collective-permute-start.3 = (bf16[512,512]{1,0:T(8,128)(2,1)S(1)}, bf16[512,512]{1,0:T(8,128)(2,1)}, u32[]{:S(2)}, u32[]{:S(2)}) collective-permute-start(bf16[512,512]{1,0:T(8,128)(2,1)S(1)} %collective-permute-done.refs_1_), channel_id=1, source_target_pairs={{4,8},{5,9},{6,10},{7,11},{8,12},{9,13},{10,14},{11,15},{20,24},{2... | collective-permute-start | bytes 1572872 | tf_op jit(solution)/shard_map/ppermute | solution.py:354
  74.1 21.8 %copy-start.6 = (bf16[512,512]{1,0:T(8,128)(2,1)}, bf16[512,512]{1,0:T(8,128)(2,1)S(1)}, u32[]{:S(2)}) copy-start(bf16[512,512]{1,0:T(8,128)(2,1)S(1)} %collective-permute-done.8.refs_6_) | copy-start | bytes 1572868
  74.2 21.8 %collective-permute-start.9 = (bf16[512,512]{1,0:T(8,128)(2,1)S(1)}, bf16[512,512]{1,0:T(8,128)(2,1)S(1)}, u32[]{:S(2)}, u32[]{:S(2)}) collective-permute-start(bf16[512,512]{1,0:T(8,128)(2,1)S(1)} %collective-permute-done.4.refs_4_), channel_id=1, source_target_pairs={{0,12},{1,13},{2,14},{3,15},{16,28},{17,29},{18,30},{19,31}} | collective-permute-start | bytes 1572872 | tf_op jit(solution)/shard_map/ppermute | solution.py:360
  83.0 18.3 %copy-start.7 = (bf16[512,512]{1,0:T(8,128)(2,1)}, bf16[512,512]{1,0:T(8,128)(2,1)S(1)}, u32[]{:S(2)}) copy-start(bf16[512,512]{1,0:T(8,128)(2,1)S(1)} %collective-permute-done.11.refs_5_) | copy-start | bytes 1572868
  83.0 18.9 %collective-permute-start.13 = (bf16[512,512]{1,0:T(8,128)(2,1)}, bf16[512,512]{1,0:T(8,128)(2,1)}, u32[]{:S(2)}, u32[]{:S(2)}) collective-permute-start(bf16[512,512]{1,0:T(8,128)(2,1)} %collective-permute-done.5.refs_3_), channel_id=1, source_target_pairs={{12,14},{13,15},{14,12},{15,13},{28,30},{29,31},{30,28},{31,29}} | collective-permute-start | bytes 1572872 | tf_op jit(solution)/shard_map/ppermute | solution.py:347
  92.3 20.3 %collective-permute-start.12 = (bf16[512,512]{1,0:T(8,128)(2,1)}, bf16[512,512]{1,0:T(8,128)(2,1)}, u32[]{:S(2)}, u32[]{:S(2)}) collective-permute-start(bf16[512,512]{1,0:T(8,128)(2,1)} %collective-permute-done.3.refs_2_), channel_id=1, source_target_pairs={{8,10},{9,11},{10,8},{11,9},{12,14},{13,15},{14,12},{15,13},{24,26... | collective-permute-start | bytes 1572872 | tf_op jit(solution)/shard_map/ppermute | solution.py:347
  96.0 5.3 %copy-start.8 = (bf16[512,512]{1,0:T(8,128)(2,1)}, bf16[512,512]{1,0:T(8,128)(2,1)S(1)}, u32[]{:S(2)}) copy-start(bf16[512,512]{1,0:T(8,128)(2,1)S(1)} %collective-permute-done.9.refs_7_) | copy-start | bytes 1572868
  96.0 16.7 %collective-permute-start.10 = (bf16[512,512]{1,0:T(8,128)(2,1)}, bf16[512,512]{1,0:T(8,128)(2,1)}, u32[]{:S(2)}, u32[]{:S(2)}) collective-permute-start(bf16[512,512]{1,0:T(8,128)(2,1)} %collective-permute-done.3.refs_2_), channel_id=1, source_target_pairs={{8,12},{9,13},{10,14},{11,15},{24,28},{25,29},{26,30},{27,31}} | collective-permute-start | bytes 1572872 | tf_op jit(solution)/shard_map/ppermute | solution.py:354

commit v9 on v7

--- a/solution.py
+++ b/solution.py
@@ -11,7 +11,7 @@
 LOG2E = 1.4426950408889634
 MASKED = -1e30
 MIB = 1024 * 1024
-CHUNKS = 4
+CHUNKS = 8
 LOADS = 8
 UNITS = 2
 BLOCKS_PER_STEP = 4
@@ -19,7 +19,7 @@
 
 def norm_project_kernel(
     x_hbm, gain_ref, key_hbm, value_hbm, normed_hbm, kv_ref,
-    x_scr, weight_scr, even_scr, odd_scr, acc_scr, scale_scr, x_sem, key_sem, value_sem, normed_sem,
+    x_scr, wide_scr, weight_scr, even_scr, odd_scr, acc_scr, scale_scr, x_sem, key_sem, value_sem, normed_sem,
 ):
     loads, rows, chunk = x_scr.shape
     width = weight_scr.shape[2] // 2
@@ -66,6 +66,7 @@
             total = scale_scr[row, :]
             for lane in range(0, chunk, lanes):
                 x = x_scr[c, row, lane : lane + lanes].astype(jnp.float32)
+                wide_scr[c, row, lane : lane + lanes] = x
                 total += x * x
             scale_scr[row, :] = total
         return carry
@@ -80,7 +81,7 @@
             inverse = scale_scr[row, :]
             for lane in range(0, chunk, lanes):
                 cols = slice(lane, lane + lanes)
-                x = x_scr[c, row, cols].astype(jnp.float32)
+                x = wide_scr[c, row, cols]
                 gain = gain_ref[c, :, cols]
                 normed_scr[c // 2, row, cols] = (x * inverse * gain).astype(jnp.bfloat16)
 
@@ -131,6 +132,7 @@
         ],
         scratch_shapes=[
             pltpu.VMEM((LOADS, rows, chunk), jnp.bfloat16),
+            pltpu.VMEM((LOADS, rows, chunk), jnp.float32),
             pltpu.VMEM((LOADS, chunk, 2 * width), jnp.bfloat16),
             pltpu.VMEM((LOADS // 2, rows, chunk), jnp.bfloat16),
             pltpu.VMEM((LOADS // 2, rows, chunk), jnp.bfloat16),
@@ -349,9 +351,9 @@
         return crossed[unit][s]
 
     def step_along(s, unit, settled):
-        source = straight[unit][1] if s == 2 else own[unit]
-        shift = 2 * (1 if s == 2 else s) * chains
-        pairs = [(i, i + shift) for i in range(size - shift) if half[i] >= (s == 2)]
+        source = own[unit] if s == 1 else straight[unit][s - 1]
+        shift = 2 * chains
+        pairs = [(i, i + shift) for i in range(size - shift) if half[i] >= s - 1]
         straight[unit][s] = lax.ppermute(after(source, *settled), "node", pairs)
         return straight[unit][s]
 
@@ -365,15 +367,14 @@
     across = [(s, unit) for s in range(near - 1) for unit in (early, late)]
     across += [(near - 1, early), (near, early), (near - 1, late)]
     along = [(1, early), (1, late)]
-    along += [(s, early) for s in range(2, near + 1)] + [(2, late), None]
-    along += [(s, late) for s in range(3, near + 1)]
+    along += [(s, early) for s in range(2, near + 1)] + [(s, late) for s in range(2, near)]
     y_chain, z_chain = [], []
-    for (s, unit), step in zip(across, along, strict=True):
+    for index, (s, unit) in enumerate(across):
         y_chain.append(step_across(s, unit, y_chain[-2:-1]))
-        if step is not None:
-            z_chain.append(step_along(*step, z_chain[-2:-1]))
-        else:
-            z_chain.append(step_down(late, z_chain[-2:-1]))
+        if index < len(along):
+            z_chain.append(step_along(*along[index], z_chain[-2:-1]))
+    step_down(late, [z_chain[-2], y_chain[-3]])
+    step_along(near, late, [z_chain[-1]])
     result = None
     for unit in range(UNITS):
         result = attention(

time: 127 us -> 121 us (0.953)
  the two profiles are of different devices: /device:TPU:0 before, /device:TPU:24 now
where the time goes in v9:
time: 121 us; the launch traced here: 120 us
  waiting for transfers between devices  49.2 us (41%)
  Pallas kernels  46.6 us (39%)
  starting transfers between devices  23.4 us (19%)
    ppermute x6, waiting for transfers between devices, step_along(): straight[unit][s] = lax.ppermute(after(source, *settled), 'node', pairs)  38 us
    pallas_call x2, Pallas kernels, attention(): pl.pallas_call(functools.partial(attention_kernel, block, near), grid_spe...  21.4 us
    ppermute x7, starting transfers between devices, step_across(): crossed[unit][s] = lax.ppermute(after(source, *settled), 'node', pairs)  14.3 us
    pallas_call x1, Pallas kernels, norm_project(): pl.pallas_call(norm_project_kernel, in_specs=[held, whole, held, held], o...  14.1 us
    ppermute x7, waiting for transfers between devices, step_across(): crossed[unit][s] = lax.ppermute(after(source, *settled), 'node', pairs)  11.2 us
    pallas_call x1, Pallas kernels, project(): pl.pallas_call(project_kernel, grid=(CHUNKS,), in_specs=[pl.BlockSpec((ro...  11.1 us
    ppermute x6, starting transfers between devices, step_along(): straight[unit][s] = lax.ppermute(after(source, *settled), 'node', pairs)  7.73 us
  transfers between devices with their start and end apart: 14, of which 8 were waited for; matrix products, arithmetic and copies ran while one was open for 1% of the time, Pallas kernels for 18%

profile of v9, /device:TPU:24, one launch (start us, length us, event | category | flops | bytes accessed | tf_op | source)
XLA Modules:
  0.0 120.1 jit_solution(14411064119468946174)
XLA Ops:
  0.0 14.1 %norm_project.1 = (bf16[512,8192]{1,0:T(8,128)(2,1)}, bf16[512,512]{1,0:T(8,128)(2,1)}) custom-call(bf16[512,8192]{1,0:T(8,128)(2,1)} %x_hbm.1, f32[8,1,1024]{2,1,0:T(1,128)} %bitcast.2, bf16[8192,512]{1,0:T(8,128)(2,1)} %key_ref.1, bf16[8192,512]{1,0:T(8,128)(2,1)} %value_ref.1), custom_call_target="tpu_custom_call" | custom-call | flops 4294967296 | bytes 25165824 | tf_op jit(solution)/shard_map/norm_project/pallas_call | solution.py:125
  14.1 1.3 %collective-permute-start.1 = (bf16[512,512]{1,0:T(8,128)(2,1)}, bf16[512,512]{1,0:T(8,128)(2,1)S(1)}, u32[]{:S(2)}, u32[]{:S(2)}) collective-permute-start(bf16[512,512]{1,0:T(8,128)(2,1)} %get-tuple-element.18.refs_0_), channel_id=1, source_target_pairs={{0,4},{1,5},{2,6},{3,7},{4,8},{5,9},{6,10},{7,11},{8,12},{9,13},{1... | collective-permute-start | bytes 1572872 | tf_op jit(solution)/shard_map/ppermute | solution.py:357
  15.4 3.5 %collective-permute-start.7 = (bf16[512,512]{1,0:T(8,128)(2,1)}, bf16[512,512]{1,0:T(8,128)(2,1)S(1)}, u32[]{:S(2)}, u32[]{:S(2)}) collective-permute-start(bf16[512,512]{1,0:T(8,128)(2,1)} %get-tuple-element.18.refs_0_), channel_id=1, source_target_pairs={{0,2},{1,3},{4,6},{5,7},{8,10},{9,11},{12,14},{13,15},{16,18},{17,... | collective-permute-start | bytes 1572872 | tf_op jit(solution)/shard_map/ppermute | solution.py:350
  18.9 0.0 copy-start.8
  18.9 11.1 %project.1.refs_0_ = bf16[512,512]{1,0:T(8,128)(2,1)} custom-call(bf16[512,8192]{1,0:T(8,128)(2,1)} %get-tuple-element.17.normed_ref, bf16[8192,512]{1,0:T(8,128)(2,1)} %key_ref.1, bf16[8192,512]{1,0:T(8,128)(2,1)} %value_ref.1), custom_call_target="tpu_custom_call" | custom-call | flops 4294967296 | bytes 16777216 | tf_op jit(solution)/shard_map/project/pallas_call | solution.py:177
  30.0 1.3 %collective-permute-start.5 = (bf16[512,512]{1,0:T(8,128)(2,1)}, bf16[512,512]{1,0:T(8,128)(2,1)S(1)}, u32[]{:S(2)}, u32[]{:S(2)}) collective-permute-start(bf16[512,512]{1,0:T(8,128)(2,1)} %project.1.refs_0_), channel_id=1, source_target_pairs={{0,2},{1,3},{2,0},{3,1},{4,6},{5,7},{8,10},{9,11},{12,14},{13,15},... | collective-permute-start | bytes 1572872 | tf_op jit(solution)/shard_map/ppermute | solution.py:350
  31.3 1.3 %collective-permute-start = (bf16[512,512]{1,0:T(8,128)(2,1)}, bf16[512,512]{1,0:T(8,128)(2,1)S(1)}, u32[]{:S(2)}, u32[]{:S(2)}) collective-permute-start(bf16[512,512]{1,0:T(8,128)(2,1)} %project.1.refs_0_), channel_id=1, source_target_pairs={{0,4},{1,5},{2,6},{3,7},{4,8},{5,9},{6,10},{7,11},{8,12},{9,13},{1... | collective-permute-start | bytes 1572872 | tf_op jit(solution)/shard_map/ppermute | solution.py:357
  32.6 0.0 collective-permute-done.1.refs_1_
  32.6 0.0 copy-start.2
  32.6 1.3 %collective-permute-start.2 = (bf16[512,512]{1,0:T(8,128)(2,1)S(1)}, bf16[512,512]{1,0:T(8,128)(2,1)S(1)}, u32[]{:S(2)}, u32[]{:S(2)}) collective-permute-start(bf16[512,512]{1,0:T(8,128)(2,1)S(1)} %collective-permute-done.1.refs_1_), channel_id=1, source_target_pairs={{4,8},{5,9},{6,10},{7,11},{8,12},{9,13},{10,14},{11,15},{20,24},{2... | collective-permute-start | bytes 1572872 | tf_op jit(solution)/shard_map/ppermute | solution.py:357
  33.9 0.0 collective-permute-done.7.refs_4_
  33.9 0.0 copy-start.3
  34.0 1.9 %collective-permute-start.8 = (bf16[512,512]{1,0:T(8,128)(2,1)S(1)}, bf16[512,512]{1,0:T(8,128)(2,1)S(1)}, u32[]{:S(2)}, u32[]{:S(2)}) collective-permute-start(bf16[512,512]{1,0:T(8,128)(2,1)S(1)} %collective-permute-done.1.refs_1_), channel_id=1, source_target_pairs={{4,6},{5,7},{6,4},{7,5},{8,10},{9,11},{10,8},{11,9},{12,14},{13,15... | collective-permute-start | bytes 1572872 | tf_op jit(solution)/shard_map/ppermute | solution.py:350
  35.9 8.0 %collective-permute-done.5.refs_4_ = bf16[512,512]{1,0:T(8,128)(2,1)S(1)} collective-permute-done((bf16[512,512]{1,0:T(8,128)(2,1)}, bf16[512,512]{1,0:T(8,128)(2,1)S(1)}, u32[]{:S(2)}, u32[]{:S(2)}) %collective-permute-start.5) | collective-permute-done | bytes 524320 | tf_op jit(solution)/shard_map/ppermute | solution.py:350
  43.9 0.0 copy-start
  43.9 5.0 %collective-permute-done.refs_1_ = bf16[512,512]{1,0:T(8,128)(2,1)S(1)} collective-permute-done((bf16[512,512]{1,0:T(8,128)(2,1)}, bf16[512,512]{1,0:T(8,128)(2,1)S(1)}, u32[]{:S(2)}, u32[]{:S(2)}) %collective-permute-start) | collective-permute-done | bytes 524320 | tf_op jit(solution)/shard_map/ppermute | solution.py:357
  48.9 1.9 %collective-permute-start.6 = (bf16[512,512]{1,0:T(8,128)(2,1)S(1)}, bf16[512,512]{1,0:T(8,128)(2,1)S(1)}, u32[]{:S(2)}, u32[]{:S(2)}) collective-permute-start(bf16[512,512]{1,0:T(8,128)(2,1)S(1)} %collective-permute-done.refs_1_), channel_id=1, source_target_pairs={{4,6},{5,7},{6,4},{7,5},{8,10},{9,11},{10,8},{11,9},{12,14},{13,15... | collective-permute-start | bytes 1572872 | tf_op jit(solution)/shard_map/ppermute | solution.py:350
  50.8 7.9 %collective-permute-done.2.refs_2_ = bf16[512,512]{1,0:T(8,128)(2,1)S(1)} collective-permute-done((bf16[512,512]{1,0:T(8,128)(2,1)S(1)}, bf16[512,512]{1,0:T(8,128)(2,1)S(1)}, u32[]{:S(2)}, u32[]{:S(2)}) %collective-permute-start.2) | collective-permute-done | bytes 524320 | tf_op jit(solution)/shard_map/ppermute | solution.py:357
  58.7 0.0 copy-start.5
  58.7 1.3 %collective-permute-start.11 = (bf16[512,512]{1,0:T(8,128)(2,1)S(1)}, bf16[512,512]{1,0:T(8,128)(2,1)}, u32[]{:S(2)}, u32[]{:S(2)}) collective-permute-start(bf16[512,512]{1,0:T(8,128)(2,1)S(1)} %collective-permute-done.2.refs_2_), channel_id=1, source_target_pairs={{8,12},{9,13},{10,14},{11,15},{24,28},{25,29},{26,30},{27,31}} | collective-permute-start | bytes 1572872 | tf_op jit(solution)/shard_map/ppermute | solution.py:357
  60.0 0.0 collective-permute-done.8.refs_5_
  60.0 0.0 copy-start.6
  60.0 1.9 %collective-permute-start.9 = (bf16[512,512]{1,0:T(8,128)(2,1)S(1)}, bf16[512,512]{1,0:T(8,128)(2,1)S(1)}, u32[]{:S(2)}, u32[]{:S(2)}) collective-permute-start(bf16[512,512]{1,0:T(8,128)(2,1)S(1)} %collective-permute-done.2.refs_2_), channel_id=1, source_target_pairs={{8,10},{9,11},{10,8},{11,9},{12,14},{13,15},{14,12},{15,13},{24,26... | collective-permute-start | bytes 1572872 | tf_op jit(solution)/shard_map/ppermute | solution.py:350
  61.9 1.3 %collective-permute-start.3 = (bf16[512,512]{1,0:T(8,128)(2,1)S(1)}, bf16[512,512]{1,0:T(8,128)(2,1)}, u32[]{:S(2)}, u32[]{:S(2)}) collective-permute-start(bf16[512,512]{1,0:T(8,128)(2,1)S(1)} %collective-permute-done.refs_1_), channel_id=1, source_target_pairs={{4,8},{5,9},{6,10},{7,11},{8,12},{9,13},{10,14},{11,15},{20,24},{2... | collective-permute-start | bytes 1572872 | tf_op jit(solution)/shard_map/ppermute | solution.py:357
  63.2 3.1 %collective-permute-done.6.refs_5_ = bf16[512,512]{1,0:T(8,128)(2,1)S(1)} collective-permute-done((bf16[512,512]{1,0:T(8,128)(2,1)S(1)}, bf16[512,512]{1,0:T(8,128)(2,1)S(1)}, u32[]{:S(2)}, u32[]{:S(2)}) %collective-permute-start.6) | collective-permute-done | bytes 524320 | tf_op jit(solution)/shard_map/ppermute | solution.py:350
  66.3 9.2 %collective-permute-done.11.refs_3_ = bf16[512,512]{1,0:T(8,128)(2,1)} collective-permute-done((bf16[512,512]{1,0:T(8,128)(2,1)S(1)}, bf16[512,512]{1,0:T(8,128)(2,1)}, u32[]{:S(2)}, u32[]{:S(2)}) %collective-permute-start.11) | collective-permute-done | bytes 524320 | tf_op jit(solution)/shard_map/ppermute | solution.py:357
  75.5 1.9 %collective-permute-start.13 = (bf16[512,512]{1,0:T(8,128)(2,1)}, bf16[512,512]{1,0:T(8,128)(2,1)}, u32[]{:S(2)}, u32[]{:S(2)}) collective-permute-start(bf16[512,512]{1,0:T(8,128)(2,1)} %collective-permute-done.11.refs_3_), channel_id=1, source_target_pairs={{12,14},{13,15},{14,12},{15,13},{28,30},{29,31},{30,28},{31,29}} | collective-permute-start | bytes 1572872 | tf_op jit(solution)/shard_map/ppermute | solution.py:350
  77.4 0.1 collective-permute-done.9.refs_6_
  77.5 6.9 %collective-permute-done.3.refs_2_ = bf16[512,512]{1,0:T(8,128)(2,1)} collective-permute-done((bf16[512,512]{1,0:T(8,128)(2,1)S(1)}, bf16[512,512]{1,0:T(8,128)(2,1)}, u32[]{:S(2)}, u32[]{:S(2)}) %collective-permute-start.3) | collective-permute-done | bytes 524320 | tf_op jit(solution)/shard_map/ppermute | solution.py:357
  84.4 1.3 %collective-permute-start.4 = (bf16[512,512]{1,0:T(8,128)(2,1)}, bf16[512,512]{1,0:T(8,128)(2,1)}, u32[]{:S(2)}, u32[]{:S(2)}) collective-permute-start(bf16[512,512]{1,0:T(8,128)(2,1)} %collective-permute-done.3.refs_2_), channel_id=1, source_target_pairs={{8,12},{9,13},{10,14},{11,15},{24,28},{25,29},{26,30},{27,31}} | collective-permute-start | bytes 1572872 | tf_op jit(solution)/shard_map/ppermute | solution.py:357
  85.7 0.0 copy-done.6
  85.7 1.9 %collective-permute-start.10 = (bf16[512,512]{1,0:T(8,128)(2,1)}, bf16[512,512]{1,0:T(8,128)(2,1)}, u32[]{:S(2)}, u32[]{:S(2)}) collective-permute-start(bf16[512,512]{1,0:T(8,128)(2,1)} %collective-permute-done.3.refs_2_), channel_id=1, source_target_pairs={{8,10},{9,11},{10,8},{11,9},{12,14},{13,15},{14,12},{15,13},{24,26... | collective-permute-start | bytes 1572872 | tf_op jit(solution)/shard_map/ppermute | solution.py:350
  87.6 0.0 copy-done.7
  87.6 1.3 %collective-permute-start.12 = (bf16[512,512]{1,0:T(8,128)(2,1)S(1)}, bf16[512,512]{1,0:T(8,128)(2,1)}, u32[]{:S(2)}, u32[]{:S(2)}) collective-permute-start(bf16[512,512]{1,0:T(8,128)(2,1)S(1)} %collective-permute-done.5.refs_4_), channel_id=1, source_target_pairs={{0,12},{1,13},{2,14},{3,15},{16,28},{17,29},{18,30},{19,31}} | collective-permute-start | bytes 1572872 | tf_op jit(solution)/shard_map/ppermute | solution.py:363
  88.9 0.0 copy-done.8
  88.9 0.6 fusion.1.slot_ref
  89.5 0.0 collective-permute-done.13.refs_7_
  89.5 0.0 copy-done.2
  89.6 0.0 copy-done.3
  89.6 0.0 copy-done.5
  89.6 10.7 %attention.2.refs_8_ = bf16[512,4096]{1,0:T(8,128)(2,1)} custom-call(s32[8,7]{1,0:T(8,128)} %fusion.1.slot_ref, s32[8,7]{1,0:T(8,128)} %cut_ref.3, s32[1]{0:T(128)} %bitcast.odd_ref, bf16[512,4096]{1,0:T(8,128)(2,1)} %q_ref.3, bf16[512,512]{1,0:T(8,128)(2,1)} %get-tuple-element.18.refs_0_, bf16[512,512]{1,0:T(8,128)(2,1)} %copy-done.2, ...), custom_call_target="tpu_custom_call" | custom-call | flops 2147483648 | bytes 8388608 | tf_op jit(solution)/shard_map/attention/pallas_call | solution.py:298
  100.3 9.1 %collective-permute-done.4.refs_3_ = bf16[512,512]{1,0:T(8,128)(2,1)} collective-permute-done((bf16[512,512]{1,0:T(8,128)(2,1)}, bf16[512,512]{1,0:T(8,128)(2,1)}, u32[]{:S(2)}, u32[]{:S(2)}) %collective-permute-start.4) | collective-permute-done | bytes 524320 | tf_op jit(solution)/shard_map/ppermute | solution.py:357
  109.4 0.0 collective-permute-done.10.refs_6_
  109.4 0.0 collective-permute-done.12.refs_7_
  109.4 0.0 copy-done
  109.4 0.0 copy-done.1
  109.4 0.0 copy-done.4
  109.4 10.7 %attention.3 = bf16[512,4096]{1,0:T(8,128)(2,1)} custom-call(s32[8,7]{1,0:T(8,128)} %fusion.1.slot_ref, s32[8,7]{1,0:T(8,128)} %cut_ref.3, s32[1]{0:T(128)} %bitcast.odd_ref, bf16[512,4096]{1,0:T(8,128)(2,1)} %q_ref.3, bf16[512,512]{1,0:T(8,128)(2,1)} %project.1.refs_0_, bf16[512,512]{1,0:T(8,128)(2,1)} %copy-done.1, ...), custom_call_target="tpu_custom_call", output_to_operand_aliasing={{}: (12, {})} | custom-call | flops 2147483648 | bytes 8388608 | tf_op jit(solution)/shard_map/attention/pallas_call | solution.py:298
  (3 shorter events, 0.0 us)
Async XLA Ops:
  14.1 18.5 %collective-permute-start.1 = (bf16[512,512]{1,0:T(8,128)(2,1)}, bf16[512,512]{1,0:T(8,128)(2,1)S(1)}, u32[]{:S(2)}, u32[]{:S(2)}) collective-permute-start(bf16[512,512]{1,0:T(8,128)(2,1)} %get-tuple-element.18.refs_0_), channel_id=1, source_target_pairs={{0,4},{1,5},{2,6},{3,7},{4,8},{5,9},{6,10},{7,11},{8,12},{9,13},{1... | collective-permute-start | bytes 1572872 | tf_op jit(solution)/shard_map/ppermute | solution.py:357
  15.4 18.5 %collective-permute-start.7 = (bf16[512,512]{1,0:T(8,128)(2,1)}, bf16[512,512]{1,0:T(8,128)(2,1)S(1)}, u32[]{:S(2)}, u32[]{:S(2)}) collective-permute-start(bf16[512,512]{1,0:T(8,128)(2,1)} %get-tuple-element.18.refs_0_), channel_id=1, source_target_pairs={{0,2},{1,3},{4,6},{5,7},{8,10},{9,11},{12,14},{13,15},{16,18},{17,... | collective-permute-start | bytes 1572872 | tf_op jit(solution)/shard_map/ppermute | solution.py:350
  18.9 70.0 %copy-start.8 = (s32[8,7]{1,0:T(8,128)S(1)}, s32[8,7]{1,0:T(8,128)}, u32[]{:S(2)}) copy-start(s32[8,7]{1,0:T(8,128)} %param.12) | copy-start | bytes 676
  30.0 13.9 %collective-permute-start.5 = (bf16[512,512]{1,0:T(8,128)(2,1)}, bf16[512,512]{1,0:T(8,128)(2,1)S(1)}, u32[]{:S(2)}, u32[]{:S(2)}) collective-permute-start(bf16[512,512]{1,0:T(8,128)(2,1)} %project.1.refs_0_), channel_id=1, source_target_pairs={{0,2},{1,3},{2,0},{3,1},{4,6},{5,7},{8,10},{9,11},{12,14},{13,15},... | collective-permute-start | bytes 1572872 | tf_op jit(solution)/shard_map/ppermute | solution.py:350
  31.3 17.6 %collective-permute-start = (bf16[512,512]{1,0:T(8,128)(2,1)}, bf16[512,512]{1,0:T(8,128)(2,1)S(1)}, u32[]{:S(2)}, u32[]{:S(2)}) collective-permute-start(bf16[512,512]{1,0:T(8,128)(2,1)} %project.1.refs_0_), channel_id=1, source_target_pairs={{0,4},{1,5},{2,6},{3,7},{4,8},{5,9},{6,10},{7,11},{8,12},{9,13},{1... | collective-permute-start | bytes 1572872 | tf_op jit(solution)/shard_map/ppermute | solution.py:357
  32.6 56.9 %copy-start.2 = (bf16[512,512]{1,0:T(8,128)(2,1)}, bf16[512,512]{1,0:T(8,128)(2,1)S(1)}, u32[]{:S(2)}) copy-start(bf16[512,512]{1,0:T(8,128)(2,1)S(1)} %collective-permute-done.1.refs_1_) | copy-start | bytes 1572868
  32.6 26.0 %collective-permute-start.2 = (bf16[512,512]{1,0:T(8,128)(2,1)S(1)}, bf16[512,512]{1,0:T(8,128)(2,1)S(1)}, u32[]{:S(2)}, u32[]{:S(2)}) collective-permute-start(bf16[512,512]{1,0:T(8,128)(2,1)S(1)} %collective-permute-done.1.refs_1_), channel_id=1, source_target_pairs={{4,8},{5,9},{6,10},{7,11},{8,12},{9,13},{10,14},{11,15},{20,24},{2... | collective-permute-start | bytes 1572872 | tf_op jit(solution)/shard_map/ppermute | solution.py:357
  33.9 55.6 %copy-start.3 = (bf16[512,512]{1,0:T(8,128)(2,1)}, bf16[512,512]{1,0:T(8,128)(2,1)S(1)}, u32[]{:S(2)}) copy-start(bf16[512,512]{1,0:T(8,128)(2,1)S(1)} %collective-permute-done.7.refs_4_) | copy-start | bytes 1572868
  34.0 26.0 %collective-permute-start.8 = (bf16[512,512]{1,0:T(8,128)(2,1)S(1)}, bf16[512,512]{1,0:T(8,128)(2,1)S(1)}, u32[]{:S(2)}, u32[]{:S(2)}) collective-permute-start(bf16[512,512]{1,0:T(8,128)(2,1)S(1)} %collective-permute-done.1.refs_1_), channel_id=1, source_target_pairs={{4,6},{5,7},{6,4},{7,5},{8,10},{9,11},{10,8},{11,9},{12,14},{13,15... | collective-permute-start | bytes 1572872 | tf_op jit(solution)/shard_map/ppermute | solution.py:350
  43.9 65.5 %copy-start = (bf16[512,512]{1,0:T(8,128)(2,1)}, bf16[512,512]{1,0:T(8,128)(2,1)S(1)}, u32[]{:S(2)}) copy-start(bf16[512,512]{1,0:T(8,128)(2,1)S(1)} %collective-permute-done.5.refs_4_) | copy-start | bytes 1572868
  48.9 60.5 %copy-start.1 = (bf16[512,512]{1,0:T(8,128)(2,1)}, bf16[512,512]{1,0:T(8,128)(2,1)S(1)}, u32[]{:S(2)}) copy-start(bf16[512,512]{1,0:T(8,128)(2,1)S(1)} %collective-permute-done.refs_1_) | copy-start | bytes 1572868
  48.9 17.4 %collective-permute-start.6 = (bf16[512,512]{1,0:T(8,128)(2,1)S(1)}, bf16[512,512]{1,0:T(8,128)(2,1)S(1)}, u32[]{:S(2)}, u32[]{:S(2)}) collective-permute-start(bf16[512,512]{1,0:T(8,128)(2,1)S(1)} %collective-permute-done.refs_1_), channel_id=1, source_target_pairs={{4,6},{5,7},{6,4},{7,5},{8,10},{9,11},{10,8},{11,9},{12,14},{13,15... | collective-permute-start | bytes 1572872 | tf_op jit(solution)/shard_map/ppermute | solution.py:350
  58.7 30.9 %copy-start.5 = (bf16[512,512]{1,0:T(8,128)(2,1)}, bf16[512,512]{1,0:T(8,128)(2,1)S(1)}, u32[]{:S(2)}) copy-start(bf16[512,512]{1,0:T(8,128)(2,1)S(1)} %collective-permute-done.2.refs_2_) | copy-start | bytes 1572868
  58.7 16.8 %collective-permute-start.11 = (bf16[512,512]{1,0:T(8,128)(2,1)S(1)}, bf16[512,512]{1,0:T(8,128)(2,1)}, u32[]{:S(2)}, u32[]{:S(2)}) collective-permute-start(bf16[512,512]{1,0:T(8,128)(2,1)S(1)} %collective-permute-done.2.refs_2_), channel_id=1, source_target_pairs={{8,12},{9,13},{10,14},{11,15},{24,28},{25,29},{26,30},{27,31}} | collective-permute-start | bytes 1572872 | tf_op jit(solution)/shard_map/ppermute | solution.py:357
  60.0 25.7 %copy-start.6 = (bf16[512,512]{1,0:T(8,128)(2,1)}, bf16[512,512]{1,0:T(8,128)(2,1)S(1)}, u32[]{:S(2)}) copy-start(bf16[512,512]{1,0:T(8,128)(2,1)S(1)} %collective-permute-done.8.refs_5_) | copy-start | bytes 1572868
  60.0 17.5 %collective-permute-start.9 = (bf16[512,512]{1,0:T(8,128)(2,1)S(1)}, bf16[512,512]{1,0:T(8,128)(2,1)S(1)}, u32[]{:S(2)}, u32[]{:S(2)}) collective-permute-start(bf16[512,512]{1,0:T(8,128)(2,1)S(1)} %collective-permute-done.2.refs_2_), channel_id=1, source_target_pairs={{8,10},{9,11},{10,8},{11,9},{12,14},{13,15},{14,12},{15,13},{24,26... | collective-permute-start | bytes 1572872 | tf_op jit(solution)/shard_map/ppermute | solution.py:350
  61.9 22.5 %collective-permute-start.3 = (bf16[512,512]{1,0:T(8,128)(2,1)S(1)}, bf16[512,512]{1,0:T(8,128)(2,1)}, u32[]{:S(2)}, u32[]{:S(2)}) collective-permute-start(bf16[512,512]{1,0:T(8,128)(2,1)S(1)} %collective-permute-done.refs_1_), channel_id=1, source_target_pairs={{4,8},{5,9},{6,10},{7,11},{8,12},{9,13},{10,14},{11,15},{20,24},{2... | collective-permute-start | bytes 1572872 | tf_op jit(solution)/shard_map/ppermute | solution.py:357
  66.3 43.1 %copy-start.4 = (bf16[512,512]{1,0:T(8,128)(2,1)}, bf16[512,512]{1,0:T(8,128)(2,1)S(1)}, u32[]{:S(2)}) copy-start(bf16[512,512]{1,0:T(8,128)(2,1)S(1)} %collective-permute-done.6.refs_5_) | copy-start | bytes 1572868
  75.5 14.0 %collective-permute-start.13 = (bf16[512,512]{1,0:T(8,128)(2,1)}, bf16[512,512]{1,0:T(8,128)(2,1)}, u32[]{:S(2)}, u32[]{:S(2)}) collective-permute-start(bf16[512,512]{1,0:T(8,128)(2,1)} %collective-permute-done.11.refs_3_), channel_id=1, source_target_pairs={{12,14},{13,15},{14,12},{15,13},{28,30},{29,31},{30,28},{31,29}} | collective-permute-start | bytes 1572872 | tf_op jit(solution)/shard_map/ppermute | solution.py:350
  77.5 10.1 %copy-start.7 = (bf16[512,512]{1,0:T(8,128)(2,1)}, bf16[512,512]{1,0:T(8,128)(2,1)S(1)}, u32[]{:S(2)}) copy-start(bf16[512,512]{1,0:T(8,128)(2,1)S(1)} %collective-permute-done.9.refs_6_) | copy-start | bytes 1572868
  84.4 25.0 %collective-permute-start.4 = (bf16[512,512]{1,0:T(8,128)(2,1)}, bf16[512,512]{1,0:T(8,128)(2,1)}, u32[]{:S(2)}, u32[]{:S(2)}) collective-permute-start(bf16[512,512]{1,0:T(8,128)(2,1)} %collective-permute-done.3.refs_2_), channel_id=1, source_target_pairs={{8,12},{9,13},{10,14},{11,15},{24,28},{25,29},{26,30},{27,31}} | collective-permute-start | bytes 1572872 | tf_op jit(solution)/shard_map/ppermute | solution.py:357
  85.7 23.7 %collective-permute-start.10 = (bf16[512,512]{1,0:T(8,128)(2,1)}, bf16[512,512]{1,0:T(8,128)(2,1)}, u32[]{:S(2)}, u32[]{:S(2)}) collective-permute-start(bf16[512,512]{1,0:T(8,128)(2,1)} %collective-permute-done.3.refs_2_), channel_id=1, source_target_pairs={{8,10},{9,11},{10,8},{11,9},{12,14},{13,15},{14,12},{15,13},{24,26... | collective-permute-start | bytes 1572872 | tf_op jit(solution)/shard_map/ppermute | solution.py:350
  87.6 21.8 %collective-permute-start.12 = (bf16[512,512]{1,0:T(8,128)(2,1)S(1)}, bf16[512,512]{1,0:T(8,128)(2,1)}, u32[]{:S(2)}, u32[]{:S(2)}) collective-permute-start(bf16[512,512]{1,0:T(8,128)(2,1)S(1)} %collective-permute-done.5.refs_4_), channel_id=1, source_target_pairs={{0,12},{1,13},{2,14},{3,15},{16,28},{17,29},{18,30},{19,31}} | collective-permute-start | bytes 1572872 | tf_op jit(solution)/shard_map/ppermute | solution.py:363

commit v10 on v7

v10 whole, which is shorter than its diff:
```python
import functools
import jax
import jax.numpy as jnp
from jax import lax
from jax.experimental import pallas as pl
from jax.experimental.pallas import tpu as pltpu
from jax.sharding import PartitionSpec as P

HEAD_DIM = 128
EPS = 1e-05
LOG2E = 1.4426950408889634
MASKED = -1e30
MIB = 1024 * 1024
CHUNKS = 4
LOADS = 8
UNITS = 2


PLAN = (
    ("across", 0, 0, ()),
    ("along", 1, 0, ()),
    ("across", 0, 1, ()),
    ("along", 1, 1, ()),
    ("across", 1, 0, (("across", 0, 0),)),
    ("along", 2, 0, (("along", 1, 0),)),
    ("across", 1, 1, (("across", 0, 1),)),
    ("along", 3, 0, (("along", 1, 1),)),
    ("across", 2, 0, (("across", 1, 0),)),
    ("along", 2, 1, (("along", 2, 0),)),
    ("across", 3, 0, (("across", 1, 1),)),
    ("across", 2, 1, (("across", 2, 0),)),
    ("down", 3, 1, (("along", 3, 0), ("across", 2, 0))),
    ("along", 3, 1, (("along", 2, 1),)),
)


def norm_project_kernel(
    x_hbm, gain_ref, key_hbm, value_hbm, scale_ref, kv_ref,
    x_scr, weight_scr, even_scr, odd_scr, acc_scr, x_sem, key_sem, value_sem,
):
    loads, rows, chunk = x_scr.shape
    width = weight_scr.shape[2] // 2
    lanes = 128
    band = 128

    def span(c):
        return pl.ds(pl.multiple_of(c * chunk, chunk), chunk)

    def load_x(c):
        return pltpu.make_async_copy(x_hbm.at[:, span(c)], x_scr.at[c], x_sem.at[c])

    def load_weights(c):
        head = pl.ds(0, width)
        return [
            pltpu.make_async_copy(
                key_hbm.at[span(c), head], weight_scr.at[c, :, pl.ds(0, width)], key_sem.at[c]
            ),
            pltpu.make_async_copy(
                value_hbm.at[span(c), head], weight_scr.at[c, :, pl.ds(width, width)], value_sem.at[c]
            ),
        ]

    for c in range(loads):
        load_x(c).start()
    scale_ref[...] = jnp.zeros_like(scale_ref)

    def square(c, carry):
        load_x(c).wait()

        @pl.when(c >= loads // 2)
        def _():
            for part in range(2):
                for copy in load_weights(2 * (c - loads // 2) + part):
                    copy.start()

        for first in range(0, rows, band):
            row = slice(first, first + band)
            total = scale_ref[row, :]
            for lane in range(0, chunk, lanes):
                x = x_scr[c, row, lane : lane + lanes].astype(jnp.float32)
                total += x * x
            scale_ref[row, :] = total
        return carry

    lax.fori_loop(0, loads, square, 0)
    mean_sq = jnp.sum(scale_ref[...], axis=-1, keepdims=True) / (loads * chunk)
    scale_ref[...] = jnp.broadcast_to(lax.rsqrt(mean_sq + EPS), scale_ref.shape)

    def normalise(normed_scr, c):
        for first in range(0, rows, band):
            row = slice(first, first + band)
            inverse = scale_ref[row, :]
            for lane in range(0, chunk, lanes):
                cols = slice(lane, lane + lanes)
                x = x_scr[c, row, cols].astype(jnp.float32)
                gain = gain_ref[c, :, cols]
                normed_scr[row, cols] = (x * inverse * gain).astype(jnp.bfloat16)

    def multiply(normed_scr, c):
        for copy in load_weights(c):
            copy.wait()
        acc_scr[...] += jnp.dot(
            normed_scr[...], weight_scr[c], preferred_element_type=jnp.float32
        )

    normalise(even_scr, 0)
    acc_scr[...] = jnp.zeros_like(acc_scr)

    def pair(p, carry):
        multiply(even_scr, 2 * p)
        normalise(odd_scr, 2 * p + 1)
        multiply(odd_scr, 2 * p + 1)
        normalise(even_scr, 2 * p + 2)
        return carry

    lax.fori_loop(0, loads // 2 - 1, pair, 0)
    multiply(even_scr, loads - 2)
    normalise(odd_scr, loads - 1)
    multiply(odd_scr, loads - 1)
    write_heads(kv_ref, acc_scr)


def write_heads(kv_ref, acc_scr):
    width = kv_ref.shape[1] // 2
    for head in range(width // HEAD_DIM):
        for part in range(2):
            source = slice(part * width + head * HEAD_DIM, part * width + (head + 1) * HEAD_DIM)
            target = slice((2 * head + part) * HEAD_DIM, (2 * head + part + 1) * HEAD_DIM)
            kv_ref[:, target] = acc_scr[:, source].astype(jnp.bfloat16)


def norm_project(hidden, gain, key_weight, value_weight):
    rows, features = hidden.shape
    width = key_weight.shape[1] // UNITS
    chunk = features // LOADS
    whole = pl.BlockSpec(memory_space=pltpu.VMEM)
    held = pl.BlockSpec(memory_space=pltpu.HBM)
    return pl.pallas_call(
        norm_project_kernel,
        in_specs=[held, whole, held, held],
        out_specs=[whole, whole],
        out_shape=[
            jax.ShapeDtypeStruct((rows, 128), jnp.float32),
            jax.ShapeDtypeStruct((rows, 2 * width), jnp.bfloat16),
        ],
        scratch_shapes=[
            pltpu.VMEM((LOADS, rows, chunk), jnp.bfloat16),
            pltpu.VMEM((LOADS, chunk, 2 * width), jnp.bfloat16),
            pltpu.VMEM((rows, chunk), jnp.bfloat16),
            pltpu.VMEM((rows, chunk), jnp.bfloat16),
            pltpu.VMEM((rows, 2 * width), jnp.float32),
            pltpu.SemaphoreType.DMA((LOADS,)),
            pltpu.SemaphoreType.DMA((LOADS,)),
            pltpu.SemaphoreType.DMA((LOADS,)),
        ],
        compiler_params=pltpu.CompilerParams(vmem_limit_bytes=57 * MIB),
        cost_estimate=pl.CostEstimate(
            flops=4 * rows * features * width, bytes_accessed=16 * MIB, transcendentals=0
        ),
        name="norm_project",
    )(hidden, gain.reshape(LOADS, 1, chunk), key_weight, value_weight)


def project_kernel(x_ref, scale_ref, gain_ref, key_ref, value_ref, kv_ref, acc_scr):
    step = pl.program_id(0)
    rows, chunk = x_ref.shape
    width = key_ref.shape[1]
    lanes = 128
    inverse = scale_ref[...]
    parts = []
    for lane in range(0, chunk, lanes):
        cols = slice(lane, lane + lanes)
        x = x_ref[:, cols].astype(jnp.float32)
        parts.append((x * inverse * gain_ref[:, cols]).astype(jnp.bfloat16))
    normed = jnp.concatenate(parts, axis=1)
    for part, weight in enumerate((key_ref, value_ref)):
        cols = slice(part * width, (part + 1) * width)
        term = jnp.dot(normed, weight[...], preferred_element_type=jnp.float32)
        acc_scr[:, cols] = jnp.where(step == 0, term, acc_scr[:, cols] + term)

    @pl.when(step == CHUNKS - 1)
    def _():
        write_heads(kv_ref, acc_scr)


def project(hidden, scale, gain, key_weight, value_weight, unit):
    rows, features = hidden.shape
    chunk = features // CHUNKS
    width = key_weight.shape[1] // UNITS
    weight = pl.BlockSpec((chunk, width), lambda i: (i, unit))
    return pl.pallas_call(
        project_kernel,
        grid=(CHUNKS,),
        in_specs=[
            pl.BlockSpec((rows, chunk), lambda i: (0, i)),
            pl.BlockSpec(scale.shape, lambda i: (0, 0)),
            pl.BlockSpec((1, chunk), lambda i: (0, i)),
            weight,
            weight,
        ],
        out_specs=pl.BlockSpec((rows, 2 * width), lambda i: (0, 0)),
        out_shape=jax.ShapeDtypeStruct((rows, 2 * width), jnp.bfloat16),
        scratch_shapes=[pltpu.VMEM((rows, 2 * width), jnp.float32)],
        compiler_params=pltpu.CompilerParams(vmem_limit_bytes=57 * MIB),
        cost_estimate=pl.CostEstimate(
            flops=4 * rows * features * width, bytes_accessed=16 * MIB, transcendentals=0
        ),
        name="project",
    )(hidden, scale, gain.reshape(1, features), key_weight, value_weight)


def attention_kernel(block, unit, near, slot_ref, cut_ref, odd_ref, q_hbm, *refs):
    own_hbm, straight, crossed = refs[0], refs[1 : near + 1], refs[near + 1 : 2 * near + 2]
    out_hbm, kv_scr, q_scr, out_scr, even_scr, odd_scr, kv_sem, q_sem, out_sem = refs[-9:]
    kv_heads, levels, _, width = kv_scr.shape
    depth = levels - 1
    blocks, wide = q_scr.shape[0] // kv_heads, q_scr.shape[2]
    per_group = wide // HEAD_DIM
    items = kv_heads * blocks
    scale = HEAD_DIM**-0.5 * LOG2E

    def load_kv(head):
        def copy(ref, level, number):
            return pltpu.make_async_copy(
                ref.at[:, head * width : (head + 1) * width],
                kv_scr.at[head, level],
                kv_sem.at[head, number],
            )

        copies = [copy(own_hbm, depth, 0)]
        for s, ref in enumerate(straight):
            copies.append(copy(ref, 2 * s + 1, s + 1))
        for s, ref in enumerate(crossed):
            level = 2 * lax.rem(s + odd_ref[0] + near, near + 1)
            copies.append(copy(ref, level, near + s + 1))
        return copies

    def place(ref, item):
        head, here = lax.div(item, blocks), lax.rem(item, blocks)
        rows = pl.ds(pl.multiple_of(here * block, block), block)
        cols = pl.ds(pl.multiple_of((unit * kv_heads + head) * wide, wide), wide)
        return ref.at[rows, cols]

    def load_q(item):
        return pltpu.make_async_copy(place(q_hbm, item), q_scr.at[item], q_sem.at[item])

    def store(item):
        return pltpu.make_async_copy(out_scr.at[item], place(out_hbm, item), out_sem.at[item])

    for head in range(kv_heads):
        for copy in load_kv(head):
            copy.start()
        for item in range(head * blocks, (head + 1) * blocks):
            load_q(item).start()

    token = lax.broadcasted_iota(jnp.int32, (block, HEAD_DIM), 0)
    lane = lax.broadcasted_iota(jnp.int32, (block, HEAD_DIM), 1)
    hidden_later = jnp.where((lane >= block) & (lane - block > token), MASKED, 0.0)
    query_mask = jnp.where(lane == 0, 1.0, hidden_later).astype(jnp.bfloat16)
    query_mask = jnp.concatenate([query_mask] * per_group, axis=0)
    own_mask = jnp.where(lane - block == token, 1.0, 0.0).astype(jnp.bfloat16)

    def gather(item, cols):
        head, here = lax.div(item, blocks), lax.rem(item, blocks)
        pieces = []
        for k in range(levels):
            slot = slot_ref[here, k] if k < depth else here
            rows = pl.ds(pl.multiple_of(slot * block, block), block)
            pieces.append(kv_scr[head, k, rows, cols])
        return jnp.concatenate(pieces, axis=0)

    def score(item, score_scr):
        here = lax.rem(item, blocks)
        masks = []
        for k in range(depth):
            unseen = (lane == 0) & (token >= cut_ref[here, k])
            masks.append(jnp.where(unseen, MASKED, 0.0).astype(jnp.bfloat16))
        masks.append(own_mask)
        keys = jnp.concatenate(
            [gather(item, slice(0, HEAD_DIM)), jnp.concatenate(masks, axis=0)], axis=1
        )
        queries = jnp.concatenate(
            [q_scr[item, :, r * HEAD_DIM : (r + 1) * HEAD_DIM] for r in range(per_group)], axis=0
        )
        queries = jnp.concatenate([queries, query_mask], axis=1)
        score_scr[...] = lax.dot_general(
            queries, keys, (((1,), (1,)), ((), ())), preferred_element_type=jnp.float32
        )

    def finish(item, score_scr):
        scores = score_scr[...]
        peak = jnp.max(scores, axis=-1, keepdims=True)
        weights = jnp.exp2((scores - peak) * scale).astype(jnp.bfloat16)
        values = gather(item, slice(HEAD_DIM, 2 * HEAD_DIM))
        padded = jnp.concatenate([values, jnp.ones_like(values)], axis=1)
        both = jnp.dot(weights, padded, preferred_element_type=jnp.float32)
        context = (both[:, :HEAD_DIM] * (1.0 / both[:, HEAD_DIM:])).astype(jnp.bfloat16)
        for r in range(per_group):
            out_scr[item, :, r * HEAD_DIM : (r + 1) * HEAD_DIM] = context[
                r * block : (r + 1) * block
            ]

    def arrive(item):
        @pl.when(item < items)
        def _():
            load_q(item).wait()

        for head in range(1, kv_heads):

            @pl.when(item == head * blocks)
            def _(head=head):
                for copy in load_kv(head):
                    copy.wait()

    for copy in load_kv(0):
        copy.wait()
    load_q(0).wait()
    score(0, even_scr)

    def pair(j, carry):
        item = 2 * j
        arrive(item + 1)
        score(item + 1, odd_scr)
        finish(item, even_scr)
        store(item).start()
        arrive(item + 2)
        score(jnp.minimum(item + 2, items - 1), even_scr)
        finish(item + 1, odd_scr)
        store(item + 1).start()
        return carry

    lax.fori_loop(0, items // 2, pair, 0)
    for item in range(items):
        store(item).wait()


def attention(slots, cuts, odd, queries, own, straight, crossed, unit, previous):
    rows, features = queries.shape
    blocks, depth = slots.shape
    block = rows // blocks
    near = len(straight)
    kv_heads = own.shape[1] // (2 * HEAD_DIM)
    wide = features // UNITS // kv_heads
    keys = (depth + 1) * block
    tall = wide // HEAD_DIM * block
    items = kv_heads * blocks
    held = pl.BlockSpec(memory_space=pltpu.HBM)
    table = pl.BlockSpec(memory_space=pltpu.SMEM)
    operands = [slots, cuts, odd, queries, own, *straight, *crossed]
    aliases = {}
    if previous is not None:
        aliases = {len(operands): 0}
        operands.append(previous)
    return pl.pallas_call(
        functools.partial(attention_kernel, block, unit, near),
        in_specs=[table] * 3 + [held] * (len(operands) - 3),
        out_specs=held,
        out_shape=jax.ShapeDtypeStruct((rows, features), jnp.bfloat16),
        input_output_aliases=aliases,
        scratch_shapes=[
            pltpu.VMEM((kv_heads, depth + 1, rows, 2 * HEAD_DIM), own.dtype),
            pltpu.VMEM((items, block, wide), jnp.bfloat16),
            pltpu.VMEM((items, block, wide), jnp.bfloat16),
            pltpu.VMEM((tall, keys), jnp.float32),
            pltpu.VMEM((tall, keys), jnp.float32),
            pltpu.SemaphoreType.DMA((kv_heads, depth + 1)),
            pltpu.SemaphoreType.DMA((items,)),
            pltpu.SemaphoreType.DMA((items,)),
        ],
        compiler_params=pltpu.CompilerParams(vmem_limit_bytes=57 * MIB),
        cost_estimate=pl.CostEstimate(
            flops=4 * items * tall * keys * HEAD_DIM,
            bytes_accessed=8 * MIB,
            transcendentals=items * tall * keys,
        ),
        name="attention",
    )(*operands)


def shards(hidden, queries, norm_gain, key_weight, value_weight, anc_ids, anc_cut):
    blocks, depth = anc_ids.shape
    levels = depth + 1
    size = lax.axis_size("node")
    chains = size // levels
    near = depth // 2
    half = [index // chains // 2 for index in range(size)]
    even = [index // chains % 2 == 0 for index in range(size)]
    other = [index + chains if even[index] else index - chains for index in range(size)]
    odd = (lax.axis_index("node") // chains % 2).astype(jnp.int32).reshape(1)
    slots = jnp.where(anc_ids >= 0, anc_ids % blocks, 0)

    scale, first = norm_project(hidden, norm_gain, key_weight, value_weight)
    own = [first, project(hidden, scale, norm_gain, key_weight, value_weight, 1)]
    def after(array, *earlier):
        return lax.optimization_barrier((array, *earlier))[0]

    column = 2 * chains
    moved = {("own", 0, 0): own[0], ("own", 0, 1): own[1]}

    def step(kind, s, unit, waits):
        if kind == "across":
            source = ("along", s, unit) if s else ("own", 0, unit)
            exchange = s > 0 or unit == UNITS - 1
            pairs = [
                (i, other[i])
                for i in range(size)
                if half[i] >= s and (even[i] or (exchange and half[i] == 0) or s > 0)
            ]
        elif kind == "along":
            source = ("along", s - 1, unit) if s > 1 else ("own", 0, unit)
            pairs = [(i, i + column) for i in range(size - column) if half[i] >= s - 1]
        else:
            source = ("across" if kind == "down" else "own", 0, unit)
            pairs = [(i, i + s * column) for i in range(size - s * column)]
        array = lax.optimization_barrier((moved[source], *[moved[w] for w in waits]))[0]
        key = "along" if kind == "direct" else kind
        moved[key, s, unit] = lax.ppermute(array, "node", pairs)

    for kind, s, unit, waits in PLAN:
        step(kind, s, unit, waits)
    result = None
    for unit in range(UNITS):
        result = attention(
            slots,
            anc_cut,
            odd,
            queries,
            own[unit],
            [moved["along", s, unit] for s in range(1, near + 1)],
            [moved["across", s, unit] for s in range(near)]
            + [moved["across" if unit == 0 else "down", near, unit]],
            unit,
            result,
        )
    return result


def solution(mesh):
    placed = (
        P(("groups", "node"), None),
        P(("groups", "node"), None),
        P(),
        P(),
        P(),
        P(("groups", "node"), None),
        P(("groups", "node"), None),
    )
    return jax.shard_map(
        shards, mesh=mesh, in_specs=placed, out_specs=P(("groups", "node"), None), check_vma=False
    )
```

time: 127 us -> 120 us (0.945)
  the two profiles are of different devices: /device:TPU:0 before, /device:TPU:24 now
where the time goes in v10:
time: 120 us; the launch traced here: 119 us
  Pallas kernels  47 us (39%)
  waiting for transfers between devices  46.8 us (39%)
  starting transfers between devices  24.3 us (20%)
    ppermute x14, waiting for transfers between devices, step(): moved[key, s, unit] = lax.ppermute(array, 'node', pairs)  46.8 us
    ppermute x14, starting transfers between devices, step(): moved[key, s, unit] = lax.ppermute(array, 'node', pairs)  24.3 us
    pallas_call x2, Pallas kernels, attention(): pl.pallas_call(functools.partial(attention_kernel, block, unit, near), in...  24.3 us
    pallas_call x1, Pallas kernels, norm_project(): pl.pallas_call(norm_project_kernel, in_specs=[held, whole, held, held], o...  13.3 us
    pallas_call x1, Pallas kernels, project(): pl.pallas_call(project_kernel, grid=(CHUNKS,), in_specs=[pl.BlockSpec((ro...  9.35 us
  transfers between devices with their start and end apart: 14, of which 8 were waited for; matrix products, arithmetic and copies ran while one was open for 1% of the time, Pallas kernels for 18%

profile of v10, /device:TPU:24, one launch (start us, length us, event | category | flops | bytes accessed | tf_op | source)
XLA Modules:
  0.0 119.0 jit_solution(5320967295619017166)
XLA Ops:
  0.0 13.3 %norm_project.1 = (f32[512,128]{1,0:T(8,128)}, bf16[512,512]{1,0:T(8,128)(2,1)}) custom-call(bf16[512,8192]{1,0:T(8,128)(2,1)} %x_ref.1, f32[8,1,1024]{2,1,0:T(1,128)} %bitcast.3, bf16[8192,512]{1,0:T(8,128)(2,1)} %key_ref.1, bf16[8192,512]{1,0:T(8,128)(2,1)} %value_ref.1), custom_call_target="tpu_custom_call" | custom-call | flops 4294967296 | bytes 16777216 | tf_op jit(solution)/shard_map/norm_project/pallas_call | solution.py:138
  13.3 1.3 %collective-permute-start.1 = (bf16[512,512]{1,0:T(8,128)(2,1)}, bf16[512,512]{1,0:T(8,128)(2,1)S(1)}, u32[]{:S(2)}, u32[]{:S(2)}) collective-permute-start(bf16[512,512]{1,0:T(8,128)(2,1)} %get-tuple-element.18.refs_0_), channel_id=1, source_target_pairs={{0,4},{1,5},{2,6},{3,7},{4,8},{5,9},{6,10},{7,11},{8,12},{9,13},{1... | collective-permute-start | bytes 1572872 | tf_op jit(solution)/shard_map/ppermute | solution.py:417
  14.6 3.5 %collective-permute-start.7 = (bf16[512,512]{1,0:T(8,128)(2,1)}, bf16[512,512]{1,0:T(8,128)(2,1)S(1)}, u32[]{:S(2)}, u32[]{:S(2)}) collective-permute-start(bf16[512,512]{1,0:T(8,128)(2,1)} %get-tuple-element.18.refs_0_), channel_id=1, source_target_pairs={{0,2},{1,3},{4,6},{5,7},{8,10},{9,11},{12,14},{13,15},{16,18},{17,... | collective-permute-start | bytes 1572872 | tf_op jit(solution)/shard_map/ppermute | solution.py:417
  18.1 0.0 copy-start.8
  18.1 9.3 %project.1.refs_0_ = bf16[512,512]{1,0:T(8,128)(2,1)} custom-call(bf16[512,8192]{1,0:T(8,128)(2,1)} %x_ref.1, f32[512,128]{1,0:T(8,128)} %get-tuple-element.17.scale_ref, f32[1,8192]{1,0:T(1,128)} %bitcast.4, bf16[8192,512]{1,0:T(8,128)(2,1)} %key_ref.1, bf16[8192,512]{1,0:T(8,128)(2,1)} %value_ref.1), custom_call_target="tpu_custom_call" | custom-call | flops 4294967296 | bytes 16777216 | tf_op jit(solution)/shard_map/project/pallas_call | solution.py:191
  27.4 1.3 %collective-permute-start.5 = (bf16[512,512]{1,0:T(8,128)(2,1)}, bf16[512,512]{1,0:T(8,128)(2,1)S(1)}, u32[]{:S(2)}, u32[]{:S(2)}) collective-permute-start(bf16[512,512]{1,0:T(8,128)(2,1)} %project.1.refs_0_), channel_id=1, source_target_pairs={{0,2},{1,3},{2,0},{3,1},{4,6},{5,7},{8,10},{9,11},{12,14},{13,15},... | collective-permute-start | bytes 1572872 | tf_op jit(solution)/shard_map/ppermute | solution.py:417
  28.7 1.3 %collective-permute-start = (bf16[512,512]{1,0:T(8,128)(2,1)}, bf16[512,512]{1,0:T(8,128)(2,1)S(1)}, u32[]{:S(2)}, u32[]{:S(2)}) collective-permute-start(bf16[512,512]{1,0:T(8,128)(2,1)} %project.1.refs_0_), channel_id=1, source_target_pairs={{0,4},{1,5},{2,6},{3,7},{4,8},{5,9},{6,10},{7,11},{8,12},{9,13},{1... | collective-permute-start | bytes 1572872 | tf_op jit(solution)/shard_map/ppermute | solution.py:417
  30.0 0.0 collective-permute-done.1.refs_1_
  30.0 0.0 copy-start.2
  30.1 1.3 %collective-permute-start.2 = (bf16[512,512]{1,0:T(8,128)(2,1)S(1)}, bf16[512,512]{1,0:T(8,128)(2,1)S(1)}, u32[]{:S(2)}, u32[]{:S(2)}) collective-permute-start(bf16[512,512]{1,0:T(8,128)(2,1)S(1)} %collective-permute-done.1.refs_1_), channel_id=1, source_target_pairs={{4,8},{5,9},{6,10},{7,11},{8,12},{9,13},{10,14},{11,15},{20,24},{2... | collective-permute-start | bytes 1572872 | tf_op jit(solution)/shard_map/ppermute | solution.py:417
  31.4 0.0 collective-permute-done.7.refs_4_
  31.4 0.0 copy-start.3
  31.4 2.9 %collective-permute-start.8 = (bf16[512,512]{1,0:T(8,128)(2,1)S(1)}, bf16[512,512]{1,0:T(8,128)(2,1)S(1)}, u32[]{:S(2)}, u32[]{:S(2)}) collective-permute-start(bf16[512,512]{1,0:T(8,128)(2,1)S(1)} %collective-permute-done.1.refs_1_), channel_id=1, source_target_pairs={{4,6},{5,7},{6,4},{7,5},{8,10},{9,11},{10,8},{11,9},{12,14},{13,15... | collective-permute-start | bytes 1572872 | tf_op jit(solution)/shard_map/ppermute | solution.py:417
  34.3 7.1 %collective-permute-done.5.refs_4_ = bf16[512,512]{1,0:T(8,128)(2,1)S(1)} collective-permute-done((bf16[512,512]{1,0:T(8,128)(2,1)}, bf16[512,512]{1,0:T(8,128)(2,1)S(1)}, u32[]{:S(2)}, u32[]{:S(2)}) %collective-permute-start.5) | collective-permute-done | bytes 524320 | tf_op jit(solution)/shard_map/ppermute | solution.py:417
  41.3 0.0 copy-start
  41.3 5.0 %collective-permute-done.refs_1_ = bf16[512,512]{1,0:T(8,128)(2,1)S(1)} collective-permute-done((bf16[512,512]{1,0:T(8,128)(2,1)}, bf16[512,512]{1,0:T(8,128)(2,1)S(1)}, u32[]{:S(2)}, u32[]{:S(2)}) %collective-permute-start) | collective-permute-done | bytes 524320 | tf_op jit(solution)/shard_map/ppermute | solution.py:417
  46.3 1.9 %collective-permute-start.6 = (bf16[512,512]{1,0:T(8,128)(2,1)S(1)}, bf16[512,512]{1,0:T(8,128)(2,1)S(1)}, u32[]{:S(2)}, u32[]{:S(2)}) collective-permute-start(bf16[512,512]{1,0:T(8,128)(2,1)S(1)} %collective-permute-done.refs_1_), channel_id=1, source_target_pairs={{4,6},{5,7},{6,4},{7,5},{8,10},{9,11},{10,8},{11,9},{12,14},{13,15... | collective-permute-start | bytes 1572872 | tf_op jit(solution)/shard_map/ppermute | solution.py:417
  48.2 7.8 %collective-permute-done.2.refs_2_ = bf16[512,512]{1,0:T(8,128)(2,1)S(1)} collective-permute-done((bf16[512,512]{1,0:T(8,128)(2,1)S(1)}, bf16[512,512]{1,0:T(8,128)(2,1)S(1)}, u32[]{:S(2)}, u32[]{:S(2)}) %collective-permute-start.2) | collective-permute-done | bytes 524320 | tf_op jit(solution)/shard_map/ppermute | solution.py:417
  56.1 1.3 %collective-permute-start.11 = (bf16[512,512]{1,0:T(8,128)(2,1)S(1)}, bf16[512,512]{1,0:T(8,128)(2,1)}, u32[]{:S(2)}, u32[]{:S(2)}) collective-permute-start(bf16[512,512]{1,0:T(8,128)(2,1)S(1)} %collective-permute-done.2.refs_2_), channel_id=1, source_target_pairs={{8,12},{9,13},{10,14},{11,15},{24,28},{25,29},{26,30},{27,31}} | collective-permute-start | bytes 1572872 | tf_op jit(solution)/shard_map/ppermute | solution.py:417
  57.4 1.3 %collective-permute-start.3 = (bf16[512,512]{1,0:T(8,128)(2,1)S(1)}, bf16[512,512]{1,0:T(8,128)(2,1)}, u32[]{:S(2)}, u32[]{:S(2)}) collective-permute-start(bf16[512,512]{1,0:T(8,128)(2,1)S(1)} %collective-permute-done.refs_1_), channel_id=1, source_target_pairs={{4,8},{5,9},{6,10},{7,11},{8,12},{9,13},{10,14},{11,15},{20,24},{2... | collective-permute-start | bytes 1572872 | tf_op jit(solution)/shard_map/ppermute | solution.py:417
  58.7 0.0 collective-permute-done.8.refs_5_
  58.7 0.0 copy-start.6
  58.7 1.9 %collective-permute-start.9 = (bf16[512,512]{1,0:T(8,128)(2,1)S(1)}, bf16[512,512]{1,0:T(8,128)(2,1)S(1)}, u32[]{:S(2)}, u32[]{:S(2)}) collective-permute-start(bf16[512,512]{1,0:T(8,128)(2,1)S(1)} %collective-permute-done.2.refs_2_), channel_id=1, source_target_pairs={{8,10},{9,11},{10,8},{11,9},{12,14},{13,15},{14,12},{15,13},{24,26... | collective-permute-start | bytes 1572872 | tf_op jit(solution)/shard_map/ppermute | solution.py:417
  60.6 3.1 %collective-permute-done.6.refs_5_ = bf16[512,512]{1,0:T(8,128)(2,1)S(1)} collective-permute-done((bf16[512,512]{1,0:T(8,128)(2,1)S(1)}, bf16[512,512]{1,0:T(8,128)(2,1)S(1)}, u32[]{:S(2)}, u32[]{:S(2)}) %collective-permute-start.6) | collective-permute-done | bytes 524320 | tf_op jit(solution)/shard_map/ppermute | solution.py:417
  63.7 9.2 %collective-permute-done.11.refs_3_ = bf16[512,512]{1,0:T(8,128)(2,1)} collective-permute-done((bf16[512,512]{1,0:T(8,128)(2,1)S(1)}, bf16[512,512]{1,0:T(8,128)(2,1)}, u32[]{:S(2)}, u32[]{:S(2)}) %collective-permute-start.11) | collective-permute-done | bytes 524320 | tf_op jit(solution)/shard_map/ppermute | solution.py:417
  72.9 1.9 %collective-permute-start.13 = (bf16[512,512]{1,0:T(8,128)(2,1)}, bf16[512,512]{1,0:T(8,128)(2,1)}, u32[]{:S(2)}, u32[]{:S(2)}) collective-permute-start(bf16[512,512]{1,0:T(8,128)(2,1)} %collective-permute-done.11.refs_3_), channel_id=1, source_target_pairs={{12,14},{13,15},{14,12},{15,13},{28,30},{29,31},{30,28},{31,29}} | collective-permute-start | bytes 1572872 | tf_op jit(solution)/shard_map/ppermute | solution.py:417
  74.8 6.9 %collective-permute-done.3.refs_2_ = bf16[512,512]{1,0:T(8,128)(2,1)} collective-permute-done((bf16[512,512]{1,0:T(8,128)(2,1)S(1)}, bf16[512,512]{1,0:T(8,128)(2,1)}, u32[]{:S(2)}, u32[]{:S(2)}) %collective-permute-start.3) | collective-permute-done | bytes 524320 | tf_op jit(solution)/shard_map/ppermute | solution.py:417
  81.8 1.3 %collective-permute-start.4 = (bf16[512,512]{1,0:T(8,128)(2,1)}, bf16[512,512]{1,0:T(8,128)(2,1)}, u32[]{:S(2)}, u32[]{:S(2)}) collective-permute-start(bf16[512,512]{1,0:T(8,128)(2,1)} %collective-permute-done.3.refs_2_), channel_id=1, source_target_pairs={{8,12},{9,13},{10,14},{11,15},{24,28},{25,29},{26,30},{27,31}} | collective-permute-start | bytes 1572872 | tf_op jit(solution)/shard_map/ppermute | solution.py:417
  83.1 0.0 collective-permute-done.9.refs_6_
  83.1 0.0 copy-done.6
  83.1 0.0 copy-start.7
  83.1 1.9 %collective-permute-start.10 = (bf16[512,512]{1,0:T(8,128)(2,1)}, bf16[512,512]{1,0:T(8,128)(2,1)}, u32[]{:S(2)}, u32[]{:S(2)}) collective-permute-start(bf16[512,512]{1,0:T(8,128)(2,1)} %collective-permute-done.3.refs_2_), channel_id=1, source_target_pairs={{8,10},{9,11},{10,8},{11,9},{12,14},{13,15},{14,12},{15,13},{24,26... | collective-permute-start | bytes 1572872 | tf_op jit(solution)/shard_map/ppermute | solution.py:417
  85.0 0.0 copy-done.7
  85.0 1.3 %collective-permute-start.12 = (bf16[512,512]{1,0:T(8,128)(2,1)S(1)}, bf16[512,512]{1,0:T(8,128)(2,1)}, u32[]{:S(2)}, u32[]{:S(2)}) collective-permute-start(bf16[512,512]{1,0:T(8,128)(2,1)S(1)} %collective-permute-done.5.refs_4_), channel_id=1, source_target_pairs={{0,12},{1,13},{2,14},{3,15},{16,28},{17,29},{18,30},{19,31}} | collective-permute-start | bytes 1572872 | tf_op jit(solution)/shard_map/ppermute | solution.py:417
  86.4 0.0 copy-done.8
  86.4 0.6 fusion.1.slot_ref
  87.0 0.6 collective-permute-done.13.refs_7_
  87.5 0.0 copy-done.2
  87.5 0.0 copy-done.3
  87.5 0.0 copy-done.5
  87.5 12.1 %attention.2.refs_8_ = bf16[512,4096]{1,0:T(8,128)(2,1)} custom-call(s32[8,7]{1,0:T(8,128)} %fusion.1.slot_ref, s32[8,7]{1,0:T(8,128)} %cut_ref.3, s32[1]{0:T(128)} %bitcast.odd_ref, bf16[512,4096]{1,0:T(8,128)(2,1)} %q_hbm.3, bf16[512,512]{1,0:T(8,128)(2,1)} %get-tuple-element.18.refs_0_, bf16[512,512]{1,0:T(8,128)(2,1)} %copy-done.2, ...), custom_call_target="tpu_custom_call" | custom-call | flops 2147483648 | bytes 8388608 | tf_op jit(solution)/shard_map/attention/pallas_call | solution.py:354
  99.7 7.1 %collective-permute-done.4.refs_3_ = bf16[512,512]{1,0:T(8,128)(2,1)} collective-permute-done((bf16[512,512]{1,0:T(8,128)(2,1)}, bf16[512,512]{1,0:T(8,128)(2,1)}, u32[]{:S(2)}, u32[]{:S(2)}) %collective-permute-start.4) | collective-permute-done | bytes 524320 | tf_op jit(solution)/shard_map/ppermute | solution.py:417
  106.8 0.0 collective-permute-done.10.refs_6_
  106.8 0.0 collective-permute-done.12.refs_7_
  106.8 0.0 copy-done
  106.8 0.0 copy-done.1
  106.8 0.0 copy-done.4
  106.8 12.2 %attention.3 = bf16[512,4096]{1,0:T(8,128)(2,1)} custom-call(s32[8,7]{1,0:T(8,128)} %fusion.1.slot_ref, s32[8,7]{1,0:T(8,128)} %cut_ref.3, s32[1]{0:T(128)} %bitcast.odd_ref, bf16[512,4096]{1,0:T(8,128)(2,1)} %q_hbm.3, bf16[512,512]{1,0:T(8,128)(2,1)} %project.1.refs_0_, bf16[512,512]{1,0:T(8,128)(2,1)} %copy-done.1, ...), custom_call_target="tpu_custom_call", output_to_operand_aliasing={{}: (12, {})} | custom-call | flops 2147483648 | bytes 8388608 | tf_op jit(solution)/shard_map/attention/pallas_call | solution.py:354
  (3 shorter events, 0.0 us)
Async XLA Ops:
  13.3 16.7 %collective-permute-start.1 = (bf16[512,512]{1,0:T(8,128)(2,1)}, bf16[512,512]{1,0:T(8,128)(2,1)S(1)}, u32[]{:S(2)}, u32[]{:S(2)}) collective-permute-start(bf16[512,512]{1,0:T(8,128)(2,1)} %get-tuple-element.18.refs_0_), channel_id=1, source_target_pairs={{0,4},{1,5},{2,6},{3,7},{4,8},{5,9},{6,10},{7,11},{8,12},{9,13},{1... | collective-permute-start | bytes 1572872 | tf_op jit(solution)/shard_map/ppermute | solution.py:417
  14.6 16.8 %collective-permute-start.7 = (bf16[512,512]{1,0:T(8,128)(2,1)}, bf16[512,512]{1,0:T(8,128)(2,1)S(1)}, u32[]{:S(2)}, u32[]{:S(2)}) collective-permute-start(bf16[512,512]{1,0:T(8,128)(2,1)} %get-tuple-element.18.refs_0_), channel_id=1, source_target_pairs={{0,2},{1,3},{4,6},{5,7},{8,10},{9,11},{12,14},{13,15},{16,18},{17,... | collective-permute-start | bytes 1572872 | tf_op jit(solution)/shard_map/ppermute | solution.py:417
  18.1 68.3 %copy-start.8 = (s32[8,7]{1,0:T(8,128)S(1)}, s32[8,7]{1,0:T(8,128)}, u32[]{:S(2)}) copy-start(s32[8,7]{1,0:T(8,128)} %param.12) | copy-start | bytes 676
  27.4 13.9 %collective-permute-start.5 = (bf16[512,512]{1,0:T(8,128)(2,1)}, bf16[512,512]{1,0:T(8,128)(2,1)S(1)}, u32[]{:S(2)}, u32[]{:S(2)}) collective-permute-start(bf16[512,512]{1,0:T(8,128)(2,1)} %project.1.refs_0_), channel_id=1, source_target_pairs={{0,2},{1,3},{2,0},{3,1},{4,6},{5,7},{8,10},{9,11},{12,14},{13,15},... | collective-permute-start | bytes 1572872 | tf_op jit(solution)/shard_map/ppermute | solution.py:417
  28.7 17.6 %collective-permute-start = (bf16[512,512]{1,0:T(8,128)(2,1)}, bf16[512,512]{1,0:T(8,128)(2,1)S(1)}, u32[]{:S(2)}, u32[]{:S(2)}) collective-permute-start(bf16[512,512]{1,0:T(8,128)(2,1)} %project.1.refs_0_), channel_id=1, source_target_pairs={{0,4},{1,5},{2,6},{3,7},{4,8},{5,9},{6,10},{7,11},{8,12},{9,13},{1... | collective-permute-start | bytes 1572872 | tf_op jit(solution)/shard_map/ppermute | solution.py:417
  30.0 57.5 %copy-start.2 = (bf16[512,512]{1,0:T(8,128)(2,1)}, bf16[512,512]{1,0:T(8,128)(2,1)S(1)}, u32[]{:S(2)}) copy-start(bf16[512,512]{1,0:T(8,128)(2,1)S(1)} %collective-permute-done.1.refs_1_) | copy-start | bytes 1572868
  30.1 26.0 %collective-permute-start.2 = (bf16[512,512]{1,0:T(8,128)(2,1)S(1)}, bf16[512,512]{1,0:T(8,128)(2,1)S(1)}, u32[]{:S(2)}, u32[]{:S(2)}) collective-permute-start(bf16[512,512]{1,0:T(8,128)(2,1)S(1)} %collective-permute-done.1.refs_1_), channel_id=1, source_target_pairs={{4,8},{5,9},{6,10},{7,11},{8,12},{9,13},{10,14},{11,15},{20,24},{2... | collective-permute-start | bytes 1572872 | tf_op jit(solution)/shard_map/ppermute | solution.py:417
  31.4 56.2 %copy-start.3 = (bf16[512,512]{1,0:T(8,128)(2,1)}, bf16[512,512]{1,0:T(8,128)(2,1)S(1)}, u32[]{:S(2)}) copy-start(bf16[512,512]{1,0:T(8,128)(2,1)S(1)} %collective-permute-done.7.refs_4_) | copy-start | bytes 1572868
  31.4 27.3 %collective-permute-start.8 = (bf16[512,512]{1,0:T(8,128)(2,1)S(1)}, bf16[512,512]{1,0:T(8,128)(2,1)S(1)}, u32[]{:S(2)}, u32[]{:S(2)}) collective-permute-start(bf16[512,512]{1,0:T(8,128)(2,1)S(1)} %collective-permute-done.1.refs_1_), channel_id=1, source_target_pairs={{4,6},{5,7},{6,4},{7,5},{8,10},{9,11},{10,8},{11,9},{12,14},{13,15... | collective-permute-start | bytes 1572872 | tf_op jit(solution)/shard_map/ppermute | solution.py:417
  41.3 65.4 %copy-start = (bf16[512,512]{1,0:T(8,128)(2,1)}, bf16[512,512]{1,0:T(8,128)(2,1)S(1)}, u32[]{:S(2)}) copy-start(bf16[512,512]{1,0:T(8,128)(2,1)S(1)} %collective-permute-done.5.refs_4_) | copy-start | bytes 1572868
  46.3 60.5 %copy-start.1 = (bf16[512,512]{1,0:T(8,128)(2,1)}, bf16[512,512]{1,0:T(8,128)(2,1)S(1)}, u32[]{:S(2)}) copy-start(bf16[512,512]{1,0:T(8,128)(2,1)S(1)} %collective-permute-done.refs_1_) | copy-start | bytes 1572868
  46.3 17.4 %collective-permute-start.6 = (bf16[512,512]{1,0:T(8,128)(2,1)S(1)}, bf16[512,512]{1,0:T(8,128)(2,1)S(1)}, u32[]{:S(2)}, u32[]{:S(2)}) collective-permute-start(bf16[512,512]{1,0:T(8,128)(2,1)S(1)} %collective-permute-done.refs_1_), channel_id=1, source_target_pairs={{4,6},{5,7},{6,4},{7,5},{8,10},{9,11},{10,8},{11,9},{12,14},{13,15... | collective-permute-start | bytes 1572872 | tf_op jit(solution)/shard_map/ppermute | solution.py:417
  56.1 31.5 %copy-start.5 = (bf16[512,512]{1,0:T(8,128)(2,1)}, bf16[512,512]{1,0:T(8,128)(2,1)S(1)}, u32[]{:S(2)}) copy-start(bf16[512,512]{1,0:T(8,128)(2,1)S(1)} %collective-permute-done.2.refs_2_) | copy-start | bytes 1572868
  56.1 16.8 %collective-permute-start.11 = (bf16[512,512]{1,0:T(8,128)(2,1)S(1)}, bf16[512,512]{1,0:T(8,128)(2,1)}, u32[]{:S(2)}, u32[]{:S(2)}) collective-permute-start(bf16[512,512]{1,0:T(8,128)(2,1)S(1)} %collective-permute-done.2.refs_2_), channel_id=1, source_target_pairs={{8,12},{9,13},{10,14},{11,15},{24,28},{25,29},{26,30},{27,31}} | collective-permute-start | bytes 1572872 | tf_op jit(solution)/shard_map/ppermute | solution.py:417
  57.4 24.4 %collective-permute-start.3 = (bf16[512,512]{1,0:T(8,128)(2,1)S(1)}, bf16[512,512]{1,0:T(8,128)(2,1)}, u32[]{:S(2)}, u32[]{:S(2)}) collective-permute-start(bf16[512,512]{1,0:T(8,128)(2,1)S(1)} %collective-permute-done.refs_1_), channel_id=1, source_target_pairs={{4,8},{5,9},{6,10},{7,11},{8,12},{9,13},{10,14},{11,15},{20,24},{2... | collective-permute-start | bytes 1572872 | tf_op jit(solution)/shard_map/ppermute | solution.py:417
  58.7 24.4 %copy-start.6 = (bf16[512,512]{1,0:T(8,128)(2,1)}, bf16[512,512]{1,0:T(8,128)(2,1)S(1)}, u32[]{:S(2)}) copy-start(bf16[512,512]{1,0:T(8,128)(2,1)S(1)} %collective-permute-done.8.refs_5_) | copy-start | bytes 1572868
  58.7 24.4 %collective-permute-start.9 = (bf16[512,512]{1,0:T(8,128)(2,1)S(1)}, bf16[512,512]{1,0:T(8,128)(2,1)S(1)}, u32[]{:S(2)}, u32[]{:S(2)}) collective-permute-start(bf16[512,512]{1,0:T(8,128)(2,1)S(1)} %collective-permute-done.2.refs_2_), channel_id=1, source_target_pairs={{8,10},{9,11},{10,8},{11,9},{12,14},{13,15},{14,12},{15,13},{24,26... | collective-permute-start | bytes 1572872 | tf_op jit(solution)/shard_map/ppermute | solution.py:417
  63.7 43.1 %copy-start.4 = (bf16[512,512]{1,0:T(8,128)(2,1)}, bf16[512,512]{1,0:T(8,128)(2,1)S(1)}, u32[]{:S(2)}) copy-start(bf16[512,512]{1,0:T(8,128)(2,1)S(1)} %collective-permute-done.6.refs_5_) | copy-start | bytes 1572868
  72.9 14.6 %collective-permute-start.13 = (bf16[512,512]{1,0:T(8,128)(2,1)}, bf16[512,512]{1,0:T(8,128)(2,1)}, u32[]{:S(2)}, u32[]{:S(2)}) collective-permute-start(bf16[512,512]{1,0:T(8,128)(2,1)} %collective-permute-done.11.refs_3_), channel_id=1, source_target_pairs={{12,14},{13,15},{14,12},{15,13},{28,30},{29,31},{30,28},{31,29}} | collective-permute-start | bytes 1572872 | tf_op jit(solution)/shard_map/ppermute | solution.py:417
  81.8 25.0 %collective-permute-start.4 = (bf16[512,512]{1,0:T(8,128)(2,1)}, bf16[512,512]{1,0:T(8,128)(2,1)}, u32[]{:S(2)}, u32[]{:S(2)}) collective-permute-start(bf16[512,512]{1,0:T(8,128)(2,1)} %collective-permute-done.3.refs_2_), channel_id=1, source_target_pairs={{8,12},{9,13},{10,14},{11,15},{24,28},{25,29},{26,30},{27,31}} | collective-permute-start | bytes 1572872 | tf_op jit(solution)/shard_map/ppermute | solution.py:417
  83.1 1.9 %copy-start.7 = (bf16[512,512]{1,0:T(8,128)(2,1)}, bf16[512,512]{1,0:T(8,128)(2,1)S(1)}, u32[]{:S(2)}) copy-start(bf16[512,512]{1,0:T(8,128)(2,1)S(1)} %collective-permute-done.9.refs_6_) | copy-start | bytes 1572868
  83.1 23.7 %collective-permute-start.10 = (bf16[512,512]{1,0:T(8,128)(2,1)}, bf16[512,512]{1,0:T(8,128)(2,1)}, u32[]{:S(2)}, u32[]{:S(2)}) collective-permute-start(bf16[512,512]{1,0:T(8,128)(2,1)} %collective-permute-done.3.refs_2_), channel_id=1, source_target_pairs={{8,10},{9,11},{10,8},{11,9},{12,14},{13,15},{14,12},{15,13},{24,26... | collective-permute-start | bytes 1572872 | tf_op jit(solution)/shard_map/ppermute | solution.py:417
  85.0 21.7 %collective-permute-start.12 = (bf16[512,512]{1,0:T(8,128)(2,1)S(1)}, bf16[512,512]{1,0:T(8,128)(2,1)}, u32[]{:S(2)}, u32[]{:S(2)}) collective-permute-start(bf16[512,512]{1,0:T(8,128)(2,1)S(1)} %collective-permute-done.5.refs_4_), channel_id=1, source_target_pairs={{0,12},{1,13},{2,14},{3,15},{16,28},{17,29},{18,30},{19,31}} | collective-permute-start | bytes 1572872 | tf_op jit(solution)/shard_map/ppermute | solution.py:417

commit v11 on v7

--- a/solution.py
+++ b/solution.py
@@ -17,9 +17,27 @@
 BLOCKS_PER_STEP = 4
 
 
+PLAN = (
+    ("across", 0, 0, ()),
+    ("along", 1, 0, ()),
+    ("across", 0, 1, ()),
+    ("along", 1, 1, (("across", 0, 0),)),
+    ("along", 2, 0, (("across", 0, 0),)),
+    ("across", 1, 0, ()),
+    ("across", 1, 1, (("across", 1, 0),)),
+    ("direct", 3, 0, (("across", 0, 0),)),
+    ("across", 2, 0, (("across", 1, 0),)),
+    ("along", 2, 1, (("across", 2, 0), ("across", 0, 1), ("along", 1, 1))),
+    ("across", 3, 0, ()),
+    ("across", 2, 1, (("along", 1, 1), ("across", 1, 1))),
+    ("down", 3, 1, (("across", 0, 0),)),
+    ("along", 3, 1, (("across", 0, 1),)),
+)
+
+
 def norm_project_kernel(
-    x_hbm, gain_ref, key_hbm, value_hbm, normed_hbm, kv_ref,
-    x_scr, weight_scr, even_scr, odd_scr, acc_scr, scale_scr, x_sem, key_sem, value_sem, normed_sem,
+    x_hbm, gain_ref, key_hbm, value_hbm, scale_ref, kv_ref,
+    x_scr, weight_scr, even_scr, odd_scr, acc_scr, x_sem, key_sem, value_sem,
 ):
     loads, rows, chunk = x_scr.shape
     width = weight_scr.shape[2] // 2
@@ -43,14 +61,9 @@
             ),
         ]
 
-    def store_normed(normed_scr, c):
-        return pltpu.make_async_copy(
-            normed_scr.at[c // 2], normed_hbm.at[:, span(c)], normed_sem.at[c]
-        )
-
     for c in range(loads):
         load_x(c).start()
-    scale_scr[...] = jnp.zeros_like(scale_scr)
+    scale_ref[...] = jnp.zeros_like(scale_ref)
 
     def square(c, carry):
         load_x(c).wait()
@@ -63,56 +76,59 @@
 
         for first in range(0, rows, band):
             row = slice(first, first + band)
-            total = scale_scr[row, :]
+            total = scale_ref[row, :]
             for lane in range(0, chunk, lanes):
                 x = x_scr[c, row, lane : lane + lanes].astype(jnp.float32)
                 total += x * x
-            scale_scr[row, :] = total
+            scale_ref[row, :] = total
         return carry
 
     lax.fori_loop(0, loads, square, 0)
-    mean_sq = jnp.sum(scale_scr[...], axis=-1, keepdims=True) / (loads * chunk)
-    scale_scr[...] = jnp.broadcast_to(lax.rsqrt(mean_sq + EPS), scale_scr.shape)
-
-    def normalise(normed_scr, c):
+    mean_sq = jnp.sum(scale_ref[...], axis=-1, keepdims=True) / (loads * chunk)
+    scale_ref[...] = jnp.broadcast_to(lax.rsqrt(mean_sq + EPS), scale_ref.shape)
+
+    def normalise(normed_scr, c, first_lane=0, last_lane=chunk):
         for first in range(0, rows, band):
             row = slice(first, first + band)
-            inverse = scale_scr[row, :]
-            for lane in range(0, chunk, lanes):
+            inverse = scale_ref[row, :]
+            for lane in range(first_lane, last_lane, lanes):
                 cols = slice(lane, lane + lanes)
                 x = x_scr[c, row, cols].astype(jnp.float32)
                 gain = gain_ref[c, :, cols]
-                normed_scr[c // 2, row, cols] = (x * inverse * gain).astype(jnp.bfloat16)
-
-    def multiply(normed_scr, c):
+                normed_scr[row, cols] = (x * inverse * gain).astype(jnp.bfloat16)
+
+    def multiply(normed_scr, c, later_scr):
         for copy in load_weights(c):
             copy.wait()
-        store_normed(normed_scr, c).start()
-        acc_scr[...] += jnp.dot(
-            normed_scr[c // 2], weight_scr[c], preferred_element_type=jnp.float32
-        )
+        for part in range(2):
+            cols = slice(part * width, (part + 1) * width)
+            acc_scr[:, cols] += jnp.dot(
+                normed_scr[...], weight_scr[c, :, cols], preferred_element_type=jnp.float32
+            )
+            if later_scr is not None:
+                normalise(later_scr, c + 1, part * chunk // 2, (part + 1) * chunk // 2)
 
     normalise(even_scr, 0)
     acc_scr[...] = jnp.zeros_like(acc_scr)
 
     def pair(p, carry):
-        multiply(even_scr, 2 * p)
-        normalise(odd_scr, 2 * p + 1)
-        multiply(odd_scr, 2 * p + 1)
-        normalise(even_scr, 2 * p + 2)
+        multiply(even_scr, 2 * p, odd_scr)
+        multiply(odd_scr, 2 * p + 1, even_scr)
         return carry
 
     lax.fori_loop(0, loads // 2 - 1, pair, 0)
-    multiply(even_scr, loads - 2)
-    normalise(odd_scr, loads - 1)
-    multiply(odd_scr, loads - 1)
+    multiply(even_scr, loads - 2, odd_scr)
+    multiply(odd_scr, loads - 1, None)
+    write_heads(kv_ref, acc_scr)
+
+
+def write_heads(kv_ref, acc_scr):
+    width = kv_ref.shape[1] // 2
     for head in range(width // HEAD_DIM):
         for part in range(2):
             source = slice(part * width + head * HEAD_DIM, part * width + (head + 1) * HEAD_DIM)
             target = slice((2 * head + part) * HEAD_DIM, (2 * head + part + 1) * HEAD_DIM)
             kv_ref[:, target] = acc_scr[:, source].astype(jnp.bfloat16)
-    for c in range(loads):
-        store_normed(odd_scr if c % 2 else even_scr, c).wait()
 
 
 def norm_project(hidden, gain, key_weight, value_weight):
@@ -124,35 +140,41 @@
     return pl.pallas_call(
         norm_project_kernel,
         in_specs=[held, whole, held, held],
-        out_specs=[held, whole],
+        out_specs=[whole, whole],
         out_shape=[
-            jax.ShapeDtypeStruct((rows, features), jnp.bfloat16),
+            jax.ShapeDtypeStruct((rows, 128), jnp.float32),
             jax.ShapeDtypeStruct((rows, 2 * width), jnp.bfloat16),
         ],
         scratch_shapes=[
             pltpu.VMEM((LOADS, rows, chunk), jnp.bfloat16),
             pltpu.VMEM((LOADS, chunk, 2 * width), jnp.bfloat16),
-            pltpu.VMEM((LOADS // 2, rows, chunk), jnp.bfloat16),
-            pltpu.VMEM((LOADS // 2, rows, chunk), jnp.bfloat16),
+            pltpu.VMEM((rows, chunk), jnp.bfloat16),
+            pltpu.VMEM((rows, chunk), jnp.bfloat16),
             pltpu.VMEM((rows, 2 * width), jnp.float32),
-            pltpu.VMEM((rows, 128), jnp.float32),
-            pltpu.SemaphoreType.DMA((LOADS,)),
             pltpu.SemaphoreType.DMA((LOADS,)),
             pltpu.SemaphoreType.DMA((LOADS,)),
             pltpu.SemaphoreType.DMA((LOADS,)),
         ],
         compiler_params=pltpu.CompilerParams(vmem_limit_bytes=57 * MIB),
         cost_estimate=pl.CostEstimate(
-            flops=4 * rows * features * width, bytes_accessed=24 * MIB, transcendentals=0
+            flops=4 * rows * features * width, bytes_accessed=16 * MIB, transcendentals=0
         ),
         name="norm_project",
     )(hidden, gain.reshape(LOADS, 1, chunk), key_weight, value_weight)
 
 
-def project_kernel(normed_ref, key_ref, value_ref, kv_ref, acc_scr):
+def project_kernel(x_ref, scale_ref, gain_ref, key_ref, value_ref, kv_ref, acc_scr):
     step = pl.program_id(0)
+    rows, chunk = x_ref.shape
     width = key_ref.shape[1]
-    normed = normed_ref[...]
+    lanes = 128
+    inverse = scale_ref[...]
+    parts = []
+    for lane in range(0, chunk, lanes):
+        cols = slice(lane, lane + lanes)
+        x = x_ref[:, cols].astype(jnp.float32)
+        parts.append((x * inverse * gain_ref[:, cols]).astype(jnp.bfloat16))
+    normed = jnp.concatenate(parts, axis=1)
     for part, weight in enumerate((key_ref, value_ref)):
         cols = slice(part * width, (part + 1) * width)
         term = jnp.dot(normed, weight[...], preferred_element_type=jnp.float32)
@@ -160,22 +182,24 @@
 
     @pl.when(step == CHUNKS - 1)
     def _():
-        for head in range(width // HEAD_DIM):
-            for part in range(2):
-                source = slice(part * width + head * HEAD_DIM, part * width + (head + 1) * HEAD_DIM)
-                target = slice((2 * head + part) * HEAD_DIM, (2 * head + part + 1) * HEAD_DIM)
-                kv_ref[:, target] = acc_scr[:, source].astype(jnp.bfloat16)
-
-
-def project(normed, key_weight, value_weight, unit):
-    rows, features = normed.shape
+        write_heads(kv_ref, acc_scr)
+
+
+def project(hidden, scale, gain, key_weight, value_weight, unit):
+    rows, features = hidden.shape
     chunk = features // CHUNKS
     width = key_weight.shape[1] // UNITS
     weight = pl.BlockSpec((chunk, width), lambda i: (i, unit))
     return pl.pallas_call(
         project_kernel,
         grid=(CHUNKS,),
-        in_specs=[pl.BlockSpec((rows, chunk), lambda i: (0, i)), weight, weight],
+        in_specs=[
+            pl.BlockSpec((rows, chunk), lambda i: (0, i)),
+            pl.BlockSpec(scale.shape, lambda i: (0, 0)),
+            pl.BlockSpec((1, chunk), lambda i: (0, i)),
+            weight,
+            weight,
+        ],
         out_specs=pl.BlockSpec((rows, 2 * width), lambda i: (0, 0)),
         out_shape=jax.ShapeDtypeStruct((rows, 2 * width), jnp.bfloat16),
         scratch_shapes=[pltpu.VMEM((rows, 2 * width), jnp.float32)],
@@ -184,7 +208,7 @@
             flops=4 * rows * features * width, bytes_accessed=16 * MIB, transcendentals=0
         ),
         name="project",
-    )(normed, key_weight, value_weight)
+    )(hidden, scale, gain.reshape(1, features), key_weight, value_weight)
 
 
 def attention_kernel(block, near, slot_ref, cut_ref, odd_ref, q_ref, *refs):
@@ -265,13 +289,13 @@
                 r * block : (r + 1) * block
             ]
 
-    waiting = None
+    waiting = []
     for local in range(BLOCKS_PER_STEP):
-        scores, values = score(local)
-        if waiting is not None:
-            finish(*waiting)
-        waiting = (local, scores, values)
-    finish(*waiting)
+        waiting.append((local, *score(local)))
+        if len(waiting) > 2:
+            finish(*waiting.pop(0))
+    for item in waiting:
+        finish(*item)
 
 
 def attention(slots, cuts, odd, queries, own, straight, crossed, unit, previous):
@@ -329,51 +353,35 @@
     odd = (lax.axis_index("node") // chains % 2).astype(jnp.int32).reshape(1)
     slots = jnp.where(anc_ids >= 0, anc_ids % blocks, 0)
 
-    normed, first = norm_project(hidden, norm_gain, key_weight, value_weight)
-    own = [first] + [project(normed, key_weight, value_weight, unit) for unit in range(1, UNITS)]
+    scale, first = norm_project(hidden, norm_gain, key_weight, value_weight)
+    own = [first, project(hidden, scale, norm_gain, key_weight, value_weight, 1)]
     def after(array, *earlier):
         return lax.optimization_barrier((array, *earlier))[0]
 
-    straight = [{} for _ in range(UNITS)]
-    crossed = [{} for _ in range(UNITS)]
-
-    def step_across(s, unit, settled):
-        source = own[unit] if s == 0 else straight[unit][s]
-        both_ways = unit == UNITS - 1 and s == 0
-        pairs = [
-            (i, other[i])
-            for i in range(size)
-            if half[i] >= s and (s > 0 or even[i] or (both_ways and half[i] == 0))
-        ]
-        crossed[unit][s] = lax.ppermute(after(source, *settled), "node", pairs)
-        return crossed[unit][s]
-
-    def step_along(s, unit, settled):
-        source = straight[unit][1] if s == 2 else own[unit]
-        shift = 2 * (1 if s == 2 else s) * chains
-        pairs = [(i, i + shift) for i in range(size - shift) if half[i] >= (s == 2)]
-        straight[unit][s] = lax.ppermute(after(source, *settled), "node", pairs)
-        return straight[unit][s]
-
-    def step_down(unit, settled):
-        shift = 2 * near * chains
-        pairs = [(i, i + shift) for i in range(size - shift)]
-        crossed[unit][near] = lax.ppermute(after(crossed[unit][0], *settled), "node", pairs)
-        return crossed[unit][near]
-
-    early, late = range(UNITS)
-    across = [(s, unit) for s in range(near - 1) for unit in (early, late)]
-    across += [(near - 1, early), (near, early), (near - 1, late)]
-    along = [(1, early), (1, late)]
-    along += [(s, early) for s in range(2, near + 1)] + [(2, late), None]
-    along += [(s, late) for s in range(3, near + 1)]
-    y_chain, z_chain = [], []
-    for (s, unit), step in zip(across, along, strict=True):
-        y_chain.append(step_across(s, unit, y_chain[-2:-1]))
-        if step is not None:
-            z_chain.append(step_along(*step, z_chain[-2:-1]))
+    column = 2 * chains
+    moved = {("own", 0, 0): own[0], ("own", 0, 1): own[1]}
+
+    def step(kind, s, unit, waits):
+        if kind == "across":
+            source = ("along", s, unit) if s else ("own", 0, unit)
+            exchange = s > 0 or unit == UNITS - 1
+            pairs = [
+                (i, other[i])
+                for i in range(size)
+                if half[i] >= s and (even[i] or (exchange and half[i] == 0) or s > 0)
+            ]
+        elif kind == "along":
+            source = ("along", s - 1, unit) if s > 1 else ("own", 0, unit)
+            pairs = [(i, i + column) for i in range(size - column) if half[i] >= s - 1]
         else:
-            z_chain.append(step_down(late, z_chain[-2:-1]))
+            source = ("across" if kind == "down" else "own", 0, unit)
+            pairs = [(i, i + s * column) for i in range(size - s * column)]
+        array = lax.optimization_barrier((moved[source], *[moved[w] for w in waits]))[0]
+        key = "along" if kind == "direct" else kind
+        moved[key, s, unit] = lax.ppermute(array, "node", pairs)
+
+    for kind, s, unit, waits in PLAN:
+        step(kind, s, unit, waits)
     result = None
     for unit in range(UNITS):
         result = attention(
@@ -382,8 +390,9 @@
             odd,
             queries,
             own[unit],
-            [straight[unit][s] for s in range(1, near + 1)],
-            [crossed[unit][s] for s in range(near + 1)],
+            [moved["along", s, unit] for s in range(1, near + 1)],
+            [moved["across", s, unit] for s in range(near)]
+            + [moved["across" if unit == 0 else "down", near, unit]],
             unit,
             result,
         )

time: 127 us -> 129 us (1.016)
  the two profiles are of different devices: /device:TPU:0 before, /device:TPU:16 now
where the time goes in v11:
time: 129 us; the launch traced here: 128 us
  waiting for transfers between devices  45.9 us (36%)
  Pallas kernels  44 us (34%)
  starting transfers between devices  36.7 us (28%)
    ppermute x14, waiting for transfers between devices, step(): moved[key, s, unit] = lax.ppermute(array, 'node', pairs)  45.9 us
    ppermute x14, starting transfers between devices, step(): moved[key, s, unit] = lax.ppermute(array, 'node', pairs)  36.7 us
    pallas_call x2, Pallas kernels, attention(): pl.pallas_call(functools.partial(attention_kernel, block, near), grid_spe...  21.4 us
    pallas_call x1, Pallas kernels, norm_project(): pl.pallas_call(norm_project_kernel, in_specs=[held, whole, held, held], o...  13.3 us
    pallas_call x1, Pallas kernels, project(): pl.pallas_call(project_kernel, grid=(CHUNKS,), in_specs=[pl.BlockSpec((ro...  9.4 us
  transfers between devices with their start and end apart: 14, of which 5 were waited for; matrix products, arithmetic and copies ran while one was open for 0% of the time, Pallas kernels for 16%

profile of v11, /device:TPU:16, one launch (start us, length us, event | category | flops | bytes accessed | tf_op | source)
XLA Modules:
  0.0 128.3 jit_solution(14634626062057113610)
XLA Ops:
  0.0 13.3 %norm_project.1 = (f32[512,128]{1,0:T(8,128)}, bf16[512,512]{1,0:T(8,128)(2,1)}) custom-call(bf16[512,8192]{1,0:T(8,128)(2,1)} %x_ref.1, f32[8,1,1024]{2,1,0:T(1,128)} %bitcast.3, bf16[8192,512]{1,0:T(8,128)(2,1)} %key_ref.1, bf16[8192,512]{1,0:T(8,128)(2,1)} %value_ref.1), custom_call_target="tpu_custom_call" | custom-call | flops 4294967296 | bytes 16777216 | tf_op jit(solution)/shard_map/norm_project/pallas_call | solution.py:140
  13.3 3.5 %collective-permute-start.2 = (bf16[512,512]{1,0:T(8,128)(2,1)}, bf16[512,512]{1,0:T(8,128)(2,1)S(1)}, u32[]{:S(2)}, u32[]{:S(2)}) collective-permute-start(bf16[512,512]{1,0:T(8,128)(2,1)} %get-tuple-element.26.refs_0_), channel_id=1, source_target_pairs={{0,4},{1,5},{2,6},{3,7},{4,8},{5,9},{6,10},{7,11},{8,12},{9,13},{1... | collective-permute-start | bytes 1572872 | tf_op jit(solution)/shard_map/ppermute | solution.py:381
  16.8 3.5 %collective-permute-start = (bf16[512,512]{1,0:T(8,128)(2,1)}, bf16[512,512]{1,0:T(8,128)(2,1)S(1)}, u32[]{:S(2)}, u32[]{:S(2)}) collective-permute-start(bf16[512,512]{1,0:T(8,128)(2,1)} %get-tuple-element.26.refs_0_), channel_id=1, source_target_pairs={{0,2},{1,3},{4,6},{5,7},{8,10},{9,11},{12,14},{13,15},{16,18},{17,... | collective-permute-start | bytes 1572872 | tf_op jit(solution)/shard_map/ppermute | solution.py:381
  20.2 8.8 %collective-permute-done.2.refs_1_ = bf16[512,512]{1,0:T(8,128)(2,1)S(1)} collective-permute-done((bf16[512,512]{1,0:T(8,128)(2,1)}, bf16[512,512]{1,0:T(8,128)(2,1)S(1)}, u32[]{:S(2)}, u32[]{:S(2)}) %collective-permute-start.2) | collective-permute-done | bytes 524320 | tf_op jit(solution)/shard_map/ppermute | solution.py:381
  29.0 3.4 %collective-permute-start.4 = (bf16[512,512]{1,0:T(8,128)(2,1)S(1)}, bf16[512,512]{1,0:T(8,128)(2,1)S(1)}, u32[]{:S(2)}, u32[]{:S(2)}) collective-permute-start(bf16[512,512]{1,0:T(8,128)(2,1)S(1)} %collective-permute-done.2.refs_1_), channel_id=1, source_target_pairs={{4,6},{5,7},{6,4},{7,5},{8,10},{9,11},{10,8},{11,9},{12,14},{13,15... | collective-permute-start | bytes 1572872 | tf_op jit(solution)/shard_map/ppermute | solution.py:381
  32.5 0.0 collective-permute-done.refs_4_
  32.5 0.0 copy-start.2
  32.5 3.5 %collective-permute-start.3 = (bf16[512,512]{1,0:T(8,128)(2,1)S(1)}, bf16[512,512]{1,0:T(8,128)(2,1)S(1)}, u32[]{:S(2)}, u32[]{:S(2)}) collective-permute-start(bf16[512,512]{1,0:T(8,128)(2,1)S(1)} %collective-permute-done.2.refs_1_), channel_id=1, source_target_pairs={{4,8},{5,9},{6,10},{7,11},{8,12},{9,13},{10,14},{11,15},{20,24},{2... | collective-permute-start | bytes 1572872 | tf_op jit(solution)/shard_map/ppermute | solution.py:381
  36.0 0.0 copy-start
  36.0 0.0 copy-start.10
  36.0 9.4 %project.1.refs_0_ = bf16[512,512]{1,0:T(8,128)(2,1)} custom-call(bf16[512,8192]{1,0:T(8,128)(2,1)} %x_ref.1, f32[512,128]{1,0:T(8,128)} %get-tuple-element.16.scale_ref, f32[1,8192]{1,0:T(1,128)} %bitcast.4, bf16[8192,512]{1,0:T(8,128)(2,1)} %key_ref.1, bf16[8192,512]{1,0:T(8,128)(2,1)} %value_ref.1), custom_call_target="tpu_custom_call" | custom-call | flops 4294967296 | bytes 16777216 | tf_op jit(solution)/shard_map/project/pallas_call | solution.py:193
  45.4 0.0 copy-done.1
  45.4 0.0 copy-done.2
  45.4 2.4 %collective-permute-start.6 = (bf16[512,512]{1,0:T(8,128)(2,1)}, bf16[512,512]{1,0:T(8,128)(2,1)S(1)}, u32[]{:S(2)}, u32[]{:S(2)}) collective-permute-start(bf16[512,512]{1,0:T(8,128)(2,1)} %project.1.refs_0_), channel_id=1, source_target_pairs={{0,2},{1,3},{2,0},{3,1},{4,6},{5,7},{8,10},{9,11},{12,14},{13,15},... | collective-permute-start | bytes 1572872 | tf_op jit(solution)/shard_map/ppermute | solution.py:381
  47.9 1.9 %collective-permute-start.1 = (bf16[512,512]{1,0:T(8,128)(2,1)}, bf16[512,512]{1,0:T(8,128)(2,1)S(1)}, u32[]{:S(2)}, u32[]{:S(2)}) collective-permute-start(bf16[512,512]{1,0:T(8,128)(2,1)} %project.1.refs_0_), channel_id=1, source_target_pairs={{0,4},{1,5},{2,6},{3,7},{4,8},{5,9},{6,10},{7,11},{8,12},{9,13},{1... | collective-permute-start | bytes 1572872 | tf_op jit(solution)/shard_map/ppermute | solution.py:381
  49.8 0.0 collective-permute-done.4.refs_5_
  49.8 0.0 copy-start.4
  49.8 0.0 collective-permute-done.3.refs_2_
  49.8 0.0 copy-start.6
  49.8 1.9 %collective-permute-start.5 = (bf16[512,512]{1,0:T(8,128)(2,1)S(1)}, bf16[512,512]{1,0:T(8,128)(2,1)S(1)}, u32[]{:S(2)}, u32[]{:S(2)}) collective-permute-start(bf16[512,512]{1,0:T(8,128)(2,1)S(1)} %collective-permute-done.3.refs_2_), channel_id=1, source_target_pairs={{8,10},{9,11},{10,8},{11,9},{12,14},{13,15},{14,12},{15,13},{24,26... | collective-permute-start | bytes 1572872 | tf_op jit(solution)/shard_map/ppermute | solution.py:381
  51.8 0.0 copy-done
  51.8 1.5 %collective-permute-start.12 = (bf16[512,512]{1,0:T(8,128)(2,1)S(1)}, bf16[512,512]{1,0:T(8,128)(2,1)}, u32[]{:S(2)}, u32[]{:S(2)}) collective-permute-start(bf16[512,512]{1,0:T(8,128)(2,1)S(1)} %copy-done), channel_id=1, source_target_pairs={{0,12},{1,13},{2,14},{3,15},{16,28},{17,29},{18,30},{19,31}} | collective-permute-start | bytes 1572872 | tf_op jit(solution)/shard_map/ppermute | solution.py:381
  53.2 11.0 %collective-permute-done.1.refs_1_ = bf16[512,512]{1,0:T(8,128)(2,1)S(1)} collective-permute-done((bf16[512,512]{1,0:T(8,128)(2,1)}, bf16[512,512]{1,0:T(8,128)(2,1)S(1)}, u32[]{:S(2)}, u32[]{:S(2)}) %collective-permute-start.1) | collective-permute-done | bytes 524320 | tf_op jit(solution)/shard_map/ppermute | solution.py:381
  64.2 1.9 %collective-permute-start.9 = (bf16[512,512]{1,0:T(8,128)(2,1)S(1)}, bf16[512,512]{1,0:T(8,128)(2,1)S(1)}, u32[]{:S(2)}, u32[]{:S(2)}) collective-permute-start(bf16[512,512]{1,0:T(8,128)(2,1)S(1)} %collective-permute-done.1.refs_1_), channel_id=1, source_target_pairs={{4,6},{5,7},{6,4},{7,5},{8,10},{9,11},{10,8},{11,9},{12,14},{13,15... | collective-permute-start | bytes 1572872 | tf_op jit(solution)/shard_map/ppermute | solution.py:381
  66.1 0.0 collective-permute-done.6.refs_4_
  66.1 0.0 copy-start.3
  66.2 5.5 %collective-permute-done.5.refs_6_ = bf16[512,512]{1,0:T(8,128)(2,1)S(1)} collective-permute-done((bf16[512,512]{1,0:T(8,128)(2,1)S(1)}, bf16[512,512]{1,0:T(8,128)(2,1)S(1)}, u32[]{:S(2)}, u32[]{:S(2)}) %collective-permute-start.5) | collective-permute-done | bytes 524320 | tf_op jit(solution)/shard_map/ppermute | solution.py:381
  71.6 1.9 %collective-permute-start.7 = (bf16[512,512]{1,0:T(8,128)(2,1)S(1)}, bf16[512,512]{1,0:T(8,128)(2,1)}, u32[]{:S(2)}, u32[]{:S(2)}) collective-permute-start(bf16[512,512]{1,0:T(8,128)(2,1)S(1)} %collective-permute-done.1.refs_1_), channel_id=1, source_target_pairs={{4,8},{5,9},{6,10},{7,11},{8,12},{9,13},{10,14},{11,15},{20,24},{2... | collective-permute-start | bytes 1572872 | tf_op jit(solution)/shard_map/ppermute | solution.py:381
  73.6 0.0 collective-permute-done.12.refs_3_
  73.6 1.5 %collective-permute-start.13 = (bf16[512,512]{1,0:T(8,128)(2,1)}, bf16[512,512]{1,0:T(8,128)(2,1)}, u32[]{:S(2)}, u32[]{:S(2)}) collective-permute-start(bf16[512,512]{1,0:T(8,128)(2,1)} %collective-permute-done.12.refs_3_), channel_id=1, source_target_pairs={{12,14},{13,15},{14,12},{15,13},{28,30},{29,31},{30,28},{31,29}} | collective-permute-start | bytes 1572872 | tf_op jit(solution)/shard_map/ppermute | solution.py:381
  75.0 0.7 collective-permute-start.11
  75.7 4.5 %collective-permute-done.9.refs_5_ = bf16[512,512]{1,0:T(8,128)(2,1)S(1)} collective-permute-done((bf16[512,512]{1,0:T(8,128)(2,1)S(1)}, bf16[512,512]{1,0:T(8,128)(2,1)S(1)}, u32[]{:S(2)}, u32[]{:S(2)}) %collective-permute-start.9) | collective-permute-done | bytes 524320 | tf_op jit(solution)/shard_map/ppermute | solution.py:381
  80.2 16.1 %collective-permute-done.7.refs_2_ = bf16[512,512]{1,0:T(8,128)(2,1)} collective-permute-done((bf16[512,512]{1,0:T(8,128)(2,1)S(1)}, bf16[512,512]{1,0:T(8,128)(2,1)}, u32[]{:S(2)}, u32[]{:S(2)}) %collective-permute-start.7) | collective-permute-done | bytes 524320 | tf_op jit(solution)/shard_map/ppermute | solution.py:381
  96.4 0.0 copy-done.8
  96.4 4.2 %collective-permute-start.8 = (bf16[512,512]{1,0:T(8,128)(2,1)}, bf16[512,512]{1,0:T(8,128)(2,1)}, u32[]{:S(2)}, u32[]{:S(2)}) collective-permute-start(bf16[512,512]{1,0:T(8,128)(2,1)} %collective-permute-done.7.refs_2_), channel_id=1, source_target_pairs={{8,12},{9,13},{10,14},{11,15},{24,28},{25,29},{26,30},{27,31}} | collective-permute-start | bytes 1572872 | tf_op jit(solution)/shard_map/ppermute | solution.py:381
  100.5 5.0 %collective-permute-start.10 = (bf16[512,512]{1,0:T(8,128)(2,1)}, bf16[512,512]{1,0:T(8,128)(2,1)}, u32[]{:S(2)}, u32[]{:S(2)}) collective-permute-start(bf16[512,512]{1,0:T(8,128)(2,1)} %collective-permute-done.7.refs_2_), channel_id=1, source_target_pairs={{8,10},{9,11},{10,8},{11,9},{12,14},{13,15},{14,12},{15,13},{24,26... | collective-permute-start | bytes 1572872 | tf_op jit(solution)/shard_map/ppermute | solution.py:381
  105.5 0.0 copy-done.10
  105.6 0.6 fusion.1.slot_ref
  106.2 0.0 collective-permute-done.13.refs_7_
  106.2 0.0 copy-done.4
  106.2 0.0 copy-done.6
  106.2 10.7 %attention.2.refs_8_ = bf16[512,4096]{1,0:T(8,128)(2,1)} custom-call(s32[8,7]{1,0:T(8,128)} %fusion.1.slot_ref, s32[8,7]{1,0:T(8,128)} %cut_ref.3, s32[1]{0:T(128)} %bitcast.odd_ref, bf16[512,4096]{1,0:T(8,128)(2,1)} %q_ref.3, bf16[512,512]{1,0:T(8,128)(2,1)} %get-tuple-element.26.refs_0_, bf16[512,512]{1,0:T(8,128)(2,1)} %copy-done.1, ...), custom_call_target="tpu_custom_call" | custom-call | flops 2147483648 | bytes 8388608 | tf_op jit(solution)/shard_map/attention/pallas_call | solution.py:320
  116.9 0.0 collective-permute-done.11.refs_7_
  116.9 0.0 copy-start.9
  116.9 0.0 collective-permute-done.8.refs_3_
  116.9 0.0 collective-permute-done.10.refs_6_
  116.9 0.7 copy-done.9
  117.7 10.7 %attention.3 = bf16[512,4096]{1,0:T(8,128)(2,1)} custom-call(s32[8,7]{1,0:T(8,128)} %fusion.1.slot_ref, s32[8,7]{1,0:T(8,128)} %cut_ref.3, s32[1]{0:T(128)} %bitcast.odd_ref, bf16[512,4096]{1,0:T(8,128)(2,1)} %q_ref.3, bf16[512,512]{1,0:T(8,128)(2,1)} %project.1.refs_0_, bf16[512,512]{1,0:T(8,128)(2,1)} %copy-done.5, ...), custom_call_target="tpu_custom_call", output_to_operand_aliasing={{}: (12, {})} | custom-call | flops 2147483648 | bytes 8388608 | tf_op jit(solution)/shard_map/attention/pallas_call | solution.py:320
  (7 shorter events, 0.0 us)
Async XLA Ops:
  13.3 15.8 %collective-permute-start.2 = (bf16[512,512]{1,0:T(8,128)(2,1)}, bf16[512,512]{1,0:T(8,128)(2,1)S(1)}, u32[]{:S(2)}, u32[]{:S(2)}) collective-permute-start(bf16[512,512]{1,0:T(8,128)(2,1)} %get-tuple-element.26.refs_0_), channel_id=1, source_target_pairs={{0,4},{1,5},{2,6},{3,7},{4,8},{5,9},{6,10},{7,11},{8,12},{9,13},{1... | collective-permute-start | bytes 1572872 | tf_op jit(solution)/shard_map/ppermute | solution.py:381
  16.8 15.7 %collective-permute-start = (bf16[512,512]{1,0:T(8,128)(2,1)}, bf16[512,512]{1,0:T(8,128)(2,1)S(1)}, u32[]{:S(2)}, u32[]{:S(2)}) collective-permute-start(bf16[512,512]{1,0:T(8,128)(2,1)} %get-tuple-element.26.refs_0_), channel_id=1, source_target_pairs={{0,2},{1,3},{4,6},{5,7},{8,10},{9,11},{12,14},{13,15},{16,18},{17,... | collective-permute-start | bytes 1572872 | tf_op jit(solution)/shard_map/ppermute | solution.py:381
  29.0 16.4 %copy-start.1 = (bf16[512,512]{1,0:T(8,128)(2,1)}, bf16[512,512]{1,0:T(8,128)(2,1)S(1)}, u32[]{:S(2)}) copy-start(bf16[512,512]{1,0:T(8,128)(2,1)S(1)} %collective-permute-done.2.refs_1_) | copy-start | bytes 1572868
  29.0 20.8 %collective-permute-start.4 = (bf16[512,512]{1,0:T(8,128)(2,1)S(1)}, bf16[512,512]{1,0:T(8,128)(2,1)S(1)}, u32[]{:S(2)}, u32[]{:S(2)}) collective-permute-start(bf16[512,512]{1,0:T(8,128)(2,1)S(1)} %collective-permute-done.2.refs_1_), channel_id=1, source_target_pairs={{4,6},{5,7},{6,4},{7,5},{8,10},{9,11},{10,8},{11,9},{12,14},{13,15... | collective-permute-start | bytes 1572872 | tf_op jit(solution)/shard_map/ppermute | solution.py:381
  32.5 12.9 %copy-start.2 = (bf16[512,512]{1,0:T(8,128)(2,1)}, bf16[512,512]{1,0:T(8,128)(2,1)S(1)}, u32[]{:S(2)}) copy-start(bf16[512,512]{1,0:T(8,128)(2,1)S(1)} %collective-permute-done.refs_4_) | copy-start | bytes 1572868
  32.5 17.3 %collective-permute-start.3 = (bf16[512,512]{1,0:T(8,128)(2,1)S(1)}, bf16[512,512]{1,0:T(8,128)(2,1)S(1)}, u32[]{:S(2)}, u32[]{:S(2)}) collective-permute-start(bf16[512,512]{1,0:T(8,128)(2,1)S(1)} %collective-permute-done.2.refs_1_), channel_id=1, source_target_pairs={{4,8},{5,9},{6,10},{7,11},{8,12},{9,13},{10,14},{11,15},{20,24},{2... | collective-permute-start | bytes 1572872 | tf_op jit(solution)/shard_map/ppermute | solution.py:381
  36.0 15.8 %copy-start = (bf16[512,512]{1,0:T(8,128)(2,1)S(1)}, bf16[512,512]{1,0:T(8,128)(2,1)}, u32[]{:S(2)}) copy-start(bf16[512,512]{1,0:T(8,128)(2,1)} %get-tuple-element.26.refs_0_) | copy-start | bytes 1572868
  36.0 69.6 %copy-start.10 = (s32[8,7]{1,0:T(8,128)S(1)}, s32[8,7]{1,0:T(8,128)}, u32[]{:S(2)}) copy-start(s32[8,7]{1,0:T(8,128)} %param.12) | copy-start | bytes 676
  45.4 20.7 %collective-permute-start.6 = (bf16[512,512]{1,0:T(8,128)(2,1)}, bf16[512,512]{1,0:T(8,128)(2,1)S(1)}, u32[]{:S(2)}, u32[]{:S(2)}) collective-permute-start(bf16[512,512]{1,0:T(8,128)(2,1)} %project.1.refs_0_), channel_id=1, source_target_pairs={{0,2},{1,3},{2,0},{3,1},{4,6},{5,7},{8,10},{9,11},{12,14},{13,15},... | collective-permute-start | bytes 1572872 | tf_op jit(solution)/shard_map/ppermute | solution.py:381
  47.9 16.4 %collective-permute-start.1 = (bf16[512,512]{1,0:T(8,128)(2,1)}, bf16[512,512]{1,0:T(8,128)(2,1)S(1)}, u32[]{:S(2)}, u32[]{:S(2)}) collective-permute-start(bf16[512,512]{1,0:T(8,128)(2,1)} %project.1.refs_0_), channel_id=1, source_target_pairs={{0,4},{1,5},{2,6},{3,7},{4,8},{5,9},{6,10},{7,11},{8,12},{9,13},{1... | collective-permute-start | bytes 1572872 | tf_op jit(solution)/shard_map/ppermute | solution.py:381
  49.8 56.4 %copy-start.4 = (bf16[512,512]{1,0:T(8,128)(2,1)}, bf16[512,512]{1,0:T(8,128)(2,1)S(1)}, u32[]{:S(2)}) copy-start(bf16[512,512]{1,0:T(8,128)(2,1)S(1)} %collective-permute-done.4.refs_5_) | copy-start | bytes 1572868
  49.8 56.3 %copy-start.6 = (bf16[512,512]{1,0:T(8,128)(2,1)}, bf16[512,512]{1,0:T(8,128)(2,1)S(1)}, u32[]{:S(2)}) copy-start(bf16[512,512]{1,0:T(8,128)(2,1)S(1)} %collective-permute-done.3.refs_2_) | copy-start | bytes 1572868
  49.8 21.8 %collective-permute-start.5 = (bf16[512,512]{1,0:T(8,128)(2,1)S(1)}, bf16[512,512]{1,0:T(8,128)(2,1)S(1)}, u32[]{:S(2)}, u32[]{:S(2)}) collective-permute-start(bf16[512,512]{1,0:T(8,128)(2,1)S(1)} %collective-permute-done.3.refs_2_), channel_id=1, source_target_pairs={{8,10},{9,11},{10,8},{11,9},{12,14},{13,15},{14,12},{15,13},{24,26... | collective-permute-start | bytes 1572872 | tf_op jit(solution)/shard_map/ppermute | solution.py:381
  51.8 21.8 %collective-permute-start.12 = (bf16[512,512]{1,0:T(8,128)(2,1)S(1)}, bf16[512,512]{1,0:T(8,128)(2,1)}, u32[]{:S(2)}, u32[]{:S(2)}) collective-permute-start(bf16[512,512]{1,0:T(8,128)(2,1)S(1)} %copy-done), channel_id=1, source_target_pairs={{0,12},{1,13},{2,14},{3,15},{16,28},{17,29},{18,30},{19,31}} | collective-permute-start | bytes 1572872 | tf_op jit(solution)/shard_map/ppermute | solution.py:381
  64.2 52.7 %copy-start.5 = (bf16[512,512]{1,0:T(8,128)(2,1)}, bf16[512,512]{1,0:T(8,128)(2,1)S(1)}, u32[]{:S(2)}) copy-start(bf16[512,512]{1,0:T(8,128)(2,1)S(1)} %collective-permute-done.1.refs_1_) | copy-start | bytes 1572868
  64.2 16.0 %collective-permute-start.9 = (bf16[512,512]{1,0:T(8,128)(2,1)S(1)}, bf16[512,512]{1,0:T(8,128)(2,1)S(1)}, u32[]{:S(2)}, u32[]{:S(2)}) collective-permute-start(bf16[512,512]{1,0:T(8,128)(2,1)S(1)} %collective-permute-done.1.refs_1_), channel_id=1, source_target_pairs={{4,6},{5,7},{6,4},{7,5},{8,10},{9,11},{10,8},{11,9},{12,14},{13,15... | collective-permute-start | bytes 1572872 | tf_op jit(solution)/shard_map/ppermute | solution.py:381
  66.1 50.8 %copy-start.3 = (bf16[512,512]{1,0:T(8,128)(2,1)}, bf16[512,512]{1,0:T(8,128)(2,1)S(1)}, u32[]{:S(2)}) copy-start(bf16[512,512]{1,0:T(8,128)(2,1)S(1)} %collective-permute-done.6.refs_4_) | copy-start | bytes 1572868
  71.6 24.7 %copy-start.8 = (bf16[512,512]{1,0:T(8,128)(2,1)}, bf16[512,512]{1,0:T(8,128)(2,1)S(1)}, u32[]{:S(2)}) copy-start(bf16[512,512]{1,0:T(8,128)(2,1)S(1)} %collective-permute-done.5.refs_6_) | copy-start | bytes 1572868
  71.6 24.7 %collective-permute-start.7 = (bf16[512,512]{1,0:T(8,128)(2,1)S(1)}, bf16[512,512]{1,0:T(8,128)(2,1)}, u32[]{:S(2)}, u32[]{:S(2)}) collective-permute-start(bf16[512,512]{1,0:T(8,128)(2,1)S(1)} %collective-permute-done.1.refs_1_), channel_id=1, source_target_pairs={{4,8},{5,9},{6,10},{7,11},{8,12},{9,13},{10,14},{11,15},{20,24},{2... | collective-permute-start | bytes 1572872 | tf_op jit(solution)/shard_map/ppermute | solution.py:381
  73.6 32.6 %collective-permute-start.13 = (bf16[512,512]{1,0:T(8,128)(2,1)}, bf16[512,512]{1,0:T(8,128)(2,1)}, u32[]{:S(2)}, u32[]{:S(2)}) collective-permute-start(bf16[512,512]{1,0:T(8,128)(2,1)} %collective-permute-done.12.refs_3_), channel_id=1, source_target_pairs={{12,14},{13,15},{14,12},{15,13},{28,30},{29,31},{30,28},{31,29}} | collective-permute-start | bytes 1572872 | tf_op jit(solution)/shard_map/ppermute | solution.py:381
  75.0 41.8 %collective-permute-start.11 = (bf16[512,512]{1,0:T(8,128)(2,1)S(1)}, bf16[512,512]{1,0:T(8,128)(2,1)S(1)}, u32[]{:S(2)}, u32[]{:S(2)}) collective-permute-start(bf16[512,512]{1,0:T(8,128)(2,1)S(1)} %collective-permute-done.6.refs_4_), channel_id=1, source_target_pairs={{0,12},{1,13},{2,14},{3,15},{16,28},{17,29},{18,30},{19,31}} | collective-permute-start | bytes 1572872 | tf_op jit(solution)/shard_map/ppermute | solution.py:381
  80.2 36.7 %copy-start.7 = (bf16[512,512]{1,0:T(8,128)(2,1)}, bf16[512,512]{1,0:T(8,128)(2,1)S(1)}, u32[]{:S(2)}) copy-start(bf16[512,512]{1,0:T(8,128)(2,1)S(1)} %collective-permute-done.9.refs_5_) | copy-start | bytes 1572868
  96.4 20.5 %collective-permute-start.8 = (bf16[512,512]{1,0:T(8,128)(2,1)}, bf16[512,512]{1,0:T(8,128)(2,1)}, u32[]{:S(2)}, u32[]{:S(2)}) collective-permute-start(bf16[512,512]{1,0:T(8,128)(2,1)} %collective-permute-done.7.refs_2_), channel_id=1, source_target_pairs={{8,12},{9,13},{10,14},{11,15},{24,28},{25,29},{26,30},{27,31}} | collective-permute-start | bytes 1572872 | tf_op jit(solution)/shard_map/ppermute | solution.py:381
  100.5 16.4 %collective-permute-start.10 = (bf16[512,512]{1,0:T(8,128)(2,1)}, bf16[512,512]{1,0:T(8,128)(2,1)}, u32[]{:S(2)}, u32[]{:S(2)}) collective-permute-start(bf16[512,512]{1,0:T(8,128)(2,1)} %collective-permute-done.7.refs_2_), channel_id=1, source_target_pairs={{8,10},{9,11},{10,8},{11,9},{12,14},{13,15},{14,12},{15,13},{24,26... | collective-permute-start | bytes 1572872 | tf_op jit(solution)/shard_map/ppermute | solution.py:381
  116.9 0.8 copy-start.9

commit v12 on v11

--- a/solution.py
+++ b/solution.py
@@ -21,17 +21,17 @@
     ("across", 0, 0, ()),
     ("along", 1, 0, ()),
     ("across", 0, 1, ()),
-    ("along", 1, 1, (("across", 0, 0),)),
-    ("along", 2, 0, (("across", 0, 0),)),
-    ("across", 1, 0, ()),
-    ("across", 1, 1, (("across", 1, 0),)),
-    ("direct", 3, 0, (("across", 0, 0),)),
+    ("along", 1, 1, ()),
+    ("across", 1, 0, (("across", 0, 0),)),
+    ("along", 2, 0, (("along", 1, 0),)),
+    ("across", 1, 1, (("across", 0, 1),)),
+    ("along", 3, 0, (("along", 1, 1),)),
     ("across", 2, 0, (("across", 1, 0),)),
-    ("along", 2, 1, (("across", 2, 0), ("across", 0, 1), ("along", 1, 1))),
-    ("across", 3, 0, ()),
-    ("across", 2, 1, (("along", 1, 1), ("across", 1, 1))),
-    ("down", 3, 1, (("across", 0, 0),)),
-    ("along", 3, 1, (("across", 0, 1),)),
+    ("along", 2, 1, (("along", 2, 0),)),
+    ("across", 3, 0, (("across", 1, 1),)),
+    ("across", 2, 1, (("across", 2, 0),)),
+    ("along", 3, 1, (("along", 2, 1),)),
+    ("down", 3, 1, (("along", 3, 0), ("across", 2, 0), ("along", 2, 1))),
 )
 
 
@@ -211,7 +211,7 @@
     )(hidden, scale, gain.reshape(1, features), key_weight, value_weight)
 
 
-def attention_kernel(block, near, slot_ref, cut_ref, odd_ref, q_ref, *refs):
+def attention_kernel(block, near, first_head, slot_ref, cut_ref, odd_ref, q_ref, *refs):
     own_hbm, straight, crossed = refs[0], refs[1 : near + 1], refs[near + 1 : 2 * near + 2]
     out_ref, kv_scr, sems = refs[-3:]
     kv_heads, levels = kv_scr.shape[:2]
@@ -223,10 +223,9 @@
 
     def fetch(index):
         def copy(ref, level, number):
+            first = 0 if ref.shape[1] == width else (first_head + index) * width
             return pltpu.make_async_copy(
-                ref.at[:, pl.ds(pl.multiple_of(index * width, width), width)],
-                kv_scr.at[index, level],
-                sems.at[index, number],
+                ref.at[:, first : first + width], kv_scr.at[index, level], sems.at[index, number]
             )
 
         copies = [copy(own_hbm, depth, 0)]
@@ -243,10 +242,12 @@
             for copy in fetch(index):
                 copy.start()
 
-    @pl.when(step == 0)
-    def _():
-        for copy in fetch(head):
-            copy.wait()
+    for index in range(kv_heads):
+
+        @pl.when((head == index) & (step == 0))
+        def _(index=index):
+            for copy in fetch(index):
+                copy.wait()
 
     token = lax.broadcasted_iota(jnp.int32, (block, HEAD_DIM), 0)
     lane = lax.broadcasted_iota(jnp.int32, (block, HEAD_DIM), 1)
@@ -280,7 +281,7 @@
 
     def finish(local, scores, values):
         peak = jnp.max(scores, axis=-1, keepdims=True)
-        weights = jnp.exp2((scores - peak) * scale).astype(jnp.bfloat16)
+        weights = jnp.exp2(((scores - peak) * scale).astype(jnp.bfloat16))
         padded = jnp.concatenate([values, jnp.ones_like(values)], axis=1)
         both = jnp.dot(weights, padded, preferred_element_type=jnp.float32)
         context = (both[:, :HEAD_DIM] * (1.0 / both[:, HEAD_DIM:])).astype(jnp.bfloat16)
@@ -298,27 +299,25 @@
         finish(*item)
 
 
-def attention(slots, cuts, odd, queries, own, straight, crossed, unit, previous):
+def attention(slots, cuts, odd, queries, own, straight, crossed, unit, first_head, kv_heads, previous):
     rows, features = queries.shape
     blocks, depth = slots.shape
     block = rows // blocks
-    wide = features // UNITS
     near = len(straight)
+    per_unit = own.shape[1] // (2 * HEAD_DIM)
+    per_head = features // UNITS // per_unit
+    first = unit * per_unit + first_head
+    part = pl.BlockSpec((BLOCKS_PER_STEP * block, per_head), lambda h, b, *_: (b, first + h))
     held = pl.BlockSpec(memory_space=pltpu.HBM)
-    kv_heads = own.shape[1] // (2 * HEAD_DIM)
-    per_head = wide // kv_heads
-    part = pl.BlockSpec(
-        (BLOCKS_PER_STEP * block, per_head), lambda h, b, *_: (b, unit * kv_heads + h)
-    )
     operands = [slots, cuts, odd, queries, own, *straight, *crossed]
-    in_specs = [part] + [held] * (1 + near + len(crossed))
+    in_specs = [part] + [held] * (len(operands) - 4)
     aliases = {}
     if previous is not None:
         aliases = {len(operands): 0}
         operands.append(previous)
         in_specs.append(held)
     return pl.pallas_call(
-        functools.partial(attention_kernel, block, near),
+        functools.partial(attention_kernel, block, near, first_head),
         grid_spec=pltpu.PrefetchScalarGridSpec(
             num_scalar_prefetch=3,
             grid=(kv_heads, blocks // BLOCKS_PER_STEP),
@@ -333,9 +332,9 @@
         input_output_aliases=aliases,
         compiler_params=pltpu.CompilerParams(vmem_limit_bytes=57 * MIB),
         cost_estimate=pl.CostEstimate(
-            flops=4 * rows * wide * (depth + 1) * block,
-            bytes_accessed=8 * MIB,
-            transcendentals=rows * wide // HEAD_DIM * (depth + 1) * block,
+            flops=4 * rows * kv_heads * per_head * (depth + 1) * block,
+            bytes_accessed=4 * kv_heads * MIB,
+            transcendentals=rows * kv_heads * per_head // HEAD_DIM * (depth + 1) * block,
         ),
         name="attention",
     )(*operands)
@@ -359,41 +358,51 @@
         return lax.optimization_barrier((array, *earlier))[0]
 
     column = 2 * chains
+    per_unit = key_weight.shape[1] // HEAD_DIM // UNITS
+    width = 2 * HEAD_DIM
     moved = {("own", 0, 0): own[0], ("own", 0, 1): own[1]}
 
     def step(kind, s, unit, waits):
         if kind == "across":
             source = ("along", s, unit) if s else ("own", 0, unit)
-            exchange = s > 0 or unit == UNITS - 1
+            exchange = unit == UNITS - 1
             pairs = [
                 (i, other[i])
                 for i in range(size)
-                if half[i] >= s and (even[i] or (exchange and half[i] == 0) or s > 0)
+                if half[i] >= s and (s > 0 or even[i] or (exchange and half[i] == 0))
             ]
         elif kind == "along":
             source = ("along", s - 1, unit) if s > 1 else ("own", 0, unit)
             pairs = [(i, i + column) for i in range(size - column) if half[i] >= s - 1]
         else:
-            source = ("across" if kind == "down" else "own", 0, unit)
+            source = ("across", 0, unit)
             pairs = [(i, i + s * column) for i in range(size - s * column)]
         array = lax.optimization_barrier((moved[source], *[moved[w] for w in waits]))[0]
-        key = "along" if kind == "direct" else kind
-        moved[key, s, unit] = lax.ppermute(array, "node", pairs)
+        if unit == 1 and s == near:
+            parts = [array[:, h * width : (h + 1) * width] for h in range(per_unit)]
+        else:
+            parts = [array]
+        for h, part in enumerate(parts):
+            moved[kind, s, unit, h] = lax.ppermute(part, "node", pairs)
+        moved[kind, s, unit] = moved[kind, s, unit, 0]
 
     for kind, s, unit, waits in PLAN:
         step(kind, s, unit, waits)
+
     result = None
-    for unit in range(UNITS):
+    for unit, first, count in ((0, 0, per_unit), *[(1, h, 1) for h in range(per_unit)]):
+        far = "across" if unit == 0 else "down"
         result = attention(
             slots,
             anc_cut,
             odd,
             queries,
             own[unit],
-            [moved["along", s, unit] for s in range(1, near + 1)],
-            [moved["across", s, unit] for s in range(near)]
-            + [moved["across" if unit == 0 else "down", near, unit]],
+            [moved["along", s, unit] for s in range(1, near)] + [moved["along", near, unit, first]],
+            [moved["across", s, unit] for s in range(near)] + [moved[far, near, unit, first]],
             unit,
+            first,
+            count,
             result,
         )
     return result

time: 129 us -> 135 us (1.047)
  the two profiles are of different devices: /device:TPU:16 before, /device:TPU:0 now
where the time goes in v12:
time: 135 us; the launch traced here: 134 us
  starting transfers between devices  70.3 us (52%)
  Pallas kernels  48.1 us (36%)
  waiting for transfers between devices  9.48 us (7%)
  local copies, waits for them, and re-layouts  5.4 us (4%)
    ppermute x16, starting transfers between devices, step(): moved[kind, s, unit, h] = lax.ppermute(part, 'node', pairs)  70.3 us
    pallas_call x3, Pallas kernels, attention(): pl.pallas_call(functools.partial(attention_kernel, block, near, first_hea...  25.5 us
    pallas_call x1, Pallas kernels, norm_project(): pl.pallas_call(norm_project_kernel, in_specs=[held, whole, held, held], o...  13.3 us
    ppermute x16, waiting for transfers between devices, step(): moved[kind, s, unit, h] = lax.ppermute(part, 'node', pairs)  9.48 us
    pallas_call x1, Pallas kernels, project(): pl.pallas_call(project_kernel, grid=(CHUNKS,), in_specs=[pl.BlockSpec((ro...  9.36 us
    unnamed x28, local copies, waits for them, and re-layouts  3.75 us
  transfers between devices with their start and end apart: 16, of which 2 were waited for; matrix products, arithmetic and copies ran while one was open for 2% of the time, Pallas kernels for 20%

profile of v12, /device:TPU:0, one launch (start us, length us, event | category | flops | bytes accessed | tf_op | source)
XLA Modules:
  0.0 134.3 jit_solution(5073116203271771020)
XLA Ops:
  0.0 13.3 %norm_project.1 = (f32[512,128]{1,0:T(8,128)}, bf16[512,512]{1,0:T(8,128)(2,1)}) custom-call(bf16[512,8192]{1,0:T(8,128)(2,1)} %x_ref.1, f32[8,1,1024]{2,1,0:T(1,128)} %bitcast.3, bf16[8192,512]{1,0:T(8,128)(2,1)} %key_ref.1, bf16[8192,512]{1,0:T(8,128)(2,1)} %value_ref.1), custom_call_target="tpu_custom_call" | custom-call | flops 4294967296 | bytes 16777216 | tf_op jit(solution)/shard_map/norm_project/pallas_call | solution.py:140
  13.3 5.0 %collective-permute-start.1 = (bf16[512,512]{1,0:T(8,128)(2,1)}, bf16[512,512]{1,0:T(8,128)(2,1)S(1)}, u32[]{:S(2)}, u32[]{:S(2)}) collective-permute-start(bf16[512,512]{1,0:T(8,128)(2,1)} %get-tuple-element.18.refs_0_), channel_id=1, source_target_pairs={{0,4},{1,5},{2,6},{3,7},{4,8},{5,9},{6,10},{7,11},{8,12},{9,13},{1... | collective-permute-start | bytes 1572872 | tf_op jit(solution)/shard_map/ppermute | solution.py:386
  18.2 3.5 %collective-permute-start.7 = (bf16[512,512]{1,0:T(8,128)(2,1)}, bf16[512,512]{1,0:T(8,128)(2,1)S(1)}, u32[]{:S(2)}, u32[]{:S(2)}) collective-permute-start(bf16[512,512]{1,0:T(8,128)(2,1)} %get-tuple-element.18.refs_0_), channel_id=1, source_target_pairs={{0,2},{1,3},{4,6},{5,7},{8,10},{9,11},{12,14},{13,15},{16,18},{17,... | collective-permute-start | bytes 1572872 | tf_op jit(solution)/shard_map/ppermute | solution.py:386
  21.7 0.0 copy-start.13
  21.7 9.4 %project.1.refs_0_ = bf16[512,512]{1,0:T(8,128)(2,1)} custom-call(bf16[512,8192]{1,0:T(8,128)(2,1)} %x_ref.1, f32[512,128]{1,0:T(8,128)} %get-tuple-element.17.scale_ref, f32[1,8192]{1,0:T(1,128)} %bitcast.4, bf16[8192,512]{1,0:T(8,128)(2,1)} %key_ref.1, bf16[8192,512]{1,0:T(8,128)(2,1)} %value_ref.1), custom_call_target="tpu_custom_call" | custom-call | flops 4294967296 | bytes 16777216 | tf_op jit(solution)/shard_map/project/pallas_call | solution.py:193
  31.1 1.9 %collective-permute-start.5 = (bf16[512,512]{1,0:T(8,128)(2,1)}, bf16[512,512]{1,0:T(8,128)(2,1)S(1)}, u32[]{:S(2)}, u32[]{:S(2)}) collective-permute-start(bf16[512,512]{1,0:T(8,128)(2,1)} %project.1.refs_0_), channel_id=1, source_target_pairs={{0,2},{1,3},{2,0},{3,1},{4,6},{5,7},{8,10},{9,11},{12,14},{13,15},... | collective-permute-start | bytes 1572872 | tf_op jit(solution)/shard_map/ppermute | solution.py:386
  33.0 2.9 %collective-permute-start = (bf16[512,512]{1,0:T(8,128)(2,1)}, bf16[512,512]{1,0:T(8,128)(2,1)S(1)}, u32[]{:S(2)}, u32[]{:S(2)}) collective-permute-start(bf16[512,512]{1,0:T(8,128)(2,1)} %project.1.refs_0_), channel_id=1, source_target_pairs={{0,4},{1,5},{2,6},{3,7},{4,8},{5,9},{6,10},{7,11},{8,12},{9,13},{1... | collective-permute-start | bytes 1572872 | tf_op jit(solution)/shard_map/ppermute | solution.py:386
  35.9 0.0 collective-permute-done.1.refs_1_
  35.9 0.0 copy-start.5
  35.9 0.7 collective-permute-start.2
  36.6 0.0 collective-permute-done.7.refs_4_
  36.6 0.7 collective-permute-start.8
  37.3 8.9 %collective-permute-done.5.refs_4_ = bf16[512,512]{1,0:T(8,128)(2,1)S(1)} collective-permute-done((bf16[512,512]{1,0:T(8,128)(2,1)}, bf16[512,512]{1,0:T(8,128)(2,1)S(1)}, u32[]{:S(2)}, u32[]{:S(2)}) %collective-permute-start.5) | collective-permute-done | bytes 524320 | tf_op jit(solution)/shard_map/ppermute | solution.py:386
  46.3 0.5 collective-permute-done.refs_1_
  46.8 0.7 collective-permute-start.6
  47.5 0.0 collective-permute-done.2.refs_2_
  47.5 0.7 collective-permute-start.3
  48.2 1.5 %collective-permute-start.11 = (bf16[512,512]{1,0:T(8,128)(2,1)S(1)}, bf16[512,512]{1,0:T(8,128)(2,1)}, u32[]{:S(2)}, u32[]{:S(2)}) collective-permute-start(bf16[512,512]{1,0:T(8,128)(2,1)S(1)} %collective-permute-done.2.refs_2_), channel_id=1, source_target_pairs={{8,12},{9,13},{10,14},{11,15},{24,28},{25,29},{26,30},{27,31}} | collective-permute-start | bytes 1572872 | tf_op jit(solution)/shard_map/ppermute | solution.py:386
  49.7 0.0 collective-permute-done.8.refs_5_
  49.7 0.7 collective-permute-start.9
  50.4 0.0 collective-permute-done.3.refs_2_
  50.4 0.0 collective-permute-done.6.refs_5_
  50.4 0.0 collective-permute-done.11.refs_3_
  50.4 0.1 copy-done.8
  50.5 1.5 %collective-permute-start.15 = (bf16[512,512]{1,0:T(8,128)(2,1)}, bf16[512,512]{1,0:T(8,128)(2,1)}, u32[]{:S(2)}, u32[]{:S(2)}) collective-permute-start(bf16[512,512]{1,0:T(8,128)(2,1)} %collective-permute-done.11.refs_3_), channel_id=1, source_target_pairs={{12,14},{13,15},{14,12},{15,13},{28,30},{29,31},{30,28},{31,29}} | collective-permute-start | bytes 1572872 | tf_op jit(solution)/shard_map/ppermute | solution.py:386
  51.9 0.8 fusion.3
  52.8 0.7 collective-permute-start.13
  53.4 0.0 collective-permute-done.9.refs_6_
  53.5 0.8 copy-done.9
  54.3 0.7 collective-permute-start.10
  55.0 0.8 fusion.2
  55.8 43.3 %collective-permute-start.14 = (bf16[512,256]{1,0:T(8,128)(2,1)}, bf16[512,256]{1,0:T(8,128)(2,1)}, u32[]{:S(2)}, u32[]{:S(2)}) collective-permute-start(bf16[512,256]{1,0:T(8,128)(2,1)} %get-tuple-element.29), channel_id=1, source_target_pairs={{0,12},{1,13},{2,14},{3,15},{16,28},{17,29},{18,30},{19,31}} | collective-permute-start | bytes 786440 | tf_op jit(solution)/shard_map/ppermute | solution.py:386
  99.1 0.6 fusion.1.slot_ref
  99.7 0.7 collective-permute-start.4
  100.3 0.0 collective-permute-done.15.refs_7_
  100.4 5.4 %collective-permute-start.12 = (bf16[512,256]{1,0:T(8,128)(2,1)}, bf16[512,256]{1,0:T(8,128)(2,1)S(1)}, u32[]{:S(2)}, u32[]{:S(2)}) collective-permute-start(bf16[512,256]{1,0:T(8,128)(2,1)} %get-tuple-element.30), channel_id=1, source_target_pairs={{0,12},{1,13},{2,14},{3,15},{16,28},{17,29},{18,30},{19,31}} | collective-permute-start | bytes 786440 | tf_op jit(solution)/shard_map/ppermute | solution.py:386
  105.8 10.7 %attention.3.refs_8_ = bf16[512,4096]{1,0:T(8,128)(2,1)} custom-call(s32[8,7]{1,0:T(8,128)} %fusion.1.slot_ref, s32[8,7]{1,0:T(8,128)} %cut_ref.5, s32[1]{0:T(128)} %bitcast.odd_ref, bf16[512,4096]{1,0:T(8,128)(2,1)} %q_ref.5, bf16[512,512]{1,0:T(8,128)(2,1)} %get-tuple-element.18.refs_0_, bf16[512,512]{1,0:T(8,128)(2,1)} %copy-done.5, ...), custom_call_target="tpu_custom_call" | custom-call | flops 2147483648 | bytes 8388608 | tf_op jit(solution)/shard_map/attention/pallas_call | solution.py:319
  116.5 0.0 collective-permute-done.13.refs_3_
  116.6 0.0 collective-permute-done.14.refs_7_
  116.6 0.0 collective-permute-done.10.refs_6_
  116.6 0.7 copy-done.10
  117.3 0.8 copy-done.4
  118.0 7.4 %attention.4.refs_8_ = bf16[512,4096]{1,0:T(8,128)(2,1)} custom-call(s32[8,7]{1,0:T(8,128)} %fusion.1.slot_ref, s32[8,7]{1,0:T(8,128)} %cut_ref.5, s32[1]{0:T(128)} %bitcast.odd_ref, bf16[512,4096]{1,0:T(8,128)(2,1)} %q_ref.5, bf16[512,512]{1,0:T(8,128)(2,1)} %project.1.refs_0_, bf16[512,512]{1,0:T(8,128)(2,1)} %copy-done.2, ...), custom_call_target="tpu_custom_call", output_to_operand_aliasing={{}: (12, {})} | custom-call | flops 1073741824 | bytes 4194304 | tf_op jit(solution)/shard_map/attention/pallas_call | solution.py:319
  125.5 0.0 collective-permute-done.4.refs_3_
  125.5 0.0 collective-permute-done.12.refs_7_
  125.5 0.7 copy-done.11
  126.2 0.7 copy-done.12
  126.9 7.4 %attention.5 = bf16[512,4096]{1,0:T(8,128)(2,1)} custom-call(s32[8,7]{1,0:T(8,128)} %fusion.1.slot_ref, s32[8,7]{1,0:T(8,128)} %cut_ref.5, s32[1]{0:T(128)} %bitcast.odd_ref, bf16[512,4096]{1,0:T(8,128)(2,1)} %q_ref.5, bf16[512,512]{1,0:T(8,128)(2,1)} %project.1.refs_0_, bf16[512,512]{1,0:T(8,128)(2,1)} %copy-done.2, ...), custom_call_target="tpu_custom_call", output_to_operand_aliasing={{}: (12, {})} | custom-call | flops 1073741824 | bytes 4194304 | tf_op jit(solution)/shard_map/attention/pallas_call | solution.py:319
  (20 shorter events, 0.0 us)
Async XLA Ops:
  13.3 22.6 %collective-permute-start.1 = (bf16[512,512]{1,0:T(8,128)(2,1)}, bf16[512,512]{1,0:T(8,128)(2,1)S(1)}, u32[]{:S(2)}, u32[]{:S(2)}) collective-permute-start(bf16[512,512]{1,0:T(8,128)(2,1)} %get-tuple-element.18.refs_0_), channel_id=1, source_target_pairs={{0,4},{1,5},{2,6},{3,7},{4,8},{5,9},{6,10},{7,11},{8,12},{9,13},{1... | collective-permute-start | bytes 1572872 | tf_op jit(solution)/shard_map/ppermute | solution.py:386
  18.2 18.4 %collective-permute-start.7 = (bf16[512,512]{1,0:T(8,128)(2,1)}, bf16[512,512]{1,0:T(8,128)(2,1)S(1)}, u32[]{:S(2)}, u32[]{:S(2)}) collective-permute-start(bf16[512,512]{1,0:T(8,128)(2,1)} %get-tuple-element.18.refs_0_), channel_id=1, source_target_pairs={{0,2},{1,3},{4,6},{5,7},{8,10},{9,11},{12,14},{13,15},{16,18},{17,... | collective-permute-start | bytes 1572872 | tf_op jit(solution)/shard_map/ppermute | solution.py:386
  21.7 77.4 %copy-start.13 = (s32[8,7]{1,0:T(8,128)S(1)}, s32[8,7]{1,0:T(8,128)}, u32[]{:S(2)}) copy-start(s32[8,7]{1,0:T(8,128)} %param.12) | copy-start | bytes 676
  31.1 15.2 %collective-permute-start.5 = (bf16[512,512]{1,0:T(8,128)(2,1)}, bf16[512,512]{1,0:T(8,128)(2,1)S(1)}, u32[]{:S(2)}, u32[]{:S(2)}) collective-permute-start(bf16[512,512]{1,0:T(8,128)(2,1)} %project.1.refs_0_), channel_id=1, source_target_pairs={{0,2},{1,3},{2,0},{3,1},{4,6},{5,7},{8,10},{9,11},{12,14},{13,15},... | collective-permute-start | bytes 1572872 | tf_op jit(solution)/shard_map/ppermute | solution.py:386
  33.0 13.8 %collective-permute-start = (bf16[512,512]{1,0:T(8,128)(2,1)}, bf16[512,512]{1,0:T(8,128)(2,1)S(1)}, u32[]{:S(2)}, u32[]{:S(2)}) collective-permute-start(bf16[512,512]{1,0:T(8,128)(2,1)} %project.1.refs_0_), channel_id=1, source_target_pairs={{0,4},{1,5},{2,6},{3,7},{4,8},{5,9},{6,10},{7,11},{8,12},{9,13},{1... | collective-permute-start | bytes 1572872 | tf_op jit(solution)/shard_map/ppermute | solution.py:386
  35.9 69.9 %copy-start.5 = (bf16[512,512]{1,0:T(8,128)(2,1)}, bf16[512,512]{1,0:T(8,128)(2,1)S(1)}, u32[]{:S(2)}) copy-start(bf16[512,512]{1,0:T(8,128)(2,1)S(1)} %collective-permute-done.1.refs_1_) | copy-start | bytes 1572868
  35.9 11.6 %collective-permute-start.2 = (bf16[512,512]{1,0:T(8,128)(2,1)S(1)}, bf16[512,512]{1,0:T(8,128)(2,1)S(1)}, u32[]{:S(2)}, u32[]{:S(2)}) collective-permute-start(bf16[512,512]{1,0:T(8,128)(2,1)S(1)} %collective-permute-done.1.refs_1_), channel_id=1, source_target_pairs={{4,8},{5,9},{6,10},{7,11},{8,12},{9,13},{10,14},{11,15},{20,24},{2... | collective-permute-start | bytes 1572872 | tf_op jit(solution)/shard_map/ppermute | solution.py:386
  36.6 10.8 %copy-start.6 = (bf16[512,512]{1,0:T(8,128)(2,1)}, bf16[512,512]{1,0:T(8,128)(2,1)S(1)}, u32[]{:S(2)}) copy-start(bf16[512,512]{1,0:T(8,128)(2,1)S(1)} %collective-permute-done.7.refs_4_) | copy-start | bytes 1572868
  36.6 13.0 %collective-permute-start.8 = (bf16[512,512]{1,0:T(8,128)(2,1)S(1)}, bf16[512,512]{1,0:T(8,128)(2,1)S(1)}, u32[]{:S(2)}, u32[]{:S(2)}) collective-permute-start(bf16[512,512]{1,0:T(8,128)(2,1)S(1)} %collective-permute-done.1.refs_1_), channel_id=1, source_target_pairs={{4,6},{5,7},{6,4},{7,5},{8,10},{9,11},{10,8},{11,9},{12,14},{13,15... | collective-permute-start | bytes 1572872 | tf_op jit(solution)/shard_map/ppermute | solution.py:386
  46.3 70.2 %copy-start = (bf16[512,512]{1,0:T(8,128)(2,1)}, bf16[512,512]{1,0:T(8,128)(2,1)S(1)}, u32[]{:S(2)}) copy-start(bf16[512,512]{1,0:T(8,128)(2,1)S(1)} %collective-permute-done.5.refs_4_) | copy-start | bytes 1572868
  46.8 69.7 %copy-start.2 = (bf16[512,512]{1,0:T(8,128)(2,1)}, bf16[512,512]{1,0:T(8,128)(2,1)S(1)}, u32[]{:S(2)}) copy-start(bf16[512,512]{1,0:T(8,128)(2,1)S(1)} %collective-permute-done.refs_1_) | copy-start | bytes 1572868
  46.8 3.6 %collective-permute-start.6 = (bf16[512,512]{1,0:T(8,128)(2,1)S(1)}, bf16[512,512]{1,0:T(8,128)(2,1)S(1)}, u32[]{:S(2)}, u32[]{:S(2)}) collective-permute-start(bf16[512,512]{1,0:T(8,128)(2,1)S(1)} %collective-permute-done.refs_1_), channel_id=1, source_target_pairs={{4,6},{5,7},{6,4},{7,5},{8,10},{9,11},{10,8},{11,9},{12,14},{13,15... | collective-permute-start | bytes 1572872 | tf_op jit(solution)/shard_map/ppermute | solution.py:386
  47.5 6.0 %copy-start.7 = (bf16[512,512]{1,0:T(8,128)(2,1)}, bf16[512,512]{1,0:T(8,128)(2,1)S(1)}, u32[]{:S(2)}) copy-start(bf16[512,512]{1,0:T(8,128)(2,1)S(1)} %collective-permute-done.2.refs_2_) | copy-start | bytes 1572868
  47.5 2.9 %collective-permute-start.3 = (bf16[512,512]{1,0:T(8,128)(2,1)S(1)}, bf16[512,512]{1,0:T(8,128)(2,1)S(1)}, u32[]{:S(2)}, u32[]{:S(2)}) collective-permute-start(bf16[512,512]{1,0:T(8,128)(2,1)S(1)} %collective-permute-done.refs_1_), channel_id=1, source_target_pairs={{4,8},{5,9},{6,10},{7,11},{8,12},{9,13},{10,14},{11,15},{20,24},{2... | collective-permute-start | bytes 1572872 | tf_op jit(solution)/shard_map/ppermute | solution.py:386
  48.2 2.2 %collective-permute-start.11 = (bf16[512,512]{1,0:T(8,128)(2,1)S(1)}, bf16[512,512]{1,0:T(8,128)(2,1)}, u32[]{:S(2)}, u32[]{:S(2)}) collective-permute-start(bf16[512,512]{1,0:T(8,128)(2,1)S(1)} %collective-permute-done.2.refs_2_), channel_id=1, source_target_pairs={{8,12},{9,13},{10,14},{11,15},{24,28},{25,29},{26,30},{27,31}} | collective-permute-start | bytes 1572872 | tf_op jit(solution)/shard_map/ppermute | solution.py:386
  49.7 0.8 copy-start.8
  49.7 3.8 %collective-permute-start.9 = (bf16[512,512]{1,0:T(8,128)(2,1)S(1)}, bf16[512,512]{1,0:T(8,128)(2,1)S(1)}, u32[]{:S(2)}, u32[]{:S(2)}) collective-permute-start(bf16[512,512]{1,0:T(8,128)(2,1)S(1)} %collective-permute-done.2.refs_2_), channel_id=1, source_target_pairs={{8,10},{9,11},{10,8},{11,9},{12,14},{13,15},{14,12},{15,13},{24,26... | collective-permute-start | bytes 1572872 | tf_op jit(solution)/shard_map/ppermute | solution.py:386
  50.4 66.2 %copy-start.1 = (bf16[512,512]{1,0:T(8,128)(2,1)}, bf16[512,512]{1,0:T(8,128)(2,1)S(1)}, u32[]{:S(2)}) copy-start(bf16[512,512]{1,0:T(8,128)(2,1)S(1)} %collective-permute-done.3.refs_2_) | copy-start | bytes 1572868
  50.4 66.1 %copy-start.3 = (bf16[512,512]{1,0:T(8,128)(2,1)}, bf16[512,512]{1,0:T(8,128)(2,1)S(1)}, u32[]{:S(2)}) copy-start(bf16[512,512]{1,0:T(8,128)(2,1)S(1)} %collective-permute-done.6.refs_5_) | copy-start | bytes 1572868
  50.5 49.9 %collective-permute-start.15 = (bf16[512,512]{1,0:T(8,128)(2,1)}, bf16[512,512]{1,0:T(8,128)(2,1)}, u32[]{:S(2)}, u32[]{:S(2)}) collective-permute-start(bf16[512,512]{1,0:T(8,128)(2,1)} %collective-permute-done.11.refs_3_), channel_id=1, source_target_pairs={{12,14},{13,15},{14,12},{15,13},{28,30},{29,31},{30,28},{31,29}} | collective-permute-start | bytes 1572872 | tf_op jit(solution)/shard_map/ppermute | solution.py:386
  52.8 63.8 %collective-permute-start.13 = (bf16[512,256]{1,0:T(8,128)(2,1)}, bf16[512,256]{1,0:T(8,128)(2,1)S(1)}, u32[]{:S(2)}, u32[]{:S(2)}) collective-permute-start(bf16[512,256]{1,0:T(8,128)(2,1)} %get-tuple-element.31), channel_id=1, source_target_pairs={{8,12},{9,13},{10,14},{11,15},{24,28},{25,29},{26,30},{27,31}} | collective-permute-start | bytes 786440 | tf_op jit(solution)/shard_map/ppermute | solution.py:386
  53.5 0.8 copy-start.9
  54.3 62.3 %collective-permute-start.10 = (bf16[512,512]{1,0:T(8,128)(2,1)S(1)}, bf16[512,512]{1,0:T(8,128)(2,1)S(1)}, u32[]{:S(2)}, u32[]{:S(2)}) collective-permute-start(bf16[512,512]{1,0:T(8,128)(2,1)S(1)} %collective-permute-done.3.refs_2_), channel_id=1, source_target_pairs={{8,10},{9,11},{10,8},{11,9},{12,14},{13,15},{14,12},{15,13},{24,26... | collective-permute-start | bytes 1572872 | tf_op jit(solution)/shard_map/ppermute | solution.py:386
  55.8 60.8 %collective-permute-start.14 = (bf16[512,256]{1,0:T(8,128)(2,1)}, bf16[512,256]{1,0:T(8,128)(2,1)}, u32[]{:S(2)}, u32[]{:S(2)}) collective-permute-start(bf16[512,256]{1,0:T(8,128)(2,1)} %get-tuple-element.29), channel_id=1, source_target_pairs={{0,12},{1,13},{2,14},{3,15},{16,28},{17,29},{18,30},{19,31}} | collective-permute-start | bytes 786440 | tf_op jit(solution)/shard_map/ppermute | solution.py:386
  99.7 25.8 %collective-permute-start.4 = (bf16[512,256]{1,0:T(8,128)(2,1)}, bf16[512,256]{1,0:T(8,128)(2,1)S(1)}, u32[]{:S(2)}, u32[]{:S(2)}) collective-permute-start(bf16[512,256]{1,0:T(8,128)(2,1)} %get-tuple-element.32), channel_id=1, source_target_pairs={{8,12},{9,13},{10,14},{11,15},{24,28},{25,29},{26,30},{27,31}} | collective-permute-start | bytes 786440 | tf_op jit(solution)/shard_map/ppermute | solution.py:386
  100.4 25.1 %collective-permute-start.12 = (bf16[512,256]{1,0:T(8,128)(2,1)}, bf16[512,256]{1,0:T(8,128)(2,1)S(1)}, u32[]{:S(2)}, u32[]{:S(2)}) collective-permute-start(bf16[512,256]{1,0:T(8,128)(2,1)} %get-tuple-element.30), channel_id=1, source_target_pairs={{0,12},{1,13},{2,14},{3,15},{16,28},{17,29},{18,30},{19,31}} | collective-permute-start | bytes 786440 | tf_op jit(solution)/shard_map/ppermute | solution.py:386
  116.6 0.7 copy-start.10
  117.3 0.8 copy-start.4
  125.5 0.7 copy-start.11
  126.2 0.7 copy-start.12

commit v13 on v10

--- a/solution.py
+++ b/solution.py
@@ -14,6 +14,7 @@
 CHUNKS = 4
 LOADS = 8
 UNITS = 2
+BLOCKS_PER_STEP = 4
 
 
 PLAN = (
@@ -211,12 +212,12 @@
 
 def attention_kernel(block, unit, near, slot_ref, cut_ref, odd_ref, q_hbm, *refs):
     own_hbm, straight, crossed = refs[0], refs[1 : near + 1], refs[near + 1 : 2 * near + 2]
-    out_hbm, kv_scr, q_scr, out_scr, even_scr, odd_scr, kv_sem, q_sem, out_sem = refs[-9:]
-    kv_heads, levels, _, width = kv_scr.shape
+    out_hbm, kv_scr, q_scr, out_scr, kv_sem, q_sem, out_sem = refs[-7:]
+    kv_heads, levels, rows, width = kv_scr.shape
     depth = levels - 1
-    blocks, wide = q_scr.shape[0] // kv_heads, q_scr.shape[2]
+    steps, tall, wide = q_scr.shape
+    per_head = steps // kv_heads
     per_group = wide // HEAD_DIM
-    items = kv_heads * blocks
     scale = HEAD_DIM**-0.5 * LOG2E
 
     def load_kv(head):
@@ -235,23 +236,23 @@
             copies.append(copy(ref, level, near + s + 1))
         return copies
 
-    def place(ref, item):
-        head, here = lax.div(item, blocks), lax.rem(item, blocks)
-        rows = pl.ds(pl.multiple_of(here * block, block), block)
+    def place(ref, step):
+        head, part = lax.div(step, per_head), lax.rem(step, per_head)
+        span = pl.ds(pl.multiple_of(part * tall, tall), tall)
         cols = pl.ds(pl.multiple_of((unit * kv_heads + head) * wide, wide), wide)
-        return ref.at[rows, cols]
-
-    def load_q(item):
-        return pltpu.make_async_copy(place(q_hbm, item), q_scr.at[item], q_sem.at[item])
-
-    def store(item):
-        return pltpu.make_async_copy(out_scr.at[item], place(out_hbm, item), out_sem.at[item])
+        return ref.at[span, cols]
+
+    def load_q(step):
+        return pltpu.make_async_copy(place(q_hbm, step), q_scr.at[step], q_sem.at[step])
+
+    def store(step):
+        return pltpu.make_async_copy(out_scr.at[step], place(out_hbm, step), out_sem.at[step])
 
     for head in range(kv_heads):
         for copy in load_kv(head):
             copy.start()
-        for item in range(head * blocks, (head + 1) * blocks):
-            load_q(item).start()
+        for step in range(head * per_head, (head + 1) * per_head):
+            load_q(step).start()
 
     token = lax.broadcasted_iota(jnp.int32, (block, HEAD_DIM), 0)
     lane = lax.broadcasted_iota(jnp.int32, (block, HEAD_DIM), 1)
@@ -260,78 +261,64 @@
     query_mask = jnp.concatenate([query_mask] * per_group, axis=0)
     own_mask = jnp.where(lane - block == token, 1.0, 0.0).astype(jnp.bfloat16)
 
-    def gather(item, cols):
-        head, here = lax.div(item, blocks), lax.rem(item, blocks)
-        pieces = []
-        for k in range(levels):
-            slot = slot_ref[here, k] if k < depth else here
-            rows = pl.ds(pl.multiple_of(slot * block, block), block)
-            pieces.append(kv_scr[head, k, rows, cols])
-        return jnp.concatenate(pieces, axis=0)
-
-    def score(item, score_scr):
-        here = lax.rem(item, blocks)
-        masks = []
+    def score(step, local):
+        head = lax.div(step, per_head)
+        here = lax.rem(step, per_head) * BLOCKS_PER_STEP + local
+        pieces, masks = [], []
         for k in range(depth):
+            span = pl.ds(pl.multiple_of(slot_ref[here, k] * block, block), block)
+            pieces.append(kv_scr[head, k, span, :])
             unseen = (lane == 0) & (token >= cut_ref[here, k])
             masks.append(jnp.where(unseen, MASKED, 0.0).astype(jnp.bfloat16))
+        span = pl.ds(pl.multiple_of(here * block, block), block)
+        pieces.append(kv_scr[head, depth, span, :])
         masks.append(own_mask)
-        keys = jnp.concatenate(
-            [gather(item, slice(0, HEAD_DIM)), jnp.concatenate(masks, axis=0)], axis=1
-        )
+        every = jnp.concatenate(pieces, axis=0)
+        keys = jnp.concatenate([every[:, :HEAD_DIM], jnp.concatenate(masks, axis=0)], axis=1)
+        span = slice(local * block, (local + 1) * block)
         queries = jnp.concatenate(
-            [q_scr[item, :, r * HEAD_DIM : (r + 1) * HEAD_DIM] for r in range(per_group)], axis=0
+            [q_scr[step, span, r * HEAD_DIM : (r + 1) * HEAD_DIM] for r in range(per_group)], axis=0
         )
         queries = jnp.concatenate([queries, query_mask], axis=1)
-        score_scr[...] = lax.dot_general(
+        scores = lax.dot_general(
             queries, keys, (((1,), (1,)), ((), ())), preferred_element_type=jnp.float32
         )
-
-    def finish(item, score_scr):
-        scores = score_scr[...]
+        return scores, every[:, HEAD_DIM:]
+
+    def finish(step, local, scores, values):
         peak = jnp.max(scores, axis=-1, keepdims=True)
         weights = jnp.exp2((scores - peak) * scale).astype(jnp.bfloat16)
-        values = gather(item, slice(HEAD_DIM, 2 * HEAD_DIM))
         padded = jnp.concatenate([values, jnp.ones_like(values)], axis=1)
         both = jnp.dot(weights, padded, preferred_element_type=jnp.float32)
         context = (both[:, :HEAD_DIM] * (1.0 / both[:, HEAD_DIM:])).astype(jnp.bfloat16)
+        span = slice(local * block, (local + 1) * block)
         for r in range(per_group):
-            out_scr[item, :, r * HEAD_DIM : (r + 1) * HEAD_DIM] = context[
+            out_scr[step, span, r * HEAD_DIM : (r + 1) * HEAD_DIM] = context[
                 r * block : (r + 1) * block
             ]
 
-    def arrive(item):
-        @pl.when(item < items)
-        def _():
-            load_q(item).wait()
-
-        for head in range(1, kv_heads):
-
-            @pl.when(item == head * blocks)
+    def body(step, carry):
+        load_q(step).wait()
+        for head in range(kv_heads):
+
+            @pl.when(step == head * per_head)
             def _(head=head):
                 for copy in load_kv(head):
                     copy.wait()
 
-    for copy in load_kv(0):
-        copy.wait()
-    load_q(0).wait()
-    score(0, even_scr)
-
-    def pair(j, carry):
-        item = 2 * j
-        arrive(item + 1)
-        score(item + 1, odd_scr)
-        finish(item, even_scr)
-        store(item).start()
-        arrive(item + 2)
-        score(jnp.minimum(item + 2, items - 1), even_scr)
-        finish(item + 1, odd_scr)
-        store(item + 1).start()
+        waiting = None
+        for local in range(BLOCKS_PER_STEP):
+            scores, values = score(step, local)
+            if waiting is not None:
+                finish(step, *waiting)
+            waiting = (local, scores, values)
+        finish(step, *waiting)
+        store(step).start()
         return carry
 
-    lax.fori_loop(0, items // 2, pair, 0)
-    for item in range(items):
-        store(item).wait()
+    lax.fori_loop(0, steps, body, 0)
+    for step in range(steps):
+        store(step).wait()
 
 
 def attention(slots, cuts, odd, queries, own, straight, crossed, unit, previous):
@@ -341,9 +328,7 @@
     near = len(straight)
     kv_heads = own.shape[1] // (2 * HEAD_DIM)
     wide = features // UNITS // kv_heads
-    keys = (depth + 1) * block
-    tall = wide // HEAD_DIM * block
-    items = kv_heads * blocks
+    steps = kv_heads * blocks // BLOCKS_PER_STEP
     held = pl.BlockSpec(memory_space=pltpu.HBM)
     table = pl.BlockSpec(memory_space=pltpu.SMEM)
     operands = [slots, cuts, odd, queries, own, *straight, *crossed]
@@ -359,19 +344,17 @@
         input_output_aliases=aliases,
         scratch_shapes=[
             pltpu.VMEM((kv_heads, depth + 1, rows, 2 * HEAD_DIM), own.dtype),
-            pltpu.VMEM((items, block, wide), jnp.bfloat16),
-            pltpu.VMEM((items, block, wide), jnp.bfloat16),
-            pltpu.VMEM((tall, keys), jnp.float32),
-            pltpu.VMEM((tall, keys), jnp.float32),
+            pltpu.VMEM((steps, BLOCKS_PER_STEP * block, wide), jnp.bfloat16),
+            pltpu.VMEM((steps, BLOCKS_PER_STEP * block, wide), jnp.bfloat16),
             pltpu.SemaphoreType.DMA((kv_heads, depth + 1)),
-            pltpu.SemaphoreType.DMA((items,)),
-            pltpu.SemaphoreType.DMA((items,)),
+            pltpu.SemaphoreType.DMA((steps,)),
+            pltpu.SemaphoreType.DMA((steps,)),
         ],
         compiler_params=pltpu.CompilerParams(vmem_limit_bytes=57 * MIB),
         cost_estimate=pl.CostEstimate(
-            flops=4 * items * tall * keys * HEAD_DIM,
+            flops=4 * rows * wide * kv_heads * (depth + 1) * block,
             bytes_accessed=8 * MIB,
-            transcendentals=items * tall * keys,
+            transcendentals=rows * wide // HEAD_DIM * kv_heads * (depth + 1) * block,
         ),
         name="attention",
     )(*operands)

time: 120 us -> 117 us (0.975)
  Pallas kernels: 47 us -> 42.8 us
  waiting for transfers between devices: 46.8 us -> 48.8 us
    pallas_call x2, Pallas kernels: 24.3 us -> 20.2 us  [attention(): pl.pallas_call(functools.partial(attention_kernel, block, unit, near), in...]
    ppermute x14, waiting for transfers between devices: 46.8 us -> 48.8 us  [step(): moved[key, s, unit] = lax.ppermute(array, 'node', pairs)]
  transfers between devices with their start and end apart: 14 -> 14, of which waited for: 8 -> 8; matrix products, arithmetic and copies ran while one was open for 1% -> 1% of each run, Pallas kernels for 18% -> 17%
where the time goes in v13:
time: 117 us
  waiting for transfers between devices  48.8 us (42%)
  Pallas kernels  42.8 us (37%)
  starting transfers between devices  24.3 us (21%)
    ppermute x14, waiting for transfers between devices, step(): moved[key, s, unit] = lax.ppermute(array, 'node', pairs)  48.8 us
    ppermute x14, starting transfers between devices, step(): moved[key, s, unit] = lax.ppermute(array, 'node', pairs)  24.3 us
    pallas_call x2, Pallas kernels, attention(): pl.pallas_call(functools.partial(attention_kernel, block, unit, near), in...  20.2 us
    pallas_call x1, Pallas kernels, norm_project(): pl.pallas_call(norm_project_kernel, in_specs=[held, whole, held, held], o...  13.3 us
    pallas_call x1, Pallas kernels, project(): pl.pallas_call(project_kernel, grid=(CHUNKS,), in_specs=[pl.BlockSpec((ro...  9.35 us
  transfers between devices with their start and end apart: 14, of which 8 were waited for; matrix products, arithmetic and copies ran while one was open for 1% of the time, Pallas kernels for 17%

profile of v13, /device:TPU:24, one launch (start us, length us, event | category | flops | bytes accessed | tf_op | source)
XLA Modules:
  0.0 116.9 jit_solution(12507033200971929823)
XLA Ops:
  0.0 13.3 %norm_project.1 = (f32[512,128]{1,0:T(8,128)}, bf16[512,512]{1,0:T(8,128)(2,1)}) custom-call(bf16[512,8192]{1,0:T(8,128)(2,1)} %x_ref.1, f32[8,1,1024]{2,1,0:T(1,128)} %bitcast.3, bf16[8192,512]{1,0:T(8,128)(2,1)} %key_ref.1, bf16[8192,512]{1,0:T(8,128)(2,1)} %value_ref.1), custom_call_target="tpu_custom_call" | custom-call | flops 4294967296 | bytes 16777216 | tf_op jit(solution)/shard_map/norm_project/pallas_call | solution.py:139
  13.3 1.3 %collective-permute-start.1 = (bf16[512,512]{1,0:T(8,128)(2,1)}, bf16[512,512]{1,0:T(8,128)(2,1)S(1)}, u32[]{:S(2)}, u32[]{:S(2)}) collective-permute-start(bf16[512,512]{1,0:T(8,128)(2,1)} %get-tuple-element.18.refs_0_), channel_id=1, source_target_pairs={{0,4},{1,5},{2,6},{3,7},{4,8},{5,9},{6,10},{7,11},{8,12},{9,13},{1... | collective-permute-start | bytes 1572872 | tf_op jit(solution)/shard_map/ppermute | solution.py:400
  14.6 3.5 %collective-permute-start.7 = (bf16[512,512]{1,0:T(8,128)(2,1)}, bf16[512,512]{1,0:T(8,128)(2,1)S(1)}, u32[]{:S(2)}, u32[]{:S(2)}) collective-permute-start(bf16[512,512]{1,0:T(8,128)(2,1)} %get-tuple-element.18.refs_0_), channel_id=1, source_target_pairs={{0,2},{1,3},{4,6},{5,7},{8,10},{9,11},{12,14},{13,15},{16,18},{17,... | collective-permute-start | bytes 1572872 | tf_op jit(solution)/shard_map/ppermute | solution.py:400
  18.1 0.0 copy-start.8
  18.1 9.3 %project.1.refs_0_ = bf16[512,512]{1,0:T(8,128)(2,1)} custom-call(bf16[512,8192]{1,0:T(8,128)(2,1)} %x_ref.1, f32[512,128]{1,0:T(8,128)} %get-tuple-element.17.scale_ref, f32[1,8192]{1,0:T(1,128)} %bitcast.4, bf16[8192,512]{1,0:T(8,128)(2,1)} %key_ref.1, bf16[8192,512]{1,0:T(8,128)(2,1)} %value_ref.1), custom_call_target="tpu_custom_call" | custom-call | flops 4294967296 | bytes 16777216 | tf_op jit(solution)/shard_map/project/pallas_call | solution.py:192
  27.4 1.3 %collective-permute-start.5 = (bf16[512,512]{1,0:T(8,128)(2,1)}, bf16[512,512]{1,0:T(8,128)(2,1)S(1)}, u32[]{:S(2)}, u32[]{:S(2)}) collective-permute-start(bf16[512,512]{1,0:T(8,128)(2,1)} %project.1.refs_0_), channel_id=1, source_target_pairs={{0,2},{1,3},{2,0},{3,1},{4,6},{5,7},{8,10},{9,11},{12,14},{13,15},... | collective-permute-start | bytes 1572872 | tf_op jit(solution)/shard_map/ppermute | solution.py:400
  28.7 1.3 %collective-permute-start = (bf16[512,512]{1,0:T(8,128)(2,1)}, bf16[512,512]{1,0:T(8,128)(2,1)S(1)}, u32[]{:S(2)}, u32[]{:S(2)}) collective-permute-start(bf16[512,512]{1,0:T(8,128)(2,1)} %project.1.refs_0_), channel_id=1, source_target_pairs={{0,4},{1,5},{2,6},{3,7},{4,8},{5,9},{6,10},{7,11},{8,12},{9,13},{1... | collective-permute-start | bytes 1572872 | tf_op jit(solution)/shard_map/ppermute | solution.py:400
  30.0 0.0 collective-permute-done.1.refs_1_
  30.0 0.0 copy-start.2
  30.1 1.3 %collective-permute-start.2 = (bf16[512,512]{1,0:T(8,128)(2,1)S(1)}, bf16[512,512]{1,0:T(8,128)(2,1)S(1)}, u32[]{:S(2)}, u32[]{:S(2)}) collective-permute-start(bf16[512,512]{1,0:T(8,128)(2,1)S(1)} %collective-permute-done.1.refs_1_), channel_id=1, source_target_pairs={{4,8},{5,9},{6,10},{7,11},{8,12},{9,13},{10,14},{11,15},{20,24},{2... | collective-permute-start | bytes 1572872 | tf_op jit(solution)/shard_map/ppermute | solution.py:400
  31.4 0.0 collective-permute-done.7.refs_4_
  31.4 0.0 copy-start.3
  31.4 2.9 %collective-permute-start.8 = (bf16[512,512]{1,0:T(8,128)(2,1)S(1)}, bf16[512,512]{1,0:T(8,128)(2,1)S(1)}, u32[]{:S(2)}, u32[]{:S(2)}) collective-permute-start(bf16[512,512]{1,0:T(8,128)(2,1)S(1)} %collective-permute-done.1.refs_1_), channel_id=1, source_target_pairs={{4,6},{5,7},{6,4},{7,5},{8,10},{9,11},{10,8},{11,9},{12,14},{13,15... | collective-permute-start | bytes 1572872 | tf_op jit(solution)/shard_map/ppermute | solution.py:400
  34.3 7.1 %collective-permute-done.5.refs_4_ = bf16[512,512]{1,0:T(8,128)(2,1)S(1)} collective-permute-done((bf16[512,512]{1,0:T(8,128)(2,1)}, bf16[512,512]{1,0:T(8,128)(2,1)S(1)}, u32[]{:S(2)}, u32[]{:S(2)}) %collective-permute-start.5) | collective-permute-done | bytes 524320 | tf_op jit(solution)/shard_map/ppermute | solution.py:400
  41.3 0.0 copy-start
  41.3 5.0 %collective-permute-done.refs_1_ = bf16[512,512]{1,0:T(8,128)(2,1)S(1)} collective-permute-done((bf16[512,512]{1,0:T(8,128)(2,1)}, bf16[512,512]{1,0:T(8,128)(2,1)S(1)}, u32[]{:S(2)}, u32[]{:S(2)}) %collective-permute-start) | collective-permute-done | bytes 524320 | tf_op jit(solution)/shard_map/ppermute | solution.py:400
  46.3 1.9 %collective-permute-start.6 = (bf16[512,512]{1,0:T(8,128)(2,1)S(1)}, bf16[512,512]{1,0:T(8,128)(2,1)S(1)}, u32[]{:S(2)}, u32[]{:S(2)}) collective-permute-start(bf16[512,512]{1,0:T(8,128)(2,1)S(1)} %collective-permute-done.refs_1_), channel_id=1, source_target_pairs={{4,6},{5,7},{6,4},{7,5},{8,10},{9,11},{10,8},{11,9},{12,14},{13,15... | collective-permute-start | bytes 1572872 | tf_op jit(solution)/shard_map/ppermute | solution.py:400
  48.2 7.8 %collective-permute-done.2.refs_2_ = bf16[512,512]{1,0:T(8,128)(2,1)S(1)} collective-permute-done((bf16[512,512]{1,0:T(8,128)(2,1)S(1)}, bf16[512,512]{1,0:T(8,128)(2,1)S(1)}, u32[]{:S(2)}, u32[]{:S(2)}) %collective-permute-start.2) | collective-permute-done | bytes 524320 | tf_op jit(solution)/shard_map/ppermute | solution.py:400
  56.1 1.3 %collective-permute-start.11 = (bf16[512,512]{1,0:T(8,128)(2,1)S(1)}, bf16[512,512]{1,0:T(8,128)(2,1)}, u32[]{:S(2)}, u32[]{:S(2)}) collective-permute-start(bf16[512,512]{1,0:T(8,128)(2,1)S(1)} %collective-permute-done.2.refs_2_), channel_id=1, source_target_pairs={{8,12},{9,13},{10,14},{11,15},{24,28},{25,29},{26,30},{27,31}} | collective-permute-start | bytes 1572872 | tf_op jit(solution)/shard_map/ppermute | solution.py:400
  57.4 1.3 %collective-permute-start.3 = (bf16[512,512]{1,0:T(8,128)(2,1)S(1)}, bf16[512,512]{1,0:T(8,128)(2,1)}, u32[]{:S(2)}, u32[]{:S(2)}) collective-permute-start(bf16[512,512]{1,0:T(8,128)(2,1)S(1)} %collective-permute-done.refs_1_), channel_id=1, source_target_pairs={{4,8},{5,9},{6,10},{7,11},{8,12},{9,13},{10,14},{11,15},{20,24},{2... | collective-permute-start | bytes 1572872 | tf_op jit(solution)/shard_map/ppermute | solution.py:400
  58.7 0.0 collective-permute-done.8.refs_5_
  58.7 0.0 copy-start.6
  58.7 1.9 %collective-permute-start.9 = (bf16[512,512]{1,0:T(8,128)(2,1)S(1)}, bf16[512,512]{1,0:T(8,128)(2,1)S(1)}, u32[]{:S(2)}, u32[]{:S(2)}) collective-permute-start(bf16[512,512]{1,0:T(8,128)(2,1)S(1)} %collective-permute-done.2.refs_2_), channel_id=1, source_target_pairs={{8,10},{9,11},{10,8},{11,9},{12,14},{13,15},{14,12},{15,13},{24,26... | collective-permute-start | bytes 1572872 | tf_op jit(solution)/shard_map/ppermute | solution.py:400
  60.6 3.1 %collective-permute-done.6.refs_5_ = bf16[512,512]{1,0:T(8,128)(2,1)S(1)} collective-permute-done((bf16[512,512]{1,0:T(8,128)(2,1)S(1)}, bf16[512,512]{1,0:T(8,128)(2,1)S(1)}, u32[]{:S(2)}, u32[]{:S(2)}) %collective-permute-start.6) | collective-permute-done | bytes 524320 | tf_op jit(solution)/shard_map/ppermute | solution.py:400
  63.7 9.2 %collective-permute-done.11.refs_3_ = bf16[512,512]{1,0:T(8,128)(2,1)} collective-permute-done((bf16[512,512]{1,0:T(8,128)(2,1)S(1)}, bf16[512,512]{1,0:T(8,128)(2,1)}, u32[]{:S(2)}, u32[]{:S(2)}) %collective-permute-start.11) | collective-permute-done | bytes 524320 | tf_op jit(solution)/shard_map/ppermute | solution.py:400
  72.9 1.9 %collective-permute-start.13 = (bf16[512,512]{1,0:T(8,128)(2,1)}, bf16[512,512]{1,0:T(8,128)(2,1)}, u32[]{:S(2)}, u32[]{:S(2)}) collective-permute-start(bf16[512,512]{1,0:T(8,128)(2,1)} %collective-permute-done.11.refs_3_), channel_id=1, source_target_pairs={{12,14},{13,15},{14,12},{15,13},{28,30},{29,31},{30,28},{31,29}} | collective-permute-start | bytes 1572872 | tf_op jit(solution)/shard_map/ppermute | solution.py:400
  74.8 6.9 %collective-permute-done.3.refs_2_ = bf16[512,512]{1,0:T(8,128)(2,1)} collective-permute-done((bf16[512,512]{1,0:T(8,128)(2,1)S(1)}, bf16[512,512]{1,0:T(8,128)(2,1)}, u32[]{:S(2)}, u32[]{:S(2)}) %collective-permute-start.3) | collective-permute-done | bytes 524320 | tf_op jit(solution)/shard_map/ppermute | solution.py:400
  81.8 1.3 %collective-permute-start.4 = (bf16[512,512]{1,0:T(8,128)(2,1)}, bf16[512,512]{1,0:T(8,128)(2,1)}, u32[]{:S(2)}, u32[]{:S(2)}) collective-permute-start(bf16[512,512]{1,0:T(8,128)(2,1)} %collective-permute-done.3.refs_2_), channel_id=1, source_target_pairs={{8,12},{9,13},{10,14},{11,15},{24,28},{25,29},{26,30},{27,31}} | collective-permute-start | bytes 1572872 | tf_op jit(solution)/shard_map/ppermute | solution.py:400
  83.1 0.0 collective-permute-done.9.refs_6_
  83.1 0.0 copy-done.6
  83.1 0.0 copy-start.7
  83.1 1.9 %collective-permute-start.10 = (bf16[512,512]{1,0:T(8,128)(2,1)}, bf16[512,512]{1,0:T(8,128)(2,1)}, u32[]{:S(2)}, u32[]{:S(2)}) collective-permute-start(bf16[512,512]{1,0:T(8,128)(2,1)} %collective-permute-done.3.refs_2_), channel_id=1, source_target_pairs={{8,10},{9,11},{10,8},{11,9},{12,14},{13,15},{14,12},{15,13},{24,26... | collective-permute-start | bytes 1572872 | tf_op jit(solution)/shard_map/ppermute | solution.py:400
  85.0 0.0 copy-done.7
  85.0 1.3 %collective-permute-start.12 = (bf16[512,512]{1,0:T(8,128)(2,1)S(1)}, bf16[512,512]{1,0:T(8,128)(2,1)}, u32[]{:S(2)}, u32[]{:S(2)}) collective-permute-start(bf16[512,512]{1,0:T(8,128)(2,1)S(1)} %collective-permute-done.5.refs_4_), channel_id=1, source_target_pairs={{0,12},{1,13},{2,14},{3,15},{16,28},{17,29},{18,30},{19,31}} | collective-permute-start | bytes 1572872 | tf_op jit(solution)/shard_map/ppermute | solution.py:400
  86.4 0.0 copy-done.8
  86.4 0.6 fusion.1.slot_ref
  87.0 0.6 collective-permute-done.13.refs_7_
  87.5 0.0 copy-done.2
  87.5 0.0 copy-done.3
  87.5 0.0 copy-done.5
  87.5 10.1 %attention.2.refs_8_ = bf16[512,4096]{1,0:T(8,128)(2,1)} custom-call(s32[8,7]{1,0:T(8,128)} %fusion.1.slot_ref, s32[8,7]{1,0:T(8,128)} %cut_ref.3, s32[1]{0:T(128)} %bitcast.odd_ref, bf16[512,4096]{1,0:T(8,128)(2,1)} %q_hbm.3, bf16[512,512]{1,0:T(8,128)(2,1)} %get-tuple-element.18.refs_0_, bf16[512,512]{1,0:T(8,128)(2,1)} %copy-done.2, ...), custom_call_target="tpu_custom_call" | custom-call | flops 2147483648 | bytes 8388608 | tf_op jit(solution)/shard_map/attention/pallas_call | solution.py:339
  97.6 9.1 %collective-permute-done.4.refs_3_ = bf16[512,512]{1,0:T(8,128)(2,1)} collective-permute-done((bf16[512,512]{1,0:T(8,128)(2,1)}, bf16[512,512]{1,0:T(8,128)(2,1)}, u32[]{:S(2)}, u32[]{:S(2)}) %collective-permute-start.4) | collective-permute-done | bytes 524320 | tf_op jit(solution)/shard_map/ppermute | solution.py:400
  106.8 0.0 collective-permute-done.10.refs_6_
  106.8 0.0 collective-permute-done.12.refs_7_
  106.8 0.0 copy-done
  106.8 0.0 copy-done.1
  106.8 0.0 copy-done.4
  106.8 10.1 %attention.3 = bf16[512,4096]{1,0:T(8,128)(2,1)} custom-call(s32[8,7]{1,0:T(8,128)} %fusion.1.slot_ref, s32[8,7]{1,0:T(8,128)} %cut_ref.3, s32[1]{0:T(128)} %bitcast.odd_ref, bf16[512,4096]{1,0:T(8,128)(2,1)} %q_hbm.3, bf16[512,512]{1,0:T(8,128)(2,1)} %project.1.refs_0_, bf16[512,512]{1,0:T(8,128)(2,1)} %copy-done.1, ...), custom_call_target="tpu_custom_call", output_to_operand_aliasing={{}: (12, {})} | custom-call | flops 2147483648 | bytes 8388608 | tf_op jit(solution)/shard_map/attention/pallas_call | solution.py:339
  (3 shorter events, 0.0 us)
Async XLA Ops:
  13.3 16.7 %collective-permute-start.1 = (bf16[512,512]{1,0:T(8,128)(2,1)}, bf16[512,512]{1,0:T(8,128)(2,1)S(1)}, u32[]{:S(2)}, u32[]{:S(2)}) collective-permute-start(bf16[512,512]{1,0:T(8,128)(2,1)} %get-tuple-element.18.refs_0_), channel_id=1, source_target_pairs={{0,4},{1,5},{2,6},{3,7},{4,8},{5,9},{6,10},{7,11},{8,12},{9,13},{1... | collective-permute-start | bytes 1572872 | tf_op jit(solution)/shard_map/ppermute | solution.py:400
  14.6 16.8 %collective-permute-start.7 = (bf16[512,512]{1,0:T(8,128)(2,1)}, bf16[512,512]{1,0:T(8,128)(2,1)S(1)}, u32[]{:S(2)}, u32[]{:S(2)}) collective-permute-start(bf16[512,512]{1,0:T(8,128)(2,1)} %get-tuple-element.18.refs_0_), channel_id=1, source_target_pairs={{0,2},{1,3},{4,6},{5,7},{8,10},{9,11},{12,14},{13,15},{16,18},{17,... | collective-permute-start | bytes 1572872 | tf_op jit(solution)/shard_map/ppermute | solution.py:400
  18.1 68.3 %copy-start.8 = (s32[8,7]{1,0:T(8,128)S(1)}, s32[8,7]{1,0:T(8,128)}, u32[]{:S(2)}) copy-start(s32[8,7]{1,0:T(8,128)} %param.12) | copy-start | bytes 676
  27.4 13.9 %collective-permute-start.5 = (bf16[512,512]{1,0:T(8,128)(2,1)}, bf16[512,512]{1,0:T(8,128)(2,1)S(1)}, u32[]{:S(2)}, u32[]{:S(2)}) collective-permute-start(bf16[512,512]{1,0:T(8,128)(2,1)} %project.1.refs_0_), channel_id=1, source_target_pairs={{0,2},{1,3},{2,0},{3,1},{4,6},{5,7},{8,10},{9,11},{12,14},{13,15},... | collective-permute-start | bytes 1572872 | tf_op jit(solution)/shard_map/ppermute | solution.py:400
  28.7 17.6 %collective-permute-start = (bf16[512,512]{1,0:T(8,128)(2,1)}, bf16[512,512]{1,0:T(8,128)(2,1)S(1)}, u32[]{:S(2)}, u32[]{:S(2)}) collective-permute-start(bf16[512,512]{1,0:T(8,128)(2,1)} %project.1.refs_0_), channel_id=1, source_target_pairs={{0,4},{1,5},{2,6},{3,7},{4,8},{5,9},{6,10},{7,11},{8,12},{9,13},{1... | collective-permute-start | bytes 1572872 | tf_op jit(solution)/shard_map/ppermute | solution.py:400
  30.0 57.5 %copy-start.2 = (bf16[512,512]{1,0:T(8,128)(2,1)}, bf16[512,512]{1,0:T(8,128)(2,1)S(1)}, u32[]{:S(2)}) copy-start(bf16[512,512]{1,0:T(8,128)(2,1)S(1)} %collective-permute-done.1.refs_1_) | copy-start | bytes 1572868
  30.1 26.0 %collective-permute-start.2 = (bf16[512,512]{1,0:T(8,128)(2,1)S(1)}, bf16[512,512]{1,0:T(8,128)(2,1)S(1)}, u32[]{:S(2)}, u32[]{:S(2)}) collective-permute-start(bf16[512,512]{1,0:T(8,128)(2,1)S(1)} %collective-permute-done.1.refs_1_), channel_id=1, source_target_pairs={{4,8},{5,9},{6,10},{7,11},{8,12},{9,13},{10,14},{11,15},{20,24},{2... | collective-permute-start | bytes 1572872 | tf_op jit(solution)/shard_map/ppermute | solution.py:400
  31.4 56.2 %copy-start.3 = (bf16[512,512]{1,0:T(8,128)(2,1)}, bf16[512,512]{1,0:T(8,128)(2,1)S(1)}, u32[]{:S(2)}) copy-start(bf16[512,512]{1,0:T(8,128)(2,1)S(1)} %collective-permute-done.7.refs_4_) | copy-start | bytes 1572868
  31.4 27.3 %collective-permute-start.8 = (bf16[512,512]{1,0:T(8,128)(2,1)S(1)}, bf16[512,512]{1,0:T(8,128)(2,1)S(1)}, u32[]{:S(2)}, u32[]{:S(2)}) collective-permute-start(bf16[512,512]{1,0:T(8,128)(2,1)S(1)} %collective-permute-done.1.refs_1_), channel_id=1, source_target_pairs={{4,6},{5,7},{6,4},{7,5},{8,10},{9,11},{10,8},{11,9},{12,14},{13,15... | collective-permute-start | bytes 1572872 | tf_op jit(solution)/shard_map/ppermute | solution.py:400
  41.3 65.4 %copy-start = (bf16[512,512]{1,0:T(8,128)(2,1)}, bf16[512,512]{1,0:T(8,128)(2,1)S(1)}, u32[]{:S(2)}) copy-start(bf16[512,512]{1,0:T(8,128)(2,1)S(1)} %collective-permute-done.5.refs_4_) | copy-start | bytes 1572868
  46.3 60.5 %copy-start.1 = (bf16[512,512]{1,0:T(8,128)(2,1)}, bf16[512,512]{1,0:T(8,128)(2,1)S(1)}, u32[]{:S(2)}) copy-start(bf16[512,512]{1,0:T(8,128)(2,1)S(1)} %collective-permute-done.refs_1_) | copy-start | bytes 1572868
  46.3 17.4 %collective-permute-start.6 = (bf16[512,512]{1,0:T(8,128)(2,1)S(1)}, bf16[512,512]{1,0:T(8,128)(2,1)S(1)}, u32[]{:S(2)}, u32[]{:S(2)}) collective-permute-start(bf16[512,512]{1,0:T(8,128)(2,1)S(1)} %collective-permute-done.refs_1_), channel_id=1, source_target_pairs={{4,6},{5,7},{6,4},{7,5},{8,10},{9,11},{10,8},{11,9},{12,14},{13,15... | collective-permute-start | bytes 1572872 | tf_op jit(solution)/shard_map/ppermute | solution.py:400
  56.1 31.5 %copy-start.5 = (bf16[512,512]{1,0:T(8,128)(2,1)}, bf16[512,512]{1,0:T(8,128)(2,1)S(1)}, u32[]{:S(2)}) copy-start(bf16[512,512]{1,0:T(8,128)(2,1)S(1)} %collective-permute-done.2.refs_2_) | copy-start | bytes 1572868
  56.1 16.8 %collective-permute-start.11 = (bf16[512,512]{1,0:T(8,128)(2,1)S(1)}, bf16[512,512]{1,0:T(8,128)(2,1)}, u32[]{:S(2)}, u32[]{:S(2)}) collective-permute-start(bf16[512,512]{1,0:T(8,128)(2,1)S(1)} %collective-permute-done.2.refs_2_), channel_id=1, source_target_pairs={{8,12},{9,13},{10,14},{11,15},{24,28},{25,29},{26,30},{27,31}} | collective-permute-start | bytes 1572872 | tf_op jit(solution)/shard_map/ppermute | solution.py:400
  57.4 24.4 %collective-permute-start.3 = (bf16[512,512]{1,0:T(8,128)(2,1)S(1)}, bf16[512,512]{1,0:T(8,128)(2,1)}, u32[]{:S(2)}, u32[]{:S(2)}) collective-permute-start(bf16[512,512]{1,0:T(8,128)(2,1)S(1)} %collective-permute-done.refs_1_), channel_id=1, source_target_pairs={{4,8},{5,9},{6,10},{7,11},{8,12},{9,13},{10,14},{11,15},{20,24},{2... | collective-permute-start | bytes 1572872 | tf_op jit(solution)/shard_map/ppermute | solution.py:400
  58.7 24.4 %copy-start.6 = (bf16[512,512]{1,0:T(8,128)(2,1)}, bf16[512,512]{1,0:T(8,128)(2,1)S(1)}, u32[]{:S(2)}) copy-start(bf16[512,512]{1,0:T(8,128)(2,1)S(1)} %collective-permute-done.8.refs_5_) | copy-start | bytes 1572868
  58.7 24.4 %collective-permute-start.9 = (bf16[512,512]{1,0:T(8,128)(2,1)S(1)}, bf16[512,512]{1,0:T(8,128)(2,1)S(1)}, u32[]{:S(2)}, u32[]{:S(2)}) collective-permute-start(bf16[512,512]{1,0:T(8,128)(2,1)S(1)} %collective-permute-done.2.refs_2_), channel_id=1, source_target_pairs={{8,10},{9,11},{10,8},{11,9},{12,14},{13,15},{14,12},{15,13},{24,26... | collective-permute-start | bytes 1572872 | tf_op jit(solution)/shard_map/ppermute | solution.py:400
  63.7 43.1 %copy-start.4 = (bf16[512,512]{1,0:T(8,128)(2,1)}, bf16[512,512]{1,0:T(8,128)(2,1)S(1)}, u32[]{:S(2)}) copy-start(bf16[512,512]{1,0:T(8,128)(2,1)S(1)} %collective-permute-done.6.refs_5_) | copy-start | bytes 1572868
  72.9 14.6 %collective-permute-start.13 = (bf16[512,512]{1,0:T(8,128)(2,1)}, bf16[512,512]{1,0:T(8,128)(2,1)}, u32[]{:S(2)}, u32[]{:S(2)}) collective-permute-start(bf16[512,512]{1,0:T(8,128)(2,1)} %collective-permute-done.11.refs_3_), channel_id=1, source_target_pairs={{12,14},{13,15},{14,12},{15,13},{28,30},{29,31},{30,28},{31,29}} | collective-permute-start | bytes 1572872 | tf_op jit(solution)/shard_map/ppermute | solution.py:400
  81.8 25.0 %collective-permute-start.4 = (bf16[512,512]{1,0:T(8,128)(2,1)}, bf16[512,512]{1,0:T(8,128)(2,1)}, u32[]{:S(2)}, u32[]{:S(2)}) collective-permute-start(bf16[512,512]{1,0:T(8,128)(2,1)} %collective-permute-done.3.refs_2_), channel_id=1, source_target_pairs={{8,12},{9,13},{10,14},{11,15},{24,28},{25,29},{26,30},{27,31}} | collective-permute-start | bytes 1572872 | tf_op jit(solution)/shard_map/ppermute | solution.py:400
  83.1 1.9 %copy-start.7 = (bf16[512,512]{1,0:T(8,128)(2,1)}, bf16[512,512]{1,0:T(8,128)(2,1)S(1)}, u32[]{:S(2)}) copy-start(bf16[512,512]{1,0:T(8,128)(2,1)S(1)} %collective-permute-done.9.refs_6_) | copy-start | bytes 1572868
  83.1 23.7 %collective-permute-start.10 = (bf16[512,512]{1,0:T(8,128)(2,1)}, bf16[512,512]{1,0:T(8,128)(2,1)}, u32[]{:S(2)}, u32[]{:S(2)}) collective-permute-start(bf16[512,512]{1,0:T(8,128)(2,1)} %collective-permute-done.3.refs_2_), channel_id=1, source_target_pairs={{8,10},{9,11},{10,8},{11,9},{12,14},{13,15},{14,12},{15,13},{24,26... | collective-permute-start | bytes 1572872 | tf_op jit(solution)/shard_map/ppermute | solution.py:400
  85.0 21.7 %collective-permute-start.12 = (bf16[512,512]{1,0:T(8,128)(2,1)S(1)}, bf16[512,512]{1,0:T(8,128)(2,1)}, u32[]{:S(2)}, u32[]{:S(2)}) collective-permute-start(bf16[512,512]{1,0:T(8,128)(2,1)S(1)} %collective-permute-done.5.refs_4_), channel_id=1, source_target_pairs={{0,12},{1,13},{2,14},{3,15},{16,28},{17,29},{18,30},{19,31}} | collective-permute-start | bytes 1572872 | tf_op jit(solution)/shard_map/ppermute | solution.py:400

commit v14 on v13

--- a/solution.py
+++ b/solution.py
@@ -27,11 +27,11 @@
     ("across", 1, 1, (("across", 0, 1),)),
     ("along", 3, 0, (("along", 1, 1),)),
     ("across", 2, 0, (("across", 1, 0),)),
-    ("along", 2, 1, (("along", 2, 0),)),
+    ("along", 2, 1, (("along", 2, 0), ("across", 1, 0))),
     ("across", 3, 0, (("across", 1, 1),)),
     ("across", 2, 1, (("across", 2, 0),)),
-    ("down", 3, 1, (("along", 3, 0), ("across", 2, 0))),
     ("along", 3, 1, (("along", 2, 1),)),
+    ("down", 3, 1, (("along", 3, 0), ("across", 2, 0), ("along", 2, 1))),
 )
 
 
@@ -39,7 +39,8 @@
     x_hbm, gain_ref, key_hbm, value_hbm, scale_ref, kv_ref,
     x_scr, weight_scr, even_scr, odd_scr, acc_scr, x_sem, key_sem, value_sem,
 ):
-    loads, rows, chunk = x_scr.shape
+    loads, rows, piece = x_scr.shape
+    chunks, chunk = weight_scr.shape[:2]
     width = weight_scr.shape[2] // 2
     lanes = 128
     band = 128
@@ -48,7 +49,8 @@
         return pl.ds(pl.multiple_of(c * chunk, chunk), chunk)
 
     def load_x(c):
-        return pltpu.make_async_copy(x_hbm.at[:, span(c)], x_scr.at[c], x_sem.at[c])
+        cols = pl.ds(pl.multiple_of(c * piece, piece), piece)
+        return pltpu.make_async_copy(x_hbm.at[:, cols], x_scr.at[c], x_sem.at[c])
 
     def load_weights(c):
         head = pl.ds(0, width)
@@ -68,23 +70,25 @@
     def square(c, carry):
         load_x(c).wait()
 
-        @pl.when(c >= loads // 2)
+        @pl.when(c == loads - 2)
         def _():
-            for part in range(2):
-                for copy in load_weights(2 * (c - loads // 2) + part):
-                    copy.start()
+            for copy in load_weights(0):
+                copy.start()
 
         for first in range(0, rows, band):
             row = slice(first, first + band)
             total = scale_ref[row, :]
-            for lane in range(0, chunk, lanes):
+            for lane in range(0, piece, lanes):
                 x = x_scr[c, row, lane : lane + lanes].astype(jnp.float32)
                 total += x * x
             scale_ref[row, :] = total
         return carry
 
     lax.fori_loop(0, loads, square, 0)
-    mean_sq = jnp.sum(scale_ref[...], axis=-1, keepdims=True) / (loads * chunk)
+    for c in range(1, chunks):
+        for copy in load_weights(c):
+            copy.start()
+    mean_sq = jnp.sum(scale_ref[...], axis=-1, keepdims=True) / (loads * piece)
     scale_ref[...] = jnp.broadcast_to(lax.rsqrt(mean_sq + EPS), scale_ref.shape)
 
     def normalise(normed_scr, c):
@@ -92,32 +96,29 @@
             row = slice(first, first + band)
             inverse = scale_ref[row, :]
             for lane in range(0, chunk, lanes):
-                cols = slice(lane, lane + lanes)
-                x = x_scr[c, row, cols].astype(jnp.float32)
-                gain = gain_ref[c, :, cols]
-                normed_scr[row, cols] = (x * inverse * gain).astype(jnp.bfloat16)
+                index, inner = c * (chunk // piece) + lane // piece, lane % piece
+                x = x_scr[index, row, inner : inner + lanes].astype(jnp.float32)
+                gain = gain_ref[index, :, inner : inner + lanes]
+                normed_scr[row, lane : lane + lanes] = (x * inverse * gain).astype(jnp.bfloat16)
 
     def multiply(normed_scr, c):
         for copy in load_weights(c):
             copy.wait()
-        acc_scr[...] += jnp.dot(
-            normed_scr[...], weight_scr[c], preferred_element_type=jnp.float32
-        )
+        return jnp.dot(normed_scr[...], weight_scr[c], preferred_element_type=jnp.float32)
 
     normalise(even_scr, 0)
-    acc_scr[...] = jnp.zeros_like(acc_scr)
+    acc_scr[...] = multiply(even_scr, 0)
+    normalise(odd_scr, 1)
 
     def pair(p, carry):
-        multiply(even_scr, 2 * p)
-        normalise(odd_scr, 2 * p + 1)
-        multiply(odd_scr, 2 * p + 1)
+        acc_scr[...] += multiply(odd_scr, 2 * p + 1)
         normalise(even_scr, 2 * p + 2)
+        acc_scr[...] += multiply(even_scr, 2 * p + 2)
+        normalise(odd_scr, 2 * p + 3)
         return carry
 
-    lax.fori_loop(0, loads // 2 - 1, pair, 0)
-    multiply(even_scr, loads - 2)
-    normalise(odd_scr, loads - 1)
-    multiply(odd_scr, loads - 1)
+    lax.fori_loop(0, chunks // 2 - 1, pair, 0)
+    acc_scr[...] += multiply(odd_scr, chunks - 1)
     write_heads(kv_ref, acc_scr)
 
 
@@ -133,7 +134,8 @@
 def norm_project(hidden, gain, key_weight, value_weight):
     rows, features = hidden.shape
     width = key_weight.shape[1] // UNITS
-    chunk = features // LOADS
+    piece = features // LOADS
+    chunk = features // CHUNKS
     whole = pl.BlockSpec(memory_space=pltpu.VMEM)
     held = pl.BlockSpec(memory_space=pltpu.HBM)
     return pl.pallas_call(
@@ -145,21 +147,21 @@
             jax.ShapeDtypeStruct((rows, 2 * width), jnp.bfloat16),
         ],
         scratch_shapes=[
-            pltpu.VMEM((LOADS, rows, chunk), jnp.bfloat16),
-            pltpu.VMEM((LOADS, chunk, 2 * width), jnp.bfloat16),
+            pltpu.VMEM((LOADS, rows, piece), jnp.bfloat16),
+            pltpu.VMEM((CHUNKS, chunk, 2 * width), jnp.bfloat16),
             pltpu.VMEM((rows, chunk), jnp.bfloat16),
             pltpu.VMEM((rows, chunk), jnp.bfloat16),
             pltpu.VMEM((rows, 2 * width), jnp.float32),
             pltpu.SemaphoreType.DMA((LOADS,)),
-            pltpu.SemaphoreType.DMA((LOADS,)),
-            pltpu.SemaphoreType.DMA((LOADS,)),
+            pltpu.SemaphoreType.DMA((CHUNKS,)),
+            pltpu.SemaphoreType.DMA((CHUNKS,)),
         ],
         compiler_params=pltpu.CompilerParams(vmem_limit_bytes=57 * MIB),
         cost_estimate=pl.CostEstimate(
             flops=4 * rows * features * width, bytes_accessed=16 * MIB, transcendentals=0
         ),
         name="norm_project",
-    )(hidden, gain.reshape(LOADS, 1, chunk), key_weight, value_weight)
+    )(hidden, gain.reshape(LOADS, 1, piece), key_weight, value_weight)
 
 
 def project_kernel(x_ref, scale_ref, gain_ref, key_ref, value_ref, kv_ref, acc_scr):
@@ -210,7 +212,7 @@
     )(hidden, scale, gain.reshape(1, features), key_weight, value_weight)
 
 
-def attention_kernel(block, unit, near, slot_ref, cut_ref, odd_ref, q_hbm, *refs):
+def attention_kernel(block, head_from, near, skip, slot_ref, cut_ref, odd_ref, q_hbm, *refs):
     own_hbm, straight, crossed = refs[0], refs[1 : near + 1], refs[near + 1 : 2 * near + 2]
     out_hbm, kv_scr, q_scr, out_scr, kv_sem, q_sem, out_sem = refs[-7:]
     kv_heads, levels, rows, width = kv_scr.shape
@@ -222,10 +224,9 @@
 
     def load_kv(head):
         def copy(ref, level, number):
+            first = 0 if ref.shape[1] == width else (skip + head) * width
             return pltpu.make_async_copy(
-                ref.at[:, head * width : (head + 1) * width],
-                kv_scr.at[head, level],
-                kv_sem.at[head, number],
+                ref.at[:, first : first + width], kv_scr.at[head, level], kv_sem.at[head, number]
             )
 
         copies = [copy(own_hbm, depth, 0)]
@@ -239,7 +240,7 @@
     def place(ref, step):
         head, part = lax.div(step, per_head), lax.rem(step, per_head)
         span = pl.ds(pl.multiple_of(part * tall, tall), tall)
-        cols = pl.ds(pl.multiple_of((unit * kv_heads + head) * wide, wide), wide)
+        cols = pl.ds(pl.multiple_of((head_from + head) * wide, wide), wide)
         return ref.at[span, cols]
 
     def load_q(step):
@@ -321,13 +322,13 @@
         store(step).wait()
 
 
-def attention(slots, cuts, odd, queries, own, straight, crossed, unit, previous):
+def attention(slots, cuts, odd, queries, own, straight, crossed, unit, skip, kv_heads, previous):
     rows, features = queries.shape
     blocks, depth = slots.shape
     block = rows // blocks
     near = len(straight)
-    kv_heads = own.shape[1] // (2 * HEAD_DIM)
-    wide = features // UNITS // kv_heads
+    per_unit = own.shape[1] // (2 * HEAD_DIM)
+    wide = features // UNITS // per_unit
     steps = kv_heads * blocks // BLOCKS_PER_STEP
     held = pl.BlockSpec(memory_space=pltpu.HBM)
     table = pl.BlockSpec(memory_space=pltpu.SMEM)
@@ -337,7 +338,7 @@
         aliases = {len(operands): 0}
         operands.append(previous)
     return pl.pallas_call(
-        functools.partial(attention_kernel, block, unit, near),
+        functools.partial(attention_kernel, block, unit * per_unit + skip, near, skip),
         in_specs=[table] * 3 + [held] * (len(operands) - 3),
         out_specs=held,
         out_shape=jax.ShapeDtypeStruct((rows, features), jnp.bfloat16),
@@ -353,7 +354,7 @@
         compiler_params=pltpu.CompilerParams(vmem_limit_bytes=57 * MIB),
         cost_estimate=pl.CostEstimate(
             flops=4 * rows * wide * kv_heads * (depth + 1) * block,
-            bytes_accessed=8 * MIB,
+            bytes_accessed=4 * kv_heads * MIB,
             transcendentals=rows * wide // HEAD_DIM * kv_heads * (depth + 1) * block,
         ),
         name="attention",
@@ -378,41 +379,51 @@
         return lax.optimization_barrier((array, *earlier))[0]
 
     column = 2 * chains
+    per_unit = key_weight.shape[1] // HEAD_DIM // UNITS
+    width = 2 * HEAD_DIM
     moved = {("own", 0, 0): own[0], ("own", 0, 1): own[1]}
 
     def step(kind, s, unit, waits):
         if kind == "across":
             source = ("along", s, unit) if s else ("own", 0, unit)
-            exchange = s > 0 or unit == UNITS - 1
+            exchange = unit == UNITS - 1
             pairs = [
                 (i, other[i])
                 for i in range(size)
-                if half[i] >= s and (even[i] or (exchange and half[i] == 0) or s > 0)
+                if half[i] >= s and (s > 0 or even[i] or (exchange and half[i] == 0))
             ]
         elif kind == "along":
             source = ("along", s - 1, unit) if s > 1 else ("own", 0, unit)
             pairs = [(i, i + column) for i in range(size - column) if half[i] >= s - 1]
         else:
-            source = ("across" if kind == "down" else "own", 0, unit)
+            source = ("across", 0, unit)
             pairs = [(i, i + s * column) for i in range(size - s * column)]
         array = lax.optimization_barrier((moved[source], *[moved[w] for w in waits]))[0]
-        key = "along" if kind == "direct" else kind
-        moved[key, s, unit] = lax.ppermute(array, "node", pairs)
+        if unit == 1 and s == near:
+            parts = [array[:, h * width : (h + 1) * width] for h in range(per_unit)]
+        else:
+            parts = [array]
+        for h, part in enumerate(parts):
+            moved[kind, s, unit, h] = lax.ppermute(part, "node", pairs)
+        moved[kind, s, unit] = moved[kind, s, unit, 0]
 
     for kind, s, unit, waits in PLAN:
         step(kind, s, unit, waits)
+
     result = None
-    for unit in range(UNITS):
+    for unit, first, count in ((0, 0, per_unit), *[(1, h, 1) for h in range(per_unit)]):
+        far = "across" if unit == 0 else "down"
         result = attention(
             slots,
             anc_cut,
             odd,
             queries,
             own[unit],
-            [moved["along", s, unit] for s in range(1, near + 1)],
-            [moved["across", s, unit] for s in range(near)]
-            + [moved["across" if unit == 0 else "down", near, unit]],
+            [moved["along", s, unit] for s in range(1, near)] + [moved["along", near, unit, first]],
+            [moved["across", s, unit] for s in range(near)] + [moved[far, near, unit, first]],
             unit,
+            first,
+            count,
             result,
         )
     return result

time: 117 us -> 125 us (1.068)
  the two profiles are of different devices: /device:TPU:24 before, /device:TPU:0 now
where the time goes in v14:
time: 125 us; the launch traced here: 124 us
  starting transfers between devices  62.4 us (50%)
  Pallas kernels  45.9 us (37%)
  waiting for transfers between devices  9.48 us (8%)
  local copies, waits for them, and re-layouts  5.39 us (4%)
    ppermute x16, starting transfers between devices, step(): moved[kind, s, unit, h] = lax.ppermute(part, 'node', pairs)  62.4 us
    pallas_call x3, Pallas kernels, attention(): pl.pallas_call(functools.partial(attention_kernel, block, unit * per_unit...  23.4 us
    pallas_call x1, Pallas kernels, norm_project(): pl.pallas_call(norm_project_kernel, in_specs=[held, whole, held, held], o...  13.1 us
    ppermute x16, waiting for transfers between devices, step(): moved[kind, s, unit, h] = lax.ppermute(part, 'node', pairs)  9.48 us
    pallas_call x1, Pallas kernels, project(): pl.pallas_call(project_kernel, grid=(CHUNKS,), in_specs=[pl.BlockSpec((ro...  9.35 us
    unnamed x28, local copies, waits for them, and re-layouts  3.69 us
  transfers between devices with their start and end apart: 16, of which 2 were waited for; matrix products, arithmetic and copies ran while one was open for 2% of the time, Pallas kernels for 21%

profile of v14, /device:TPU:0, one launch (start us, length us, event | category | flops | bytes accessed | tf_op | source)
XLA Modules:
  0.0 124.3 jit_solution(596055934972882981)
XLA Ops:
  0.0 13.1 %norm_project.1 = (f32[512,128]{1,0:T(8,128)}, bf16[512,512]{1,0:T(8,128)(2,1)}) custom-call(bf16[512,8192]{1,0:T(8,128)(2,1)} %x_ref.1, f32[8,1,1024]{2,1,0:T(1,128)} %bitcast.3, bf16[8192,512]{1,0:T(8,128)(2,1)} %key_ref.1, bf16[8192,512]{1,0:T(8,128)(2,1)} %value_ref.1), custom_call_target="tpu_custom_call" | custom-call | flops 4294967296 | bytes 16777216 | tf_op jit(solution)/shard_map/norm_project/pallas_call | solution.py:141
  13.1 5.0 %collective-permute-start.1 = (bf16[512,512]{1,0:T(8,128)(2,1)}, bf16[512,512]{1,0:T(8,128)(2,1)S(1)}, u32[]{:S(2)}, u32[]{:S(2)}) collective-permute-start(bf16[512,512]{1,0:T(8,128)(2,1)} %get-tuple-element.18.refs_0_), channel_id=1, source_target_pairs={{0,4},{1,5},{2,6},{3,7},{4,8},{5,9},{6,10},{7,11},{8,12},{9,13},{1... | collective-permute-start | bytes 1572872 | tf_op jit(solution)/shard_map/ppermute | solution.py:407
  18.1 3.5 %collective-permute-start.3 = (bf16[512,512]{1,0:T(8,128)(2,1)}, bf16[512,512]{1,0:T(8,128)(2,1)S(1)}, u32[]{:S(2)}, u32[]{:S(2)}) collective-permute-start(bf16[512,512]{1,0:T(8,128)(2,1)} %get-tuple-element.18.refs_0_), channel_id=1, source_target_pairs={{0,2},{1,3},{4,6},{5,7},{8,10},{9,11},{12,14},{13,15},{16,18},{17,... | collective-permute-start | bytes 1572872 | tf_op jit(solution)/shard_map/ppermute | solution.py:407
  21.6 0.0 copy-start.13
  21.6 9.4 %project.1.refs_0_ = bf16[512,512]{1,0:T(8,128)(2,1)} custom-call(bf16[512,8192]{1,0:T(8,128)(2,1)} %x_ref.1, f32[512,128]{1,0:T(8,128)} %get-tuple-element.17.scale_ref, f32[1,8192]{1,0:T(1,128)} %bitcast.4, bf16[8192,512]{1,0:T(8,128)(2,1)} %key_ref.1, bf16[8192,512]{1,0:T(8,128)(2,1)} %value_ref.1), custom_call_target="tpu_custom_call" | custom-call | flops 4294967296 | bytes 16777216 | tf_op jit(solution)/shard_map/project/pallas_call | solution.py:194
  30.9 1.9 %collective-permute-start.7 = (bf16[512,512]{1,0:T(8,128)(2,1)}, bf16[512,512]{1,0:T(8,128)(2,1)S(1)}, u32[]{:S(2)}, u32[]{:S(2)}) collective-permute-start(bf16[512,512]{1,0:T(8,128)(2,1)} %project.1.refs_0_), channel_id=1, source_target_pairs={{0,2},{1,3},{2,0},{3,1},{4,6},{5,7},{8,10},{9,11},{12,14},{13,15},... | collective-permute-start | bytes 1572872 | tf_op jit(solution)/shard_map/ppermute | solution.py:407
  32.8 2.9 %collective-permute-start = (bf16[512,512]{1,0:T(8,128)(2,1)}, bf16[512,512]{1,0:T(8,128)(2,1)S(1)}, u32[]{:S(2)}, u32[]{:S(2)}) collective-permute-start(bf16[512,512]{1,0:T(8,128)(2,1)} %project.1.refs_0_), channel_id=1, source_target_pairs={{0,4},{1,5},{2,6},{3,7},{4,8},{5,9},{6,10},{7,11},{8,12},{9,13},{1... | collective-permute-start | bytes 1572872 | tf_op jit(solution)/shard_map/ppermute | solution.py:407
  35.7 0.0 collective-permute-done.1.refs_1_
  35.8 0.7 collective-permute-start.2
  36.5 0.0 collective-permute-done.3.refs_4_
  36.5 0.0 copy-start.6
  36.5 0.7 collective-permute-start.4
  37.2 8.9 %collective-permute-done.7.refs_4_ = bf16[512,512]{1,0:T(8,128)(2,1)S(1)} collective-permute-done((bf16[512,512]{1,0:T(8,128)(2,1)}, bf16[512,512]{1,0:T(8,128)(2,1)S(1)}, u32[]{:S(2)}, u32[]{:S(2)}) %collective-permute-start.7) | collective-permute-done | bytes 524320 | tf_op jit(solution)/shard_map/ppermute | solution.py:407
  46.1 0.5 collective-permute-done.refs_1_
  46.6 0.7 collective-permute-start.8
  47.3 0.0 collective-permute-done.2.refs_2_
  47.3 0.0 copy-start.7
  47.3 1.5 %collective-permute-start.11 = (bf16[512,512]{1,0:T(8,128)(2,1)S(1)}, bf16[512,512]{1,0:T(8,128)(2,1)}, u32[]{:S(2)}, u32[]{:S(2)}) collective-permute-start(bf16[512,512]{1,0:T(8,128)(2,1)S(1)} %collective-permute-done.2.refs_2_), channel_id=1, source_target_pairs={{8,12},{9,13},{10,14},{11,15},{24,28},{25,29},{26,30},{27,31}} | collective-permute-start | bytes 1572872 | tf_op jit(solution)/shard_map/ppermute | solution.py:407
  48.8 0.0 collective-permute-done.4.refs_5_
  48.8 0.7 collective-permute-start.5
  49.5 0.7 collective-permute-start.9
  50.2 0.0 collective-permute-done.8.refs_5_
  50.2 0.0 collective-permute-done.11.refs_3_
  50.2 1.5 %collective-permute-start.15 = (bf16[512,512]{1,0:T(8,128)(2,1)}, bf16[512,512]{1,0:T(8,128)(2,1)}, u32[]{:S(2)}, u32[]{:S(2)}) collective-permute-start(bf16[512,512]{1,0:T(8,128)(2,1)} %collective-permute-done.11.refs_3_), channel_id=1, source_target_pairs={{12,14},{13,15},{14,12},{15,13},{28,30},{29,31},{30,28},{31,29}} | collective-permute-start | bytes 1572872 | tf_op jit(solution)/shard_map/ppermute | solution.py:407
  51.7 0.0 collective-permute-done.5.refs_2_
  51.7 0.9 fusion.3
  52.6 0.7 collective-permute-start.13
  53.3 0.0 collective-permute-done.9.refs_6_
  53.3 0.8 copy-done.9
  54.1 0.7 collective-permute-start.10
  54.8 0.8 fusion.2
  55.6 39.3 %collective-permute-start.14 = (bf16[512,256]{1,0:T(8,128)(2,1)}, bf16[512,256]{1,0:T(8,128)(2,1)}, u32[]{:S(2)}, u32[]{:S(2)}) collective-permute-start(bf16[512,256]{1,0:T(8,128)(2,1)} %get-tuple-element.29), channel_id=1, source_target_pairs={{0,12},{1,13},{2,14},{3,15},{16,28},{17,29},{18,30},{19,31}} | collective-permute-start | bytes 786440 | tf_op jit(solution)/shard_map/ppermute | solution.py:407
  95.0 0.6 fusion.1.slot_ref
  95.6 0.7 collective-permute-start.6
  96.2 0.0 collective-permute-done.15.refs_7_
  96.2 1.5 %collective-permute-start.12 = (bf16[512,256]{1,0:T(8,128)(2,1)}, bf16[512,256]{1,0:T(8,128)(2,1)S(1)}, u32[]{:S(2)}, u32[]{:S(2)}) collective-permute-start(bf16[512,256]{1,0:T(8,128)(2,1)} %get-tuple-element.30), channel_id=1, source_target_pairs={{0,12},{1,13},{2,14},{3,15},{16,28},{17,29},{18,30},{19,31}} | collective-permute-start | bytes 786440 | tf_op jit(solution)/shard_map/ppermute | solution.py:407
  97.7 10.1 %attention.3.refs_8_ = bf16[512,4096]{1,0:T(8,128)(2,1)} custom-call(s32[8,7]{1,0:T(8,128)} %fusion.1.slot_ref, s32[8,7]{1,0:T(8,128)} %cut_ref.5, s32[1]{0:T(128)} %bitcast.odd_ref, bf16[512,4096]{1,0:T(8,128)(2,1)} %q_hbm.5, bf16[512,512]{1,0:T(8,128)(2,1)} %get-tuple-element.18.refs_0_, bf16[512,512]{1,0:T(8,128)(2,1)} %copy-done.5, ...), custom_call_target="tpu_custom_call" | custom-call | flops 2147483648 | bytes 8388608 | tf_op jit(solution)/shard_map/attention/pallas_call | solution.py:340
  107.9 0.0 collective-permute-done.13.refs_3_
  107.9 0.0 collective-permute-done.14.refs_7_
  107.9 0.0 collective-permute-done.10.refs_6_
  107.9 0.7 copy-done.10
  108.6 0.8 copy-done.4
  109.4 6.6 %attention.4.refs_8_ = bf16[512,4096]{1,0:T(8,128)(2,1)} custom-call(s32[8,7]{1,0:T(8,128)} %fusion.1.slot_ref, s32[8,7]{1,0:T(8,128)} %cut_ref.5, s32[1]{0:T(128)} %bitcast.odd_ref, bf16[512,4096]{1,0:T(8,128)(2,1)} %q_hbm.5, bf16[512,512]{1,0:T(8,128)(2,1)} %project.1.refs_0_, bf16[512,512]{1,0:T(8,128)(2,1)} %copy-done.2, ...), custom_call_target="tpu_custom_call", output_to_operand_aliasing={{}: (12, {})} | custom-call | flops 1073741824 | bytes 4194304 | tf_op jit(solution)/shard_map/attention/pallas_call | solution.py:340
  116.0 0.0 collective-permute-done.6.refs_3_
  116.1 0.0 collective-permute-done.12.refs_7_
  116.1 0.7 copy-done.11
  116.7 0.7 copy-done.12
  117.5 6.7 %attention.5 = bf16[512,4096]{1,0:T(8,128)(2,1)} custom-call(s32[8,7]{1,0:T(8,128)} %fusion.1.slot_ref, s32[8,7]{1,0:T(8,128)} %cut_ref.5, s32[1]{0:T(128)} %bitcast.odd_ref, bf16[512,4096]{1,0:T(8,128)(2,1)} %q_hbm.5, bf16[512,512]{1,0:T(8,128)(2,1)} %project.1.refs_0_, bf16[512,512]{1,0:T(8,128)(2,1)} %copy-done.2, ...), custom_call_target="tpu_custom_call", output_to_operand_aliasing={{}: (12, {})} | custom-call | flops 1073741824 | bytes 4194304 | tf_op jit(solution)/shard_map/attention/pallas_call | solution.py:340
  (20 shorter events, 0.0 us)
Async XLA Ops:
  13.1 22.6 %collective-permute-start.1 = (bf16[512,512]{1,0:T(8,128)(2,1)}, bf16[512,512]{1,0:T(8,128)(2,1)S(1)}, u32[]{:S(2)}, u32[]{:S(2)}) collective-permute-start(bf16[512,512]{1,0:T(8,128)(2,1)} %get-tuple-element.18.refs_0_), channel_id=1, source_target_pairs={{0,4},{1,5},{2,6},{3,7},{4,8},{5,9},{6,10},{7,11},{8,12},{9,13},{1... | collective-permute-start | bytes 1572872 | tf_op jit(solution)/shard_map/ppermute | solution.py:407
  18.1 18.4 %collective-permute-start.3 = (bf16[512,512]{1,0:T(8,128)(2,1)}, bf16[512,512]{1,0:T(8,128)(2,1)S(1)}, u32[]{:S(2)}, u32[]{:S(2)}) collective-permute-start(bf16[512,512]{1,0:T(8,128)(2,1)} %get-tuple-element.18.refs_0_), channel_id=1, source_target_pairs={{0,2},{1,3},{4,6},{5,7},{8,10},{9,11},{12,14},{13,15},{16,18},{17,... | collective-permute-start | bytes 1572872 | tf_op jit(solution)/shard_map/ppermute | solution.py:407
  21.6 73.4 %copy-start.13 = (s32[8,7]{1,0:T(8,128)S(1)}, s32[8,7]{1,0:T(8,128)}, u32[]{:S(2)}) copy-start(s32[8,7]{1,0:T(8,128)} %param.12) | copy-start | bytes 676
  30.9 15.2 %collective-permute-start.7 = (bf16[512,512]{1,0:T(8,128)(2,1)}, bf16[512,512]{1,0:T(8,128)(2,1)S(1)}, u32[]{:S(2)}, u32[]{:S(2)}) collective-permute-start(bf16[512,512]{1,0:T(8,128)(2,1)} %project.1.refs_0_), channel_id=1, source_target_pairs={{0,2},{1,3},{2,0},{3,1},{4,6},{5,7},{8,10},{9,11},{12,14},{13,15},... | collective-permute-start | bytes 1572872 | tf_op jit(solution)/shard_map/ppermute | solution.py:407
  32.8 13.8 %collective-permute-start = (bf16[512,512]{1,0:T(8,128)(2,1)}, bf16[512,512]{1,0:T(8,128)(2,1)S(1)}, u32[]{:S(2)}, u32[]{:S(2)}) collective-permute-start(bf16[512,512]{1,0:T(8,128)(2,1)} %project.1.refs_0_), channel_id=1, source_target_pairs={{0,4},{1,5},{2,6},{3,7},{4,8},{5,9},{6,10},{7,11},{8,12},{9,13},{1... | collective-permute-start | bytes 1572872 | tf_op jit(solution)/shard_map/ppermute | solution.py:407
  35.7 62.0 %copy-start.5 = (bf16[512,512]{1,0:T(8,128)(2,1)}, bf16[512,512]{1,0:T(8,128)(2,1)S(1)}, u32[]{:S(2)}) copy-start(bf16[512,512]{1,0:T(8,128)(2,1)S(1)} %collective-permute-done.1.refs_1_) | copy-start | bytes 1572868
  35.8 11.6 %collective-permute-start.2 = (bf16[512,512]{1,0:T(8,128)(2,1)S(1)}, bf16[512,512]{1,0:T(8,128)(2,1)S(1)}, u32[]{:S(2)}, u32[]{:S(2)}) collective-permute-start(bf16[512,512]{1,0:T(8,128)(2,1)S(1)} %collective-permute-done.1.refs_1_), channel_id=1, source_target_pairs={{4,8},{5,9},{6,10},{7,11},{8,12},{9,13},{10,14},{11,15},{20,24},{2... | collective-permute-start | bytes 1572872 | tf_op jit(solution)/shard_map/ppermute | solution.py:407
  36.5 12.3 %copy-start.6 = (bf16[512,512]{1,0:T(8,128)(2,1)}, bf16[512,512]{1,0:T(8,128)(2,1)S(1)}, u32[]{:S(2)}) copy-start(bf16[512,512]{1,0:T(8,128)(2,1)S(1)} %collective-permute-done.3.refs_4_) | copy-start | bytes 1572868
  36.5 12.3 %collective-permute-start.4 = (bf16[512,512]{1,0:T(8,128)(2,1)S(1)}, bf16[512,512]{1,0:T(8,128)(2,1)S(1)}, u32[]{:S(2)}, u32[]{:S(2)}) collective-permute-start(bf16[512,512]{1,0:T(8,128)(2,1)S(1)} %collective-permute-done.1.refs_1_), channel_id=1, source_target_pairs={{4,6},{5,7},{6,4},{7,5},{8,10},{9,11},{10,8},{11,9},{12,14},{13,15... | collective-permute-start | bytes 1572872 | tf_op jit(solution)/shard_map/ppermute | solution.py:407
  46.1 61.7 %copy-start = (bf16[512,512]{1,0:T(8,128)(2,1)}, bf16[512,512]{1,0:T(8,128)(2,1)S(1)}, u32[]{:S(2)}) copy-start(bf16[512,512]{1,0:T(8,128)(2,1)S(1)} %collective-permute-done.7.refs_4_) | copy-start | bytes 1572868
  46.6 61.2 %copy-start.2 = (bf16[512,512]{1,0:T(8,128)(2,1)}, bf16[512,512]{1,0:T(8,128)(2,1)S(1)}, u32[]{:S(2)}) copy-start(bf16[512,512]{1,0:T(8,128)(2,1)S(1)} %collective-permute-done.refs_1_) | copy-start | bytes 1572868
  46.6 3.6 %collective-permute-start.8 = (bf16[512,512]{1,0:T(8,128)(2,1)S(1)}, bf16[512,512]{1,0:T(8,128)(2,1)S(1)}, u32[]{:S(2)}, u32[]{:S(2)}) collective-permute-start(bf16[512,512]{1,0:T(8,128)(2,1)S(1)} %collective-permute-done.refs_1_), channel_id=1, source_target_pairs={{4,6},{5,7},{6,4},{7,5},{8,10},{9,11},{10,8},{11,9},{12,14},{13,15... | collective-permute-start | bytes 1572872 | tf_op jit(solution)/shard_map/ppermute | solution.py:407
  47.3 6.0 %copy-start.7 = (bf16[512,512]{1,0:T(8,128)(2,1)}, bf16[512,512]{1,0:T(8,128)(2,1)S(1)}, u32[]{:S(2)}) copy-start(bf16[512,512]{1,0:T(8,128)(2,1)S(1)} %collective-permute-done.2.refs_2_) | copy-start | bytes 1572868
  47.3 2.9 %collective-permute-start.11 = (bf16[512,512]{1,0:T(8,128)(2,1)S(1)}, bf16[512,512]{1,0:T(8,128)(2,1)}, u32[]{:S(2)}, u32[]{:S(2)}) collective-permute-start(bf16[512,512]{1,0:T(8,128)(2,1)S(1)} %collective-permute-done.2.refs_2_), channel_id=1, source_target_pairs={{8,12},{9,13},{10,14},{11,15},{24,28},{25,29},{26,30},{27,31}} | collective-permute-start | bytes 1572872 | tf_op jit(solution)/shard_map/ppermute | solution.py:407
  48.8 1.4 %copy-start.8 = (bf16[512,512]{1,0:T(8,128)(2,1)}, bf16[512,512]{1,0:T(8,128)(2,1)S(1)}, u32[]{:S(2)}) copy-start(bf16[512,512]{1,0:T(8,128)(2,1)S(1)} %collective-permute-done.4.refs_5_) | copy-start | bytes 1572868
  48.8 2.9 %collective-permute-start.5 = (bf16[512,512]{1,0:T(8,128)(2,1)S(1)}, bf16[512,512]{1,0:T(8,128)(2,1)S(1)}, u32[]{:S(2)}, u32[]{:S(2)}) collective-permute-start(bf16[512,512]{1,0:T(8,128)(2,1)S(1)} %collective-permute-done.refs_1_), channel_id=1, source_target_pairs={{4,8},{5,9},{6,10},{7,11},{8,12},{9,13},{10,14},{11,15},{20,24},{2... | collective-permute-start | bytes 1572872 | tf_op jit(solution)/shard_map/ppermute | solution.py:407
  49.5 3.8 %collective-permute-start.9 = (bf16[512,512]{1,0:T(8,128)(2,1)S(1)}, bf16[512,512]{1,0:T(8,128)(2,1)S(1)}, u32[]{:S(2)}, u32[]{:S(2)}) collective-permute-start(bf16[512,512]{1,0:T(8,128)(2,1)S(1)} %collective-permute-done.2.refs_2_), channel_id=1, source_target_pairs={{8,10},{9,11},{10,8},{11,9},{12,14},{13,15},{14,12},{15,13},{24,26... | collective-permute-start | bytes 1572872 | tf_op jit(solution)/shard_map/ppermute | solution.py:407
  50.2 57.6 %copy-start.3 = (bf16[512,512]{1,0:T(8,128)(2,1)}, bf16[512,512]{1,0:T(8,128)(2,1)S(1)}, u32[]{:S(2)}) copy-start(bf16[512,512]{1,0:T(8,128)(2,1)S(1)} %collective-permute-done.8.refs_5_) | copy-start | bytes 1572868
  50.2 46.0 %collective-permute-start.15 = (bf16[512,512]{1,0:T(8,128)(2,1)}, bf16[512,512]{1,0:T(8,128)(2,1)}, u32[]{:S(2)}, u32[]{:S(2)}) collective-permute-start(bf16[512,512]{1,0:T(8,128)(2,1)} %collective-permute-done.11.refs_3_), channel_id=1, source_target_pairs={{12,14},{13,15},{14,12},{15,13},{28,30},{29,31},{30,28},{31,29}} | collective-permute-start | bytes 1572872 | tf_op jit(solution)/shard_map/ppermute | solution.py:407
  51.7 56.2 %copy-start.1 = (bf16[512,512]{1,0:T(8,128)(2,1)}, bf16[512,512]{1,0:T(8,128)(2,1)S(1)}, u32[]{:S(2)}) copy-start(bf16[512,512]{1,0:T(8,128)(2,1)S(1)} %collective-permute-done.5.refs_2_) | copy-start | bytes 1572868
  52.6 55.3 %collective-permute-start.13 = (bf16[512,256]{1,0:T(8,128)(2,1)}, bf16[512,256]{1,0:T(8,128)(2,1)S(1)}, u32[]{:S(2)}, u32[]{:S(2)}) collective-permute-start(bf16[512,256]{1,0:T(8,128)(2,1)} %get-tuple-element.31), channel_id=1, source_target_pairs={{8,12},{9,13},{10,14},{11,15},{24,28},{25,29},{26,30},{27,31}} | collective-permute-start | bytes 786440 | tf_op jit(solution)/shard_map/ppermute | solution.py:407
  53.3 0.8 copy-start.9
  54.1 53.8 %collective-permute-start.10 = (bf16[512,512]{1,0:T(8,128)(2,1)S(1)}, bf16[512,512]{1,0:T(8,128)(2,1)S(1)}, u32[]{:S(2)}, u32[]{:S(2)}) collective-permute-start(bf16[512,512]{1,0:T(8,128)(2,1)S(1)} %collective-permute-done.5.refs_2_), channel_id=1, source_target_pairs={{8,10},{9,11},{10,8},{11,9},{12,14},{13,15},{14,12},{15,13},{24,26... | collective-permute-start | bytes 1572872 | tf_op jit(solution)/shard_map/ppermute | solution.py:407
  55.6 52.3 %collective-permute-start.14 = (bf16[512,256]{1,0:T(8,128)(2,1)}, bf16[512,256]{1,0:T(8,128)(2,1)}, u32[]{:S(2)}, u32[]{:S(2)}) collective-permute-start(bf16[512,256]{1,0:T(8,128)(2,1)} %get-tuple-element.29), channel_id=1, source_target_pairs={{0,12},{1,13},{2,14},{3,15},{16,28},{17,29},{18,30},{19,31}} | collective-permute-start | bytes 786440 | tf_op jit(solution)/shard_map/ppermute | solution.py:407
  95.6 20.5 %collective-permute-start.6 = (bf16[512,256]{1,0:T(8,128)(2,1)}, bf16[512,256]{1,0:T(8,128)(2,1)S(1)}, u32[]{:S(2)}, u32[]{:S(2)}) collective-permute-start(bf16[512,256]{1,0:T(8,128)(2,1)} %get-tuple-element.32), channel_id=1, source_target_pairs={{8,12},{9,13},{10,14},{11,15},{24,28},{25,29},{26,30},{27,31}} | collective-permute-start | bytes 786440 | tf_op jit(solution)/shard_map/ppermute | solution.py:407
  96.2 19.8 %collective-permute-start.12 = (bf16[512,256]{1,0:T(8,128)(2,1)}, bf16[512,256]{1,0:T(8,128)(2,1)S(1)}, u32[]{:S(2)}, u32[]{:S(2)}) collective-permute-start(bf16[512,256]{1,0:T(8,128)(2,1)} %get-tuple-element.30), channel_id=1, source_target_pairs={{0,12},{1,13},{2,14},{3,15},{16,28},{17,29},{18,30},{19,31}} | collective-permute-start | bytes 786440 | tf_op jit(solution)/shard_map/ppermute | solution.py:407
  107.9 0.7 copy-start.10
  108.6 0.8 copy-start.4
  116.1 0.7 copy-start.11
  116.7 0.7 copy-start.12

commit v15 on v13

--- a/solution.py
+++ b/solution.py
@@ -39,7 +39,10 @@
     x_hbm, gain_ref, key_hbm, value_hbm, scale_ref, kv_ref,
     x_scr, weight_scr, even_scr, odd_scr, acc_scr, x_sem, key_sem, value_sem,
 ):
-    loads, rows, chunk = x_scr.shape
+    rows, features = x_scr.shape
+    loads = LOADS
+    tall = rows // loads
+    chunks, chunk = weight_scr.shape[:2]
     width = weight_scr.shape[2] // 2
     lanes = 128
     band = 128
@@ -48,7 +51,8 @@
         return pl.ds(pl.multiple_of(c * chunk, chunk), chunk)
 
     def load_x(c):
-        return pltpu.make_async_copy(x_hbm.at[:, span(c)], x_scr.at[c], x_sem.at[c])
+        row = pl.ds(pl.multiple_of(c * tall, tall), tall)
+        return pltpu.make_async_copy(x_hbm.at[row], x_scr.at[row], x_sem.at[c])
 
     def load_weights(c):
         head = pl.ds(0, width)
@@ -63,28 +67,28 @@
 
     for c in range(loads):
         load_x(c).start()
-    scale_ref[...] = jnp.zeros_like(scale_ref)
 
     def square(c, carry):
         load_x(c).wait()
 
-        @pl.when(c >= loads // 2)
+        @pl.when(c == loads - 2)
         def _():
-            for part in range(2):
-                for copy in load_weights(2 * (c - loads // 2) + part):
-                    copy.start()
-
-        for first in range(0, rows, band):
-            row = slice(first, first + band)
-            total = scale_ref[row, :]
-            for lane in range(0, chunk, lanes):
-                x = x_scr[c, row, lane : lane + lanes].astype(jnp.float32)
-                total += x * x
-            scale_ref[row, :] = total
+            for copy in load_weights(0):
+                copy.start()
+
+        row = pl.ds(pl.multiple_of(c * tall, tall), tall)
+        total = jnp.zeros((tall, lanes), jnp.float32)
+        for lane in range(0, features, lanes):
+            x = x_scr[row, lane : lane + lanes].astype(jnp.float32)
+            total += x * x
+        scale_ref[row, :] = total
         return carry
 
     lax.fori_loop(0, loads, square, 0)
-    mean_sq = jnp.sum(scale_ref[...], axis=-1, keepdims=True) / (loads * chunk)
+    for c in range(1, chunks):
+        for copy in load_weights(c):
+            copy.start()
+    mean_sq = jnp.sum(scale_ref[...], axis=-1, keepdims=True) / features
     scale_ref[...] = jnp.broadcast_to(lax.rsqrt(mean_sq + EPS), scale_ref.shape)
 
     def normalise(normed_scr, c):
@@ -92,32 +96,30 @@
             row = slice(first, first + band)
             inverse = scale_ref[row, :]
             for lane in range(0, chunk, lanes):
-                cols = slice(lane, lane + lanes)
-                x = x_scr[c, row, cols].astype(jnp.float32)
-                gain = gain_ref[c, :, cols]
-                normed_scr[row, cols] = (x * inverse * gain).astype(jnp.bfloat16)
+                cols = pl.ds(pl.multiple_of(c * chunk + lane, lanes), lanes)
+                x = x_scr[row, cols].astype(jnp.float32)
+                normed_scr[row, lane : lane + lanes] = (
+                    x * inverse * gain_ref[:, cols]
+                ).astype(jnp.bfloat16)
 
     def multiply(normed_scr, c):
         for copy in load_weights(c):
             copy.wait()
-        acc_scr[...] += jnp.dot(
-            normed_scr[...], weight_scr[c], preferred_element_type=jnp.float32
-        )
+        return jnp.dot(normed_scr[...], weight_scr[c], preferred_element_type=jnp.float32)
 
     normalise(even_scr, 0)
-    acc_scr[...] = jnp.zeros_like(acc_scr)
+    acc_scr[...] = multiply(even_scr, 0)
+    normalise(odd_scr, 1)
 
     def pair(p, carry):
-        multiply(even_scr, 2 * p)
-        normalise(odd_scr, 2 * p + 1)
-        multiply(odd_scr, 2 * p + 1)
+        acc_scr[...] += multiply(odd_scr, 2 * p + 1)
         normalise(even_scr, 2 * p + 2)
+        acc_scr[...] += multiply(even_scr, 2 * p + 2)
+        normalise(odd_scr, 2 * p + 3)
         return carry
 
-    lax.fori_loop(0, loads // 2 - 1, pair, 0)
-    multiply(even_scr, loads - 2)
-    normalise(odd_scr, loads - 1)
-    multiply(odd_scr, loads - 1)
+    lax.fori_loop(0, chunks // 2 - 1, pair, 0)
+    acc_scr[...] += multiply(odd_scr, chunks - 1)
     write_heads(kv_ref, acc_scr)
 
 
@@ -133,7 +135,7 @@
 def norm_project(hidden, gain, key_weight, value_weight):
     rows, features = hidden.shape
     width = key_weight.shape[1] // UNITS
-    chunk = features // LOADS
+    chunk = features // CHUNKS
     whole = pl.BlockSpec(memory_space=pltpu.VMEM)
     held = pl.BlockSpec(memory_space=pltpu.HBM)
     return pl.pallas_call(
@@ -145,21 +147,21 @@
             jax.ShapeDtypeStruct((rows, 2 * width), jnp.bfloat16),
         ],
         scratch_shapes=[
-            pltpu.VMEM((LOADS, rows, chunk), jnp.bfloat16),
-            pltpu.VMEM((LOADS, chunk, 2 * width), jnp.bfloat16),
+            pltpu.VMEM((rows, features), jnp.bfloat16),
+            pltpu.VMEM((CHUNKS, chunk, 2 * width), jnp.bfloat16),
             pltpu.VMEM((rows, chunk), jnp.bfloat16),
             pltpu.VMEM((rows, chunk), jnp.bfloat16),
             pltpu.VMEM((rows, 2 * width), jnp.float32),
             pltpu.SemaphoreType.DMA((LOADS,)),
-            pltpu.SemaphoreType.DMA((LOADS,)),
-            pltpu.SemaphoreType.DMA((LOADS,)),
+            pltpu.SemaphoreType.DMA((CHUNKS,)),
+            pltpu.SemaphoreType.DMA((CHUNKS,)),
         ],
         compiler_params=pltpu.CompilerParams(vmem_limit_bytes=57 * MIB),
         cost_estimate=pl.CostEstimate(
             flops=4 * rows * features * width, bytes_accessed=16 * MIB, transcendentals=0
         ),
         name="norm_project",
-    )(hidden, gain.reshape(LOADS, 1, chunk), key_weight, value_weight)
+    )(hidden, gain.reshape(1, features), key_weight, value_weight)
 
 
 def project_kernel(x_ref, scale_ref, gain_ref, key_ref, value_ref, kv_ref, acc_scr):

time: 117 us -> 117 us (level)
  no operation moved by 1% of the time
where the time goes in v15:
time: 117 us
  waiting for transfers between devices  48.8 us (42%)
  Pallas kernels  42.6 us (36%)
  starting transfers between devices  24.3 us (21%)
    ppermute x14, waiting for transfers between devices, step(): moved[key, s, unit] = lax.ppermute(array, 'node', pairs)  48.8 us
    ppermute x14, starting transfers between devices, step(): moved[key, s, unit] = lax.ppermute(array, 'node', pairs)  24.3 us
    pallas_call x2, Pallas kernels, attention(): pl.pallas_call(functools.partial(attention_kernel, block, unit, near), in...  20.2 us
    pallas_call x1, Pallas kernels, norm_project(): pl.pallas_call(norm_project_kernel, in_specs=[held, whole, held, held], o...  13.1 us
    pallas_call x1, Pallas kernels, project(): pl.pallas_call(project_kernel, grid=(CHUNKS,), in_specs=[pl.BlockSpec((ro...  9.35 us
  transfers between devices with their start and end apart: 14, of which 8 were waited for; matrix products, arithmetic and copies ran while one was open for 1% of the time, Pallas kernels for 17%

profile of v15, /device:TPU:24, one launch (start us, length us, event | category | flops | bytes accessed | tf_op | source)
XLA Modules:
  0.0 116.7 jit_solution(15389016215088439628)
XLA Ops:
  0.0 13.1 %norm_project.1 = (f32[512,128]{1,0:T(8,128)}, bf16[512,512]{1,0:T(8,128)(2,1)}) custom-call(bf16[512,8192]{1,0:T(8,128)(2,1)} %x_ref.1, f32[1,8192]{1,0:T(1,128)} %bitcast.2, bf16[8192,512]{1,0:T(8,128)(2,1)} %key_ref.1, bf16[8192,512]{1,0:T(8,128)(2,1)} %value_ref.1), custom_call_target="tpu_custom_call" | custom-call | flops 4294967296 | bytes 16777216 | tf_op jit(solution)/shard_map/norm_project/pallas_call | solution.py:141
  13.1 1.3 %collective-permute-start.1 = (bf16[512,512]{1,0:T(8,128)(2,1)}, bf16[512,512]{1,0:T(8,128)(2,1)S(1)}, u32[]{:S(2)}, u32[]{:S(2)}) collective-permute-start(bf16[512,512]{1,0:T(8,128)(2,1)} %get-tuple-element.18.refs_0_), channel_id=1, source_target_pairs={{0,4},{1,5},{2,6},{3,7},{4,8},{5,9},{6,10},{7,11},{8,12},{9,13},{1... | collective-permute-start | bytes 1572872 | tf_op jit(solution)/shard_map/ppermute | solution.py:402
  14.4 3.5 %collective-permute-start.7 = (bf16[512,512]{1,0:T(8,128)(2,1)}, bf16[512,512]{1,0:T(8,128)(2,1)S(1)}, u32[]{:S(2)}, u32[]{:S(2)}) collective-permute-start(bf16[512,512]{1,0:T(8,128)(2,1)} %get-tuple-element.18.refs_0_), channel_id=1, source_target_pairs={{0,2},{1,3},{4,6},{5,7},{8,10},{9,11},{12,14},{13,15},{16,18},{17,... | collective-permute-start | bytes 1572872 | tf_op jit(solution)/shard_map/ppermute | solution.py:402
  17.9 0.0 copy-start.8
  17.9 9.3 %project.1.refs_0_ = bf16[512,512]{1,0:T(8,128)(2,1)} custom-call(bf16[512,8192]{1,0:T(8,128)(2,1)} %x_ref.1, f32[512,128]{1,0:T(8,128)} %get-tuple-element.17.scale_ref, f32[1,8192]{1,0:T(1,128)} %bitcast.3, bf16[8192,512]{1,0:T(8,128)(2,1)} %key_ref.1, bf16[8192,512]{1,0:T(8,128)(2,1)} %value_ref.1), custom_call_target="tpu_custom_call" | custom-call | flops 4294967296 | bytes 16777216 | tf_op jit(solution)/shard_map/project/pallas_call | solution.py:194
  27.2 1.3 %collective-permute-start.5 = (bf16[512,512]{1,0:T(8,128)(2,1)}, bf16[512,512]{1,0:T(8,128)(2,1)S(1)}, u32[]{:S(2)}, u32[]{:S(2)}) collective-permute-start(bf16[512,512]{1,0:T(8,128)(2,1)} %project.1.refs_0_), channel_id=1, source_target_pairs={{0,2},{1,3},{2,0},{3,1},{4,6},{5,7},{8,10},{9,11},{12,14},{13,15},... | collective-permute-start | bytes 1572872 | tf_op jit(solution)/shard_map/ppermute | solution.py:402
  28.5 1.3 %collective-permute-start = (bf16[512,512]{1,0:T(8,128)(2,1)}, bf16[512,512]{1,0:T(8,128)(2,1)S(1)}, u32[]{:S(2)}, u32[]{:S(2)}) collective-permute-start(bf16[512,512]{1,0:T(8,128)(2,1)} %project.1.refs_0_), channel_id=1, source_target_pairs={{0,4},{1,5},{2,6},{3,7},{4,8},{5,9},{6,10},{7,11},{8,12},{9,13},{1... | collective-permute-start | bytes 1572872 | tf_op jit(solution)/shard_map/ppermute | solution.py:402
  29.8 0.0 collective-permute-done.1.refs_1_
  29.8 0.0 copy-start.2
  29.9 1.3 %collective-permute-start.2 = (bf16[512,512]{1,0:T(8,128)(2,1)S(1)}, bf16[512,512]{1,0:T(8,128)(2,1)S(1)}, u32[]{:S(2)}, u32[]{:S(2)}) collective-permute-start(bf16[512,512]{1,0:T(8,128)(2,1)S(1)} %collective-permute-done.1.refs_1_), channel_id=1, source_target_pairs={{4,8},{5,9},{6,10},{7,11},{8,12},{9,13},{10,14},{11,15},{20,24},{2... | collective-permute-start | bytes 1572872 | tf_op jit(solution)/shard_map/ppermute | solution.py:402
  31.2 0.0 collective-permute-done.7.refs_4_
  31.2 0.0 copy-start.3
  31.2 2.9 %collective-permute-start.8 = (bf16[512,512]{1,0:T(8,128)(2,1)S(1)}, bf16[512,512]{1,0:T(8,128)(2,1)S(1)}, u32[]{:S(2)}, u32[]{:S(2)}) collective-permute-start(bf16[512,512]{1,0:T(8,128)(2,1)S(1)} %collective-permute-done.1.refs_1_), channel_id=1, source_target_pairs={{4,6},{5,7},{6,4},{7,5},{8,10},{9,11},{10,8},{11,9},{12,14},{13,15... | collective-permute-start | bytes 1572872 | tf_op jit(solution)/shard_map/ppermute | solution.py:402
  34.1 7.1 %collective-permute-done.5.refs_4_ = bf16[512,512]{1,0:T(8,128)(2,1)S(1)} collective-permute-done((bf16[512,512]{1,0:T(8,128)(2,1)}, bf16[512,512]{1,0:T(8,128)(2,1)S(1)}, u32[]{:S(2)}, u32[]{:S(2)}) %collective-permute-start.5) | collective-permute-done | bytes 524320 | tf_op jit(solution)/shard_map/ppermute | solution.py:402
  41.1 0.0 copy-start
  41.1 5.0 %collective-permute-done.refs_1_ = bf16[512,512]{1,0:T(8,128)(2,1)S(1)} collective-permute-done((bf16[512,512]{1,0:T(8,128)(2,1)}, bf16[512,512]{1,0:T(8,128)(2,1)S(1)}, u32[]{:S(2)}, u32[]{:S(2)}) %collective-permute-start) | collective-permute-done | bytes 524320 | tf_op jit(solution)/shard_map/ppermute | solution.py:402
  46.1 1.9 %collective-permute-start.6 = (bf16[512,512]{1,0:T(8,128)(2,1)S(1)}, bf16[512,512]{1,0:T(8,128)(2,1)S(1)}, u32[]{:S(2)}, u32[]{:S(2)}) collective-permute-start(bf16[512,512]{1,0:T(8,128)(2,1)S(1)} %collective-permute-done.refs_1_), channel_id=1, source_target_pairs={{4,6},{5,7},{6,4},{7,5},{8,10},{9,11},{10,8},{11,9},{12,14},{13,15... | collective-permute-start | bytes 1572872 | tf_op jit(solution)/shard_map/ppermute | solution.py:402
  48.0 7.9 %collective-permute-done.2.refs_2_ = bf16[512,512]{1,0:T(8,128)(2,1)S(1)} collective-permute-done((bf16[512,512]{1,0:T(8,128)(2,1)S(1)}, bf16[512,512]{1,0:T(8,128)(2,1)S(1)}, u32[]{:S(2)}, u32[]{:S(2)}) %collective-permute-start.2) | collective-permute-done | bytes 524320 | tf_op jit(solution)/shard_map/ppermute | solution.py:402
  55.9 1.3 %collective-permute-start.11 = (bf16[512,512]{1,0:T(8,128)(2,1)S(1)}, bf16[512,512]{1,0:T(8,128)(2,1)}, u32[]{:S(2)}, u32[]{:S(2)}) collective-permute-start(bf16[512,512]{1,0:T(8,128)(2,1)S(1)} %collective-permute-done.2.refs_2_), channel_id=1, source_target_pairs={{8,12},{9,13},{10,14},{11,15},{24,28},{25,29},{26,30},{27,31}} | collective-permute-start | bytes 1572872 | tf_op jit(solution)/shard_map/ppermute | solution.py:402
  57.2 1.3 %collective-permute-start.3 = (bf16[512,512]{1,0:T(8,128)(2,1)S(1)}, bf16[512,512]{1,0:T(8,128)(2,1)}, u32[]{:S(2)}, u32[]{:S(2)}) collective-permute-start(bf16[512,512]{1,0:T(8,128)(2,1)S(1)} %collective-permute-done.refs_1_), channel_id=1, source_target_pairs={{4,8},{5,9},{6,10},{7,11},{8,12},{9,13},{10,14},{11,15},{20,24},{2... | collective-permute-start | bytes 1572872 | tf_op jit(solution)/shard_map/ppermute | solution.py:402
  58.5 0.0 collective-permute-done.8.refs_5_
  58.5 0.0 copy-start.6
  58.5 1.9 %collective-permute-start.9 = (bf16[512,512]{1,0:T(8,128)(2,1)S(1)}, bf16[512,512]{1,0:T(8,128)(2,1)S(1)}, u32[]{:S(2)}, u32[]{:S(2)}) collective-permute-start(bf16[512,512]{1,0:T(8,128)(2,1)S(1)} %collective-permute-done.2.refs_2_), channel_id=1, source_target_pairs={{8,10},{9,11},{10,8},{11,9},{12,14},{13,15},{14,12},{15,13},{24,26... | collective-permute-start | bytes 1572872 | tf_op jit(solution)/shard_map/ppermute | solution.py:402
  60.4 3.1 %collective-permute-done.6.refs_5_ = bf16[512,512]{1,0:T(8,128)(2,1)S(1)} collective-permute-done((bf16[512,512]{1,0:T(8,128)(2,1)S(1)}, bf16[512,512]{1,0:T(8,128)(2,1)S(1)}, u32[]{:S(2)}, u32[]{:S(2)}) %collective-permute-start.6) | collective-permute-done | bytes 524320 | tf_op jit(solution)/shard_map/ppermute | solution.py:402
  63.5 9.2 %collective-permute-done.11.refs_3_ = bf16[512,512]{1,0:T(8,128)(2,1)} collective-permute-done((bf16[512,512]{1,0:T(8,128)(2,1)S(1)}, bf16[512,512]{1,0:T(8,128)(2,1)}, u32[]{:S(2)}, u32[]{:S(2)}) %collective-permute-start.11) | collective-permute-done | bytes 524320 | tf_op jit(solution)/shard_map/ppermute | solution.py:402
  72.7 1.9 %collective-permute-start.13 = (bf16[512,512]{1,0:T(8,128)(2,1)}, bf16[512,512]{1,0:T(8,128)(2,1)}, u32[]{:S(2)}, u32[]{:S(2)}) collective-permute-start(bf16[512,512]{1,0:T(8,128)(2,1)} %collective-permute-done.11.refs_3_), channel_id=1, source_target_pairs={{12,14},{13,15},{14,12},{15,13},{28,30},{29,31},{30,28},{31,29}} | collective-permute-start | bytes 1572872 | tf_op jit(solution)/shard_map/ppermute | solution.py:402
  74.7 6.9 %collective-permute-done.3.refs_2_ = bf16[512,512]{1,0:T(8,128)(2,1)} collective-permute-done((bf16[512,512]{1,0:T(8,128)(2,1)S(1)}, bf16[512,512]{1,0:T(8,128)(2,1)}, u32[]{:S(2)}, u32[]{:S(2)}) %collective-permute-start.3) | collective-permute-done | bytes 524320 | tf_op jit(solution)/shard_map/ppermute | solution.py:402
  81.6 1.3 %collective-permute-start.4 = (bf16[512,512]{1,0:T(8,128)(2,1)}, bf16[512,512]{1,0:T(8,128)(2,1)}, u32[]{:S(2)}, u32[]{:S(2)}) collective-permute-start(bf16[512,512]{1,0:T(8,128)(2,1)} %collective-permute-done.3.refs_2_), channel_id=1, source_target_pairs={{8,12},{9,13},{10,14},{11,15},{24,28},{25,29},{26,30},{27,31}} | collective-permute-start | bytes 1572872 | tf_op jit(solution)/shard_map/ppermute | solution.py:402
  82.9 0.0 collective-permute-done.9.refs_6_
  82.9 0.0 copy-done.6
  82.9 0.0 copy-start.7
  82.9 1.9 %collective-permute-start.10 = (bf16[512,512]{1,0:T(8,128)(2,1)}, bf16[512,512]{1,0:T(8,128)(2,1)}, u32[]{:S(2)}, u32[]{:S(2)}) collective-permute-start(bf16[512,512]{1,0:T(8,128)(2,1)} %collective-permute-done.3.refs_2_), channel_id=1, source_target_pairs={{8,10},{9,11},{10,8},{11,9},{12,14},{13,15},{14,12},{15,13},{24,26... | collective-permute-start | bytes 1572872 | tf_op jit(solution)/shard_map/ppermute | solution.py:402
  84.8 0.0 copy-done.7
  84.8 1.3 %collective-permute-start.12 = (bf16[512,512]{1,0:T(8,128)(2,1)S(1)}, bf16[512,512]{1,0:T(8,128)(2,1)}, u32[]{:S(2)}, u32[]{:S(2)}) collective-permute-start(bf16[512,512]{1,0:T(8,128)(2,1)S(1)} %collective-permute-done.5.refs_4_), channel_id=1, source_target_pairs={{0,12},{1,13},{2,14},{3,15},{16,28},{17,29},{18,30},{19,31}} | collective-permute-start | bytes 1572872 | tf_op jit(solution)/shard_map/ppermute | solution.py:402
  86.2 0.0 copy-done.8
  86.2 0.6 fusion.1.slot_ref
  86.8 0.5 collective-permute-done.13.refs_7_
  87.3 0.0 copy-done.2
  87.3 0.0 copy-done.3
  87.3 0.0 copy-done.5
  87.3 10.1 %attention.2.refs_8_ = bf16[512,4096]{1,0:T(8,128)(2,1)} custom-call(s32[8,7]{1,0:T(8,128)} %fusion.1.slot_ref, s32[8,7]{1,0:T(8,128)} %cut_ref.3, s32[1]{0:T(128)} %bitcast.odd_ref, bf16[512,4096]{1,0:T(8,128)(2,1)} %q_hbm.3, bf16[512,512]{1,0:T(8,128)(2,1)} %get-tuple-element.18.refs_0_, bf16[512,512]{1,0:T(8,128)(2,1)} %copy-done.2, ...), custom_call_target="tpu_custom_call" | custom-call | flops 2147483648 | bytes 8388608 | tf_op jit(solution)/shard_map/attention/pallas_call | solution.py:341
  97.4 9.1 %collective-permute-done.4.refs_3_ = bf16[512,512]{1,0:T(8,128)(2,1)} collective-permute-done((bf16[512,512]{1,0:T(8,128)(2,1)}, bf16[512,512]{1,0:T(8,128)(2,1)}, u32[]{:S(2)}, u32[]{:S(2)}) %collective-permute-start.4) | collective-permute-done | bytes 524320 | tf_op jit(solution)/shard_map/ppermute | solution.py:402
  106.6 0.0 collective-permute-done.10.refs_6_
  106.6 0.0 collective-permute-done.12.refs_7_
  106.6 0.0 copy-done
  106.6 0.0 copy-done.1
  106.6 0.0 copy-done.4
  106.6 10.1 %attention.3 = bf16[512,4096]{1,0:T(8,128)(2,1)} custom-call(s32[8,7]{1,0:T(8,128)} %fusion.1.slot_ref, s32[8,7]{1,0:T(8,128)} %cut_ref.3, s32[1]{0:T(128)} %bitcast.odd_ref, bf16[512,4096]{1,0:T(8,128)(2,1)} %q_hbm.3, bf16[512,512]{1,0:T(8,128)(2,1)} %project.1.refs_0_, bf16[512,512]{1,0:T(8,128)(2,1)} %copy-done.1, ...), custom_call_target="tpu_custom_call", output_to_operand_aliasing={{}: (12, {})} | custom-call | flops 2147483648 | bytes 8388608 | tf_op jit(solution)/shard_map/attention/pallas_call | solution.py:341
  (3 shorter events, 0.0 us)
Async XLA Ops:
  13.1 16.7 %collective-permute-start.1 = (bf16[512,512]{1,0:T(8,128)(2,1)}, bf16[512,512]{1,0:T(8,128)(2,1)S(1)}, u32[]{:S(2)}, u32[]{:S(2)}) collective-permute-start(bf16[512,512]{1,0:T(8,128)(2,1)} %get-tuple-element.18.refs_0_), channel_id=1, source_target_pairs={{0,4},{1,5},{2,6},{3,7},{4,8},{5,9},{6,10},{7,11},{8,12},{9,13},{1... | collective-permute-start | bytes 1572872 | tf_op jit(solution)/shard_map/ppermute | solution.py:402
  14.4 16.8 %collective-permute-start.7 = (bf16[512,512]{1,0:T(8,128)(2,1)}, bf16[512,512]{1,0:T(8,128)(2,1)S(1)}, u32[]{:S(2)}, u32[]{:S(2)}) collective-permute-start(bf16[512,512]{1,0:T(8,128)(2,1)} %get-tuple-element.18.refs_0_), channel_id=1, source_target_pairs={{0,2},{1,3},{4,6},{5,7},{8,10},{9,11},{12,14},{13,15},{16,18},{17,... | collective-permute-start | bytes 1572872 | tf_op jit(solution)/shard_map/ppermute | solution.py:402
  17.9 68.3 %copy-start.8 = (s32[8,7]{1,0:T(8,128)S(1)}, s32[8,7]{1,0:T(8,128)}, u32[]{:S(2)}) copy-start(s32[8,7]{1,0:T(8,128)} %param.12) | copy-start | bytes 676
  27.2 13.9 %collective-permute-start.5 = (bf16[512,512]{1,0:T(8,128)(2,1)}, bf16[512,512]{1,0:T(8,128)(2,1)S(1)}, u32[]{:S(2)}, u32[]{:S(2)}) collective-permute-start(bf16[512,512]{1,0:T(8,128)(2,1)} %project.1.refs_0_), channel_id=1, source_target_pairs={{0,2},{1,3},{2,0},{3,1},{4,6},{5,7},{8,10},{9,11},{12,14},{13,15},... | collective-permute-start | bytes 1572872 | tf_op jit(solution)/shard_map/ppermute | solution.py:402
  28.5 17.6 %collective-permute-start = (bf16[512,512]{1,0:T(8,128)(2,1)}, bf16[512,512]{1,0:T(8,128)(2,1)S(1)}, u32[]{:S(2)}, u32[]{:S(2)}) collective-permute-start(bf16[512,512]{1,0:T(8,128)(2,1)} %project.1.refs_0_), channel_id=1, source_target_pairs={{0,4},{1,5},{2,6},{3,7},{4,8},{5,9},{6,10},{7,11},{8,12},{9,13},{1... | collective-permute-start | bytes 1572872 | tf_op jit(solution)/shard_map/ppermute | solution.py:402
  29.8 57.5 %copy-start.2 = (bf16[512,512]{1,0:T(8,128)(2,1)}, bf16[512,512]{1,0:T(8,128)(2,1)S(1)}, u32[]{:S(2)}) copy-start(bf16[512,512]{1,0:T(8,128)(2,1)S(1)} %collective-permute-done.1.refs_1_) | copy-start | bytes 1572868
  29.9 26.0 %collective-permute-start.2 = (bf16[512,512]{1,0:T(8,128)(2,1)S(1)}, bf16[512,512]{1,0:T(8,128)(2,1)S(1)}, u32[]{:S(2)}, u32[]{:S(2)}) collective-permute-start(bf16[512,512]{1,0:T(8,128)(2,1)S(1)} %collective-permute-done.1.refs_1_), channel_id=1, source_target_pairs={{4,8},{5,9},{6,10},{7,11},{8,12},{9,13},{10,14},{11,15},{20,24},{2... | collective-permute-start | bytes 1572872 | tf_op jit(solution)/shard_map/ppermute | solution.py:402
  31.2 56.2 %copy-start.3 = (bf16[512,512]{1,0:T(8,128)(2,1)}, bf16[512,512]{1,0:T(8,128)(2,1)S(1)}, u32[]{:S(2)}) copy-start(bf16[512,512]{1,0:T(8,128)(2,1)S(1)} %collective-permute-done.7.refs_4_) | copy-start | bytes 1572868
  31.2 27.3 %collective-permute-start.8 = (bf16[512,512]{1,0:T(8,128)(2,1)S(1)}, bf16[512,512]{1,0:T(8,128)(2,1)S(1)}, u32[]{:S(2)}, u32[]{:S(2)}) collective-permute-start(bf16[512,512]{1,0:T(8,128)(2,1)S(1)} %collective-permute-done.1.refs_1_), channel_id=1, source_target_pairs={{4,6},{5,7},{6,4},{7,5},{8,10},{9,11},{10,8},{11,9},{12,14},{13,15... | collective-permute-start | bytes 1572872 | tf_op jit(solution)/shard_map/ppermute | solution.py:402
  41.1 65.4 %copy-start = (bf16[512,512]{1,0:T(8,128)(2,1)}, bf16[512,512]{1,0:T(8,128)(2,1)S(1)}, u32[]{:S(2)}) copy-start(bf16[512,512]{1,0:T(8,128)(2,1)S(1)} %collective-permute-done.5.refs_4_) | copy-start | bytes 1572868
  46.1 60.5 %copy-start.1 = (bf16[512,512]{1,0:T(8,128)(2,1)}, bf16[512,512]{1,0:T(8,128)(2,1)S(1)}, u32[]{:S(2)}) copy-start(bf16[512,512]{1,0:T(8,128)(2,1)S(1)} %collective-permute-done.refs_1_) | copy-start | bytes 1572868
  46.1 17.4 %collective-permute-start.6 = (bf16[512,512]{1,0:T(8,128)(2,1)S(1)}, bf16[512,512]{1,0:T(8,128)(2,1)S(1)}, u32[]{:S(2)}, u32[]{:S(2)}) collective-permute-start(bf16[512,512]{1,0:T(8,128)(2,1)S(1)} %collective-permute-done.refs_1_), channel_id=1, source_target_pairs={{4,6},{5,7},{6,4},{7,5},{8,10},{9,11},{10,8},{11,9},{12,14},{13,15... | collective-permute-start | bytes 1572872 | tf_op jit(solution)/shard_map/ppermute | solution.py:402
  55.9 31.5 %copy-start.5 = (bf16[512,512]{1,0:T(8,128)(2,1)}, bf16[512,512]{1,0:T(8,128)(2,1)S(1)}, u32[]{:S(2)}) copy-start(bf16[512,512]{1,0:T(8,128)(2,1)S(1)} %collective-permute-done.2.refs_2_) | copy-start | bytes 1572868
  55.9 16.8 %collective-permute-start.11 = (bf16[512,512]{1,0:T(8,128)(2,1)S(1)}, bf16[512,512]{1,0:T(8,128)(2,1)}, u32[]{:S(2)}, u32[]{:S(2)}) collective-permute-start(bf16[512,512]{1,0:T(8,128)(2,1)S(1)} %collective-permute-done.2.refs_2_), channel_id=1, source_target_pairs={{8,12},{9,13},{10,14},{11,15},{24,28},{25,29},{26,30},{27,31}} | collective-permute-start | bytes 1572872 | tf_op jit(solution)/shard_map/ppermute | solution.py:402
  57.2 24.4 %collective-permute-start.3 = (bf16[512,512]{1,0:T(8,128)(2,1)S(1)}, bf16[512,512]{1,0:T(8,128)(2,1)}, u32[]{:S(2)}, u32[]{:S(2)}) collective-permute-start(bf16[512,512]{1,0:T(8,128)(2,1)S(1)} %collective-permute-done.refs_1_), channel_id=1, source_target_pairs={{4,8},{5,9},{6,10},{7,11},{8,12},{9,13},{10,14},{11,15},{20,24},{2... | collective-permute-start | bytes 1572872 | tf_op jit(solution)/shard_map/ppermute | solution.py:402
  58.5 24.4 %copy-start.6 = (bf16[512,512]{1,0:T(8,128)(2,1)}, bf16[512,512]{1,0:T(8,128)(2,1)S(1)}, u32[]{:S(2)}) copy-start(bf16[512,512]{1,0:T(8,128)(2,1)S(1)} %collective-permute-done.8.refs_5_) | copy-start | bytes 1572868
  58.5 24.4 %collective-permute-start.9 = (bf16[512,512]{1,0:T(8,128)(2,1)S(1)}, bf16[512,512]{1,0:T(8,128)(2,1)S(1)}, u32[]{:S(2)}, u32[]{:S(2)}) collective-permute-start(bf16[512,512]{1,0:T(8,128)(2,1)S(1)} %collective-permute-done.2.refs_2_), channel_id=1, source_target_pairs={{8,10},{9,11},{10,8},{11,9},{12,14},{13,15},{14,12},{15,13},{24,26... | collective-permute-start | bytes 1572872 | tf_op jit(solution)/shard_map/ppermute | solution.py:402
  63.5 43.1 %copy-start.4 = (bf16[512,512]{1,0:T(8,128)(2,1)}, bf16[512,512]{1,0:T(8,128)(2,1)S(1)}, u32[]{:S(2)}) copy-start(bf16[512,512]{1,0:T(8,128)(2,1)S(1)} %collective-permute-done.6.refs_5_) | copy-start | bytes 1572868
  72.7 14.6 %collective-permute-start.13 = (bf16[512,512]{1,0:T(8,128)(2,1)}, bf16[512,512]{1,0:T(8,128)(2,1)}, u32[]{:S(2)}, u32[]{:S(2)}) collective-permute-start(bf16[512,512]{1,0:T(8,128)(2,1)} %collective-permute-done.11.refs_3_), channel_id=1, source_target_pairs={{12,14},{13,15},{14,12},{15,13},{28,30},{29,31},{30,28},{31,29}} | collective-permute-start | bytes 1572872 | tf_op jit(solution)/shard_map/ppermute | solution.py:402
  81.6 25.0 %collective-permute-start.4 = (bf16[512,512]{1,0:T(8,128)(2,1)}, bf16[512,512]{1,0:T(8,128)(2,1)}, u32[]{:S(2)}, u32[]{:S(2)}) collective-permute-start(bf16[512,512]{1,0:T(8,128)(2,1)} %collective-permute-done.3.refs_2_), channel_id=1, source_target_pairs={{8,12},{9,13},{10,14},{11,15},{24,28},{25,29},{26,30},{27,31}} | collective-permute-start | bytes 1572872 | tf_op jit(solution)/shard_map/ppermute | solution.py:402
  82.9 1.9 %copy-start.7 = (bf16[512,512]{1,0:T(8,128)(2,1)}, bf16[512,512]{1,0:T(8,128)(2,1)S(1)}, u32[]{:S(2)}) copy-start(bf16[512,512]{1,0:T(8,128)(2,1)S(1)} %collective-permute-done.9.refs_6_) | copy-start | bytes 1572868
  82.9 23.7 %collective-permute-start.10 = (bf16[512,512]{1,0:T(8,128)(2,1)}, bf16[512,512]{1,0:T(8,128)(2,1)}, u32[]{:S(2)}, u32[]{:S(2)}) collective-permute-start(bf16[512,512]{1,0:T(8,128)(2,1)} %collective-permute-done.3.refs_2_), channel_id=1, source_target_pairs={{8,10},{9,11},{10,8},{11,9},{12,14},{13,15},{14,12},{15,13},{24,26... | collective-permute-start | bytes 1572872 | tf_op jit(solution)/shard_map/ppermute | solution.py:402
  84.8 21.7 %collective-permute-start.12 = (bf16[512,512]{1,0:T(8,128)(2,1)S(1)}, bf16[512,512]{1,0:T(8,128)(2,1)}, u32[]{:S(2)}, u32[]{:S(2)}) collective-permute-start(bf16[512,512]{1,0:T(8,128)(2,1)S(1)} %collective-permute-done.5.refs_4_), channel_id=1, source_target_pairs={{0,12},{1,13},{2,14},{3,15},{16,28},{17,29},{18,30},{19,31}} | collective-permute-start | bytes 1572872 | tf_op jit(solution)/shard_map/ppermute | solution.py:402

commit v16 on v15

--- a/solution.py
+++ b/solution.py
@@ -37,13 +37,13 @@
 
 def norm_project_kernel(
     x_hbm, gain_ref, key_hbm, value_hbm, scale_ref, kv_ref,
-    x_scr, weight_scr, even_scr, odd_scr, acc_scr, x_sem, key_sem, value_sem,
+    x_scr, key_scr, value_scr, even_scr, odd_scr, acc_scr, x_sem, key_sem, value_sem,
 ):
     rows, features = x_scr.shape
     loads = LOADS
     tall = rows // loads
-    chunks, chunk = weight_scr.shape[:2]
-    width = weight_scr.shape[2] // 2
+    chunks, chunk = key_scr.shape[:2]
+    width = key_scr.shape[2] // UNITS
     lanes = 128
     band = 128
 
@@ -55,14 +55,9 @@
         return pltpu.make_async_copy(x_hbm.at[row], x_scr.at[row], x_sem.at[c])
 
     def load_weights(c):
-        head = pl.ds(0, width)
         return [
-            pltpu.make_async_copy(
-                key_hbm.at[span(c), head], weight_scr.at[c, :, pl.ds(0, width)], key_sem.at[c]
-            ),
-            pltpu.make_async_copy(
-                value_hbm.at[span(c), head], weight_scr.at[c, :, pl.ds(width, width)], value_sem.at[c]
-            ),
+            pltpu.make_async_copy(hbm.at[span(c)], scr.at[c], sem.at[c])
+            for hbm, scr, sem in ((key_hbm, key_scr, key_sem), (value_hbm, value_scr, value_sem))
         ]
 
     for c in range(loads):
@@ -105,21 +100,26 @@
     def multiply(normed_scr, c):
         for copy in load_weights(c):
             copy.wait()
-        return jnp.dot(normed_scr[...], weight_scr[c], preferred_element_type=jnp.float32)
+        normed = normed_scr[...]
+        for part, weight in enumerate((key_scr, value_scr)):
+            acc_scr[:, part * width : (part + 1) * width] += jnp.dot(
+                normed, weight[c, :, :width], preferred_element_type=jnp.float32
+            )
 
     normalise(even_scr, 0)
-    acc_scr[...] = multiply(even_scr, 0)
-    normalise(odd_scr, 1)
+    acc_scr[...] = jnp.zeros_like(acc_scr)
 
     def pair(p, carry):
-        acc_scr[...] += multiply(odd_scr, 2 * p + 1)
+        multiply(even_scr, 2 * p)
+        normalise(odd_scr, 2 * p + 1)
+        multiply(odd_scr, 2 * p + 1)
         normalise(even_scr, 2 * p + 2)
-        acc_scr[...] += multiply(even_scr, 2 * p + 2)
-        normalise(odd_scr, 2 * p + 3)
         return carry
 
     lax.fori_loop(0, chunks // 2 - 1, pair, 0)
-    acc_scr[...] += multiply(odd_scr, chunks - 1)
+    multiply(even_scr, chunks - 2)
+    normalise(odd_scr, chunks - 1)
+    multiply(odd_scr, chunks - 1)
     write_heads(kv_ref, acc_scr)
 
 
@@ -135,7 +135,7 @@
 def norm_project(hidden, gain, key_weight, value_weight):
     rows, features = hidden.shape
     width = key_weight.shape[1] // UNITS
-    chunk = features // CHUNKS
+    chunk = features // LOADS
     whole = pl.BlockSpec(memory_space=pltpu.VMEM)
     held = pl.BlockSpec(memory_space=pltpu.HBM)
     return pl.pallas_call(
@@ -148,13 +148,14 @@
         ],
         scratch_shapes=[
             pltpu.VMEM((rows, features), jnp.bfloat16),
-            pltpu.VMEM((CHUNKS, chunk, 2 * width), jnp.bfloat16),
+            pltpu.VMEM((LOADS, chunk, key_weight.shape[1]), jnp.bfloat16),
+            pltpu.VMEM((LOADS, chunk, key_weight.shape[1]), jnp.bfloat16),
             pltpu.VMEM((rows, chunk), jnp.bfloat16),
             pltpu.VMEM((rows, chunk), jnp.bfloat16),
             pltpu.VMEM((rows, 2 * width), jnp.float32),
             pltpu.SemaphoreType.DMA((LOADS,)),
-            pltpu.SemaphoreType.DMA((CHUNKS,)),
-            pltpu.SemaphoreType.DMA((CHUNKS,)),
+            pltpu.SemaphoreType.DMA((LOADS,)),
+            pltpu.SemaphoreType.DMA((LOADS,)),
         ],
         compiler_params=pltpu.CompilerParams(vmem_limit_bytes=57 * MIB),
         cost_estimate=pl.CostEstimate(

time: 117 us -> 119 us (1.017)
  Pallas kernels: 42.6 us -> 44.3 us
    pallas_call x1, Pallas kernels: 13.1 us -> 14.7 us  [norm_project(): pl.pallas_call(norm_project_kernel, in_specs=[held, whole, held, held], o...]
  transfers between devices with their start and end apart: 14 -> 14, of which waited for: 8 -> 8; matrix products, arithmetic and copies ran while one was open for 1% -> 1% of each run, Pallas kernels for 17% -> 16%
where the time goes in v16:
time: 119 us; the launch traced here: 118 us
  waiting for transfers between devices  48.8 us (41%)
  Pallas kernels  44.3 us (37%)
  starting transfers between devices  24.3 us (20%)
    ppermute x14, waiting for transfers between devices, step(): moved[key, s, unit] = lax.ppermute(array, 'node', pairs)  48.8 us
    ppermute x14, starting transfers between devices, step(): moved[key, s, unit] = lax.ppermute(array, 'node', pairs)  24.3 us
    pallas_call x2, Pallas kernels, attention(): pl.pallas_call(functools.partial(attention_kernel, block, unit, near), in...  20.2 us
    pallas_call x1, Pallas kernels, norm_project(): pl.pallas_call(norm_project_kernel, in_specs=[held, whole, held, held], o...  14.7 us
    pallas_call x1, Pallas kernels, project(): pl.pallas_call(project_kernel, grid=(CHUNKS,), in_specs=[pl.BlockSpec((ro...  9.35 us
  transfers between devices with their start and end apart: 14, of which 8 were waited for; matrix products, arithmetic and copies ran while one was open for 1% of the time, Pallas kernels for 16%

profile of v16, /device:TPU:24, one launch (start us, length us, event | category | flops | bytes accessed | tf_op | source)
XLA Modules:
  0.0 118.3 jit_solution(12496331365468448477)
XLA Ops:
  0.0 14.7 %norm_project.1 = (f32[512,128]{1,0:T(8,128)}, bf16[512,512]{1,0:T(8,128)(2,1)}) custom-call(bf16[512,8192]{1,0:T(8,128)(2,1)} %x_ref.1, f32[1,8192]{1,0:T(1,128)} %bitcast.2, bf16[8192,512]{1,0:T(8,128)(2,1)} %key_ref.1, bf16[8192,512]{1,0:T(8,128)(2,1)} %value_ref.1), custom_call_target="tpu_custom_call" | custom-call | flops 4294967296 | bytes 16777216 | tf_op jit(solution)/shard_map/norm_project/pallas_call | solution.py:141
  14.7 1.3 %collective-permute-start.1 = (bf16[512,512]{1,0:T(8,128)(2,1)}, bf16[512,512]{1,0:T(8,128)(2,1)S(1)}, u32[]{:S(2)}, u32[]{:S(2)}) collective-permute-start(bf16[512,512]{1,0:T(8,128)(2,1)} %get-tuple-element.18.refs_0_), channel_id=1, source_target_pairs={{0,4},{1,5},{2,6},{3,7},{4,8},{5,9},{6,10},{7,11},{8,12},{9,13},{1... | collective-permute-start | bytes 1572872 | tf_op jit(solution)/shard_map/ppermute | solution.py:403
  16.0 3.5 %collective-permute-start.7 = (bf16[512,512]{1,0:T(8,128)(2,1)}, bf16[512,512]{1,0:T(8,128)(2,1)S(1)}, u32[]{:S(2)}, u32[]{:S(2)}) collective-permute-start(bf16[512,512]{1,0:T(8,128)(2,1)} %get-tuple-element.18.refs_0_), channel_id=1, source_target_pairs={{0,2},{1,3},{4,6},{5,7},{8,10},{9,11},{12,14},{13,15},{16,18},{17,... | collective-permute-start | bytes 1572872 | tf_op jit(solution)/shard_map/ppermute | solution.py:403
  19.5 0.0 copy-start.8
  19.5 9.3 %project.1.refs_0_ = bf16[512,512]{1,0:T(8,128)(2,1)} custom-call(bf16[512,8192]{1,0:T(8,128)(2,1)} %x_ref.1, f32[512,128]{1,0:T(8,128)} %get-tuple-element.17.scale_ref, f32[1,8192]{1,0:T(1,128)} %bitcast.3, bf16[8192,512]{1,0:T(8,128)(2,1)} %key_ref.1, bf16[8192,512]{1,0:T(8,128)(2,1)} %value_ref.1), custom_call_target="tpu_custom_call" | custom-call | flops 4294967296 | bytes 16777216 | tf_op jit(solution)/shard_map/project/pallas_call | solution.py:195
  28.9 1.3 %collective-permute-start.5 = (bf16[512,512]{1,0:T(8,128)(2,1)}, bf16[512,512]{1,0:T(8,128)(2,1)S(1)}, u32[]{:S(2)}, u32[]{:S(2)}) collective-permute-start(bf16[512,512]{1,0:T(8,128)(2,1)} %project.1.refs_0_), channel_id=1, source_target_pairs={{0,2},{1,3},{2,0},{3,1},{4,6},{5,7},{8,10},{9,11},{12,14},{13,15},... | collective-permute-start | bytes 1572872 | tf_op jit(solution)/shard_map/ppermute | solution.py:403
  30.2 1.3 %collective-permute-start = (bf16[512,512]{1,0:T(8,128)(2,1)}, bf16[512,512]{1,0:T(8,128)(2,1)S(1)}, u32[]{:S(2)}, u32[]{:S(2)}) collective-permute-start(bf16[512,512]{1,0:T(8,128)(2,1)} %project.1.refs_0_), channel_id=1, source_target_pairs={{0,4},{1,5},{2,6},{3,7},{4,8},{5,9},{6,10},{7,11},{8,12},{9,13},{1... | collective-permute-start | bytes 1572872 | tf_op jit(solution)/shard_map/ppermute | solution.py:403
  31.5 0.0 collective-permute-done.1.refs_1_
  31.5 0.0 copy-start.2
  31.5 1.3 %collective-permute-start.2 = (bf16[512,512]{1,0:T(8,128)(2,1)S(1)}, bf16[512,512]{1,0:T(8,128)(2,1)S(1)}, u32[]{:S(2)}, u32[]{:S(2)}) collective-permute-start(bf16[512,512]{1,0:T(8,128)(2,1)S(1)} %collective-permute-done.1.refs_1_), channel_id=1, source_target_pairs={{4,8},{5,9},{6,10},{7,11},{8,12},{9,13},{10,14},{11,15},{20,24},{2... | collective-permute-start | bytes 1572872 | tf_op jit(solution)/shard_map/ppermute | solution.py:403
  32.8 0.0 collective-permute-done.7.refs_4_
  32.8 0.0 copy-start.3
  32.8 2.9 %collective-permute-start.8 = (bf16[512,512]{1,0:T(8,128)(2,1)S(1)}, bf16[512,512]{1,0:T(8,128)(2,1)S(1)}, u32[]{:S(2)}, u32[]{:S(2)}) collective-permute-start(bf16[512,512]{1,0:T(8,128)(2,1)S(1)} %collective-permute-done.1.refs_1_), channel_id=1, source_target_pairs={{4,6},{5,7},{6,4},{7,5},{8,10},{9,11},{10,8},{11,9},{12,14},{13,15... | collective-permute-start | bytes 1572872 | tf_op jit(solution)/shard_map/ppermute | solution.py:403
  35.7 7.1 %collective-permute-done.5.refs_4_ = bf16[512,512]{1,0:T(8,128)(2,1)S(1)} collective-permute-done((bf16[512,512]{1,0:T(8,128)(2,1)}, bf16[512,512]{1,0:T(8,128)(2,1)S(1)}, u32[]{:S(2)}, u32[]{:S(2)}) %collective-permute-start.5) | collective-permute-done | bytes 524320 | tf_op jit(solution)/shard_map/ppermute | solution.py:403
  42.8 0.0 copy-start
  42.8 5.0 %collective-permute-done.refs_1_ = bf16[512,512]{1,0:T(8,128)(2,1)S(1)} collective-permute-done((bf16[512,512]{1,0:T(8,128)(2,1)}, bf16[512,512]{1,0:T(8,128)(2,1)S(1)}, u32[]{:S(2)}, u32[]{:S(2)}) %collective-permute-start) | collective-permute-done | bytes 524320 | tf_op jit(solution)/shard_map/ppermute | solution.py:403
  47.8 1.9 %collective-permute-start.6 = (bf16[512,512]{1,0:T(8,128)(2,1)S(1)}, bf16[512,512]{1,0:T(8,128)(2,1)S(1)}, u32[]{:S(2)}, u32[]{:S(2)}) collective-permute-start(bf16[512,512]{1,0:T(8,128)(2,1)S(1)} %collective-permute-done.refs_1_), channel_id=1, source_target_pairs={{4,6},{5,7},{6,4},{7,5},{8,10},{9,11},{10,8},{11,9},{12,14},{13,15... | collective-permute-start | bytes 1572872 | tf_op jit(solution)/shard_map/ppermute | solution.py:403
  49.7 7.8 %collective-permute-done.2.refs_2_ = bf16[512,512]{1,0:T(8,128)(2,1)S(1)} collective-permute-done((bf16[512,512]{1,0:T(8,128)(2,1)S(1)}, bf16[512,512]{1,0:T(8,128)(2,1)S(1)}, u32[]{:S(2)}, u32[]{:S(2)}) %collective-permute-start.2) | collective-permute-done | bytes 524320 | tf_op jit(solution)/shard_map/ppermute | solution.py:403
  57.5 1.3 %collective-permute-start.11 = (bf16[512,512]{1,0:T(8,128)(2,1)S(1)}, bf16[512,512]{1,0:T(8,128)(2,1)}, u32[]{:S(2)}, u32[]{:S(2)}) collective-permute-start(bf16[512,512]{1,0:T(8,128)(2,1)S(1)} %collective-permute-done.2.refs_2_), channel_id=1, source_target_pairs={{8,12},{9,13},{10,14},{11,15},{24,28},{25,29},{26,30},{27,31}} | collective-permute-start | bytes 1572872 | tf_op jit(solution)/shard_map/ppermute | solution.py:403
  58.8 1.3 %collective-permute-start.3 = (bf16[512,512]{1,0:T(8,128)(2,1)S(1)}, bf16[512,512]{1,0:T(8,128)(2,1)}, u32[]{:S(2)}, u32[]{:S(2)}) collective-permute-start(bf16[512,512]{1,0:T(8,128)(2,1)S(1)} %collective-permute-done.refs_1_), channel_id=1, source_target_pairs={{4,8},{5,9},{6,10},{7,11},{8,12},{9,13},{10,14},{11,15},{20,24},{2... | collective-permute-start | bytes 1572872 | tf_op jit(solution)/shard_map/ppermute | solution.py:403
  60.1 0.0 collective-permute-done.8.refs_5_
  60.1 0.0 copy-start.6
  60.1 1.9 %collective-permute-start.9 = (bf16[512,512]{1,0:T(8,128)(2,1)S(1)}, bf16[512,512]{1,0:T(8,128)(2,1)S(1)}, u32[]{:S(2)}, u32[]{:S(2)}) collective-permute-start(bf16[512,512]{1,0:T(8,128)(2,1)S(1)} %collective-permute-done.2.refs_2_), channel_id=1, source_target_pairs={{8,10},{9,11},{10,8},{11,9},{12,14},{13,15},{14,12},{15,13},{24,26... | collective-permute-start | bytes 1572872 | tf_op jit(solution)/shard_map/ppermute | solution.py:403
  62.1 3.1 %collective-permute-done.6.refs_5_ = bf16[512,512]{1,0:T(8,128)(2,1)S(1)} collective-permute-done((bf16[512,512]{1,0:T(8,128)(2,1)S(1)}, bf16[512,512]{1,0:T(8,128)(2,1)S(1)}, u32[]{:S(2)}, u32[]{:S(2)}) %collective-permute-start.6) | collective-permute-done | bytes 524320 | tf_op jit(solution)/shard_map/ppermute | solution.py:403
  65.1 9.2 %collective-permute-done.11.refs_3_ = bf16[512,512]{1,0:T(8,128)(2,1)} collective-permute-done((bf16[512,512]{1,0:T(8,128)(2,1)S(1)}, bf16[512,512]{1,0:T(8,128)(2,1)}, u32[]{:S(2)}, u32[]{:S(2)}) %collective-permute-start.11) | collective-permute-done | bytes 524320 | tf_op jit(solution)/shard_map/ppermute | solution.py:403
  74.4 1.9 %collective-permute-start.13 = (bf16[512,512]{1,0:T(8,128)(2,1)}, bf16[512,512]{1,0:T(8,128)(2,1)}, u32[]{:S(2)}, u32[]{:S(2)}) collective-permute-start(bf16[512,512]{1,0:T(8,128)(2,1)} %collective-permute-done.11.refs_3_), channel_id=1, source_target_pairs={{12,14},{13,15},{14,12},{15,13},{28,30},{29,31},{30,28},{31,29}} | collective-permute-start | bytes 1572872 | tf_op jit(solution)/shard_map/ppermute | solution.py:403
  76.3 6.9 %collective-permute-done.3.refs_2_ = bf16[512,512]{1,0:T(8,128)(2,1)} collective-permute-done((bf16[512,512]{1,0:T(8,128)(2,1)S(1)}, bf16[512,512]{1,0:T(8,128)(2,1)}, u32[]{:S(2)}, u32[]{:S(2)}) %collective-permute-start.3) | collective-permute-done | bytes 524320 | tf_op jit(solution)/shard_map/ppermute | solution.py:403
  83.2 1.3 %collective-permute-start.4 = (bf16[512,512]{1,0:T(8,128)(2,1)}, bf16[512,512]{1,0:T(8,128)(2,1)}, u32[]{:S(2)}, u32[]{:S(2)}) collective-permute-start(bf16[512,512]{1,0:T(8,128)(2,1)} %collective-permute-done.3.refs_2_), channel_id=1, source_target_pairs={{8,12},{9,13},{10,14},{11,15},{24,28},{25,29},{26,30},{27,31}} | collective-permute-start | bytes 1572872 | tf_op jit(solution)/shard_map/ppermute | solution.py:403
  84.5 0.0 collective-permute-done.9.refs_6_
  84.5 0.0 copy-done.6
  84.5 0.0 copy-start.7
  84.5 1.9 %collective-permute-start.10 = (bf16[512,512]{1,0:T(8,128)(2,1)}, bf16[512,512]{1,0:T(8,128)(2,1)}, u32[]{:S(2)}, u32[]{:S(2)}) collective-permute-start(bf16[512,512]{1,0:T(8,128)(2,1)} %collective-permute-done.3.refs_2_), channel_id=1, source_target_pairs={{8,10},{9,11},{10,8},{11,9},{12,14},{13,15},{14,12},{15,13},{24,26... | collective-permute-start | bytes 1572872 | tf_op jit(solution)/shard_map/ppermute | solution.py:403
  86.5 0.0 copy-done.7
  86.5 1.3 %collective-permute-start.12 = (bf16[512,512]{1,0:T(8,128)(2,1)S(1)}, bf16[512,512]{1,0:T(8,128)(2,1)}, u32[]{:S(2)}, u32[]{:S(2)}) collective-permute-start(bf16[512,512]{1,0:T(8,128)(2,1)S(1)} %collective-permute-done.5.refs_4_), channel_id=1, source_target_pairs={{0,12},{1,13},{2,14},{3,15},{16,28},{17,29},{18,30},{19,31}} | collective-permute-start | bytes 1572872 | tf_op jit(solution)/shard_map/ppermute | solution.py:403
  87.8 0.0 copy-done.8
  87.8 0.6 fusion.1.slot_ref
  88.4 0.6 collective-permute-done.13.refs_7_
  89.0 0.0 copy-done.2
  89.0 0.0 copy-done.3
  89.0 0.0 copy-done.5
  89.0 10.1 %attention.2.refs_8_ = bf16[512,4096]{1,0:T(8,128)(2,1)} custom-call(s32[8,7]{1,0:T(8,128)} %fusion.1.slot_ref, s32[8,7]{1,0:T(8,128)} %cut_ref.3, s32[1]{0:T(128)} %bitcast.odd_ref, bf16[512,4096]{1,0:T(8,128)(2,1)} %q_hbm.3, bf16[512,512]{1,0:T(8,128)(2,1)} %get-tuple-element.18.refs_0_, bf16[512,512]{1,0:T(8,128)(2,1)} %copy-done.2, ...), custom_call_target="tpu_custom_call" | custom-call | flops 2147483648 | bytes 8388608 | tf_op jit(solution)/shard_map/attention/pallas_call | solution.py:342
  99.1 9.1 %collective-permute-done.4.refs_3_ = bf16[512,512]{1,0:T(8,128)(2,1)} collective-permute-done((bf16[512,512]{1,0:T(8,128)(2,1)}, bf16[512,512]{1,0:T(8,128)(2,1)}, u32[]{:S(2)}, u32[]{:S(2)}) %collective-permute-start.4) | collective-permute-done | bytes 524320 | tf_op jit(solution)/shard_map/ppermute | solution.py:403
  108.2 0.0 collective-permute-done.10.refs_6_
  108.2 0.0 collective-permute-done.12.refs_7_
  108.2 0.0 copy-done
  108.2 0.0 copy-done.1
  108.2 0.0 copy-done.4
  108.2 10.1 %attention.3 = bf16[512,4096]{1,0:T(8,128)(2,1)} custom-call(s32[8,7]{1,0:T(8,128)} %fusion.1.slot_ref, s32[8,7]{1,0:T(8,128)} %cut_ref.3, s32[1]{0:T(128)} %bitcast.odd_ref, bf16[512,4096]{1,0:T(8,128)(2,1)} %q_hbm.3, bf16[512,512]{1,0:T(8,128)(2,1)} %project.1.refs_0_, bf16[512,512]{1,0:T(8,128)(2,1)} %copy-done.1, ...), custom_call_target="tpu_custom_call", output_to_operand_aliasing={{}: (12, {})} | custom-call | flops 2147483648 | bytes 8388608 | tf_op jit(solution)/shard_map/attention/pallas_call | solution.py:342
  (3 shorter events, 0.0 us)
Async XLA Ops:
  14.7 16.7 %collective-permute-start.1 = (bf16[512,512]{1,0:T(8,128)(2,1)}, bf16[512,512]{1,0:T(8,128)(2,1)S(1)}, u32[]{:S(2)}, u32[]{:S(2)}) collective-permute-start(bf16[512,512]{1,0:T(8,128)(2,1)} %get-tuple-element.18.refs_0_), channel_id=1, source_target_pairs={{0,4},{1,5},{2,6},{3,7},{4,8},{5,9},{6,10},{7,11},{8,12},{9,13},{1... | collective-permute-start | bytes 1572872 | tf_op jit(solution)/shard_map/ppermute | solution.py:403
  16.0 16.8 %collective-permute-start.7 = (bf16[512,512]{1,0:T(8,128)(2,1)}, bf16[512,512]{1,0:T(8,128)(2,1)S(1)}, u32[]{:S(2)}, u32[]{:S(2)}) collective-permute-start(bf16[512,512]{1,0:T(8,128)(2,1)} %get-tuple-element.18.refs_0_), channel_id=1, source_target_pairs={{0,2},{1,3},{4,6},{5,7},{8,10},{9,11},{12,14},{13,15},{16,18},{17,... | collective-permute-start | bytes 1572872 | tf_op jit(solution)/shard_map/ppermute | solution.py:403
  19.5 68.3 %copy-start.8 = (s32[8,7]{1,0:T(8,128)S(1)}, s32[8,7]{1,0:T(8,128)}, u32[]{:S(2)}) copy-start(s32[8,7]{1,0:T(8,128)} %param.12) | copy-start | bytes 676
  28.9 13.9 %collective-permute-start.5 = (bf16[512,512]{1,0:T(8,128)(2,1)}, bf16[512,512]{1,0:T(8,128)(2,1)S(1)}, u32[]{:S(2)}, u32[]{:S(2)}) collective-permute-start(bf16[512,512]{1,0:T(8,128)(2,1)} %project.1.refs_0_), channel_id=1, source_target_pairs={{0,2},{1,3},{2,0},{3,1},{4,6},{5,7},{8,10},{9,11},{12,14},{13,15},... | collective-permute-start | bytes 1572872 | tf_op jit(solution)/shard_map/ppermute | solution.py:403
  30.2 17.6 %collective-permute-start = (bf16[512,512]{1,0:T(8,128)(2,1)}, bf16[512,512]{1,0:T(8,128)(2,1)S(1)}, u32[]{:S(2)}, u32[]{:S(2)}) collective-permute-start(bf16[512,512]{1,0:T(8,128)(2,1)} %project.1.refs_0_), channel_id=1, source_target_pairs={{0,4},{1,5},{2,6},{3,7},{4,8},{5,9},{6,10},{7,11},{8,12},{9,13},{1... | collective-permute-start | bytes 1572872 | tf_op jit(solution)/shard_map/ppermute | solution.py:403
  31.5 57.5 %copy-start.2 = (bf16[512,512]{1,0:T(8,128)(2,1)}, bf16[512,512]{1,0:T(8,128)(2,1)S(1)}, u32[]{:S(2)}) copy-start(bf16[512,512]{1,0:T(8,128)(2,1)S(1)} %collective-permute-done.1.refs_1_) | copy-start | bytes 1572868
  31.5 26.0 %collective-permute-start.2 = (bf16[512,512]{1,0:T(8,128)(2,1)S(1)}, bf16[512,512]{1,0:T(8,128)(2,1)S(1)}, u32[]{:S(2)}, u32[]{:S(2)}) collective-permute-start(bf16[512,512]{1,0:T(8,128)(2,1)S(1)} %collective-permute-done.1.refs_1_), channel_id=1, source_target_pairs={{4,8},{5,9},{6,10},{7,11},{8,12},{9,13},{10,14},{11,15},{20,24},{2... | collective-permute-start | bytes 1572872 | tf_op jit(solution)/shard_map/ppermute | solution.py:403
  32.8 56.2 %copy-start.3 = (bf16[512,512]{1,0:T(8,128)(2,1)}, bf16[512,512]{1,0:T(8,128)(2,1)S(1)}, u32[]{:S(2)}) copy-start(bf16[512,512]{1,0:T(8,128)(2,1)S(1)} %collective-permute-done.7.refs_4_) | copy-start | bytes 1572868
  32.8 27.3 %collective-permute-start.8 = (bf16[512,512]{1,0:T(8,128)(2,1)S(1)}, bf16[512,512]{1,0:T(8,128)(2,1)S(1)}, u32[]{:S(2)}, u32[]{:S(2)}) collective-permute-start(bf16[512,512]{1,0:T(8,128)(2,1)S(1)} %collective-permute-done.1.refs_1_), channel_id=1, source_target_pairs={{4,6},{5,7},{6,4},{7,5},{8,10},{9,11},{10,8},{11,9},{12,14},{13,15... | collective-permute-start | bytes 1572872 | tf_op jit(solution)/shard_map/ppermute | solution.py:403
  42.8 65.4 %copy-start = (bf16[512,512]{1,0:T(8,128)(2,1)}, bf16[512,512]{1,0:T(8,128)(2,1)S(1)}, u32[]{:S(2)}) copy-start(bf16[512,512]{1,0:T(8,128)(2,1)S(1)} %collective-permute-done.5.refs_4_) | copy-start | bytes 1572868
  47.8 60.5 %copy-start.1 = (bf16[512,512]{1,0:T(8,128)(2,1)}, bf16[512,512]{1,0:T(8,128)(2,1)S(1)}, u32[]{:S(2)}) copy-start(bf16[512,512]{1,0:T(8,128)(2,1)S(1)} %collective-permute-done.refs_1_) | copy-start | bytes 1572868
  47.8 17.4 %collective-permute-start.6 = (bf16[512,512]{1,0:T(8,128)(2,1)S(1)}, bf16[512,512]{1,0:T(8,128)(2,1)S(1)}, u32[]{:S(2)}, u32[]{:S(2)}) collective-permute-start(bf16[512,512]{1,0:T(8,128)(2,1)S(1)} %collective-permute-done.refs_1_), channel_id=1, source_target_pairs={{4,6},{5,7},{6,4},{7,5},{8,10},{9,11},{10,8},{11,9},{12,14},{13,15... | collective-permute-start | bytes 1572872 | tf_op jit(solution)/shard_map/ppermute | solution.py:403
  57.5 31.5 %copy-start.5 = (bf16[512,512]{1,0:T(8,128)(2,1)}, bf16[512,512]{1,0:T(8,128)(2,1)S(1)}, u32[]{:S(2)}) copy-start(bf16[512,512]{1,0:T(8,128)(2,1)S(1)} %collective-permute-done.2.refs_2_) | copy-start | bytes 1572868
  57.5 16.8 %collective-permute-start.11 = (bf16[512,512]{1,0:T(8,128)(2,1)S(1)}, bf16[512,512]{1,0:T(8,128)(2,1)}, u32[]{:S(2)}, u32[]{:S(2)}) collective-permute-start(bf16[512,512]{1,0:T(8,128)(2,1)S(1)} %collective-permute-done.2.refs_2_), channel_id=1, source_target_pairs={{8,12},{9,13},{10,14},{11,15},{24,28},{25,29},{26,30},{27,31}} | collective-permute-start | bytes 1572872 | tf_op jit(solution)/shard_map/ppermute | solution.py:403
  58.8 24.4 %collective-permute-start.3 = (bf16[512,512]{1,0:T(8,128)(2,1)S(1)}, bf16[512,512]{1,0:T(8,128)(2,1)}, u32[]{:S(2)}, u32[]{:S(2)}) collective-permute-start(bf16[512,512]{1,0:T(8,128)(2,1)S(1)} %collective-permute-done.refs_1_), channel_id=1, source_target_pairs={{4,8},{5,9},{6,10},{7,11},{8,12},{9,13},{10,14},{11,15},{20,24},{2... | collective-permute-start | bytes 1572872 | tf_op jit(solution)/shard_map/ppermute | solution.py:403
  60.1 24.4 %copy-start.6 = (bf16[512,512]{1,0:T(8,128)(2,1)}, bf16[512,512]{1,0:T(8,128)(2,1)S(1)}, u32[]{:S(2)}) copy-start(bf16[512,512]{1,0:T(8,128)(2,1)S(1)} %collective-permute-done.8.refs_5_) | copy-start | bytes 1572868
  60.1 24.4 %collective-permute-start.9 = (bf16[512,512]{1,0:T(8,128)(2,1)S(1)}, bf16[512,512]{1,0:T(8,128)(2,1)S(1)}, u32[]{:S(2)}, u32[]{:S(2)}) collective-permute-start(bf16[512,512]{1,0:T(8,128)(2,1)S(1)} %collective-permute-done.2.refs_2_), channel_id=1, source_target_pairs={{8,10},{9,11},{10,8},{11,9},{12,14},{13,15},{14,12},{15,13},{24,26... | collective-permute-start | bytes 1572872 | tf_op jit(solution)/shard_map/ppermute | solution.py:403
  65.1 43.1 %copy-start.4 = (bf16[512,512]{1,0:T(8,128)(2,1)}, bf16[512,512]{1,0:T(8,128)(2,1)S(1)}, u32[]{:S(2)}) copy-start(bf16[512,512]{1,0:T(8,128)(2,1)S(1)} %collective-permute-done.6.refs_5_) | copy-start | bytes 1572868
  74.4 14.6 %collective-permute-start.13 = (bf16[512,512]{1,0:T(8,128)(2,1)}, bf16[512,512]{1,0:T(8,128)(2,1)}, u32[]{:S(2)}, u32[]{:S(2)}) collective-permute-start(bf16[512,512]{1,0:T(8,128)(2,1)} %collective-permute-done.11.refs_3_), channel_id=1, source_target_pairs={{12,14},{13,15},{14,12},{15,13},{28,30},{29,31},{30,28},{31,29}} | collective-permute-start | bytes 1572872 | tf_op jit(solution)/shard_map/ppermute | solution.py:403
  83.2 25.0 %collective-permute-start.4 = (bf16[512,512]{1,0:T(8,128)(2,1)}, bf16[512,512]{1,0:T(8,128)(2,1)}, u32[]{:S(2)}, u32[]{:S(2)}) collective-permute-start(bf16[512,512]{1,0:T(8,128)(2,1)} %collective-permute-done.3.refs_2_), channel_id=1, source_target_pairs={{8,12},{9,13},{10,14},{11,15},{24,28},{25,29},{26,30},{27,31}} | collective-permute-start | bytes 1572872 | tf_op jit(solution)/shard_map/ppermute | solution.py:403
  84.5 1.9 %copy-start.7 = (bf16[512,512]{1,0:T(8,128)(2,1)}, bf16[512,512]{1,0:T(8,128)(2,1)S(1)}, u32[]{:S(2)}) copy-start(bf16[512,512]{1,0:T(8,128)(2,1)S(1)} %collective-permute-done.9.refs_6_) | copy-start | bytes 1572868
  84.5 23.7 %collective-permute-start.10 = (bf16[512,512]{1,0:T(8,128)(2,1)}, bf16[512,512]{1,0:T(8,128)(2,1)}, u32[]{:S(2)}, u32[]{:S(2)}) collective-permute-start(bf16[512,512]{1,0:T(8,128)(2,1)} %collective-permute-done.3.refs_2_), channel_id=1, source_target_pairs={{8,10},{9,11},{10,8},{11,9},{12,14},{13,15},{14,12},{15,13},{24,26... | collective-permute-start | bytes 1572872 | tf_op jit(solution)/shard_map/ppermute | solution.py:403
  86.5 21.7 %collective-permute-start.12 = (bf16[512,512]{1,0:T(8,128)(2,1)S(1)}, bf16[512,512]{1,0:T(8,128)(2,1)}, u32[]{:S(2)}, u32[]{:S(2)}) collective-permute-start(bf16[512,512]{1,0:T(8,128)(2,1)S(1)} %collective-permute-done.5.refs_4_), channel_id=1, source_target_pairs={{0,12},{1,13},{2,14},{3,15},{16,28},{17,29},{18,30},{19,31}} | collective-permute-start | bytes 1572872 | tf_op jit(solution)/shard_map/ppermute | solution.py:403

commit v17 on v13

--- a/solution.py
+++ b/solution.py
@@ -14,7 +14,7 @@
 CHUNKS = 4
 LOADS = 8
 UNITS = 2
-BLOCKS_PER_STEP = 4
+BLOCKS_PER_STEP = 8
 
 
 PLAN = (
@@ -30,8 +30,8 @@
     ("along", 2, 1, (("along", 2, 0),)),
     ("across", 3, 0, (("across", 1, 1),)),
     ("across", 2, 1, (("across", 2, 0),)),
-    ("down", 3, 1, (("along", 3, 0), ("across", 2, 0))),
-    ("along", 3, 1, (("along", 2, 1),)),
+    ("down", 3, 1, (("along", 3, 0),)),
+    ("along", 3, 1, (("along", 2, 1), ("down", 3, 1))),
 )
 
 

time: 117 us -> 119 us (1.017); the launches traced: 117 us -> 117 us
  starting transfers between devices: 24.3 us -> 27.5 us
  waiting for transfers between devices: 48.8 us -> 46.4 us
    ppermute x14, starting transfers between devices: 24.3 us -> 27.5 us  [step(): moved[key, s, unit] = lax.ppermute(array, 'node', pairs)]
    ppermute x14, waiting for transfers between devices: 48.8 us -> 46.4 us  [step(): moved[key, s, unit] = lax.ppermute(array, 'node', pairs)]
  transfers between devices with their start and end apart: 14 -> 14, of which waited for: 8 -> 6; matrix products, arithmetic and copies ran while one was open for 1% -> 1% of each run, Pallas kernels for 17% -> 16%
where the time goes in v17:
time: 119 us; the launch traced here: 117 us
  waiting for transfers between devices  46.4 us (39%)
  Pallas kernels  42.2 us (35%)
  starting transfers between devices  27.5 us (23%)
    ppermute x14, waiting for transfers between devices, step(): moved[key, s, unit] = lax.ppermute(array, 'node', pairs)  46.4 us
    ppermute x14, starting transfers between devices, step(): moved[key, s, unit] = lax.ppermute(array, 'node', pairs)  27.5 us
    pallas_call x2, Pallas kernels, attention(): pl.pallas_call(functools.partial(attention_kernel, block, unit, near), in...  19.6 us
    pallas_call x1, Pallas kernels, norm_project(): pl.pallas_call(norm_project_kernel, in_specs=[held, whole, held, held], o...  13.3 us
    pallas_call x1, Pallas kernels, project(): pl.pallas_call(project_kernel, grid=(CHUNKS,), in_specs=[pl.BlockSpec((ro...  9.36 us
  transfers between devices with their start and end apart: 14, of which 6 were waited for; matrix products, arithmetic and copies ran while one was open for 1% of the time, Pallas kernels for 16%

profile of v17, /device:TPU:24, one launch (start us, length us, event | category | flops | bytes accessed | tf_op | source)
XLA Modules:
  0.0 117.1 jit_solution(10886375914490133066)
XLA Ops:
  0.0 13.3 %norm_project.1 = (f32[512,128]{1,0:T(8,128)}, bf16[512,512]{1,0:T(8,128)(2,1)}) custom-call(bf16[512,8192]{1,0:T(8,128)(2,1)} %x_ref.1, f32[8,1,1024]{2,1,0:T(1,128)} %bitcast.3, bf16[8192,512]{1,0:T(8,128)(2,1)} %key_ref.1, bf16[8192,512]{1,0:T(8,128)(2,1)} %value_ref.1), custom_call_target="tpu_custom_call" | custom-call | flops 4294967296 | bytes 16777216 | tf_op jit(solution)/shard_map/norm_project/pallas_call | solution.py:139
  13.3 1.3 %collective-permute-start.1 = (bf16[512,512]{1,0:T(8,128)(2,1)}, bf16[512,512]{1,0:T(8,128)(2,1)S(1)}, u32[]{:S(2)}, u32[]{:S(2)}) collective-permute-start(bf16[512,512]{1,0:T(8,128)(2,1)} %get-tuple-element.18.refs_0_), channel_id=1, source_target_pairs={{0,4},{1,5},{2,6},{3,7},{4,8},{5,9},{6,10},{7,11},{8,12},{9,13},{1... | collective-permute-start | bytes 1572872 | tf_op jit(solution)/shard_map/ppermute | solution.py:400
  14.6 3.5 %collective-permute-start.9 = (bf16[512,512]{1,0:T(8,128)(2,1)}, bf16[512,512]{1,0:T(8,128)(2,1)S(1)}, u32[]{:S(2)}, u32[]{:S(2)}) collective-permute-start(bf16[512,512]{1,0:T(8,128)(2,1)} %get-tuple-element.18.refs_0_), channel_id=1, source_target_pairs={{0,2},{1,3},{4,6},{5,7},{8,10},{9,11},{12,14},{13,15},{16,18},{17,... | collective-permute-start | bytes 1572872 | tf_op jit(solution)/shard_map/ppermute | solution.py:400
  18.1 0.0 copy-start.9
  18.1 9.4 %project.1.refs_0_ = bf16[512,512]{1,0:T(8,128)(2,1)} custom-call(bf16[512,8192]{1,0:T(8,128)(2,1)} %x_ref.1, f32[512,128]{1,0:T(8,128)} %get-tuple-element.17.scale_ref, f32[1,8192]{1,0:T(1,128)} %bitcast.4, bf16[8192,512]{1,0:T(8,128)(2,1)} %key_ref.1, bf16[8192,512]{1,0:T(8,128)(2,1)} %value_ref.1), custom_call_target="tpu_custom_call" | custom-call | flops 4294967296 | bytes 16777216 | tf_op jit(solution)/shard_map/project/pallas_call | solution.py:192
  27.4 1.3 %collective-permute-start = (bf16[512,512]{1,0:T(8,128)(2,1)}, bf16[512,512]{1,0:T(8,128)(2,1)S(1)}, u32[]{:S(2)}, u32[]{:S(2)}) collective-permute-start(bf16[512,512]{1,0:T(8,128)(2,1)} %project.1.refs_0_), channel_id=1, source_target_pairs={{0,4},{1,5},{2,6},{3,7},{4,8},{5,9},{6,10},{7,11},{8,12},{9,13},{1... | collective-permute-start | bytes 1572872 | tf_op jit(solution)/shard_map/ppermute | solution.py:400
  28.7 0.3 collective-permute-done.1.refs_1_
  29.1 1.3 %collective-permute-start.2 = (bf16[512,512]{1,0:T(8,128)(2,1)S(1)}, bf16[512,512]{1,0:T(8,128)(2,1)S(1)}, u32[]{:S(2)}, u32[]{:S(2)}) collective-permute-start(bf16[512,512]{1,0:T(8,128)(2,1)S(1)} %collective-permute-done.1.refs_1_), channel_id=1, source_target_pairs={{4,8},{5,9},{6,10},{7,11},{8,12},{9,13},{10,14},{11,15},{20,24},{2... | collective-permute-start | bytes 1572872 | tf_op jit(solution)/shard_map/ppermute | solution.py:400
  30.4 3.5 %collective-permute-start.4 = (bf16[512,512]{1,0:T(8,128)(2,1)}, bf16[512,512]{1,0:T(8,128)(2,1)S(1)}, u32[]{:S(2)}, u32[]{:S(2)}) collective-permute-start(bf16[512,512]{1,0:T(8,128)(2,1)} %project.1.refs_0_), channel_id=1, source_target_pairs={{0,2},{1,3},{2,0},{3,1},{4,6},{5,7},{8,10},{9,11},{12,14},{13,15},... | collective-permute-start | bytes 1572872 | tf_op jit(solution)/shard_map/ppermute | solution.py:400
  33.8 0.0 collective-permute-done.9.refs_4_
  33.8 0.0 copy-start.2
  33.8 1.9 %collective-permute-start.10 = (bf16[512,512]{1,0:T(8,128)(2,1)S(1)}, bf16[512,512]{1,0:T(8,128)(2,1)S(1)}, u32[]{:S(2)}, u32[]{:S(2)}) collective-permute-start(bf16[512,512]{1,0:T(8,128)(2,1)S(1)} %collective-permute-done.1.refs_1_), channel_id=1, source_target_pairs={{4,6},{5,7},{6,4},{7,5},{8,10},{9,11},{10,8},{11,9},{12,14},{13,15... | collective-permute-start | bytes 1572872 | tf_op jit(solution)/shard_map/ppermute | solution.py:400
  35.8 9.2 %collective-permute-done.refs_1_ = bf16[512,512]{1,0:T(8,128)(2,1)S(1)} collective-permute-done((bf16[512,512]{1,0:T(8,128)(2,1)}, bf16[512,512]{1,0:T(8,128)(2,1)S(1)}, u32[]{:S(2)}, u32[]{:S(2)}) %collective-permute-start) | collective-permute-done | bytes 524320 | tf_op jit(solution)/shard_map/ppermute | solution.py:400
  45.0 9.8 %collective-permute-done.2.refs_2_ = bf16[512,512]{1,0:T(8,128)(2,1)S(1)} collective-permute-done((bf16[512,512]{1,0:T(8,128)(2,1)S(1)}, bf16[512,512]{1,0:T(8,128)(2,1)S(1)}, u32[]{:S(2)}, u32[]{:S(2)}) %collective-permute-start.2) | collective-permute-done | bytes 524320 | tf_op jit(solution)/shard_map/ppermute | solution.py:400
  54.8 1.3 %collective-permute-start.5 = (bf16[512,512]{1,0:T(8,128)(2,1)S(1)}, bf16[512,512]{1,0:T(8,128)(2,1)}, u32[]{:S(2)}, u32[]{:S(2)}) collective-permute-start(bf16[512,512]{1,0:T(8,128)(2,1)S(1)} %collective-permute-done.2.refs_2_), channel_id=1, source_target_pairs={{8,12},{9,13},{10,14},{11,15},{24,28},{25,29},{26,30},{27,31}} | collective-permute-start | bytes 1572872 | tf_op jit(solution)/shard_map/ppermute | solution.py:400
  56.1 0.0 collective-permute-done.4.refs_4_
  56.1 0.0 copy-start.3
  56.1 1.9 %collective-permute-start.8 = (bf16[512,512]{1,0:T(8,128)(2,1)S(1)}, bf16[512,512]{1,0:T(8,128)(2,1)S(1)}, u32[]{:S(2)}, u32[]{:S(2)}) collective-permute-start(bf16[512,512]{1,0:T(8,128)(2,1)S(1)} %collective-permute-done.refs_1_), channel_id=1, source_target_pairs={{4,6},{5,7},{6,4},{7,5},{8,10},{9,11},{10,8},{11,9},{12,14},{13,15... | collective-permute-start | bytes 1572872 | tf_op jit(solution)/shard_map/ppermute | solution.py:400
  58.0 1.3 %collective-permute-start.3 = (bf16[512,512]{1,0:T(8,128)(2,1)S(1)}, bf16[512,512]{1,0:T(8,128)(2,1)}, u32[]{:S(2)}, u32[]{:S(2)}) collective-permute-start(bf16[512,512]{1,0:T(8,128)(2,1)S(1)} %collective-permute-done.refs_1_), channel_id=1, source_target_pairs={{4,8},{5,9},{6,10},{7,11},{8,12},{9,13},{10,14},{11,15},{20,24},{2... | collective-permute-start | bytes 1572872 | tf_op jit(solution)/shard_map/ppermute | solution.py:400
  59.3 0.0 collective-permute-done.10.refs_5_
  59.3 0.0 copy-start.5
  59.3 3.9 %collective-permute-start.11 = (bf16[512,512]{1,0:T(8,128)(2,1)S(1)}, bf16[512,512]{1,0:T(8,128)(2,1)S(1)}, u32[]{:S(2)}, u32[]{:S(2)}) collective-permute-start(bf16[512,512]{1,0:T(8,128)(2,1)S(1)} %collective-permute-done.2.refs_2_), channel_id=1, source_target_pairs={{8,10},{9,11},{10,8},{11,9},{12,14},{13,15},{14,12},{15,13},{24,26... | collective-permute-start | bytes 1572872 | tf_op jit(solution)/shard_map/ppermute | solution.py:400
  63.3 8.4 %collective-permute-done.5.refs_3_ = bf16[512,512]{1,0:T(8,128)(2,1)} collective-permute-done((bf16[512,512]{1,0:T(8,128)(2,1)S(1)}, bf16[512,512]{1,0:T(8,128)(2,1)}, u32[]{:S(2)}, u32[]{:S(2)}) %collective-permute-start.5) | collective-permute-done | bytes 524320 | tf_op jit(solution)/shard_map/ppermute | solution.py:400
  71.6 1.3 %collective-permute-start.6 = (bf16[512,512]{1,0:T(8,128)(2,1)S(1)}, bf16[512,512]{1,0:T(8,128)(2,1)S(1)}, u32[]{:S(2)}, u32[]{:S(2)}) collective-permute-start(bf16[512,512]{1,0:T(8,128)(2,1)S(1)} %collective-permute-done.4.refs_4_), channel_id=1, source_target_pairs={{0,12},{1,13},{2,14},{3,15},{16,28},{17,29},{18,30},{19,31}} | collective-permute-start | bytes 1572872 | tf_op jit(solution)/shard_map/ppermute | solution.py:400
  72.9 0.0 collective-permute-done.8.refs_5_
  72.9 0.0 copy-start.6
  72.9 1.9 %collective-permute-start.13 = (bf16[512,512]{1,0:T(8,128)(2,1)}, bf16[512,512]{1,0:T(8,128)(2,1)}, u32[]{:S(2)}, u32[]{:S(2)}) collective-permute-start(bf16[512,512]{1,0:T(8,128)(2,1)} %collective-permute-done.5.refs_3_), channel_id=1, source_target_pairs={{12,14},{13,15},{14,12},{15,13},{28,30},{29,31},{30,28},{31,29}} | collective-permute-start | bytes 1572872 | tf_op jit(solution)/shard_map/ppermute | solution.py:400
  74.9 16.8 %collective-permute-done.3.refs_2_ = bf16[512,512]{1,0:T(8,128)(2,1)} collective-permute-done((bf16[512,512]{1,0:T(8,128)(2,1)S(1)}, bf16[512,512]{1,0:T(8,128)(2,1)}, u32[]{:S(2)}, u32[]{:S(2)}) %collective-permute-start.3) | collective-permute-done | bytes 524320 | tf_op jit(solution)/shard_map/ppermute | solution.py:400
  91.7 0.0 collective-permute-done.11.refs_6_
  91.7 1.9 %collective-permute-start.12 = (bf16[512,512]{1,0:T(8,128)(2,1)}, bf16[512,512]{1,0:T(8,128)(2,1)}, u32[]{:S(2)}, u32[]{:S(2)}) collective-permute-start(bf16[512,512]{1,0:T(8,128)(2,1)} %collective-permute-done.3.refs_2_), channel_id=1, source_target_pairs={{8,10},{9,11},{10,8},{11,9},{12,14},{13,15},{14,12},{15,13},{24,26... | collective-permute-start | bytes 1572872 | tf_op jit(solution)/shard_map/ppermute | solution.py:400
  93.6 0.0 collective-permute-done.6.refs_7_
  93.6 0.0 copy-done.6
  93.6 0.0 copy-start.7
  93.7 1.3 %collective-permute-start.7 = (bf16[512,512]{1,0:T(8,128)(2,1)}, bf16[512,512]{1,0:T(8,128)(2,1)}, u32[]{:S(2)}, u32[]{:S(2)}) collective-permute-start(bf16[512,512]{1,0:T(8,128)(2,1)} %collective-permute-done.3.refs_2_), channel_id=1, source_target_pairs={{8,12},{9,13},{10,14},{11,15},{24,28},{25,29},{26,30},{27,31}} | collective-permute-start | bytes 1572872 | tf_op jit(solution)/shard_map/ppermute | solution.py:400
  95.0 0.0 copy-done.8
  95.0 0.0 copy-done.7
  95.0 0.0 copy-done.9
  95.0 0.6 fusion.1.slot_ref
  95.6 0.0 collective-permute-done.13.refs_7_
  95.6 0.0 copy-done.1
  95.6 0.0 copy-done.2
  95.6 0.0 copy-done.4
  95.6 0.0 copy-done.5
  95.7 9.9 %attention.2.refs_8_ = bf16[512,4096]{1,0:T(8,128)(2,1)} custom-call(s32[8,7]{1,0:T(8,128)} %fusion.1.slot_ref, s32[8,7]{1,0:T(8,128)} %cut_ref.3, s32[1]{0:T(128)} %bitcast.odd_ref, bf16[512,4096]{1,0:T(8,128)(2,1)} %q_hbm.3, bf16[512,512]{1,0:T(8,128)(2,1)} %get-tuple-element.18.refs_0_, bf16[512,512]{1,0:T(8,128)(2,1)} %copy-done.1, ...), custom_call_target="tpu_custom_call" | custom-call | flops 2147483648 | bytes 8388608 | tf_op jit(solution)/shard_map/attention/pallas_call | solution.py:339
  105.5 0.0 collective-permute-done.12.refs_6_
  105.5 1.9 %collective-permute-done.7.refs_3_ = bf16[512,512]{1,0:T(8,128)(2,1)} collective-permute-done((bf16[512,512]{1,0:T(8,128)(2,1)}, bf16[512,512]{1,0:T(8,128)(2,1)}, u32[]{:S(2)}, u32[]{:S(2)}) %collective-permute-start.7) | collective-permute-done | bytes 524320 | tf_op jit(solution)/shard_map/ppermute | solution.py:400
  107.4 0.0 copy-done
  107.4 9.7 %attention.3 = bf16[512,4096]{1,0:T(8,128)(2,1)} custom-call(s32[8,7]{1,0:T(8,128)} %fusion.1.slot_ref, s32[8,7]{1,0:T(8,128)} %cut_ref.3, s32[1]{0:T(128)} %bitcast.odd_ref, bf16[512,4096]{1,0:T(8,128)(2,1)} %q_hbm.3, bf16[512,512]{1,0:T(8,128)(2,1)} %project.1.refs_0_, bf16[512,512]{1,0:T(8,128)(2,1)} %copy-done, ...), custom_call_target="tpu_custom_call", output_to_operand_aliasing={{}: (12, {})} | custom-call | flops 2147483648 | bytes 8388608 | tf_op jit(solution)/shard_map/attention/pallas_call | solution.py:339
  (5 shorter events, 0.0 us)
Async XLA Ops:
  13.3 15.8 %collective-permute-start.1 = (bf16[512,512]{1,0:T(8,128)(2,1)}, bf16[512,512]{1,0:T(8,128)(2,1)S(1)}, u32[]{:S(2)}, u32[]{:S(2)}) collective-permute-start(bf16[512,512]{1,0:T(8,128)(2,1)} %get-tuple-element.18.refs_0_), channel_id=1, source_target_pairs={{0,4},{1,5},{2,6},{3,7},{4,8},{5,9},{6,10},{7,11},{8,12},{9,13},{1... | collective-permute-start | bytes 1572872 | tf_op jit(solution)/shard_map/ppermute | solution.py:400
  14.6 19.2 %collective-permute-start.9 = (bf16[512,512]{1,0:T(8,128)(2,1)}, bf16[512,512]{1,0:T(8,128)(2,1)S(1)}, u32[]{:S(2)}, u32[]{:S(2)}) collective-permute-start(bf16[512,512]{1,0:T(8,128)(2,1)} %get-tuple-element.18.refs_0_), channel_id=1, source_target_pairs={{0,2},{1,3},{4,6},{5,7},{8,10},{9,11},{12,14},{13,15},{16,18},{17,... | collective-permute-start | bytes 1572872 | tf_op jit(solution)/shard_map/ppermute | solution.py:400
  18.1 76.9 %copy-start.9 = (s32[8,7]{1,0:T(8,128)S(1)}, s32[8,7]{1,0:T(8,128)}, u32[]{:S(2)}) copy-start(s32[8,7]{1,0:T(8,128)} %param.12) | copy-start | bytes 676
  27.4 17.6 %collective-permute-start = (bf16[512,512]{1,0:T(8,128)(2,1)}, bf16[512,512]{1,0:T(8,128)(2,1)S(1)}, u32[]{:S(2)}, u32[]{:S(2)}) collective-permute-start(bf16[512,512]{1,0:T(8,128)(2,1)} %project.1.refs_0_), channel_id=1, source_target_pairs={{0,4},{1,5},{2,6},{3,7},{4,8},{5,9},{6,10},{7,11},{8,12},{9,13},{1... | collective-permute-start | bytes 1572872 | tf_op jit(solution)/shard_map/ppermute | solution.py:400
  29.1 66.6 %copy-start.1 = (bf16[512,512]{1,0:T(8,128)(2,1)}, bf16[512,512]{1,0:T(8,128)(2,1)S(1)}, u32[]{:S(2)}) copy-start(bf16[512,512]{1,0:T(8,128)(2,1)S(1)} %collective-permute-done.1.refs_1_) | copy-start | bytes 1572868
  29.1 25.7 %collective-permute-start.2 = (bf16[512,512]{1,0:T(8,128)(2,1)S(1)}, bf16[512,512]{1,0:T(8,128)(2,1)S(1)}, u32[]{:S(2)}, u32[]{:S(2)}) collective-permute-start(bf16[512,512]{1,0:T(8,128)(2,1)S(1)} %collective-permute-done.1.refs_1_), channel_id=1, source_target_pairs={{4,8},{5,9},{6,10},{7,11},{8,12},{9,13},{10,14},{11,15},{20,24},{2... | collective-permute-start | bytes 1572872 | tf_op jit(solution)/shard_map/ppermute | solution.py:400
  30.4 25.7 %collective-permute-start.4 = (bf16[512,512]{1,0:T(8,128)(2,1)}, bf16[512,512]{1,0:T(8,128)(2,1)S(1)}, u32[]{:S(2)}, u32[]{:S(2)}) collective-permute-start(bf16[512,512]{1,0:T(8,128)(2,1)} %project.1.refs_0_), channel_id=1, source_target_pairs={{0,2},{1,3},{2,0},{3,1},{4,6},{5,7},{8,10},{9,11},{12,14},{13,15},... | collective-permute-start | bytes 1572872 | tf_op jit(solution)/shard_map/ppermute | solution.py:400
  33.8 61.8 %copy-start.2 = (bf16[512,512]{1,0:T(8,128)(2,1)}, bf16[512,512]{1,0:T(8,128)(2,1)S(1)}, u32[]{:S(2)}) copy-start(bf16[512,512]{1,0:T(8,128)(2,1)S(1)} %collective-permute-done.9.refs_4_) | copy-start | bytes 1572868
  33.8 25.5 %collective-permute-start.10 = (bf16[512,512]{1,0:T(8,128)(2,1)S(1)}, bf16[512,512]{1,0:T(8,128)(2,1)S(1)}, u32[]{:S(2)}, u32[]{:S(2)}) collective-permute-start(bf16[512,512]{1,0:T(8,128)(2,1)S(1)} %collective-permute-done.1.refs_1_), channel_id=1, source_target_pairs={{4,6},{5,7},{6,4},{7,5},{8,10},{9,11},{10,8},{11,9},{12,14},{13,15... | collective-permute-start | bytes 1572872 | tf_op jit(solution)/shard_map/ppermute | solution.py:400
  45.0 62.4 %copy-start = (bf16[512,512]{1,0:T(8,128)(2,1)}, bf16[512,512]{1,0:T(8,128)(2,1)S(1)}, u32[]{:S(2)}) copy-start(bf16[512,512]{1,0:T(8,128)(2,1)S(1)} %collective-permute-done.refs_1_) | copy-start | bytes 1572868
  54.8 40.9 %copy-start.4 = (bf16[512,512]{1,0:T(8,128)(2,1)}, bf16[512,512]{1,0:T(8,128)(2,1)S(1)}, u32[]{:S(2)}) copy-start(bf16[512,512]{1,0:T(8,128)(2,1)S(1)} %collective-permute-done.2.refs_2_) | copy-start | bytes 1572868
  54.8 16.8 %collective-permute-start.5 = (bf16[512,512]{1,0:T(8,128)(2,1)S(1)}, bf16[512,512]{1,0:T(8,128)(2,1)}, u32[]{:S(2)}, u32[]{:S(2)}) collective-permute-start(bf16[512,512]{1,0:T(8,128)(2,1)S(1)} %collective-permute-done.2.refs_2_), channel_id=1, source_target_pairs={{8,12},{9,13},{10,14},{11,15},{24,28},{25,29},{26,30},{27,31}} | collective-permute-start | bytes 1572872 | tf_op jit(solution)/shard_map/ppermute | solution.py:400
  56.1 51.3 %copy-start.3 = (bf16[512,512]{1,0:T(8,128)(2,1)}, bf16[512,512]{1,0:T(8,128)(2,1)S(1)}, u32[]{:S(2)}) copy-start(bf16[512,512]{1,0:T(8,128)(2,1)S(1)} %collective-permute-done.4.refs_4_) | copy-start | bytes 1572868
  56.1 16.8 %collective-permute-start.8 = (bf16[512,512]{1,0:T(8,128)(2,1)S(1)}, bf16[512,512]{1,0:T(8,128)(2,1)S(1)}, u32[]{:S(2)}, u32[]{:S(2)}) collective-permute-start(bf16[512,512]{1,0:T(8,128)(2,1)S(1)} %collective-permute-done.refs_1_), channel_id=1, source_target_pairs={{4,6},{5,7},{6,4},{7,5},{8,10},{9,11},{10,8},{11,9},{12,14},{13,15... | collective-permute-start | bytes 1572872 | tf_op jit(solution)/shard_map/ppermute | solution.py:400
  58.0 33.7 %collective-permute-start.3 = (bf16[512,512]{1,0:T(8,128)(2,1)S(1)}, bf16[512,512]{1,0:T(8,128)(2,1)}, u32[]{:S(2)}, u32[]{:S(2)}) collective-permute-start(bf16[512,512]{1,0:T(8,128)(2,1)S(1)} %collective-permute-done.refs_1_), channel_id=1, source_target_pairs={{4,8},{5,9},{6,10},{7,11},{8,12},{9,13},{10,14},{11,15},{20,24},{2... | collective-permute-start | bytes 1572872 | tf_op jit(solution)/shard_map/ppermute | solution.py:400
  59.3 36.3 %copy-start.5 = (bf16[512,512]{1,0:T(8,128)(2,1)}, bf16[512,512]{1,0:T(8,128)(2,1)S(1)}, u32[]{:S(2)}) copy-start(bf16[512,512]{1,0:T(8,128)(2,1)S(1)} %collective-permute-done.10.refs_5_) | copy-start | bytes 1572868
  59.3 32.4 %collective-permute-start.11 = (bf16[512,512]{1,0:T(8,128)(2,1)S(1)}, bf16[512,512]{1,0:T(8,128)(2,1)S(1)}, u32[]{:S(2)}, u32[]{:S(2)}) collective-permute-start(bf16[512,512]{1,0:T(8,128)(2,1)S(1)} %collective-permute-done.2.refs_2_), channel_id=1, source_target_pairs={{8,10},{9,11},{10,8},{11,9},{12,14},{13,15},{14,12},{15,13},{24,26... | collective-permute-start | bytes 1572872 | tf_op jit(solution)/shard_map/ppermute | solution.py:400
  71.6 22.0 %collective-permute-start.6 = (bf16[512,512]{1,0:T(8,128)(2,1)S(1)}, bf16[512,512]{1,0:T(8,128)(2,1)S(1)}, u32[]{:S(2)}, u32[]{:S(2)}) collective-permute-start(bf16[512,512]{1,0:T(8,128)(2,1)S(1)} %collective-permute-done.4.refs_4_), channel_id=1, source_target_pairs={{0,12},{1,13},{2,14},{3,15},{16,28},{17,29},{18,30},{19,31}} | collective-permute-start | bytes 1572872 | tf_op jit(solution)/shard_map/ppermute | solution.py:400
  72.9 20.7 %copy-start.6 = (bf16[512,512]{1,0:T(8,128)(2,1)}, bf16[512,512]{1,0:T(8,128)(2,1)S(1)}, u32[]{:S(2)}) copy-start(bf16[512,512]{1,0:T(8,128)(2,1)S(1)} %collective-permute-done.8.refs_5_) | copy-start | bytes 1572868
  72.9 22.7 %collective-permute-start.13 = (bf16[512,512]{1,0:T(8,128)(2,1)}, bf16[512,512]{1,0:T(8,128)(2,1)}, u32[]{:S(2)}, u32[]{:S(2)}) collective-permute-start(bf16[512,512]{1,0:T(8,128)(2,1)} %collective-permute-done.5.refs_3_), channel_id=1, source_target_pairs={{12,14},{13,15},{14,12},{15,13},{28,30},{29,31},{30,28},{31,29}} | collective-permute-start | bytes 1572872 | tf_op jit(solution)/shard_map/ppermute | solution.py:400
  91.7 3.3 %copy-start.8 = (bf16[512,512]{1,0:T(8,128)(2,1)}, bf16[512,512]{1,0:T(8,128)(2,1)S(1)}, u32[]{:S(2)}) copy-start(bf16[512,512]{1,0:T(8,128)(2,1)S(1)} %collective-permute-done.11.refs_6_) | copy-start | bytes 1572868
  91.7 13.8 %collective-permute-start.12 = (bf16[512,512]{1,0:T(8,128)(2,1)}, bf16[512,512]{1,0:T(8,128)(2,1)}, u32[]{:S(2)}, u32[]{:S(2)}) collective-permute-start(bf16[512,512]{1,0:T(8,128)(2,1)} %collective-permute-done.3.refs_2_), channel_id=1, source_target_pairs={{8,10},{9,11},{10,8},{11,9},{12,14},{13,15},{14,12},{15,13},{24,26... | collective-permute-start | bytes 1572872 | tf_op jit(solution)/shard_map/ppermute | solution.py:400
  93.6 1.3 %copy-start.7 = (bf16[512,512]{1,0:T(8,128)(2,1)}, bf16[512,512]{1,0:T(8,128)(2,1)S(1)}, u32[]{:S(2)}) copy-start(bf16[512,512]{1,0:T(8,128)(2,1)S(1)} %collective-permute-done.6.refs_7_) | copy-start | bytes 1572868
  93.7 13.8 %collective-permute-start.7 = (bf16[512,512]{1,0:T(8,128)(2,1)}, bf16[512,512]{1,0:T(8,128)(2,1)}, u32[]{:S(2)}, u32[]{:S(2)}) collective-permute-start(bf16[512,512]{1,0:T(8,128)(2,1)} %collective-permute-done.3.refs_2_), channel_id=1, source_target_pairs={{8,12},{9,13},{10,14},{11,15},{24,28},{25,29},{26,30},{27,31}} | collective-permute-start | bytes 1572872 | tf_op jit(solution)/shard_map/ppermute | solution.py:400

commit v18 on v17

--- a/solution.py
+++ b/solution.py
@@ -29,9 +29,9 @@
     ("across", 2, 0, (("across", 1, 0),)),
     ("along", 2, 1, (("along", 2, 0),)),
     ("across", 3, 0, (("across", 1, 1),)),
-    ("across", 2, 1, (("across", 2, 0),)),
+    ("across", 2, 1, (("across", 2, 0), ("across", 1, 1))),
     ("down", 3, 1, (("along", 3, 0),)),
-    ("along", 3, 1, (("along", 2, 1), ("down", 3, 1))),
+    ("along", 3, 1, (("along", 2, 1),)),
 )
 
 
@@ -122,12 +122,12 @@
 
 
 def write_heads(kv_ref, acc_scr):
-    width = kv_ref.shape[1] // 2
-    for head in range(width // HEAD_DIM):
+    heads = kv_ref.shape[0]
+    for head in range(heads):
         for part in range(2):
-            source = slice(part * width + head * HEAD_DIM, part * width + (head + 1) * HEAD_DIM)
-            target = slice((2 * head + part) * HEAD_DIM, (2 * head + part + 1) * HEAD_DIM)
-            kv_ref[:, target] = acc_scr[:, source].astype(jnp.bfloat16)
+            first = (part * heads + head) * HEAD_DIM
+            source = acc_scr[:, first : first + HEAD_DIM]
+            kv_ref[head, :, part * HEAD_DIM : (part + 1) * HEAD_DIM] = source.astype(jnp.bfloat16)
 
 
 def norm_project(hidden, gain, key_weight, value_weight):
@@ -142,7 +142,7 @@
         out_specs=[whole, whole],
         out_shape=[
             jax.ShapeDtypeStruct((rows, 128), jnp.float32),
-            jax.ShapeDtypeStruct((rows, 2 * width), jnp.bfloat16),
+            jax.ShapeDtypeStruct((width // HEAD_DIM, rows, 2 * HEAD_DIM), jnp.bfloat16),
         ],
         scratch_shapes=[
             pltpu.VMEM((LOADS, rows, chunk), jnp.bfloat16),
@@ -199,8 +199,8 @@
             weight,
             weight,
         ],
-        out_specs=pl.BlockSpec((rows, 2 * width), lambda i: (0, 0)),
-        out_shape=jax.ShapeDtypeStruct((rows, 2 * width), jnp.bfloat16),
+        out_specs=pl.BlockSpec((width // HEAD_DIM, rows, 2 * HEAD_DIM), lambda i: (0, 0, 0)),
+        out_shape=jax.ShapeDtypeStruct((width // HEAD_DIM, rows, 2 * HEAD_DIM), jnp.bfloat16),
         scratch_shapes=[pltpu.VMEM((rows, 2 * width), jnp.float32)],
         compiler_params=pltpu.CompilerParams(vmem_limit_bytes=57 * MIB),
         cost_estimate=pl.CostEstimate(
@@ -223,7 +223,7 @@
     def load_kv(head):
         def copy(ref, level, number):
             return pltpu.make_async_copy(
-                ref.at[:, head * width : (head + 1) * width],
+                ref.at[head],
                 kv_scr.at[head, level],
                 kv_sem.at[head, number],
             )
@@ -326,7 +326,7 @@
     blocks, depth = slots.shape
     block = rows // blocks
     near = len(straight)
-    kv_heads = own.shape[1] // (2 * HEAD_DIM)
+    kv_heads = own.shape[0]
     wide = features // UNITS // kv_heads
     steps = kv_heads * blocks // BLOCKS_PER_STEP
     held = pl.BlockSpec(memory_space=pltpu.HBM)

time: 119 us -> 117 us (0.983); the launches traced: 117 us -> 117 us
  starting transfers between devices: 27.5 us -> 24.3 us
  waiting for transfers between devices: 46.4 us -> 49.2 us
    ppermute x14, starting transfers between devices: 27.5 us -> 24.3 us  [step(): moved[key, s, unit] = lax.ppermute(array, 'node', pairs)]
    ppermute x14, waiting for transfers between devices: 46.4 us -> 49.2 us  [step(): moved[key, s, unit] = lax.ppermute(array, 'node', pairs)]
  transfers between devices with their start and end apart: 14 -> 14, of which waited for: 6 -> 7; matrix products, arithmetic and copies ran while one was open for 1% -> 1% of each run, Pallas kernels for 16% -> 16%
where the time goes in v18:
time: 117 us
  waiting for transfers between devices  49.2 us (42%)
  Pallas kernels  42.1 us (36%)
  starting transfers between devices  24.3 us (21%)
    ppermute x14, waiting for transfers between devices, step(): moved[key, s, unit] = lax.ppermute(array, 'node', pairs)  49.2 us
    ppermute x14, starting transfers between devices, step(): moved[key, s, unit] = lax.ppermute(array, 'node', pairs)  24.3 us
    pallas_call x2, Pallas kernels, attention(): pl.pallas_call(functools.partial(attention_kernel, block, unit, near), in...  19.4 us
    pallas_call x1, Pallas kernels, norm_project(): pl.pallas_call(norm_project_kernel, in_specs=[held, whole, held, held], o...  13.3 us
    pallas_call x1, Pallas kernels, project(): pl.pallas_call(project_kernel, grid=(CHUNKS,), in_specs=[pl.BlockSpec((ro...  9.35 us
  transfers between devices with their start and end apart: 14, of which 7 were waited for; matrix products, arithmetic and copies ran while one was open for 1% of the time, Pallas kernels for 16%

profile of v18, /device:TPU:24, one launch (start us, length us, event | category | flops | bytes accessed | tf_op | source)
XLA Modules:
  0.0 116.5 jit_solution(29791125374318274)
XLA Ops:
  0.0 13.3 %norm_project.1 = (f32[512,128]{1,0:T(8,128)}, bf16[2,512,256]{2,1,0:T(8,128)(2,1)}) custom-call(bf16[512,8192]{1,0:T(8,128)(2,1)} %x_ref.1, f32[8,1,1024]{2,1,0:T(1,128)} %bitcast.3, bf16[8192,512]{1,0:T(8,128)(2,1)} %key_ref.1, bf16[8192,512]{1,0:T(8,128)(2,1)} %value_ref.1), custom_call_target="tpu_custom_call" | custom-call | flops 4294967296 | bytes 16777216 | tf_op jit(solution)/shard_map/norm_project/pallas_call | solution.py:139
  13.3 1.3 %collective-permute-start.1 = (bf16[2,512,256]{2,1,0:T(8,128)(2,1)}, bf16[2,512,256]{2,1,0:T(8,128)(2,1)S(1)}, u32[]{:S(2)}, u32[]{:S(2)}) collective-permute-start(bf16[2,512,256]{2,1,0:T(8,128)(2,1)} %get-tuple-element.18.refs_0_), channel_id=1, source_target_pairs={{0,4},{1,5},{2,6},{3,7},{4,8},{5,9},{6,10},{7,11},{8,12},{9,13},{1... | collective-permute-start | bytes 1572872 | tf_op jit(solution)/shard_map/ppermute | solution.py:400
  14.6 3.5 %collective-permute-start.7 = (bf16[2,512,256]{2,1,0:T(8,128)(2,1)}, bf16[2,512,256]{2,1,0:T(8,128)(2,1)S(1)}, u32[]{:S(2)}, u32[]{:S(2)}) collective-permute-start(bf16[2,512,256]{2,1,0:T(8,128)(2,1)} %get-tuple-element.18.refs_0_), channel_id=1, source_target_pairs={{0,2},{1,3},{4,6},{5,7},{8,10},{9,11},{12,14},{13,15},{16,18},{17,... | collective-permute-start | bytes 1572872 | tf_op jit(solution)/shard_map/ppermute | solution.py:400
  18.1 0.0 copy-start.8
  18.1 9.3 %project.1.refs_0_ = bf16[2,512,256]{2,1,0:T(8,128)(2,1)} custom-call(bf16[512,8192]{1,0:T(8,128)(2,1)} %x_ref.1, f32[512,128]{1,0:T(8,128)} %get-tuple-element.17.scale_ref, f32[1,8192]{1,0:T(1,128)} %bitcast.4, bf16[8192,512]{1,0:T(8,128)(2,1)} %key_ref.1, bf16[8192,512]{1,0:T(8,128)(2,1)} %value_ref.1), custom_call_target="tpu_custom_call" | custom-call | flops 4294967296 | bytes 16777216 | tf_op jit(solution)/shard_map/project/pallas_call | solution.py:192
  27.4 1.3 %collective-permute-start.5 = (bf16[2,512,256]{2,1,0:T(8,128)(2,1)}, bf16[2,512,256]{2,1,0:T(8,128)(2,1)S(1)}, u32[]{:S(2)}, u32[]{:S(2)}) collective-permute-start(bf16[2,512,256]{2,1,0:T(8,128)(2,1)} %project.1.refs_0_), channel_id=1, source_target_pairs={{0,2},{1,3},{2,0},{3,1},{4,6},{5,7},{8,10},{9,11},{12,14},{13,15},... | collective-permute-start | bytes 1572872 | tf_op jit(solution)/shard_map/ppermute | solution.py:400
  28.7 1.3 %collective-permute-start = (bf16[2,512,256]{2,1,0:T(8,128)(2,1)}, bf16[2,512,256]{2,1,0:T(8,128)(2,1)S(1)}, u32[]{:S(2)}, u32[]{:S(2)}) collective-permute-start(bf16[2,512,256]{2,1,0:T(8,128)(2,1)} %project.1.refs_0_), channel_id=1, source_target_pairs={{0,4},{1,5},{2,6},{3,7},{4,8},{5,9},{6,10},{7,11},{8,12},{9,13},{1... | collective-permute-start | bytes 1572872 | tf_op jit(solution)/shard_map/ppermute | solution.py:400
  30.0 0.0 collective-permute-done.1.refs_1_
  30.1 0.0 copy-start.2
  30.1 1.3 %collective-permute-start.2 = (bf16[2,512,256]{2,1,0:T(8,128)(2,1)S(1)}, bf16[2,512,256]{2,1,0:T(8,128)(2,1)S(1)}, u32[]{:S(2)}, u32[]{:S(2)}) collective-permute-start(bf16[2,512,256]{2,1,0:T(8,128)(2,1)S(1)} %collective-permute-done.1.refs_1_), channel_id=1, source_target_pairs={{4,8},{5,9},{6,10},{7,11},{8,12},{9,13},{10,14},{11,15},{20,24},{2... | collective-permute-start | bytes 1572872 | tf_op jit(solution)/shard_map/ppermute | solution.py:400
  31.4 0.0 collective-permute-done.7.refs_4_
  31.4 0.0 copy-start.3
  31.4 2.9 %collective-permute-start.8 = (bf16[2,512,256]{2,1,0:T(8,128)(2,1)S(1)}, bf16[2,512,256]{2,1,0:T(8,128)(2,1)S(1)}, u32[]{:S(2)}, u32[]{:S(2)}) collective-permute-start(bf16[2,512,256]{2,1,0:T(8,128)(2,1)S(1)} %collective-permute-done.1.refs_1_), channel_id=1, source_target_pairs={{4,6},{5,7},{6,4},{7,5},{8,10},{9,11},{10,8},{11,9},{12,14},{13,15... | collective-permute-start | bytes 1572872 | tf_op jit(solution)/shard_map/ppermute | solution.py:400
  34.3 7.1 %collective-permute-done.5.refs_4_ = bf16[2,512,256]{2,1,0:T(8,128)(2,1)S(1)} collective-permute-done((bf16[2,512,256]{2,1,0:T(8,128)(2,1)}, bf16[2,512,256]{2,1,0:T(8,128)(2,1)S(1)}, u32[]{:S(2)}, u32[]{:S(2)}) %collective-permute-start.5) | collective-permute-done | bytes 524320 | tf_op jit(solution)/shard_map/ppermute | solution.py:400
  41.3 0.0 copy-start
  41.3 5.0 %collective-permute-done.refs_1_ = bf16[2,512,256]{2,1,0:T(8,128)(2,1)S(1)} collective-permute-done((bf16[2,512,256]{2,1,0:T(8,128)(2,1)}, bf16[2,512,256]{2,1,0:T(8,128)(2,1)S(1)}, u32[]{:S(2)}, u32[]{:S(2)}) %collective-permute-start) | collective-permute-done | bytes 524320 | tf_op jit(solution)/shard_map/ppermute | solution.py:400
  46.3 1.9 %collective-permute-start.6 = (bf16[2,512,256]{2,1,0:T(8,128)(2,1)S(1)}, bf16[2,512,256]{2,1,0:T(8,128)(2,1)S(1)}, u32[]{:S(2)}, u32[]{:S(2)}) collective-permute-start(bf16[2,512,256]{2,1,0:T(8,128)(2,1)S(1)} %collective-permute-done.refs_1_), channel_id=1, source_target_pairs={{4,6},{5,7},{6,4},{7,5},{8,10},{9,11},{10,8},{11,9},{12,14},{13,15... | collective-permute-start | bytes 1572872 | tf_op jit(solution)/shard_map/ppermute | solution.py:400
  48.2 7.8 %collective-permute-done.2.refs_2_ = bf16[2,512,256]{2,1,0:T(8,128)(2,1)S(1)} collective-permute-done((bf16[2,512,256]{2,1,0:T(8,128)(2,1)S(1)}, bf16[2,512,256]{2,1,0:T(8,128)(2,1)S(1)}, u32[]{:S(2)}, u32[]{:S(2)}) %collective-permute-start.2) | collective-permute-done | bytes 524320 | tf_op jit(solution)/shard_map/ppermute | solution.py:400
  56.1 1.3 %collective-permute-start.11 = (bf16[2,512,256]{2,1,0:T(8,128)(2,1)S(1)}, bf16[2,512,256]{2,1,0:T(8,128)(2,1)}, u32[]{:S(2)}, u32[]{:S(2)}) collective-permute-start(bf16[2,512,256]{2,1,0:T(8,128)(2,1)S(1)} %collective-permute-done.2.refs_2_), channel_id=1, source_target_pairs={{8,12},{9,13},{10,14},{11,15},{24,28},{25,29},{26,30},{27,31}} | collective-permute-start | bytes 1572872 | tf_op jit(solution)/shard_map/ppermute | solution.py:400
  57.4 1.3 %collective-permute-start.3 = (bf16[2,512,256]{2,1,0:T(8,128)(2,1)S(1)}, bf16[2,512,256]{2,1,0:T(8,128)(2,1)}, u32[]{:S(2)}, u32[]{:S(2)}) collective-permute-start(bf16[2,512,256]{2,1,0:T(8,128)(2,1)S(1)} %collective-permute-done.refs_1_), channel_id=1, source_target_pairs={{4,8},{5,9},{6,10},{7,11},{8,12},{9,13},{10,14},{11,15},{20,24},{2... | collective-permute-start | bytes 1572872 | tf_op jit(solution)/shard_map/ppermute | solution.py:400
  58.7 0.0 collective-permute-done.8.refs_5_
  58.7 0.0 copy-start.6
  58.7 1.9 %collective-permute-start.9 = (bf16[2,512,256]{2,1,0:T(8,128)(2,1)S(1)}, bf16[2,512,256]{2,1,0:T(8,128)(2,1)S(1)}, u32[]{:S(2)}, u32[]{:S(2)}) collective-permute-start(bf16[2,512,256]{2,1,0:T(8,128)(2,1)S(1)} %collective-permute-done.2.refs_2_), channel_id=1, source_target_pairs={{8,10},{9,11},{10,8},{11,9},{12,14},{13,15},{14,12},{15,13},{24,26... | collective-permute-start | bytes 1572872 | tf_op jit(solution)/shard_map/ppermute | solution.py:400
  60.6 3.1 %collective-permute-done.6.refs_5_ = bf16[2,512,256]{2,1,0:T(8,128)(2,1)S(1)} collective-permute-done((bf16[2,512,256]{2,1,0:T(8,128)(2,1)S(1)}, bf16[2,512,256]{2,1,0:T(8,128)(2,1)S(1)}, u32[]{:S(2)}, u32[]{:S(2)}) %collective-permute-start.6) | collective-permute-done | bytes 524320 | tf_op jit(solution)/shard_map/ppermute | solution.py:400
  63.7 9.2 %collective-permute-done.11.refs_3_ = bf16[2,512,256]{2,1,0:T(8,128)(2,1)} collective-permute-done((bf16[2,512,256]{2,1,0:T(8,128)(2,1)S(1)}, bf16[2,512,256]{2,1,0:T(8,128)(2,1)}, u32[]{:S(2)}, u32[]{:S(2)}) %collective-permute-start.11) | collective-permute-done | bytes 524320 | tf_op jit(solution)/shard_map/ppermute | solution.py:400
  72.9 1.9 %collective-permute-start.13 = (bf16[2,512,256]{2,1,0:T(8,128)(2,1)}, bf16[2,512,256]{2,1,0:T(8,128)(2,1)}, u32[]{:S(2)}, u32[]{:S(2)}) collective-permute-start(bf16[2,512,256]{2,1,0:T(8,128)(2,1)} %collective-permute-done.11.refs_3_), channel_id=1, source_target_pairs={{12,14},{13,15},{14,12},{15,13},{28,30},{29,31},{30,28},{31,29}} | collective-permute-start | bytes 1572872 | tf_op jit(solution)/shard_map/ppermute | solution.py:400
  74.9 6.9 %collective-permute-done.3.refs_2_ = bf16[2,512,256]{2,1,0:T(8,128)(2,1)} collective-permute-done((bf16[2,512,256]{2,1,0:T(8,128)(2,1)S(1)}, bf16[2,512,256]{2,1,0:T(8,128)(2,1)}, u32[]{:S(2)}, u32[]{:S(2)}) %collective-permute-start.3) | collective-permute-done | bytes 524320 | tf_op jit(solution)/shard_map/ppermute | solution.py:400
  81.8 1.3 %collective-permute-start.4 = (bf16[2,512,256]{2,1,0:T(8,128)(2,1)}, bf16[2,512,256]{2,1,0:T(8,128)(2,1)}, u32[]{:S(2)}, u32[]{:S(2)}) collective-permute-start(bf16[2,512,256]{2,1,0:T(8,128)(2,1)} %collective-permute-done.3.refs_2_), channel_id=1, source_target_pairs={{8,12},{9,13},{10,14},{11,15},{24,28},{25,29},{26,30},{27,31}} | collective-permute-start | bytes 1572872 | tf_op jit(solution)/shard_map/ppermute | solution.py:400
  83.1 1.3 %collective-permute-start.12 = (bf16[2,512,256]{2,1,0:T(8,128)(2,1)S(1)}, bf16[2,512,256]{2,1,0:T(8,128)(2,1)}, u32[]{:S(2)}, u32[]{:S(2)}) collective-permute-start(bf16[2,512,256]{2,1,0:T(8,128)(2,1)S(1)} %collective-permute-done.5.refs_4_), channel_id=1, source_target_pairs={{0,12},{1,13},{2,14},{3,15},{16,28},{17,29},{18,30},{19,31}} | collective-permute-start | bytes 1572872 | tf_op jit(solution)/shard_map/ppermute | solution.py:400
  84.4 0.0 collective-permute-done.9.refs_6_
  84.4 0.0 copy-done.6
  84.4 0.0 copy-start.7
  84.4 1.9 %collective-permute-start.10 = (bf16[2,512,256]{2,1,0:T(8,128)(2,1)}, bf16[2,512,256]{2,1,0:T(8,128)(2,1)}, u32[]{:S(2)}, u32[]{:S(2)}) collective-permute-start(bf16[2,512,256]{2,1,0:T(8,128)(2,1)} %collective-permute-done.3.refs_2_), channel_id=1, source_target_pairs={{8,10},{9,11},{10,8},{11,9},{12,14},{13,15},{14,12},{15,13},{24,26... | collective-permute-start | bytes 1572872 | tf_op jit(solution)/shard_map/ppermute | solution.py:400
  86.3 0.0 copy-done.7
  86.4 0.0 copy-done.8
  86.4 0.6 fusion.1.slot_ref
  87.0 0.0 collective-permute-done.13.refs_7_
  87.0 0.0 copy-done.2
  87.0 0.0 copy-done.3
  87.0 0.0 copy-done.5
  87.0 9.7 %attention.2.refs_8_ = bf16[512,4096]{1,0:T(8,128)(2,1)} custom-call(s32[8,7]{1,0:T(8,128)} %fusion.1.slot_ref, s32[8,7]{1,0:T(8,128)} %cut_ref.3, s32[1]{0:T(128)} %bitcast.odd_ref, bf16[512,4096]{1,0:T(8,128)(2,1)} %q_hbm.3, bf16[2,512,256]{2,1,0:T(8,128)(2,1)} %get-tuple-element.18.refs_0_, bf16[2,512,256]{2,1,0:T(8,128)(2,1)} %copy-done.2, ...), custom_call_target="tpu_custom_call" | custom-call | flops 2147483648 | bytes 8388608 | tf_op jit(solution)/shard_map/attention/pallas_call | solution.py:339
  96.7 10.0 %collective-permute-done.4.refs_3_ = bf16[2,512,256]{2,1,0:T(8,128)(2,1)} collective-permute-done((bf16[2,512,256]{2,1,0:T(8,128)(2,1)}, bf16[2,512,256]{2,1,0:T(8,128)(2,1)}, u32[]{:S(2)}, u32[]{:S(2)}) %collective-permute-start.4) | collective-permute-done | bytes 524320 | tf_op jit(solution)/shard_map/ppermute | solution.py:400
  106.8 0.0 collective-permute-done.12.refs_7_
  106.8 0.0 collective-permute-done.10.refs_6_
  106.8 0.0 copy-done
  106.8 0.0 copy-done.1
  106.8 0.0 copy-done.4
  106.8 9.7 %attention.3 = bf16[512,4096]{1,0:T(8,128)(2,1)} custom-call(s32[8,7]{1,0:T(8,128)} %fusion.1.slot_ref, s32[8,7]{1,0:T(8,128)} %cut_ref.3, s32[1]{0:T(128)} %bitcast.odd_ref, bf16[512,4096]{1,0:T(8,128)(2,1)} %q_hbm.3, bf16[2,512,256]{2,1,0:T(8,128)(2,1)} %project.1.refs_0_, bf16[2,512,256]{2,1,0:T(8,128)(2,1)} %copy-done.1, ...), custom_call_target="tpu_custom_call", output_to_operand_aliasing={{}: (12, {})} | custom-call | flops 2147483648 | bytes 8388608 | tf_op jit(solution)/shard_map/attention/pallas_call | solution.py:339
  (3 shorter events, 0.0 us)
Async XLA Ops:
  13.3 16.7 %collective-permute-start.1 = (bf16[2,512,256]{2,1,0:T(8,128)(2,1)}, bf16[2,512,256]{2,1,0:T(8,128)(2,1)S(1)}, u32[]{:S(2)}, u32[]{:S(2)}) collective-permute-start(bf16[2,512,256]{2,1,0:T(8,128)(2,1)} %get-tuple-element.18.refs_0_), channel_id=1, source_target_pairs={{0,4},{1,5},{2,6},{3,7},{4,8},{5,9},{6,10},{7,11},{8,12},{9,13},{1... | collective-permute-start | bytes 1572872 | tf_op jit(solution)/shard_map/ppermute | solution.py:400
  14.6 16.8 %collective-permute-start.7 = (bf16[2,512,256]{2,1,0:T(8,128)(2,1)}, bf16[2,512,256]{2,1,0:T(8,128)(2,1)S(1)}, u32[]{:S(2)}, u32[]{:S(2)}) collective-permute-start(bf16[2,512,256]{2,1,0:T(8,128)(2,1)} %get-tuple-element.18.refs_0_), channel_id=1, source_target_pairs={{0,2},{1,3},{4,6},{5,7},{8,10},{9,11},{12,14},{13,15},{16,18},{17,... | collective-permute-start | bytes 1572872 | tf_op jit(solution)/shard_map/ppermute | solution.py:400
  18.1 68.3 %copy-start.8 = (s32[8,7]{1,0:T(8,128)S(1)}, s32[8,7]{1,0:T(8,128)}, u32[]{:S(2)}) copy-start(s32[8,7]{1,0:T(8,128)} %param.12) | copy-start | bytes 676
  27.4 13.9 %collective-permute-start.5 = (bf16[2,512,256]{2,1,0:T(8,128)(2,1)}, bf16[2,512,256]{2,1,0:T(8,128)(2,1)S(1)}, u32[]{:S(2)}, u32[]{:S(2)}) collective-permute-start(bf16[2,512,256]{2,1,0:T(8,128)(2,1)} %project.1.refs_0_), channel_id=1, source_target_pairs={{0,2},{1,3},{2,0},{3,1},{4,6},{5,7},{8,10},{9,11},{12,14},{13,15},... | collective-permute-start | bytes 1572872 | tf_op jit(solution)/shard_map/ppermute | solution.py:400
  28.7 17.6 %collective-permute-start = (bf16[2,512,256]{2,1,0:T(8,128)(2,1)}, bf16[2,512,256]{2,1,0:T(8,128)(2,1)S(1)}, u32[]{:S(2)}, u32[]{:S(2)}) collective-permute-start(bf16[2,512,256]{2,1,0:T(8,128)(2,1)} %project.1.refs_0_), channel_id=1, source_target_pairs={{0,4},{1,5},{2,6},{3,7},{4,8},{5,9},{6,10},{7,11},{8,12},{9,13},{1... | collective-permute-start | bytes 1572872 | tf_op jit(solution)/shard_map/ppermute | solution.py:400
  30.1 56.9 %copy-start.2 = (bf16[2,512,256]{2,1,0:T(8,128)(2,1)}, bf16[2,512,256]{2,1,0:T(8,128)(2,1)S(1)}, u32[]{:S(2)}) copy-start(bf16[2,512,256]{2,1,0:T(8,128)(2,1)S(1)} %collective-permute-done.1.refs_1_) | copy-start | bytes 1572868
  30.1 26.0 %collective-permute-start.2 = (bf16[2,512,256]{2,1,0:T(8,128)(2,1)S(1)}, bf16[2,512,256]{2,1,0:T(8,128)(2,1)S(1)}, u32[]{:S(2)}, u32[]{:S(2)}) collective-permute-start(bf16[2,512,256]{2,1,0:T(8,128)(2,1)S(1)} %collective-permute-done.1.refs_1_), channel_id=1, source_target_pairs={{4,8},{5,9},{6,10},{7,11},{8,12},{9,13},{10,14},{11,15},{20,24},{2... | collective-permute-start | bytes 1572872 | tf_op jit(solution)/shard_map/ppermute | solution.py:400
  31.4 55.6 %copy-start.3 = (bf16[2,512,256]{2,1,0:T(8,128)(2,1)}, bf16[2,512,256]{2,1,0:T(8,128)(2,1)S(1)}, u32[]{:S(2)}) copy-start(bf16[2,512,256]{2,1,0:T(8,128)(2,1)S(1)} %collective-permute-done.7.refs_4_) | copy-start | bytes 1572868
  31.4 27.3 %collective-permute-start.8 = (bf16[2,512,256]{2,1,0:T(8,128)(2,1)S(1)}, bf16[2,512,256]{2,1,0:T(8,128)(2,1)S(1)}, u32[]{:S(2)}, u32[]{:S(2)}) collective-permute-start(bf16[2,512,256]{2,1,0:T(8,128)(2,1)S(1)} %collective-permute-done.1.refs_1_), channel_id=1, source_target_pairs={{4,6},{5,7},{6,4},{7,5},{8,10},{9,11},{10,8},{11,9},{12,14},{13,15... | collective-permute-start | bytes 1572872 | tf_op jit(solution)/shard_map/ppermute | solution.py:400
  41.3 65.4 %copy-start = (bf16[2,512,256]{2,1,0:T(8,128)(2,1)}, bf16[2,512,256]{2,1,0:T(8,128)(2,1)S(1)}, u32[]{:S(2)}) copy-start(bf16[2,512,256]{2,1,0:T(8,128)(2,1)S(1)} %collective-permute-done.5.refs_4_) | copy-start | bytes 1572868
  46.3 60.5 %copy-start.1 = (bf16[2,512,256]{2,1,0:T(8,128)(2,1)}, bf16[2,512,256]{2,1,0:T(8,128)(2,1)S(1)}, u32[]{:S(2)}) copy-start(bf16[2,512,256]{2,1,0:T(8,128)(2,1)S(1)} %collective-permute-done.refs_1_) | copy-start | bytes 1572868
  46.3 17.4 %collective-permute-start.6 = (bf16[2,512,256]{2,1,0:T(8,128)(2,1)S(1)}, bf16[2,512,256]{2,1,0:T(8,128)(2,1)S(1)}, u32[]{:S(2)}, u32[]{:S(2)}) collective-permute-start(bf16[2,512,256]{2,1,0:T(8,128)(2,1)S(1)} %collective-permute-done.refs_1_), channel_id=1, source_target_pairs={{4,6},{5,7},{6,4},{7,5},{8,10},{9,11},{10,8},{11,9},{12,14},{13,15... | collective-permute-start | bytes 1572872 | tf_op jit(solution)/shard_map/ppermute | solution.py:400
  56.1 30.9 %copy-start.5 = (bf16[2,512,256]{2,1,0:T(8,128)(2,1)}, bf16[2,512,256]{2,1,0:T(8,128)(2,1)S(1)}, u32[]{:S(2)}) copy-start(bf16[2,512,256]{2,1,0:T(8,128)(2,1)S(1)} %collective-permute-done.2.refs_2_) | copy-start | bytes 1572868
  56.1 16.8 %collective-permute-start.11 = (bf16[2,512,256]{2,1,0:T(8,128)(2,1)S(1)}, bf16[2,512,256]{2,1,0:T(8,128)(2,1)}, u32[]{:S(2)}, u32[]{:S(2)}) collective-permute-start(bf16[2,512,256]{2,1,0:T(8,128)(2,1)S(1)} %collective-permute-done.2.refs_2_), channel_id=1, source_target_pairs={{8,12},{9,13},{10,14},{11,15},{24,28},{25,29},{26,30},{27,31}} | collective-permute-start | bytes 1572872 | tf_op jit(solution)/shard_map/ppermute | solution.py:400
  57.4 24.4 %collective-permute-start.3 = (bf16[2,512,256]{2,1,0:T(8,128)(2,1)S(1)}, bf16[2,512,256]{2,1,0:T(8,128)(2,1)}, u32[]{:S(2)}, u32[]{:S(2)}) collective-permute-start(bf16[2,512,256]{2,1,0:T(8,128)(2,1)S(1)} %collective-permute-done.refs_1_), channel_id=1, source_target_pairs={{4,8},{5,9},{6,10},{7,11},{8,12},{9,13},{10,14},{11,15},{20,24},{2... | collective-permute-start | bytes 1572872 | tf_op jit(solution)/shard_map/ppermute | solution.py:400
  58.7 25.7 %copy-start.6 = (bf16[2,512,256]{2,1,0:T(8,128)(2,1)}, bf16[2,512,256]{2,1,0:T(8,128)(2,1)S(1)}, u32[]{:S(2)}) copy-start(bf16[2,512,256]{2,1,0:T(8,128)(2,1)S(1)} %collective-permute-done.8.refs_5_) | copy-start | bytes 1572868
  58.7 25.7 %collective-permute-start.9 = (bf16[2,512,256]{2,1,0:T(8,128)(2,1)S(1)}, bf16[2,512,256]{2,1,0:T(8,128)(2,1)S(1)}, u32[]{:S(2)}, u32[]{:S(2)}) collective-permute-start(bf16[2,512,256]{2,1,0:T(8,128)(2,1)S(1)} %collective-permute-done.2.refs_2_), channel_id=1, source_target_pairs={{8,10},{9,11},{10,8},{11,9},{12,14},{13,15},{14,12},{15,13},{24,26... | collective-permute-start | bytes 1572872 | tf_op jit(solution)/shard_map/ppermute | solution.py:400
  63.7 43.1 %copy-start.4 = (bf16[2,512,256]{2,1,0:T(8,128)(2,1)}, bf16[2,512,256]{2,1,0:T(8,128)(2,1)S(1)}, u32[]{:S(2)}) copy-start(bf16[2,512,256]{2,1,0:T(8,128)(2,1)S(1)} %collective-permute-done.6.refs_5_) | copy-start | bytes 1572868
  72.9 14.0 %collective-permute-start.13 = (bf16[2,512,256]{2,1,0:T(8,128)(2,1)}, bf16[2,512,256]{2,1,0:T(8,128)(2,1)}, u32[]{:S(2)}, u32[]{:S(2)}) collective-permute-start(bf16[2,512,256]{2,1,0:T(8,128)(2,1)} %collective-permute-done.11.refs_3_), channel_id=1, source_target_pairs={{12,14},{13,15},{14,12},{15,13},{28,30},{29,31},{30,28},{31,29}} | collective-permute-start | bytes 1572872 | tf_op jit(solution)/shard_map/ppermute | solution.py:400
  81.8 25.0 %collective-permute-start.4 = (bf16[2,512,256]{2,1,0:T(8,128)(2,1)}, bf16[2,512,256]{2,1,0:T(8,128)(2,1)}, u32[]{:S(2)}, u32[]{:S(2)}) collective-permute-start(bf16[2,512,256]{2,1,0:T(8,128)(2,1)} %collective-permute-done.3.refs_2_), channel_id=1, source_target_pairs={{8,12},{9,13},{10,14},{11,15},{24,28},{25,29},{26,30},{27,31}} | collective-permute-start | bytes 1572872 | tf_op jit(solution)/shard_map/ppermute | solution.py:400
  83.1 23.7 %collective-permute-start.12 = (bf16[2,512,256]{2,1,0:T(8,128)(2,1)S(1)}, bf16[2,512,256]{2,1,0:T(8,128)(2,1)}, u32[]{:S(2)}, u32[]{:S(2)}) collective-permute-start(bf16[2,512,256]{2,1,0:T(8,128)(2,1)S(1)} %collective-permute-done.5.refs_4_), channel_id=1, source_target_pairs={{0,12},{1,13},{2,14},{3,15},{16,28},{17,29},{18,30},{19,31}} | collective-permute-start | bytes 1572872 | tf_op jit(solution)/shard_map/ppermute | solution.py:400
  84.4 1.9 %copy-start.7 = (bf16[2,512,256]{2,1,0:T(8,128)(2,1)}, bf16[2,512,256]{2,1,0:T(8,128)(2,1)S(1)}, u32[]{:S(2)}) copy-start(bf16[2,512,256]{2,1,0:T(8,128)(2,1)S(1)} %collective-permute-done.9.refs_6_) | copy-start | bytes 1572868
  84.4 22.4 %collective-permute-start.10 = (bf16[2,512,256]{2,1,0:T(8,128)(2,1)}, bf16[2,512,256]{2,1,0:T(8,128)(2,1)}, u32[]{:S(2)}, u32[]{:S(2)}) collective-permute-start(bf16[2,512,256]{2,1,0:T(8,128)(2,1)} %collective-permute-done.3.refs_2_), channel_id=1, source_target_pairs={{8,10},{9,11},{10,8},{11,9},{12,14},{13,15},{14,12},{15,13},{24,26... | collective-permute-start | bytes 1572872 | tf_op jit(solution)/shard_map/ppermute | solution.py:400

commit v19 on v15

--- a/solution.py
+++ b/solution.py
@@ -14,7 +14,7 @@
 CHUNKS = 4
 LOADS = 8
 UNITS = 2
-BLOCKS_PER_STEP = 4
+BLOCKS_PER_STEP = 8
 
 
 PLAN = (
@@ -29,8 +29,8 @@
     ("across", 2, 0, (("across", 1, 0),)),
     ("along", 2, 1, (("along", 2, 0),)),
     ("across", 3, 0, (("across", 1, 1),)),
-    ("across", 2, 1, (("across", 2, 0),)),
-    ("down", 3, 1, (("along", 3, 0), ("across", 2, 0))),
+    ("across", 2, 1, (("across", 2, 0), ("across", 1, 1))),
+    ("down", 3, 1, (("along", 3, 0),)),
     ("along", 3, 1, (("along", 2, 1),)),
 )
 
@@ -67,14 +67,12 @@
 
     for c in range(loads):
         load_x(c).start()
+    for c in range(chunks):
+        for copy in load_weights(c):
+            copy.start()
 
     def square(c, carry):
         load_x(c).wait()
-
-        @pl.when(c == loads - 2)
-        def _():
-            for copy in load_weights(0):
-                copy.start()
 
         row = pl.ds(pl.multiple_of(c * tall, tall), tall)
         total = jnp.zeros((tall, lanes), jnp.float32)
@@ -85,9 +83,6 @@
         return carry
 
     lax.fori_loop(0, loads, square, 0)
-    for c in range(1, chunks):
-        for copy in load_weights(c):
-            copy.start()
     mean_sq = jnp.sum(scale_ref[...], axis=-1, keepdims=True) / features
     scale_ref[...] = jnp.broadcast_to(lax.rsqrt(mean_sq + EPS), scale_ref.shape)
 
@@ -124,12 +119,12 @@
 
 
 def write_heads(kv_ref, acc_scr):
-    width = kv_ref.shape[1] // 2
-    for head in range(width // HEAD_DIM):
+    heads = kv_ref.shape[0]
+    for head in range(heads):
         for part in range(2):
-            source = slice(part * width + head * HEAD_DIM, part * width + (head + 1) * HEAD_DIM)
-            target = slice((2 * head + part) * HEAD_DIM, (2 * head + part + 1) * HEAD_DIM)
-            kv_ref[:, target] = acc_scr[:, source].astype(jnp.bfloat16)
+            first = (part * heads + head) * HEAD_DIM
+            source = acc_scr[:, first : first + HEAD_DIM]
+            kv_ref[head, :, part * HEAD_DIM : (part + 1) * HEAD_DIM] = source.astype(jnp.bfloat16)
 
 
 def norm_project(hidden, gain, key_weight, value_weight):
@@ -144,7 +139,7 @@
         out_specs=[whole, whole],
         out_shape=[
             jax.ShapeDtypeStruct((rows, 128), jnp.float32),
-            jax.ShapeDtypeStruct((rows, 2 * width), jnp.bfloat16),
+            jax.ShapeDtypeStruct((width // HEAD_DIM, rows, 2 * HEAD_DIM), jnp.bfloat16),
         ],
         scratch_shapes=[
             pltpu.VMEM((rows, features), jnp.bfloat16),
@@ -201,8 +196,8 @@
             weight,
             weight,
         ],
-        out_specs=pl.BlockSpec((rows, 2 * width), lambda i: (0, 0)),
-        out_shape=jax.ShapeDtypeStruct((rows, 2 * width), jnp.bfloat16),
+        out_specs=pl.BlockSpec((width // HEAD_DIM, rows, 2 * HEAD_DIM), lambda i: (0, 0, 0)),
+        out_shape=jax.ShapeDtypeStruct((width // HEAD_DIM, rows, 2 * HEAD_DIM), jnp.bfloat16),
         scratch_shapes=[pltpu.VMEM((rows, 2 * width), jnp.float32)],
         compiler_params=pltpu.CompilerParams(vmem_limit_bytes=57 * MIB),
         cost_estimate=pl.CostEstimate(
@@ -225,7 +220,7 @@
     def load_kv(head):
         def copy(ref, level, number):
             return pltpu.make_async_copy(
-                ref.at[:, head * width : (head + 1) * width],
+                ref.at[head],
                 kv_scr.at[head, level],
                 kv_sem.at[head, number],
             )
@@ -328,7 +323,7 @@
     blocks, depth = slots.shape
     block = rows // blocks
     near = len(straight)
-    kv_heads = own.shape[1] // (2 * HEAD_DIM)
+    kv_heads = own.shape[0]
     wide = features // UNITS // kv_heads
     steps = kv_heads * blocks // BLOCKS_PER_STEP
     held = pl.BlockSpec(memory_space=pltpu.HBM)

time: 117 us -> 119 us (1.017)
    pallas_call x1, Pallas kernels: 13.1 us -> 14.8 us  [norm_project(): pl.pallas_call(norm_project_kernel, in_specs=[held, whole, held, held], o...]
  transfers between devices with their start and end apart: 14 -> 14, of which waited for: 8 -> 7; matrix products, arithmetic and copies ran while one was open for 1% -> 1% of each run, Pallas kernels for 17% -> 16%
where the time goes in v19:
time: 119 us; the launch traced here: 118 us
  waiting for transfers between devices  49 us (41%)
  Pallas kernels  43.6 us (37%)
  starting transfers between devices  24.5 us (21%)
    ppermute x14, waiting for transfers between devices, step(): moved[key, s, unit] = lax.ppermute(array, 'node', pairs)  49 us
    ppermute x14, starting transfers between devices, step(): moved[key, s, unit] = lax.ppermute(array, 'node', pairs)  24.5 us
    pallas_call x2, Pallas kernels, attention(): pl.pallas_call(functools.partial(attention_kernel, block, unit, near), in...  19.4 us
    pallas_call x1, Pallas kernels, norm_project(): pl.pallas_call(norm_project_kernel, in_specs=[held, whole, held, held], o...  14.8 us
    pallas_call x1, Pallas kernels, project(): pl.pallas_call(project_kernel, grid=(CHUNKS,), in_specs=[pl.BlockSpec((ro...  9.35 us
  transfers between devices with their start and end apart: 14, of which 7 were waited for; matrix products, arithmetic and copies ran while one was open for 1% of the time, Pallas kernels for 16%

profile of v19, /device:TPU:24, one launch (start us, length us, event | category | flops | bytes accessed | tf_op | source)
XLA Modules:
  0.0 118.2 jit_solution(15984007258707291751)
XLA Ops:
  0.0 14.8 %norm_project.1 = (f32[512,128]{1,0:T(8,128)}, bf16[2,512,256]{2,1,0:T(8,128)(2,1)}) custom-call(bf16[512,8192]{1,0:T(8,128)(2,1)} %x_ref.1, f32[1,8192]{1,0:T(1,128)} %bitcast.2, bf16[8192,512]{1,0:T(8,128)(2,1)} %key_ref.1, bf16[8192,512]{1,0:T(8,128)(2,1)} %value_ref.1), custom_call_target="tpu_custom_call" | custom-call | flops 4294967296 | bytes 16777216 | tf_op jit(solution)/shard_map/norm_project/pallas_call | solution.py:136
  14.8 1.3 %collective-permute-start.1 = (bf16[2,512,256]{2,1,0:T(8,128)(2,1)}, bf16[2,512,256]{2,1,0:T(8,128)(2,1)S(1)}, u32[]{:S(2)}, u32[]{:S(2)}) collective-permute-start(bf16[2,512,256]{2,1,0:T(8,128)(2,1)} %get-tuple-element.18.refs_0_), channel_id=1, source_target_pairs={{0,4},{1,5},{2,6},{3,7},{4,8},{5,9},{6,10},{7,11},{8,12},{9,13},{1... | collective-permute-start | bytes 1572872 | tf_op jit(solution)/shard_map/ppermute | solution.py:397
  16.1 3.5 %collective-permute-start.7 = (bf16[2,512,256]{2,1,0:T(8,128)(2,1)}, bf16[2,512,256]{2,1,0:T(8,128)(2,1)S(1)}, u32[]{:S(2)}, u32[]{:S(2)}) collective-permute-start(bf16[2,512,256]{2,1,0:T(8,128)(2,1)} %get-tuple-element.18.refs_0_), channel_id=1, source_target_pairs={{0,2},{1,3},{4,6},{5,7},{8,10},{9,11},{12,14},{13,15},{16,18},{17,... | collective-permute-start | bytes 1572872 | tf_op jit(solution)/shard_map/ppermute | solution.py:397
  19.6 0.0 copy-start.8
  19.6 9.3 %project.1.refs_0_ = bf16[2,512,256]{2,1,0:T(8,128)(2,1)} custom-call(bf16[512,8192]{1,0:T(8,128)(2,1)} %x_ref.1, f32[512,128]{1,0:T(8,128)} %get-tuple-element.17.scale_ref, f32[1,8192]{1,0:T(1,128)} %bitcast.3, bf16[8192,512]{1,0:T(8,128)(2,1)} %key_ref.1, bf16[8192,512]{1,0:T(8,128)(2,1)} %value_ref.1), custom_call_target="tpu_custom_call" | custom-call | flops 4294967296 | bytes 16777216 | tf_op jit(solution)/shard_map/project/pallas_call | solution.py:189
  28.9 1.3 %collective-permute-start.5 = (bf16[2,512,256]{2,1,0:T(8,128)(2,1)}, bf16[2,512,256]{2,1,0:T(8,128)(2,1)S(1)}, u32[]{:S(2)}, u32[]{:S(2)}) collective-permute-start(bf16[2,512,256]{2,1,0:T(8,128)(2,1)} %project.1.refs_0_), channel_id=1, source_target_pairs={{0,2},{1,3},{2,0},{3,1},{4,6},{5,7},{8,10},{9,11},{12,14},{13,15},... | collective-permute-start | bytes 1572872 | tf_op jit(solution)/shard_map/ppermute | solution.py:397
  30.2 1.3 %collective-permute-start = (bf16[2,512,256]{2,1,0:T(8,128)(2,1)}, bf16[2,512,256]{2,1,0:T(8,128)(2,1)S(1)}, u32[]{:S(2)}, u32[]{:S(2)}) collective-permute-start(bf16[2,512,256]{2,1,0:T(8,128)(2,1)} %project.1.refs_0_), channel_id=1, source_target_pairs={{0,4},{1,5},{2,6},{3,7},{4,8},{5,9},{6,10},{7,11},{8,12},{9,13},{1... | collective-permute-start | bytes 1572872 | tf_op jit(solution)/shard_map/ppermute | solution.py:397
  31.5 0.0 collective-permute-done.1.refs_1_
  31.6 0.0 copy-start.2
  31.6 1.3 %collective-permute-start.2 = (bf16[2,512,256]{2,1,0:T(8,128)(2,1)S(1)}, bf16[2,512,256]{2,1,0:T(8,128)(2,1)S(1)}, u32[]{:S(2)}, u32[]{:S(2)}) collective-permute-start(bf16[2,512,256]{2,1,0:T(8,128)(2,1)S(1)} %collective-permute-done.1.refs_1_), channel_id=1, source_target_pairs={{4,8},{5,9},{6,10},{7,11},{8,12},{9,13},{10,14},{11,15},{20,24},{2... | collective-permute-start | bytes 1572872 | tf_op jit(solution)/shard_map/ppermute | solution.py:397
  32.9 0.0 collective-permute-done.7.refs_4_
  32.9 0.0 copy-start.3
  32.9 2.9 %collective-permute-start.8 = (bf16[2,512,256]{2,1,0:T(8,128)(2,1)S(1)}, bf16[2,512,256]{2,1,0:T(8,128)(2,1)S(1)}, u32[]{:S(2)}, u32[]{:S(2)}) collective-permute-start(bf16[2,512,256]{2,1,0:T(8,128)(2,1)S(1)} %collective-permute-done.1.refs_1_), channel_id=1, source_target_pairs={{4,6},{5,7},{6,4},{7,5},{8,10},{9,11},{10,8},{11,9},{12,14},{13,15... | collective-permute-start | bytes 1572872 | tf_op jit(solution)/shard_map/ppermute | solution.py:397
  35.8 7.1 %collective-permute-done.5.refs_4_ = bf16[2,512,256]{2,1,0:T(8,128)(2,1)S(1)} collective-permute-done((bf16[2,512,256]{2,1,0:T(8,128)(2,1)}, bf16[2,512,256]{2,1,0:T(8,128)(2,1)S(1)}, u32[]{:S(2)}, u32[]{:S(2)}) %collective-permute-start.5) | collective-permute-done | bytes 524320 | tf_op jit(solution)/shard_map/ppermute | solution.py:397
  42.8 0.0 copy-start
  42.8 5.0 %collective-permute-done.refs_1_ = bf16[2,512,256]{2,1,0:T(8,128)(2,1)S(1)} collective-permute-done((bf16[2,512,256]{2,1,0:T(8,128)(2,1)}, bf16[2,512,256]{2,1,0:T(8,128)(2,1)S(1)}, u32[]{:S(2)}, u32[]{:S(2)}) %collective-permute-start) | collective-permute-done | bytes 524320 | tf_op jit(solution)/shard_map/ppermute | solution.py:397
  47.8 1.9 %collective-permute-start.6 = (bf16[2,512,256]{2,1,0:T(8,128)(2,1)S(1)}, bf16[2,512,256]{2,1,0:T(8,128)(2,1)S(1)}, u32[]{:S(2)}, u32[]{:S(2)}) collective-permute-start(bf16[2,512,256]{2,1,0:T(8,128)(2,1)S(1)} %collective-permute-done.refs_1_), channel_id=1, source_target_pairs={{4,6},{5,7},{6,4},{7,5},{8,10},{9,11},{10,8},{11,9},{12,14},{13,15... | collective-permute-start | bytes 1572872 | tf_op jit(solution)/shard_map/ppermute | solution.py:397
  49.8 7.8 %collective-permute-done.2.refs_2_ = bf16[2,512,256]{2,1,0:T(8,128)(2,1)S(1)} collective-permute-done((bf16[2,512,256]{2,1,0:T(8,128)(2,1)S(1)}, bf16[2,512,256]{2,1,0:T(8,128)(2,1)S(1)}, u32[]{:S(2)}, u32[]{:S(2)}) %collective-permute-start.2) | collective-permute-done | bytes 524320 | tf_op jit(solution)/shard_map/ppermute | solution.py:397
  57.6 1.3 %collective-permute-start.11 = (bf16[2,512,256]{2,1,0:T(8,128)(2,1)S(1)}, bf16[2,512,256]{2,1,0:T(8,128)(2,1)}, u32[]{:S(2)}, u32[]{:S(2)}) collective-permute-start(bf16[2,512,256]{2,1,0:T(8,128)(2,1)S(1)} %collective-permute-done.2.refs_2_), channel_id=1, source_target_pairs={{8,12},{9,13},{10,14},{11,15},{24,28},{25,29},{26,30},{27,31}} | collective-permute-start | bytes 1572872 | tf_op jit(solution)/shard_map/ppermute | solution.py:397
  58.9 1.3 %collective-permute-start.3 = (bf16[2,512,256]{2,1,0:T(8,128)(2,1)S(1)}, bf16[2,512,256]{2,1,0:T(8,128)(2,1)}, u32[]{:S(2)}, u32[]{:S(2)}) collective-permute-start(bf16[2,512,256]{2,1,0:T(8,128)(2,1)S(1)} %collective-permute-done.refs_1_), channel_id=1, source_target_pairs={{4,8},{5,9},{6,10},{7,11},{8,12},{9,13},{10,14},{11,15},{20,24},{2... | collective-permute-start | bytes 1572872 | tf_op jit(solution)/shard_map/ppermute | solution.py:397
  60.2 0.0 collective-permute-done.8.refs_5_
  60.2 0.0 copy-start.6
  60.2 1.9 %collective-permute-start.9 = (bf16[2,512,256]{2,1,0:T(8,128)(2,1)S(1)}, bf16[2,512,256]{2,1,0:T(8,128)(2,1)S(1)}, u32[]{:S(2)}, u32[]{:S(2)}) collective-permute-start(bf16[2,512,256]{2,1,0:T(8,128)(2,1)S(1)} %collective-permute-done.2.refs_2_), channel_id=1, source_target_pairs={{8,10},{9,11},{10,8},{11,9},{12,14},{13,15},{14,12},{15,13},{24,26... | collective-permute-start | bytes 1572872 | tf_op jit(solution)/shard_map/ppermute | solution.py:397
  62.1 3.1 %collective-permute-done.6.refs_5_ = bf16[2,512,256]{2,1,0:T(8,128)(2,1)S(1)} collective-permute-done((bf16[2,512,256]{2,1,0:T(8,128)(2,1)S(1)}, bf16[2,512,256]{2,1,0:T(8,128)(2,1)S(1)}, u32[]{:S(2)}, u32[]{:S(2)}) %collective-permute-start.6) | collective-permute-done | bytes 524320 | tf_op jit(solution)/shard_map/ppermute | solution.py:397
  65.2 9.2 %collective-permute-done.11.refs_3_ = bf16[2,512,256]{2,1,0:T(8,128)(2,1)} collective-permute-done((bf16[2,512,256]{2,1,0:T(8,128)(2,1)S(1)}, bf16[2,512,256]{2,1,0:T(8,128)(2,1)}, u32[]{:S(2)}, u32[]{:S(2)}) %collective-permute-start.11) | collective-permute-done | bytes 524320 | tf_op jit(solution)/shard_map/ppermute | solution.py:397
  74.4 1.9 %collective-permute-start.13 = (bf16[2,512,256]{2,1,0:T(8,128)(2,1)}, bf16[2,512,256]{2,1,0:T(8,128)(2,1)}, u32[]{:S(2)}, u32[]{:S(2)}) collective-permute-start(bf16[2,512,256]{2,1,0:T(8,128)(2,1)} %collective-permute-done.11.refs_3_), channel_id=1, source_target_pairs={{12,14},{13,15},{14,12},{15,13},{28,30},{29,31},{30,28},{31,29}} | collective-permute-start | bytes 1572872 | tf_op jit(solution)/shard_map/ppermute | solution.py:397
  76.4 6.9 %collective-permute-done.3.refs_2_ = bf16[2,512,256]{2,1,0:T(8,128)(2,1)} collective-permute-done((bf16[2,512,256]{2,1,0:T(8,128)(2,1)S(1)}, bf16[2,512,256]{2,1,0:T(8,128)(2,1)}, u32[]{:S(2)}, u32[]{:S(2)}) %collective-permute-start.3) | collective-permute-done | bytes 524320 | tf_op jit(solution)/shard_map/ppermute | solution.py:397
  83.3 1.3 %collective-permute-start.4 = (bf16[2,512,256]{2,1,0:T(8,128)(2,1)}, bf16[2,512,256]{2,1,0:T(8,128)(2,1)}, u32[]{:S(2)}, u32[]{:S(2)}) collective-permute-start(bf16[2,512,256]{2,1,0:T(8,128)(2,1)} %collective-permute-done.3.refs_2_), channel_id=1, source_target_pairs={{8,12},{9,13},{10,14},{11,15},{24,28},{25,29},{26,30},{27,31}} | collective-permute-start | bytes 1572872 | tf_op jit(solution)/shard_map/ppermute | solution.py:397
  84.6 1.3 %collective-permute-start.12 = (bf16[2,512,256]{2,1,0:T(8,128)(2,1)S(1)}, bf16[2,512,256]{2,1,0:T(8,128)(2,1)}, u32[]{:S(2)}, u32[]{:S(2)}) collective-permute-start(bf16[2,512,256]{2,1,0:T(8,128)(2,1)S(1)} %collective-permute-done.5.refs_4_), channel_id=1, source_target_pairs={{0,12},{1,13},{2,14},{3,15},{16,28},{17,29},{18,30},{19,31}} | collective-permute-start | bytes 1572872 | tf_op jit(solution)/shard_map/ppermute | solution.py:397
  85.9 0.0 collective-permute-done.9.refs_6_
  85.9 0.0 copy-done.6
  85.9 0.0 copy-start.7
  85.9 2.1 %collective-permute-start.10 = (bf16[2,512,256]{2,1,0:T(8,128)(2,1)}, bf16[2,512,256]{2,1,0:T(8,128)(2,1)}, u32[]{:S(2)}, u32[]{:S(2)}) collective-permute-start(bf16[2,512,256]{2,1,0:T(8,128)(2,1)} %collective-permute-done.3.refs_2_), channel_id=1, source_target_pairs={{8,10},{9,11},{10,8},{11,9},{12,14},{13,15},{14,12},{15,13},{24,26... | collective-permute-start | bytes 1572872 | tf_op jit(solution)/shard_map/ppermute | solution.py:397
  88.0 0.0 copy-done.7
  88.1 0.0 copy-done.8
  88.1 0.6 fusion.1.slot_ref
  88.7 0.0 collective-permute-done.13.refs_7_
  88.7 0.0 copy-done.2
  88.7 0.0 copy-done.3
  88.7 0.0 copy-done.5
  88.7 9.7 %attention.2.refs_8_ = bf16[512,4096]{1,0:T(8,128)(2,1)} custom-call(s32[8,7]{1,0:T(8,128)} %fusion.1.slot_ref, s32[8,7]{1,0:T(8,128)} %cut_ref.3, s32[1]{0:T(128)} %bitcast.odd_ref, bf16[512,4096]{1,0:T(8,128)(2,1)} %q_hbm.3, bf16[2,512,256]{2,1,0:T(8,128)(2,1)} %get-tuple-element.18.refs_0_, bf16[2,512,256]{2,1,0:T(8,128)(2,1)} %copy-done.2, ...), custom_call_target="tpu_custom_call" | custom-call | flops 2147483648 | bytes 8388608 | tf_op jit(solution)/shard_map/attention/pallas_call | solution.py:336
  98.4 9.9 %collective-permute-done.4.refs_3_ = bf16[2,512,256]{2,1,0:T(8,128)(2,1)} collective-permute-done((bf16[2,512,256]{2,1,0:T(8,128)(2,1)}, bf16[2,512,256]{2,1,0:T(8,128)(2,1)}, u32[]{:S(2)}, u32[]{:S(2)}) %collective-permute-start.4) | collective-permute-done | bytes 524320 | tf_op jit(solution)/shard_map/ppermute | solution.py:397
  108.3 0.0 collective-permute-done.12.refs_7_
  108.3 0.0 collective-permute-done.10.refs_6_
  108.3 0.0 copy-done
  108.3 0.0 copy-done.1
  108.3 0.0 copy-done.4
  108.3 9.7 %attention.3 = bf16[512,4096]{1,0:T(8,128)(2,1)} custom-call(s32[8,7]{1,0:T(8,128)} %fusion.1.slot_ref, s32[8,7]{1,0:T(8,128)} %cut_ref.3, s32[1]{0:T(128)} %bitcast.odd_ref, bf16[512,4096]{1,0:T(8,128)(2,1)} %q_hbm.3, bf16[2,512,256]{2,1,0:T(8,128)(2,1)} %project.1.refs_0_, bf16[2,512,256]{2,1,0:T(8,128)(2,1)} %copy-done.1, ...), custom_call_target="tpu_custom_call", output_to_operand_aliasing={{}: (12, {})} | custom-call | flops 2147483648 | bytes 8388608 | tf_op jit(solution)/shard_map/attention/pallas_call | solution.py:336
  (3 shorter events, 0.0 us)
Async XLA Ops:
  14.8 16.7 %collective-permute-start.1 = (bf16[2,512,256]{2,1,0:T(8,128)(2,1)}, bf16[2,512,256]{2,1,0:T(8,128)(2,1)S(1)}, u32[]{:S(2)}, u32[]{:S(2)}) collective-permute-start(bf16[2,512,256]{2,1,0:T(8,128)(2,1)} %get-tuple-element.18.refs_0_), channel_id=1, source_target_pairs={{0,4},{1,5},{2,6},{3,7},{4,8},{5,9},{6,10},{7,11},{8,12},{9,13},{1... | collective-permute-start | bytes 1572872 | tf_op jit(solution)/shard_map/ppermute | solution.py:397
  16.1 16.8 %collective-permute-start.7 = (bf16[2,512,256]{2,1,0:T(8,128)(2,1)}, bf16[2,512,256]{2,1,0:T(8,128)(2,1)S(1)}, u32[]{:S(2)}, u32[]{:S(2)}) collective-permute-start(bf16[2,512,256]{2,1,0:T(8,128)(2,1)} %get-tuple-element.18.refs_0_), channel_id=1, source_target_pairs={{0,2},{1,3},{4,6},{5,7},{8,10},{9,11},{12,14},{13,15},{16,18},{17,... | collective-permute-start | bytes 1572872 | tf_op jit(solution)/shard_map/ppermute | solution.py:397
  19.6 68.5 %copy-start.8 = (s32[8,7]{1,0:T(8,128)S(1)}, s32[8,7]{1,0:T(8,128)}, u32[]{:S(2)}) copy-start(s32[8,7]{1,0:T(8,128)} %param.12) | copy-start | bytes 676
  28.9 13.9 %collective-permute-start.5 = (bf16[2,512,256]{2,1,0:T(8,128)(2,1)}, bf16[2,512,256]{2,1,0:T(8,128)(2,1)S(1)}, u32[]{:S(2)}, u32[]{:S(2)}) collective-permute-start(bf16[2,512,256]{2,1,0:T(8,128)(2,1)} %project.1.refs_0_), channel_id=1, source_target_pairs={{0,2},{1,3},{2,0},{3,1},{4,6},{5,7},{8,10},{9,11},{12,14},{13,15},... | collective-permute-start | bytes 1572872 | tf_op jit(solution)/shard_map/ppermute | solution.py:397
  30.2 17.6 %collective-permute-start = (bf16[2,512,256]{2,1,0:T(8,128)(2,1)}, bf16[2,512,256]{2,1,0:T(8,128)(2,1)S(1)}, u32[]{:S(2)}, u32[]{:S(2)}) collective-permute-start(bf16[2,512,256]{2,1,0:T(8,128)(2,1)} %project.1.refs_0_), channel_id=1, source_target_pairs={{0,4},{1,5},{2,6},{3,7},{4,8},{5,9},{6,10},{7,11},{8,12},{9,13},{1... | collective-permute-start | bytes 1572872 | tf_op jit(solution)/shard_map/ppermute | solution.py:397
  31.6 57.1 %copy-start.2 = (bf16[2,512,256]{2,1,0:T(8,128)(2,1)}, bf16[2,512,256]{2,1,0:T(8,128)(2,1)S(1)}, u32[]{:S(2)}) copy-start(bf16[2,512,256]{2,1,0:T(8,128)(2,1)S(1)} %collective-permute-done.1.refs_1_) | copy-start | bytes 1572868
  31.6 26.0 %collective-permute-start.2 = (bf16[2,512,256]{2,1,0:T(8,128)(2,1)S(1)}, bf16[2,512,256]{2,1,0:T(8,128)(2,1)S(1)}, u32[]{:S(2)}, u32[]{:S(2)}) collective-permute-start(bf16[2,512,256]{2,1,0:T(8,128)(2,1)S(1)} %collective-permute-done.1.refs_1_), channel_id=1, source_target_pairs={{4,8},{5,9},{6,10},{7,11},{8,12},{9,13},{10,14},{11,15},{20,24},{2... | collective-permute-start | bytes 1572872 | tf_op jit(solution)/shard_map/ppermute | solution.py:397
  32.9 55.8 %copy-start.3 = (bf16[2,512,256]{2,1,0:T(8,128)(2,1)}, bf16[2,512,256]{2,1,0:T(8,128)(2,1)S(1)}, u32[]{:S(2)}) copy-start(bf16[2,512,256]{2,1,0:T(8,128)(2,1)S(1)} %collective-permute-done.7.refs_4_) | copy-start | bytes 1572868
  32.9 27.3 %collective-permute-start.8 = (bf16[2,512,256]{2,1,0:T(8,128)(2,1)S(1)}, bf16[2,512,256]{2,1,0:T(8,128)(2,1)S(1)}, u32[]{:S(2)}, u32[]{:S(2)}) collective-permute-start(bf16[2,512,256]{2,1,0:T(8,128)(2,1)S(1)} %collective-permute-done.1.refs_1_), channel_id=1, source_target_pairs={{4,6},{5,7},{6,4},{7,5},{8,10},{9,11},{10,8},{11,9},{12,14},{13,15... | collective-permute-start | bytes 1572872 | tf_op jit(solution)/shard_map/ppermute | solution.py:397
  42.8 65.4 %copy-start = (bf16[2,512,256]{2,1,0:T(8,128)(2,1)}, bf16[2,512,256]{2,1,0:T(8,128)(2,1)S(1)}, u32[]{:S(2)}) copy-start(bf16[2,512,256]{2,1,0:T(8,128)(2,1)S(1)} %collective-permute-done.5.refs_4_) | copy-start | bytes 1572868
  47.8 60.5 %copy-start.1 = (bf16[2,512,256]{2,1,0:T(8,128)(2,1)}, bf16[2,512,256]{2,1,0:T(8,128)(2,1)S(1)}, u32[]{:S(2)}) copy-start(bf16[2,512,256]{2,1,0:T(8,128)(2,1)S(1)} %collective-permute-done.refs_1_) | copy-start | bytes 1572868
  47.8 17.4 %collective-permute-start.6 = (bf16[2,512,256]{2,1,0:T(8,128)(2,1)S(1)}, bf16[2,512,256]{2,1,0:T(8,128)(2,1)S(1)}, u32[]{:S(2)}, u32[]{:S(2)}) collective-permute-start(bf16[2,512,256]{2,1,0:T(8,128)(2,1)S(1)} %collective-permute-done.refs_1_), channel_id=1, source_target_pairs={{4,6},{5,7},{6,4},{7,5},{8,10},{9,11},{10,8},{11,9},{12,14},{13,15... | collective-permute-start | bytes 1572872 | tf_op jit(solution)/shard_map/ppermute | solution.py:397
  57.6 31.1 %copy-start.5 = (bf16[2,512,256]{2,1,0:T(8,128)(2,1)}, bf16[2,512,256]{2,1,0:T(8,128)(2,1)S(1)}, u32[]{:S(2)}) copy-start(bf16[2,512,256]{2,1,0:T(8,128)(2,1)S(1)} %collective-permute-done.2.refs_2_) | copy-start | bytes 1572868
  57.6 16.8 %collective-permute-start.11 = (bf16[2,512,256]{2,1,0:T(8,128)(2,1)S(1)}, bf16[2,512,256]{2,1,0:T(8,128)(2,1)}, u32[]{:S(2)}, u32[]{:S(2)}) collective-permute-start(bf16[2,512,256]{2,1,0:T(8,128)(2,1)S(1)} %collective-permute-done.2.refs_2_), channel_id=1, source_target_pairs={{8,12},{9,13},{10,14},{11,15},{24,28},{25,29},{26,30},{27,31}} | collective-permute-start | bytes 1572872 | tf_op jit(solution)/shard_map/ppermute | solution.py:397
  58.9 24.4 %collective-permute-start.3 = (bf16[2,512,256]{2,1,0:T(8,128)(2,1)S(1)}, bf16[2,512,256]{2,1,0:T(8,128)(2,1)}, u32[]{:S(2)}, u32[]{:S(2)}) collective-permute-start(bf16[2,512,256]{2,1,0:T(8,128)(2,1)S(1)} %collective-permute-done.refs_1_), channel_id=1, source_target_pairs={{4,8},{5,9},{6,10},{7,11},{8,12},{9,13},{10,14},{11,15},{20,24},{2... | collective-permute-start | bytes 1572872 | tf_op jit(solution)/shard_map/ppermute | solution.py:397
  60.2 25.7 %copy-start.6 = (bf16[2,512,256]{2,1,0:T(8,128)(2,1)}, bf16[2,512,256]{2,1,0:T(8,128)(2,1)S(1)}, u32[]{:S(2)}) copy-start(bf16[2,512,256]{2,1,0:T(8,128)(2,1)S(1)} %collective-permute-done.8.refs_5_) | copy-start | bytes 1572868
  60.2 25.7 %collective-permute-start.9 = (bf16[2,512,256]{2,1,0:T(8,128)(2,1)S(1)}, bf16[2,512,256]{2,1,0:T(8,128)(2,1)S(1)}, u32[]{:S(2)}, u32[]{:S(2)}) collective-permute-start(bf16[2,512,256]{2,1,0:T(8,128)(2,1)S(1)} %collective-permute-done.2.refs_2_), channel_id=1, source_target_pairs={{8,10},{9,11},{10,8},{11,9},{12,14},{13,15},{14,12},{15,13},{24,26... | collective-permute-start | bytes 1572872 | tf_op jit(solution)/shard_map/ppermute | solution.py:397
  65.2 43.1 %copy-start.4 = (bf16[2,512,256]{2,1,0:T(8,128)(2,1)}, bf16[2,512,256]{2,1,0:T(8,128)(2,1)S(1)}, u32[]{:S(2)}) copy-start(bf16[2,512,256]{2,1,0:T(8,128)(2,1)S(1)} %collective-permute-done.6.refs_5_) | copy-start | bytes 1572868
  74.4 14.2 %collective-permute-start.13 = (bf16[2,512,256]{2,1,0:T(8,128)(2,1)}, bf16[2,512,256]{2,1,0:T(8,128)(2,1)}, u32[]{:S(2)}, u32[]{:S(2)}) collective-permute-start(bf16[2,512,256]{2,1,0:T(8,128)(2,1)} %collective-permute-done.11.refs_3_), channel_id=1, source_target_pairs={{12,14},{13,15},{14,12},{15,13},{28,30},{29,31},{30,28},{31,29}} | collective-permute-start | bytes 1572872 | tf_op jit(solution)/shard_map/ppermute | solution.py:397
  83.3 25.0 %collective-permute-start.4 = (bf16[2,512,256]{2,1,0:T(8,128)(2,1)}, bf16[2,512,256]{2,1,0:T(8,128)(2,1)}, u32[]{:S(2)}, u32[]{:S(2)}) collective-permute-start(bf16[2,512,256]{2,1,0:T(8,128)(2,1)} %collective-permute-done.3.refs_2_), channel_id=1, source_target_pairs={{8,12},{9,13},{10,14},{11,15},{24,28},{25,29},{26,30},{27,31}} | collective-permute-start | bytes 1572872 | tf_op jit(solution)/shard_map/ppermute | solution.py:397
  84.6 23.7 %collective-permute-start.12 = (bf16[2,512,256]{2,1,0:T(8,128)(2,1)S(1)}, bf16[2,512,256]{2,1,0:T(8,128)(2,1)}, u32[]{:S(2)}, u32[]{:S(2)}) collective-permute-start(bf16[2,512,256]{2,1,0:T(8,128)(2,1)S(1)} %collective-permute-done.5.refs_4_), channel_id=1, source_target_pairs={{0,12},{1,13},{2,14},{3,15},{16,28},{17,29},{18,30},{19,31}} | collective-permute-start | bytes 1572872 | tf_op jit(solution)/shard_map/ppermute | solution.py:397
  85.9 2.1 %copy-start.7 = (bf16[2,512,256]{2,1,0:T(8,128)(2,1)}, bf16[2,512,256]{2,1,0:T(8,128)(2,1)S(1)}, u32[]{:S(2)}) copy-start(bf16[2,512,256]{2,1,0:T(8,128)(2,1)S(1)} %collective-permute-done.9.refs_6_) | copy-start | bytes 1572868
  85.9 22.4 %collective-permute-start.10 = (bf16[2,512,256]{2,1,0:T(8,128)(2,1)}, bf16[2,512,256]{2,1,0:T(8,128)(2,1)}, u32[]{:S(2)}, u32[]{:S(2)}) collective-permute-start(bf16[2,512,256]{2,1,0:T(8,128)(2,1)} %collective-permute-done.3.refs_2_), channel_id=1, source_target_pairs={{8,10},{9,11},{10,8},{11,9},{12,14},{13,15},{14,12},{15,13},{24,26... | collective-permute-start | bytes 1572872 | tf_op jit(solution)/shard_map/ppermute | solution.py:397

commit v20 on v19

--- a/solution.py
+++ b/solution.py
@@ -37,7 +37,7 @@
 
 def norm_project_kernel(
     x_hbm, gain_ref, key_hbm, value_hbm, scale_ref, kv_ref,
-    x_scr, weight_scr, even_scr, odd_scr, acc_scr, x_sem, key_sem, value_sem,
+    x_scr, weight_scr, acc_scr, x_sem, key_sem, value_sem,
 ):
     rows, features = x_scr.shape
     loads = LOADS
@@ -45,7 +45,6 @@
     chunks, chunk = weight_scr.shape[:2]
     width = weight_scr.shape[2] // 2
     lanes = 128
-    band = 128
 
     def span(c):
         return pl.ds(pl.multiple_of(c * chunk, chunk), chunk)
@@ -67,12 +66,14 @@
 
     for c in range(loads):
         load_x(c).start()
-    for c in range(chunks):
-        for copy in load_weights(c):
-            copy.start()
 
     def square(c, carry):
         load_x(c).wait()
+
+        @pl.when(c == loads - 2)
+        def _():
+            for copy in load_weights(0):
+                copy.start()
 
         row = pl.ds(pl.multiple_of(c * tall, tall), tall)
         total = jnp.zeros((tall, lanes), jnp.float32)
@@ -83,38 +84,32 @@
         return carry
 
     lax.fori_loop(0, loads, square, 0)
+    for c in range(1, chunks):
+        for copy in load_weights(c):
+            copy.start()
     mean_sq = jnp.sum(scale_ref[...], axis=-1, keepdims=True) / features
     scale_ref[...] = jnp.broadcast_to(lax.rsqrt(mean_sq + EPS), scale_ref.shape)
 
-    def normalise(normed_scr, c):
-        for first in range(0, rows, band):
-            row = slice(first, first + band)
-            inverse = scale_ref[row, :]
-            for lane in range(0, chunk, lanes):
-                cols = pl.ds(pl.multiple_of(c * chunk + lane, lanes), lanes)
-                x = x_scr[row, cols].astype(jnp.float32)
-                normed_scr[row, lane : lane + lanes] = (
-                    x * inverse * gain_ref[:, cols]
-                ).astype(jnp.bfloat16)
-
-    def multiply(normed_scr, c):
+    acc_scr[...] = jnp.zeros_like(acc_scr)
+
+    def multiply(c, carry):
         for copy in load_weights(c):
             copy.wait()
-        return jnp.dot(normed_scr[...], weight_scr[c], preferred_element_type=jnp.float32)
-
-    normalise(even_scr, 0)
-    acc_scr[...] = multiply(even_scr, 0)
-    normalise(odd_scr, 1)
-
-    def pair(p, carry):
-        acc_scr[...] += multiply(odd_scr, 2 * p + 1)
-        normalise(even_scr, 2 * p + 2)
-        acc_scr[...] += multiply(even_scr, 2 * p + 2)
-        normalise(odd_scr, 2 * p + 3)
+        inverse = scale_ref[...]
+        parts = []
+        for lane in range(0, chunk, lanes):
+            cols = pl.ds(pl.multiple_of(c * chunk + lane, lanes), lanes)
+            x = x_scr[:, cols].astype(jnp.float32)
+            parts.append((x * inverse * gain_ref[:, cols]).astype(jnp.bfloat16))
+        normed = jnp.concatenate(parts, axis=1)
+        for part in range(2):
+            cols = slice(part * width, (part + 1) * width)
+            acc_scr[:, cols] += jnp.dot(
+                normed, weight_scr[c, :, cols], preferred_element_type=jnp.float32
+            )
         return carry
 
-    lax.fori_loop(0, chunks // 2 - 1, pair, 0)
-    acc_scr[...] += multiply(odd_scr, chunks - 1)
+    lax.fori_loop(0, chunks, multiply, 0)
     write_heads(kv_ref, acc_scr)
 
 
@@ -144,8 +139,6 @@
         scratch_shapes=[
             pltpu.VMEM((rows, features), jnp.bfloat16),
             pltpu.VMEM((CHUNKS, chunk, 2 * width), jnp.bfloat16),
-            pltpu.VMEM((rows, chunk), jnp.bfloat16),
-            pltpu.VMEM((rows, chunk), jnp.bfloat16),
             pltpu.VMEM((rows, 2 * width), jnp.float32),
             pltpu.SemaphoreType.DMA((LOADS,)),
             pltpu.SemaphoreType.DMA((CHUNKS,)),

time: 119 us -> 115 us (0.966)
  Pallas kernels: 43.6 us -> 40.4 us
    pallas_call x1, Pallas kernels: 14.8 us -> 11.7 us  [norm_project(): pl.pallas_call(norm_project_kernel, in_specs=[held, whole, held, held], o...]
  transfers between devices with their start and end apart: 14 -> 14, of which waited for: 7 -> 7; matrix products, arithmetic and copies ran while one was open for 1% -> 1% of each run, Pallas kernels for 16% -> 17%
where the time goes in v20:
time: 115 us
  waiting for transfers between devices  49.2 us (43%)
  Pallas kernels  40.4 us (35%)
  starting transfers between devices  24.3 us (21%)
    ppermute x14, waiting for transfers between devices, step(): moved[key, s, unit] = lax.ppermute(array, 'node', pairs)  49.2 us
    ppermute x14, starting transfers between devices, step(): moved[key, s, unit] = lax.ppermute(array, 'node', pairs)  24.3 us
    pallas_call x2, Pallas kernels, attention(): pl.pallas_call(functools.partial(attention_kernel, block, unit, near), in...  19.4 us
    pallas_call x1, Pallas kernels, norm_project(): pl.pallas_call(norm_project_kernel, in_specs=[held, whole, held, held], o...  11.7 us
    pallas_call x1, Pallas kernels, project(): pl.pallas_call(project_kernel, grid=(CHUNKS,), in_specs=[pl.BlockSpec((ro...  9.35 us
  transfers between devices with their start and end apart: 14, of which 7 were waited for; matrix products, arithmetic and copies ran while one was open for 1% of the time, Pallas kernels for 17%

profile of v20, /device:TPU:24, one launch (start us, length us, event | category | flops | bytes accessed | tf_op | source)
XLA Modules:
  0.0 114.9 jit_solution(1886588001136887519)
XLA Ops:
  0.0 11.7 %norm_project.1 = (f32[512,128]{1,0:T(8,128)}, bf16[2,512,256]{2,1,0:T(8,128)(2,1)}) custom-call(bf16[512,8192]{1,0:T(8,128)(2,1)} %x_ref.1, f32[1,8192]{1,0:T(1,128)} %bitcast.2, bf16[8192,512]{1,0:T(8,128)(2,1)} %key_ref.1, bf16[8192,512]{1,0:T(8,128)(2,1)} %value_ref.1), custom_call_target="tpu_custom_call" | custom-call | flops 4294967296 | bytes 16777216 | tf_op jit(solution)/shard_map/norm_project/pallas_call | solution.py:131
  11.7 1.3 %collective-permute-start.1 = (bf16[2,512,256]{2,1,0:T(8,128)(2,1)}, bf16[2,512,256]{2,1,0:T(8,128)(2,1)S(1)}, u32[]{:S(2)}, u32[]{:S(2)}) collective-permute-start(bf16[2,512,256]{2,1,0:T(8,128)(2,1)} %get-tuple-element.18.refs_0_), channel_id=1, source_target_pairs={{0,4},{1,5},{2,6},{3,7},{4,8},{5,9},{6,10},{7,11},{8,12},{9,13},{1... | collective-permute-start | bytes 1572872 | tf_op jit(solution)/shard_map/ppermute | solution.py:390
  13.0 3.4 %collective-permute-start.7 = (bf16[2,512,256]{2,1,0:T(8,128)(2,1)}, bf16[2,512,256]{2,1,0:T(8,128)(2,1)S(1)}, u32[]{:S(2)}, u32[]{:S(2)}) collective-permute-start(bf16[2,512,256]{2,1,0:T(8,128)(2,1)} %get-tuple-element.18.refs_0_), channel_id=1, source_target_pairs={{0,2},{1,3},{4,6},{5,7},{8,10},{9,11},{12,14},{13,15},{16,18},{17,... | collective-permute-start | bytes 1572872 | tf_op jit(solution)/shard_map/ppermute | solution.py:390
  16.4 0.0 copy-start.8
  16.4 9.3 %project.1.refs_0_ = bf16[2,512,256]{2,1,0:T(8,128)(2,1)} custom-call(bf16[512,8192]{1,0:T(8,128)(2,1)} %x_ref.1, f32[512,128]{1,0:T(8,128)} %get-tuple-element.17.scale_ref, f32[1,8192]{1,0:T(1,128)} %bitcast.3, bf16[8192,512]{1,0:T(8,128)(2,1)} %key_ref.1, bf16[8192,512]{1,0:T(8,128)(2,1)} %value_ref.1), custom_call_target="tpu_custom_call" | custom-call | flops 4294967296 | bytes 16777216 | tf_op jit(solution)/shard_map/project/pallas_call | solution.py:182
  25.8 1.3 %collective-permute-start.5 = (bf16[2,512,256]{2,1,0:T(8,128)(2,1)}, bf16[2,512,256]{2,1,0:T(8,128)(2,1)S(1)}, u32[]{:S(2)}, u32[]{:S(2)}) collective-permute-start(bf16[2,512,256]{2,1,0:T(8,128)(2,1)} %project.1.refs_0_), channel_id=1, source_target_pairs={{0,2},{1,3},{2,0},{3,1},{4,6},{5,7},{8,10},{9,11},{12,14},{13,15},... | collective-permute-start | bytes 1572872 | tf_op jit(solution)/shard_map/ppermute | solution.py:390
  27.1 1.3 %collective-permute-start = (bf16[2,512,256]{2,1,0:T(8,128)(2,1)}, bf16[2,512,256]{2,1,0:T(8,128)(2,1)S(1)}, u32[]{:S(2)}, u32[]{:S(2)}) collective-permute-start(bf16[2,512,256]{2,1,0:T(8,128)(2,1)} %project.1.refs_0_), channel_id=1, source_target_pairs={{0,4},{1,5},{2,6},{3,7},{4,8},{5,9},{6,10},{7,11},{8,12},{9,13},{1... | collective-permute-start | bytes 1572872 | tf_op jit(solution)/shard_map/ppermute | solution.py:390
  28.4 0.0 collective-permute-done.1.refs_1_
  28.4 0.0 copy-start.2
  28.4 1.3 %collective-permute-start.2 = (bf16[2,512,256]{2,1,0:T(8,128)(2,1)S(1)}, bf16[2,512,256]{2,1,0:T(8,128)(2,1)S(1)}, u32[]{:S(2)}, u32[]{:S(2)}) collective-permute-start(bf16[2,512,256]{2,1,0:T(8,128)(2,1)S(1)} %collective-permute-done.1.refs_1_), channel_id=1, source_target_pairs={{4,8},{5,9},{6,10},{7,11},{8,12},{9,13},{10,14},{11,15},{20,24},{2... | collective-permute-start | bytes 1572872 | tf_op jit(solution)/shard_map/ppermute | solution.py:390
  29.7 0.0 collective-permute-done.7.refs_4_
  29.7 0.0 copy-start.3
  29.7 2.9 %collective-permute-start.8 = (bf16[2,512,256]{2,1,0:T(8,128)(2,1)S(1)}, bf16[2,512,256]{2,1,0:T(8,128)(2,1)S(1)}, u32[]{:S(2)}, u32[]{:S(2)}) collective-permute-start(bf16[2,512,256]{2,1,0:T(8,128)(2,1)S(1)} %collective-permute-done.1.refs_1_), channel_id=1, source_target_pairs={{4,6},{5,7},{6,4},{7,5},{8,10},{9,11},{10,8},{11,9},{12,14},{13,15... | collective-permute-start | bytes 1572872 | tf_op jit(solution)/shard_map/ppermute | solution.py:390
  32.6 7.1 %collective-permute-done.5.refs_4_ = bf16[2,512,256]{2,1,0:T(8,128)(2,1)S(1)} collective-permute-done((bf16[2,512,256]{2,1,0:T(8,128)(2,1)}, bf16[2,512,256]{2,1,0:T(8,128)(2,1)S(1)}, u32[]{:S(2)}, u32[]{:S(2)}) %collective-permute-start.5) | collective-permute-done | bytes 524320 | tf_op jit(solution)/shard_map/ppermute | solution.py:390
  39.7 0.0 copy-start
  39.7 5.0 %collective-permute-done.refs_1_ = bf16[2,512,256]{2,1,0:T(8,128)(2,1)S(1)} collective-permute-done((bf16[2,512,256]{2,1,0:T(8,128)(2,1)}, bf16[2,512,256]{2,1,0:T(8,128)(2,1)S(1)}, u32[]{:S(2)}, u32[]{:S(2)}) %collective-permute-start) | collective-permute-done | bytes 524320 | tf_op jit(solution)/shard_map/ppermute | solution.py:390
  44.7 1.9 %collective-permute-start.6 = (bf16[2,512,256]{2,1,0:T(8,128)(2,1)S(1)}, bf16[2,512,256]{2,1,0:T(8,128)(2,1)S(1)}, u32[]{:S(2)}, u32[]{:S(2)}) collective-permute-start(bf16[2,512,256]{2,1,0:T(8,128)(2,1)S(1)} %collective-permute-done.refs_1_), channel_id=1, source_target_pairs={{4,6},{5,7},{6,4},{7,5},{8,10},{9,11},{10,8},{11,9},{12,14},{13,15... | collective-permute-start | bytes 1572872 | tf_op jit(solution)/shard_map/ppermute | solution.py:390
  46.6 7.9 %collective-permute-done.2.refs_2_ = bf16[2,512,256]{2,1,0:T(8,128)(2,1)S(1)} collective-permute-done((bf16[2,512,256]{2,1,0:T(8,128)(2,1)S(1)}, bf16[2,512,256]{2,1,0:T(8,128)(2,1)S(1)}, u32[]{:S(2)}, u32[]{:S(2)}) %collective-permute-start.2) | collective-permute-done | bytes 524320 | tf_op jit(solution)/shard_map/ppermute | solution.py:390
  54.4 1.3 %collective-permute-start.11 = (bf16[2,512,256]{2,1,0:T(8,128)(2,1)S(1)}, bf16[2,512,256]{2,1,0:T(8,128)(2,1)}, u32[]{:S(2)}, u32[]{:S(2)}) collective-permute-start(bf16[2,512,256]{2,1,0:T(8,128)(2,1)S(1)} %collective-permute-done.2.refs_2_), channel_id=1, source_target_pairs={{8,12},{9,13},{10,14},{11,15},{24,28},{25,29},{26,30},{27,31}} | collective-permute-start | bytes 1572872 | tf_op jit(solution)/shard_map/ppermute | solution.py:390
  55.7 1.3 %collective-permute-start.3 = (bf16[2,512,256]{2,1,0:T(8,128)(2,1)S(1)}, bf16[2,512,256]{2,1,0:T(8,128)(2,1)}, u32[]{:S(2)}, u32[]{:S(2)}) collective-permute-start(bf16[2,512,256]{2,1,0:T(8,128)(2,1)S(1)} %collective-permute-done.refs_1_), channel_id=1, source_target_pairs={{4,8},{5,9},{6,10},{7,11},{8,12},{9,13},{10,14},{11,15},{20,24},{2... | collective-permute-start | bytes 1572872 | tf_op jit(solution)/shard_map/ppermute | solution.py:390
  57.0 0.0 collective-permute-done.8.refs_5_
  57.0 0.0 copy-start.6
  57.1 1.9 %collective-permute-start.9 = (bf16[2,512,256]{2,1,0:T(8,128)(2,1)S(1)}, bf16[2,512,256]{2,1,0:T(8,128)(2,1)S(1)}, u32[]{:S(2)}, u32[]{:S(2)}) collective-permute-start(bf16[2,512,256]{2,1,0:T(8,128)(2,1)S(1)} %collective-permute-done.2.refs_2_), channel_id=1, source_target_pairs={{8,10},{9,11},{10,8},{11,9},{12,14},{13,15},{14,12},{15,13},{24,26... | collective-permute-start | bytes 1572872 | tf_op jit(solution)/shard_map/ppermute | solution.py:390
  59.0 3.1 %collective-permute-done.6.refs_5_ = bf16[2,512,256]{2,1,0:T(8,128)(2,1)S(1)} collective-permute-done((bf16[2,512,256]{2,1,0:T(8,128)(2,1)S(1)}, bf16[2,512,256]{2,1,0:T(8,128)(2,1)S(1)}, u32[]{:S(2)}, u32[]{:S(2)}) %collective-permute-start.6) | collective-permute-done | bytes 524320 | tf_op jit(solution)/shard_map/ppermute | solution.py:390
  62.1 9.2 %collective-permute-done.11.refs_3_ = bf16[2,512,256]{2,1,0:T(8,128)(2,1)} collective-permute-done((bf16[2,512,256]{2,1,0:T(8,128)(2,1)S(1)}, bf16[2,512,256]{2,1,0:T(8,128)(2,1)}, u32[]{:S(2)}, u32[]{:S(2)}) %collective-permute-start.11) | collective-permute-done | bytes 524320 | tf_op jit(solution)/shard_map/ppermute | solution.py:390
  71.3 1.9 %collective-permute-start.13 = (bf16[2,512,256]{2,1,0:T(8,128)(2,1)}, bf16[2,512,256]{2,1,0:T(8,128)(2,1)}, u32[]{:S(2)}, u32[]{:S(2)}) collective-permute-start(bf16[2,512,256]{2,1,0:T(8,128)(2,1)} %collective-permute-done.11.refs_3_), channel_id=1, source_target_pairs={{12,14},{13,15},{14,12},{15,13},{28,30},{29,31},{30,28},{31,29}} | collective-permute-start | bytes 1572872 | tf_op jit(solution)/shard_map/ppermute | solution.py:390
  73.2 6.9 %collective-permute-done.3.refs_2_ = bf16[2,512,256]{2,1,0:T(8,128)(2,1)} collective-permute-done((bf16[2,512,256]{2,1,0:T(8,128)(2,1)S(1)}, bf16[2,512,256]{2,1,0:T(8,128)(2,1)}, u32[]{:S(2)}, u32[]{:S(2)}) %collective-permute-start.3) | collective-permute-done | bytes 524320 | tf_op jit(solution)/shard_map/ppermute | solution.py:390
  80.1 1.3 %collective-permute-start.4 = (bf16[2,512,256]{2,1,0:T(8,128)(2,1)}, bf16[2,512,256]{2,1,0:T(8,128)(2,1)}, u32[]{:S(2)}, u32[]{:S(2)}) collective-permute-start(bf16[2,512,256]{2,1,0:T(8,128)(2,1)} %collective-permute-done.3.refs_2_), channel_id=1, source_target_pairs={{8,12},{9,13},{10,14},{11,15},{24,28},{25,29},{26,30},{27,31}} | collective-permute-start | bytes 1572872 | tf_op jit(solution)/shard_map/ppermute | solution.py:390
  81.4 1.3 %collective-permute-start.12 = (bf16[2,512,256]{2,1,0:T(8,128)(2,1)S(1)}, bf16[2,512,256]{2,1,0:T(8,128)(2,1)}, u32[]{:S(2)}, u32[]{:S(2)}) collective-permute-start(bf16[2,512,256]{2,1,0:T(8,128)(2,1)S(1)} %collective-permute-done.5.refs_4_), channel_id=1, source_target_pairs={{0,12},{1,13},{2,14},{3,15},{16,28},{17,29},{18,30},{19,31}} | collective-permute-start | bytes 1572872 | tf_op jit(solution)/shard_map/ppermute | solution.py:390
  82.7 0.0 collective-permute-done.9.refs_6_
  82.7 0.0 copy-done.6
  82.8 0.0 copy-start.7
  82.8 1.9 %collective-permute-start.10 = (bf16[2,512,256]{2,1,0:T(8,128)(2,1)}, bf16[2,512,256]{2,1,0:T(8,128)(2,1)}, u32[]{:S(2)}, u32[]{:S(2)}) collective-permute-start(bf16[2,512,256]{2,1,0:T(8,128)(2,1)} %collective-permute-done.3.refs_2_), channel_id=1, source_target_pairs={{8,10},{9,11},{10,8},{11,9},{12,14},{13,15},{14,12},{15,13},{24,26... | collective-permute-start | bytes 1572872 | tf_op jit(solution)/shard_map/ppermute | solution.py:390
  84.7 0.0 copy-done.7
  84.7 0.0 copy-done.8
  84.7 0.6 fusion.1.slot_ref
  85.3 0.0 collective-permute-done.13.refs_7_
  85.3 0.0 copy-done.2
  85.3 0.0 copy-done.3
  85.4 0.0 copy-done.5
  85.4 9.7 %attention.2.refs_8_ = bf16[512,4096]{1,0:T(8,128)(2,1)} custom-call(s32[8,7]{1,0:T(8,128)} %fusion.1.slot_ref, s32[8,7]{1,0:T(8,128)} %cut_ref.3, s32[1]{0:T(128)} %bitcast.odd_ref, bf16[512,4096]{1,0:T(8,128)(2,1)} %q_hbm.3, bf16[2,512,256]{2,1,0:T(8,128)(2,1)} %get-tuple-element.18.refs_0_, bf16[2,512,256]{2,1,0:T(8,128)(2,1)} %copy-done.2, ...), custom_call_target="tpu_custom_call" | custom-call | flops 2147483648 | bytes 8388608 | tf_op jit(solution)/shard_map/attention/pallas_call | solution.py:329
  95.1 10.0 %collective-permute-done.4.refs_3_ = bf16[2,512,256]{2,1,0:T(8,128)(2,1)} collective-permute-done((bf16[2,512,256]{2,1,0:T(8,128)(2,1)}, bf16[2,512,256]{2,1,0:T(8,128)(2,1)}, u32[]{:S(2)}, u32[]{:S(2)}) %collective-permute-start.4) | collective-permute-done | bytes 524320 | tf_op jit(solution)/shard_map/ppermute | solution.py:390
  105.1 0.0 collective-permute-done.12.refs_7_
  105.1 0.0 collective-permute-done.10.refs_6_
  105.1 0.0 copy-done
  105.1 0.0 copy-done.1
  105.2 0.0 copy-done.4
  105.2 9.7 %attention.3 = bf16[512,4096]{1,0:T(8,128)(2,1)} custom-call(s32[8,7]{1,0:T(8,128)} %fusion.1.slot_ref, s32[8,7]{1,0:T(8,128)} %cut_ref.3, s32[1]{0:T(128)} %bitcast.odd_ref, bf16[512,4096]{1,0:T(8,128)(2,1)} %q_hbm.3, bf16[2,512,256]{2,1,0:T(8,128)(2,1)} %project.1.refs_0_, bf16[2,512,256]{2,1,0:T(8,128)(2,1)} %copy-done.1, ...), custom_call_target="tpu_custom_call", output_to_operand_aliasing={{}: (12, {})} | custom-call | flops 2147483648 | bytes 8388608 | tf_op jit(solution)/shard_map/attention/pallas_call | solution.py:329
  (3 shorter events, 0.0 us)
Async XLA Ops:
  11.7 16.7 %collective-permute-start.1 = (bf16[2,512,256]{2,1,0:T(8,128)(2,1)}, bf16[2,512,256]{2,1,0:T(8,128)(2,1)S(1)}, u32[]{:S(2)}, u32[]{:S(2)}) collective-permute-start(bf16[2,512,256]{2,1,0:T(8,128)(2,1)} %get-tuple-element.18.refs_0_), channel_id=1, source_target_pairs={{0,4},{1,5},{2,6},{3,7},{4,8},{5,9},{6,10},{7,11},{8,12},{9,13},{1... | collective-permute-start | bytes 1572872 | tf_op jit(solution)/shard_map/ppermute | solution.py:390
  13.0 16.8 %collective-permute-start.7 = (bf16[2,512,256]{2,1,0:T(8,128)(2,1)}, bf16[2,512,256]{2,1,0:T(8,128)(2,1)S(1)}, u32[]{:S(2)}, u32[]{:S(2)}) collective-permute-start(bf16[2,512,256]{2,1,0:T(8,128)(2,1)} %get-tuple-element.18.refs_0_), channel_id=1, source_target_pairs={{0,2},{1,3},{4,6},{5,7},{8,10},{9,11},{12,14},{13,15},{16,18},{17,... | collective-permute-start | bytes 1572872 | tf_op jit(solution)/shard_map/ppermute | solution.py:390
  16.4 68.3 %copy-start.8 = (s32[8,7]{1,0:T(8,128)S(1)}, s32[8,7]{1,0:T(8,128)}, u32[]{:S(2)}) copy-start(s32[8,7]{1,0:T(8,128)} %param.12) | copy-start | bytes 676
  25.8 13.9 %collective-permute-start.5 = (bf16[2,512,256]{2,1,0:T(8,128)(2,1)}, bf16[2,512,256]{2,1,0:T(8,128)(2,1)S(1)}, u32[]{:S(2)}, u32[]{:S(2)}) collective-permute-start(bf16[2,512,256]{2,1,0:T(8,128)(2,1)} %project.1.refs_0_), channel_id=1, source_target_pairs={{0,2},{1,3},{2,0},{3,1},{4,6},{5,7},{8,10},{9,11},{12,14},{13,15},... | collective-permute-start | bytes 1572872 | tf_op jit(solution)/shard_map/ppermute | solution.py:390
  27.1 17.6 %collective-permute-start = (bf16[2,512,256]{2,1,0:T(8,128)(2,1)}, bf16[2,512,256]{2,1,0:T(8,128)(2,1)S(1)}, u32[]{:S(2)}, u32[]{:S(2)}) collective-permute-start(bf16[2,512,256]{2,1,0:T(8,128)(2,1)} %project.1.refs_0_), channel_id=1, source_target_pairs={{0,4},{1,5},{2,6},{3,7},{4,8},{5,9},{6,10},{7,11},{8,12},{9,13},{1... | collective-permute-start | bytes 1572872 | tf_op jit(solution)/shard_map/ppermute | solution.py:390
  28.4 56.9 %copy-start.2 = (bf16[2,512,256]{2,1,0:T(8,128)(2,1)}, bf16[2,512,256]{2,1,0:T(8,128)(2,1)S(1)}, u32[]{:S(2)}) copy-start(bf16[2,512,256]{2,1,0:T(8,128)(2,1)S(1)} %collective-permute-done.1.refs_1_) | copy-start | bytes 1572868
  28.4 26.0 %collective-permute-start.2 = (bf16[2,512,256]{2,1,0:T(8,128)(2,1)S(1)}, bf16[2,512,256]{2,1,0:T(8,128)(2,1)S(1)}, u32[]{:S(2)}, u32[]{:S(2)}) collective-permute-start(bf16[2,512,256]{2,1,0:T(8,128)(2,1)S(1)} %collective-permute-done.1.refs_1_), channel_id=1, source_target_pairs={{4,8},{5,9},{6,10},{7,11},{8,12},{9,13},{10,14},{11,15},{20,24},{2... | collective-permute-start | bytes 1572872 | tf_op jit(solution)/shard_map/ppermute | solution.py:390
  29.7 55.6 %copy-start.3 = (bf16[2,512,256]{2,1,0:T(8,128)(2,1)}, bf16[2,512,256]{2,1,0:T(8,128)(2,1)S(1)}, u32[]{:S(2)}) copy-start(bf16[2,512,256]{2,1,0:T(8,128)(2,1)S(1)} %collective-permute-done.7.refs_4_) | copy-start | bytes 1572868
  29.7 27.3 %collective-permute-start.8 = (bf16[2,512,256]{2,1,0:T(8,128)(2,1)S(1)}, bf16[2,512,256]{2,1,0:T(8,128)(2,1)S(1)}, u32[]{:S(2)}, u32[]{:S(2)}) collective-permute-start(bf16[2,512,256]{2,1,0:T(8,128)(2,1)S(1)} %collective-permute-done.1.refs_1_), channel_id=1, source_target_pairs={{4,6},{5,7},{6,4},{7,5},{8,10},{9,11},{10,8},{11,9},{12,14},{13,15... | collective-permute-start | bytes 1572872 | tf_op jit(solution)/shard_map/ppermute | solution.py:390
  39.7 65.4 %copy-start = (bf16[2,512,256]{2,1,0:T(8,128)(2,1)}, bf16[2,512,256]{2,1,0:T(8,128)(2,1)S(1)}, u32[]{:S(2)}) copy-start(bf16[2,512,256]{2,1,0:T(8,128)(2,1)S(1)} %collective-permute-done.5.refs_4_) | copy-start | bytes 1572868
  44.7 60.5 %copy-start.1 = (bf16[2,512,256]{2,1,0:T(8,128)(2,1)}, bf16[2,512,256]{2,1,0:T(8,128)(2,1)S(1)}, u32[]{:S(2)}) copy-start(bf16[2,512,256]{2,1,0:T(8,128)(2,1)S(1)} %collective-permute-done.refs_1_) | copy-start | bytes 1572868
  44.7 17.4 %collective-permute-start.6 = (bf16[2,512,256]{2,1,0:T(8,128)(2,1)S(1)}, bf16[2,512,256]{2,1,0:T(8,128)(2,1)S(1)}, u32[]{:S(2)}, u32[]{:S(2)}) collective-permute-start(bf16[2,512,256]{2,1,0:T(8,128)(2,1)S(1)} %collective-permute-done.refs_1_), channel_id=1, source_target_pairs={{4,6},{5,7},{6,4},{7,5},{8,10},{9,11},{10,8},{11,9},{12,14},{13,15... | collective-permute-start | bytes 1572872 | tf_op jit(solution)/shard_map/ppermute | solution.py:390
  54.4 30.9 %copy-start.5 = (bf16[2,512,256]{2,1,0:T(8,128)(2,1)}, bf16[2,512,256]{2,1,0:T(8,128)(2,1)S(1)}, u32[]{:S(2)}) copy-start(bf16[2,512,256]{2,1,0:T(8,128)(2,1)S(1)} %collective-permute-done.2.refs_2_) | copy-start | bytes 1572868
  54.4 16.8 %collective-permute-start.11 = (bf16[2,512,256]{2,1,0:T(8,128)(2,1)S(1)}, bf16[2,512,256]{2,1,0:T(8,128)(2,1)}, u32[]{:S(2)}, u32[]{:S(2)}) collective-permute-start(bf16[2,512,256]{2,1,0:T(8,128)(2,1)S(1)} %collective-permute-done.2.refs_2_), channel_id=1, source_target_pairs={{8,12},{9,13},{10,14},{11,15},{24,28},{25,29},{26,30},{27,31}} | collective-permute-start | bytes 1572872 | tf_op jit(solution)/shard_map/ppermute | solution.py:390
  55.7 24.4 %collective-permute-start.3 = (bf16[2,512,256]{2,1,0:T(8,128)(2,1)S(1)}, bf16[2,512,256]{2,1,0:T(8,128)(2,1)}, u32[]{:S(2)}, u32[]{:S(2)}) collective-permute-start(bf16[2,512,256]{2,1,0:T(8,128)(2,1)S(1)} %collective-permute-done.refs_1_), channel_id=1, source_target_pairs={{4,8},{5,9},{6,10},{7,11},{8,12},{9,13},{10,14},{11,15},{20,24},{2... | collective-permute-start | bytes 1572872 | tf_op jit(solution)/shard_map/ppermute | solution.py:390
  57.0 25.7 %copy-start.6 = (bf16[2,512,256]{2,1,0:T(8,128)(2,1)}, bf16[2,512,256]{2,1,0:T(8,128)(2,1)S(1)}, u32[]{:S(2)}) copy-start(bf16[2,512,256]{2,1,0:T(8,128)(2,1)S(1)} %collective-permute-done.8.refs_5_) | copy-start | bytes 1572868
  57.1 25.7 %collective-permute-start.9 = (bf16[2,512,256]{2,1,0:T(8,128)(2,1)S(1)}, bf16[2,512,256]{2,1,0:T(8,128)(2,1)S(1)}, u32[]{:S(2)}, u32[]{:S(2)}) collective-permute-start(bf16[2,512,256]{2,1,0:T(8,128)(2,1)S(1)} %collective-permute-done.2.refs_2_), channel_id=1, source_target_pairs={{8,10},{9,11},{10,8},{11,9},{12,14},{13,15},{14,12},{15,13},{24,26... | collective-permute-start | bytes 1572872 | tf_op jit(solution)/shard_map/ppermute | solution.py:390
  62.1 43.1 %copy-start.4 = (bf16[2,512,256]{2,1,0:T(8,128)(2,1)}, bf16[2,512,256]{2,1,0:T(8,128)(2,1)S(1)}, u32[]{:S(2)}) copy-start(bf16[2,512,256]{2,1,0:T(8,128)(2,1)S(1)} %collective-permute-done.6.refs_5_) | copy-start | bytes 1572868
  71.3 14.0 %collective-permute-start.13 = (bf16[2,512,256]{2,1,0:T(8,128)(2,1)}, bf16[2,512,256]{2,1,0:T(8,128)(2,1)}, u32[]{:S(2)}, u32[]{:S(2)}) collective-permute-start(bf16[2,512,256]{2,1,0:T(8,128)(2,1)} %collective-permute-done.11.refs_3_), channel_id=1, source_target_pairs={{12,14},{13,15},{14,12},{15,13},{28,30},{29,31},{30,28},{31,29}} | collective-permute-start | bytes 1572872 | tf_op jit(solution)/shard_map/ppermute | solution.py:390
  80.1 25.0 %collective-permute-start.4 = (bf16[2,512,256]{2,1,0:T(8,128)(2,1)}, bf16[2,512,256]{2,1,0:T(8,128)(2,1)}, u32[]{:S(2)}, u32[]{:S(2)}) collective-permute-start(bf16[2,512,256]{2,1,0:T(8,128)(2,1)} %collective-permute-done.3.refs_2_), channel_id=1, source_target_pairs={{8,12},{9,13},{10,14},{11,15},{24,28},{25,29},{26,30},{27,31}} | collective-permute-start | bytes 1572872 | tf_op jit(solution)/shard_map/ppermute | solution.py:390
  81.4 23.7 %collective-permute-start.12 = (bf16[2,512,256]{2,1,0:T(8,128)(2,1)S(1)}, bf16[2,512,256]{2,1,0:T(8,128)(2,1)}, u32[]{:S(2)}, u32[]{:S(2)}) collective-permute-start(bf16[2,512,256]{2,1,0:T(8,128)(2,1)S(1)} %collective-permute-done.5.refs_4_), channel_id=1, source_target_pairs={{0,12},{1,13},{2,14},{3,15},{16,28},{17,29},{18,30},{19,31}} | collective-permute-start | bytes 1572872 | tf_op jit(solution)/shard_map/ppermute | solution.py:390
  82.8 1.9 %copy-start.7 = (bf16[2,512,256]{2,1,0:T(8,128)(2,1)}, bf16[2,512,256]{2,1,0:T(8,128)(2,1)S(1)}, u32[]{:S(2)}) copy-start(bf16[2,512,256]{2,1,0:T(8,128)(2,1)S(1)} %collective-permute-done.9.refs_6_) | copy-start | bytes 1572868
  82.8 22.4 %collective-permute-start.10 = (bf16[2,512,256]{2,1,0:T(8,128)(2,1)}, bf16[2,512,256]{2,1,0:T(8,128)(2,1)}, u32[]{:S(2)}, u32[]{:S(2)}) collective-permute-start(bf16[2,512,256]{2,1,0:T(8,128)(2,1)} %collective-permute-done.3.refs_2_), channel_id=1, source_target_pairs={{8,10},{9,11},{10,8},{11,9},{12,14},{13,15},{14,12},{15,13},{24,26... | collective-permute-start | bytes 1572872 | tf_op jit(solution)/shard_map/ppermute | solution.py:390

commit v21 on v20

--- a/solution.py
+++ b/solution.py
@@ -12,7 +12,7 @@
 MASKED = -1e30
 MIB = 1024 * 1024
 CHUNKS = 4
-LOADS = 8
+LOADS = 16
 UNITS = 2
 BLOCKS_PER_STEP = 8
 
@@ -70,7 +70,7 @@
     def square(c, carry):
         load_x(c).wait()
 
-        @pl.when(c == loads - 2)
+        @pl.when(c == loads - 4)
         def _():
             for copy in load_weights(0):
                 copy.start()
@@ -102,11 +102,7 @@
             x = x_scr[:, cols].astype(jnp.float32)
             parts.append((x * inverse * gain_ref[:, cols]).astype(jnp.bfloat16))
         normed = jnp.concatenate(parts, axis=1)
-        for part in range(2):
-            cols = slice(part * width, (part + 1) * width)
-            acc_scr[:, cols] += jnp.dot(
-                normed, weight_scr[c, :, cols], preferred_element_type=jnp.float32
-            )
+        acc_scr[...] += jnp.dot(normed, weight_scr[c], preferred_element_type=jnp.float32)
         return carry
 
     lax.fori_loop(0, chunks, multiply, 0)

time: 115 us -> 115 us (level)
  no operation moved by 1% of the time
where the time goes in v21:
time: 115 us
  waiting for transfers between devices  49.2 us (43%)
  Pallas kernels  40.4 us (35%)
  starting transfers between devices  24.3 us (21%)
    ppermute x14, waiting for transfers between devices, step(): moved[key, s, unit] = lax.ppermute(array, 'node', pairs)  49.2 us
    ppermute x14, starting transfers between devices, step(): moved[key, s, unit] = lax.ppermute(array, 'node', pairs)  24.3 us
    pallas_call x2, Pallas kernels, attention(): pl.pallas_call(functools.partial(attention_kernel, block, unit, near), in...  19.4 us
    pallas_call x1, Pallas kernels, norm_project(): pl.pallas_call(norm_project_kernel, in_specs=[held, whole, held, held], o...  11.6 us
    pallas_call x1, Pallas kernels, project(): pl.pallas_call(project_kernel, grid=(CHUNKS,), in_specs=[pl.BlockSpec((ro...  9.35 us
  transfers between devices with their start and end apart: 14, of which 7 were waited for; matrix products, arithmetic and copies ran while one was open for 1% of the time, Pallas kernels for 17%

profile of v21, /device:TPU:24, one launch (start us, length us, event | category | flops | bytes accessed | tf_op | source)
XLA Modules:
  0.0 114.8 jit_solution(15348223995049957005)
XLA Ops:
  0.0 11.6 %norm_project.1 = (f32[512,128]{1,0:T(8,128)}, bf16[2,512,256]{2,1,0:T(8,128)(2,1)}) custom-call(bf16[512,8192]{1,0:T(8,128)(2,1)} %x_ref.1, f32[1,8192]{1,0:T(1,128)} %bitcast.2, bf16[8192,512]{1,0:T(8,128)(2,1)} %key_ref.1, bf16[8192,512]{1,0:T(8,128)(2,1)} %value_ref.1), custom_call_target="tpu_custom_call" | custom-call | flops 4294967296 | bytes 16777216 | tf_op jit(solution)/shard_map/norm_project/pallas_call | solution.py:127
  11.6 1.3 %collective-permute-start.1 = (bf16[2,512,256]{2,1,0:T(8,128)(2,1)}, bf16[2,512,256]{2,1,0:T(8,128)(2,1)S(1)}, u32[]{:S(2)}, u32[]{:S(2)}) collective-permute-start(bf16[2,512,256]{2,1,0:T(8,128)(2,1)} %get-tuple-element.18.refs_0_), channel_id=1, source_target_pairs={{0,4},{1,5},{2,6},{3,7},{4,8},{5,9},{6,10},{7,11},{8,12},{9,13},{1... | collective-permute-start | bytes 1572872 | tf_op jit(solution)/shard_map/ppermute | solution.py:386
  12.9 3.5 %collective-permute-start.7 = (bf16[2,512,256]{2,1,0:T(8,128)(2,1)}, bf16[2,512,256]{2,1,0:T(8,128)(2,1)S(1)}, u32[]{:S(2)}, u32[]{:S(2)}) collective-permute-start(bf16[2,512,256]{2,1,0:T(8,128)(2,1)} %get-tuple-element.18.refs_0_), channel_id=1, source_target_pairs={{0,2},{1,3},{4,6},{5,7},{8,10},{9,11},{12,14},{13,15},{16,18},{17,... | collective-permute-start | bytes 1572872 | tf_op jit(solution)/shard_map/ppermute | solution.py:386
  16.3 0.0 copy-start.8
  16.4 9.3 %project.1.refs_0_ = bf16[2,512,256]{2,1,0:T(8,128)(2,1)} custom-call(bf16[512,8192]{1,0:T(8,128)(2,1)} %x_ref.1, f32[512,128]{1,0:T(8,128)} %get-tuple-element.17.scale_ref, f32[1,8192]{1,0:T(1,128)} %bitcast.3, bf16[8192,512]{1,0:T(8,128)(2,1)} %key_ref.1, bf16[8192,512]{1,0:T(8,128)(2,1)} %value_ref.1), custom_call_target="tpu_custom_call" | custom-call | flops 4294967296 | bytes 16777216 | tf_op jit(solution)/shard_map/project/pallas_call | solution.py:178
  25.7 1.3 %collective-permute-start.5 = (bf16[2,512,256]{2,1,0:T(8,128)(2,1)}, bf16[2,512,256]{2,1,0:T(8,128)(2,1)S(1)}, u32[]{:S(2)}, u32[]{:S(2)}) collective-permute-start(bf16[2,512,256]{2,1,0:T(8,128)(2,1)} %project.1.refs_0_), channel_id=1, source_target_pairs={{0,2},{1,3},{2,0},{3,1},{4,6},{5,7},{8,10},{9,11},{12,14},{13,15},... | collective-permute-start | bytes 1572872 | tf_op jit(solution)/shard_map/ppermute | solution.py:386
  27.0 1.3 %collective-permute-start = (bf16[2,512,256]{2,1,0:T(8,128)(2,1)}, bf16[2,512,256]{2,1,0:T(8,128)(2,1)S(1)}, u32[]{:S(2)}, u32[]{:S(2)}) collective-permute-start(bf16[2,512,256]{2,1,0:T(8,128)(2,1)} %project.1.refs_0_), channel_id=1, source_target_pairs={{0,4},{1,5},{2,6},{3,7},{4,8},{5,9},{6,10},{7,11},{8,12},{9,13},{1... | collective-permute-start | bytes 1572872 | tf_op jit(solution)/shard_map/ppermute | solution.py:386
  28.3 0.0 collective-permute-done.1.refs_1_
  28.3 0.0 copy-start.2
  28.3 1.3 %collective-permute-start.2 = (bf16[2,512,256]{2,1,0:T(8,128)(2,1)S(1)}, bf16[2,512,256]{2,1,0:T(8,128)(2,1)S(1)}, u32[]{:S(2)}, u32[]{:S(2)}) collective-permute-start(bf16[2,512,256]{2,1,0:T(8,128)(2,1)S(1)} %collective-permute-done.1.refs_1_), channel_id=1, source_target_pairs={{4,8},{5,9},{6,10},{7,11},{8,12},{9,13},{10,14},{11,15},{20,24},{2... | collective-permute-start | bytes 1572872 | tf_op jit(solution)/shard_map/ppermute | solution.py:386
  29.6 0.0 collective-permute-done.7.refs_4_
  29.7 0.0 copy-start.3
  29.7 2.9 %collective-permute-start.8 = (bf16[2,512,256]{2,1,0:T(8,128)(2,1)S(1)}, bf16[2,512,256]{2,1,0:T(8,128)(2,1)S(1)}, u32[]{:S(2)}, u32[]{:S(2)}) collective-permute-start(bf16[2,512,256]{2,1,0:T(8,128)(2,1)S(1)} %collective-permute-done.1.refs_1_), channel_id=1, source_target_pairs={{4,6},{5,7},{6,4},{7,5},{8,10},{9,11},{10,8},{11,9},{12,14},{13,15... | collective-permute-start | bytes 1572872 | tf_op jit(solution)/shard_map/ppermute | solution.py:386
  32.6 7.1 %collective-permute-done.5.refs_4_ = bf16[2,512,256]{2,1,0:T(8,128)(2,1)S(1)} collective-permute-done((bf16[2,512,256]{2,1,0:T(8,128)(2,1)}, bf16[2,512,256]{2,1,0:T(8,128)(2,1)S(1)}, u32[]{:S(2)}, u32[]{:S(2)}) %collective-permute-start.5) | collective-permute-done | bytes 524320 | tf_op jit(solution)/shard_map/ppermute | solution.py:386
  39.6 0.0 copy-start
  39.6 5.0 %collective-permute-done.refs_1_ = bf16[2,512,256]{2,1,0:T(8,128)(2,1)S(1)} collective-permute-done((bf16[2,512,256]{2,1,0:T(8,128)(2,1)}, bf16[2,512,256]{2,1,0:T(8,128)(2,1)S(1)}, u32[]{:S(2)}, u32[]{:S(2)}) %collective-permute-start) | collective-permute-done | bytes 524320 | tf_op jit(solution)/shard_map/ppermute | solution.py:386
  44.6 1.9 %collective-permute-start.6 = (bf16[2,512,256]{2,1,0:T(8,128)(2,1)S(1)}, bf16[2,512,256]{2,1,0:T(8,128)(2,1)S(1)}, u32[]{:S(2)}, u32[]{:S(2)}) collective-permute-start(bf16[2,512,256]{2,1,0:T(8,128)(2,1)S(1)} %collective-permute-done.refs_1_), channel_id=1, source_target_pairs={{4,6},{5,7},{6,4},{7,5},{8,10},{9,11},{10,8},{11,9},{12,14},{13,15... | collective-permute-start | bytes 1572872 | tf_op jit(solution)/shard_map/ppermute | solution.py:386
  46.5 7.9 %collective-permute-done.2.refs_2_ = bf16[2,512,256]{2,1,0:T(8,128)(2,1)S(1)} collective-permute-done((bf16[2,512,256]{2,1,0:T(8,128)(2,1)S(1)}, bf16[2,512,256]{2,1,0:T(8,128)(2,1)S(1)}, u32[]{:S(2)}, u32[]{:S(2)}) %collective-permute-start.2) | collective-permute-done | bytes 524320 | tf_op jit(solution)/shard_map/ppermute | solution.py:386
  54.4 1.3 %collective-permute-start.11 = (bf16[2,512,256]{2,1,0:T(8,128)(2,1)S(1)}, bf16[2,512,256]{2,1,0:T(8,128)(2,1)}, u32[]{:S(2)}, u32[]{:S(2)}) collective-permute-start(bf16[2,512,256]{2,1,0:T(8,128)(2,1)S(1)} %collective-permute-done.2.refs_2_), channel_id=1, source_target_pairs={{8,12},{9,13},{10,14},{11,15},{24,28},{25,29},{26,30},{27,31}} | collective-permute-start | bytes 1572872 | tf_op jit(solution)/shard_map/ppermute | solution.py:386
  55.7 1.3 %collective-permute-start.3 = (bf16[2,512,256]{2,1,0:T(8,128)(2,1)S(1)}, bf16[2,512,256]{2,1,0:T(8,128)(2,1)}, u32[]{:S(2)}, u32[]{:S(2)}) collective-permute-start(bf16[2,512,256]{2,1,0:T(8,128)(2,1)S(1)} %collective-permute-done.refs_1_), channel_id=1, source_target_pairs={{4,8},{5,9},{6,10},{7,11},{8,12},{9,13},{10,14},{11,15},{20,24},{2... | collective-permute-start | bytes 1572872 | tf_op jit(solution)/shard_map/ppermute | solution.py:386
  57.0 0.0 collective-permute-done.8.refs_5_
  57.0 0.0 copy-start.6
  57.0 1.9 %collective-permute-start.9 = (bf16[2,512,256]{2,1,0:T(8,128)(2,1)S(1)}, bf16[2,512,256]{2,1,0:T(8,128)(2,1)S(1)}, u32[]{:S(2)}, u32[]{:S(2)}) collective-permute-start(bf16[2,512,256]{2,1,0:T(8,128)(2,1)S(1)} %collective-permute-done.2.refs_2_), channel_id=1, source_target_pairs={{8,10},{9,11},{10,8},{11,9},{12,14},{13,15},{14,12},{15,13},{24,26... | collective-permute-start | bytes 1572872 | tf_op jit(solution)/shard_map/ppermute | solution.py:386
  58.9 3.1 %collective-permute-done.6.refs_5_ = bf16[2,512,256]{2,1,0:T(8,128)(2,1)S(1)} collective-permute-done((bf16[2,512,256]{2,1,0:T(8,128)(2,1)S(1)}, bf16[2,512,256]{2,1,0:T(8,128)(2,1)S(1)}, u32[]{:S(2)}, u32[]{:S(2)}) %collective-permute-start.6) | collective-permute-done | bytes 524320 | tf_op jit(solution)/shard_map/ppermute | solution.py:386
  62.0 9.2 %collective-permute-done.11.refs_3_ = bf16[2,512,256]{2,1,0:T(8,128)(2,1)} collective-permute-done((bf16[2,512,256]{2,1,0:T(8,128)(2,1)S(1)}, bf16[2,512,256]{2,1,0:T(8,128)(2,1)}, u32[]{:S(2)}, u32[]{:S(2)}) %collective-permute-start.11) | collective-permute-done | bytes 524320 | tf_op jit(solution)/shard_map/ppermute | solution.py:386
  71.2 1.9 %collective-permute-start.13 = (bf16[2,512,256]{2,1,0:T(8,128)(2,1)}, bf16[2,512,256]{2,1,0:T(8,128)(2,1)}, u32[]{:S(2)}, u32[]{:S(2)}) collective-permute-start(bf16[2,512,256]{2,1,0:T(8,128)(2,1)} %collective-permute-done.11.refs_3_), channel_id=1, source_target_pairs={{12,14},{13,15},{14,12},{15,13},{28,30},{29,31},{30,28},{31,29}} | collective-permute-start | bytes 1572872 | tf_op jit(solution)/shard_map/ppermute | solution.py:386
  73.1 6.9 %collective-permute-done.3.refs_2_ = bf16[2,512,256]{2,1,0:T(8,128)(2,1)} collective-permute-done((bf16[2,512,256]{2,1,0:T(8,128)(2,1)S(1)}, bf16[2,512,256]{2,1,0:T(8,128)(2,1)}, u32[]{:S(2)}, u32[]{:S(2)}) %collective-permute-start.3) | collective-permute-done | bytes 524320 | tf_op jit(solution)/shard_map/ppermute | solution.py:386
  80.1 1.3 %collective-permute-start.4 = (bf16[2,512,256]{2,1,0:T(8,128)(2,1)}, bf16[2,512,256]{2,1,0:T(8,128)(2,1)}, u32[]{:S(2)}, u32[]{:S(2)}) collective-permute-start(bf16[2,512,256]{2,1,0:T(8,128)(2,1)} %collective-permute-done.3.refs_2_), channel_id=1, source_target_pairs={{8,12},{9,13},{10,14},{11,15},{24,28},{25,29},{26,30},{27,31}} | collective-permute-start | bytes 1572872 | tf_op jit(solution)/shard_map/ppermute | solution.py:386
  81.4 1.3 %collective-permute-start.12 = (bf16[2,512,256]{2,1,0:T(8,128)(2,1)S(1)}, bf16[2,512,256]{2,1,0:T(8,128)(2,1)}, u32[]{:S(2)}, u32[]{:S(2)}) collective-permute-start(bf16[2,512,256]{2,1,0:T(8,128)(2,1)S(1)} %collective-permute-done.5.refs_4_), channel_id=1, source_target_pairs={{0,12},{1,13},{2,14},{3,15},{16,28},{17,29},{18,30},{19,31}} | collective-permute-start | bytes 1572872 | tf_op jit(solution)/shard_map/ppermute | solution.py:386
  82.7 0.0 collective-permute-done.9.refs_6_
  82.7 0.0 copy-done.6
  82.7 0.0 copy-start.7
  82.7 1.9 %collective-permute-start.10 = (bf16[2,512,256]{2,1,0:T(8,128)(2,1)}, bf16[2,512,256]{2,1,0:T(8,128)(2,1)}, u32[]{:S(2)}, u32[]{:S(2)}) collective-permute-start(bf16[2,512,256]{2,1,0:T(8,128)(2,1)} %collective-permute-done.3.refs_2_), channel_id=1, source_target_pairs={{8,10},{9,11},{10,8},{11,9},{12,14},{13,15},{14,12},{15,13},{24,26... | collective-permute-start | bytes 1572872 | tf_op jit(solution)/shard_map/ppermute | solution.py:386
  84.6 0.0 copy-done.7
  84.7 0.0 copy-done.8
  84.7 0.6 fusion.1.slot_ref
  85.3 0.0 collective-permute-done.13.refs_7_
  85.3 0.0 copy-done.2
  85.3 0.0 copy-done.3
  85.3 0.0 copy-done.5
  85.3 9.7 %attention.2.refs_8_ = bf16[512,4096]{1,0:T(8,128)(2,1)} custom-call(s32[8,7]{1,0:T(8,128)} %fusion.1.slot_ref, s32[8,7]{1,0:T(8,128)} %cut_ref.3, s32[1]{0:T(128)} %bitcast.odd_ref, bf16[512,4096]{1,0:T(8,128)(2,1)} %q_hbm.3, bf16[2,512,256]{2,1,0:T(8,128)(2,1)} %get-tuple-element.18.refs_0_, bf16[2,512,256]{2,1,0:T(8,128)(2,1)} %copy-done.2, ...), custom_call_target="tpu_custom_call" | custom-call | flops 2147483648 | bytes 8388608 | tf_op jit(solution)/shard_map/attention/pallas_call | solution.py:325
  95.0 10.1 %collective-permute-done.4.refs_3_ = bf16[2,512,256]{2,1,0:T(8,128)(2,1)} collective-permute-done((bf16[2,512,256]{2,1,0:T(8,128)(2,1)}, bf16[2,512,256]{2,1,0:T(8,128)(2,1)}, u32[]{:S(2)}, u32[]{:S(2)}) %collective-permute-start.4) | collective-permute-done | bytes 524320 | tf_op jit(solution)/shard_map/ppermute | solution.py:386
  105.1 0.0 collective-permute-done.12.refs_7_
  105.1 0.0 collective-permute-done.10.refs_6_
  105.1 0.0 copy-done
  105.1 0.0 copy-done.1
  105.1 0.0 copy-done.4
  105.1 9.7 %attention.3 = bf16[512,4096]{1,0:T(8,128)(2,1)} custom-call(s32[8,7]{1,0:T(8,128)} %fusion.1.slot_ref, s32[8,7]{1,0:T(8,128)} %cut_ref.3, s32[1]{0:T(128)} %bitcast.odd_ref, bf16[512,4096]{1,0:T(8,128)(2,1)} %q_hbm.3, bf16[2,512,256]{2,1,0:T(8,128)(2,1)} %project.1.refs_0_, bf16[2,512,256]{2,1,0:T(8,128)(2,1)} %copy-done.1, ...), custom_call_target="tpu_custom_call", output_to_operand_aliasing={{}: (12, {})} | custom-call | flops 2147483648 | bytes 8388608 | tf_op jit(solution)/shard_map/attention/pallas_call | solution.py:325
  (3 shorter events, 0.0 us)
Async XLA Ops:
  11.6 16.7 %collective-permute-start.1 = (bf16[2,512,256]{2,1,0:T(8,128)(2,1)}, bf16[2,512,256]{2,1,0:T(8,128)(2,1)S(1)}, u32[]{:S(2)}, u32[]{:S(2)}) collective-permute-start(bf16[2,512,256]{2,1,0:T(8,128)(2,1)} %get-tuple-element.18.refs_0_), channel_id=1, source_target_pairs={{0,4},{1,5},{2,6},{3,7},{4,8},{5,9},{6,10},{7,11},{8,12},{9,13},{1... | collective-permute-start | bytes 1572872 | tf_op jit(solution)/shard_map/ppermute | solution.py:386
  12.9 16.8 %collective-permute-start.7 = (bf16[2,512,256]{2,1,0:T(8,128)(2,1)}, bf16[2,512,256]{2,1,0:T(8,128)(2,1)S(1)}, u32[]{:S(2)}, u32[]{:S(2)}) collective-permute-start(bf16[2,512,256]{2,1,0:T(8,128)(2,1)} %get-tuple-element.18.refs_0_), channel_id=1, source_target_pairs={{0,2},{1,3},{4,6},{5,7},{8,10},{9,11},{12,14},{13,15},{16,18},{17,... | collective-permute-start | bytes 1572872 | tf_op jit(solution)/shard_map/ppermute | solution.py:386
  16.3 68.3 %copy-start.8 = (s32[8,7]{1,0:T(8,128)S(1)}, s32[8,7]{1,0:T(8,128)}, u32[]{:S(2)}) copy-start(s32[8,7]{1,0:T(8,128)} %param.12) | copy-start | bytes 676
  25.7 13.9 %collective-permute-start.5 = (bf16[2,512,256]{2,1,0:T(8,128)(2,1)}, bf16[2,512,256]{2,1,0:T(8,128)(2,1)S(1)}, u32[]{:S(2)}, u32[]{:S(2)}) collective-permute-start(bf16[2,512,256]{2,1,0:T(8,128)(2,1)} %project.1.refs_0_), channel_id=1, source_target_pairs={{0,2},{1,3},{2,0},{3,1},{4,6},{5,7},{8,10},{9,11},{12,14},{13,15},... | collective-permute-start | bytes 1572872 | tf_op jit(solution)/shard_map/ppermute | solution.py:386
  27.0 17.6 %collective-permute-start = (bf16[2,512,256]{2,1,0:T(8,128)(2,1)}, bf16[2,512,256]{2,1,0:T(8,128)(2,1)S(1)}, u32[]{:S(2)}, u32[]{:S(2)}) collective-permute-start(bf16[2,512,256]{2,1,0:T(8,128)(2,1)} %project.1.refs_0_), channel_id=1, source_target_pairs={{0,4},{1,5},{2,6},{3,7},{4,8},{5,9},{6,10},{7,11},{8,12},{9,13},{1... | collective-permute-start | bytes 1572872 | tf_op jit(solution)/shard_map/ppermute | solution.py:386
  28.3 57.0 %copy-start.2 = (bf16[2,512,256]{2,1,0:T(8,128)(2,1)}, bf16[2,512,256]{2,1,0:T(8,128)(2,1)S(1)}, u32[]{:S(2)}) copy-start(bf16[2,512,256]{2,1,0:T(8,128)(2,1)S(1)} %collective-permute-done.1.refs_1_) | copy-start | bytes 1572868
  28.3 26.0 %collective-permute-start.2 = (bf16[2,512,256]{2,1,0:T(8,128)(2,1)S(1)}, bf16[2,512,256]{2,1,0:T(8,128)(2,1)S(1)}, u32[]{:S(2)}, u32[]{:S(2)}) collective-permute-start(bf16[2,512,256]{2,1,0:T(8,128)(2,1)S(1)} %collective-permute-done.1.refs_1_), channel_id=1, source_target_pairs={{4,8},{5,9},{6,10},{7,11},{8,12},{9,13},{10,14},{11,15},{20,24},{2... | collective-permute-start | bytes 1572872 | tf_op jit(solution)/shard_map/ppermute | solution.py:386
  29.7 55.6 %copy-start.3 = (bf16[2,512,256]{2,1,0:T(8,128)(2,1)}, bf16[2,512,256]{2,1,0:T(8,128)(2,1)S(1)}, u32[]{:S(2)}) copy-start(bf16[2,512,256]{2,1,0:T(8,128)(2,1)S(1)} %collective-permute-done.7.refs_4_) | copy-start | bytes 1572868
  29.7 27.3 %collective-permute-start.8 = (bf16[2,512,256]{2,1,0:T(8,128)(2,1)S(1)}, bf16[2,512,256]{2,1,0:T(8,128)(2,1)S(1)}, u32[]{:S(2)}, u32[]{:S(2)}) collective-permute-start(bf16[2,512,256]{2,1,0:T(8,128)(2,1)S(1)} %collective-permute-done.1.refs_1_), channel_id=1, source_target_pairs={{4,6},{5,7},{6,4},{7,5},{8,10},{9,11},{10,8},{11,9},{12,14},{13,15... | collective-permute-start | bytes 1572872 | tf_op jit(solution)/shard_map/ppermute | solution.py:386
  39.6 65.5 %copy-start = (bf16[2,512,256]{2,1,0:T(8,128)(2,1)}, bf16[2,512,256]{2,1,0:T(8,128)(2,1)S(1)}, u32[]{:S(2)}) copy-start(bf16[2,512,256]{2,1,0:T(8,128)(2,1)S(1)} %collective-permute-done.5.refs_4_) | copy-start | bytes 1572868
  44.6 60.5 %copy-start.1 = (bf16[2,512,256]{2,1,0:T(8,128)(2,1)}, bf16[2,512,256]{2,1,0:T(8,128)(2,1)S(1)}, u32[]{:S(2)}) copy-start(bf16[2,512,256]{2,1,0:T(8,128)(2,1)S(1)} %collective-permute-done.refs_1_) | copy-start | bytes 1572868
  44.6 17.4 %collective-permute-start.6 = (bf16[2,512,256]{2,1,0:T(8,128)(2,1)S(1)}, bf16[2,512,256]{2,1,0:T(8,128)(2,1)S(1)}, u32[]{:S(2)}, u32[]{:S(2)}) collective-permute-start(bf16[2,512,256]{2,1,0:T(8,128)(2,1)S(1)} %collective-permute-done.refs_1_), channel_id=1, source_target_pairs={{4,6},{5,7},{6,4},{7,5},{8,10},{9,11},{10,8},{11,9},{12,14},{13,15... | collective-permute-start | bytes 1572872 | tf_op jit(solution)/shard_map/ppermute | solution.py:386
  54.4 30.9 %copy-start.5 = (bf16[2,512,256]{2,1,0:T(8,128)(2,1)}, bf16[2,512,256]{2,1,0:T(8,128)(2,1)S(1)}, u32[]{:S(2)}) copy-start(bf16[2,512,256]{2,1,0:T(8,128)(2,1)S(1)} %collective-permute-done.2.refs_2_) | copy-start | bytes 1572868
  54.4 16.8 %collective-permute-start.11 = (bf16[2,512,256]{2,1,0:T(8,128)(2,1)S(1)}, bf16[2,512,256]{2,1,0:T(8,128)(2,1)}, u32[]{:S(2)}, u32[]{:S(2)}) collective-permute-start(bf16[2,512,256]{2,1,0:T(8,128)(2,1)S(1)} %collective-permute-done.2.refs_2_), channel_id=1, source_target_pairs={{8,12},{9,13},{10,14},{11,15},{24,28},{25,29},{26,30},{27,31}} | collective-permute-start | bytes 1572872 | tf_op jit(solution)/shard_map/ppermute | solution.py:386
  55.7 24.4 %collective-permute-start.3 = (bf16[2,512,256]{2,1,0:T(8,128)(2,1)S(1)}, bf16[2,512,256]{2,1,0:T(8,128)(2,1)}, u32[]{:S(2)}, u32[]{:S(2)}) collective-permute-start(bf16[2,512,256]{2,1,0:T(8,128)(2,1)S(1)} %collective-permute-done.refs_1_), channel_id=1, source_target_pairs={{4,8},{5,9},{6,10},{7,11},{8,12},{9,13},{10,14},{11,15},{20,24},{2... | collective-permute-start | bytes 1572872 | tf_op jit(solution)/shard_map/ppermute | solution.py:386
  57.0 25.7 %copy-start.6 = (bf16[2,512,256]{2,1,0:T(8,128)(2,1)}, bf16[2,512,256]{2,1,0:T(8,128)(2,1)S(1)}, u32[]{:S(2)}) copy-start(bf16[2,512,256]{2,1,0:T(8,128)(2,1)S(1)} %collective-permute-done.8.refs_5_) | copy-start | bytes 1572868
  57.0 25.7 %collective-permute-start.9 = (bf16[2,512,256]{2,1,0:T(8,128)(2,1)S(1)}, bf16[2,512,256]{2,1,0:T(8,128)(2,1)S(1)}, u32[]{:S(2)}, u32[]{:S(2)}) collective-permute-start(bf16[2,512,256]{2,1,0:T(8,128)(2,1)S(1)} %collective-permute-done.2.refs_2_), channel_id=1, source_target_pairs={{8,10},{9,11},{10,8},{11,9},{12,14},{13,15},{14,12},{15,13},{24,26... | collective-permute-start | bytes 1572872 | tf_op jit(solution)/shard_map/ppermute | solution.py:386
  62.0 43.1 %copy-start.4 = (bf16[2,512,256]{2,1,0:T(8,128)(2,1)}, bf16[2,512,256]{2,1,0:T(8,128)(2,1)S(1)}, u32[]{:S(2)}) copy-start(bf16[2,512,256]{2,1,0:T(8,128)(2,1)S(1)} %collective-permute-done.6.refs_5_) | copy-start | bytes 1572868
  71.2 14.1 %collective-permute-start.13 = (bf16[2,512,256]{2,1,0:T(8,128)(2,1)}, bf16[2,512,256]{2,1,0:T(8,128)(2,1)}, u32[]{:S(2)}, u32[]{:S(2)}) collective-permute-start(bf16[2,512,256]{2,1,0:T(8,128)(2,1)} %collective-permute-done.11.refs_3_), channel_id=1, source_target_pairs={{12,14},{13,15},{14,12},{15,13},{28,30},{29,31},{30,28},{31,29}} | collective-permute-start | bytes 1572872 | tf_op jit(solution)/shard_map/ppermute | solution.py:386
  80.1 25.0 %collective-permute-start.4 = (bf16[2,512,256]{2,1,0:T(8,128)(2,1)}, bf16[2,512,256]{2,1,0:T(8,128)(2,1)}, u32[]{:S(2)}, u32[]{:S(2)}) collective-permute-start(bf16[2,512,256]{2,1,0:T(8,128)(2,1)} %collective-permute-done.3.refs_2_), channel_id=1, source_target_pairs={{8,12},{9,13},{10,14},{11,15},{24,28},{25,29},{26,30},{27,31}} | collective-permute-start | bytes 1572872 | tf_op jit(solution)/shard_map/ppermute | solution.py:386
  81.4 23.7 %collective-permute-start.12 = (bf16[2,512,256]{2,1,0:T(8,128)(2,1)S(1)}, bf16[2,512,256]{2,1,0:T(8,128)(2,1)}, u32[]{:S(2)}, u32[]{:S(2)}) collective-permute-start(bf16[2,512,256]{2,1,0:T(8,128)(2,1)S(1)} %collective-permute-done.5.refs_4_), channel_id=1, source_target_pairs={{0,12},{1,13},{2,14},{3,15},{16,28},{17,29},{18,30},{19,31}} | collective-permute-start | bytes 1572872 | tf_op jit(solution)/shard_map/ppermute | solution.py:386
  82.7 1.9 %copy-start.7 = (bf16[2,512,256]{2,1,0:T(8,128)(2,1)}, bf16[2,512,256]{2,1,0:T(8,128)(2,1)S(1)}, u32[]{:S(2)}) copy-start(bf16[2,512,256]{2,1,0:T(8,128)(2,1)S(1)} %collective-permute-done.9.refs_6_) | copy-start | bytes 1572868
  82.7 22.4 %collective-permute-start.10 = (bf16[2,512,256]{2,1,0:T(8,128)(2,1)}, bf16[2,512,256]{2,1,0:T(8,128)(2,1)}, u32[]{:S(2)}, u32[]{:S(2)}) collective-permute-start(bf16[2,512,256]{2,1,0:T(8,128)(2,1)} %collective-permute-done.3.refs_2_), channel_id=1, source_target_pairs={{8,10},{9,11},{10,8},{11,9},{12,14},{13,15},{14,12},{15,13},{24,26... | collective-permute-start | bytes 1572872 | tf_op jit(solution)/shard_map/ppermute | solution.py:386

commit v22 on v21

--- a/solution.py
+++ b/solution.py
@@ -15,6 +15,7 @@
 LOADS = 16
 UNITS = 2
 BLOCKS_PER_STEP = 8
+STORED = 2
 
 
 PLAN = (
@@ -231,8 +232,11 @@
     def load_q(step):
         return pltpu.make_async_copy(place(q_hbm, step), q_scr.at[step], q_sem.at[step])
 
-    def store(step):
-        return pltpu.make_async_copy(out_scr.at[step], place(out_hbm, step), out_sem.at[step])
+    def store(step, part):
+        span = pl.ds(part * STORED * block, STORED * block)
+        return pltpu.make_async_copy(
+            out_scr.at[step, span], place(out_hbm, step).at[span], out_sem.at[step, part]
+        )
 
     for head in range(kv_heads):
         for copy in load_kv(head):
@@ -292,19 +296,24 @@
                 for copy in load_kv(head):
                     copy.wait()
 
+        def complete(local, scores, values):
+            finish(step, local, scores, values)
+            if local % STORED == STORED - 1:
+                store(step, local // STORED).start()
+
         waiting = None
         for local in range(BLOCKS_PER_STEP):
             scores, values = score(step, local)
             if waiting is not None:
-                finish(step, *waiting)
+                complete(*waiting)
             waiting = (local, scores, values)
-        finish(step, *waiting)
-        store(step).start()
+        complete(*waiting)
         return carry
 
     lax.fori_loop(0, steps, body, 0)
     for step in range(steps):
-        store(step).wait()
+        for part in range(BLOCKS_PER_STEP // STORED):
+            store(step, part).wait()
 
 
 def attention(slots, cuts, odd, queries, own, straight, crossed, unit, previous):
@@ -334,7 +343,7 @@
             pltpu.VMEM((steps, BLOCKS_PER_STEP * block, wide), jnp.bfloat16),
             pltpu.SemaphoreType.DMA((kv_heads, depth + 1)),
             pltpu.SemaphoreType.DMA((steps,)),
-            pltpu.SemaphoreType.DMA((steps,)),
+            pltpu.SemaphoreType.DMA((steps, BLOCKS_PER_STEP // STORED)),
         ],
         compiler_params=pltpu.CompilerParams(vmem_limit_bytes=57 * MIB),
         cost_estimate=pl.CostEstimate(

time: 115 us -> 115 us (level)
  transfers between devices with their start and end apart: 14 -> 14, of which waited for: 7 -> 7; matrix products, arithmetic and copies ran while one was open for 1% -> 1% of each run, Pallas kernels for 17% -> 16%
where the time goes in v22:
time: 115 us
  waiting for transfers between devices  49.4 us (43%)
  Pallas kernels  40 us (35%)
  starting transfers between devices  24.3 us (21%)
    ppermute x14, waiting for transfers between devices, step(): moved[key, s, unit] = lax.ppermute(array, 'node', pairs)  49.4 us
    ppermute x14, starting transfers between devices, step(): moved[key, s, unit] = lax.ppermute(array, 'node', pairs)  24.3 us
    pallas_call x2, Pallas kernels, attention(): pl.pallas_call(functools.partial(attention_kernel, block, unit, near), in...  19 us
    pallas_call x1, Pallas kernels, norm_project(): pl.pallas_call(norm_project_kernel, in_specs=[held, whole, held, held], o...  11.6 us
    pallas_call x1, Pallas kernels, project(): pl.pallas_call(project_kernel, grid=(CHUNKS,), in_specs=[pl.BlockSpec((ro...  9.35 us
  transfers between devices with their start and end apart: 14, of which 7 were waited for; matrix products, arithmetic and copies ran while one was open for 1% of the time, Pallas kernels for 16%

profile of v22, /device:TPU:24, one launch (start us, length us, event | category | flops | bytes accessed | tf_op | source)
XLA Modules:
  0.0 114.6 jit_solution(3911668974441622742)
XLA Ops:
  0.0 11.6 %norm_project.1 = (f32[512,128]{1,0:T(8,128)}, bf16[2,512,256]{2,1,0:T(8,128)(2,1)}) custom-call(bf16[512,8192]{1,0:T(8,128)(2,1)} %x_ref.1, f32[1,8192]{1,0:T(1,128)} %bitcast.2, bf16[8192,512]{1,0:T(8,128)(2,1)} %key_ref.1, bf16[8192,512]{1,0:T(8,128)(2,1)} %value_ref.1), custom_call_target="tpu_custom_call" | custom-call | flops 4294967296 | bytes 16777216 | tf_op jit(solution)/shard_map/norm_project/pallas_call | solution.py:128
  11.6 1.3 %collective-permute-start.1 = (bf16[2,512,256]{2,1,0:T(8,128)(2,1)}, bf16[2,512,256]{2,1,0:T(8,128)(2,1)S(1)}, u32[]{:S(2)}, u32[]{:S(2)}) collective-permute-start(bf16[2,512,256]{2,1,0:T(8,128)(2,1)} %get-tuple-element.18.refs_0_), channel_id=1, source_target_pairs={{0,4},{1,5},{2,6},{3,7},{4,8},{5,9},{6,10},{7,11},{8,12},{9,13},{1... | collective-permute-start | bytes 1572872 | tf_op jit(solution)/shard_map/ppermute | solution.py:395
  12.9 3.5 %collective-permute-start.7 = (bf16[2,512,256]{2,1,0:T(8,128)(2,1)}, bf16[2,512,256]{2,1,0:T(8,128)(2,1)S(1)}, u32[]{:S(2)}, u32[]{:S(2)}) collective-permute-start(bf16[2,512,256]{2,1,0:T(8,128)(2,1)} %get-tuple-element.18.refs_0_), channel_id=1, source_target_pairs={{0,2},{1,3},{4,6},{5,7},{8,10},{9,11},{12,14},{13,15},{16,18},{17,... | collective-permute-start | bytes 1572872 | tf_op jit(solution)/shard_map/ppermute | solution.py:395
  16.3 0.0 copy-start.8
  16.4 9.3 %project.1.refs_0_ = bf16[2,512,256]{2,1,0:T(8,128)(2,1)} custom-call(bf16[512,8192]{1,0:T(8,128)(2,1)} %x_ref.1, f32[512,128]{1,0:T(8,128)} %get-tuple-element.17.scale_ref, f32[1,8192]{1,0:T(1,128)} %bitcast.3, bf16[8192,512]{1,0:T(8,128)(2,1)} %key_ref.1, bf16[8192,512]{1,0:T(8,128)(2,1)} %value_ref.1), custom_call_target="tpu_custom_call" | custom-call | flops 4294967296 | bytes 16777216 | tf_op jit(solution)/shard_map/project/pallas_call | solution.py:179
  25.7 1.3 %collective-permute-start.5 = (bf16[2,512,256]{2,1,0:T(8,128)(2,1)}, bf16[2,512,256]{2,1,0:T(8,128)(2,1)S(1)}, u32[]{:S(2)}, u32[]{:S(2)}) collective-permute-start(bf16[2,512,256]{2,1,0:T(8,128)(2,1)} %project.1.refs_0_), channel_id=1, source_target_pairs={{0,2},{1,3},{2,0},{3,1},{4,6},{5,7},{8,10},{9,11},{12,14},{13,15},... | collective-permute-start | bytes 1572872 | tf_op jit(solution)/shard_map/ppermute | solution.py:395
  27.0 1.3 %collective-permute-start = (bf16[2,512,256]{2,1,0:T(8,128)(2,1)}, bf16[2,512,256]{2,1,0:T(8,128)(2,1)S(1)}, u32[]{:S(2)}, u32[]{:S(2)}) collective-permute-start(bf16[2,512,256]{2,1,0:T(8,128)(2,1)} %project.1.refs_0_), channel_id=1, source_target_pairs={{0,4},{1,5},{2,6},{3,7},{4,8},{5,9},{6,10},{7,11},{8,12},{9,13},{1... | collective-permute-start | bytes 1572872 | tf_op jit(solution)/shard_map/ppermute | solution.py:395
  28.3 0.0 collective-permute-done.1.refs_1_
  28.3 0.0 copy-start.2
  28.3 1.3 %collective-permute-start.2 = (bf16[2,512,256]{2,1,0:T(8,128)(2,1)S(1)}, bf16[2,512,256]{2,1,0:T(8,128)(2,1)S(1)}, u32[]{:S(2)}, u32[]{:S(2)}) collective-permute-start(bf16[2,512,256]{2,1,0:T(8,128)(2,1)S(1)} %collective-permute-done.1.refs_1_), channel_id=1, source_target_pairs={{4,8},{5,9},{6,10},{7,11},{8,12},{9,13},{10,14},{11,15},{20,24},{2... | collective-permute-start | bytes 1572872 | tf_op jit(solution)/shard_map/ppermute | solution.py:395
  29.6 0.0 collective-permute-done.7.refs_4_
  29.7 0.0 copy-start.3
  29.7 2.9 %collective-permute-start.8 = (bf16[2,512,256]{2,1,0:T(8,128)(2,1)S(1)}, bf16[2,512,256]{2,1,0:T(8,128)(2,1)S(1)}, u32[]{:S(2)}, u32[]{:S(2)}) collective-permute-start(bf16[2,512,256]{2,1,0:T(8,128)(2,1)S(1)} %collective-permute-done.1.refs_1_), channel_id=1, source_target_pairs={{4,6},{5,7},{6,4},{7,5},{8,10},{9,11},{10,8},{11,9},{12,14},{13,15... | collective-permute-start | bytes 1572872 | tf_op jit(solution)/shard_map/ppermute | solution.py:395
  32.6 7.1 %collective-permute-done.5.refs_4_ = bf16[2,512,256]{2,1,0:T(8,128)(2,1)S(1)} collective-permute-done((bf16[2,512,256]{2,1,0:T(8,128)(2,1)}, bf16[2,512,256]{2,1,0:T(8,128)(2,1)S(1)}, u32[]{:S(2)}, u32[]{:S(2)}) %collective-permute-start.5) | collective-permute-done | bytes 524320 | tf_op jit(solution)/shard_map/ppermute | solution.py:395
  39.6 0.0 copy-start
  39.6 5.0 %collective-permute-done.refs_1_ = bf16[2,512,256]{2,1,0:T(8,128)(2,1)S(1)} collective-permute-done((bf16[2,512,256]{2,1,0:T(8,128)(2,1)}, bf16[2,512,256]{2,1,0:T(8,128)(2,1)S(1)}, u32[]{:S(2)}, u32[]{:S(2)}) %collective-permute-start) | collective-permute-done | bytes 524320 | tf_op jit(solution)/shard_map/ppermute | solution.py:395
  44.6 1.9 %collective-permute-start.6 = (bf16[2,512,256]{2,1,0:T(8,128)(2,1)S(1)}, bf16[2,512,256]{2,1,0:T(8,128)(2,1)S(1)}, u32[]{:S(2)}, u32[]{:S(2)}) collective-permute-start(bf16[2,512,256]{2,1,0:T(8,128)(2,1)S(1)} %collective-permute-done.refs_1_), channel_id=1, source_target_pairs={{4,6},{5,7},{6,4},{7,5},{8,10},{9,11},{10,8},{11,9},{12,14},{13,15... | collective-permute-start | bytes 1572872 | tf_op jit(solution)/shard_map/ppermute | solution.py:395
  46.5 7.9 %collective-permute-done.2.refs_2_ = bf16[2,512,256]{2,1,0:T(8,128)(2,1)S(1)} collective-permute-done((bf16[2,512,256]{2,1,0:T(8,128)(2,1)S(1)}, bf16[2,512,256]{2,1,0:T(8,128)(2,1)S(1)}, u32[]{:S(2)}, u32[]{:S(2)}) %collective-permute-start.2) | collective-permute-done | bytes 524320 | tf_op jit(solution)/shard_map/ppermute | solution.py:395
  54.4 1.3 %collective-permute-start.11 = (bf16[2,512,256]{2,1,0:T(8,128)(2,1)S(1)}, bf16[2,512,256]{2,1,0:T(8,128)(2,1)}, u32[]{:S(2)}, u32[]{:S(2)}) collective-permute-start(bf16[2,512,256]{2,1,0:T(8,128)(2,1)S(1)} %collective-permute-done.2.refs_2_), channel_id=1, source_target_pairs={{8,12},{9,13},{10,14},{11,15},{24,28},{25,29},{26,30},{27,31}} | collective-permute-start | bytes 1572872 | tf_op jit(solution)/shard_map/ppermute | solution.py:395
  55.7 1.3 %collective-permute-start.3 = (bf16[2,512,256]{2,1,0:T(8,128)(2,1)S(1)}, bf16[2,512,256]{2,1,0:T(8,128)(2,1)}, u32[]{:S(2)}, u32[]{:S(2)}) collective-permute-start(bf16[2,512,256]{2,1,0:T(8,128)(2,1)S(1)} %collective-permute-done.refs_1_), channel_id=1, source_target_pairs={{4,8},{5,9},{6,10},{7,11},{8,12},{9,13},{10,14},{11,15},{20,24},{2... | collective-permute-start | bytes 1572872 | tf_op jit(solution)/shard_map/ppermute | solution.py:395
  57.0 0.0 collective-permute-done.8.refs_5_
  57.0 0.0 copy-start.6
  57.0 1.9 %collective-permute-start.9 = (bf16[2,512,256]{2,1,0:T(8,128)(2,1)S(1)}, bf16[2,512,256]{2,1,0:T(8,128)(2,1)S(1)}, u32[]{:S(2)}, u32[]{:S(2)}) collective-permute-start(bf16[2,512,256]{2,1,0:T(8,128)(2,1)S(1)} %collective-permute-done.2.refs_2_), channel_id=1, source_target_pairs={{8,10},{9,11},{10,8},{11,9},{12,14},{13,15},{14,12},{15,13},{24,26... | collective-permute-start | bytes 1572872 | tf_op jit(solution)/shard_map/ppermute | solution.py:395
  58.9 3.1 %collective-permute-done.6.refs_5_ = bf16[2,512,256]{2,1,0:T(8,128)(2,1)S(1)} collective-permute-done((bf16[2,512,256]{2,1,0:T(8,128)(2,1)S(1)}, bf16[2,512,256]{2,1,0:T(8,128)(2,1)S(1)}, u32[]{:S(2)}, u32[]{:S(2)}) %collective-permute-start.6) | collective-permute-done | bytes 524320 | tf_op jit(solution)/shard_map/ppermute | solution.py:395
  62.0 9.2 %collective-permute-done.11.refs_3_ = bf16[2,512,256]{2,1,0:T(8,128)(2,1)} collective-permute-done((bf16[2,512,256]{2,1,0:T(8,128)(2,1)S(1)}, bf16[2,512,256]{2,1,0:T(8,128)(2,1)}, u32[]{:S(2)}, u32[]{:S(2)}) %collective-permute-start.11) | collective-permute-done | bytes 524320 | tf_op jit(solution)/shard_map/ppermute | solution.py:395
  71.2 1.9 %collective-permute-start.13 = (bf16[2,512,256]{2,1,0:T(8,128)(2,1)}, bf16[2,512,256]{2,1,0:T(8,128)(2,1)}, u32[]{:S(2)}, u32[]{:S(2)}) collective-permute-start(bf16[2,512,256]{2,1,0:T(8,128)(2,1)} %collective-permute-done.11.refs_3_), channel_id=1, source_target_pairs={{12,14},{13,15},{14,12},{15,13},{28,30},{29,31},{30,28},{31,29}} | collective-permute-start | bytes 1572872 | tf_op jit(solution)/shard_map/ppermute | solution.py:395
  73.1 6.9 %collective-permute-done.3.refs_2_ = bf16[2,512,256]{2,1,0:T(8,128)(2,1)} collective-permute-done((bf16[2,512,256]{2,1,0:T(8,128)(2,1)S(1)}, bf16[2,512,256]{2,1,0:T(8,128)(2,1)}, u32[]{:S(2)}, u32[]{:S(2)}) %collective-permute-start.3) | collective-permute-done | bytes 524320 | tf_op jit(solution)/shard_map/ppermute | solution.py:395
  80.1 1.3 %collective-permute-start.4 = (bf16[2,512,256]{2,1,0:T(8,128)(2,1)}, bf16[2,512,256]{2,1,0:T(8,128)(2,1)}, u32[]{:S(2)}, u32[]{:S(2)}) collective-permute-start(bf16[2,512,256]{2,1,0:T(8,128)(2,1)} %collective-permute-done.3.refs_2_), channel_id=1, source_target_pairs={{8,12},{9,13},{10,14},{11,15},{24,28},{25,29},{26,30},{27,31}} | collective-permute-start | bytes 1572872 | tf_op jit(solution)/shard_map/ppermute | solution.py:395
  81.4 1.3 %collective-permute-start.12 = (bf16[2,512,256]{2,1,0:T(8,128)(2,1)S(1)}, bf16[2,512,256]{2,1,0:T(8,128)(2,1)}, u32[]{:S(2)}, u32[]{:S(2)}) collective-permute-start(bf16[2,512,256]{2,1,0:T(8,128)(2,1)S(1)} %collective-permute-done.5.refs_4_), channel_id=1, source_target_pairs={{0,12},{1,13},{2,14},{3,15},{16,28},{17,29},{18,30},{19,31}} | collective-permute-start | bytes 1572872 | tf_op jit(solution)/shard_map/ppermute | solution.py:395
  82.7 0.0 collective-permute-done.9.refs_6_
  82.7 0.0 copy-done.6
  82.7 0.0 copy-start.7
  82.7 1.9 %collective-permute-start.10 = (bf16[2,512,256]{2,1,0:T(8,128)(2,1)}, bf16[2,512,256]{2,1,0:T(8,128)(2,1)}, u32[]{:S(2)}, u32[]{:S(2)}) collective-permute-start(bf16[2,512,256]{2,1,0:T(8,128)(2,1)} %collective-permute-done.3.refs_2_), channel_id=1, source_target_pairs={{8,10},{9,11},{10,8},{11,9},{12,14},{13,15},{14,12},{15,13},{24,26... | collective-permute-start | bytes 1572872 | tf_op jit(solution)/shard_map/ppermute | solution.py:395
  84.6 0.0 copy-done.7
  84.7 0.0 copy-done.8
  84.7 0.6 fusion.1.slot_ref
  85.3 0.0 collective-permute-done.13.refs_7_
  85.3 0.0 copy-done.2
  85.3 0.0 copy-done.3
  85.3 0.0 copy-done.5
  85.3 9.5 %attention.2.refs_8_ = bf16[512,4096]{1,0:T(8,128)(2,1)} custom-call(s32[8,7]{1,0:T(8,128)} %fusion.1.slot_ref, s32[8,7]{1,0:T(8,128)} %cut_ref.3, s32[1]{0:T(128)} %bitcast.odd_ref, bf16[512,4096]{1,0:T(8,128)(2,1)} %q_hbm.3, bf16[2,512,256]{2,1,0:T(8,128)(2,1)} %get-tuple-element.18.refs_0_, bf16[2,512,256]{2,1,0:T(8,128)(2,1)} %copy-done.2, ...), custom_call_target="tpu_custom_call" | custom-call | flops 2147483648 | bytes 8388608 | tf_op jit(solution)/shard_map/attention/pallas_call | solution.py:334
  94.8 10.3 %collective-permute-done.4.refs_3_ = bf16[2,512,256]{2,1,0:T(8,128)(2,1)} collective-permute-done((bf16[2,512,256]{2,1,0:T(8,128)(2,1)}, bf16[2,512,256]{2,1,0:T(8,128)(2,1)}, u32[]{:S(2)}, u32[]{:S(2)}) %collective-permute-start.4) | collective-permute-done | bytes 524320 | tf_op jit(solution)/shard_map/ppermute | solution.py:395
  105.1 0.0 collective-permute-done.12.refs_7_
  105.1 0.0 collective-permute-done.10.refs_6_
  105.1 0.0 copy-done
  105.1 0.0 copy-done.1
  105.1 0.0 copy-done.4
  105.1 9.5 %attention.3 = bf16[512,4096]{1,0:T(8,128)(2,1)} custom-call(s32[8,7]{1,0:T(8,128)} %fusion.1.slot_ref, s32[8,7]{1,0:T(8,128)} %cut_ref.3, s32[1]{0:T(128)} %bitcast.odd_ref, bf16[512,4096]{1,0:T(8,128)(2,1)} %q_hbm.3, bf16[2,512,256]{2,1,0:T(8,128)(2,1)} %project.1.refs_0_, bf16[2,512,256]{2,1,0:T(8,128)(2,1)} %copy-done.1, ...), custom_call_target="tpu_custom_call", output_to_operand_aliasing={{}: (12, {})} | custom-call | flops 2147483648 | bytes 8388608 | tf_op jit(solution)/shard_map/attention/pallas_call | solution.py:334
  (3 shorter events, 0.0 us)
Async XLA Ops:
  11.6 16.7 %collective-permute-start.1 = (bf16[2,512,256]{2,1,0:T(8,128)(2,1)}, bf16[2,512,256]{2,1,0:T(8,128)(2,1)S(1)}, u32[]{:S(2)}, u32[]{:S(2)}) collective-permute-start(bf16[2,512,256]{2,1,0:T(8,128)(2,1)} %get-tuple-element.18.refs_0_), channel_id=1, source_target_pairs={{0,4},{1,5},{2,6},{3,7},{4,8},{5,9},{6,10},{7,11},{8,12},{9,13},{1... | collective-permute-start | bytes 1572872 | tf_op jit(solution)/shard_map/ppermute | solution.py:395
  12.9 16.8 %collective-permute-start.7 = (bf16[2,512,256]{2,1,0:T(8,128)(2,1)}, bf16[2,512,256]{2,1,0:T(8,128)(2,1)S(1)}, u32[]{:S(2)}, u32[]{:S(2)}) collective-permute-start(bf16[2,512,256]{2,1,0:T(8,128)(2,1)} %get-tuple-element.18.refs_0_), channel_id=1, source_target_pairs={{0,2},{1,3},{4,6},{5,7},{8,10},{9,11},{12,14},{13,15},{16,18},{17,... | collective-permute-start | bytes 1572872 | tf_op jit(solution)/shard_map/ppermute | solution.py:395
  16.3 68.3 %copy-start.8 = (s32[8,7]{1,0:T(8,128)S(1)}, s32[8,7]{1,0:T(8,128)}, u32[]{:S(2)}) copy-start(s32[8,7]{1,0:T(8,128)} %param.12) | copy-start | bytes 676
  25.7 13.9 %collective-permute-start.5 = (bf16[2,512,256]{2,1,0:T(8,128)(2,1)}, bf16[2,512,256]{2,1,0:T(8,128)(2,1)S(1)}, u32[]{:S(2)}, u32[]{:S(2)}) collective-permute-start(bf16[2,512,256]{2,1,0:T(8,128)(2,1)} %project.1.refs_0_), channel_id=1, source_target_pairs={{0,2},{1,3},{2,0},{3,1},{4,6},{5,7},{8,10},{9,11},{12,14},{13,15},... | collective-permute-start | bytes 1572872 | tf_op jit(solution)/shard_map/ppermute | solution.py:395
  27.0 17.6 %collective-permute-start = (bf16[2,512,256]{2,1,0:T(8,128)(2,1)}, bf16[2,512,256]{2,1,0:T(8,128)(2,1)S(1)}, u32[]{:S(2)}, u32[]{:S(2)}) collective-permute-start(bf16[2,512,256]{2,1,0:T(8,128)(2,1)} %project.1.refs_0_), channel_id=1, source_target_pairs={{0,4},{1,5},{2,6},{3,7},{4,8},{5,9},{6,10},{7,11},{8,12},{9,13},{1... | collective-permute-start | bytes 1572872 | tf_op jit(solution)/shard_map/ppermute | solution.py:395
  28.3 57.0 %copy-start.2 = (bf16[2,512,256]{2,1,0:T(8,128)(2,1)}, bf16[2,512,256]{2,1,0:T(8,128)(2,1)S(1)}, u32[]{:S(2)}) copy-start(bf16[2,512,256]{2,1,0:T(8,128)(2,1)S(1)} %collective-permute-done.1.refs_1_) | copy-start | bytes 1572868
  28.3 26.0 %collective-permute-start.2 = (bf16[2,512,256]{2,1,0:T(8,128)(2,1)S(1)}, bf16[2,512,256]{2,1,0:T(8,128)(2,1)S(1)}, u32[]{:S(2)}, u32[]{:S(2)}) collective-permute-start(bf16[2,512,256]{2,1,0:T(8,128)(2,1)S(1)} %collective-permute-done.1.refs_1_), channel_id=1, source_target_pairs={{4,8},{5,9},{6,10},{7,11},{8,12},{9,13},{10,14},{11,15},{20,24},{2... | collective-permute-start | bytes 1572872 | tf_op jit(solution)/shard_map/ppermute | solution.py:395
  29.7 55.6 %copy-start.3 = (bf16[2,512,256]{2,1,0:T(8,128)(2,1)}, bf16[2,512,256]{2,1,0:T(8,128)(2,1)S(1)}, u32[]{:S(2)}) copy-start(bf16[2,512,256]{2,1,0:T(8,128)(2,1)S(1)} %collective-permute-done.7.refs_4_) | copy-start | bytes 1572868
  29.7 27.3 %collective-permute-start.8 = (bf16[2,512,256]{2,1,0:T(8,128)(2,1)S(1)}, bf16[2,512,256]{2,1,0:T(8,128)(2,1)S(1)}, u32[]{:S(2)}, u32[]{:S(2)}) collective-permute-start(bf16[2,512,256]{2,1,0:T(8,128)(2,1)S(1)} %collective-permute-done.1.refs_1_), channel_id=1, source_target_pairs={{4,6},{5,7},{6,4},{7,5},{8,10},{9,11},{10,8},{11,9},{12,14},{13,15... | collective-permute-start | bytes 1572872 | tf_op jit(solution)/shard_map/ppermute | solution.py:395
  39.6 65.5 %copy-start = (bf16[2,512,256]{2,1,0:T(8,128)(2,1)}, bf16[2,512,256]{2,1,0:T(8,128)(2,1)S(1)}, u32[]{:S(2)}) copy-start(bf16[2,512,256]{2,1,0:T(8,128)(2,1)S(1)} %collective-permute-done.5.refs_4_) | copy-start | bytes 1572868
  44.6 60.5 %copy-start.1 = (bf16[2,512,256]{2,1,0:T(8,128)(2,1)}, bf16[2,512,256]{2,1,0:T(8,128)(2,1)S(1)}, u32[]{:S(2)}) copy-start(bf16[2,512,256]{2,1,0:T(8,128)(2,1)S(1)} %collective-permute-done.refs_1_) | copy-start | bytes 1572868
  44.6 17.4 %collective-permute-start.6 = (bf16[2,512,256]{2,1,0:T(8,128)(2,1)S(1)}, bf16[2,512,256]{2,1,0:T(8,128)(2,1)S(1)}, u32[]{:S(2)}, u32[]{:S(2)}) collective-permute-start(bf16[2,512,256]{2,1,0:T(8,128)(2,1)S(1)} %collective-permute-done.refs_1_), channel_id=1, source_target_pairs={{4,6},{5,7},{6,4},{7,5},{8,10},{9,11},{10,8},{11,9},{12,14},{13,15... | collective-permute-start | bytes 1572872 | tf_op jit(solution)/shard_map/ppermute | solution.py:395
  54.4 30.9 %copy-start.5 = (bf16[2,512,256]{2,1,0:T(8,128)(2,1)}, bf16[2,512,256]{2,1,0:T(8,128)(2,1)S(1)}, u32[]{:S(2)}) copy-start(bf16[2,512,256]{2,1,0:T(8,128)(2,1)S(1)} %collective-permute-done.2.refs_2_) | copy-start | bytes 1572868
  54.4 16.8 %collective-permute-start.11 = (bf16[2,512,256]{2,1,0:T(8,128)(2,1)S(1)}, bf16[2,512,256]{2,1,0:T(8,128)(2,1)}, u32[]{:S(2)}, u32[]{:S(2)}) collective-permute-start(bf16[2,512,256]{2,1,0:T(8,128)(2,1)S(1)} %collective-permute-done.2.refs_2_), channel_id=1, source_target_pairs={{8,12},{9,13},{10,14},{11,15},{24,28},{25,29},{26,30},{27,31}} | collective-permute-start | bytes 1572872 | tf_op jit(solution)/shard_map/ppermute | solution.py:395
  55.7 24.4 %collective-permute-start.3 = (bf16[2,512,256]{2,1,0:T(8,128)(2,1)S(1)}, bf16[2,512,256]{2,1,0:T(8,128)(2,1)}, u32[]{:S(2)}, u32[]{:S(2)}) collective-permute-start(bf16[2,512,256]{2,1,0:T(8,128)(2,1)S(1)} %collective-permute-done.refs_1_), channel_id=1, source_target_pairs={{4,8},{5,9},{6,10},{7,11},{8,12},{9,13},{10,14},{11,15},{20,24},{2... | collective-permute-start | bytes 1572872 | tf_op jit(solution)/shard_map/ppermute | solution.py:395
  57.0 25.7 %copy-start.6 = (bf16[2,512,256]{2,1,0:T(8,128)(2,1)}, bf16[2,512,256]{2,1,0:T(8,128)(2,1)S(1)}, u32[]{:S(2)}) copy-start(bf16[2,512,256]{2,1,0:T(8,128)(2,1)S(1)} %collective-permute-done.8.refs_5_) | copy-start | bytes 1572868
  57.0 25.7 %collective-permute-start.9 = (bf16[2,512,256]{2,1,0:T(8,128)(2,1)S(1)}, bf16[2,512,256]{2,1,0:T(8,128)(2,1)S(1)}, u32[]{:S(2)}, u32[]{:S(2)}) collective-permute-start(bf16[2,512,256]{2,1,0:T(8,128)(2,1)S(1)} %collective-permute-done.2.refs_2_), channel_id=1, source_target_pairs={{8,10},{9,11},{10,8},{11,9},{12,14},{13,15},{14,12},{15,13},{24,26... | collective-permute-start | bytes 1572872 | tf_op jit(solution)/shard_map/ppermute | solution.py:395
  62.0 43.1 %copy-start.4 = (bf16[2,512,256]{2,1,0:T(8,128)(2,1)}, bf16[2,512,256]{2,1,0:T(8,128)(2,1)S(1)}, u32[]{:S(2)}) copy-start(bf16[2,512,256]{2,1,0:T(8,128)(2,1)S(1)} %collective-permute-done.6.refs_5_) | copy-start | bytes 1572868
  71.2 14.1 %collective-permute-start.13 = (bf16[2,512,256]{2,1,0:T(8,128)(2,1)}, bf16[2,512,256]{2,1,0:T(8,128)(2,1)}, u32[]{:S(2)}, u32[]{:S(2)}) collective-permute-start(bf16[2,512,256]{2,1,0:T(8,128)(2,1)} %collective-permute-done.11.refs_3_), channel_id=1, source_target_pairs={{12,14},{13,15},{14,12},{15,13},{28,30},{29,31},{30,28},{31,29}} | collective-permute-start | bytes 1572872 | tf_op jit(solution)/shard_map/ppermute | solution.py:395
  80.1 25.0 %collective-permute-start.4 = (bf16[2,512,256]{2,1,0:T(8,128)(2,1)}, bf16[2,512,256]{2,1,0:T(8,128)(2,1)}, u32[]{:S(2)}, u32[]{:S(2)}) collective-permute-start(bf16[2,512,256]{2,1,0:T(8,128)(2,1)} %collective-permute-done.3.refs_2_), channel_id=1, source_target_pairs={{8,12},{9,13},{10,14},{11,15},{24,28},{25,29},{26,30},{27,31}} | collective-permute-start | bytes 1572872 | tf_op jit(solution)/shard_map/ppermute | solution.py:395
  81.4 23.7 %collective-permute-start.12 = (bf16[2,512,256]{2,1,0:T(8,128)(2,1)S(1)}, bf16[2,512,256]{2,1,0:T(8,128)(2,1)}, u32[]{:S(2)}, u32[]{:S(2)}) collective-permute-start(bf16[2,512,256]{2,1,0:T(8,128)(2,1)S(1)} %collective-permute-done.5.refs_4_), channel_id=1, source_target_pairs={{0,12},{1,13},{2,14},{3,15},{16,28},{17,29},{18,30},{19,31}} | collective-permute-start | bytes 1572872 | tf_op jit(solution)/shard_map/ppermute | solution.py:395
  82.7 1.9 %copy-start.7 = (bf16[2,512,256]{2,1,0:T(8,128)(2,1)}, bf16[2,512,256]{2,1,0:T(8,128)(2,1)S(1)}, u32[]{:S(2)}) copy-start(bf16[2,512,256]{2,1,0:T(8,128)(2,1)S(1)} %collective-permute-done.9.refs_6_) | copy-start | bytes 1572868
  82.7 22.4 %collective-permute-start.10 = (bf16[2,512,256]{2,1,0:T(8,128)(2,1)}, bf16[2,512,256]{2,1,0:T(8,128)(2,1)}, u32[]{:S(2)}, u32[]{:S(2)}) collective-permute-start(bf16[2,512,256]{2,1,0:T(8,128)(2,1)} %collective-permute-done.3.refs_2_), channel_id=1, source_target_pairs={{8,10},{9,11},{10,8},{11,9},{12,14},{13,15},{14,12},{15,13},{24,26... | collective-permute-start | bytes 1572872 | tf_op jit(solution)/shard_map/ppermute | solution.py:395

commit v23 on v22

--- a/solution.py
+++ b/solution.py
@@ -67,14 +67,17 @@
 
     for c in range(loads):
         load_x(c).start()
+    acc_scr[...] = jnp.zeros_like(acc_scr)
 
     def square(c, carry):
         load_x(c).wait()
 
-        @pl.when(c == loads - 4)
-        def _():
-            for copy in load_weights(0):
-                copy.start()
+        for early in range(2):
+
+            @pl.when(c == loads - 4 + 2 * early)
+            def _(early=early):
+                for copy in load_weights(early):
+                    copy.start()
 
         row = pl.ds(pl.multiple_of(c * tall, tall), tall)
         total = jnp.zeros((tall, lanes), jnp.float32)
@@ -85,13 +88,11 @@
         return carry
 
     lax.fori_loop(0, loads, square, 0)
-    for c in range(1, chunks):
+    for c in range(2, chunks):
         for copy in load_weights(c):
             copy.start()
     mean_sq = jnp.sum(scale_ref[...], axis=-1, keepdims=True) / features
     scale_ref[...] = jnp.broadcast_to(lax.rsqrt(mean_sq + EPS), scale_ref.shape)
-
-    acc_scr[...] = jnp.zeros_like(acc_scr)
 
     def multiply(c, carry):
         for copy in load_weights(c):

time: 115 us -> 115 us (level)
  no operation moved by 1% of the time
where the time goes in v23:
time: 115 us
  waiting for transfers between devices  49.4 us (43%)
  Pallas kernels  39.9 us (35%)
  starting transfers between devices  24.3 us (21%)
    ppermute x14, waiting for transfers between devices, step(): moved[key, s, unit] = lax.ppermute(array, 'node', pairs)  49.4 us
    ppermute x14, starting transfers between devices, step(): moved[key, s, unit] = lax.ppermute(array, 'node', pairs)  24.3 us
    pallas_call x2, Pallas kernels, attention(): pl.pallas_call(functools.partial(attention_kernel, block, unit, near), in...  19 us
    pallas_call x1, Pallas kernels, norm_project(): pl.pallas_call(norm_project_kernel, in_specs=[held, whole, held, held], o...  11.6 us
    pallas_call x1, Pallas kernels, project(): pl.pallas_call(project_kernel, grid=(CHUNKS,), in_specs=[pl.BlockSpec((ro...  9.35 us
  transfers between devices with their start and end apart: 14, of which 7 were waited for; matrix products, arithmetic and copies ran while one was open for 1% of the time, Pallas kernels for 16%

profile of v23, /device:TPU:24, one launch (start us, length us, event | category | flops | bytes accessed | tf_op | source)
XLA Modules:
  0.0 114.6 jit_solution(1702324522831690796)
XLA Ops:
  0.0 11.6 %norm_project.1 = (f32[512,128]{1,0:T(8,128)}, bf16[2,512,256]{2,1,0:T(8,128)(2,1)}) custom-call(bf16[512,8192]{1,0:T(8,128)(2,1)} %x_ref.1, f32[1,8192]{1,0:T(1,128)} %bitcast.2, bf16[8192,512]{1,0:T(8,128)(2,1)} %key_ref.1, bf16[8192,512]{1,0:T(8,128)(2,1)} %value_ref.1), custom_call_target="tpu_custom_call" | custom-call | flops 4294967296 | bytes 16777216 | tf_op jit(solution)/shard_map/norm_project/pallas_call | solution.py:129
  11.6 1.3 %collective-permute-start.1 = (bf16[2,512,256]{2,1,0:T(8,128)(2,1)}, bf16[2,512,256]{2,1,0:T(8,128)(2,1)S(1)}, u32[]{:S(2)}, u32[]{:S(2)}) collective-permute-start(bf16[2,512,256]{2,1,0:T(8,128)(2,1)} %get-tuple-element.18.refs_0_), channel_id=1, source_target_pairs={{0,4},{1,5},{2,6},{3,7},{4,8},{5,9},{6,10},{7,11},{8,12},{9,13},{1... | collective-permute-start | bytes 1572872 | tf_op jit(solution)/shard_map/ppermute | solution.py:396
  12.9 3.5 %collective-permute-start.7 = (bf16[2,512,256]{2,1,0:T(8,128)(2,1)}, bf16[2,512,256]{2,1,0:T(8,128)(2,1)S(1)}, u32[]{:S(2)}, u32[]{:S(2)}) collective-permute-start(bf16[2,512,256]{2,1,0:T(8,128)(2,1)} %get-tuple-element.18.refs_0_), channel_id=1, source_target_pairs={{0,2},{1,3},{4,6},{5,7},{8,10},{9,11},{12,14},{13,15},{16,18},{17,... | collective-permute-start | bytes 1572872 | tf_op jit(solution)/shard_map/ppermute | solution.py:396
  16.3 0.0 copy-start.8
  16.4 9.3 %project.1.refs_0_ = bf16[2,512,256]{2,1,0:T(8,128)(2,1)} custom-call(bf16[512,8192]{1,0:T(8,128)(2,1)} %x_ref.1, f32[512,128]{1,0:T(8,128)} %get-tuple-element.17.scale_ref, f32[1,8192]{1,0:T(1,128)} %bitcast.3, bf16[8192,512]{1,0:T(8,128)(2,1)} %key_ref.1, bf16[8192,512]{1,0:T(8,128)(2,1)} %value_ref.1), custom_call_target="tpu_custom_call" | custom-call | flops 4294967296 | bytes 16777216 | tf_op jit(solution)/shard_map/project/pallas_call | solution.py:180
  25.7 1.3 %collective-permute-start.5 = (bf16[2,512,256]{2,1,0:T(8,128)(2,1)}, bf16[2,512,256]{2,1,0:T(8,128)(2,1)S(1)}, u32[]{:S(2)}, u32[]{:S(2)}) collective-permute-start(bf16[2,512,256]{2,1,0:T(8,128)(2,1)} %project.1.refs_0_), channel_id=1, source_target_pairs={{0,2},{1,3},{2,0},{3,1},{4,6},{5,7},{8,10},{9,11},{12,14},{13,15},... | collective-permute-start | bytes 1572872 | tf_op jit(solution)/shard_map/ppermute | solution.py:396
  27.0 1.3 %collective-permute-start = (bf16[2,512,256]{2,1,0:T(8,128)(2,1)}, bf16[2,512,256]{2,1,0:T(8,128)(2,1)S(1)}, u32[]{:S(2)}, u32[]{:S(2)}) collective-permute-start(bf16[2,512,256]{2,1,0:T(8,128)(2,1)} %project.1.refs_0_), channel_id=1, source_target_pairs={{0,4},{1,5},{2,6},{3,7},{4,8},{5,9},{6,10},{7,11},{8,12},{9,13},{1... | collective-permute-start | bytes 1572872 | tf_op jit(solution)/shard_map/ppermute | solution.py:396
  28.3 0.0 collective-permute-done.1.refs_1_
  28.3 0.0 copy-start.2
  28.3 1.3 %collective-permute-start.2 = (bf16[2,512,256]{2,1,0:T(8,128)(2,1)S(1)}, bf16[2,512,256]{2,1,0:T(8,128)(2,1)S(1)}, u32[]{:S(2)}, u32[]{:S(2)}) collective-permute-start(bf16[2,512,256]{2,1,0:T(8,128)(2,1)S(1)} %collective-permute-done.1.refs_1_), channel_id=1, source_target_pairs={{4,8},{5,9},{6,10},{7,11},{8,12},{9,13},{10,14},{11,15},{20,24},{2... | collective-permute-start | bytes 1572872 | tf_op jit(solution)/shard_map/ppermute | solution.py:396
  29.6 0.0 collective-permute-done.7.refs_4_
  29.7 0.0 copy-start.3
  29.7 2.9 %collective-permute-start.8 = (bf16[2,512,256]{2,1,0:T(8,128)(2,1)S(1)}, bf16[2,512,256]{2,1,0:T(8,128)(2,1)S(1)}, u32[]{:S(2)}, u32[]{:S(2)}) collective-permute-start(bf16[2,512,256]{2,1,0:T(8,128)(2,1)S(1)} %collective-permute-done.1.refs_1_), channel_id=1, source_target_pairs={{4,6},{5,7},{6,4},{7,5},{8,10},{9,11},{10,8},{11,9},{12,14},{13,15... | collective-permute-start | bytes 1572872 | tf_op jit(solution)/shard_map/ppermute | solution.py:396
  32.6 7.1 %collective-permute-done.5.refs_4_ = bf16[2,512,256]{2,1,0:T(8,128)(2,1)S(1)} collective-permute-done((bf16[2,512,256]{2,1,0:T(8,128)(2,1)}, bf16[2,512,256]{2,1,0:T(8,128)(2,1)S(1)}, u32[]{:S(2)}, u32[]{:S(2)}) %collective-permute-start.5) | collective-permute-done | bytes 524320 | tf_op jit(solution)/shard_map/ppermute | solution.py:396
  39.6 0.0 copy-start
  39.6 5.0 %collective-permute-done.refs_1_ = bf16[2,512,256]{2,1,0:T(8,128)(2,1)S(1)} collective-permute-done((bf16[2,512,256]{2,1,0:T(8,128)(2,1)}, bf16[2,512,256]{2,1,0:T(8,128)(2,1)S(1)}, u32[]{:S(2)}, u32[]{:S(2)}) %collective-permute-start) | collective-permute-done | bytes 524320 | tf_op jit(solution)/shard_map/ppermute | solution.py:396
  44.6 1.9 %collective-permute-start.6 = (bf16[2,512,256]{2,1,0:T(8,128)(2,1)S(1)}, bf16[2,512,256]{2,1,0:T(8,128)(2,1)S(1)}, u32[]{:S(2)}, u32[]{:S(2)}) collective-permute-start(bf16[2,512,256]{2,1,0:T(8,128)(2,1)S(1)} %collective-permute-done.refs_1_), channel_id=1, source_target_pairs={{4,6},{5,7},{6,4},{7,5},{8,10},{9,11},{10,8},{11,9},{12,14},{13,15... | collective-permute-start | bytes 1572872 | tf_op jit(solution)/shard_map/ppermute | solution.py:396
  46.5 7.9 %collective-permute-done.2.refs_2_ = bf16[2,512,256]{2,1,0:T(8,128)(2,1)S(1)} collective-permute-done((bf16[2,512,256]{2,1,0:T(8,128)(2,1)S(1)}, bf16[2,512,256]{2,1,0:T(8,128)(2,1)S(1)}, u32[]{:S(2)}, u32[]{:S(2)}) %collective-permute-start.2) | collective-permute-done | bytes 524320 | tf_op jit(solution)/shard_map/ppermute | solution.py:396
  54.4 1.3 %collective-permute-start.11 = (bf16[2,512,256]{2,1,0:T(8,128)(2,1)S(1)}, bf16[2,512,256]{2,1,0:T(8,128)(2,1)}, u32[]{:S(2)}, u32[]{:S(2)}) collective-permute-start(bf16[2,512,256]{2,1,0:T(8,128)(2,1)S(1)} %collective-permute-done.2.refs_2_), channel_id=1, source_target_pairs={{8,12},{9,13},{10,14},{11,15},{24,28},{25,29},{26,30},{27,31}} | collective-permute-start | bytes 1572872 | tf_op jit(solution)/shard_map/ppermute | solution.py:396
  55.7 1.3 %collective-permute-start.3 = (bf16[2,512,256]{2,1,0:T(8,128)(2,1)S(1)}, bf16[2,512,256]{2,1,0:T(8,128)(2,1)}, u32[]{:S(2)}, u32[]{:S(2)}) collective-permute-start(bf16[2,512,256]{2,1,0:T(8,128)(2,1)S(1)} %collective-permute-done.refs_1_), channel_id=1, source_target_pairs={{4,8},{5,9},{6,10},{7,11},{8,12},{9,13},{10,14},{11,15},{20,24},{2... | collective-permute-start | bytes 1572872 | tf_op jit(solution)/shard_map/ppermute | solution.py:396
  57.0 0.0 collective-permute-done.8.refs_5_
  57.0 0.0 copy-start.6
  57.0 1.9 %collective-permute-start.9 = (bf16[2,512,256]{2,1,0:T(8,128)(2,1)S(1)}, bf16[2,512,256]{2,1,0:T(8,128)(2,1)S(1)}, u32[]{:S(2)}, u32[]{:S(2)}) collective-permute-start(bf16[2,512,256]{2,1,0:T(8,128)(2,1)S(1)} %collective-permute-done.2.refs_2_), channel_id=1, source_target_pairs={{8,10},{9,11},{10,8},{11,9},{12,14},{13,15},{14,12},{15,13},{24,26... | collective-permute-start | bytes 1572872 | tf_op jit(solution)/shard_map/ppermute | solution.py:396
  58.9 3.1 %collective-permute-done.6.refs_5_ = bf16[2,512,256]{2,1,0:T(8,128)(2,1)S(1)} collective-permute-done((bf16[2,512,256]{2,1,0:T(8,128)(2,1)S(1)}, bf16[2,512,256]{2,1,0:T(8,128)(2,1)S(1)}, u32[]{:S(2)}, u32[]{:S(2)}) %collective-permute-start.6) | collective-permute-done | bytes 524320 | tf_op jit(solution)/shard_map/ppermute | solution.py:396
  62.0 9.2 %collective-permute-done.11.refs_3_ = bf16[2,512,256]{2,1,0:T(8,128)(2,1)} collective-permute-done((bf16[2,512,256]{2,1,0:T(8,128)(2,1)S(1)}, bf16[2,512,256]{2,1,0:T(8,128)(2,1)}, u32[]{:S(2)}, u32[]{:S(2)}) %collective-permute-start.11) | collective-permute-done | bytes 524320 | tf_op jit(solution)/shard_map/ppermute | solution.py:396
  71.2 1.9 %collective-permute-start.13 = (bf16[2,512,256]{2,1,0:T(8,128)(2,1)}, bf16[2,512,256]{2,1,0:T(8,128)(2,1)}, u32[]{:S(2)}, u32[]{:S(2)}) collective-permute-start(bf16[2,512,256]{2,1,0:T(8,128)(2,1)} %collective-permute-done.11.refs_3_), channel_id=1, source_target_pairs={{12,14},{13,15},{14,12},{15,13},{28,30},{29,31},{30,28},{31,29}} | collective-permute-start | bytes 1572872 | tf_op jit(solution)/shard_map/ppermute | solution.py:396
  73.1 6.9 %collective-permute-done.3.refs_2_ = bf16[2,512,256]{2,1,0:T(8,128)(2,1)} collective-permute-done((bf16[2,512,256]{2,1,0:T(8,128)(2,1)S(1)}, bf16[2,512,256]{2,1,0:T(8,128)(2,1)}, u32[]{:S(2)}, u32[]{:S(2)}) %collective-permute-start.3) | collective-permute-done | bytes 524320 | tf_op jit(solution)/shard_map/ppermute | solution.py:396
  80.1 1.3 %collective-permute-start.4 = (bf16[2,512,256]{2,1,0:T(8,128)(2,1)}, bf16[2,512,256]{2,1,0:T(8,128)(2,1)}, u32[]{:S(2)}, u32[]{:S(2)}) collective-permute-start(bf16[2,512,256]{2,1,0:T(8,128)(2,1)} %collective-permute-done.3.refs_2_), channel_id=1, source_target_pairs={{8,12},{9,13},{10,14},{11,15},{24,28},{25,29},{26,30},{27,31}} | collective-permute-start | bytes 1572872 | tf_op jit(solution)/shard_map/ppermute | solution.py:396
  81.4 1.3 %collective-permute-start.12 = (bf16[2,512,256]{2,1,0:T(8,128)(2,1)S(1)}, bf16[2,512,256]{2,1,0:T(8,128)(2,1)}, u32[]{:S(2)}, u32[]{:S(2)}) collective-permute-start(bf16[2,512,256]{2,1,0:T(8,128)(2,1)S(1)} %collective-permute-done.5.refs_4_), channel_id=1, source_target_pairs={{0,12},{1,13},{2,14},{3,15},{16,28},{17,29},{18,30},{19,31}} | collective-permute-start | bytes 1572872 | tf_op jit(solution)/shard_map/ppermute | solution.py:396
  82.7 0.0 collective-permute-done.9.refs_6_
  82.7 0.0 copy-done.6
  82.7 0.0 copy-start.7
  82.7 1.9 %collective-permute-start.10 = (bf16[2,512,256]{2,1,0:T(8,128)(2,1)}, bf16[2,512,256]{2,1,0:T(8,128)(2,1)}, u32[]{:S(2)}, u32[]{:S(2)}) collective-permute-start(bf16[2,512,256]{2,1,0:T(8,128)(2,1)} %collective-permute-done.3.refs_2_), channel_id=1, source_target_pairs={{8,10},{9,11},{10,8},{11,9},{12,14},{13,15},{14,12},{15,13},{24,26... | collective-permute-start | bytes 1572872 | tf_op jit(solution)/shard_map/ppermute | solution.py:396
  84.6 0.0 copy-done.7
  84.7 0.0 copy-done.8
  84.7 0.6 fusion.1.slot_ref
  85.3 0.0 collective-permute-done.13.refs_7_
  85.3 0.0 copy-done.2
  85.3 0.0 copy-done.3
  85.3 0.0 copy-done.5
  85.3 9.5 %attention.2.refs_8_ = bf16[512,4096]{1,0:T(8,128)(2,1)} custom-call(s32[8,7]{1,0:T(8,128)} %fusion.1.slot_ref, s32[8,7]{1,0:T(8,128)} %cut_ref.3, s32[1]{0:T(128)} %bitcast.odd_ref, bf16[512,4096]{1,0:T(8,128)(2,1)} %q_hbm.3, bf16[2,512,256]{2,1,0:T(8,128)(2,1)} %get-tuple-element.18.refs_0_, bf16[2,512,256]{2,1,0:T(8,128)(2,1)} %copy-done.2, ...), custom_call_target="tpu_custom_call" | custom-call | flops 2147483648 | bytes 8388608 | tf_op jit(solution)/shard_map/attention/pallas_call | solution.py:335
  94.8 10.3 %collective-permute-done.4.refs_3_ = bf16[2,512,256]{2,1,0:T(8,128)(2,1)} collective-permute-done((bf16[2,512,256]{2,1,0:T(8,128)(2,1)}, bf16[2,512,256]{2,1,0:T(8,128)(2,1)}, u32[]{:S(2)}, u32[]{:S(2)}) %collective-permute-start.4) | collective-permute-done | bytes 524320 | tf_op jit(solution)/shard_map/ppermute | solution.py:396
  105.1 0.0 collective-permute-done.12.refs_7_
  105.1 0.0 collective-permute-done.10.refs_6_
  105.1 0.0 copy-done
  105.1 0.0 copy-done.1
  105.1 0.0 copy-done.4
  105.1 9.5 %attention.3 = bf16[512,4096]{1,0:T(8,128)(2,1)} custom-call(s32[8,7]{1,0:T(8,128)} %fusion.1.slot_ref, s32[8,7]{1,0:T(8,128)} %cut_ref.3, s32[1]{0:T(128)} %bitcast.odd_ref, bf16[512,4096]{1,0:T(8,128)(2,1)} %q_hbm.3, bf16[2,512,256]{2,1,0:T(8,128)(2,1)} %project.1.refs_0_, bf16[2,512,256]{2,1,0:T(8,128)(2,1)} %copy-done.1, ...), custom_call_target="tpu_custom_call", output_to_operand_aliasing={{}: (12, {})} | custom-call | flops 2147483648 | bytes 8388608 | tf_op jit(solution)/shard_map/attention/pallas_call | solution.py:335
  (3 shorter events, 0.0 us)
Async XLA Ops:
  11.6 16.7 %collective-permute-start.1 = (bf16[2,512,256]{2,1,0:T(8,128)(2,1)}, bf16[2,512,256]{2,1,0:T(8,128)(2,1)S(1)}, u32[]{:S(2)}, u32[]{:S(2)}) collective-permute-start(bf16[2,512,256]{2,1,0:T(8,128)(2,1)} %get-tuple-element.18.refs_0_), channel_id=1, source_target_pairs={{0,4},{1,5},{2,6},{3,7},{4,8},{5,9},{6,10},{7,11},{8,12},{9,13},{1... | collective-permute-start | bytes 1572872 | tf_op jit(solution)/shard_map/ppermute | solution.py:396
  12.9 16.8 %collective-permute-start.7 = (bf16[2,512,256]{2,1,0:T(8,128)(2,1)}, bf16[2,512,256]{2,1,0:T(8,128)(2,1)S(1)}, u32[]{:S(2)}, u32[]{:S(2)}) collective-permute-start(bf16[2,512,256]{2,1,0:T(8,128)(2,1)} %get-tuple-element.18.refs_0_), channel_id=1, source_target_pairs={{0,2},{1,3},{4,6},{5,7},{8,10},{9,11},{12,14},{13,15},{16,18},{17,... | collective-permute-start | bytes 1572872 | tf_op jit(solution)/shard_map/ppermute | solution.py:396
  16.3 68.3 %copy-start.8 = (s32[8,7]{1,0:T(8,128)S(1)}, s32[8,7]{1,0:T(8,128)}, u32[]{:S(2)}) copy-start(s32[8,7]{1,0:T(8,128)} %param.12) | copy-start | bytes 676
  25.7 13.9 %collective-permute-start.5 = (bf16[2,512,256]{2,1,0:T(8,128)(2,1)}, bf16[2,512,256]{2,1,0:T(8,128)(2,1)S(1)}, u32[]{:S(2)}, u32[]{:S(2)}) collective-permute-start(bf16[2,512,256]{2,1,0:T(8,128)(2,1)} %project.1.refs_0_), channel_id=1, source_target_pairs={{0,2},{1,3},{2,0},{3,1},{4,6},{5,7},{8,10},{9,11},{12,14},{13,15},... | collective-permute-start | bytes 1572872 | tf_op jit(solution)/shard_map/ppermute | solution.py:396
  27.0 17.6 %collective-permute-start = (bf16[2,512,256]{2,1,0:T(8,128)(2,1)}, bf16[2,512,256]{2,1,0:T(8,128)(2,1)S(1)}, u32[]{:S(2)}, u32[]{:S(2)}) collective-permute-start(bf16[2,512,256]{2,1,0:T(8,128)(2,1)} %project.1.refs_0_), channel_id=1, source_target_pairs={{0,4},{1,5},{2,6},{3,7},{4,8},{5,9},{6,10},{7,11},{8,12},{9,13},{1... | collective-permute-start | bytes 1572872 | tf_op jit(solution)/shard_map/ppermute | solution.py:396
  28.3 56.9 %copy-start.2 = (bf16[2,512,256]{2,1,0:T(8,128)(2,1)}, bf16[2,512,256]{2,1,0:T(8,128)(2,1)S(1)}, u32[]{:S(2)}) copy-start(bf16[2,512,256]{2,1,0:T(8,128)(2,1)S(1)} %collective-permute-done.1.refs_1_) | copy-start | bytes 1572868
  28.3 26.0 %collective-permute-start.2 = (bf16[2,512,256]{2,1,0:T(8,128)(2,1)S(1)}, bf16[2,512,256]{2,1,0:T(8,128)(2,1)S(1)}, u32[]{:S(2)}, u32[]{:S(2)}) collective-permute-start(bf16[2,512,256]{2,1,0:T(8,128)(2,1)S(1)} %collective-permute-done.1.refs_1_), channel_id=1, source_target_pairs={{4,8},{5,9},{6,10},{7,11},{8,12},{9,13},{10,14},{11,15},{20,24},{2... | collective-permute-start | bytes 1572872 | tf_op jit(solution)/shard_map/ppermute | solution.py:396
  29.7 55.6 %copy-start.3 = (bf16[2,512,256]{2,1,0:T(8,128)(2,1)}, bf16[2,512,256]{2,1,0:T(8,128)(2,1)S(1)}, u32[]{:S(2)}) copy-start(bf16[2,512,256]{2,1,0:T(8,128)(2,1)S(1)} %collective-permute-done.7.refs_4_) | copy-start | bytes 1572868
  29.7 27.3 %collective-permute-start.8 = (bf16[2,512,256]{2,1,0:T(8,128)(2,1)S(1)}, bf16[2,512,256]{2,1,0:T(8,128)(2,1)S(1)}, u32[]{:S(2)}, u32[]{:S(2)}) collective-permute-start(bf16[2,512,256]{2,1,0:T(8,128)(2,1)S(1)} %collective-permute-done.1.refs_1_), channel_id=1, source_target_pairs={{4,6},{5,7},{6,4},{7,5},{8,10},{9,11},{10,8},{11,9},{12,14},{13,15... | collective-permute-start | bytes 1572872 | tf_op jit(solution)/shard_map/ppermute | solution.py:396
  39.6 65.4 %copy-start = (bf16[2,512,256]{2,1,0:T(8,128)(2,1)}, bf16[2,512,256]{2,1,0:T(8,128)(2,1)S(1)}, u32[]{:S(2)}) copy-start(bf16[2,512,256]{2,1,0:T(8,128)(2,1)S(1)} %collective-permute-done.5.refs_4_) | copy-start | bytes 1572868
  44.6 60.5 %copy-start.1 = (bf16[2,512,256]{2,1,0:T(8,128)(2,1)}, bf16[2,512,256]{2,1,0:T(8,128)(2,1)S(1)}, u32[]{:S(2)}) copy-start(bf16[2,512,256]{2,1,0:T(8,128)(2,1)S(1)} %collective-permute-done.refs_1_) | copy-start | bytes 1572868
  44.6 17.4 %collective-permute-start.6 = (bf16[2,512,256]{2,1,0:T(8,128)(2,1)S(1)}, bf16[2,512,256]{2,1,0:T(8,128)(2,1)S(1)}, u32[]{:S(2)}, u32[]{:S(2)}) collective-permute-start(bf16[2,512,256]{2,1,0:T(8,128)(2,1)S(1)} %collective-permute-done.refs_1_), channel_id=1, source_target_pairs={{4,6},{5,7},{6,4},{7,5},{8,10},{9,11},{10,8},{11,9},{12,14},{13,15... | collective-permute-start | bytes 1572872 | tf_op jit(solution)/shard_map/ppermute | solution.py:396
  54.4 30.9 %copy-start.5 = (bf16[2,512,256]{2,1,0:T(8,128)(2,1)}, bf16[2,512,256]{2,1,0:T(8,128)(2,1)S(1)}, u32[]{:S(2)}) copy-start(bf16[2,512,256]{2,1,0:T(8,128)(2,1)S(1)} %collective-permute-done.2.refs_2_) | copy-start | bytes 1572868
  54.4 16.8 %collective-permute-start.11 = (bf16[2,512,256]{2,1,0:T(8,128)(2,1)S(1)}, bf16[2,512,256]{2,1,0:T(8,128)(2,1)}, u32[]{:S(2)}, u32[]{:S(2)}) collective-permute-start(bf16[2,512,256]{2,1,0:T(8,128)(2,1)S(1)} %collective-permute-done.2.refs_2_), channel_id=1, source_target_pairs={{8,12},{9,13},{10,14},{11,15},{24,28},{25,29},{26,30},{27,31}} | collective-permute-start | bytes 1572872 | tf_op jit(solution)/shard_map/ppermute | solution.py:396
  55.7 24.4 %collective-permute-start.3 = (bf16[2,512,256]{2,1,0:T(8,128)(2,1)S(1)}, bf16[2,512,256]{2,1,0:T(8,128)(2,1)}, u32[]{:S(2)}, u32[]{:S(2)}) collective-permute-start(bf16[2,512,256]{2,1,0:T(8,128)(2,1)S(1)} %collective-permute-done.refs_1_), channel_id=1, source_target_pairs={{4,8},{5,9},{6,10},{7,11},{8,12},{9,13},{10,14},{11,15},{20,24},{2... | collective-permute-start | bytes 1572872 | tf_op jit(solution)/shard_map/ppermute | solution.py:396
  57.0 25.7 %copy-start.6 = (bf16[2,512,256]{2,1,0:T(8,128)(2,1)}, bf16[2,512,256]{2,1,0:T(8,128)(2,1)S(1)}, u32[]{:S(2)}) copy-start(bf16[2,512,256]{2,1,0:T(8,128)(2,1)S(1)} %collective-permute-done.8.refs_5_) | copy-start | bytes 1572868
  57.0 25.7 %collective-permute-start.9 = (bf16[2,512,256]{2,1,0:T(8,128)(2,1)S(1)}, bf16[2,512,256]{2,1,0:T(8,128)(2,1)S(1)}, u32[]{:S(2)}, u32[]{:S(2)}) collective-permute-start(bf16[2,512,256]{2,1,0:T(8,128)(2,1)S(1)} %collective-permute-done.2.refs_2_), channel_id=1, source_target_pairs={{8,10},{9,11},{10,8},{11,9},{12,14},{13,15},{14,12},{15,13},{24,26... | collective-permute-start | bytes 1572872 | tf_op jit(solution)/shard_map/ppermute | solution.py:396
  62.0 43.1 %copy-start.4 = (bf16[2,512,256]{2,1,0:T(8,128)(2,1)}, bf16[2,512,256]{2,1,0:T(8,128)(2,1)S(1)}, u32[]{:S(2)}) copy-start(bf16[2,512,256]{2,1,0:T(8,128)(2,1)S(1)} %collective-permute-done.6.refs_5_) | copy-start | bytes 1572868
  71.2 14.0 %collective-permute-start.13 = (bf16[2,512,256]{2,1,0:T(8,128)(2,1)}, bf16[2,512,256]{2,1,0:T(8,128)(2,1)}, u32[]{:S(2)}, u32[]{:S(2)}) collective-permute-start(bf16[2,512,256]{2,1,0:T(8,128)(2,1)} %collective-permute-done.11.refs_3_), channel_id=1, source_target_pairs={{12,14},{13,15},{14,12},{15,13},{28,30},{29,31},{30,28},{31,29}} | collective-permute-start | bytes 1572872 | tf_op jit(solution)/shard_map/ppermute | solution.py:396
  80.1 25.0 %collective-permute-start.4 = (bf16[2,512,256]{2,1,0:T(8,128)(2,1)}, bf16[2,512,256]{2,1,0:T(8,128)(2,1)}, u32[]{:S(2)}, u32[]{:S(2)}) collective-permute-start(bf16[2,512,256]{2,1,0:T(8,128)(2,1)} %collective-permute-done.3.refs_2_), channel_id=1, source_target_pairs={{8,12},{9,13},{10,14},{11,15},{24,28},{25,29},{26,30},{27,31}} | collective-permute-start | bytes 1572872 | tf_op jit(solution)/shard_map/ppermute | solution.py:396
  81.4 23.7 %collective-permute-start.12 = (bf16[2,512,256]{2,1,0:T(8,128)(2,1)S(1)}, bf16[2,512,256]{2,1,0:T(8,128)(2,1)}, u32[]{:S(2)}, u32[]{:S(2)}) collective-permute-start(bf16[2,512,256]{2,1,0:T(8,128)(2,1)S(1)} %collective-permute-done.5.refs_4_), channel_id=1, source_target_pairs={{0,12},{1,13},{2,14},{3,15},{16,28},{17,29},{18,30},{19,31}} | collective-permute-start | bytes 1572872 | tf_op jit(solution)/shard_map/ppermute | solution.py:396
  82.7 1.9 %copy-start.7 = (bf16[2,512,256]{2,1,0:T(8,128)(2,1)}, bf16[2,512,256]{2,1,0:T(8,128)(2,1)S(1)}, u32[]{:S(2)}) copy-start(bf16[2,512,256]{2,1,0:T(8,128)(2,1)S(1)} %collective-permute-done.9.refs_6_) | copy-start | bytes 1572868
  82.7 22.4 %collective-permute-start.10 = (bf16[2,512,256]{2,1,0:T(8,128)(2,1)}, bf16[2,512,256]{2,1,0:T(8,128)(2,1)}, u32[]{:S(2)}, u32[]{:S(2)}) collective-permute-start(bf16[2,512,256]{2,1,0:T(8,128)(2,1)} %collective-permute-done.3.refs_2_), channel_id=1, source_target_pairs={{8,10},{9,11},{10,8},{11,9},{12,14},{13,15},{14,12},{15,13},{24,26... | collective-permute-start | bytes 1572872 | tf_op jit(solution)/shard_map/ppermute | solution.py:396
